TPU v7x, 32 devices: a whole 2x2x4 slice. The times are simulated.
32 devices in a mesh: groups: 2 (over x), dp: 16 (over z, y, core).
Axes of the slice: x: 2, y: 2, z: 4, core: 2. Of those that a mesh axis runs over, the one named last changes fastest.
Arguments:
- acts: bfloat16 [5120, 8192], P(('groups', 'dp')), parts along dimension 0, may hold values from -6 to 6
- grads: bfloat16 [5120, 32768], P(('groups', 'dp')), parts along dimension 0, may hold values from -6 to 6
- out_factors: bfloat16 [65536, 256], P(('groups', 'dp')), parts along dimension 0, may hold values from -0.03125 to 0.03125
- in_factors: bfloat16 [16384, 256], P(('groups', 'dp')), parts along dimension 0, may hold values from -0.0625 to 0.0625
- seq_slot: int32 [64], P(('groups', 'dp')), parts along dimension 0, may hold values from 0 to 31, each once
- lengths: int32 [64], P(('groups', 'dp')), parts along dimension 0, may hold values from 1 to 80, 2240 in all
Outputs:
- influence: float32 [64, 8], P(('groups', 'dp')), parts along dimension 0
There are 2 independent parts, one for each index of `groups`. A program takes and returns all parts, laid end to end along the dimension named above; each array names one. Nothing has to cross between parts.
Inputs may be any that keep to these rules, and one draw needn't show every extreme that they name: seq_slot is a permutation of 0 to 31. `lengths`: some slot has exactly 80 tokens.
All inputs are finite; a program needn't handle non-finite values. No bound on the sum of `lengths` on one device may be relied on, other than what follows from the above.
Results may differ from a plain program's by a relative error of at most 0.0003.
Values may be sent and summed in bfloat16 or wider, within the bound.
No kernel may reach another device: no remote copies, remote signals or barrier semaphores. Data moves between devices by JAX's collectives and lax.ppermute only.
A program may use at most 128 MiB of HBM per device.

v0:
```python
import math

import jax
import jax.numpy as jnp
from jax import lax
from jax.sharding import PartitionSpec as P

RANK = 32
LEN = 80


def shards(acts, grads, out_factors, in_factors, seq_slot, lengths):
    columns = out_factors.shape[1]
    proj_out = jnp.dot(
        grads,
        lax.all_gather(out_factors, "dp", axis=0, tiled=True),
        preferred_element_type=jnp.float32,
    )
    proj_in = jnp.dot(
        acts,
        lax.all_gather(in_factors, "dp", axis=0, tiled=True),
        preferred_element_type=jnp.float32,
    )
    slots = lengths.shape[0]
    queries = columns // RANK
    contrib = (proj_out * proj_in).reshape(slots, LEN, queries, RANK).sum(axis=3)
    position = jnp.arange(LEN, dtype=jnp.int32)
    keep = (position[None, :] < lengths[:, None]).astype(jnp.float32)
    slot_score = jnp.sum(contrib * keep[:, :, None], axis=1) / math.sqrt(RANK * LEN)
    all_seqs = slots * lax.axis_size("dp")
    onehot = (seq_slot[:, None] == jnp.arange(all_seqs, dtype=jnp.int32)[None, :]).astype(
        jnp.float32
    )
    table = jnp.dot(
        onehot.T, slot_score, precision=lax.Precision.HIGHEST, preferred_element_type=jnp.float32
    )
    return lax.psum_scatter(table, "dp", scatter_dimension=0, tiled=True)


def solution(mesh):
    return jax.shard_map(
        shards,
        mesh=mesh,
        in_specs=(
            P(("groups", "dp"), None),
            P(("groups", "dp"), None),
            P(("groups", "dp"), None),
            P(("groups", "dp"), None),
            P(("groups", "dp")),
            P(("groups", "dp")),
        ),
        out_specs=P(("groups", "dp"), None),
        check_vma=False,
    )
```

profile of v0, /device:TPU:0, one launch (start us, length us, event | category | flops | bytes accessed | tf_op | source)
XLA Modules:
  0.0 260.6 jit_solution(11634360499962575307)
XLA Ops:
  6.5 0.0 copy-start
  6.5 0.0 all-gather.3.cloned.1.call-start
  6.5 0.7 all-gather.3.cloned.1.call-update
  7.3 0.0 all-gather.5.cloned.1.call-start
  7.3 0.7 all-gather.5.cloned.1.call-update
  8.0 1.2 dynamic-slice
  9.9 0.7 compare_convert_fusion
  10.6 0.0 copy-start.1
  10.6 128.5 %all-gather.3.cloned.1.call-done = bf16[32768,256]{1,0:T(8,128)(2,1)} async-done(((bf16[2048,256]{1,0:T(8,128)(2,1)}), bf16[32768,256]{1,0:T(8,128)(2,1)}) %all-gather.3.cloned.1.call-update) | async-done | bytes 16777232 | tf_op jit(solution)/shard_map/all_gather | solution.py:16
  139.1 11.8 %fusion.5 = f32[160,256]{1,0:T(8,128)S(1)} fusion(bf16[160,32768]{1,0:T(8,128)(2,1)} %param.7, bf16[32768,256]{1,0:T(8,128)(2,1)} %all-gather.3.cloned.1.call-done), kind=kOutput, calls=%fused_computation.10 | convolution fusion | flops 2684354560 | bytes 27426816 | tf_op jit(solution)/shard_map/dot_general | solution.py:14
  151.0 39.2 %all-gather.5.cloned.1.call-done = bf16[8192,256]{1,0:T(8,128)(2,1)} async-done(((bf16[512,256]{1,0:T(8,128)(2,1)}), bf16[8192,256]{1,0:T(8,128)(2,1)}) %all-gather.5.cloned.1.call-update) | async-done | bytes 4194320 | tf_op jit(solution)/shard_map/all_gather | solution.py:21
  190.2 0.0 copy-done
  190.2 3.0 %convolution_multiply_fusion = f32[160,256]{1,0:T(8,128)S(1)} fusion(f32[160,256]{1,0:T(8,128)S(1)} %fusion.5, bf16[160,8192]{1,0:T(8,128)(2,1)S(1)} %copy-done, bf16[8192,256]{1,0:T(8,128)(2,1)} %all-gather.5.cloned.1.call-done), kind=kOutput, calls=%fused_computation | convolution fusion | flops 671129600 | bytes 7143424 | tf_op jit(solution)/shard_map/dot_general | solution.py:19
  193.2 0.1 copy.9
  193.4 0.2 reshape.26
  193.6 0.1 reduce_sum.18
  193.7 0.1 multiply_reduce_fusion
  193.8 0.0 copy-done.1
  193.8 0.3 fusion
  194.1 59.2 %all-reduce = f32[32,8]{1,0:T(8,128)S(1)} all-reduce(f32[32,8]{1,0:T(8,128)S(1)} %fusion), channel_id=2, replica_groups=mesh['groups'=2,'dp'=16] {'dp'}, use_global_device_ids=true, to_apply=%region_2.0.clone | all-reduce | flops 256 | bytes 2048
  253.2 0.6 constant_dynamic-slice_fusion
Async XLA Ops:
  6.5 183.7 %copy-start = (bf16[160,8192]{1,0:T(8,128)(2,1)S(1)}, bf16[160,8192]{1,0:T(8,128)(2,1)}, u32[]{:S(2)}) copy-start(bf16[160,8192]{1,0:T(8,128)(2,1)} %param.6) | copy-start | bytes 7864324
  6.5 132.6 %all-gather.3.cloned.1.call-start = ((), (), s32[]{:S(2)}) async-start(), calls=%async_computation | async-start | bytes 17825792 | tf_op jit(solution)/shard_map/all_gather | solution.py:16
  7.3 182.9 %all-gather.5.cloned.1.call-start = ((), (), s32[]{:S(2)}) async-start(), calls=%async_computation.1 | async-start | bytes 4456448 | tf_op jit(solution)/shard_map/all_gather | solution.py:21
  10.6 183.2 %copy-start.1 = (s32[2]{0:T(128)S(1)}, s32[2]{0:T(128)}, u32[]{:S(2)}) copy-start(s32[2]{0:T(128)} %param.10) | copy-start | bytes 28
Sparse Core Ops, SparseCore 0:
  9.5 129.5 all-gather.2
  141.3 48.8 all-gather.4
where the time goes:
time: 261 us
  waiting for transfers between devices  169 us (65%)
  blocking collectives  59.2 us (23%)
  matrix products  15.1 us (6%)
  between operations  14.1 us (5%)
    all_gather x1, waiting for transfers between devices, shards(): lax.all_gather(out_factors, 'dp', axis=0, tiled=True)  129 us
    unnamed x1, blocking collectives  59.2 us
    all_gather x1, waiting for transfers between devices, shards(): lax.all_gather(in_factors, 'dp', axis=0, tiled=True)  39.2 us
    dot_general x1, matrix products, shards(): jnp.dot(grads, lax.all_gather(out_factors, 'dp', axis=0, tiled=True), pre...  11.8 us
  transfers between devices with their start and end apart: 2, of which 2 were waited for; matrix products, arithmetic and copies ran while one was open for 5% of the time, Pallas kernels for 0%

commit v1 on v0

v1 whole, which is shorter than its diff:
```python
import functools
import math

import jax
import jax.numpy as jnp
import numpy as np
from jax import lax
from jax.experimental import pallas as pl
from jax.experimental.pallas import tpu as pltpu
from jax.sharding import PartitionSpec as P

RANK = 32
LEN = 80
F32 = jnp.float32


def ring_of(chips):
    cols = max([d for d in range(1, math.isqrt(chips) + 1) if chips % d == 0 and d % 2 == 0] or [1])
    rows = chips // cols
    if cols == 1 or rows % 2:
        return list(range(chips))
    walk = []
    for r in range(rows):
        line = range(1, cols) if r % 2 == 0 else range(cols - 1, 0, -1)
        walk += [r * cols + c for c in line]
    return walk + [r * cols for r in reversed(range(rows))]


def block_orders(chips):
    ring = ring_of(chips)
    order = np.zeros((2 * chips, chips), np.int32)
    for p, chip in enumerate(ring):
        for s in range(chips):
            order[2 * chip, s] = 2 * ring[(p - s) % chips]
            order[2 * chip + 1, s] = 2 * ring[(p + s) % chips] + 1
    return order


def ring_pairs(chips):
    ring = ring_of(chips)
    pairs = []
    for p, chip in enumerate(ring):
        pairs.append((2 * chip, 2 * ring[(p + 1) % chips]))
        pairs.append((2 * chip + 1, 2 * ring[(p - 1) % chips] + 1))
    return pairs


def pack_kernel(order_ref, own_ref, out_ref):
    out_ref[...] = own_ref[...]


def pack(order, own, rows):
    tokens, steps = own.shape[0], order.shape[0]
    return pl.pallas_call(
        pack_kernel,
        grid_spec=pltpu.PrefetchScalarGridSpec(
            num_scalar_prefetch=1,
            grid=(steps,),
            in_specs=[pl.BlockSpec((tokens, rows), lambda s, o: (0, o[s]))],
            out_specs=pl.BlockSpec((tokens, rows), lambda s, o: (0, s)),
        ),
        out_shape=jax.ShapeDtypeStruct((tokens, steps * rows), own.dtype),
        cost_estimate=pl.CostEstimate(
            flops=0, bytes_accessed=4 * tokens * steps * rows, transcendentals=0
        ),
        name="pack",
    )(order, own)


def step_kernel(first, order_ref, own_ref, sib_ref, block_ref, *refs):
    out_ref = refs[-1]
    tokens = own_ref.shape[0]
    block = block_ref[...]
    own = jnp.dot(own_ref[...], block, preferred_element_type=F32)
    sib = jnp.dot(sib_ref[...], block, preferred_element_type=F32)
    if first:
        out_ref[:tokens] = own
        out_ref[tokens:] = sib
    else:
        out_ref[:tokens] = refs[0][:tokens] + own
        out_ref[tokens:] = refs[0][tokens:] + sib


def step(order, own, sib, block, total, s, part, parts):
    tokens, columns = own.shape[0], block.shape[1]
    depth = block.shape[0]
    whole = pl.BlockSpec((2 * tokens, columns), lambda i, o: (0, 0))
    in_specs = [
        pl.BlockSpec((tokens, depth), lambda i, o: (0, o[s] * parts + part)),
        pl.BlockSpec((tokens, depth), lambda i, o: (0, s * parts + part)),
        pl.BlockSpec((depth, columns), lambda i, o: (0, 0)),
    ]
    args = [order, own, sib, block]
    if total is not None:
        in_specs.append(whole)
        args.append(total)
    return pl.pallas_call(
        functools.partial(step_kernel, total is None),
        grid_spec=pltpu.PrefetchScalarGridSpec(
            num_scalar_prefetch=1, grid=(1,), in_specs=in_specs, out_specs=whole
        ),
        out_shape=jax.ShapeDtypeStruct((2 * tokens, columns), F32),
        cost_estimate=pl.CostEstimate(
            flops=4 * tokens * depth * columns,
            bytes_accessed=2 * depth * (2 * tokens + columns),
            transcendentals=0,
        ),
        name="step",
    )(*args)


def score_kernel(terms, seq_ref, len_ref, *refs):
    outs, inns, table_ref = refs[:terms], refs[terms:-1], refs[-1]
    tokens, columns = outs[-1].shape
    slots = tokens // LEN
    queries = columns // RANK
    contrib = sum(r[:tokens] for r in outs) * sum(r[:tokens] for r in inns)
    column = lax.broadcasted_iota(jnp.int32, (columns, queries), 0) // RANK
    query = lax.broadcasted_iota(jnp.int32, (columns, queries), 1)
    fold = (column == query).astype(F32)
    position = lax.broadcasted_iota(jnp.int32, (LEN, columns), 0)
    row = lax.broadcasted_iota(jnp.int32, table_ref.shape, 0)
    table = jnp.zeros(table_ref.shape, F32)
    for i in range(slots):
        kept = jnp.where(position < len_ref[i], contrib[i * LEN:(i + 1) * LEN], 0.0)
        summed = jnp.sum(kept, axis=0, keepdims=True)
        score = jnp.dot(
            summed, fold, precision=lax.Precision.HIGHEST, preferred_element_type=F32
        ) * (1.0 / math.sqrt(RANK * LEN))
        table = jnp.where(row == seq_ref[i], score, table)
    table_ref[...] = table


def score_table(seq_slot, lengths, outs, inns, rows, queries):
    vmem = pl.BlockSpec(memory_space=pltpu.VMEM)
    smem = pl.BlockSpec(memory_space=pltpu.SMEM)
    return pl.pallas_call(
        functools.partial(score_kernel, len(outs)),
        in_specs=[smem, smem] + [vmem] * (len(outs) + len(inns)),
        out_specs=vmem,
        out_shape=jax.ShapeDtypeStruct((rows, queries), F32),
        name="score",
    )(seq_slot, lengths, *outs, *inns)


def shards(acts, grads, out_factors, in_factors, seq_slot, lengths):
    devices = lax.axis_size("dp")
    chips = devices // 2
    me = lax.axis_index("dp")
    tokens = grads.shape[0]
    rows, columns = out_factors.shape
    rows_in = in_factors.shape[0]
    orders = jnp.asarray(block_orders(chips))
    mine = lax.dynamic_index_in_dim(orders, me, keepdims=False)
    theirs = lax.dynamic_index_in_dim(orders, me ^ 1, keepdims=False)
    pairs = ring_pairs(chips)
    swap = [(d, d ^ 1) for d in range(devices)]

    parts = 2 if rows >= 1024 else 1
    depth = rows // parts
    held = [out_factors[i * depth:(i + 1) * depth] for i in range(parts)]

    ring_in = rows_in % 128 == 0
    sib_grads = lax.ppermute(pack(theirs, grads, rows), "dp", swap)
    if ring_in:
        sib_acts = lax.ppermute(pack(theirs, acts, rows_in), "dp", swap)
        held.append(in_factors)

    out = inn = None
    for s in range(chips):
        coming = [lax.ppermute(b, "dp", pairs) for b in held] if s < chips - 1 else None
        for i in range(parts):
            out = step(mine, grads, sib_grads, held[i], out, s, i, parts)
        if ring_in:
            inn = step(mine, acts, sib_acts, held[parts], inn, s, 0, 1)
        held = coming

    if ring_in:
        inns = [inn, lax.ppermute(inn[tokens:], "dp", swap)]
    else:
        every = lax.all_gather(in_factors, "dp", axis=0, tiled=True)
        inns = [jnp.dot(acts, every, preferred_element_type=F32)]
    outs = [out, lax.ppermute(out[tokens:], "dp", swap)]
    slots = lengths.shape[0]
    queries = columns // RANK
    table = score_table(seq_slot, lengths, outs, inns, slots * devices, queries)
    got = lax.all_to_all(table.reshape(devices, slots, queries), "dp", 0, 0, tiled=True)
    return jnp.sum(got, axis=0)


def solution(mesh):
    return jax.shard_map(
        shards,
        mesh=mesh,
        in_specs=(
            P(("groups", "dp"), None),
            P(("groups", "dp"), None),
            P(("groups", "dp"), None),
            P(("groups", "dp"), None),
            P(("groups", "dp")),
            P(("groups", "dp")),
        ),
        out_specs=P(("groups", "dp"), None),
        check_vma=False,
    )
```

time: 261 us -> 208 us (0.80)
  waiting for transfers between devices: 169 us -> 64.5 us
  Pallas kernels: 0 us -> 88.2 us
  blocking collectives: 59.2 us -> 10.7 us
  starting transfers between devices: 0.04 us -> 38 us
  matrix products: 15.1 us -> 0 us
  between operations: 14.1 us -> 0.14 us
  local copies, waits for them, and re-layouts: 2.15 us -> 4.97 us
    all_gather x2 -> x0, waiting for transfers between devices: 168 us -> none  [the longest x1 129 us: shards(): lax.all_gather(out_factors, 'dp', axis=0, tiled=True)]
    pallas_call x0 -> x27, Pallas kernels: none -> 88.2 us  [the longest x24 71.9 us: step(): pl.pallas_call(functools.partial(step_kernel, total is None), grid_spec=p...]
    ppermute x0 -> x25, waiting for transfers between devices: none -> 64.5 us  [the longest x21 63.4 us: shards(): lax.ppermute(b, 'dp', pairs)]
    unnamed x1 -> x0, blocking collectives: 59.2 us -> none
    ppermute x0 -> x25, starting transfers between devices: none -> 38 us  [the longest x21 36.9 us: shards(): lax.ppermute(b, 'dp', pairs)]
    dot_general x3 -> x0, matrix products: 15.1 us -> none  [the longest x1 11.8 us: shards(): jnp.dot(grads, lax.all_gather(out_factors, 'dp', axis=0, tiled=True), pre...]
    all_to_all x0 -> x1, blocking collectives: none -> 10.7 us  [shards(): lax.all_to_all(table.reshape(devices, slots, queries), 'dp', 0, 0, tiled=...]
  transfers between devices with their start and end apart: 2 -> 25, of which waited for: 2 -> 12; matrix products, arithmetic and copies ran while one was open for 5% -> 1% of each run, Pallas kernels for 0% -> 38%
where the time goes in v1:
time: 208 us; the launch traced here: 207 us
  Pallas kernels  88.2 us (42%)
  waiting for transfers between devices  64.5 us (31%)
  starting transfers between devices  38 us (18%)
  blocking collectives  10.7 us (5%)
  local copies, waits for them, and re-layouts  4.97 us (2%)
    pallas_call x24, Pallas kernels, step(): pl.pallas_call(functools.partial(step_kernel, total is None), grid_spec=p...  71.9 us
    ppermute x21, waiting for transfers between devices, shards(): lax.ppermute(b, 'dp', pairs)  63.4 us
    ppermute x21, starting transfers between devices, shards(): lax.ppermute(b, 'dp', pairs)  36.9 us
    pallas_call x2, Pallas kernels, pack(): pl.pallas_call(pack_kernel, grid_spec=pltpu.PrefetchScalarGridSpec(num_sc...  14.2 us
    all_to_all x1, blocking collectives, shards(): lax.all_to_all(table.reshape(devices, slots, queries), 'dp', 0, 0, tiled=...  10.7 us
  transfers between devices with their start and end apart: 25, of which 12 were waited for; matrix products, arithmetic and copies ran while one was open for 1% of the time, Pallas kernels for 38%

profile of v1, /device:TPU:0, one launch (start us, length us, event | category | flops | bytes accessed | tf_op | source)
XLA Modules:
  0.0 207.0 jit_solution(10789675032166784778)
XLA Ops:
  0.0 1.3 dynamic-slice_bitcast_fusion
  1.3 8.1 %pack.2 = bf16[160,16384]{1,0:T(8,128)(2,1)} custom-call(s32[8]{0:T(128)} %get-tuple-element.7.order_ref, bf16[160,32768]{1,0:T(8,128)(2,1)} %own_ref.42), custom_call_target="tpu_custom_call" | custom-call | bytes 10485760 | tf_op jit(solution)/shard_map/pack/pallas_call | solution.py:54
  10.0 2.6 %collective-permute-start.8 = (bf16[1024,256]{1,0:T(8,128)(2,1)S(1)}, bf16[1024,256]{1,0:T(8,128)(2,1)S(1)}, u32[]{:S(2)}, u32[]{:S(2)}) collective-permute-start(bf16[1024,256]{1,0:T(8,128)(2,1)S(1)} %get-tuple-element.5.block_ref), channel_id=1, source_target_pairs={{2,6},{3,1},{6,10},{7,3},{10,14},{11,7},{14,12},{15,11},{12,8},{13... | collective-permute-start | bytes 1572872 | tf_op jit(solution)/shard_map/ppermute | solution.py:171
  12.6 1.6 collective-permute-start.1
  14.1 5.6 %collective-permute-done.8.block_ref = bf16[1024,256]{1,0:T(8,128)(2,1)S(1)} collective-permute-done((bf16[1024,256]{1,0:T(8,128)(2,1)S(1)}, bf16[1024,256]{1,0:T(8,128)(2,1)S(1)}, u32[]{:S(2)}, u32[]{:S(2)}) %collective-permute-start.8) | collective-permute-done | bytes 524320 | tf_op jit(solution)/shard_map/ppermute | solution.py:171
  19.8 2.0 collective-permute-start.9
  21.7 3.7 %collective-permute-done.1.block_ref = bf16[1024,256]{1,0:T(8,128)(2,1)S(1)} collective-permute-done((bf16[1024,256]{1,0:T(8,128)(2,1)S(1)}, bf16[1024,256]{1,0:T(8,128)(2,1)S(1)}, u32[]{:S(2)}, u32[]{:S(2)}) %collective-permute-start.1) | collective-permute-done | bytes 524320 | tf_op jit(solution)/shard_map/ppermute | solution.py:171
  25.4 2.0 collective-permute-start.2
  27.4 3.7 %collective-permute-done.9.block_ref = bf16[1024,256]{1,0:T(8,128)(2,1)S(1)} collective-permute-done((bf16[1024,256]{1,0:T(8,128)(2,1)S(1)}, bf16[1024,256]{1,0:T(8,128)(2,1)S(1)}, u32[]{:S(2)}, u32[]{:S(2)}) %collective-permute-start.9) | collective-permute-done | bytes 524320 | tf_op jit(solution)/shard_map/ppermute | solution.py:171
  31.0 2.0 collective-permute-start.10
  33.0 3.7 %collective-permute-done.2.block_ref = bf16[1024,256]{1,0:T(8,128)(2,1)S(1)} collective-permute-done((bf16[1024,256]{1,0:T(8,128)(2,1)S(1)}, bf16[1024,256]{1,0:T(8,128)(2,1)S(1)}, u32[]{:S(2)}, u32[]{:S(2)}) %collective-permute-start.2) | collective-permute-done | bytes 524320 | tf_op jit(solution)/shard_map/ppermute | solution.py:171
  36.6 2.0 collective-permute-start.3
  38.6 3.8 %collective-permute-done.10.block_ref = bf16[1024,256]{1,0:T(8,128)(2,1)} collective-permute-done((bf16[1024,256]{1,0:T(8,128)(2,1)S(1)}, bf16[1024,256]{1,0:T(8,128)(2,1)}, u32[]{:S(2)}, u32[]{:S(2)}) %collective-permute-start.10) | collective-permute-done | bytes 524320 | tf_op jit(solution)/shard_map/ppermute | solution.py:171
  42.4 2.0 collective-permute-start.11
  44.3 3.7 %collective-permute-done.3.block_ref = bf16[1024,256]{1,0:T(8,128)(2,1)} collective-permute-done((bf16[1024,256]{1,0:T(8,128)(2,1)S(1)}, bf16[1024,256]{1,0:T(8,128)(2,1)}, u32[]{:S(2)}, u32[]{:S(2)}) %collective-permute-start.3) | collective-permute-done | bytes 524320 | tf_op jit(solution)/shard_map/ppermute | solution.py:171
  48.0 2.0 collective-permute-start.4
  49.9 1.6 collective-permute-start.17
  51.5 10.5 %collective-permute-done.17.block_ref = bf16[512,256]{1,0:T(8,128)(2,1)} collective-permute-done((bf16[512,256]{1,0:T(8,128)(2,1)S(1)}, bf16[512,256]{1,0:T(8,128)(2,1)}, u32[]{:S(2)}, u32[]{:S(2)}) %collective-permute-start.17) | collective-permute-done | bytes 262176 | tf_op jit(solution)/shard_map/ppermute | solution.py:171
  62.0 2.0 collective-permute-start.18
  64.0 6.0 %pack.3 = bf16[160,4096]{1,0:T(8,128)(2,1)} custom-call(s32[8]{0:T(128)} %get-tuple-element.7.order_ref, bf16[160,8192]{1,0:T(8,128)(2,1)} %own_ref.51), custom_call_target="tpu_custom_call" | custom-call | bytes 2621440 | tf_op jit(solution)/shard_map/pack/pallas_call | solution.py:54
  70.0 1.6 collective-permute-start.12
  71.6 1.6 collective-permute-start.5
  73.2 1.6 collective-permute-start.19
  74.8 13.1 %collective-permute-done.19.block_ref = bf16[512,256]{1,0:T(8,128)(2,1)S(1)} collective-permute-done((bf16[512,256]{1,0:T(8,128)(2,1)}, bf16[512,256]{1,0:T(8,128)(2,1)S(1)}, u32[]{:S(2)}, u32[]{:S(2)}) %collective-permute-start.19) | collective-permute-done | bytes 262176 | tf_op jit(solution)/shard_map/ppermute | solution.py:171
  87.9 1.6 collective-permute-start.20
  89.5 1.6 collective-permute-start.13
  91.0 1.6 collective-permute-start.6
  92.6 1.6 collective-permute-done.20.block_ref
  94.3 1.6 collective-permute-start.21
  95.8 12.5 %collective-permute-done.21.block_ref = bf16[512,256]{1,0:T(8,128)(2,1)S(1)} collective-permute-done((bf16[512,256]{1,0:T(8,128)(2,1)S(1)}, bf16[512,256]{1,0:T(8,128)(2,1)S(1)}, u32[]{:S(2)}, u32[]{:S(2)}) %collective-permute-start.21) | collective-permute-done | bytes 262176 | tf_op jit(solution)/shard_map/ppermute | solution.py:171
  108.3 1.6 collective-permute-start.22
  109.9 1.6 collective-permute-start.14
  111.5 1.6 collective-permute-start.7
  113.0 1.7 collective-permute-done.22.block_ref
  114.8 1.6 collective-permute-start.23
  116.4 1.0 copy-done
  117.4 2.8 %step.40.refs_0_ = f32[320,256]{1,0:T(8,128)} custom-call(s32[8]{0:T(128)} %get-tuple-element.8.order_ref, bf16[160,8192]{1,0:T(8,128)(2,1)} %own_ref.51, bf16[160,4096]{1,0:T(8,128)(2,1)} %copy-done, bf16[512,256]{1,0:T(8,128)(2,1)} %block_ref.1), custom_call_target="tpu_custom_call" | custom-call | flops 83886080 | bytes 589824 | tf_op jit(solution)/shard_map/step/pallas_call | solution.py:97
  120.2 2.9 %step.41.refs_0_ = f32[320,256]{1,0:T(8,128)} custom-call(s32[8]{0:T(128)} %get-tuple-element.8.order_ref, bf16[160,8192]{1,0:T(8,128)(2,1)} %own_ref.51, bf16[160,4096]{1,0:T(8,128)(2,1)} %copy-done, bf16[512,256]{1,0:T(8,128)(2,1)} %collective-permute-done.17.block_ref, f32[320,256]{1,0:T(8,128)} %step.40.refs_0_), custom_call_target="tpu_custom_call" | custom-call | flops 83886080 | bytes 589824 | tf_op jit(solution)/shard_map/step/pallas_call | solution.py:97
  123.1 2.9 %step.42.refs_0_ = f32[320,256]{1,0:T(8,128)} custom-call(s32[8]{0:T(128)} %get-tuple-element.8.order_ref, bf16[160,8192]{1,0:T(8,128)(2,1)} %own_ref.51, bf16[160,4096]{1,0:T(8,128)(2,1)} %copy-done, bf16[512,256]{1,0:T(8,128)(2,1)} %collective-permute-done.18.block_ref, f32[320,256]{1,0:T(8,128)} %step.41.refs_0_), custom_call_target="tpu_custom_call" | custom-call | flops 83886080 | bytes 589824 | tf_op jit(solution)/shard_map/step/pallas_call | solution.py:97
  125.9 2.9 %step.43.refs_0_ = f32[320,256]{1,0:T(8,128)} custom-call(s32[8]{0:T(128)} %get-tuple-element.8.order_ref, bf16[160,8192]{1,0:T(8,128)(2,1)} %own_ref.51, bf16[160,4096]{1,0:T(8,128)(2,1)} %copy-done, bf16[512,256]{1,0:T(8,128)(2,1)} %copy-done.11, f32[320,256]{1,0:T(8,128)} %step.42.refs_0_), custom_call_target="tpu_custom_call" | custom-call | flops 83886080 | bytes 589824 | tf_op jit(solution)/shard_map/step/pallas_call | solution.py:97
  128.8 2.9 %step.44.refs_0_ = f32[320,256]{1,0:T(8,128)} custom-call(s32[8]{0:T(128)} %get-tuple-element.8.order_ref, bf16[160,8192]{1,0:T(8,128)(2,1)} %own_ref.51, bf16[160,4096]{1,0:T(8,128)(2,1)} %copy-done, bf16[512,256]{1,0:T(8,128)(2,1)} %copy-done.12, f32[320,256]{1,0:T(8,128)} %step.43.refs_0_), custom_call_target="tpu_custom_call" | custom-call | flops 83886080 | bytes 589824 | tf_op jit(solution)/shard_map/step/pallas_call | solution.py:97
  131.7 2.9 %step.45.refs_0_ = f32[320,256]{1,0:T(8,128)} custom-call(s32[8]{0:T(128)} %get-tuple-element.8.order_ref, bf16[160,8192]{1,0:T(8,128)(2,1)} %own_ref.51, bf16[160,4096]{1,0:T(8,128)(2,1)} %copy-done, bf16[512,256]{1,0:T(8,128)(2,1)} %copy-done.13, f32[320,256]{1,0:T(8,128)} %step.44.refs_0_), custom_call_target="tpu_custom_call" | custom-call | flops 83886080 | bytes 589824 | tf_op jit(solution)/shard_map/step/pallas_call | solution.py:97
  134.5 2.9 %step.46.refs_0_ = f32[320,256]{1,0:T(8,128)} custom-call(s32[8]{0:T(128)} %get-tuple-element.8.order_ref, bf16[160,8192]{1,0:T(8,128)(2,1)} %own_ref.51, bf16[160,4096]{1,0:T(8,128)(2,1)} %copy-done, bf16[512,256]{1,0:T(8,128)(2,1)} %collective-permute-done.22.block_ref, f32[320,256]{1,0:T(8,128)} %step.45.refs_0_), custom_call_target="tpu_custom_call" | custom-call | flops 83886080 | bytes 589824 | tf_op jit(solution)/shard_map/step/pallas_call | solution.py:97
  137.4 2.9 %step.47.refs_2_ = f32[320,256]{1,0:T(8,128)} custom-call(s32[8]{0:T(128)} %get-tuple-element.8.order_ref, bf16[160,8192]{1,0:T(8,128)(2,1)} %own_ref.51, bf16[160,4096]{1,0:T(8,128)(2,1)} %copy-done, bf16[512,256]{1,0:T(8,128)(2,1)} %collective-permute-done.23.block_ref, f32[320,256]{1,0:T(8,128)} %step.46.refs_0_), custom_call_target="tpu_custom_call" | custom-call | flops 83886080 | bytes 589824 | tf_op jit(solution)/shard_map/step/pallas_call | solution.py:97
  140.2 0.9 slice.17
  141.3 3.0 %step.24.refs_0_ = f32[320,256]{1,0:T(8,128)} custom-call(s32[8]{0:T(128)} %get-tuple-element.8.order_ref, bf16[160,32768]{1,0:T(8,128)(2,1)} %own_ref.42, bf16[160,16384]{1,0:T(8,128)(2,1)} %collective-permute-done.sib_ref, bf16[1024,256]{1,0:T(8,128)(2,1)} %copy-done.2), custom_call_target="tpu_custom_call" | custom-call | flops 167772160 | bytes 1179648 | tf_op jit(solution)/shard_map/step/pallas_call | solution.py:97
  144.2 3.1 %step.25.refs_0_ = f32[320,256]{1,0:T(8,128)} custom-call(s32[8]{0:T(128)} %get-tuple-element.8.order_ref, bf16[160,32768]{1,0:T(8,128)(2,1)} %own_ref.42, bf16[160,16384]{1,0:T(8,128)(2,1)} %collective-permute-done.sib_ref, bf16[1024,256]{1,0:T(8,128)(2,1)} %copy-done.1, f32[320,256]{1,0:T(8,128)} %step.24.refs_0_), custom_call_target="tpu_custom_call" | custom-call | flops 167772160 | bytes 1179648 | tf_op jit(solution)/shard_map/step/pallas_call | solution.py:97
  147.3 3.1 %step.26.refs_0_ = f32[320,256]{1,0:T(8,128)} custom-call(s32[8]{0:T(128)} %get-tuple-element.8.order_ref, bf16[160,32768]{1,0:T(8,128)(2,1)} %own_ref.42, bf16[160,16384]{1,0:T(8,128)(2,1)} %collective-permute-done.sib_ref, bf16[1024,256]{1,0:T(8,128)(2,1)} %copy-done.4, f32[320,256]{1,0:T(8,128)} %step.25.refs_0_), custom_call_target="tpu_custom_call" | custom-call | flops 167772160 | bytes 1179648 | tf_op jit(solution)/shard_map/step/pallas_call | solution.py:97
  150.4 3.1 %step.27.refs_0_ = f32[320,256]{1,0:T(8,128)} custom-call(s32[8]{0:T(128)} %get-tuple-element.8.order_ref, bf16[160,32768]{1,0:T(8,128)(2,1)} %own_ref.42, bf16[160,16384]{1,0:T(8,128)(2,1)} %collective-permute-done.sib_ref, bf16[1024,256]{1,0:T(8,128)(2,1)} %copy-done.5, f32[320,256]{1,0:T(8,128)} %step.26.refs_0_), custom_call_target="tpu_custom_call" | custom-call | flops 167772160 | bytes 1179648 | tf_op jit(solution)/shard_map/step/pallas_call | solution.py:97
  153.5 3.1 %step.28.refs_0_ = f32[320,256]{1,0:T(8,128)} custom-call(s32[8]{0:T(128)} %get-tuple-element.8.order_ref, bf16[160,32768]{1,0:T(8,128)(2,1)} %own_ref.42, bf16[160,16384]{1,0:T(8,128)(2,1)} %collective-permute-done.sib_ref, bf16[1024,256]{1,0:T(8,128)(2,1)} %copy-done.6, f32[320,256]{1,0:T(8,128)} %step.27.refs_0_), custom_call_target="tpu_custom_call" | custom-call | flops 167772160 | bytes 1179648 | tf_op jit(solution)/shard_map/step/pallas_call | solution.py:97
  156.6 3.1 %step.29.refs_0_ = f32[320,256]{1,0:T(8,128)} custom-call(s32[8]{0:T(128)} %get-tuple-element.8.order_ref, bf16[160,32768]{1,0:T(8,128)(2,1)} %own_ref.42, bf16[160,16384]{1,0:T(8,128)(2,1)} %collective-permute-done.sib_ref, bf16[1024,256]{1,0:T(8,128)(2,1)} %copy-done.7, f32[320,256]{1,0:T(8,128)} %step.28.refs_0_), custom_call_target="tpu_custom_call" | custom-call | flops 167772160 | bytes 1179648 | tf_op jit(solution)/shard_map/step/pallas_call | solution.py:97
  159.6 3.1 %step.30.refs_0_ = f32[320,256]{1,0:T(8,128)} custom-call(s32[8]{0:T(128)} %get-tuple-element.8.order_ref, bf16[160,32768]{1,0:T(8,128)(2,1)} %own_ref.42, bf16[160,16384]{1,0:T(8,128)(2,1)} %collective-permute-done.sib_ref, bf16[1024,256]{1,0:T(8,128)(2,1)} %collective-permute-done.10.block_ref, f32[320,256]{1,0:T(8,128)} %step.29.refs_0_), custom_call_target="tpu_custom_call" | custom-call | flops 167772160 | bytes 1179648 | tf_op jit(solution)/shard_map/step/pallas_call | solution.py:97
  162.7 3.1 %step.31.refs_0_ = f32[320,256]{1,0:T(8,128)} custom-call(s32[8]{0:T(128)} %get-tuple-element.8.order_ref, bf16[160,32768]{1,0:T(8,128)(2,1)} %own_ref.42, bf16[160,16384]{1,0:T(8,128)(2,1)} %collective-permute-done.sib_ref, bf16[1024,256]{1,0:T(8,128)(2,1)} %collective-permute-done.3.block_ref, f32[320,256]{1,0:T(8,128)} %step.30.refs_0_), custom_call_target="tpu_custom_call" | custom-call | flops 167772160 | bytes 1179648 | tf_op jit(solution)/shard_map/step/pallas_call | solution.py:97
  165.8 3.1 %step.32.refs_0_ = f32[320,256]{1,0:T(8,128)} custom-call(s32[8]{0:T(128)} %get-tuple-element.8.order_ref, bf16[160,32768]{1,0:T(8,128)(2,1)} %own_ref.42, bf16[160,16384]{1,0:T(8,128)(2,1)} %collective-permute-done.sib_ref, bf16[1024,256]{1,0:T(8,128)(2,1)} %collective-permute-done.11.block_ref, f32[320,256]{1,0:T(8,128)} %step.31.refs_0_), custom_call_target="tpu_custom_call" | custom-call | flops 167772160 | bytes 1179648 | tf_op jit(solution)/shard_map/step/pallas_call | solution.py:97
  168.8 3.1 %step.33.refs_0_ = f32[320,256]{1,0:T(8,128)} custom-call(s32[8]{0:T(128)} %get-tuple-element.8.order_ref, bf16[160,32768]{1,0:T(8,128)(2,1)} %own_ref.42, bf16[160,16384]{1,0:T(8,128)(2,1)} %collective-permute-done.sib_ref, bf16[1024,256]{1,0:T(8,128)(2,1)} %collective-permute-done.4.block_ref, f32[320,256]{1,0:T(8,128)} %step.32.refs_0_), custom_call_target="tpu_custom_call" | custom-call | flops 167772160 | bytes 1179648 | tf_op jit(solution)/shard_map/step/pallas_call | solution.py:97
  171.9 3.1 %step.34.refs_0_ = f32[320,256]{1,0:T(8,128)} custom-call(s32[8]{0:T(128)} %get-tuple-element.8.order_ref, bf16[160,32768]{1,0:T(8,128)(2,1)} %own_ref.42, bf16[160,16384]{1,0:T(8,128)(2,1)} %collective-permute-done.sib_ref, bf16[1024,256]{1,0:T(8,128)(2,1)} %copy-done.8, f32[320,256]{1,0:T(8,128)} %step.33.refs_0_), custom_call_target="tpu_custom_call" | custom-call | flops 167772160 | bytes 1179648 | tf_op jit(solution)/shard_map/step/pallas_call | solution.py:97
  175.0 3.1 %step.35.refs_0_ = f32[320,256]{1,0:T(8,128)} custom-call(s32[8]{0:T(128)} %get-tuple-element.8.order_ref, bf16[160,32768]{1,0:T(8,128)(2,1)} %own_ref.42, bf16[160,16384]{1,0:T(8,128)(2,1)} %collective-permute-done.sib_ref, bf16[1024,256]{1,0:T(8,128)(2,1)} %copy-done.9, f32[320,256]{1,0:T(8,128)} %step.34.refs_0_), custom_call_target="tpu_custom_call" | custom-call | flops 167772160 | bytes 1179648 | tf_op jit(solution)/shard_map/step/pallas_call | solution.py:97
  178.1 3.1 %step.36.refs_0_ = f32[320,256]{1,0:T(8,128)} custom-call(s32[8]{0:T(128)} %get-tuple-element.8.order_ref, bf16[160,32768]{1,0:T(8,128)(2,1)} %own_ref.42, bf16[160,16384]{1,0:T(8,128)(2,1)} %collective-permute-done.sib_ref, bf16[1024,256]{1,0:T(8,128)(2,1)} %collective-permute-done.13.block_ref, f32[320,256]{1,0:T(8,128)} %step.35.refs_0_), custom_call_target="tpu_custom_call" | custom-call | flops 167772160 | bytes 1179648 | tf_op jit(solution)/shard_map/step/pallas_call | solution.py:97
  181.2 3.1 %step.37.refs_0_ = f32[320,256]{1,0:T(8,128)} custom-call(s32[8]{0:T(128)} %get-tuple-element.8.order_ref, bf16[160,32768]{1,0:T(8,128)(2,1)} %own_ref.42, bf16[160,16384]{1,0:T(8,128)(2,1)} %collective-permute-done.sib_ref, bf16[1024,256]{1,0:T(8,128)(2,1)} %collective-permute-done.6.block_ref, f32[320,256]{1,0:T(8,128)} %step.36.refs_0_), custom_call_target="tpu_custom_call" | custom-call | flops 167772160 | bytes 1179648 | tf_op jit(solution)/shard_map/step/pallas_call | solution.py:97
  184.3 3.1 %step.38.refs_0_ = f32[320,256]{1,0:T(8,128)} custom-call(s32[8]{0:T(128)} %get-tuple-element.8.order_ref, bf16[160,32768]{1,0:T(8,128)(2,1)} %own_ref.42, bf16[160,16384]{1,0:T(8,128)(2,1)} %collective-permute-done.sib_ref, bf16[1024,256]{1,0:T(8,128)(2,1)} %collective-permute-done.14.block_ref, f32[320,256]{1,0:T(8,128)} %step.37.refs_0_), custom_call_target="tpu_custom_call" | custom-call | flops 167772160 | bytes 1179648 | tf_op jit(solution)/shard_map/step/pallas_call | solution.py:97
  187.3 3.1 %step.39.refs_0_ = f32[320,256]{1,0:T(8,128)} custom-call(s32[8]{0:T(128)} %get-tuple-element.8.order_ref, bf16[160,32768]{1,0:T(8,128)(2,1)} %own_ref.42, bf16[160,16384]{1,0:T(8,128)(2,1)} %collective-permute-done.sib_ref, bf16[1024,256]{1,0:T(8,128)(2,1)} %collective-permute-done.7.block_ref, f32[320,256]{1,0:T(8,128)} %step.38.refs_0_), custom_call_target="tpu_custom_call" | custom-call | flops 167772160 | bytes 1179648 | tf_op jit(solution)/shard_map/step/pallas_call | solution.py:97
  191.9 1.0 collective-permute-done.15.refs_1_
  193.6 2.1 %score.1 = f32[32,8]{1,0:T(8,128)} custom-call(s32[2]{0:T(128)} %seq_ref.1, s32[2]{0:T(128)} %len_ref.1, f32[320,256]{1,0:T(8,128)} %step.39.refs_0_, f32[160,256]{1,0:T(8,128)} %copy-done.15, f32[320,256]{1,0:T(8,128)} %step.47.refs_2_, f32[160,256]{1,0:T(8,128)} %copy-done.14), custom_call_target="tpu_custom_call" | custom-call | tf_op jit(solution)/shard_map/score/pallas_call | solution.py:137
  195.7 10.7 %all_to_all.5 = f32[16,2,8]{2,1,0:T(2,128)S(1)} all-to-all(f32[16,2,8]{2,1,0:T(2,128)} %bitcast.5), channel_id=1, replica_groups=mesh['groups'=2,'dp'=16] {'dp'}, dimensions={0} | all-to-all | bytes 2048 | tf_op jit(solution)/shard_map/all_to_all | solution.py:187
  (51 shorter events, 3.4 us)
Async XLA Ops:
  1.3 8.6 %copy-start.3 = (bf16[2048,256]{1,0:T(8,128)(2,1)S(1)}, bf16[2048,256]{1,0:T(8,128)(2,1)}, u32[]{:S(2)}) copy-start(bf16[2048,256]{1,0:T(8,128)(2,1)} %param.9) | copy-start | bytes 3145732
  1.3 48.6 %copy-start.10 = (bf16[512,256]{1,0:T(8,128)(2,1)S(1)}, bf16[512,256]{1,0:T(8,128)(2,1)}, u32[]{:S(2)}) copy-start(bf16[512,256]{1,0:T(8,128)(2,1)} %block_ref.1) | copy-start | bytes 786436
  9.4 131.8 %collective-permute-start = (bf16[160,16384]{1,0:T(8,128)(2,1)}, bf16[160,16384]{1,0:T(8,128)(2,1)}, u32[]{:S(2)}, u32[]{:S(2)}) collective-permute-start(bf16[160,16384]{1,0:T(8,128)(2,1)} %pack.2), channel_id=1, source_target_pairs={{0,1},{1,0},{2,3},{3,2},{4,5},{5,4},{6,7},{7,6},{8,9},{9,8},{10,11... | collective-permute-start | bytes 15728648 | tf_op jit(solution)/shard_map/ppermute | solution.py:164
  10.0 113.1 %copy-start.1 = (bf16[1024,256]{1,0:T(8,128)(2,1)}, bf16[1024,256]{1,0:T(8,128)(2,1)S(1)}, u32[]{:S(2)}) copy-start(bf16[1024,256]{1,0:T(8,128)(2,1)S(1)} %get-tuple-element.6.block_ref) | copy-start | bytes 1572868
  10.0 113.1 %copy-start.2 = (bf16[1024,256]{1,0:T(8,128)(2,1)}, bf16[1024,256]{1,0:T(8,128)(2,1)S(1)}, u32[]{:S(2)}) copy-start(bf16[1024,256]{1,0:T(8,128)(2,1)S(1)} %get-tuple-element.5.block_ref) | copy-start | bytes 1572868
  10.0 9.8 %collective-permute-start.8 = (bf16[1024,256]{1,0:T(8,128)(2,1)S(1)}, bf16[1024,256]{1,0:T(8,128)(2,1)S(1)}, u32[]{:S(2)}, u32[]{:S(2)}) collective-permute-start(bf16[1024,256]{1,0:T(8,128)(2,1)S(1)} %get-tuple-element.5.block_ref), channel_id=1, source_target_pairs={{2,6},{3,1},{6,10},{7,3},{10,14},{11,7},{14,12},{15,11},{12,8},{13... | collective-permute-start | bytes 1572872 | tf_op jit(solution)/shard_map/ppermute | solution.py:171
  12.6 12.8 %collective-permute-start.1 = (bf16[1024,256]{1,0:T(8,128)(2,1)S(1)}, bf16[1024,256]{1,0:T(8,128)(2,1)S(1)}, u32[]{:S(2)}, u32[]{:S(2)}) collective-permute-start(bf16[1024,256]{1,0:T(8,128)(2,1)S(1)} %get-tuple-element.6.block_ref), channel_id=1, source_target_pairs={{2,6},{3,1},{6,10},{7,3},{10,14},{11,7},{14,12},{15,11},{12,8},{13... | collective-permute-start | bytes 1572872 | tf_op jit(solution)/shard_map/ppermute | solution.py:171
  19.8 103.3 %copy-start.4 = (bf16[1024,256]{1,0:T(8,128)(2,1)}, bf16[1024,256]{1,0:T(8,128)(2,1)S(1)}, u32[]{:S(2)}) copy-start(bf16[1024,256]{1,0:T(8,128)(2,1)S(1)} %collective-permute-done.8.block_ref) | copy-start | bytes 1572868
  19.8 11.2 %collective-permute-start.9 = (bf16[1024,256]{1,0:T(8,128)(2,1)S(1)}, bf16[1024,256]{1,0:T(8,128)(2,1)S(1)}, u32[]{:S(2)}, u32[]{:S(2)}) collective-permute-start(bf16[1024,256]{1,0:T(8,128)(2,1)S(1)} %collective-permute-done.8.block_ref), channel_id=1, source_target_pairs={{2,6},{3,1},{6,10},{7,3},{10,14},{11,7},{14,12},{15,11},{12,8},{13... | collective-permute-start | bytes 1572872 | tf_op jit(solution)/shard_map/ppermute | solution.py:171
  25.4 97.7 %copy-start.5 = (bf16[1024,256]{1,0:T(8,128)(2,1)}, bf16[1024,256]{1,0:T(8,128)(2,1)S(1)}, u32[]{:S(2)}) copy-start(bf16[1024,256]{1,0:T(8,128)(2,1)S(1)} %collective-permute-done.1.block_ref) | copy-start | bytes 1572868
  25.4 11.2 %collective-permute-start.2 = (bf16[1024,256]{1,0:T(8,128)(2,1)S(1)}, bf16[1024,256]{1,0:T(8,128)(2,1)S(1)}, u32[]{:S(2)}, u32[]{:S(2)}) collective-permute-start(bf16[1024,256]{1,0:T(8,128)(2,1)S(1)} %collective-permute-done.1.block_ref), channel_id=1, source_target_pairs={{2,6},{3,1},{6,10},{7,3},{10,14},{11,7},{14,12},{15,11},{12,8},{13... | collective-permute-start | bytes 1572872 | tf_op jit(solution)/shard_map/ppermute | solution.py:171
  31.0 33.0 %copy-start.6 = (bf16[1024,256]{1,0:T(8,128)(2,1)}, bf16[1024,256]{1,0:T(8,128)(2,1)S(1)}, u32[]{:S(2)}) copy-start(bf16[1024,256]{1,0:T(8,128)(2,1)S(1)} %collective-permute-done.9.block_ref) | copy-start | bytes 1572868
  31.0 11.3 %collective-permute-start.10 = (bf16[1024,256]{1,0:T(8,128)(2,1)S(1)}, bf16[1024,256]{1,0:T(8,128)(2,1)}, u32[]{:S(2)}, u32[]{:S(2)}) collective-permute-start(bf16[1024,256]{1,0:T(8,128)(2,1)S(1)} %collective-permute-done.9.block_ref), channel_id=1, source_target_pairs={{2,6},{3,1},{6,10},{7,3},{10,14},{11,7},{14,12},{15,11},{12,8},{13... | collective-permute-start | bytes 1572872 | tf_op jit(solution)/shard_map/ppermute | solution.py:171
  36.6 27.4 %copy-start.7 = (bf16[1024,256]{1,0:T(8,128)(2,1)}, bf16[1024,256]{1,0:T(8,128)(2,1)S(1)}, u32[]{:S(2)}) copy-start(bf16[1024,256]{1,0:T(8,128)(2,1)S(1)} %collective-permute-done.2.block_ref) | copy-start | bytes 1572868
  36.6 11.3 %collective-permute-start.3 = (bf16[1024,256]{1,0:T(8,128)(2,1)S(1)}, bf16[1024,256]{1,0:T(8,128)(2,1)}, u32[]{:S(2)}, u32[]{:S(2)}) collective-permute-start(bf16[1024,256]{1,0:T(8,128)(2,1)S(1)} %collective-permute-done.2.block_ref), channel_id=1, source_target_pairs={{2,6},{3,1},{6,10},{7,3},{10,14},{11,7},{14,12},{15,11},{12,8},{13... | collective-permute-start | bytes 1572872 | tf_op jit(solution)/shard_map/ppermute | solution.py:171
  42.4 27.7 %collective-permute-start.11 = (bf16[1024,256]{1,0:T(8,128)(2,1)}, bf16[1024,256]{1,0:T(8,128)(2,1)}, u32[]{:S(2)}, u32[]{:S(2)}) collective-permute-start(bf16[1024,256]{1,0:T(8,128)(2,1)} %collective-permute-done.10.block_ref), channel_id=1, source_target_pairs={{2,6},{3,1},{6,10},{7,3},{10,14},{11,7},{14,12},{15,11},{12,8},{13... | collective-permute-start | bytes 1572872 | tf_op jit(solution)/shard_map/ppermute | solution.py:171
  48.0 23.7 %collective-permute-start.4 = (bf16[1024,256]{1,0:T(8,128)(2,1)}, bf16[1024,256]{1,0:T(8,128)(2,1)}, u32[]{:S(2)}, u32[]{:S(2)}) collective-permute-start(bf16[1024,256]{1,0:T(8,128)(2,1)} %collective-permute-done.3.block_ref), channel_id=1, source_target_pairs={{2,6},{3,1},{6,10},{7,3},{10,14},{11,7},{14,12},{15,11},{12,8},{13... | collective-permute-start | bytes 1572872 | tf_op jit(solution)/shard_map/ppermute | solution.py:171
  49.9 12.1 %collective-permute-start.17 = (bf16[512,256]{1,0:T(8,128)(2,1)S(1)}, bf16[512,256]{1,0:T(8,128)(2,1)}, u32[]{:S(2)}, u32[]{:S(2)}) collective-permute-start(bf16[512,256]{1,0:T(8,128)(2,1)S(1)} %copy-done.10), channel_id=1, source_target_pairs={{2,6},{3,1},{6,10},{7,3},{10,14},{11,7},{14,12},{15,11},{12,8},{13... | collective-permute-start | bytes 786440 | tf_op jit(solution)/shard_map/ppermute | solution.py:171
  62.0 11.2 %collective-permute-start.18 = (bf16[512,256]{1,0:T(8,128)(2,1)}, bf16[512,256]{1,0:T(8,128)(2,1)}, u32[]{:S(2)}, u32[]{:S(2)}) collective-permute-start(bf16[512,256]{1,0:T(8,128)(2,1)} %collective-permute-done.17.block_ref), channel_id=1, source_target_pairs={{2,6},{3,1},{6,10},{7,3},{10,14},{11,7},{14,12},{15,11},{12,8},{13... | collective-permute-start | bytes 786440 | tf_op jit(solution)/shard_map/ppermute | solution.py:171
  70.0 46.4 %collective-permute-start.16 = (bf16[160,4096]{1,0:T(8,128)(2,1)}, bf16[160,4096]{1,0:T(8,128)(2,1)S(1)}, u32[]{:S(2)}, u32[]{:S(2)}) collective-permute-start(bf16[160,4096]{1,0:T(8,128)(2,1)} %pack.3), channel_id=1, source_target_pairs={{0,1},{1,0},{2,3},{3,2},{4,5},{5,4},{6,7},{7,6},{8,9},{9,8},{10,11... | collective-permute-start | bytes 3932168 | tf_op jit(solution)/shard_map/ppermute | solution.py:166
  70.0 19.4 %collective-permute-start.12 = (bf16[1024,256]{1,0:T(8,128)(2,1)}, bf16[1024,256]{1,0:T(8,128)(2,1)S(1)}, u32[]{:S(2)}, u32[]{:S(2)}) collective-permute-start(bf16[1024,256]{1,0:T(8,128)(2,1)} %collective-permute-done.11.block_ref), channel_id=1, source_target_pairs={{2,6},{3,1},{6,10},{7,3},{10,14},{11,7},{14,12},{15,11},{12,8},{13... | collective-permute-start | bytes 1572872 | tf_op jit(solution)/shard_map/ppermute | solution.py:171
  71.6 19.4 %collective-permute-start.5 = (bf16[1024,256]{1,0:T(8,128)(2,1)}, bf16[1024,256]{1,0:T(8,128)(2,1)S(1)}, u32[]{:S(2)}, u32[]{:S(2)}) collective-permute-start(bf16[1024,256]{1,0:T(8,128)(2,1)} %collective-permute-done.4.block_ref), channel_id=1, source_target_pairs={{2,6},{3,1},{6,10},{7,3},{10,14},{11,7},{14,12},{15,11},{12,8},{13... | collective-permute-start | bytes 1572872 | tf_op jit(solution)/shard_map/ppermute | solution.py:171
  73.2 14.7 %collective-permute-start.19 = (bf16[512,256]{1,0:T(8,128)(2,1)}, bf16[512,256]{1,0:T(8,128)(2,1)S(1)}, u32[]{:S(2)}, u32[]{:S(2)}) collective-permute-start(bf16[512,256]{1,0:T(8,128)(2,1)} %collective-permute-done.18.block_ref), channel_id=1, source_target_pairs={{2,6},{3,1},{6,10},{7,3},{10,14},{11,7},{14,12},{15,11},{12,8},{13... | collective-permute-start | bytes 786440 | tf_op jit(solution)/shard_map/ppermute | solution.py:171
  87.9 28.5 %copy-start.11 = (bf16[512,256]{1,0:T(8,128)(2,1)}, bf16[512,256]{1,0:T(8,128)(2,1)S(1)}, u32[]{:S(2)}) copy-start(bf16[512,256]{1,0:T(8,128)(2,1)S(1)} %collective-permute-done.19.block_ref) | copy-start | bytes 786436
  87.9 6.4 %collective-permute-start.20 = (bf16[512,256]{1,0:T(8,128)(2,1)S(1)}, bf16[512,256]{1,0:T(8,128)(2,1)S(1)}, u32[]{:S(2)}, u32[]{:S(2)}) collective-permute-start(bf16[512,256]{1,0:T(8,128)(2,1)S(1)} %collective-permute-done.19.block_ref), channel_id=1, source_target_pairs={{2,6},{3,1},{6,10},{7,3},{10,14},{11,7},{14,12},{15,11},{12,8},{13... | collective-permute-start | bytes 786440 | tf_op jit(solution)/shard_map/ppermute | solution.py:171
  89.5 26.9 %copy-start.8 = (bf16[1024,256]{1,0:T(8,128)(2,1)}, bf16[1024,256]{1,0:T(8,128)(2,1)S(1)}, u32[]{:S(2)}) copy-start(bf16[1024,256]{1,0:T(8,128)(2,1)S(1)} %collective-permute-done.12.block_ref) | copy-start | bytes 1572868
  89.5 20.4 %collective-permute-start.13 = (bf16[1024,256]{1,0:T(8,128)(2,1)S(1)}, bf16[1024,256]{1,0:T(8,128)(2,1)}, u32[]{:S(2)}, u32[]{:S(2)}) collective-permute-start(bf16[1024,256]{1,0:T(8,128)(2,1)S(1)} %collective-permute-done.12.block_ref), channel_id=1, source_target_pairs={{2,6},{3,1},{6,10},{7,3},{10,14},{11,7},{14,12},{15,11},{12,8},{13... | collective-permute-start | bytes 1572872 | tf_op jit(solution)/shard_map/ppermute | solution.py:171
  91.0 25.3 %copy-start.9 = (bf16[1024,256]{1,0:T(8,128)(2,1)}, bf16[1024,256]{1,0:T(8,128)(2,1)S(1)}, u32[]{:S(2)}) copy-start(bf16[1024,256]{1,0:T(8,128)(2,1)S(1)} %collective-permute-done.5.block_ref) | copy-start | bytes 1572868
  91.0 20.4 %collective-permute-start.6 = (bf16[1024,256]{1,0:T(8,128)(2,1)S(1)}, bf16[1024,256]{1,0:T(8,128)(2,1)}, u32[]{:S(2)}, u32[]{:S(2)}) collective-permute-start(bf16[1024,256]{1,0:T(8,128)(2,1)S(1)} %collective-permute-done.5.block_ref), channel_id=1, source_target_pairs={{2,6},{3,1},{6,10},{7,3},{10,14},{11,7},{14,12},{15,11},{12,8},{13... | collective-permute-start | bytes 1572872 | tf_op jit(solution)/shard_map/ppermute | solution.py:171
  94.3 22.1 %copy-start.12 = (bf16[512,256]{1,0:T(8,128)(2,1)}, bf16[512,256]{1,0:T(8,128)(2,1)S(1)}, u32[]{:S(2)}) copy-start(bf16[512,256]{1,0:T(8,128)(2,1)S(1)} %collective-permute-done.20.block_ref) | copy-start | bytes 786436
  94.3 14.0 %collective-permute-start.21 = (bf16[512,256]{1,0:T(8,128)(2,1)S(1)}, bf16[512,256]{1,0:T(8,128)(2,1)S(1)}, u32[]{:S(2)}, u32[]{:S(2)}) collective-permute-start(bf16[512,256]{1,0:T(8,128)(2,1)S(1)} %collective-permute-done.20.block_ref), channel_id=1, source_target_pairs={{2,6},{3,1},{6,10},{7,3},{10,14},{11,7},{14,12},{15,11},{12,8},{13... | collective-permute-start | bytes 786440 | tf_op jit(solution)/shard_map/ppermute | solution.py:171
  108.3 8.1 %copy-start.13 = (bf16[512,256]{1,0:T(8,128)(2,1)}, bf16[512,256]{1,0:T(8,128)(2,1)S(1)}, u32[]{:S(2)}) copy-start(bf16[512,256]{1,0:T(8,128)(2,1)S(1)} %collective-permute-done.21.block_ref) | copy-start | bytes 786436
  108.3 6.5 %collective-permute-start.22 = (bf16[512,256]{1,0:T(8,128)(2,1)S(1)}, bf16[512,256]{1,0:T(8,128)(2,1)}, u32[]{:S(2)}, u32[]{:S(2)}) collective-permute-start(bf16[512,256]{1,0:T(8,128)(2,1)S(1)} %collective-permute-done.21.block_ref), channel_id=1, source_target_pairs={{2,6},{3,1},{6,10},{7,3},{10,14},{11,7},{14,12},{15,11},{12,8},{13... | collective-permute-start | bytes 786440 | tf_op jit(solution)/shard_map/ppermute | solution.py:171
  109.9 74.4 %collective-permute-start.14 = (bf16[1024,256]{1,0:T(8,128)(2,1)}, bf16[1024,256]{1,0:T(8,128)(2,1)}, u32[]{:S(2)}, u32[]{:S(2)}) collective-permute-start(bf16[1024,256]{1,0:T(8,128)(2,1)} %collective-permute-done.13.block_ref), channel_id=1, source_target_pairs={{2,6},{3,1},{6,10},{7,3},{10,14},{11,7},{14,12},{15,11},{12,8},{13... | collective-permute-start | bytes 1572872 | tf_op jit(solution)/shard_map/ppermute | solution.py:171
  111.5 75.9 %collective-permute-start.7 = (bf16[1024,256]{1,0:T(8,128)(2,1)}, bf16[1024,256]{1,0:T(8,128)(2,1)}, u32[]{:S(2)}, u32[]{:S(2)}) collective-permute-start(bf16[1024,256]{1,0:T(8,128)(2,1)} %collective-permute-done.6.block_ref), channel_id=1, source_target_pairs={{2,6},{3,1},{6,10},{7,3},{10,14},{11,7},{14,12},{15,11},{12,8},{13... | collective-permute-start | bytes 1572872 | tf_op jit(solution)/shard_map/ppermute | solution.py:171
  114.8 22.6 %collective-permute-start.23 = (bf16[512,256]{1,0:T(8,128)(2,1)}, bf16[512,256]{1,0:T(8,128)(2,1)}, u32[]{:S(2)}, u32[]{:S(2)}) collective-permute-start(bf16[512,256]{1,0:T(8,128)(2,1)} %collective-permute-done.22.block_ref), channel_id=1, source_target_pairs={{2,6},{3,1},{6,10},{7,3},{10,14},{11,7},{14,12},{15,11},{12,8},{13... | collective-permute-start | bytes 786440 | tf_op jit(solution)/shard_map/ppermute | solution.py:171
  116.4 1.1 copy-start
  141.2 50.8 %collective-permute-start.24 = (f32[160,256]{1,0:T(8,128)S(1)}, f32[160,256]{1,0:T(8,128)S(1)}, u32[]{:S(2)}, u32[]{:S(2)}) collective-permute-start(f32[160,256]{1,0:T(8,128)S(1)} %slice.17), channel_id=1, source_target_pairs={{0,1},{1,0},{2,3},{3,2},{4,5},{5,4},{6,7},{7,6},{8,9},{9,8},{10,11... | collective-permute-start | bytes 491528 | tf_op jit(solution)/shard_map/ppermute | solution.py:179
  191.3 1.6 collective-permute-start.15
  191.9 1.0 copy-start.14
  192.9 0.7 copy-start.15

commit v2 on v0

v2 whole, which is shorter than its diff:
```python
import functools
import math

import jax
import jax.numpy as jnp
import numpy as np
from jax import lax
from jax.experimental import pallas as pl
from jax.experimental.pallas import tpu as pltpu
from jax.sharding import PartitionSpec as P

RANK = 32
LEN = 80
F32 = jnp.float32
VMEM = 20 << 20


def ring_of(chips):
    cols = max([d for d in range(1, math.isqrt(chips) + 1) if chips % d == 0 and d % 2 == 0] or [1])
    rows = chips // cols
    if cols == 1 or rows % 2:
        return list(range(chips))
    walk = []
    for r in range(rows):
        line = range(1, cols) if r % 2 == 0 else range(cols - 1, 0, -1)
        walk += [r * cols + c for c in line]
    return walk + [r * cols for r in reversed(range(rows))]


def block_orders(chips):
    ring = ring_of(chips)
    order = np.zeros((2 * chips, chips), np.int32)
    for p, chip in enumerate(ring):
        for s in range(chips):
            order[2 * chip, s] = 2 * ring[(p - s) % chips]
            order[2 * chip + 1, s] = 2 * ring[(p + s) % chips] + 1
    return order


def ring_pairs(chips):
    ring = ring_of(chips)
    pairs = []
    for p, chip in enumerate(ring):
        pairs.append((2 * chip, 2 * ring[(p + 1) % chips]))
        pairs.append((2 * chip + 1, 2 * ring[(p - 1) % chips] + 1))
    return pairs


def dot(a, b):
    return jnp.dot(a, b, preferred_element_type=F32)


def call(kernel, order, windows, whole, scalars, out_shape, flops, name):
    in_specs = [pl.BlockSpec((x.shape[0], w), at) for x, w, at in windows]
    in_specs += [pl.BlockSpec(x.shape, lambda i, o: (0, 0)) for x in whole]
    in_specs += [pl.BlockSpec(memory_space=pltpu.SMEM) for _ in scalars]
    size = sum(2 * x.shape[0] * w for x, w, _ in windows)
    size += sum(x.size * x.dtype.itemsize for x in list(whole) + list(out_shape))
    return pl.pallas_call(
        kernel,
        grid_spec=pltpu.PrefetchScalarGridSpec(
            num_scalar_prefetch=1,
            grid=(1,),
            in_specs=in_specs,
            out_specs=[pl.BlockSpec(x.shape, lambda i, o: (0, 0)) for x in out_shape],
        ),
        out_shape=out_shape,
        cost_estimate=pl.CostEstimate(flops=flops, bytes_accessed=size, transcendentals=0),
        compiler_params=pltpu.CompilerParams(vmem_limit_bytes=VMEM),
        name=name,
    )(order, *[x for x, _, _ in windows], *whole, *scalars)


def step_kernel(lead, rows_in, with_b, summed, order_ref, *refs):
    refs = list(refs)
    own_g, sib_g = refs.pop(0), refs.pop(0)
    own_a, sib_a = (refs.pop(0), refs.pop(0)) if rows_in else (None, None)
    a_ref = refs.pop(0)
    b_ref = refs.pop(0) if with_b else None
    tokens = own_g.shape[0]
    for k, (g, a) in enumerate(((own_g, own_a), (sib_g, sib_a))):
        at = pl.ds(k * tokens, tokens)
        out = dot(g[:, :lead], a_ref[rows_in:])
        if with_b:
            out += dot(g[:, lead:], b_ref[...])
        if summed:
            out += refs[0][at]
        if rows_in:
            inn = dot(a[...], a_ref[:rows_in])
            if summed:
                inn += refs[1][at]
            refs[-1][at] = inn
            refs[-2][at] = out
        else:
            refs[-1][at] = out


def step(order, own, sib, blocks, totals, s, lead, rows, rows_in):
    here = lambda i, o: (0, o[s])
    windows = [(own[0], rows, here), (sib[0], rows, here)]
    if rows_in:
        windows += [(own[1], rows_in, here), (sib[1], rows_in, here)]
    tokens, columns = own[0].shape[0], blocks[0].shape[1]
    depth = sum(b.shape[0] for b in blocks)
    shape = jax.ShapeDtypeStruct((2 * tokens, columns), F32)
    return call(
        functools.partial(step_kernel, lead, rows_in, len(blocks) > 1, bool(totals)),
        order, windows, list(blocks) + list(totals), [],
        [shape] * (2 if rows_in else 1), 4 * tokens * depth * columns, "step",
    )


def score_kernel(lead, order_ref, own_g, sib_g, b_ref, out_ref, inn_ref, got_ref,
                 seq_ref, len_ref, seq_sib, len_sib, table_ref):
    tokens = own_g.shape[0]
    columns = b_ref.shape[1]
    queries = columns // RANK
    column = lax.broadcasted_iota(jnp.int32, (columns, queries), 0) // RANK
    query = lax.broadcasted_iota(jnp.int32, (columns, queries), 1)
    fold = (column == query).astype(F32)
    position = lax.broadcasted_iota(jnp.int32, (LEN, columns), 0)
    row = lax.broadcasted_iota(jnp.int32, table_ref.shape, 0)
    table = jnp.zeros(table_ref.shape, F32)
    for k, (g, seq, lens) in enumerate(((own_g, seq_ref, len_ref), (sib_g, seq_sib, len_sib))):
        mine, other = pl.ds(k * tokens, tokens), pl.ds((1 - k) * tokens, tokens)
        out = out_ref[mine] + dot(g[:, lead:], b_ref[...])
        contrib = out * (inn_ref[mine] + got_ref[other])
        for i in range(tokens // LEN):
            kept = jnp.where(position < lens[i], contrib[i * LEN:(i + 1) * LEN], 0.0)
            summed = jnp.sum(kept, axis=0, keepdims=True)
            score = jnp.dot(
                summed, fold, precision=lax.Precision.HIGHEST, preferred_element_type=F32
            ) * (1.0 / math.sqrt(RANK * LEN))
            table = jnp.where(row == seq[i], score, table)
    table_ref[...] = table


def shards(acts, grads, out_factors, in_factors, seq_slot, lengths):
    devices = lax.axis_size("dp")
    chips = devices // 2
    me = lax.axis_index("dp")
    tokens = grads.shape[0]
    rows, columns = out_factors.shape
    rows_in = in_factors.shape[0]
    orders = jnp.asarray(block_orders(chips))
    mine = lax.dynamic_index_in_dim(orders, me, keepdims=False)
    pairs = ring_pairs(chips)
    swap = [(d, d ^ 1) for d in range(devices)]

    own = [grads, acts]
    every = None
    if rows_in % 128:
        every = lax.all_gather(in_factors, "dp", axis=0, tiled=True)
        own, rows_in = own[:1], 0
    lead = (rows - rows_in) // 2
    first = out_factors[:lead]
    if rows_in:
        first = jnp.concatenate([in_factors, first])
    held = [(first, out_factors[lead:])]

    seq_sib, len_sib = lax.ppermute(jnp.stack([seq_slot, lengths]), "dp", swap)
    sib = [lax.ppermute(x, "dp", swap) for x in own]

    totals, summed = [], 0

    def sum_to(k, totals, summed):
        for j in range(summed, k):
            totals = step(mine, own, sib, held[j], totals, j, lead, rows, rows_in)
        return totals, max(k, summed)

    for s in range(chips - 1):
        a, b = held[s]
        if s >= 3:
            totals, summed = sum_to(min(2 * s - 5, s), totals, summed)
            a, *totals = lax.optimization_barrier((a, *totals))
            b, *totals = lax.optimization_barrier((b, *totals))
        held.append((lax.ppermute(a, "dp", pairs), lax.ppermute(b, "dp", pairs)))
    totals, summed = sum_to(chips - 1, totals, summed)
    s = chips - 1
    a, b = held[s]
    totals = step(mine, own, sib, [a], totals, s, lead, rows, rows_in)
    if every is not None:
        inn = dot(acts, every)
        totals = [totals[0], jnp.concatenate([inn, jnp.zeros_like(inn)])]
    got = lax.ppermute(totals[1], "dp", swap)

    slots = lengths.shape[0]
    queries = columns // RANK
    windows = [(x, rows, lambda i, o: (0, o[s])) for x in (grads, sib[0])]
    table = call(
        functools.partial(score_kernel, lead), mine, windows, [b, *totals, got],
        [seq_slot, lengths, seq_sib, len_sib],
        [jax.ShapeDtypeStruct((slots * devices, queries), F32)],
        4 * tokens * rows * columns, "score",
    )[0]
    got = lax.all_to_all(table.reshape(devices, slots, queries), "dp", 0, 0, tiled=True)
    return jnp.sum(got, axis=0)


def solution(mesh):
    return jax.shard_map(
        shards,
        mesh=mesh,
        in_specs=(
            P(("groups", "dp"), None),
            P(("groups", "dp"), None),
            P(("groups", "dp"), None),
            P(("groups", "dp"), None),
            P(("groups", "dp")),
            P(("groups", "dp")),
        ),
        out_specs=P(("groups", "dp"), None),
        check_vma=False,
    )
```

time: 261 us -> 122 us (0.47)
  waiting for transfers between devices: 169 us -> 45.9 us
  blocking collectives: 59.2 us -> 12.7 us
  starting transfers between devices: 0.04 us -> 28.8 us
  Pallas kernels: 0 us -> 21.9 us
  matrix products: 15.1 us -> 0 us
  between operations: 14.1 us -> 0.17 us
  local copies, waits for them, and re-layouts: 2.15 us -> 10.7 us
    all_gather x2 -> x0, waiting for transfers between devices: 168 us -> none  [the longest x1 129 us: shards(): lax.all_gather(out_factors, 'dp', axis=0, tiled=True)]
    unnamed x1 -> x0, blocking collectives: 59.2 us -> none
    ppermute x0 -> x18, waiting for transfers between devices: none -> 45.9 us  [the longest x14 44.8 us: shards(): held.append((lax.ppermute(a, 'dp', pairs), lax.ppermute(b, 'dp', pairs)))]
    ppermute x0 -> x18, starting transfers between devices: none -> 28.8 us  [the longest x14 27.7 us: shards(): held.append((lax.ppermute(a, 'dp', pairs), lax.ppermute(b, 'dp', pairs)))]
    pallas_call x0 -> x9, Pallas kernels: none -> 21.9 us  [call(): pl.pallas_call(kernel, grid_spec=pltpu.PrefetchScalarGridSpec(num_scalar_...]
    dot_general x3 -> x0, matrix products: 15.1 us -> none  [the longest x1 11.8 us: shards(): jnp.dot(grads, lax.all_gather(out_factors, 'dp', axis=0, tiled=True), pre...]
    all_to_all x0 -> x1, blocking collectives: none -> 12.7 us  [shards(): lax.all_to_all(table.reshape(devices, slots, queries), 'dp', 0, 0, tiled=...]
    unnamed x6 -> x20, local copies, waits for them, and re-layouts: 1.82 us -> 7.64 us
  transfers between devices with their start and end apart: 2 -> 18, of which waited for: 2 -> 12; matrix products, arithmetic and copies ran while one was open for 5% -> 3% of each run, Pallas kernels for 0% -> 16%
where the time goes in v2:
time: 122 us
  waiting for transfers between devices  45.9 us (38%)
  starting transfers between devices  28.8 us (24%)
  Pallas kernels  21.9 us (18%)
  blocking collectives  12.7 us (10%)
  local copies, waits for them, and re-layouts  10.7 us (9%)
  other arithmetic  1.59 us (1%)
    ppermute x14, waiting for transfers between devices, shards(): held.append((lax.ppermute(a, 'dp', pairs), lax.ppermute(b, 'dp', pairs)))  44.8 us
    ppermute x14, starting transfers between devices, shards(): held.append((lax.ppermute(a, 'dp', pairs), lax.ppermute(b, 'dp', pairs)))  27.7 us
    pallas_call x9, Pallas kernels, call(): pl.pallas_call(kernel, grid_spec=pltpu.PrefetchScalarGridSpec(num_scalar_...  21.9 us
    all_to_all x1, blocking collectives, shards(): lax.all_to_all(table.reshape(devices, slots, queries), 'dp', 0, 0, tiled=...  12.7 us
    unnamed x20, local copies, waits for them, and re-layouts  7.64 us
  transfers between devices with their start and end apart: 18, of which 12 were waited for; matrix products, arithmetic and copies ran while one was open for 3% of the time, Pallas kernels for 16%

profile of v2, /device:TPU:0, one launch (start us, length us, event | category | flops | bytes accessed | tf_op | source)
XLA Modules:
  0.0 121.8 jit_solution(7343288125611503559)
XLA Ops:
  0.0 0.0 copy-start.1
  0.0 0.5 collective-permute-start
  0.5 0.1 collective-permute-start.7
  0.5 1.3 %slice.7 = bf16[768,256]{1,0:T(8,128)(2,1)S(1)} slice(bf16[2048,256]{1,0:T(8,128)(2,1)} %param.9), slice={[0:768], [0:256]} | slice | bytes 786432 | tf_op jit(solution)/shard_map/slice | solution.py:156
  1.8 1.0 pad_maximum_fusion.refs_4_
  2.8 3.0 %collective-permute-start.4 = (bf16[1280,256]{1,0:T(8,128)(2,1)S(1)}, bf16[1280,256]{1,0:T(8,128)(2,1)S(1)}, u32[]{:S(2)}, u32[]{:S(2)}) collective-permute-start(bf16[1280,256]{1,0:T(8,128)(2,1)S(1)} %pad_maximum_fusion.refs_4_), channel_id=1, source_target_pairs={{2,6},{3,1},{6,10},{7,3},{10,14},{11,7},{14,12},{15,11},{12,8},{13... | collective-permute-start | bytes 1966088 | tf_op jit(solution)/shard_map/ppermute | solution.py:177
  5.8 1.1 slice.6.refs_5_
  6.9 1.6 %collective-permute-start.1 = (bf16[1280,256]{1,0:T(8,128)(2,1)S(1)}, bf16[1280,256]{1,0:T(8,128)(2,1)S(1)}, u32[]{:S(2)}, u32[]{:S(2)}) collective-permute-start(bf16[1280,256]{1,0:T(8,128)(2,1)S(1)} %slice.6.refs_5_), channel_id=1, source_target_pairs={{2,6},{3,1},{6,10},{7,3},{10,14},{11,7},{14,12},{15,11},{12,8},{13... | collective-permute-start | bytes 1966088 | tf_op jit(solution)/shard_map/ppermute | solution.py:177
  8.6 0.0 copy-start.2
  8.6 0.8 copy-done.2
  9.4 5.0 %collective-permute-done.4.refs_4_ = bf16[1280,256]{1,0:T(8,128)(2,1)S(1)} collective-permute-done((bf16[1280,256]{1,0:T(8,128)(2,1)S(1)}, bf16[1280,256]{1,0:T(8,128)(2,1)S(1)}, u32[]{:S(2)}, u32[]{:S(2)}) %collective-permute-start.4) | collective-permute-done | bytes 655392 | tf_op jit(solution)/shard_map/ppermute | solution.py:177
  14.4 2.0 %collective-permute-start.5 = (bf16[1280,256]{1,0:T(8,128)(2,1)S(1)}, bf16[1280,256]{1,0:T(8,128)(2,1)}, u32[]{:S(2)}, u32[]{:S(2)}) collective-permute-start(bf16[1280,256]{1,0:T(8,128)(2,1)S(1)} %collective-permute-done.4.refs_4_), channel_id=1, source_target_pairs={{2,6},{3,1},{6,10},{7,3},{10,14},{11,7},{14,12},{15,11},{12,8},{13... | collective-permute-start | bytes 1966088 | tf_op jit(solution)/shard_map/ppermute | solution.py:177
  16.4 0.9 copy-done.4
  17.3 4.2 %collective-permute-done.1.refs_5_ = bf16[1280,256]{1,0:T(8,128)(2,1)S(1)} collective-permute-done((bf16[1280,256]{1,0:T(8,128)(2,1)S(1)}, bf16[1280,256]{1,0:T(8,128)(2,1)S(1)}, u32[]{:S(2)}, u32[]{:S(2)}) %collective-permute-start.1) | collective-permute-done | bytes 655392 | tf_op jit(solution)/shard_map/ppermute | solution.py:177
  21.5 2.0 %collective-permute-start.2 = (bf16[1280,256]{1,0:T(8,128)(2,1)S(1)}, bf16[1280,256]{1,0:T(8,128)(2,1)}, u32[]{:S(2)}, u32[]{:S(2)}) collective-permute-start(bf16[1280,256]{1,0:T(8,128)(2,1)S(1)} %collective-permute-done.1.refs_5_), channel_id=1, source_target_pairs={{2,6},{3,1},{6,10},{7,3},{10,14},{11,7},{14,12},{15,11},{12,8},{13... | collective-permute-start | bytes 1966088 | tf_op jit(solution)/shard_map/ppermute | solution.py:177
  23.4 0.9 copy-done.6
  24.3 4.3 %collective-permute-done.5.refs_4_ = bf16[1280,256]{1,0:T(8,128)(2,1)} collective-permute-done((bf16[1280,256]{1,0:T(8,128)(2,1)S(1)}, bf16[1280,256]{1,0:T(8,128)(2,1)}, u32[]{:S(2)}, u32[]{:S(2)}) %collective-permute-start.5) | collective-permute-done | bytes 655392 | tf_op jit(solution)/shard_map/ppermute | solution.py:177
  28.6 2.0 %collective-permute-start.6 = (bf16[1280,256]{1,0:T(8,128)(2,1)}, bf16[1280,256]{1,0:T(8,128)(2,1)}, u32[]{:S(2)}, u32[]{:S(2)}) collective-permute-start(bf16[1280,256]{1,0:T(8,128)(2,1)} %collective-permute-done.5.refs_4_), channel_id=1, source_target_pairs={{2,6},{3,1},{6,10},{7,3},{10,14},{11,7},{14,12},{15,11},{12,8},{13... | collective-permute-start | bytes 1966088 | tf_op jit(solution)/shard_map/ppermute | solution.py:177
  30.5 5.1 %collective-permute-done.2.refs_5_ = bf16[1280,256]{1,0:T(8,128)(2,1)} collective-permute-done((bf16[1280,256]{1,0:T(8,128)(2,1)S(1)}, bf16[1280,256]{1,0:T(8,128)(2,1)}, u32[]{:S(2)}, u32[]{:S(2)}) %collective-permute-start.2) | collective-permute-done | bytes 655392 | tf_op jit(solution)/shard_map/ppermute | solution.py:177
  35.6 2.0 %collective-permute-start.3 = (bf16[1280,256]{1,0:T(8,128)(2,1)}, bf16[1280,256]{1,0:T(8,128)(2,1)}, u32[]{:S(2)}, u32[]{:S(2)}) collective-permute-start(bf16[1280,256]{1,0:T(8,128)(2,1)} %collective-permute-done.2.refs_5_), channel_id=1, source_target_pairs={{2,6},{3,1},{6,10},{7,3},{10,14},{11,7},{14,12},{15,11},{12,8},{13... | collective-permute-start | bytes 1966088 | tf_op jit(solution)/shard_map/ppermute | solution.py:177
  37.6 0.7 dynamic-slice_bitcast_fusion.order_ref
  38.3 0.0 collective-permute-done.7.refs_3_
  38.3 0.0 collective-permute-done.refs_1_.sib_g
  38.3 0.0 copy-done.1
  38.3 0.0 copy-start
  38.3 4.0 %copy-done = bf16[160,32768]{1,0:T(8,128)(2,1)S(1)} copy-done((bf16[160,32768]{1,0:T(8,128)(2,1)S(1)}, bf16[160,32768]{1,0:T(8,128)(2,1)}, u32[]{:S(2)}) %copy-start) | copy-done | bytes 10485784
  42.3 1.1 copy-done.3
  43.4 2.3 %step.8 = (f32[320,256]{1,0:T(8,128)S(1)}, f32[320,256]{1,0:T(8,128)S(1)}) custom-call(s32[8]{0:T(128)S(1)} %dynamic-slice_bitcast_fusion.order_ref, bf16[160,32768]{1,0:T(8,128)(2,1)S(1)} %copy-done, bf16[160,32768]{1,0:T(8,128)(2,1)} %collective-permute-done.refs_1_.sib_g, bf16[160,8192]{1,0:T(8,128)(2,1)S(1)} %copy-done.1, ...), custom_call_target="tpu_custom_call" | custom-call | flops 419430400 | bytes 3604480 | tf_op jit(solution)/shard_map/step/pallas_call | solution.py:59
  45.7 0.0 collective-permute-done.6.refs_4_
  45.7 1.6 %collective-permute-start.9 = (bf16[1280,256]{1,0:T(8,128)(2,1)}, bf16[1280,256]{1,0:T(8,128)(2,1)S(1)}, u32[]{:S(2)}, u32[]{:S(2)}) collective-permute-start(bf16[1280,256]{1,0:T(8,128)(2,1)} %collective-permute-done.6.refs_4_), channel_id=1, source_target_pairs={{2,6},{3,1},{6,10},{7,3},{10,14},{11,7},{14,12},{15,11},{12,8},{13... | collective-permute-start | bytes 1966088 | tf_op jit(solution)/shard_map/ppermute | solution.py:177
  47.3 2.3 %collective-permute-done.3.refs_5_ = bf16[1280,256]{1,0:T(8,128)(2,1)} collective-permute-done((bf16[1280,256]{1,0:T(8,128)(2,1)}, bf16[1280,256]{1,0:T(8,128)(2,1)}, u32[]{:S(2)}, u32[]{:S(2)}) %collective-permute-start.3) | collective-permute-done | bytes 655392 | tf_op jit(solution)/shard_map/ppermute | solution.py:177
  49.6 2.0 %collective-permute-start.8 = (bf16[1280,256]{1,0:T(8,128)(2,1)}, bf16[1280,256]{1,0:T(8,128)(2,1)S(1)}, u32[]{:S(2)}, u32[]{:S(2)}) collective-permute-start(bf16[1280,256]{1,0:T(8,128)(2,1)} %collective-permute-done.3.refs_5_), channel_id=1, source_target_pairs={{2,6},{3,1},{6,10},{7,3},{10,14},{11,7},{14,12},{15,11},{12,8},{13... | collective-permute-start | bytes 1966088 | tf_op jit(solution)/shard_map/ppermute | solution.py:177
  51.6 0.0 copy-done.5
  51.6 0.0 copy-done.7
  51.6 2.3 %step.9 = (f32[320,256]{1,0:T(8,128)S(1)}, f32[320,256]{1,0:T(8,128)S(1)}) custom-call(s32[8]{0:T(128)S(1)} %dynamic-slice_bitcast_fusion.order_ref, bf16[160,32768]{1,0:T(8,128)(2,1)S(1)} %copy-done, bf16[160,32768]{1,0:T(8,128)(2,1)} %collective-permute-done.refs_1_.sib_g, bf16[160,8192]{1,0:T(8,128)(2,1)S(1)} %copy-done.1, ...), custom_call_target="tpu_custom_call" | custom-call | flops 419430400 | bytes 4259840 | tf_op jit(solution)/shard_map/step/pallas_call | solution.py:59
  53.9 2.7 %step.10 = (f32[320,256]{1,0:T(8,128)S(1)}, f32[320,256]{1,0:T(8,128)S(1)}) custom-call(s32[8]{0:T(128)S(1)} %dynamic-slice_bitcast_fusion.order_ref, bf16[160,32768]{1,0:T(8,128)(2,1)S(1)} %copy-done, bf16[160,32768]{1,0:T(8,128)(2,1)} %collective-permute-done.refs_1_.sib_g, bf16[160,8192]{1,0:T(8,128)(2,1)S(1)} %copy-done.1, ...), custom_call_target="tpu_custom_call" | custom-call | flops 419430400 | bytes 4259840 | tf_op jit(solution)/shard_map/step/pallas_call | solution.py:59
  56.7 0.0 collective-permute-done.9.refs_4_
  56.7 1.8 %collective-permute-start.11 = (bf16[1280,256]{1,0:T(8,128)(2,1)S(1)}, bf16[1280,256]{1,0:T(8,128)(2,1)S(1)}, u32[]{:S(2)}, u32[]{:S(2)}) collective-permute-start(bf16[1280,256]{1,0:T(8,128)(2,1)S(1)} %collective-permute-done.9.refs_4_), channel_id=1, source_target_pairs={{2,6},{3,1},{6,10},{7,3},{10,14},{11,7},{14,12},{15,11},{12,8},{13... | collective-permute-start | bytes 1966088 | tf_op jit(solution)/shard_map/ppermute | solution.py:177
  58.5 5.1 %collective-permute-done.8.refs_5_ = bf16[1280,256]{1,0:T(8,128)(2,1)S(1)} collective-permute-done((bf16[1280,256]{1,0:T(8,128)(2,1)}, bf16[1280,256]{1,0:T(8,128)(2,1)S(1)}, u32[]{:S(2)}, u32[]{:S(2)}) %collective-permute-start.8) | collective-permute-done | bytes 655392 | tf_op jit(solution)/shard_map/ppermute | solution.py:177
  63.6 2.0 %collective-permute-start.10 = (bf16[1280,256]{1,0:T(8,128)(2,1)S(1)}, bf16[1280,256]{1,0:T(8,128)(2,1)S(1)}, u32[]{:S(2)}, u32[]{:S(2)}) collective-permute-start(bf16[1280,256]{1,0:T(8,128)(2,1)S(1)} %collective-permute-done.8.refs_5_), channel_id=1, source_target_pairs={{2,6},{3,1},{6,10},{7,3},{10,14},{11,7},{14,12},{15,11},{12,8},{13... | collective-permute-start | bytes 1966088 | tf_op jit(solution)/shard_map/ppermute | solution.py:177
  65.6 2.7 %step.11 = (f32[320,256]{1,0:T(8,128)S(1)}, f32[320,256]{1,0:T(8,128)S(1)}) custom-call(s32[8]{0:T(128)S(1)} %dynamic-slice_bitcast_fusion.order_ref, bf16[160,32768]{1,0:T(8,128)(2,1)S(1)} %copy-done, bf16[160,32768]{1,0:T(8,128)(2,1)} %collective-permute-done.refs_1_.sib_g, bf16[160,8192]{1,0:T(8,128)(2,1)S(1)} %copy-done.1, ...), custom_call_target="tpu_custom_call" | custom-call | flops 419430400 | bytes 4259840 | tf_op jit(solution)/shard_map/step/pallas_call | solution.py:59
  68.3 2.3 %step.12 = (f32[320,256]{1,0:T(8,128)S(1)}, f32[320,256]{1,0:T(8,128)S(1)}) custom-call(s32[8]{0:T(128)S(1)} %dynamic-slice_bitcast_fusion.order_ref, bf16[160,32768]{1,0:T(8,128)(2,1)S(1)} %copy-done, bf16[160,32768]{1,0:T(8,128)(2,1)} %collective-permute-done.refs_1_.sib_g, bf16[160,8192]{1,0:T(8,128)(2,1)S(1)} %copy-done.1, ...), custom_call_target="tpu_custom_call" | custom-call | flops 419430400 | bytes 4259840 | tf_op jit(solution)/shard_map/step/pallas_call | solution.py:59
  70.6 0.0 collective-permute-done.11.refs_4_
  70.6 1.9 %collective-permute-start.13 = (bf16[1280,256]{1,0:T(8,128)(2,1)S(1)}, bf16[1280,256]{1,0:T(8,128)(2,1)S(1)}, u32[]{:S(2)}, u32[]{:S(2)}) collective-permute-start(bf16[1280,256]{1,0:T(8,128)(2,1)S(1)} %collective-permute-done.11.refs_4_), channel_id=1, source_target_pairs={{2,6},{3,1},{6,10},{7,3},{10,14},{11,7},{14,12},{15,11},{12,8},{13... | collective-permute-start | bytes 1966088 | tf_op jit(solution)/shard_map/ppermute | solution.py:177
  72.6 5.1 %collective-permute-done.10.refs_5_ = bf16[1280,256]{1,0:T(8,128)(2,1)S(1)} collective-permute-done((bf16[1280,256]{1,0:T(8,128)(2,1)S(1)}, bf16[1280,256]{1,0:T(8,128)(2,1)S(1)}, u32[]{:S(2)}, u32[]{:S(2)}) %collective-permute-start.10) | collective-permute-done | bytes 655392 | tf_op jit(solution)/shard_map/ppermute | solution.py:177
  77.6 2.0 %collective-permute-start.12 = (bf16[1280,256]{1,0:T(8,128)(2,1)S(1)}, bf16[1280,256]{1,0:T(8,128)(2,1)S(1)}, u32[]{:S(2)}, u32[]{:S(2)}) collective-permute-start(bf16[1280,256]{1,0:T(8,128)(2,1)S(1)} %collective-permute-done.10.refs_5_), channel_id=1, source_target_pairs={{2,6},{3,1},{6,10},{7,3},{10,14},{11,7},{14,12},{15,11},{12,8},{13... | collective-permute-start | bytes 1966088 | tf_op jit(solution)/shard_map/ppermute | solution.py:177
  79.6 2.3 %step.13 = (f32[320,256]{1,0:T(8,128)S(1)}, f32[320,256]{1,0:T(8,128)S(1)}) custom-call(s32[8]{0:T(128)S(1)} %dynamic-slice_bitcast_fusion.order_ref, bf16[160,32768]{1,0:T(8,128)(2,1)S(1)} %copy-done, bf16[160,32768]{1,0:T(8,128)(2,1)} %collective-permute-done.refs_1_.sib_g, bf16[160,8192]{1,0:T(8,128)(2,1)S(1)} %copy-done.1, ...), custom_call_target="tpu_custom_call" | custom-call | flops 419430400 | bytes 4259840 | tf_op jit(solution)/shard_map/step/pallas_call | solution.py:59
  81.9 2.7 %collective-permute-done.13.refs_4_ = bf16[1280,256]{1,0:T(8,128)(2,1)S(1)} collective-permute-done((bf16[1280,256]{1,0:T(8,128)(2,1)S(1)}, bf16[1280,256]{1,0:T(8,128)(2,1)S(1)}, u32[]{:S(2)}, u32[]{:S(2)}) %collective-permute-start.13) | collective-permute-done | bytes 655392 | tf_op jit(solution)/shard_map/ppermute | solution.py:177
  84.7 2.0 %collective-permute-start.15 = (bf16[1280,256]{1,0:T(8,128)(2,1)S(1)}, bf16[1280,256]{1,0:T(8,128)(2,1)S(1)}, u32[]{:S(2)}, u32[]{:S(2)}) collective-permute-start(bf16[1280,256]{1,0:T(8,128)(2,1)S(1)} %collective-permute-done.13.refs_4_), channel_id=1, source_target_pairs={{2,6},{3,1},{6,10},{7,3},{10,14},{11,7},{14,12},{15,11},{12,8},{13... | collective-permute-start | bytes 1966088 | tf_op jit(solution)/shard_map/ppermute | solution.py:177
  86.6 5.1 %collective-permute-done.12.refs_5_ = bf16[1280,256]{1,0:T(8,128)(2,1)S(1)} collective-permute-done((bf16[1280,256]{1,0:T(8,128)(2,1)S(1)}, bf16[1280,256]{1,0:T(8,128)(2,1)S(1)}, u32[]{:S(2)}, u32[]{:S(2)}) %collective-permute-start.12) | collective-permute-done | bytes 655392 | tf_op jit(solution)/shard_map/ppermute | solution.py:177
  91.7 2.0 %collective-permute-start.14 = (bf16[1280,256]{1,0:T(8,128)(2,1)S(1)}, bf16[1280,256]{1,0:T(8,128)(2,1)S(1)}, u32[]{:S(2)}, u32[]{:S(2)}) collective-permute-start(bf16[1280,256]{1,0:T(8,128)(2,1)S(1)} %collective-permute-done.12.refs_5_), channel_id=1, source_target_pairs={{2,6},{3,1},{6,10},{7,3},{10,14},{11,7},{14,12},{15,11},{12,8},{13... | collective-permute-start | bytes 1966088 | tf_op jit(solution)/shard_map/ppermute | solution.py:177
  93.6 2.3 %step.14 = (f32[320,256]{1,0:T(8,128)S(1)}, f32[320,256]{1,0:T(8,128)S(1)}) custom-call(s32[8]{0:T(128)S(1)} %dynamic-slice_bitcast_fusion.order_ref, bf16[160,32768]{1,0:T(8,128)(2,1)S(1)} %copy-done, bf16[160,32768]{1,0:T(8,128)(2,1)} %collective-permute-done.refs_1_.sib_g, bf16[160,8192]{1,0:T(8,128)(2,1)S(1)} %copy-done.1, ...), custom_call_target="tpu_custom_call" | custom-call | flops 419430400 | bytes 4259840 | tf_op jit(solution)/shard_map/step/pallas_call | solution.py:59
  96.0 2.7 %collective-permute-done.15.refs_4_ = bf16[1280,256]{1,0:T(8,128)(2,1)S(1)} collective-permute-done((bf16[1280,256]{1,0:T(8,128)(2,1)S(1)}, bf16[1280,256]{1,0:T(8,128)(2,1)S(1)}, u32[]{:S(2)}, u32[]{:S(2)}) %collective-permute-start.15) | collective-permute-done | bytes 655392 | tf_op jit(solution)/shard_map/ppermute | solution.py:177
  98.7 2.1 %step.15 = (f32[320,256]{1,0:T(8,128)S(1)}, f32[320,256]{1,0:T(8,128)S(1)}) custom-call(s32[8]{0:T(128)S(1)} %dynamic-slice_bitcast_fusion.order_ref, bf16[160,32768]{1,0:T(8,128)(2,1)S(1)} %copy-done, bf16[160,32768]{1,0:T(8,128)(2,1)} %collective-permute-done.refs_1_.sib_g, bf16[160,8192]{1,0:T(8,128)(2,1)S(1)} %copy-done.1, ...), custom_call_target="tpu_custom_call" | custom-call | flops 209715200 | bytes 3604480 | tf_op jit(solution)/shard_map/step/pallas_call | solution.py:59
  100.8 0.1 collective-permute-start.16
  100.8 0.0 copy-done.8
  100.9 0.0 copy-done.9
  100.9 0.5 collective-permute-start.17
  101.4 1.0 collective-permute-done.17
  102.5 3.3 %collective-permute-done.14.b_ref = bf16[1280,256]{1,0:T(8,128)(2,1)S(1)} collective-permute-done((bf16[1280,256]{1,0:T(8,128)(2,1)S(1)}, bf16[1280,256]{1,0:T(8,128)(2,1)S(1)}, u32[]{:S(2)}, u32[]{:S(2)}) %collective-permute-start.14) | collective-permute-done | bytes 655392 | tf_op jit(solution)/shard_map/ppermute | solution.py:177
  105.7 0.0 collective-permute-done.16.got_ref
  105.7 2.8 %score.1 = f32[32,8]{1,0:T(8,128)S(1)} custom-call(s32[8]{0:T(128)S(1)} %dynamic-slice_bitcast_fusion.order_ref, bf16[160,32768]{1,0:T(8,128)(2,1)S(1)} %copy-done, bf16[160,32768]{1,0:T(8,128)(2,1)} %collective-permute-done.refs_1_.sib_g, bf16[1280,256]{1,0:T(8,128)(2,1)S(1)} %collective-permute-done.14.b_ref, f32[320,256]{1,0:T(8,128)S(1)} %get-tuple-element.83.out_ref, ...), custom_call_target="tpu_custom_call" | custom-call | flops 335544320 | bytes 2950144 | tf_op jit(solution)/shard_map/score/pallas_call | solution.py:59
  108.6 12.7 %all_to_all.5 = f32[16,2,8]{2,1,0:T(2,128)S(1)} all-to-all(f32[16,2,8]{2,1,0:T(2,128)S(1)} %bitcast.9), channel_id=1, replica_groups=mesh['groups'=2,'dp'=16] {'dp'}, dimensions={0} | all-to-all | bytes 2048 | tf_op jit(solution)/shard_map/all_to_all | solution.py:196
  121.3 0.6 reduce_sum.9
  (9 shorter events, 0.0 us)
Async XLA Ops:
  0.0 38.3 %copy-start.1 = (bf16[160,8192]{1,0:T(8,128)(2,1)S(1)}, bf16[160,8192]{1,0:T(8,128)(2,1)}, u32[]{:S(2)}) copy-start(bf16[160,8192]{1,0:T(8,128)(2,1)} %refs_2_.15) | copy-start | bytes 7864324
  0.0 38.3 %collective-permute-start = (bf16[160,32768]{1,0:T(8,128)(2,1)}, bf16[160,32768]{1,0:T(8,128)(2,1)}, u32[]{:S(2)}, u32[]{:S(2)}) collective-permute-start(bf16[160,32768]{1,0:T(8,128)(2,1)} %own_g.1), channel_id=1, source_target_pairs={{0,1},{1,0},{2,3},{3,2},{4,5},{5,4},{6,7},{7,6},{8,9},{9,8},{10,11... | collective-permute-start | bytes 31457288 | tf_op jit(solution)/shard_map/ppermute | solution.py:162
  0.5 37.8 %collective-permute-start.7 = (bf16[160,8192]{1,0:T(8,128)(2,1)}, bf16[160,8192]{1,0:T(8,128)(2,1)}, u32[]{:S(2)}, u32[]{:S(2)}) collective-permute-start(bf16[160,8192]{1,0:T(8,128)(2,1)} %refs_2_.15), channel_id=1, source_target_pairs={{0,1},{1,0},{2,3},{3,2},{4,5},{5,4},{6,7},{7,6},{8,9},{9,8},{10,11... | collective-permute-start | bytes 7864328 | tf_op jit(solution)/shard_map/ppermute | solution.py:162
  2.8 11.6 %collective-permute-start.4 = (bf16[1280,256]{1,0:T(8,128)(2,1)S(1)}, bf16[1280,256]{1,0:T(8,128)(2,1)S(1)}, u32[]{:S(2)}, u32[]{:S(2)}) collective-permute-start(bf16[1280,256]{1,0:T(8,128)(2,1)S(1)} %pad_maximum_fusion.refs_4_), channel_id=1, source_target_pairs={{2,6},{3,1},{6,10},{7,3},{10,14},{11,7},{14,12},{15,11},{12,8},{13... | collective-permute-start | bytes 1966088 | tf_op jit(solution)/shard_map/ppermute | solution.py:177
  6.9 14.5 %collective-permute-start.1 = (bf16[1280,256]{1,0:T(8,128)(2,1)S(1)}, bf16[1280,256]{1,0:T(8,128)(2,1)S(1)}, u32[]{:S(2)}, u32[]{:S(2)}) collective-permute-start(bf16[1280,256]{1,0:T(8,128)(2,1)S(1)} %slice.6.refs_5_), channel_id=1, source_target_pairs={{2,6},{3,1},{6,10},{7,3},{10,14},{11,7},{14,12},{15,11},{12,8},{13... | collective-permute-start | bytes 1966088 | tf_op jit(solution)/shard_map/ppermute | solution.py:177
  8.6 0.8 copy-start.2
  14.4 14.1 %collective-permute-start.5 = (bf16[1280,256]{1,0:T(8,128)(2,1)S(1)}, bf16[1280,256]{1,0:T(8,128)(2,1)}, u32[]{:S(2)}, u32[]{:S(2)}) collective-permute-start(bf16[1280,256]{1,0:T(8,128)(2,1)S(1)} %collective-permute-done.4.refs_4_), channel_id=1, source_target_pairs={{2,6},{3,1},{6,10},{7,3},{10,14},{11,7},{14,12},{15,11},{12,8},{13... | collective-permute-start | bytes 1966088 | tf_op jit(solution)/shard_map/ppermute | solution.py:177
  16.4 0.9 copy-start.4
  21.5 14.1 %collective-permute-start.2 = (bf16[1280,256]{1,0:T(8,128)(2,1)S(1)}, bf16[1280,256]{1,0:T(8,128)(2,1)}, u32[]{:S(2)}, u32[]{:S(2)}) collective-permute-start(bf16[1280,256]{1,0:T(8,128)(2,1)S(1)} %collective-permute-done.1.refs_5_), channel_id=1, source_target_pairs={{2,6},{3,1},{6,10},{7,3},{10,14},{11,7},{14,12},{15,11},{12,8},{13... | collective-permute-start | bytes 1966088 | tf_op jit(solution)/shard_map/ppermute | solution.py:177
  23.4 0.9 copy-start.6
  28.6 17.1 %collective-permute-start.6 = (bf16[1280,256]{1,0:T(8,128)(2,1)}, bf16[1280,256]{1,0:T(8,128)(2,1)}, u32[]{:S(2)}, u32[]{:S(2)}) collective-permute-start(bf16[1280,256]{1,0:T(8,128)(2,1)} %collective-permute-done.5.refs_4_), channel_id=1, source_target_pairs={{2,6},{3,1},{6,10},{7,3},{10,14},{11,7},{14,12},{15,11},{12,8},{13... | collective-permute-start | bytes 1966088 | tf_op jit(solution)/shard_map/ppermute | solution.py:177
  35.6 14.0 %collective-permute-start.3 = (bf16[1280,256]{1,0:T(8,128)(2,1)}, bf16[1280,256]{1,0:T(8,128)(2,1)}, u32[]{:S(2)}, u32[]{:S(2)}) collective-permute-start(bf16[1280,256]{1,0:T(8,128)(2,1)} %collective-permute-done.2.refs_5_), channel_id=1, source_target_pairs={{2,6},{3,1},{6,10},{7,3},{10,14},{11,7},{14,12},{15,11},{12,8},{13... | collective-permute-start | bytes 1966088 | tf_op jit(solution)/shard_map/ppermute | solution.py:177
  38.3 4.0 %copy-start = (bf16[160,32768]{1,0:T(8,128)(2,1)S(1)}, bf16[160,32768]{1,0:T(8,128)(2,1)}, u32[]{:S(2)}) copy-start(bf16[160,32768]{1,0:T(8,128)(2,1)} %own_g.1) | copy-start | bytes 31457284
  42.3 1.1 copy-start.3
  43.3 8.3 %copy-start.5 = (bf16[1280,256]{1,0:T(8,128)(2,1)S(1)}, bf16[1280,256]{1,0:T(8,128)(2,1)}, u32[]{:S(2)}) copy-start(bf16[1280,256]{1,0:T(8,128)(2,1)} %copy-done.4) | copy-start | bytes 1966084
  43.3 8.3 %copy-start.7 = (bf16[1280,256]{1,0:T(8,128)(2,1)S(1)}, bf16[1280,256]{1,0:T(8,128)(2,1)}, u32[]{:S(2)}) copy-start(bf16[1280,256]{1,0:T(8,128)(2,1)} %copy-done.6) | copy-start | bytes 1966084
  45.7 11.0 %collective-permute-start.9 = (bf16[1280,256]{1,0:T(8,128)(2,1)}, bf16[1280,256]{1,0:T(8,128)(2,1)S(1)}, u32[]{:S(2)}, u32[]{:S(2)}) collective-permute-start(bf16[1280,256]{1,0:T(8,128)(2,1)} %collective-permute-done.6.refs_4_), channel_id=1, source_target_pairs={{2,6},{3,1},{6,10},{7,3},{10,14},{11,7},{14,12},{15,11},{12,8},{13... | collective-permute-start | bytes 1966088 | tf_op jit(solution)/shard_map/ppermute | solution.py:177
  49.6 13.9 %collective-permute-start.8 = (bf16[1280,256]{1,0:T(8,128)(2,1)}, bf16[1280,256]{1,0:T(8,128)(2,1)S(1)}, u32[]{:S(2)}, u32[]{:S(2)}) collective-permute-start(bf16[1280,256]{1,0:T(8,128)(2,1)} %collective-permute-done.3.refs_5_), channel_id=1, source_target_pairs={{2,6},{3,1},{6,10},{7,3},{10,14},{11,7},{14,12},{15,11},{12,8},{13... | collective-permute-start | bytes 1966088 | tf_op jit(solution)/shard_map/ppermute | solution.py:177
  56.7 13.9 %collective-permute-start.11 = (bf16[1280,256]{1,0:T(8,128)(2,1)S(1)}, bf16[1280,256]{1,0:T(8,128)(2,1)S(1)}, u32[]{:S(2)}, u32[]{:S(2)}) collective-permute-start(bf16[1280,256]{1,0:T(8,128)(2,1)S(1)} %collective-permute-done.9.refs_4_), channel_id=1, source_target_pairs={{2,6},{3,1},{6,10},{7,3},{10,14},{11,7},{14,12},{15,11},{12,8},{13... | collective-permute-start | bytes 1966088 | tf_op jit(solution)/shard_map/ppermute | solution.py:177
  63.6 14.0 %collective-permute-start.10 = (bf16[1280,256]{1,0:T(8,128)(2,1)S(1)}, bf16[1280,256]{1,0:T(8,128)(2,1)S(1)}, u32[]{:S(2)}, u32[]{:S(2)}) collective-permute-start(bf16[1280,256]{1,0:T(8,128)(2,1)S(1)} %collective-permute-done.8.refs_5_), channel_id=1, source_target_pairs={{2,6},{3,1},{6,10},{7,3},{10,14},{11,7},{14,12},{15,11},{12,8},{13... | collective-permute-start | bytes 1966088 | tf_op jit(solution)/shard_map/ppermute | solution.py:177
  70.6 14.0 %collective-permute-start.13 = (bf16[1280,256]{1,0:T(8,128)(2,1)S(1)}, bf16[1280,256]{1,0:T(8,128)(2,1)S(1)}, u32[]{:S(2)}, u32[]{:S(2)}) collective-permute-start(bf16[1280,256]{1,0:T(8,128)(2,1)S(1)} %collective-permute-done.11.refs_4_), channel_id=1, source_target_pairs={{2,6},{3,1},{6,10},{7,3},{10,14},{11,7},{14,12},{15,11},{12,8},{13... | collective-permute-start | bytes 1966088 | tf_op jit(solution)/shard_map/ppermute | solution.py:177
  77.6 14.0 %collective-permute-start.12 = (bf16[1280,256]{1,0:T(8,128)(2,1)S(1)}, bf16[1280,256]{1,0:T(8,128)(2,1)S(1)}, u32[]{:S(2)}, u32[]{:S(2)}) collective-permute-start(bf16[1280,256]{1,0:T(8,128)(2,1)S(1)} %collective-permute-done.10.refs_5_), channel_id=1, source_target_pairs={{2,6},{3,1},{6,10},{7,3},{10,14},{11,7},{14,12},{15,11},{12,8},{13... | collective-permute-start | bytes 1966088 | tf_op jit(solution)/shard_map/ppermute | solution.py:177
  84.7 14.0 %collective-permute-start.15 = (bf16[1280,256]{1,0:T(8,128)(2,1)S(1)}, bf16[1280,256]{1,0:T(8,128)(2,1)S(1)}, u32[]{:S(2)}, u32[]{:S(2)}) collective-permute-start(bf16[1280,256]{1,0:T(8,128)(2,1)S(1)} %collective-permute-done.13.refs_4_), channel_id=1, source_target_pairs={{2,6},{3,1},{6,10},{7,3},{10,14},{11,7},{14,12},{15,11},{12,8},{13... | collective-permute-start | bytes 1966088 | tf_op jit(solution)/shard_map/ppermute | solution.py:177
  91.7 14.0 %collective-permute-start.14 = (bf16[1280,256]{1,0:T(8,128)(2,1)S(1)}, bf16[1280,256]{1,0:T(8,128)(2,1)S(1)}, u32[]{:S(2)}, u32[]{:S(2)}) collective-permute-start(bf16[1280,256]{1,0:T(8,128)(2,1)S(1)} %collective-permute-done.12.refs_5_), channel_id=1, source_target_pairs={{2,6},{3,1},{6,10},{7,3},{10,14},{11,7},{14,12},{15,11},{12,8},{13... | collective-permute-start | bytes 1966088 | tf_op jit(solution)/shard_map/ppermute | solution.py:177
  98.7 2.1 %copy-start.8 = (s32[2]{0:T(128)S(1)}, s32[2]{0:T(128)}, u32[]{:S(2)}) copy-start(s32[2]{0:T(128)} %seq_ref.1) | copy-start | bytes 28
  98.7 2.2 %copy-start.9 = (s32[2]{0:T(128)S(1)}, s32[2]{0:T(128)}, u32[]{:S(2)}) copy-start(s32[2]{0:T(128)} %len_ref.1) | copy-start | bytes 28
  100.8 5.0 %collective-permute-start.16 = (f32[320,256]{1,0:T(8,128)S(1)}, f32[320,256]{1,0:T(8,128)S(1)}, u32[]{:S(2)}, u32[]{:S(2)}) collective-permute-start(f32[320,256]{1,0:T(8,128)S(1)} %get-tuple-element.84.inn_ref), channel_id=1, source_target_pairs={{0,1},{1,0},{2,3},{3,2},{4,5},{5,4},{6,7},{7,6},{8,9},{9,8},{10,11... | collective-permute-start | bytes 983048 | tf_op jit(solution)/shard_map/ppermute | solution.py:185
  100.9 1.6 %collective-permute-start.17 = (s32[2,2]{1,0:T(2,128)S(1)}, s32[2,2]{1,0:T(2,128)S(1)}, u32[]{:S(2)}, u32[]{:S(2)}) collective-permute-start(s32[2,2]{1,0:T(2,128)S(1)} %pad_add_fusion), channel_id=1, source_target_pairs={{0,1},{1,0},{2,3},{3,2},{4,5},{5,4},{6,7},{7,6},{8,9},{9,8},{10,11... | collective-permute-start | bytes 56 | tf_op jit(solution)/shard_map/ppermute | solution.py:161

commit v3 on v2

--- a/solution.py
+++ b/solution.py
@@ -12,7 +12,7 @@
 RANK = 32
 LEN = 80
 F32 = jnp.float32
-VMEM = 20 << 20
+VMEM = 26 << 20
 
 
 def ring_of(chips):
@@ -135,7 +135,7 @@
     table_ref[...] = table
 
 
-def shards(acts, grads, out_factors, in_factors, seq_slot, lengths):
+def ring_shards(acts, grads, out_factors, in_factors, seq_slot, lengths):
     devices = lax.axis_size("dp")
     chips = devices // 2
     me = lax.axis_index("dp")
@@ -197,6 +197,262 @@
     return jnp.sum(got, axis=0)
 
 
+FORWARD = {1: 2, 2: 5, 5: 6, 6: 1}
+MIDDLE = {0: 1, 7: 6, 3: 2, 4: 5}
+ACROSS = {0: 7, 7: 0, 3: 4, 4: 3}
+LANE = {0: 0, 7: 1, 3: 1, 4: 0}
+
+
+class Grid:
+    def __init__(self):
+        ring = ring_of(8)
+        at = lambda place, core: 2 * ring[place] + core
+        self.inner = [(at(m, 0), at(n, 0)) for m, n in FORWARD.items()]
+        self.inner += [(at(n, 1), at(m, 1)) for m, n in FORWARD.items()]
+        feed = [(at(m, LANE[q]), at(q, LANE[q])) for q, m in MIDDLE.items()]
+        self.feed = feed
+        self.other = [(at(m, 1 - LANE[q]), at(q, 1 - LANE[q])) for q, m in MIDDLE.items()]
+        self.relay = [(at(q, LANE[q]), at(n, LANE[q])) for q, n in ACROSS.items()]
+        cross = [(at(q, 1 - LANE[q]), at(n, 1 - LANE[q])) for q, n in ACROSS.items()]
+        self.inward = [(at(q, c), at(m, c)) for q, m in MIDDLE.items() for c in (0, 1)]
+        self.first = self.inner + self.relay + cross
+        self.second = self.inward + feed
+        self.third = self.inner + self.relay
+
+        def sent(ids, pairs):
+            got = np.full(16, -1)
+            for i, j in pairs:
+                got[j] = ids[i]
+            return got
+
+        stages = []
+        last, early = self.flow(np.arange(16), sent, lambda *arrays: stages.append(arrays))
+        stages.append(last)
+        table = np.stack([np.max(np.stack(x), axis=0) for x in stages], axis=1)
+        late = [src for src, _ in feed]
+        skipped = np.zeros(16, int)
+        for q, m in self.inward:
+            skipped[q] = (last[0] if m in late else early)[m]
+        places = [ring.index(d // 2) for d in range(16)]
+        own_in = []
+        for d in range(16):
+            core = d % 2
+            turn = -1 if core == 0 else 1
+            row = [d]
+            for k in (1, 2, 3):
+                chip = ring[(places[d] + turn * k) % 8]
+                row += [2 * chip + core, 2 * chip + 1 - core]
+            own_in.append(row + [2 * ring[(places[d] + 4) % 8] + core])
+        flag = np.array([d in late for d in range(16)], int)
+        for d in range(16):
+            blocks = sorted(x for x in table[d] if x >= 0)
+            extra = [skipped[d]] if len(blocks) == 7 else []
+            lane = sorted(set(range(16)) - set(blocks) - set(extra))
+            assert len(blocks) + len(extra) == 8
+            assert [x % 2 for x in lane] == [1 - d % 2] * 8
+        table = np.maximum(table, 0)
+        self.table = np.concatenate(
+            [table, skipped[:, None], flag[:, None], np.array(own_in)], axis=1
+        ).astype(np.int32)
+
+    def flow(self, own, send, sums=lambda *arrays: None, tie=lambda x: x):
+        m0 = send(own, self.first)
+        m1 = send(own, self.second)
+        r1 = send(m0, self.inner)
+        z1 = send(m0, self.feed)
+        m2 = send(m1, self.third)
+        r3 = send(r1, self.inner)
+        z2 = send(r1, self.feed)
+        y2 = send(z1, self.relay)
+        sums(own)
+        sums(m0)
+        r4 = send(tie(m2), self.inner)
+        w = send(m2, self.other)
+        y3 = send(z2, self.relay)
+        z4 = send(r3, self.feed)
+        sums(m1)
+        sums(m2)
+        r5 = send(tie(r4), self.inner)
+        z5 = send(r4, self.feed)
+        sums(r1, z1, y2)
+        y5 = send(tie(z4), self.relay)
+        sums(r3, z2, y3)
+        sums(r4, z4, w)
+        return (r5, z5, y5), r4
+
+
+SKIPPED, LATE, OWN_IN = 8, 9, 10
+
+
+def joined(refs):
+    block = refs[0][...]
+    for ref in refs[1:]:
+        block = block + ref[...]
+    return block
+
+
+def stage_kernel(count, summed, order_ref, own_ref, sib_ref, *refs):
+    block = joined(refs[:count])
+    tokens = own_ref.shape[0]
+    for k, ref in enumerate((own_ref, sib_ref)):
+        at = pl.ds(k * tokens, tokens)
+        new = dot(ref[...], block)
+        refs[-1][at] = refs[count][at] + new if summed else new
+
+
+def stage(order, pair, arrays, total, j):
+    rows, columns = arrays[0].shape
+    tokens = pair[0].shape[0]
+    windows = [(x, rows, lambda i, o: (0, o[j])) for x in pair]
+    return call(
+        functools.partial(stage_kernel, len(arrays), total is not None),
+        order, windows, list(arrays) + ([] if total is None else [total]), [],
+        [jax.ShapeDtypeStruct((2 * tokens, columns), F32)],
+        4 * tokens * rows * columns, "stage",
+    )[0]
+
+
+def inside_kernel(sizes, summed, order_ref, *refs):
+    windows, refs = refs[:2 * sum(sizes)], refs[2 * sum(sizes):]
+    blocks, refs = refs[:len(sizes)], refs[len(sizes):]
+    tokens = windows[0].shape[0]
+    rows = windows[0].shape[1]
+    for k in range(2):
+        at = pl.ds(k * tokens, tokens)
+        new = refs[0][at] if summed else 0.0
+        w = 0
+        for block, size in zip(blocks, sizes):
+            for i in range(size):
+                new += dot(windows[2 * w + k][...], block[i * rows:(i + 1) * rows])
+                w += 1
+        refs[-1][at] = new
+
+
+def inside(order, pair, rows, arrays, total, first):
+    tokens, columns = pair[0].shape[0], arrays[0].shape[1]
+    sizes = [x.shape[0] // rows for x in arrays]
+    windows = []
+    for w in range(sum(sizes)):
+        pick = functools.partial(lambda i, o, col: (0, o[col]), col=first + w)
+        windows += [(x, rows, pick) for x in pair]
+    return call(
+        functools.partial(inside_kernel, sizes, total is not None),
+        order, windows, list(arrays) + ([] if total is None else [total]), [],
+        [jax.ShapeDtypeStruct((2 * tokens, columns), F32)],
+        4 * tokens * rows * sum(sizes) * columns, "inside",
+    )[0]
+
+
+def window_kernel(order_ref, own_ref, sib_ref, out_ref):
+    tokens = own_ref.shape[0]
+    out_ref[:tokens] = own_ref[...]
+    out_ref[tokens:] = sib_ref[...]
+
+
+def finish_kernel(count, order_ref, own_ref, sib_ref, *refs):
+    arrays, refs = refs[:count], refs[count:]
+    early_ref, total_ref, inn_ref, job_ref, job_inn_ref, slots_ref, job_slots_ref, table_ref = refs
+    tokens, columns = own_ref.shape[0], total_ref.shape[1]
+    queries = columns // RANK
+    column = lax.broadcasted_iota(jnp.int32, (columns, queries), 0) // RANK
+    query = lax.broadcasted_iota(jnp.int32, (columns, queries), 1)
+    fold = (column == query).astype(F32)
+    position = lax.broadcasted_iota(jnp.int32, (LEN, columns), 0)
+    row = lax.broadcasted_iota(jnp.int32, table_ref.shape, 0)
+    late = jnp.full(early_ref.shape, order_ref[LATE], jnp.int32) == 1
+    block = joined(arrays)
+    skipped = jnp.where(late, arrays[0][...], early_ref[...])
+    sums, slots = [], []
+    parts = [
+        (total_ref[:tokens] + dot(own_ref[...], block), inn_ref[:tokens], slots_ref, 0),
+        (total_ref[tokens:] + dot(sib_ref[...], block), inn_ref[tokens:], slots_ref, 1),
+        (dot(job_ref[:tokens], skipped), job_inn_ref[:tokens], job_slots_ref, 0),
+        (dot(job_ref[tokens:], skipped), job_inn_ref[tokens:], job_slots_ref, 1),
+    ]
+    held = tokens // LEN
+    for out, inn, ids, k in parts:
+        contrib = out * inn
+        for i in range(held):
+            kept = jnp.where(
+                position < ids[1, k * held + i], contrib[i * LEN:(i + 1) * LEN], 0.0
+            )
+            sums.append(jnp.sum(kept, axis=0, keepdims=True))
+            slots.append(ids[0, k * held + i])
+    scores = jnp.dot(
+        jnp.concatenate(sums), fold, precision=lax.Precision.HIGHEST, preferred_element_type=F32
+    ) * (1.0 / math.sqrt(RANK * LEN))
+    table = jnp.zeros(table_ref.shape, F32)
+    for i, slot in enumerate(slots):
+        table += jnp.where(row == slot, scores[i:i + 1], 0.0)
+    table_ref[...] = table
+
+
+def grid_shards(acts, grads, out_factors, in_factors, seq_slot, lengths):
+    devices = lax.axis_size("dp")
+    grid = Grid()
+    tokens = grads.shape[0]
+    rows, columns = out_factors.shape
+    rows_in = in_factors.shape[0]
+    order = lax.dynamic_index_in_dim(jnp.asarray(grid.table), lax.axis_index("dp"), keepdims=False)
+    send = lambda x, pairs: lax.ppermute(x, "dp", pairs)
+    swap = lambda x: send(x, [(d, d ^ 1) for d in range(devices)])
+    around = ring_pairs(devices // 2)
+
+    in_hops = [in_factors]
+    hop = jnp.concatenate([send(in_factors, around), send(swap(in_factors), around)])
+    for k in range(2):
+        in_hops.append(hop)
+        hop = send(hop, around)
+    in_hops += [hop, send(hop[:rows_in], around)]
+
+    pair = (grads, swap(grads))
+    pair_in = (acts, swap(acts))
+    slots = jnp.stack([seq_slot, lengths])
+    slots = jnp.concatenate([slots, swap(slots)], axis=1)
+    job_slots = send(slots, grid.inward)
+
+    totals = [None]
+
+    def sums(*arrays):
+        totals.append(stage(order, pair, arrays, totals[-1], len(totals) - 1))
+
+    def tie(x):
+        x, totals[-1] = lax.optimization_barrier((x, totals[-1]))
+        return x
+
+    last, early = grid.flow(out_factors, send, sums, tie)
+
+    job = call(
+        window_kernel, order, [(x, rows, lambda i, o: (0, o[SKIPPED])) for x in pair], [], [],
+        [jax.ShapeDtypeStruct((2 * tokens, rows), grads.dtype)], 0, "window",
+    )[0]
+    job = send(job, grid.inward)
+
+    inn = inside(order, pair_in, rows_in, in_hops[:2], None, OWN_IN)
+    inn = inside(order, pair_in, rows_in, in_hops[2:], inn, OWN_IN + 3)
+    got = swap(inn)
+    inn = inn + jnp.concatenate([got[tokens:], got[:tokens]])
+    job_inn = send(inn, grid.inward)
+
+    queries = columns // RANK
+    held = lengths.shape[0]
+    table = call(
+        functools.partial(finish_kernel, len(last)), order,
+        [(x, rows, lambda i, o: (0, o[7])) for x in pair],
+        list(last) + [early, totals[-1], inn, job, job_inn], [slots, job_slots],
+        [jax.ShapeDtypeStruct((held * devices, queries), F32)],
+        8 * tokens * rows * columns, "finish",
+    )[0]
+    got = lax.all_to_all(table.reshape(devices, held, queries), "dp", 0, 0, tiled=True)
+    return jnp.sum(got, axis=0)
+
+
+def shards(acts, grads, out_factors, in_factors, seq_slot, lengths):
+    small = lax.axis_size("dp") == 16 and in_factors.shape[0] % 128 == 0
+    run = grid_shards if small else ring_shards
+    return run(acts, grads, out_factors, in_factors, seq_slot, lengths)
+
+
 def solution(mesh):
     return jax.shard_map(
         shards,

time: 122 us -> 175 us (1.43)
  starting transfers between devices: 28.8 us -> 54.6 us
  waiting for transfers between devices: 45.9 us -> 66.4 us
  local copies, waits for them, and re-layouts: 10.7 us -> 13.4 us
  Pallas kernels: 21.9 us -> 24.3 us
    ppermute x18 -> x28, starting transfers between devices: 28.8 us -> 54.6 us  [grid_shards(): send = lambda x, pairs: lax.ppermute(x, 'dp', pairs)]
    ppermute x18 -> x28, waiting for transfers between devices: 45.9 us -> 66.4 us  [grid_shards(): send = lambda x, pairs: lax.ppermute(x, 'dp', pairs)]
    unnamed x20 -> x35, local copies, waits for them, and re-layouts: 7.64 us -> 12 us
    pallas_call x9 -> x11, Pallas kernels: 21.9 us -> 24.3 us  [call(): pl.pallas_call(kernel, grid_spec=pltpu.PrefetchScalarGridSpec(num_scalar_...]
  transfers between devices with their start and end apart: 18 -> 28, of which waited for: 12 -> 11; matrix products, arithmetic and copies ran while one was open for 3% -> 1% of each run, Pallas kernels for 16% -> 12%
where the time goes in v3:
time: 175 us; the launch traced here: 174 us
  waiting for transfers between devices  66.4 us (38%)
  starting transfers between devices  54.6 us (31%)
  Pallas kernels  24.3 us (14%)
  blocking collectives  13.5 us (8%)
  local copies, waits for them, and re-layouts  13.4 us (8%)
    ppermute x28, waiting for transfers between devices, grid_shards(): send = lambda x, pairs: lax.ppermute(x, 'dp', pairs)  66.4 us
    ppermute x28, starting transfers between devices, grid_shards(): send = lambda x, pairs: lax.ppermute(x, 'dp', pairs)  54.6 us
    pallas_call x11, Pallas kernels, call(): pl.pallas_call(kernel, grid_spec=pltpu.PrefetchScalarGridSpec(num_scalar_...  24.3 us
    all_to_all x1, blocking collectives, grid_shards(): lax.all_to_all(table.reshape(devices, held, queries), 'dp', 0, 0, tiled=T...  13.5 us
    unnamed x35, local copies, waits for them, and re-layouts  12 us
  transfers between devices with their start and end apart: 28, of which 11 were waited for; matrix products, arithmetic and copies ran while one was open for 1% of the time, Pallas kernels for 12%

profile of v3, /device:TPU:0, one launch (start us, length us, event | category | flops | bytes accessed | tf_op | source)
XLA Modules:
  0.0 174.1 jit_solution(13297681440764154086)
XLA Ops:
  0.0 0.5 collective-permute-start
  0.5 0.1 collective-permute-start.18
  0.5 3.0 %collective-permute-start.3 = (bf16[2048,256]{1,0:T(8,128)(2,1)}, bf16[2048,256]{1,0:T(8,128)(2,1)}, u32[]{:S(2)}, u32[]{:S(2)}) collective-permute-start(bf16[2048,256]{1,0:T(8,128)(2,1)} %refs_0_.3), channel_id=1, source_target_pairs={{6,10},{10,8},{8,4},{4,6},{11,7},{9,11},{5,9},{7,5},{2,0},{1,3},{1... | collective-permute-start | bytes 3145736 | tf_op jit(solution)/shard_map/ppermute | solution.py:397
  3.5 0.0 collective-permute-start.17
  3.5 3.1 %collective-permute-done.18 = bf16[512,256]{1,0:T(8,128)(2,1)S(1)} collective-permute-done((bf16[512,256]{1,0:T(8,128)(2,1)}, bf16[512,256]{1,0:T(8,128)(2,1)S(1)}, u32[]{:S(2)}, u32[]{:S(2)}) %collective-permute-start.18) | collective-permute-done | bytes 262176 | tf_op jit(solution)/shard_map/ppermute | solution.py:397
  6.7 3.1 %collective-permute-start.19 = (bf16[512,256]{1,0:T(8,128)(2,1)S(1)}, bf16[512,256]{1,0:T(8,128)(2,1)S(1)}, u32[]{:S(2)}, u32[]{:S(2)}) collective-permute-start(bf16[512,256]{1,0:T(8,128)(2,1)S(1)} %collective-permute-done.18), channel_id=1, source_target_pairs={{2,6},{3,1},{6,10},{7,3},{10,14},{11,7},{14,12},{15,11},{12,8},{13... | collective-permute-start | bytes 786440 | tf_op jit(solution)/shard_map/ppermute | solution.py:397
  9.8 2.0 %collective-permute-start.1 = (bf16[2048,256]{1,0:T(8,128)(2,1)}, bf16[2048,256]{1,0:T(8,128)(2,1)S(1)}, u32[]{:S(2)}, u32[]{:S(2)}) collective-permute-start(bf16[2048,256]{1,0:T(8,128)(2,1)} %refs_0_.3), channel_id=1, source_target_pairs={{2,6},{3,7},{0,4},{1,5},{14,10},{15,11},{12,8},{13,9},{6,2},{5,1},... | collective-permute-start | bytes 3145736 | tf_op jit(solution)/shard_map/ppermute | solution.py:397
  11.8 0.7 pad_add_fusion
  12.5 16.7 %collective-permute-done.17 = bf16[512,256]{1,0:T(8,128)(2,1)S(1)} collective-permute-done((bf16[512,256]{1,0:T(8,128)(2,1)}, bf16[512,256]{1,0:T(8,128)(2,1)S(1)}, u32[]{:S(2)}, u32[]{:S(2)}) %collective-permute-start.17) | collective-permute-done | bytes 262176 | tf_op jit(solution)/shard_map/ppermute | solution.py:397
  29.2 0.5 collective-permute-start.16
  29.7 2.2 %collective-permute-done.19 = bf16[512,256]{1,0:T(8,128)(2,1)S(1)} collective-permute-done((bf16[512,256]{1,0:T(8,128)(2,1)S(1)}, bf16[512,256]{1,0:T(8,128)(2,1)S(1)}, u32[]{:S(2)}, u32[]{:S(2)}) %collective-permute-start.19) | collective-permute-done | bytes 262176 | tf_op jit(solution)/shard_map/ppermute | solution.py:397
  31.9 0.6 collective-permute-start.26
  32.5 1.7 collective-permute-done.26
  34.2 2.3 %collective-permute-start.20 = (bf16[1024,256]{1,0:T(8,128)(2,1)S(1)}, bf16[1024,256]{1,0:T(8,128)(2,1)S(1)}, u32[]{:S(2)}, u32[]{:S(2)}) collective-permute-start(bf16[1024,256]{1,0:T(8,128)(2,1)S(1)} %constant_dynamic-update-slice_fusion.refs_7_), channel_id=1, source_target_pairs={{2,6},{3,1},{6,10},{7,3},{10,14},{11,7},{14,12},{15,11},{12,8},{13... | collective-permute-start | bytes 1572872 | tf_op jit(solution)/shard_map/ppermute | solution.py:397
  36.5 1.6 collective-permute-start.7
  38.1 5.3 %collective-permute-done.20.refs_10_ = bf16[1024,256]{1,0:T(8,128)(2,1)S(1)} collective-permute-done((bf16[1024,256]{1,0:T(8,128)(2,1)S(1)}, bf16[1024,256]{1,0:T(8,128)(2,1)S(1)}, u32[]{:S(2)}, u32[]{:S(2)}) %collective-permute-start.20) | collective-permute-done | bytes 524320 | tf_op jit(solution)/shard_map/ppermute | solution.py:397
  43.4 2.3 %collective-permute-start.21 = (bf16[1024,256]{1,0:T(8,128)(2,1)S(1)}, bf16[1024,256]{1,0:T(8,128)(2,1)S(1)}, u32[]{:S(2)}, u32[]{:S(2)}) collective-permute-start(bf16[1024,256]{1,0:T(8,128)(2,1)S(1)} %collective-permute-done.20.refs_10_), channel_id=1, source_target_pairs={{2,6},{3,1},{6,10},{7,3},{10,14},{11,7},{14,12},{15,11},{12,8},{13... | collective-permute-start | bytes 1572872 | tf_op jit(solution)/shard_map/ppermute | solution.py:397
  45.6 0.8 copy-done.9
  46.4 1.3 collective-permute-start.2
  47.7 1.0 copy-done.7
  48.7 8.2 %collective-permute-done.21.refs_11_ = bf16[1024,256]{1,0:T(8,128)(2,1)S(1)} collective-permute-done((bf16[1024,256]{1,0:T(8,128)(2,1)S(1)}, bf16[1024,256]{1,0:T(8,128)(2,1)S(1)}, u32[]{:S(2)}, u32[]{:S(2)}) %collective-permute-start.21) | collective-permute-done | bytes 524320 | tf_op jit(solution)/shard_map/ppermute | solution.py:397
  56.9 1.7 collective-permute-start.10
  58.6 1.6 collective-permute-start.8
  60.2 0.7 slice.12
  61.0 0.8 copy-done.4
  61.8 1.5 collective-permute-done.2.refs_0_
  63.2 0.7 collective-permute-start.22
  63.9 1.6 collective-permute-start.14
  65.6 1.3 collective-permute-start.11
  66.8 0.7 dynamic-slice_bitcast_fusion.order_ref
  67.5 4.0 %copy-done = bf16[160,32768]{1,0:T(8,128)(2,1)S(1)} copy-done((bf16[160,32768]{1,0:T(8,128)(2,1)S(1)}, bf16[160,32768]{1,0:T(8,128)(2,1)}, u32[]{:S(2)}) %copy-start) | copy-done | bytes 10485784
  71.5 1.2 copy-done.6
  72.7 2.2 %stage.7.refs_1_ = f32[320,256]{1,0:T(8,128)S(1)} custom-call(s32[18]{0:T(128)S(1)} %dynamic-slice_bitcast_fusion.order_ref, bf16[160,32768]{1,0:T(8,128)(2,1)S(1)} %copy-done, bf16[160,32768]{1,0:T(8,128)(2,1)} %collective-permute-done.sib_ref, bf16[2048,256]{1,0:T(8,128)(2,1)S(1)} %copy-done.6), custom_call_target="tpu_custom_call" | custom-call | flops 335544320 | bytes 2686976 | tf_op jit(solution)/shard_map/stage/pallas_call | solution.py:59
  75.0 2.7 %stage.8.refs_1_ = f32[320,256]{1,0:T(8,128)S(1)} custom-call(s32[18]{0:T(128)S(1)} %dynamic-slice_bitcast_fusion.order_ref, bf16[160,32768]{1,0:T(8,128)(2,1)S(1)} %copy-done, bf16[160,32768]{1,0:T(8,128)(2,1)} %collective-permute-done.sib_ref, bf16[2048,256]{1,0:T(8,128)(2,1)} %collective-permute-done.3.refs_0_, f32[320,256]{1,0:T(8,128)S(1)} %stage.7.refs_1_), custom_call_target="tpu_custom_call" | custom-call | flops 335544320 | bytes 3014656 | tf_op jit(solution)/shard_map/stage/pallas_call | solution.py:59
  77.7 0.9 collective-permute-start.4
  78.6 0.7 collective-permute-start.9
  79.3 1.3 collective-permute-start.13
  80.7 0.0 slice-start
  80.7 1.0 inside.2.refs_13_
  81.7 1.6 copy-done.2
  83.3 2.5 %copy-done.3 = bf16[160,8192]{1,0:T(8,128)(2,1)S(1)} copy-done((bf16[160,8192]{1,0:T(8,128)(2,1)S(1)}, bf16[160,8192]{1,0:T(8,128)(2,1)}, u32[]{:S(2)}) %copy-start.3) | copy-done | bytes 2621464
  85.8 1.1 inside.3
  87.0 1.4 collective-permute-start.15
  88.4 6.5 %collective-permute-done.11.refs_2_ = bf16[2048,256]{1,0:T(8,128)(2,1)} collective-permute-done((bf16[2048,256]{1,0:T(8,128)(2,1)}, bf16[2048,256]{1,0:T(8,128)(2,1)}, u32[]{:S(2)}, u32[]{:S(2)}) %collective-permute-start.11) | collective-permute-done | bytes 1048608 | tf_op jit(solution)/shard_map/ppermute | solution.py:397
  94.9 3.2 %collective-permute-start.23 = (f32[320,256]{1,0:T(8,128)S(1)}, f32[320,256]{1,0:T(8,128)S(1)}, u32[]{:S(2)}, u32[]{:S(2)}) collective-permute-start(f32[320,256]{1,0:T(8,128)S(1)} %inside.3), channel_id=1, source_target_pairs={{0,1},{1,0},{2,3},{3,2},{4,5},{5,4},{6,7},{7,6},{8,9},{9,8},{10,11... | collective-permute-start | bytes 983048 | tf_op jit(solution)/shard_map/ppermute | solution.py:397
  98.1 1.8 %window.1 = bf16[320,2048]{1,0:T(8,128)(2,1)S(1)} custom-call(s32[18]{0:T(128)S(1)} %dynamic-slice_bitcast_fusion.order_ref, bf16[160,32768]{1,0:T(8,128)(2,1)S(1)} %bitcast.6, bf16[160,32768]{1,0:T(8,128)(2,1)} %collective-permute-done.sib_ref), custom_call_target="tpu_custom_call" | custom-call | bytes 2621440 | tf_op jit(solution)/shard_map/window/pallas_call | solution.py:59
  99.9 14.0 %collective-permute-start.24 = (bf16[320,2048]{1,0:T(8,128)(2,1)S(1)}, bf16[320,2048]{1,0:T(8,128)(2,1)S(1)}, u32[]{:S(2)}, u32[]{:S(2)}) collective-permute-start(bf16[320,2048]{1,0:T(8,128)(2,1)S(1)} %window.1), channel_id=1, source_target_pairs={{2,6},{3,7},{0,4},{1,5},{14,10},{15,11},{12,8},{13,9},{18,22},{19,... | collective-permute-start | bytes 3932168 | tf_op jit(solution)/shard_map/ppermute | solution.py:397
  113.9 0.1 pad_add_fusion.1.refs_8_
  114.0 2.2 %stage.9.refs_1_ = f32[320,256]{1,0:T(8,128)S(1)} custom-call(s32[18]{0:T(128)S(1)} %dynamic-slice_bitcast_fusion.order_ref, bf16[160,32768]{1,0:T(8,128)(2,1)S(1)} %bitcast.6, bf16[160,32768]{1,0:T(8,128)(2,1)} %collective-permute-done.sib_ref, bf16[2048,256]{1,0:T(8,128)(2,1)S(1)} %copy-done.8, f32[320,256]{1,0:T(8,128)S(1)} %stage.8.refs_1_), custom_call_target="tpu_custom_call" | custom-call | flops 335544320 | bytes 3014656 | tf_op jit(solution)/shard_map/stage/pallas_call | solution.py:59
  116.2 2.5 %stage.10.refs_3_ = f32[320,256]{1,0:T(8,128)S(1)} custom-call(s32[18]{0:T(128)S(1)} %dynamic-slice_bitcast_fusion.order_ref, bf16[160,32768]{1,0:T(8,128)(2,1)S(1)} %bitcast.6, bf16[160,32768]{1,0:T(8,128)(2,1)} %collective-permute-done.sib_ref, bf16[2048,256]{1,0:T(8,128)(2,1)} %collective-permute-done.2.refs_0_, f32[320,256]{1,0:T(8,128)S(1)} %stage.9.refs_1_), custom_call_target="tpu_custom_call" | custom-call | flops 335544320 | bytes 3014656 | tf_op jit(solution)/shard_map/stage/pallas_call | solution.py:59
  118.6 3.1 %stage.11.refs_3_ = f32[320,256]{1,0:T(8,128)S(1)} custom-call(s32[18]{0:T(128)S(1)} %dynamic-slice_bitcast_fusion.order_ref, bf16[160,32768]{1,0:T(8,128)(2,1)S(1)} %bitcast.6, bf16[160,32768]{1,0:T(8,128)(2,1)} %collective-permute-done.sib_ref, bf16[2048,256]{1,0:T(8,128)(2,1)} %collective-permute-done.7.refs_0_, ...), custom_call_target="tpu_custom_call" | custom-call | flops 335544320 | bytes 5111808 | tf_op jit(solution)/shard_map/stage/pallas_call | solution.py:59
  121.8 1.3 collective-permute-start.27
  123.1 17.5 %collective-permute-done.27.refs_9_ = s32[2,4]{1,0:T(2,128)S(1)} collective-permute-done((s32[2,4]{1,0:T(2,128)S(1)}, s32[2,4]{1,0:T(2,128)S(1)}, u32[]{:S(2)}, u32[]{:S(2)}) %collective-permute-start.27) | collective-permute-done | bytes 64 | tf_op jit(solution)/shard_map/ppermute | solution.py:397
  140.5 1.3 collective-permute-start.12
  141.8 0.7 collective-permute-start.5
  142.6 0.7 collective-permute-start.6
  143.4 5.1 %collective-permute-start.25 = (f32[320,256]{1,0:T(8,128)S(1)}, f32[320,256]{1,0:T(8,128)S(1)}, u32[]{:S(2)}, u32[]{:S(2)}) collective-permute-start(f32[320,256]{1,0:T(8,128)S(1)} %maximum_add_fusion.refs_5_), channel_id=1, source_target_pairs={{2,6},{3,7},{0,4},{1,5},{14,10},{15,11},{12,8},{13,9},{18,22},{19,... | collective-permute-start | bytes 983048 | tf_op jit(solution)/shard_map/ppermute | solution.py:397
  148.5 2.8 %stage.12.refs_3_ = f32[320,256]{1,0:T(8,128)S(1)} custom-call(s32[18]{0:T(128)S(1)} %dynamic-slice_bitcast_fusion.order_ref, bf16[160,32768]{1,0:T(8,128)(2,1)S(1)} %bitcast.6, bf16[160,32768]{1,0:T(8,128)(2,1)} %collective-permute-done.sib_ref, bf16[2048,256]{1,0:T(8,128)(2,1)} %collective-permute-done.8.refs_0_, ...), custom_call_target="tpu_custom_call" | custom-call | flops 335544320 | bytes 5111808 | tf_op jit(solution)/shard_map/stage/pallas_call | solution.py:59
  151.3 2.2 %stage.13.refs_4_ = f32[320,256]{1,0:T(8,128)S(1)} custom-call(s32[18]{0:T(128)S(1)} %dynamic-slice_bitcast_fusion.order_ref, bf16[160,32768]{1,0:T(8,128)(2,1)S(1)} %bitcast.6, bf16[160,32768]{1,0:T(8,128)(2,1)} %collective-permute-done.sib_ref, bf16[2048,256]{1,0:T(8,128)(2,1)S(1)} %collective-permute-done.4.refs_0_.refs_3_, ...), custom_call_target="tpu_custom_call" | custom-call | flops 335544320 | bytes 5111808 | tf_op jit(solution)/shard_map/stage/pallas_call | solution.py:59
  153.5 0.2 collective-permute-done.25.refs_7_
  153.7 3.5 %collective-permute-done.12.refs_2_ = bf16[2048,256]{1,0:T(8,128)(2,1)S(1)} collective-permute-done((bf16[2048,256]{1,0:T(8,128)(2,1)S(1)}, bf16[2048,256]{1,0:T(8,128)(2,1)S(1)}, u32[]{:S(2)}, u32[]{:S(2)}) %collective-permute-start.12) | collective-permute-done | bytes 1048608 | tf_op jit(solution)/shard_map/ppermute | solution.py:397
  157.2 2.8 %finish.1 = f32[32,8]{1,0:T(8,128)S(1)} custom-call(s32[18]{0:T(128)S(1)} %dynamic-slice_bitcast_fusion.order_ref, bf16[160,32768]{1,0:T(8,128)(2,1)S(1)} %bitcast.6, bf16[160,32768]{1,0:T(8,128)(2,1)} %collective-permute-done.sib_ref, bf16[2048,256]{1,0:T(8,128)(2,1)S(1)} %collective-permute-done.5.refs_0_, ...), custom_call_target="tpu_custom_call" | custom-call | flops 671088640 | bytes 7799808 | tf_op jit(solution)/shard_map/finish/pallas_call | solution.py:59
  160.0 13.5 %all_to_all.5 = f32[16,2,8]{2,1,0:T(2,128)S(1)} all-to-all(f32[16,2,8]{2,1,0:T(2,128)S(1)} %bitcast.7), channel_id=1, replica_groups=mesh['groups'=2,'dp'=16] {'dp'}, dimensions={0} | all-to-all | bytes 2048 | tf_op jit(solution)/shard_map/all_to_all | solution.py:446
  173.5 0.6 reduce_sum.9
  (48 shorter events, 0.2 us)
Async XLA Ops:
  0.0 65.5 %collective-permute-start = (bf16[160,32768]{1,0:T(8,128)(2,1)}, bf16[160,32768]{1,0:T(8,128)(2,1)}, u32[]{:S(2)}, u32[]{:S(2)}) collective-permute-start(bf16[160,32768]{1,0:T(8,128)(2,1)} %own_ref.17), channel_id=1, source_target_pairs={{0,1},{1,0},{2,3},{3,2},{4,5},{5,4},{6,7},{7,6},{8,9},{9,8},{10,11... | collective-permute-start | bytes 31457288 | tf_op jit(solution)/shard_map/ppermute | solution.py:397
  0.5 6.2 %collective-permute-start.18 = (bf16[512,256]{1,0:T(8,128)(2,1)}, bf16[512,256]{1,0:T(8,128)(2,1)S(1)}, u32[]{:S(2)}, u32[]{:S(2)}) collective-permute-start(bf16[512,256]{1,0:T(8,128)(2,1)} %refs_6_.2), channel_id=1, source_target_pairs={{0,1},{1,0},{2,3},{3,2},{4,5},{5,4},{6,7},{7,6},{8,9},{9,8},{10,11... | collective-permute-start | bytes 786440 | tf_op jit(solution)/shard_map/ppermute | solution.py:397
  0.5 35.9 %collective-permute-start.3 = (bf16[2048,256]{1,0:T(8,128)(2,1)}, bf16[2048,256]{1,0:T(8,128)(2,1)}, u32[]{:S(2)}, u32[]{:S(2)}) collective-permute-start(bf16[2048,256]{1,0:T(8,128)(2,1)} %refs_0_.3), channel_id=1, source_target_pairs={{6,10},{10,8},{8,4},{4,6},{11,7},{9,11},{5,9},{7,5},{2,0},{1,3},{1... | collective-permute-start | bytes 3145736 | tf_op jit(solution)/shard_map/ppermute | solution.py:397
  3.5 25.7 %collective-permute-start.17 = (bf16[512,256]{1,0:T(8,128)(2,1)}, bf16[512,256]{1,0:T(8,128)(2,1)S(1)}, u32[]{:S(2)}, u32[]{:S(2)}) collective-permute-start(bf16[512,256]{1,0:T(8,128)(2,1)} %refs_6_.2), channel_id=1, source_target_pairs={{2,6},{3,1},{6,10},{7,3},{10,14},{11,7},{14,12},{15,11},{12,8},{13... | collective-permute-start | bytes 786440 | tf_op jit(solution)/shard_map/ppermute | solution.py:397
  6.7 25.2 %collective-permute-start.19 = (bf16[512,256]{1,0:T(8,128)(2,1)S(1)}, bf16[512,256]{1,0:T(8,128)(2,1)S(1)}, u32[]{:S(2)}, u32[]{:S(2)}) collective-permute-start(bf16[512,256]{1,0:T(8,128)(2,1)S(1)} %collective-permute-done.18), channel_id=1, source_target_pairs={{2,6},{3,1},{6,10},{7,3},{10,14},{11,7},{14,12},{15,11},{12,8},{13... | collective-permute-start | bytes 786440 | tf_op jit(solution)/shard_map/ppermute | solution.py:397
  9.8 36.6 %collective-permute-start.1 = (bf16[2048,256]{1,0:T(8,128)(2,1)}, bf16[2048,256]{1,0:T(8,128)(2,1)S(1)}, u32[]{:S(2)}, u32[]{:S(2)}) collective-permute-start(bf16[2048,256]{1,0:T(8,128)(2,1)} %refs_0_.3), channel_id=1, source_target_pairs={{2,6},{3,7},{0,4},{1,5},{14,10},{15,11},{12,8},{13,9},{6,2},{5,1},... | collective-permute-start | bytes 3145736 | tf_op jit(solution)/shard_map/ppermute | solution.py:397
  29.2 50.1 %collective-permute-start.16 = (bf16[160,8192]{1,0:T(8,128)(2,1)}, bf16[160,8192]{1,0:T(8,128)(2,1)S(1)}, u32[]{:S(2)}, u32[]{:S(2)}) collective-permute-start(bf16[160,8192]{1,0:T(8,128)(2,1)} %refs_8_.1), channel_id=1, source_target_pairs={{0,1},{1,0},{2,3},{3,2},{4,5},{5,4},{6,7},{7,6},{8,9},{9,8},{10,11... | collective-permute-start | bytes 7864328 | tf_op jit(solution)/shard_map/ppermute | solution.py:397
  31.9 2.3 %collective-permute-start.26 = (s32[2,2]{1,0:T(2,128)S(1)}, s32[2,2]{1,0:T(2,128)S(1)}, u32[]{:S(2)}, u32[]{:S(2)}) collective-permute-start(s32[2,2]{1,0:T(2,128)S(1)} %pad_add_fusion), channel_id=1, source_target_pairs={{0,1},{1,0},{2,3},{3,2},{4,5},{5,4},{6,7},{7,6},{8,9},{9,8},{10,11... | collective-permute-start | bytes 56 | tf_op jit(solution)/shard_map/ppermute | solution.py:397
  34.2 9.2 %collective-permute-start.20 = (bf16[1024,256]{1,0:T(8,128)(2,1)S(1)}, bf16[1024,256]{1,0:T(8,128)(2,1)S(1)}, u32[]{:S(2)}, u32[]{:S(2)}) collective-permute-start(bf16[1024,256]{1,0:T(8,128)(2,1)S(1)} %constant_dynamic-update-slice_fusion.refs_7_), channel_id=1, source_target_pairs={{2,6},{3,1},{6,10},{7,3},{10,14},{11,7},{14,12},{15,11},{12,8},{13... | collective-permute-start | bytes 1572872 | tf_op jit(solution)/shard_map/ppermute | solution.py:397
  36.5 22.1 %collective-permute-start.7 = (bf16[2048,256]{1,0:T(8,128)(2,1)}, bf16[2048,256]{1,0:T(8,128)(2,1)}, u32[]{:S(2)}, u32[]{:S(2)}) collective-permute-start(bf16[2048,256]{1,0:T(8,128)(2,1)} %collective-permute-done.3.refs_0_), channel_id=1, source_target_pairs={{6,10},{10,8},{8,4},{4,6},{11,7},{9,11},{5,9},{7,5},{22,26},{26,24... | collective-permute-start | bytes 3145736 | tf_op jit(solution)/shard_map/ppermute | solution.py:397
  43.4 13.6 %collective-permute-start.21 = (bf16[1024,256]{1,0:T(8,128)(2,1)S(1)}, bf16[1024,256]{1,0:T(8,128)(2,1)S(1)}, u32[]{:S(2)}, u32[]{:S(2)}) collective-permute-start(bf16[1024,256]{1,0:T(8,128)(2,1)S(1)} %collective-permute-done.20.refs_10_), channel_id=1, source_target_pairs={{2,6},{3,1},{6,10},{7,3},{10,14},{11,7},{14,12},{15,11},{12,8},{13... | collective-permute-start | bytes 1572872 | tf_op jit(solution)/shard_map/ppermute | solution.py:397
  45.6 0.8 copy-start.9
  46.4 16.8 %collective-permute-start.2 = (bf16[2048,256]{1,0:T(8,128)(2,1)S(1)}, bf16[2048,256]{1,0:T(8,128)(2,1)}, u32[]{:S(2)}, u32[]{:S(2)}) collective-permute-start(bf16[2048,256]{1,0:T(8,128)(2,1)S(1)} %collective-permute-done.1.refs_0_), channel_id=1, source_target_pairs={{6,10},{10,8},{8,4},{4,6},{11,7},{9,11},{5,9},{7,5},{2,0},{1,3},{1... | collective-permute-start | bytes 3145736 | tf_op jit(solution)/shard_map/ppermute | solution.py:397
  47.7 1.0 copy-start.7
  56.9 7.0 %collective-permute-start.10 = (bf16[2048,256]{1,0:T(8,128)(2,1)}, bf16[2048,256]{1,0:T(8,128)(2,1)}, u32[]{:S(2)}, u32[]{:S(2)}) collective-permute-start(bf16[2048,256]{1,0:T(8,128)(2,1)} %collective-permute-done.3.refs_0_), channel_id=1, source_target_pairs={{6,2},{5,1},{11,15},{8,12},{22,18},{21,17},{27,31},{24,28}} | collective-permute-start | bytes 3145736 | tf_op jit(solution)/shard_map/ppermute | solution.py:397
  58.6 20.0 %collective-permute-start.8 = (bf16[2048,256]{1,0:T(8,128)(2,1)}, bf16[2048,256]{1,0:T(8,128)(2,1)}, u32[]{:S(2)}, u32[]{:S(2)}) collective-permute-start(bf16[2048,256]{1,0:T(8,128)(2,1)} %collective-permute-done.7.refs_0_), channel_id=1, source_target_pairs={{6,10},{10,8},{8,4},{4,6},{11,7},{9,11},{5,9},{7,5},{22,26},{26,24... | collective-permute-start | bytes 3145736 | tf_op jit(solution)/shard_map/ppermute | solution.py:397
  61.0 0.8 copy-start.4
  63.2 14.5 %collective-permute-start.22 = (bf16[512,256]{1,0:T(8,128)(2,1)}, bf16[512,256]{1,0:T(8,128)(2,1)S(1)}, u32[]{:S(2)}, u32[]{:S(2)}) collective-permute-start(bf16[512,256]{1,0:T(8,128)(2,1)} %slice.12), channel_id=1, source_target_pairs={{2,6},{3,1},{6,10},{7,3},{10,14},{11,7},{14,12},{15,11},{12,8},{13... | collective-permute-start | bytes 786440 | tf_op jit(solution)/shard_map/ppermute | solution.py:397
  63.9 23.1 %collective-permute-start.14 = (bf16[2048,256]{1,0:T(8,128)(2,1)}, bf16[2048,256]{1,0:T(8,128)(2,1)}, u32[]{:S(2)}, u32[]{:S(2)}) collective-permute-start(bf16[2048,256]{1,0:T(8,128)(2,1)} %collective-permute-done.7.refs_0_), channel_id=1, source_target_pairs={{6,2},{5,1},{11,15},{8,12},{22,18},{21,17},{27,31},{24,28}} | collective-permute-start | bytes 3145736 | tf_op jit(solution)/shard_map/ppermute | solution.py:397
  65.6 29.3 %collective-permute-start.11 = (bf16[2048,256]{1,0:T(8,128)(2,1)}, bf16[2048,256]{1,0:T(8,128)(2,1)}, u32[]{:S(2)}, u32[]{:S(2)}) collective-permute-start(bf16[2048,256]{1,0:T(8,128)(2,1)} %collective-permute-done.10.refs_1_), channel_id=1, source_target_pairs={{2,0},{1,3},{15,13},{12,14},{18,16},{17,19},{31,29},{28,30}} | collective-permute-start | bytes 3145736 | tf_op jit(solution)/shard_map/ppermute | solution.py:397
  67.5 4.0 %copy-start = (bf16[160,32768]{1,0:T(8,128)(2,1)S(1)}, bf16[160,32768]{1,0:T(8,128)(2,1)}, u32[]{:S(2)}) copy-start(bf16[160,32768]{1,0:T(8,128)(2,1)} %own_ref.17) | copy-start | bytes 31457284
  71.5 1.2 copy-start.6
  74.9 5.7 %copy-start.1 = (bf16[160,8192]{1,0:T(8,128)(2,1)S(1)}, bf16[160,8192]{1,0:T(8,128)(2,1)}, u32[]{:S(2)}) copy-start(bf16[160,8192]{1,0:T(8,128)(2,1)} %refs_8_.1) | copy-start | bytes 7864324
  74.9 5.7 %copy-start.11 = (bf16[512,256]{1,0:T(8,128)(2,1)S(1)}, bf16[512,256]{1,0:T(8,128)(2,1)}, u32[]{:S(2)}) copy-start(bf16[512,256]{1,0:T(8,128)(2,1)} %refs_6_.2) | copy-start | bytes 786436
  77.7 5.6 %copy-start.5 = (bf16[1024,256]{1,0:T(8,128)(2,1)S(1)}, bf16[1024,256]{1,0:T(8,128)(2,1)}, u32[]{:S(2)}) copy-start(bf16[1024,256]{1,0:T(8,128)(2,1)} %copy-done.4) | copy-start | bytes 1572868
  77.7 5.6 %copy-start.10 = (bf16[1024,256]{1,0:T(8,128)(2,1)S(1)}, bf16[1024,256]{1,0:T(8,128)(2,1)}, u32[]{:S(2)}) copy-start(bf16[1024,256]{1,0:T(8,128)(2,1)} %copy-done.9) | copy-start | bytes 1572868
  77.7 22.2 %collective-permute-start.4 = (bf16[2048,256]{1,0:T(8,128)(2,1)}, bf16[2048,256]{1,0:T(8,128)(2,1)S(1)}, u32[]{:S(2)}, u32[]{:S(2)}) collective-permute-start(bf16[2048,256]{1,0:T(8,128)(2,1)} %collective-permute-done.2.refs_0_), channel_id=1, source_target_pairs={{6,10},{10,8},{8,4},{4,6},{11,7},{9,11},{5,9},{7,5},{22,26},{26,24... | collective-permute-start | bytes 3145736 | tf_op jit(solution)/shard_map/ppermute | solution.py:397
  78.6 43.2 %collective-permute-start.9 = (bf16[2048,256]{1,0:T(8,128)(2,1)}, bf16[2048,256]{1,0:T(8,128)(2,1)S(1)}, u32[]{:S(2)}, u32[]{:S(2)}) collective-permute-start(bf16[2048,256]{1,0:T(8,128)(2,1)} %collective-permute-done.8.refs_0_), channel_id=1, source_target_pairs={{6,2},{5,1},{11,15},{8,12},{22,18},{21,17},{27,31},{24,28}} | collective-permute-start | bytes 3145736 | tf_op jit(solution)/shard_map/ppermute | solution.py:397
  79.3 63.2 %collective-permute-start.13 = (bf16[2048,256]{1,0:T(8,128)(2,1)}, bf16[2048,256]{1,0:T(8,128)(2,1)S(1)}, u32[]{:S(2)}, u32[]{:S(2)}) collective-permute-start(bf16[2048,256]{1,0:T(8,128)(2,1)} %collective-permute-done.2.refs_0_), channel_id=1, source_target_pairs={{7,3},{4,0},{10,14},{9,13},{23,19},{20,16},{26,30},{25,29}} | collective-permute-start | bytes 3145736 | tf_op jit(solution)/shard_map/ppermute | solution.py:397
  80.7 17.4 %slice-start = ((s8[10485760]{0:T(1024)(128)(4,1)}), s8[4194304]{0:T(1024)(128)(4,1)S(1)}, s32[]{:S(2)}) async-start(s8[10485760]{0:T(1024)(128)(4,1)} %bitcast.5), calls=%async_computation.1 | async-start | bytes 8388608
  80.7 17.4 %slice-start.1 = ((s8[10485760]{0:T(1024)(128)(4,1)}), s8[4194304]{0:T(1024)(128)(4,1)S(1)}, s32[]{:S(2)}) async-start(s8[10485760]{0:T(1024)(128)(4,1)} %bitcast.5), calls=%async_computation.2 | async-start | bytes 8388608
  81.7 1.6 copy-start.2
  83.3 2.5 %copy-start.3 = (bf16[160,8192]{1,0:T(8,128)(2,1)S(1)}, bf16[160,8192]{1,0:T(8,128)(2,1)}, u32[]{:S(2)}) copy-start(bf16[160,8192]{1,0:T(8,128)(2,1)} %copy-done.2) | copy-start | bytes 7864324
  85.8 12.3 %slice-start.2 = ((s8[10485760]{0:T(1024)(128)(4,1)}), s8[2097152]{0:T(1024)(128)(4,1)S(1)}, s32[]{:S(2)}) async-start(s8[10485760]{0:T(1024)(128)(4,1)} %bitcast.5), calls=%async_computation.3 | async-start | bytes 4194304
  86.9 26.9 %copy-start.12 = (s32[2]{0:T(128)S(1)}, s32[2]{0:T(128)}, u32[]{:S(2)}) copy-start(s32[2]{0:T(128)} %param.12) | copy-start | bytes 28
  86.9 26.9 %copy-start.13 = (s32[2]{0:T(128)S(1)}, s32[2]{0:T(128)}, u32[]{:S(2)}) copy-start(s32[2]{0:T(128)} %param.11) | copy-start | bytes 28
  87.0 27.0 %copy-start.8 = (bf16[2048,256]{1,0:T(8,128)(2,1)S(1)}, bf16[2048,256]{1,0:T(8,128)(2,1)}, u32[]{:S(2)}) copy-start(bf16[2048,256]{1,0:T(8,128)(2,1)} %copy-done.7) | copy-start | bytes 3145732
  87.0 56.4 %collective-permute-start.15 = (bf16[2048,256]{1,0:T(8,128)(2,1)}, bf16[2048,256]{1,0:T(8,128)(2,1)S(1)}, u32[]{:S(2)}, u32[]{:S(2)}) collective-permute-start(bf16[2048,256]{1,0:T(8,128)(2,1)} %collective-permute-done.14.refs_1_), channel_id=1, source_target_pairs={{2,0},{1,3},{15,13},{12,14},{18,16},{17,19},{31,29},{28,30}} | collective-permute-start | bytes 3145736 | tf_op jit(solution)/shard_map/ppermute | solution.py:397
  94.9 46.9 %collective-permute-start.23 = (f32[320,256]{1,0:T(8,128)S(1)}, f32[320,256]{1,0:T(8,128)S(1)}, u32[]{:S(2)}, u32[]{:S(2)}) collective-permute-start(f32[320,256]{1,0:T(8,128)S(1)} %inside.3), channel_id=1, source_target_pairs={{0,1},{1,0},{2,3},{3,2},{4,5},{5,4},{6,7},{7,6},{8,9},{9,8},{10,11... | collective-permute-start | bytes 983048 | tf_op jit(solution)/shard_map/ppermute | solution.py:397
  99.9 53.9 %collective-permute-start.24 = (bf16[320,2048]{1,0:T(8,128)(2,1)S(1)}, bf16[320,2048]{1,0:T(8,128)(2,1)S(1)}, u32[]{:S(2)}, u32[]{:S(2)}) collective-permute-start(bf16[320,2048]{1,0:T(8,128)(2,1)S(1)} %window.1), channel_id=1, source_target_pairs={{2,6},{3,7},{0,4},{1,5},{14,10},{15,11},{12,8},{13,9},{18,22},{19,... | collective-permute-start | bytes 3932168 | tf_op jit(solution)/shard_map/ppermute | solution.py:397
  121.8 18.8 %collective-permute-start.27 = (s32[2,4]{1,0:T(2,128)S(1)}, s32[2,4]{1,0:T(2,128)S(1)}, u32[]{:S(2)}, u32[]{:S(2)}) collective-permute-start(s32[2,4]{1,0:T(2,128)S(1)} %pad_add_fusion.1.refs_8_), channel_id=1, source_target_pairs={{2,6},{3,7},{0,4},{1,5},{14,10},{15,11},{12,8},{13,9},{18,22},{19,... | collective-permute-start | bytes 104 | tf_op jit(solution)/shard_map/ppermute | solution.py:397
  140.5 16.7 %collective-permute-start.12 = (bf16[2048,256]{1,0:T(8,128)(2,1)S(1)}, bf16[2048,256]{1,0:T(8,128)(2,1)S(1)}, u32[]{:S(2)}, u32[]{:S(2)}) collective-permute-start(bf16[2048,256]{1,0:T(8,128)(2,1)S(1)} %collective-permute-done.9.refs_1_), channel_id=1, source_target_pairs={{2,0},{1,3},{15,13},{12,14},{18,16},{17,19},{31,29},{28,30}} | collective-permute-start | bytes 3145736 | tf_op jit(solution)/shard_map/ppermute | solution.py:397
  141.8 15.4 %collective-permute-start.5 = (bf16[2048,256]{1,0:T(8,128)(2,1)S(1)}, bf16[2048,256]{1,0:T(8,128)(2,1)S(1)}, u32[]{:S(2)}, u32[]{:S(2)}) collective-permute-start(bf16[2048,256]{1,0:T(8,128)(2,1)S(1)} %collective-permute-done.4.refs_0_.refs_3_), channel_id=1, source_target_pairs={{6,10},{10,8},{8,4},{4,6},{11,7},{9,11},{5,9},{7,5},{22,26},{26,24... | collective-permute-start | bytes 3145736 | tf_op jit(solution)/shard_map/ppermute | solution.py:397
  142.6 14.6 %collective-permute-start.6 = (bf16[2048,256]{1,0:T(8,128)(2,1)S(1)}, bf16[2048,256]{1,0:T(8,128)(2,1)S(1)}, u32[]{:S(2)}, u32[]{:S(2)}) collective-permute-start(bf16[2048,256]{1,0:T(8,128)(2,1)S(1)} %collective-permute-done.4.refs_0_.refs_3_), channel_id=1, source_target_pairs={{6,2},{5,1},{11,15},{8,12},{22,18},{21,17},{27,31},{24,28}} | collective-permute-start | bytes 3145736 | tf_op jit(solution)/shard_map/ppermute | solution.py:397
  143.4 10.3 %collective-permute-start.25 = (f32[320,256]{1,0:T(8,128)S(1)}, f32[320,256]{1,0:T(8,128)S(1)}, u32[]{:S(2)}, u32[]{:S(2)}) collective-permute-start(f32[320,256]{1,0:T(8,128)S(1)} %maximum_add_fusion.refs_5_), channel_id=1, source_target_pairs={{2,6},{3,7},{0,4},{1,5},{14,10},{15,11},{12,8},{13,9},{18,22},{19,... | collective-permute-start | bytes 983048 | tf_op jit(solution)/shard_map/ppermute | solution.py:397

commit v4 on v3

--- a/solution.py
+++ b/solution.py
@@ -12,7 +12,7 @@
 RANK = 32
 LEN = 80
 F32 = jnp.float32
-VMEM = 26 << 20
+VMEM = 56 << 20
 
 
 def ring_of(chips):
@@ -213,11 +213,9 @@
         self.feed = feed
         self.other = [(at(m, 1 - LANE[q]), at(q, 1 - LANE[q])) for q, m in MIDDLE.items()]
         self.relay = [(at(q, LANE[q]), at(n, LANE[q])) for q, n in ACROSS.items()]
-        cross = [(at(q, 1 - LANE[q]), at(n, 1 - LANE[q])) for q, n in ACROSS.items()]
+        self.cross = [(at(q, 1 - LANE[q]), at(n, 1 - LANE[q])) for q, n in ACROSS.items()]
         self.inward = [(at(q, c), at(m, c)) for q, m in MIDDLE.items() for c in (0, 1)]
-        self.first = self.inner + self.relay + cross
-        self.second = self.inward + feed
-        self.third = self.inner + self.relay
+        self.first = self.inner + self.relay
 
         def sent(ids, pairs):
             got = np.full(16, -1)
@@ -233,16 +231,7 @@
         skipped = np.zeros(16, int)
         for q, m in self.inward:
             skipped[q] = (last[0] if m in late else early)[m]
-        places = [ring.index(d // 2) for d in range(16)]
-        own_in = []
-        for d in range(16):
-            core = d % 2
-            turn = -1 if core == 0 else 1
-            row = [d]
-            for k in (1, 2, 3):
-                chip = ring[(places[d] + turn * k) % 8]
-                row += [2 * chip + core, 2 * chip + 1 - core]
-            own_in.append(row + [2 * ring[(places[d] + 4) % 8] + core])
+        own_in = [[(e - 4 * k) % 16 for e in (d, d ^ 2) for k in range(4)] for d in range(16)]
         flag = np.array([d in late for d in range(16)], int)
         for d in range(16):
             blocks = sorted(x for x in table[d] if x >= 0)
@@ -255,29 +244,36 @@
             [table, skipped[:, None], flag[:, None], np.array(own_in)], axis=1
         ).astype(np.int32)
 
-    def flow(self, own, send, sums=lambda *arrays: None, tie=lambda x: x):
+    def flow(self, own, send, sums=lambda *arrays: None, tie=lambda level, *x: x):
         m0 = send(own, self.first)
-        m1 = send(own, self.second)
+        z0 = send(own, self.feed)
+        c = send(own, self.inward)
+        (m0,) = tie(1, m0)
         r1 = send(m0, self.inner)
         z1 = send(m0, self.feed)
-        m2 = send(m1, self.third)
-        r3 = send(r1, self.inner)
+        y1 = send(z0, self.relay)
+        r2 = send(c, self.inner)
         z2 = send(r1, self.feed)
         y2 = send(z1, self.relay)
         sums(own)
-        sums(m0)
-        r4 = send(tie(m2), self.inner)
-        w = send(m2, self.other)
+        sums(m0, z0)
+        r1, r2, z2 = tie(3, r1, r2, z2)
+        r3 = send(r1, self.inner)
+        w = send(r2, self.other)
         y3 = send(z2, self.relay)
+        sums(c, y1, z1)
+        sums(r1, y2, z2)
+        r2, r3, own = tie(4, r2, r3, own)
+        r4 = send(r2, self.inner)
         z4 = send(r3, self.feed)
-        sums(m1)
-        sums(m2)
-        r5 = send(tie(r4), self.inner)
+        u = send(own, self.cross)
+        sums(r2, w)
+        r4, z4 = tie(5, r4, z4)
+        r5 = send(r4, self.inner)
         z5 = send(r4, self.feed)
-        sums(r1, z1, y2)
-        y5 = send(tie(z4), self.relay)
-        sums(r3, z2, y3)
-        sums(r4, z4, w)
+        y5 = send(z4, self.relay)
+        sums(r3, y3, z4)
+        sums(r4, u)
         return (r5, z5, y5), r4
 
 
@@ -312,11 +308,13 @@
     )[0]
 
 
+EXTRA = 8
+
+
 def inside_kernel(sizes, summed, order_ref, *refs):
     windows, refs = refs[:2 * sum(sizes)], refs[2 * sum(sizes):]
     blocks, refs = refs[:len(sizes)], refs[len(sizes):]
-    tokens = windows[0].shape[0]
-    rows = windows[0].shape[1]
+    tokens, rows = windows[0].shape
     for k in range(2):
         at = pl.ds(k * tokens, tokens)
         new = refs[0][at] if summed else 0.0
@@ -326,21 +324,52 @@
                 new += dot(windows[2 * w + k][...], block[i * rows:(i + 1) * rows])
                 w += 1
         refs[-1][at] = new
-
-
-def inside(order, pair, rows, arrays, total, first):
+    if summed:
+        seq_ref, len_ref = refs[1:3]
+        held = seq_ref.shape[0]
+        lane = lax.broadcasted_iota(jnp.int32, (EXTRA, refs[-1].shape[1]), 1)
+        numbers = jnp.zeros(lane.shape, F32)
+        for i in range(held):
+            numbers = jnp.where(lane == i, seq_ref[i].astype(F32), numbers)
+            numbers = jnp.where(lane == held + i, len_ref[i].astype(F32), numbers)
+        refs[-1][2 * tokens:] = numbers
+
+
+def inside(order, pair, rows, arrays, total, first, slots):
     tokens, columns = pair[0].shape[0], arrays[0].shape[1]
     sizes = [x.shape[0] // rows for x in arrays]
     windows = []
     for w in range(sum(sizes)):
         pick = functools.partial(lambda i, o, col: (0, o[col]), col=first + w)
         windows += [(x, rows, pick) for x in pair]
+    height = 2 * tokens + (0 if total is None else EXTRA)
     return call(
         functools.partial(inside_kernel, sizes, total is not None),
-        order, windows, list(arrays) + ([] if total is None else [total]), [],
-        [jax.ShapeDtypeStruct((2 * tokens, columns), F32)],
+        order, windows, list(arrays) + ([] if total is None else [total]), slots,
+        [jax.ShapeDtypeStruct((height, columns), F32)],
         4 * tokens * rows * sum(sizes) * columns, "inside",
     )[0]
+
+
+def masked_kernel(order_ref, own_ref, got_ref, out_ref):
+    tokens = (own_ref.shape[0] - EXTRA) // 2
+    columns = own_ref.shape[1]
+    held = tokens // LEN
+    position = lax.broadcasted_iota(jnp.int32, (LEN, columns), 0).astype(F32)
+    for k, (mine, other) in enumerate(((own_ref, got_ref), (got_ref, own_ref))):
+        for i in range(held):
+            at, across = pl.ds(i * LEN, LEN), pl.ds(tokens + i * LEN, LEN)
+            length = mine[2 * tokens:2 * tokens + 1, held + i:held + i + 1]
+            out_ref[pl.ds(k * tokens + i * LEN, LEN)] = jnp.where(
+                position < length, mine[at] + other[across], 0.0
+            )
+    lane = lax.broadcasted_iota(jnp.int32, (EXTRA, columns), 1)
+    numbers = jnp.zeros(lane.shape, F32)
+    for k, ref in enumerate((own_ref, got_ref)):
+        for i in range(held):
+            slot = ref[2 * tokens:2 * tokens + 1, i:i + 1]
+            numbers = jnp.where(lane == k * held + i, slot, numbers)
+    out_ref[2 * tokens:] = numbers
 
 
 def window_kernel(order_ref, own_ref, sib_ref, out_ref):
@@ -351,33 +380,30 @@
 
 def finish_kernel(count, order_ref, own_ref, sib_ref, *refs):
     arrays, refs = refs[:count], refs[count:]
-    early_ref, total_ref, inn_ref, job_ref, job_inn_ref, slots_ref, job_slots_ref, table_ref = refs
+    early_ref, total_ref, inn_ref, job_ref, job_inn_ref, table_ref = refs
     tokens, columns = own_ref.shape[0], total_ref.shape[1]
     queries = columns // RANK
+    held = tokens // LEN
     column = lax.broadcasted_iota(jnp.int32, (columns, queries), 0) // RANK
     query = lax.broadcasted_iota(jnp.int32, (columns, queries), 1)
     fold = (column == query).astype(F32)
-    position = lax.broadcasted_iota(jnp.int32, (LEN, columns), 0)
-    row = lax.broadcasted_iota(jnp.int32, table_ref.shape, 0)
+    row = lax.broadcasted_iota(jnp.int32, table_ref.shape, 0).astype(F32)
     late = jnp.full(early_ref.shape, order_ref[LATE], jnp.int32) == 1
     block = joined(arrays)
     skipped = jnp.where(late, arrays[0][...], early_ref[...])
     sums, slots = [], []
     parts = [
-        (total_ref[:tokens] + dot(own_ref[...], block), inn_ref[:tokens], slots_ref, 0),
-        (total_ref[tokens:] + dot(sib_ref[...], block), inn_ref[tokens:], slots_ref, 1),
-        (dot(job_ref[:tokens], skipped), job_inn_ref[:tokens], job_slots_ref, 0),
-        (dot(job_ref[tokens:], skipped), job_inn_ref[tokens:], job_slots_ref, 1),
+        (total_ref[:tokens] + dot(own_ref[...], block), inn_ref, 0),
+        (total_ref[tokens:] + dot(sib_ref[...], block), inn_ref, 1),
+        (dot(job_ref[:tokens], skipped), job_inn_ref, 0),
+        (dot(job_ref[tokens:], skipped), job_inn_ref, 1),
     ]
-    held = tokens // LEN
-    for out, inn, ids, k in parts:
-        contrib = out * inn
+    for out, inn, k in parts:
+        contrib = out * inn[k * tokens:(k + 1) * tokens]
         for i in range(held):
-            kept = jnp.where(
-                position < ids[1, k * held + i], contrib[i * LEN:(i + 1) * LEN], 0.0
-            )
-            sums.append(jnp.sum(kept, axis=0, keepdims=True))
-            slots.append(ids[0, k * held + i])
+            sums.append(jnp.sum(contrib[i * LEN:(i + 1) * LEN], axis=0, keepdims=True))
+            at = k * held + i
+            slots.append(inn[2 * tokens:2 * tokens + 1, at:at + 1])
     scores = jnp.dot(
         jnp.concatenate(sums), fold, precision=lax.Precision.HIGHEST, preferred_element_type=F32
     ) * (1.0 / math.sqrt(RANK * LEN))
@@ -396,42 +422,41 @@
     order = lax.dynamic_index_in_dim(jnp.asarray(grid.table), lax.axis_index("dp"), keepdims=False)
     send = lambda x, pairs: lax.ppermute(x, "dp", pairs)
     swap = lambda x: send(x, [(d, d ^ 1) for d in range(devices)])
-    around = ring_pairs(devices // 2)
-
-    in_hops = [in_factors]
-    hop = jnp.concatenate([send(in_factors, around), send(swap(in_factors), around)])
-    for k in range(2):
-        in_hops.append(hop)
-        hop = send(hop, around)
-    in_hops += [hop, send(hop[:rows_in], around)]
-
+
+    across = [(d, d ^ 2) for d in range(devices)]
+    column, beside = [in_factors], [send(in_factors, across)]
+    for k in range(1, 4):
+        column.append(send(in_factors, [(d, (d + 4 * k) % devices) for d in range(devices)]))
+        beside.append(send(column[k], across))
+    pair_in = (acts, swap(acts))
     pair = (grads, swap(grads))
-    pair_in = (acts, swap(acts))
-    slots = jnp.stack([seq_slot, lengths])
-    slots = jnp.concatenate([slots, swap(slots)], axis=1)
-    job_slots = send(slots, grid.inward)
-
-    totals = [None]
-
-    def sums(*arrays):
-        totals.append(stage(order, pair, arrays, totals[-1], len(totals) - 1))
-
-    def tie(x):
-        x, totals[-1] = lax.optimization_barrier((x, totals[-1]))
-        return x
-
-    last, early = grid.flow(out_factors, send, sums, tie)
-
     job = call(
         window_kernel, order, [(x, rows, lambda i, o: (0, o[SKIPPED])) for x in pair], [], [],
         [jax.ShapeDtypeStruct((2 * tokens, rows), grads.dtype)], 0, "window",
     )[0]
+    inn = inside(order, pair_in, rows_in, column, None, OWN_IN, [])
+    half_inn = inn
+    inn = inside(order, pair_in, rows_in, beside, inn, OWN_IN + 4, [seq_slot, lengths])
+    inn = call(
+        masked_kernel, order, [], [inn, swap(inn)], [],
+        [jax.ShapeDtypeStruct(inn.shape, F32)], 0, "masked",
+    )[0]
+
+    totals = [None]
+    aside = {1: column[1:], 3: beside + [job], 4: [half_inn], 5: [inn]}
+
+    def sums(*arrays):
+        totals.append(stage(order, pair, arrays, totals[-1], len(totals) - 1))
+
+    def tie(level, *x):
+        keep = [t for t in totals[-1:] if t is not None]
+        out = lax.optimization_barrier((*x, *keep, *aside.get(level, [])))
+        if keep:
+            totals[-1] = out[len(x)]
+        return out[:len(x)]
+
+    last, early = grid.flow(out_factors, send, sums, tie)
     job = send(job, grid.inward)
-
-    inn = inside(order, pair_in, rows_in, in_hops[:2], None, OWN_IN)
-    inn = inside(order, pair_in, rows_in, in_hops[2:], inn, OWN_IN + 3)
-    got = swap(inn)
-    inn = inn + jnp.concatenate([got[tokens:], got[:tokens]])
     job_inn = send(inn, grid.inward)
 
     queries = columns // RANK
@@ -439,7 +464,7 @@
     table = call(
         functools.partial(finish_kernel, len(last)), order,
         [(x, rows, lambda i, o: (0, o[7])) for x in pair],
-        list(last) + [early, totals[-1], inn, job, job_inn], [slots, job_slots],
+        list(last) + [early, totals[-1], inn, job, job_inn], [],
         [jax.ShapeDtypeStruct((held * devices, queries), F32)],
         8 * tokens * rows * columns, "finish",
     )[0]

time: 175 us -> 211 us (1.21)
  Pallas kernels: 24.3 us -> 46.7 us
  waiting for transfers between devices: 66.4 us -> 86.2 us
  local copies, waits for them, and re-layouts: 13.4 us -> 6.61 us
  starting transfers between devices: 54.6 us -> 57.4 us
    pallas_call x11 -> x12, Pallas kernels: 24.3 us -> 46.7 us  [call(): pl.pallas_call(kernel, grid_spec=pltpu.PrefetchScalarGridSpec(num_scalar_...]
    ppermute x28 -> x30, waiting for transfers between devices: 66.4 us -> 86.2 us  [grid_shards(): send = lambda x, pairs: lax.ppermute(x, 'dp', pairs)]
    unnamed x35 -> x40, local copies, waits for them, and re-layouts: 12 us -> 5.41 us
    ppermute x28 -> x30, starting transfers between devices: 54.6 us -> 57.4 us  [grid_shards(): send = lambda x, pairs: lax.ppermute(x, 'dp', pairs)]
  transfers between devices with their start and end apart: 28 -> 30, of which waited for: 11 -> 11; matrix products, arithmetic and copies ran while one was open for 1% -> 1% of each run, Pallas kernels for 12% -> 20%
where the time goes in v4:
time: 211 us; the launch traced here: 210 us
  waiting for transfers between devices  86.2 us (41%)
  starting transfers between devices  57.4 us (27%)
  Pallas kernels  46.7 us (22%)
  blocking collectives  12.4 us (6%)
  local copies, waits for them, and re-layouts  6.61 us (3%)
    ppermute x30, waiting for transfers between devices, grid_shards(): send = lambda x, pairs: lax.ppermute(x, 'dp', pairs)  86.2 us
    ppermute x30, starting transfers between devices, grid_shards(): send = lambda x, pairs: lax.ppermute(x, 'dp', pairs)  57.4 us
    pallas_call x12, Pallas kernels, call(): pl.pallas_call(kernel, grid_spec=pltpu.PrefetchScalarGridSpec(num_scalar_...  46.7 us
    all_to_all x1, blocking collectives, grid_shards(): lax.all_to_all(table.reshape(devices, held, queries), 'dp', 0, 0, tiled=T...  12.4 us
    unnamed x40, local copies, waits for them, and re-layouts  5.41 us
  transfers between devices with their start and end apart: 30, of which 11 were waited for; matrix products, arithmetic and copies ran while one was open for 1% of the time, Pallas kernels for 20%

profile of v4, /device:TPU:0, one launch (start us, length us, event | category | flops | bytes accessed | tf_op | source)
XLA Modules:
  0.0 210.2 jit_solution(8366965841636084896)
XLA Ops:
  0.0 0.5 collective-permute-start
  0.5 1.3 collective-permute-start.1
  1.7 4.8 %collective-permute-start.2 = (bf16[512,256]{1,0:T(8,128)(2,1)}, bf16[512,256]{1,0:T(8,128)(2,1)S(1)}, u32[]{:S(2)}, u32[]{:S(2)}) collective-permute-start(bf16[512,256]{1,0:T(8,128)(2,1)} %refs_8_.1), channel_id=1, source_target_pairs={{0,4},{1,5},{2,6},{3,7},{4,8},{5,9},{6,10},{7,11},{8,12},{9,13},{1... | collective-permute-start | bytes 786440 | tf_op jit(solution)/shard_map/ppermute | solution.py:423
  6.5 3.5 %collective-permute-start.3 = (bf16[512,256]{1,0:T(8,128)(2,1)}, bf16[512,256]{1,0:T(8,128)(2,1)S(1)}, u32[]{:S(2)}, u32[]{:S(2)}) collective-permute-start(bf16[512,256]{1,0:T(8,128)(2,1)} %refs_8_.1), channel_id=1, source_target_pairs={{0,8},{1,9},{2,10},{3,11},{4,12},{5,13},{6,14},{7,15},{8,0},{9,1},... | collective-permute-start | bytes 786440 | tf_op jit(solution)/shard_map/ppermute | solution.py:423
  10.0 0.0 collective-permute-start.4
  10.0 6.9 %collective-permute-done.2.refs_9_ = bf16[512,256]{1,0:T(8,128)(2,1)S(1)} collective-permute-done((bf16[512,256]{1,0:T(8,128)(2,1)}, bf16[512,256]{1,0:T(8,128)(2,1)S(1)}, u32[]{:S(2)}, u32[]{:S(2)}) %collective-permute-start.2) | collective-permute-done | bytes 262176 | tf_op jit(solution)/shard_map/ppermute | solution.py:423
  16.9 2.3 %collective-permute-start.6 = (bf16[2048,256]{1,0:T(8,128)(2,1)}, bf16[2048,256]{1,0:T(8,128)(2,1)}, u32[]{:S(2)}, u32[]{:S(2)}) collective-permute-start(bf16[2048,256]{1,0:T(8,128)(2,1)} %refs_0_.3), channel_id=1, source_target_pairs={{2,6},{3,7},{0,4},{1,5},{14,10},{15,11},{12,8},{13,9},{18,22},{19,... | collective-permute-start | bytes 3145736 | tf_op jit(solution)/shard_map/ppermute | solution.py:423
  19.2 19.9 %collective-permute-done.3.refs_10_ = bf16[512,256]{1,0:T(8,128)(2,1)S(1)} collective-permute-done((bf16[512,256]{1,0:T(8,128)(2,1)}, bf16[512,256]{1,0:T(8,128)(2,1)S(1)}, u32[]{:S(2)}, u32[]{:S(2)}) %collective-permute-start.3) | collective-permute-done | bytes 262176 | tf_op jit(solution)/shard_map/ppermute | solution.py:423
  39.1 1.7 collective-permute-start.5
  40.7 3.9 %collective-permute-start.10 = (bf16[512,256]{1,0:T(8,128)(2,1)}, bf16[512,256]{1,0:T(8,128)(2,1)S(1)}, u32[]{:S(2)}, u32[]{:S(2)}) collective-permute-start(bf16[512,256]{1,0:T(8,128)(2,1)} %refs_8_.1), channel_id=1, source_target_pairs={{0,2},{1,3},{2,0},{3,1},{4,6},{5,7},{6,4},{7,5},{8,10},{9,11},{10,... | collective-permute-start | bytes 786440 | tf_op jit(solution)/shard_map/ppermute | solution.py:423
  44.7 0.0 collective-permute-start.11
  44.7 7.3 %collective-permute-done.10.refs_8_ = bf16[512,256]{1,0:T(8,128)(2,1)S(1)} collective-permute-done((bf16[512,256]{1,0:T(8,128)(2,1)}, bf16[512,256]{1,0:T(8,128)(2,1)S(1)}, u32[]{:S(2)}, u32[]{:S(2)}) %collective-permute-start.10) | collective-permute-done | bytes 262176 | tf_op jit(solution)/shard_map/ppermute | solution.py:423
  52.0 4.8 %collective-permute-done.11.refs_9_ = bf16[512,256]{1,0:T(8,128)(2,1)S(1)} collective-permute-done((bf16[512,256]{1,0:T(8,128)(2,1)S(1)}, bf16[512,256]{1,0:T(8,128)(2,1)S(1)}, u32[]{:S(2)}, u32[]{:S(2)}) %collective-permute-start.11) | collective-permute-done | bytes 262176 | tf_op jit(solution)/shard_map/ppermute | solution.py:423
  56.8 0.3 collective-permute-start.12
  57.1 7.2 %collective-permute-done.12.refs_10_ = bf16[512,256]{1,0:T(8,128)(2,1)S(1)} collective-permute-done((bf16[512,256]{1,0:T(8,128)(2,1)S(1)}, bf16[512,256]{1,0:T(8,128)(2,1)S(1)}, u32[]{:S(2)}, u32[]{:S(2)}) %collective-permute-start.12) | collective-permute-done | bytes 262176 | tf_op jit(solution)/shard_map/ppermute | solution.py:423
  64.3 0.3 collective-permute-start.13
  64.5 6.3 %collective-permute-done.13.refs_11_ = bf16[512,256]{1,0:T(8,128)(2,1)S(1)} collective-permute-done((bf16[512,256]{1,0:T(8,128)(2,1)S(1)}, bf16[512,256]{1,0:T(8,128)(2,1)S(1)}, u32[]{:S(2)}, u32[]{:S(2)}) %collective-permute-start.13) | collective-permute-done | bytes 262176 | tf_op jit(solution)/shard_map/ppermute | solution.py:423
  70.8 1.7 collective-permute-start.9
  72.5 1.7 collective-permute-start.15
  74.2 1.7 collective-permute-start.7
  75.9 0.0 collective-permute-done.sib_ref
  75.9 1.6 collective-permute-start.8
  77.5 1.2 dynamic-slice_bitcast_fusion.order_ref
  78.7 3.1 %window.1 = bf16[320,2048]{1,0:T(8,128)(2,1)} custom-call(s32[18]{0:T(128)} %dynamic-slice_bitcast_fusion.order_ref, bf16[160,32768]{1,0:T(8,128)(2,1)} %own_ref.17, bf16[160,32768]{1,0:T(8,128)(2,1)} %collective-permute-done.sib_ref), custom_call_target="tpu_custom_call" | custom-call | bytes 2621440 | tf_op jit(solution)/shard_map/window/pallas_call | solution.py:59
  81.9 0.0 collective-permute-done.9.refs_1_
  81.9 1.3 collective-permute-start.17
  83.2 3.5 %stage.7.refs_2_ = f32[320,256]{1,0:T(8,128)} custom-call(s32[18]{0:T(128)} %dynamic-slice_bitcast_fusion.order_ref, bf16[160,32768]{1,0:T(8,128)(2,1)} %own_ref.17, bf16[160,32768]{1,0:T(8,128)(2,1)} %collective-permute-done.sib_ref, bf16[2048,256]{1,0:T(8,128)(2,1)} %refs_0_.3), custom_call_target="tpu_custom_call" | custom-call | flops 335544320 | bytes 2686976 | tf_op jit(solution)/shard_map/stage/pallas_call | solution.py:59
  86.7 1.3 collective-permute-start.16
  88.0 4.0 %stage.8.refs_3_ = f32[320,256]{1,0:T(8,128)} custom-call(s32[18]{0:T(128)} %dynamic-slice_bitcast_fusion.order_ref, bf16[160,32768]{1,0:T(8,128)(2,1)} %own_ref.17, bf16[160,32768]{1,0:T(8,128)(2,1)} %collective-permute-done.sib_ref, bf16[2048,256]{1,0:T(8,128)(2,1)} %collective-permute-done.1.refs_0_, bf16[2048,256]{1,0:T(8,128)(2,1)} %collective-permute-done.9.refs_1_, ...), custom_call_target="tpu_custom_call" | custom-call | flops 335544320 | bytes 4063232 | tf_op jit(solution)/shard_map/stage/pallas_call | solution.py:59
  92.0 1.6 collective-permute-start.14
  93.6 1.3 collective-permute-start.21
  94.9 1.5 copy-done
  96.4 3.6 %inside.2.refs_12_ = f32[320,256]{1,0:T(8,128)} custom-call(s32[18]{0:T(128)} %dynamic-slice_bitcast_fusion.order_ref, bf16[160,8192]{1,0:T(8,128)(2,1)} %refs_6_.3, bf16[160,8192]{1,0:T(8,128)(2,1)} %copy-done, bf16[160,8192]{1,0:T(8,128)(2,1)} %refs_6_.3, bf16[160,8192]{1,0:T(8,128)(2,1)} %copy-done, bf16[160,8192]{1,0:T(8,128)(2,1)} %refs_6_.3, ...), custom_call_target="tpu_custom_call" | custom-call | flops 335544320 | bytes 2686976 | tf_op jit(solution)/shard_map/inside/pallas_call | solution.py:59
  100.1 12.9 %collective-permute-done.17.refs_1_ = bf16[2048,256]{1,0:T(8,128)(2,1)S(1)} collective-permute-done((bf16[2048,256]{1,0:T(8,128)(2,1)}, bf16[2048,256]{1,0:T(8,128)(2,1)S(1)}, u32[]{:S(2)}, u32[]{:S(2)}) %collective-permute-start.17) | collective-permute-done | bytes 1048608 | tf_op jit(solution)/shard_map/ppermute | solution.py:423
  113.0 1.1 copy-done.9
  114.1 4.2 %stage.9.refs_3_ = f32[320,256]{1,0:T(8,128)} custom-call(s32[18]{0:T(128)} %dynamic-slice_bitcast_fusion.order_ref, bf16[160,32768]{1,0:T(8,128)(2,1)} %own_ref.17, bf16[160,32768]{1,0:T(8,128)(2,1)} %collective-permute-done.sib_ref, bf16[2048,256]{1,0:T(8,128)(2,1)} %collective-permute-done.6.refs_0_, bf16[2048,256]{1,0:T(8,128)(2,1)} %copy-done.9, ...), custom_call_target="tpu_custom_call" | custom-call | flops 335544320 | bytes 5111808 | tf_op jit(solution)/shard_map/stage/pallas_call | solution.py:59
  118.3 6.0 %collective-permute-done.16.refs_1_ = bf16[2048,256]{1,0:T(8,128)(2,1)S(1)} collective-permute-done((bf16[2048,256]{1,0:T(8,128)(2,1)}, bf16[2048,256]{1,0:T(8,128)(2,1)S(1)}, u32[]{:S(2)}, u32[]{:S(2)}) %collective-permute-start.16) | collective-permute-done | bytes 1048608 | tf_op jit(solution)/shard_map/ppermute | solution.py:423
  124.2 1.0 copy-done.10
  125.2 4.2 %stage.10.refs_2_ = f32[320,256]{1,0:T(8,128)} custom-call(s32[18]{0:T(128)} %dynamic-slice_bitcast_fusion.order_ref, bf16[160,32768]{1,0:T(8,128)(2,1)} %own_ref.17, bf16[160,32768]{1,0:T(8,128)(2,1)} %collective-permute-done.sib_ref, bf16[2048,256]{1,0:T(8,128)(2,1)} %collective-permute-done.5.refs_0_, bf16[2048,256]{1,0:T(8,128)(2,1)} %copy-done.10, ...), custom_call_target="tpu_custom_call" | custom-call | flops 335544320 | bytes 5111808 | tf_op jit(solution)/shard_map/stage/pallas_call | solution.py:59
  129.5 0.9 collective-permute-start.19
  130.3 1.7 collective-permute-start.20
  132.0 1.3 collective-permute-start.27
  133.3 3.8 %inside.3.own_ref = f32[328,256]{1,0:T(8,128)} custom-call(s32[18]{0:T(128)} %dynamic-slice_bitcast_fusion.order_ref, bf16[160,8192]{1,0:T(8,128)(2,1)} %refs_6_.3, bf16[160,8192]{1,0:T(8,128)(2,1)} %copy-done, bf16[160,8192]{1,0:T(8,128)(2,1)} %refs_6_.3, bf16[160,8192]{1,0:T(8,128)(2,1)} %copy-done, bf16[160,8192]{1,0:T(8,128)(2,1)} %refs_6_.3, ...), custom_call_target="tpu_custom_call" | custom-call | flops 335544320 | bytes 3022848 | tf_op jit(solution)/shard_map/inside/pallas_call | solution.py:59
  137.0 8.6 %collective-permute-start.22 = (f32[328,256]{1,0:T(8,128)}, f32[328,256]{1,0:T(8,128)S(1)}, u32[]{:S(2)}, u32[]{:S(2)}) collective-permute-start(f32[328,256]{1,0:T(8,128)} %inside.3.own_ref), channel_id=1, source_target_pairs={{0,1},{1,0},{2,3},{3,2},{4,5},{5,4},{6,7},{7,6},{8,9},{9,8},{10,11... | collective-permute-start | bytes 1007624 | tf_op jit(solution)/shard_map/ppermute | solution.py:423
  145.7 1.5 collective-permute-done.22.got_ref
  147.2 5.1 %collective-permute-start.26 = (bf16[2048,256]{1,0:T(8,128)(2,1)S(1)}, bf16[2048,256]{1,0:T(8,128)(2,1)S(1)}, u32[]{:S(2)}, u32[]{:S(2)}) collective-permute-start(bf16[2048,256]{1,0:T(8,128)(2,1)S(1)} %copy-done.5), channel_id=1, source_target_pairs={{3,1},{0,2},{14,12},{13,15},{19,17},{16,18},{30,28},{29,31}} | collective-permute-start | bytes 3145736 | tf_op jit(solution)/shard_map/ppermute | solution.py:423
  152.2 2.1 %collective-permute-start.28 = (bf16[320,2048]{1,0:T(8,128)(2,1)S(1)}, bf16[320,2048]{1,0:T(8,128)(2,1)S(1)}, u32[]{:S(2)}, u32[]{:S(2)}) collective-permute-start(bf16[320,2048]{1,0:T(8,128)(2,1)S(1)} %copy-done.3), channel_id=1, source_target_pairs={{2,6},{3,7},{0,4},{1,5},{14,10},{15,11},{12,8},{13,9},{18,22},{19,... | collective-permute-start | bytes 3932168 | tf_op jit(solution)/shard_map/ppermute | solution.py:423
  154.4 2.5 %masked.1.refs_5_ = f32[328,256]{1,0:T(8,128)} custom-call(s32[18]{0:T(128)} %dynamic-slice_bitcast_fusion.order_ref, f32[328,256]{1,0:T(8,128)} %inside.3.own_ref, f32[328,256]{1,0:T(8,128)} %copy-done.11), custom_call_target="tpu_custom_call" | custom-call | bytes 1007616 | tf_op jit(solution)/shard_map/masked/pallas_call | solution.py:59
  156.9 4.1 %stage.11.refs_3_ = f32[320,256]{1,0:T(8,128)} custom-call(s32[18]{0:T(128)} %dynamic-slice_bitcast_fusion.order_ref, bf16[160,32768]{1,0:T(8,128)(2,1)} %own_ref.17, bf16[160,32768]{1,0:T(8,128)(2,1)} %collective-permute-done.sib_ref, bf16[2048,256]{1,0:T(8,128)(2,1)} %collective-permute-done.7.refs_0_, bf16[2048,256]{1,0:T(8,128)(2,1)} %collective-permute-done.21.refs_1_, ...), custom_call_target="tpu_custom_call" | custom-call | flops 335544320 | bytes 4063232 | tf_op jit(solution)/shard_map/stage/pallas_call | solution.py:59
  161.0 0.7 collective-permute-start.23
  161.7 0.7 collective-permute-start.24
  162.5 1.3 collective-permute-start.25
  163.8 0.7 collective-permute-done.26.refs_1_
  164.5 4.3 %collective-permute-start.29 = (f32[328,256]{1,0:T(8,128)S(1)}, f32[328,256]{1,0:T(8,128)S(1)}, u32[]{:S(2)}, u32[]{:S(2)}) collective-permute-start(f32[328,256]{1,0:T(8,128)S(1)} %copy-done.2), channel_id=1, source_target_pairs={{2,6},{3,7},{0,4},{1,5},{14,10},{15,11},{12,8},{13,9},{18,22},{19,... | collective-permute-start | bytes 1007624 | tf_op jit(solution)/shard_map/ppermute | solution.py:423
  168.8 4.2 %stage.12.refs_2_ = f32[320,256]{1,0:T(8,128)} custom-call(s32[18]{0:T(128)} %dynamic-slice_bitcast_fusion.order_ref, bf16[160,32768]{1,0:T(8,128)(2,1)} %own_ref.17, bf16[160,32768]{1,0:T(8,128)(2,1)} %collective-permute-done.sib_ref, bf16[2048,256]{1,0:T(8,128)(2,1)} %collective-permute-done.14.refs_0_, bf16[2048,256]{1,0:T(8,128)(2,1)} %collective-permute-done.27.refs_1_, ...), custom_call_target="tpu_custom_call" | custom-call | flops 335544320 | bytes 5111808 | tf_op jit(solution)/shard_map/stage/pallas_call | solution.py:59
  173.0 3.9 %stage.13.refs_4_ = f32[320,256]{1,0:T(8,128)} custom-call(s32[18]{0:T(128)} %dynamic-slice_bitcast_fusion.order_ref, bf16[160,32768]{1,0:T(8,128)(2,1)} %own_ref.17, bf16[160,32768]{1,0:T(8,128)(2,1)} %collective-permute-done.sib_ref, bf16[2048,256]{1,0:T(8,128)(2,1)} %copy-done.1, bf16[2048,256]{1,0:T(8,128)(2,1)} %copy-done.7, f32[320,256]{1,0:T(8,128)} %stage.12.refs_2_), custom_call_target="tpu_custom_call" | custom-call | flops 335544320 | bytes 4063232 | tf_op jit(solution)/shard_map/stage/pallas_call | solution.py:59
  177.0 12.9 %collective-permute-done.29.refs_7_ = f32[328,256]{1,0:T(8,128)S(1)} collective-permute-done((f32[328,256]{1,0:T(8,128)S(1)}, f32[328,256]{1,0:T(8,128)S(1)}, u32[]{:S(2)}, u32[]{:S(2)}) %collective-permute-start.29) | collective-permute-done | bytes 335904 | tf_op jit(solution)/shard_map/ppermute | solution.py:423
  189.9 0.7 copy-done.12
  190.5 0.5 copy-done.4
  191.0 0.4 copy-done.6
  191.4 0.3 copy-done.8
  191.7 5.5 %finish.1 = f32[32,8]{1,0:T(8,128)} custom-call(s32[18]{0:T(128)} %dynamic-slice_bitcast_fusion.order_ref, bf16[160,32768]{1,0:T(8,128)(2,1)} %own_ref.17, bf16[160,32768]{1,0:T(8,128)(2,1)} %collective-permute-done.sib_ref, bf16[2048,256]{1,0:T(8,128)(2,1)} %copy-done.6, bf16[2048,256]{1,0:T(8,128)(2,1)} %copy-done.8, ...), custom_call_target="tpu_custom_call" | custom-call | flops 671088640 | bytes 7816192 | tf_op jit(solution)/shard_map/finish/pallas_call | solution.py:59
  197.2 12.4 %all_to_all.5 = f32[16,2,8]{2,1,0:T(2,128)S(1)} all-to-all(f32[16,2,8]{2,1,0:T(2,128)} %bitcast.3), channel_id=1, replica_groups=mesh['groups'=2,'dp'=16] {'dp'}, dimensions={0} | all-to-all | bytes 2048 | tf_op jit(solution)/shard_map/all_to_all | solution.py:471
  209.6 0.6 reduce_sum.9
  (51 shorter events, 0.1 us)
Async XLA Ops:
  0.0 75.9 %collective-permute-start = (bf16[160,32768]{1,0:T(8,128)(2,1)}, bf16[160,32768]{1,0:T(8,128)(2,1)}, u32[]{:S(2)}, u32[]{:S(2)}) collective-permute-start(bf16[160,32768]{1,0:T(8,128)(2,1)} %own_ref.17), channel_id=1, source_target_pairs={{0,1},{1,0},{2,3},{3,2},{4,5},{5,4},{6,7},{7,6},{8,9},{9,8},{10,11... | collective-permute-start | bytes 31457288 | tf_op jit(solution)/shard_map/ppermute | solution.py:423
  0.5 38.6 %collective-permute-start.1 = (bf16[2048,256]{1,0:T(8,128)(2,1)}, bf16[2048,256]{1,0:T(8,128)(2,1)}, u32[]{:S(2)}, u32[]{:S(2)}) collective-permute-start(bf16[2048,256]{1,0:T(8,128)(2,1)} %refs_0_.3), channel_id=1, source_target_pairs={{6,10},{10,8},{8,4},{4,6},{11,7},{9,11},{5,9},{7,5},{2,0},{1,3},{1... | collective-permute-start | bytes 3145736 | tf_op jit(solution)/shard_map/ppermute | solution.py:423
  1.7 15.1 %collective-permute-start.2 = (bf16[512,256]{1,0:T(8,128)(2,1)}, bf16[512,256]{1,0:T(8,128)(2,1)S(1)}, u32[]{:S(2)}, u32[]{:S(2)}) collective-permute-start(bf16[512,256]{1,0:T(8,128)(2,1)} %refs_8_.1), channel_id=1, source_target_pairs={{0,4},{1,5},{2,6},{3,7},{4,8},{5,9},{6,10},{7,11},{8,12},{9,13},{1... | collective-permute-start | bytes 786440 | tf_op jit(solution)/shard_map/ppermute | solution.py:423
  6.5 32.5 %collective-permute-start.3 = (bf16[512,256]{1,0:T(8,128)(2,1)}, bf16[512,256]{1,0:T(8,128)(2,1)S(1)}, u32[]{:S(2)}, u32[]{:S(2)}) collective-permute-start(bf16[512,256]{1,0:T(8,128)(2,1)} %refs_8_.1), channel_id=1, source_target_pairs={{0,8},{1,9},{2,10},{3,11},{4,12},{5,13},{6,14},{7,15},{8,0},{9,1},... | collective-permute-start | bytes 786440 | tf_op jit(solution)/shard_map/ppermute | solution.py:423
  10.0 29.1 %collective-permute-start.4 = (bf16[512,256]{1,0:T(8,128)(2,1)}, bf16[512,256]{1,0:T(8,128)(2,1)S(1)}, u32[]{:S(2)}, u32[]{:S(2)}) collective-permute-start(bf16[512,256]{1,0:T(8,128)(2,1)} %refs_8_.1), channel_id=1, source_target_pairs={{0,12},{1,13},{2,14},{3,15},{4,0},{5,1},{6,2},{7,3},{8,4},{9,5},{1... | collective-permute-start | bytes 786440 | tf_op jit(solution)/shard_map/ppermute | solution.py:423
  16.9 65.0 %copy-start.14 = (bf16[512,256]{1,0:T(8,128)(2,1)}, bf16[512,256]{1,0:T(8,128)(2,1)S(1)}, u32[]{:S(2)}) copy-start(bf16[512,256]{1,0:T(8,128)(2,1)S(1)} %collective-permute-done.2.refs_9_) | copy-start | bytes 786436
  16.9 55.7 %collective-permute-start.6 = (bf16[2048,256]{1,0:T(8,128)(2,1)}, bf16[2048,256]{1,0:T(8,128)(2,1)}, u32[]{:S(2)}, u32[]{:S(2)}) collective-permute-start(bf16[2048,256]{1,0:T(8,128)(2,1)} %refs_0_.3), channel_id=1, source_target_pairs={{2,6},{3,7},{0,4},{1,5},{14,10},{15,11},{12,8},{13,9},{18,22},{19,... | collective-permute-start | bytes 3145736 | tf_op jit(solution)/shard_map/ppermute | solution.py:423
  39.1 17.7 %copy-start.16 = (bf16[512,256]{1,0:T(8,128)(2,1)}, bf16[512,256]{1,0:T(8,128)(2,1)S(1)}, u32[]{:S(2)}) copy-start(bf16[512,256]{1,0:T(8,128)(2,1)S(1)} %collective-permute-done.3.refs_10_) | copy-start | bytes 786436
  39.1 25.2 %copy-start.17 = (bf16[512,256]{1,0:T(8,128)(2,1)}, bf16[512,256]{1,0:T(8,128)(2,1)S(1)}, u32[]{:S(2)}) copy-start(bf16[512,256]{1,0:T(8,128)(2,1)S(1)} %collective-permute-done.4.refs_11_) | copy-start | bytes 786436
  39.1 35.1 %collective-permute-start.5 = (bf16[2048,256]{1,0:T(8,128)(2,1)}, bf16[2048,256]{1,0:T(8,128)(2,1)}, u32[]{:S(2)}, u32[]{:S(2)}) collective-permute-start(bf16[2048,256]{1,0:T(8,128)(2,1)} %collective-permute-done.1.refs_0_), channel_id=1, source_target_pairs={{6,10},{10,8},{8,4},{4,6},{11,7},{9,11},{5,9},{7,5},{22,26},{26,24... | collective-permute-start | bytes 3145736 | tf_op jit(solution)/shard_map/ppermute | solution.py:423
  40.7 11.3 %collective-permute-start.10 = (bf16[512,256]{1,0:T(8,128)(2,1)}, bf16[512,256]{1,0:T(8,128)(2,1)S(1)}, u32[]{:S(2)}, u32[]{:S(2)}) collective-permute-start(bf16[512,256]{1,0:T(8,128)(2,1)} %refs_8_.1), channel_id=1, source_target_pairs={{0,2},{1,3},{2,0},{3,1},{4,6},{5,7},{6,4},{7,5},{8,10},{9,11},{10,... | collective-permute-start | bytes 786440 | tf_op jit(solution)/shard_map/ppermute | solution.py:423
  44.7 12.1 %collective-permute-start.11 = (bf16[512,256]{1,0:T(8,128)(2,1)S(1)}, bf16[512,256]{1,0:T(8,128)(2,1)S(1)}, u32[]{:S(2)}, u32[]{:S(2)}) collective-permute-start(bf16[512,256]{1,0:T(8,128)(2,1)S(1)} %collective-permute-done.2.refs_9_), channel_id=1, source_target_pairs={{0,2},{1,3},{2,0},{3,1},{4,6},{5,7},{6,4},{7,5},{8,10},{9,11},{10,... | collective-permute-start | bytes 786440 | tf_op jit(solution)/shard_map/ppermute | solution.py:423
  52.0 29.8 %copy-start.13 = (bf16[512,256]{1,0:T(8,128)(2,1)}, bf16[512,256]{1,0:T(8,128)(2,1)S(1)}, u32[]{:S(2)}) copy-start(bf16[512,256]{1,0:T(8,128)(2,1)S(1)} %collective-permute-done.10.refs_8_) | copy-start | bytes 786436
  52.0 42.9 %collective-permute-start.18 = (bf16[160,8192]{1,0:T(8,128)(2,1)}, bf16[160,8192]{1,0:T(8,128)(2,1)S(1)}, u32[]{:S(2)}, u32[]{:S(2)}) collective-permute-start(bf16[160,8192]{1,0:T(8,128)(2,1)} %refs_6_.3), channel_id=1, source_target_pairs={{0,1},{1,0},{2,3},{3,2},{4,5},{5,4},{6,7},{7,6},{8,9},{9,8},{10,11... | collective-permute-start | bytes 7864328 | tf_op jit(solution)/shard_map/ppermute | solution.py:423
  56.8 25.1 %copy-start.15 = (bf16[512,256]{1,0:T(8,128)(2,1)}, bf16[512,256]{1,0:T(8,128)(2,1)S(1)}, u32[]{:S(2)}) copy-start(bf16[512,256]{1,0:T(8,128)(2,1)S(1)} %collective-permute-done.11.refs_9_) | copy-start | bytes 786436
  56.8 7.5 %collective-permute-start.12 = (bf16[512,256]{1,0:T(8,128)(2,1)S(1)}, bf16[512,256]{1,0:T(8,128)(2,1)S(1)}, u32[]{:S(2)}, u32[]{:S(2)}) collective-permute-start(bf16[512,256]{1,0:T(8,128)(2,1)S(1)} %collective-permute-done.3.refs_10_), channel_id=1, source_target_pairs={{0,2},{1,3},{2,0},{3,1},{4,6},{5,7},{6,4},{7,5},{8,10},{9,11},{10,... | collective-permute-start | bytes 786440 | tf_op jit(solution)/shard_map/ppermute | solution.py:423
  64.3 6.6 %copy-start.18 = (bf16[512,256]{1,0:T(8,128)(2,1)}, bf16[512,256]{1,0:T(8,128)(2,1)S(1)}, u32[]{:S(2)}) copy-start(bf16[512,256]{1,0:T(8,128)(2,1)S(1)} %collective-permute-done.12.refs_10_) | copy-start | bytes 786436
  64.3 6.5 %collective-permute-start.13 = (bf16[512,256]{1,0:T(8,128)(2,1)S(1)}, bf16[512,256]{1,0:T(8,128)(2,1)S(1)}, u32[]{:S(2)}, u32[]{:S(2)}) collective-permute-start(bf16[512,256]{1,0:T(8,128)(2,1)S(1)} %collective-permute-done.4.refs_11_), channel_id=1, source_target_pairs={{0,2},{1,3},{2,0},{3,1},{4,6},{5,7},{6,4},{7,5},{8,10},{9,11},{10,... | collective-permute-start | bytes 786440 | tf_op jit(solution)/shard_map/ppermute | solution.py:423
  70.8 1.7 copy-start.19
  70.8 11.0 %collective-permute-start.9 = (bf16[2048,256]{1,0:T(8,128)(2,1)}, bf16[2048,256]{1,0:T(8,128)(2,1)}, u32[]{:S(2)}, u32[]{:S(2)}) collective-permute-start(bf16[2048,256]{1,0:T(8,128)(2,1)} %refs_0_.3), channel_id=1, source_target_pairs={{6,2},{5,1},{11,15},{8,12},{22,18},{21,17},{27,31},{24,28}} | collective-permute-start | bytes 3145736 | tf_op jit(solution)/shard_map/ppermute | solution.py:423
  72.5 14.2 %collective-permute-start.15 = (bf16[2048,256]{1,0:T(8,128)(2,1)}, bf16[2048,256]{1,0:T(8,128)(2,1)}, u32[]{:S(2)}, u32[]{:S(2)}) collective-permute-start(bf16[2048,256]{1,0:T(8,128)(2,1)} %collective-permute-done.1.refs_0_), channel_id=1, source_target_pairs={{6,2},{5,1},{11,15},{8,12},{22,18},{21,17},{27,31},{24,28}} | collective-permute-start | bytes 3145736 | tf_op jit(solution)/shard_map/ppermute | solution.py:423
  74.2 17.8 %collective-permute-start.7 = (bf16[2048,256]{1,0:T(8,128)(2,1)}, bf16[2048,256]{1,0:T(8,128)(2,1)}, u32[]{:S(2)}, u32[]{:S(2)}) collective-permute-start(bf16[2048,256]{1,0:T(8,128)(2,1)} %collective-permute-done.6.refs_0_), channel_id=1, source_target_pairs={{6,10},{10,8},{8,4},{4,6},{11,7},{9,11},{5,9},{7,5},{22,26},{26,24... | collective-permute-start | bytes 3145736 | tf_op jit(solution)/shard_map/ppermute | solution.py:423
  75.9 16.1 %collective-permute-start.8 = (bf16[2048,256]{1,0:T(8,128)(2,1)}, bf16[2048,256]{1,0:T(8,128)(2,1)}, u32[]{:S(2)}, u32[]{:S(2)}) collective-permute-start(bf16[2048,256]{1,0:T(8,128)(2,1)} %collective-permute-done.5.refs_0_), channel_id=1, source_target_pairs={{6,2},{5,1},{11,15},{8,12},{22,18},{21,17},{27,31},{24,28}} | collective-permute-start | bytes 3145736 | tf_op jit(solution)/shard_map/ppermute | solution.py:423
  81.9 31.1 %collective-permute-start.17 = (bf16[2048,256]{1,0:T(8,128)(2,1)}, bf16[2048,256]{1,0:T(8,128)(2,1)S(1)}, u32[]{:S(2)}, u32[]{:S(2)}) collective-permute-start(bf16[2048,256]{1,0:T(8,128)(2,1)} %collective-permute-done.9.refs_1_), channel_id=1, source_target_pairs={{2,0},{1,3},{15,13},{12,14},{18,16},{17,19},{31,29},{28,30}} | collective-permute-start | bytes 3145736 | tf_op jit(solution)/shard_map/ppermute | solution.py:423
  86.7 37.5 %collective-permute-start.16 = (bf16[2048,256]{1,0:T(8,128)(2,1)}, bf16[2048,256]{1,0:T(8,128)(2,1)S(1)}, u32[]{:S(2)}, u32[]{:S(2)}) collective-permute-start(bf16[2048,256]{1,0:T(8,128)(2,1)} %collective-permute-done.15.refs_2_), channel_id=1, source_target_pairs={{2,0},{1,3},{15,13},{12,14},{18,16},{17,19},{31,29},{28,30}} | collective-permute-start | bytes 3145736 | tf_op jit(solution)/shard_map/ppermute | solution.py:423
  92.0 37.5 %collective-permute-start.14 = (bf16[2048,256]{1,0:T(8,128)(2,1)}, bf16[2048,256]{1,0:T(8,128)(2,1)}, u32[]{:S(2)}, u32[]{:S(2)}) collective-permute-start(bf16[2048,256]{1,0:T(8,128)(2,1)} %collective-permute-done.5.refs_0_), channel_id=1, source_target_pairs={{6,10},{10,8},{8,4},{4,6},{11,7},{9,11},{5,9},{7,5},{22,26},{26,24... | collective-permute-start | bytes 3145736 | tf_op jit(solution)/shard_map/ppermute | solution.py:423
  93.6 58.6 %collective-permute-start.21 = (bf16[2048,256]{1,0:T(8,128)(2,1)}, bf16[2048,256]{1,0:T(8,128)(2,1)}, u32[]{:S(2)}, u32[]{:S(2)}) collective-permute-start(bf16[2048,256]{1,0:T(8,128)(2,1)} %collective-permute-done.7.refs_0_), channel_id=1, source_target_pairs={{7,3},{4,0},{10,14},{9,13},{23,19},{20,16},{26,30},{25,29}} | collective-permute-start | bytes 3145736 | tf_op jit(solution)/shard_map/ppermute | solution.py:423
  94.9 1.5 copy-start
  113.0 1.1 copy-start.9
  124.2 1.0 copy-start.10
  129.5 17.7 %copy-start.5 = (bf16[2048,256]{1,0:T(8,128)(2,1)S(1)}, bf16[2048,256]{1,0:T(8,128)(2,1)}, u32[]{:S(2)}) copy-start(bf16[2048,256]{1,0:T(8,128)(2,1)} %refs_0_.3) | copy-start | bytes 3145732
  129.5 22.8 %copy-start.3 = (bf16[320,2048]{1,0:T(8,128)(2,1)S(1)}, bf16[320,2048]{1,0:T(8,128)(2,1)}, u32[]{:S(2)}) copy-start(bf16[320,2048]{1,0:T(8,128)(2,1)} %window.1) | copy-start | bytes 3932164
  129.5 31.5 %collective-permute-start.19 = (bf16[2048,256]{1,0:T(8,128)(2,1)}, bf16[2048,256]{1,0:T(8,128)(2,1)S(1)}, u32[]{:S(2)}, u32[]{:S(2)}) collective-permute-start(bf16[2048,256]{1,0:T(8,128)(2,1)} %collective-permute-done.7.refs_0_), channel_id=1, source_target_pairs={{6,10},{10,8},{8,4},{4,6},{11,7},{9,11},{5,9},{7,5},{22,26},{26,24... | collective-permute-start | bytes 3145736 | tf_op jit(solution)/shard_map/ppermute | solution.py:423
  130.3 30.7 %collective-permute-start.20 = (bf16[2048,256]{1,0:T(8,128)(2,1)}, bf16[2048,256]{1,0:T(8,128)(2,1)}, u32[]{:S(2)}, u32[]{:S(2)}) collective-permute-start(bf16[2048,256]{1,0:T(8,128)(2,1)} %collective-permute-done.14.refs_0_), channel_id=1, source_target_pairs={{6,2},{5,1},{11,15},{8,12},{22,18},{21,17},{27,31},{24,28}} | collective-permute-start | bytes 3145736 | tf_op jit(solution)/shard_map/ppermute | solution.py:423
  132.0 30.5 %collective-permute-start.27 = (bf16[2048,256]{1,0:T(8,128)(2,1)}, bf16[2048,256]{1,0:T(8,128)(2,1)}, u32[]{:S(2)}, u32[]{:S(2)}) collective-permute-start(bf16[2048,256]{1,0:T(8,128)(2,1)} %collective-permute-done.8.refs_2_), channel_id=1, source_target_pairs={{2,0},{1,3},{15,13},{12,14},{18,16},{17,19},{31,29},{28,30}} | collective-permute-start | bytes 3145736 | tf_op jit(solution)/shard_map/ppermute | solution.py:423
  137.0 10.1 %collective-permute-start.22 = (f32[328,256]{1,0:T(8,128)}, f32[328,256]{1,0:T(8,128)S(1)}, u32[]{:S(2)}, u32[]{:S(2)}) collective-permute-start(f32[328,256]{1,0:T(8,128)} %inside.3.own_ref), channel_id=1, source_target_pairs={{0,1},{1,0},{2,3},{3,2},{4,5},{5,4},{6,7},{7,6},{8,9},{9,8},{10,11... | collective-permute-start | bytes 1007624 | tf_op jit(solution)/shard_map/ppermute | solution.py:423
  147.1 7.2 %copy-start.11 = (f32[328,256]{1,0:T(8,128)}, f32[328,256]{1,0:T(8,128)S(1)}, u32[]{:S(2)}) copy-start(f32[328,256]{1,0:T(8,128)S(1)} %collective-permute-done.22.got_ref) | copy-start | bytes 1007620
  147.2 17.3 %collective-permute-start.26 = (bf16[2048,256]{1,0:T(8,128)(2,1)S(1)}, bf16[2048,256]{1,0:T(8,128)(2,1)S(1)}, u32[]{:S(2)}, u32[]{:S(2)}) collective-permute-start(bf16[2048,256]{1,0:T(8,128)(2,1)S(1)} %copy-done.5), channel_id=1, source_target_pairs={{3,1},{0,2},{14,12},{13,15},{19,17},{16,18},{30,28},{29,31}} | collective-permute-start | bytes 3145736 | tf_op jit(solution)/shard_map/ppermute | solution.py:423
  152.2 37.6 %collective-permute-start.28 = (bf16[320,2048]{1,0:T(8,128)(2,1)S(1)}, bf16[320,2048]{1,0:T(8,128)(2,1)S(1)}, u32[]{:S(2)}, u32[]{:S(2)}) collective-permute-start(bf16[320,2048]{1,0:T(8,128)(2,1)S(1)} %copy-done.3), channel_id=1, source_target_pairs={{2,6},{3,7},{0,4},{1,5},{14,10},{15,11},{12,8},{13,9},{18,22},{19,... | collective-permute-start | bytes 3932168 | tf_op jit(solution)/shard_map/ppermute | solution.py:423
  156.9 7.5 %copy-start.2 = (f32[328,256]{1,0:T(8,128)S(1)}, f32[328,256]{1,0:T(8,128)}, u32[]{:S(2)}) copy-start(f32[328,256]{1,0:T(8,128)} %masked.1.refs_5_) | copy-start | bytes 1007620
  161.0 12.0 %copy-start.1 = (bf16[2048,256]{1,0:T(8,128)(2,1)}, bf16[2048,256]{1,0:T(8,128)(2,1)S(1)}, u32[]{:S(2)}) copy-start(bf16[2048,256]{1,0:T(8,128)(2,1)S(1)} %collective-permute-done.19.refs_0_.refs_3_) | copy-start | bytes 3145732
  161.0 28.8 %collective-permute-start.23 = (bf16[2048,256]{1,0:T(8,128)(2,1)S(1)}, bf16[2048,256]{1,0:T(8,128)(2,1)S(1)}, u32[]{:S(2)}, u32[]{:S(2)}) collective-permute-start(bf16[2048,256]{1,0:T(8,128)(2,1)S(1)} %collective-permute-done.19.refs_0_.refs_3_), channel_id=1, source_target_pairs={{6,10},{10,8},{8,4},{4,6},{11,7},{9,11},{5,9},{7,5},{22,26},{26,24... | collective-permute-start | bytes 3145736 | tf_op jit(solution)/shard_map/ppermute | solution.py:423
  161.7 28.1 %collective-permute-start.24 = (bf16[2048,256]{1,0:T(8,128)(2,1)S(1)}, bf16[2048,256]{1,0:T(8,128)(2,1)S(1)}, u32[]{:S(2)}, u32[]{:S(2)}) collective-permute-start(bf16[2048,256]{1,0:T(8,128)(2,1)S(1)} %collective-permute-done.19.refs_0_.refs_3_), channel_id=1, source_target_pairs={{6,2},{5,1},{11,15},{8,12},{22,18},{21,17},{27,31},{24,28}} | collective-permute-start | bytes 3145736 | tf_op jit(solution)/shard_map/ppermute | solution.py:423
  162.5 27.4 %collective-permute-start.25 = (bf16[2048,256]{1,0:T(8,128)(2,1)}, bf16[2048,256]{1,0:T(8,128)(2,1)}, u32[]{:S(2)}, u32[]{:S(2)}) collective-permute-start(bf16[2048,256]{1,0:T(8,128)(2,1)} %collective-permute-done.20.refs_2_), channel_id=1, source_target_pairs={{2,0},{1,3},{15,13},{12,14},{18,16},{17,19},{31,29},{28,30}} | collective-permute-start | bytes 3145736 | tf_op jit(solution)/shard_map/ppermute | solution.py:423
  164.5 8.6 %copy-start.7 = (bf16[2048,256]{1,0:T(8,128)(2,1)}, bf16[2048,256]{1,0:T(8,128)(2,1)S(1)}, u32[]{:S(2)}) copy-start(bf16[2048,256]{1,0:T(8,128)(2,1)S(1)} %collective-permute-done.26.refs_1_) | copy-start | bytes 3145732
  164.5 25.3 %collective-permute-start.29 = (f32[328,256]{1,0:T(8,128)S(1)}, f32[328,256]{1,0:T(8,128)S(1)}, u32[]{:S(2)}, u32[]{:S(2)}) collective-permute-start(f32[328,256]{1,0:T(8,128)S(1)} %copy-done.2), channel_id=1, source_target_pairs={{2,6},{3,7},{0,4},{1,5},{14,10},{15,11},{12,8},{13,9},{18,22},{19,... | collective-permute-start | bytes 1007624 | tf_op jit(solution)/shard_map/ppermute | solution.py:423
  189.8 0.7 copy-start.12
  189.8 1.2 copy-start.4
  189.8 1.5 copy-start.6
  189.8 1.8 copy-start.8

commit v5 on v2

--- a/solution.py
+++ b/solution.py
@@ -110,29 +110,85 @@
     )
 
 
-def score_kernel(lead, order_ref, own_g, sib_g, b_ref, out_ref, inn_ref, got_ref,
-                 seq_ref, len_ref, seq_sib, len_sib, table_ref):
-    tokens = own_g.shape[0]
+def join_kernel(lead, in_ref, out_ref, joined_ref, sems):
+    rows_in = in_ref.shape[0]
+    copies = [
+        pltpu.make_async_copy(in_ref, joined_ref.at[pl.ds(0, rows_in)], sems.at[0]),
+        pltpu.make_async_copy(
+            out_ref.at[pl.ds(0, lead)], joined_ref.at[pl.ds(rows_in, lead)], sems.at[1]
+        ),
+    ]
+    for copy in copies:
+        copy.start()
+    for copy in copies:
+        copy.wait()
+
+
+def join(in_factors, out_factors, lead):
+    rows_in, columns = in_factors.shape
+    anywhere = pl.BlockSpec(memory_space=pl.ANY)
+    return pl.pallas_call(
+        functools.partial(join_kernel, lead),
+        in_specs=[anywhere] * 2,
+        out_specs=anywhere,
+        out_shape=jax.ShapeDtypeStruct((rows_in + lead, columns), in_factors.dtype),
+        scratch_shapes=[pltpu.SemaphoreType.DMA((2,))],
+        cost_estimate=pl.CostEstimate(
+            flops=0, bytes_accessed=4 * (rows_in + lead) * columns, transcendentals=0
+        ),
+        name="join",
+    )(in_factors, out_factors)
+
+
+def window_kernel(lead, order_ref, own_ref, sib_ref, out_ref):
+    tokens = own_ref.shape[0]
+    out_ref[:tokens] = own_ref[:, lead:]
+    out_ref[tokens:] = sib_ref[:, lead:]
+
+
+def score_kernel(seq_ref, len_ref, seq_sib, len_sib, window_ref, b_ref, out_ref, inn_ref, got_ref,
+                 table_ref):
     columns = b_ref.shape[1]
+    tokens = window_ref.shape[0] // 2
     queries = columns // RANK
     column = lax.broadcasted_iota(jnp.int32, (columns, queries), 0) // RANK
     query = lax.broadcasted_iota(jnp.int32, (columns, queries), 1)
     fold = (column == query).astype(F32)
     position = lax.broadcasted_iota(jnp.int32, (LEN, columns), 0)
     row = lax.broadcasted_iota(jnp.int32, table_ref.shape, 0)
-    table = jnp.zeros(table_ref.shape, F32)
-    for k, (g, seq, lens) in enumerate(((own_g, seq_ref, len_ref), (sib_g, seq_sib, len_sib))):
+    out = out_ref[...] + dot(window_ref[...], b_ref[...])
+    sums, slots = [], []
+    for k, (seq, lens) in enumerate(((seq_ref, len_ref), (seq_sib, len_sib))):
         mine, other = pl.ds(k * tokens, tokens), pl.ds((1 - k) * tokens, tokens)
-        out = out_ref[mine] + dot(g[:, lead:], b_ref[...])
-        contrib = out * (inn_ref[mine] + got_ref[other])
+        contrib = out[k * tokens:(k + 1) * tokens] * (inn_ref[mine] + got_ref[other])
         for i in range(tokens // LEN):
             kept = jnp.where(position < lens[i], contrib[i * LEN:(i + 1) * LEN], 0.0)
-            summed = jnp.sum(kept, axis=0, keepdims=True)
-            score = jnp.dot(
-                summed, fold, precision=lax.Precision.HIGHEST, preferred_element_type=F32
-            ) * (1.0 / math.sqrt(RANK * LEN))
-            table = jnp.where(row == seq[i], score, table)
+            sums.append(jnp.sum(kept, axis=0, keepdims=True))
+            slots.append(seq[i])
+    scores = jnp.dot(
+        jnp.concatenate(sums), fold, precision=lax.Precision.HIGHEST, preferred_element_type=F32
+    ) * (1.0 / math.sqrt(RANK * LEN))
+    table = jnp.zeros(table_ref.shape, F32)
+    for i, slot in enumerate(slots):
+        table = jnp.where(row == slot, scores[i:i + 1], table)
     table_ref[...] = table
+
+
+def score_table(numbers, arrays, rows, queries):
+    smem, vmem = (pl.BlockSpec(memory_space=m) for m in (pltpu.SMEM, pltpu.VMEM))
+    window, block = arrays[:2]
+    size = sum(x.size * x.dtype.itemsize for x in arrays)
+    return pl.pallas_call(
+        score_kernel,
+        in_specs=[smem] * len(numbers) + [vmem] * len(arrays),
+        out_specs=vmem,
+        out_shape=jax.ShapeDtypeStruct((rows, queries), F32),
+        cost_estimate=pl.CostEstimate(
+            flops=2 * window.size * block.shape[1], bytes_accessed=size, transcendentals=0
+        ),
+        compiler_params=pltpu.CompilerParams(vmem_limit_bytes=VMEM),
+        name="score",
+    )(*numbers, *arrays)
 
 
 def shards(acts, grads, out_factors, in_factors, seq_slot, lengths):
@@ -153,14 +209,11 @@
         every = lax.all_gather(in_factors, "dp", axis=0, tiled=True)
         own, rows_in = own[:1], 0
     lead = (rows - rows_in) // 2
-    first = out_factors[:lead]
-    if rows_in:
-        first = jnp.concatenate([in_factors, first])
+    first = join(in_factors, out_factors, lead) if rows_in else out_factors[:lead]
     held = [(first, out_factors[lead:])]
 
     seq_sib, len_sib = lax.ppermute(jnp.stack([seq_slot, lengths]), "dp", swap)
     sib = [lax.ppermute(x, "dp", swap) for x in own]
-
     totals, summed = [], 0
 
     def sum_to(k, totals, summed):
@@ -175,8 +228,14 @@
             a, *totals = lax.optimization_barrier((a, *totals))
             b, *totals = lax.optimization_barrier((b, *totals))
         held.append((lax.ppermute(a, "dp", pairs), lax.ppermute(b, "dp", pairs)))
-    totals, summed = sum_to(chips - 1, totals, summed)
     s = chips - 1
+    window = call(
+        functools.partial(window_kernel, lead), mine,
+        [(x, rows, lambda i, o: (0, o[s])) for x in (own[0], sib[0])], [], [],
+        [jax.ShapeDtypeStruct((2 * tokens, rows - lead), grads.dtype)], 0, "window",
+    )[0]
+    totals[0], window = lax.optimization_barrier((totals[0], window))
+    totals, summed = sum_to(s, totals, summed)
     a, b = held[s]
     totals = step(mine, own, sib, [a], totals, s, lead, rows, rows_in)
     if every is not None:
@@ -186,13 +245,9 @@
 
     slots = lengths.shape[0]
     queries = columns // RANK
-    windows = [(x, rows, lambda i, o: (0, o[s])) for x in (grads, sib[0])]
-    table = call(
-        functools.partial(score_kernel, lead), mine, windows, [b, *totals, got],
-        [seq_slot, lengths, seq_sib, len_sib],
-        [jax.ShapeDtypeStruct((slots * devices, queries), F32)],
-        4 * tokens * rows * columns, "score",
-    )[0]
+    table = score_table(
+        [seq_slot, lengths, seq_sib, len_sib], [window, b, *totals, got], slots * devices, queries
+    )
     got = lax.all_to_all(table.reshape(devices, slots, queries), "dp", 0, 0, tiled=True)
     return jnp.sum(got, axis=0)
 

time: 122 us -> 140 us (1.15)
  Pallas kernels: 21.9 us -> 42.9 us
  starting transfers between devices: 28.8 us -> 26.7 us
  waiting for transfers between devices: 45.9 us -> 47.7 us
    pallas_call x0 -> x2, Pallas kernels: none -> 22.2 us  [the longest x1 21 us: join(): pl.pallas_call(functools.partial(join_kernel, lead), in_specs=[anywhere]...]
    ppermute x14, starting transfers between devices: 27.7 us -> 25.6 us  [shards(): held.append((lax.ppermute(a, 'dp', pairs), lax.ppermute(b, 'dp', pairs)))]
    ppermute x14, waiting for transfers between devices: 44.8 us -> 46.6 us  [shards(): held.append((lax.ppermute(a, 'dp', pairs), lax.ppermute(b, 'dp', pairs)))]
    all_to_all x1, blocking collectives: 12.7 us -> 11.3 us  [shards(): lax.all_to_all(table.reshape(devices, slots, queries), 'dp', 0, 0, tiled=...]
  transfers between devices with their start and end apart: 18 -> 18, of which waited for: 12 -> 14; matrix products, arithmetic and copies ran while one was open for 3% -> 1% of each run, Pallas kernels for 16% -> 30%
where the time goes in v5:
time: 140 us
  waiting for transfers between devices  47.7 us (34%)
  Pallas kernels  42.9 us (31%)
  starting transfers between devices  26.7 us (19%)
  blocking collectives  11.3 us (8%)
  local copies, waits for them, and re-layouts  10.3 us (7%)
    ppermute x14, waiting for transfers between devices, shards(): held.append((lax.ppermute(a, 'dp', pairs), lax.ppermute(b, 'dp', pairs)))  46.6 us
    ppermute x14, starting transfers between devices, shards(): held.append((lax.ppermute(a, 'dp', pairs), lax.ppermute(b, 'dp', pairs)))  25.6 us
    pallas_call x1, Pallas kernels, join(): pl.pallas_call(functools.partial(join_kernel, lead), in_specs=[anywhere]...  21 us
    pallas_call x9, Pallas kernels, call(): pl.pallas_call(kernel, grid_spec=pltpu.PrefetchScalarGridSpec(num_scalar_...  20.8 us
    all_to_all x1, blocking collectives, shards(): lax.all_to_all(table.reshape(devices, slots, queries), 'dp', 0, 0, tiled=...  11.3 us
    unnamed x20, local copies, waits for them, and re-layouts  8.51 us
  transfers between devices with their start and end apart: 18, of which 14 were waited for; matrix products, arithmetic and copies ran while one was open for 1% of the time, Pallas kernels for 30%

profile of v5, /device:TPU:0, one launch (start us, length us, event | category | flops | bytes accessed | tf_op | source)
XLA Modules:
  0.0 139.7 jit_solution(3495673477137942526)
XLA Ops:
  0.0 0.5 collective-permute-start.7
  0.5 0.1 collective-permute-start.8
  0.5 21.0 %join.1.refs_4_ = bf16[1280,256]{1,0:T(8,128)(2,1)} custom-call(bf16[512,256]{1,0:T(8,128)(2,1)} %in_ref.1, bf16[2048,256]{1,0:T(8,128)(2,1)} %out_ref.1), custom_call_target="tpu_custom_call" | custom-call | bytes 1310720 | tf_op jit(solution)/shard_map/join/pallas_call | solution.py:130
  21.5 3.0 %collective-permute-start.4 = (bf16[1280,256]{1,0:T(8,128)(2,1)}, bf16[1280,256]{1,0:T(8,128)(2,1)S(1)}, u32[]{:S(2)}, u32[]{:S(2)}) collective-permute-start(bf16[1280,256]{1,0:T(8,128)(2,1)} %join.1.refs_4_), channel_id=1, source_target_pairs={{2,6},{3,1},{6,10},{7,3},{10,14},{11,7},{14,12},{15,11},{12,8},{13... | collective-permute-start | bytes 1966088 | tf_op jit(solution)/shard_map/ppermute | solution.py:230
  24.5 1.1 slice.3.refs_5_
  25.6 1.6 %collective-permute-start.1 = (bf16[1280,256]{1,0:T(8,128)(2,1)S(1)}, bf16[1280,256]{1,0:T(8,128)(2,1)S(1)}, u32[]{:S(2)}, u32[]{:S(2)}) collective-permute-start(bf16[1280,256]{1,0:T(8,128)(2,1)S(1)} %slice.3.refs_5_), channel_id=1, source_target_pairs={{2,6},{3,1},{6,10},{7,3},{10,14},{11,7},{14,12},{15,11},{12,8},{13... | collective-permute-start | bytes 1966088 | tf_op jit(solution)/shard_map/ppermute | solution.py:230
  27.3 6.1 %collective-permute-done.4.refs_4_ = bf16[1280,256]{1,0:T(8,128)(2,1)S(1)} collective-permute-done((bf16[1280,256]{1,0:T(8,128)(2,1)}, bf16[1280,256]{1,0:T(8,128)(2,1)S(1)}, u32[]{:S(2)}, u32[]{:S(2)}) %collective-permute-start.4) | collective-permute-done | bytes 655392 | tf_op jit(solution)/shard_map/ppermute | solution.py:230
  33.3 2.0 %collective-permute-start.5 = (bf16[1280,256]{1,0:T(8,128)(2,1)S(1)}, bf16[1280,256]{1,0:T(8,128)(2,1)}, u32[]{:S(2)}, u32[]{:S(2)}) collective-permute-start(bf16[1280,256]{1,0:T(8,128)(2,1)S(1)} %collective-permute-done.4.refs_4_), channel_id=1, source_target_pairs={{2,6},{3,1},{6,10},{7,3},{10,14},{11,7},{14,12},{15,11},{12,8},{13... | collective-permute-start | bytes 1966088 | tf_op jit(solution)/shard_map/ppermute | solution.py:230
  35.3 0.0 copy-start.4
  35.3 0.8 copy-done.4
  36.2 4.2 %collective-permute-done.1.refs_5_ = bf16[1280,256]{1,0:T(8,128)(2,1)S(1)} collective-permute-done((bf16[1280,256]{1,0:T(8,128)(2,1)S(1)}, bf16[1280,256]{1,0:T(8,128)(2,1)S(1)}, u32[]{:S(2)}, u32[]{:S(2)}) %collective-permute-start.1) | collective-permute-done | bytes 655392 | tf_op jit(solution)/shard_map/ppermute | solution.py:230
  40.4 2.0 %collective-permute-start.2 = (bf16[1280,256]{1,0:T(8,128)(2,1)S(1)}, bf16[1280,256]{1,0:T(8,128)(2,1)}, u32[]{:S(2)}, u32[]{:S(2)}) collective-permute-start(bf16[1280,256]{1,0:T(8,128)(2,1)S(1)} %collective-permute-done.1.refs_5_), channel_id=1, source_target_pairs={{2,6},{3,1},{6,10},{7,3},{10,14},{11,7},{14,12},{15,11},{12,8},{13... | collective-permute-start | bytes 1966088 | tf_op jit(solution)/shard_map/ppermute | solution.py:230
  42.3 0.0 copy-start.6
  42.3 0.8 copy-done.6
  43.2 4.3 %collective-permute-done.5.refs_4_ = bf16[1280,256]{1,0:T(8,128)(2,1)} collective-permute-done((bf16[1280,256]{1,0:T(8,128)(2,1)S(1)}, bf16[1280,256]{1,0:T(8,128)(2,1)}, u32[]{:S(2)}, u32[]{:S(2)}) %collective-permute-start.5) | collective-permute-done | bytes 655392 | tf_op jit(solution)/shard_map/ppermute | solution.py:230
  47.5 2.0 %collective-permute-start.6 = (bf16[1280,256]{1,0:T(8,128)(2,1)}, bf16[1280,256]{1,0:T(8,128)(2,1)}, u32[]{:S(2)}, u32[]{:S(2)}) collective-permute-start(bf16[1280,256]{1,0:T(8,128)(2,1)} %collective-permute-done.5.refs_4_), channel_id=1, source_target_pairs={{2,6},{3,1},{6,10},{7,3},{10,14},{11,7},{14,12},{15,11},{12,8},{13... | collective-permute-start | bytes 1966088 | tf_op jit(solution)/shard_map/ppermute | solution.py:230
  49.5 5.1 %collective-permute-done.2.refs_5_ = bf16[1280,256]{1,0:T(8,128)(2,1)} collective-permute-done((bf16[1280,256]{1,0:T(8,128)(2,1)S(1)}, bf16[1280,256]{1,0:T(8,128)(2,1)}, u32[]{:S(2)}, u32[]{:S(2)}) %collective-permute-start.2) | collective-permute-done | bytes 655392 | tf_op jit(solution)/shard_map/ppermute | solution.py:230
  54.5 2.0 %collective-permute-start.3 = (bf16[1280,256]{1,0:T(8,128)(2,1)}, bf16[1280,256]{1,0:T(8,128)(2,1)}, u32[]{:S(2)}, u32[]{:S(2)}) collective-permute-start(bf16[1280,256]{1,0:T(8,128)(2,1)} %collective-permute-done.2.refs_5_), channel_id=1, source_target_pairs={{2,6},{3,1},{6,10},{7,3},{10,14},{11,7},{14,12},{15,11},{12,8},{13... | collective-permute-start | bytes 1966088 | tf_op jit(solution)/shard_map/ppermute | solution.py:230
  56.5 0.7 dynamic-slice_bitcast_fusion.order_ref
  57.2 0.0 collective-permute-done.8.refs_3_
  57.2 0.0 collective-permute-done.7.refs_1_.sib_ref
  57.2 0.0 copy-start
  57.2 4.0 %copy-done = bf16[160,32768]{1,0:T(8,128)(2,1)S(1)} copy-done((bf16[160,32768]{1,0:T(8,128)(2,1)S(1)}, bf16[160,32768]{1,0:T(8,128)(2,1)}, u32[]{:S(2)}) %copy-start) | copy-done | bytes 10485784
  61.2 1.7 %copy-done.1 = bf16[160,8192]{1,0:T(8,128)(2,1)S(1)} copy-done((bf16[160,8192]{1,0:T(8,128)(2,1)S(1)}, bf16[160,8192]{1,0:T(8,128)(2,1)}, u32[]{:S(2)}) %copy-start.1) | copy-done | bytes 2621464
  62.9 1.1 copy-done.3
  64.0 2.6 %step.8 = (f32[320,256]{1,0:T(8,128)S(1)}, f32[320,256]{1,0:T(8,128)S(1)}) custom-call(s32[8]{0:T(128)S(1)} %dynamic-slice_bitcast_fusion.order_ref, bf16[160,32768]{1,0:T(8,128)(2,1)S(1)} %copy-done, bf16[160,32768]{1,0:T(8,128)(2,1)} %collective-permute-done.7.refs_1_.sib_ref, bf16[160,8192]{1,0:T(8,128)(2,1)S(1)} %copy-done.1, ...), custom_call_target="tpu_custom_call" | custom-call | flops 419430400 | bytes 3604480 | tf_op jit(solution)/shard_map/step/pallas_call | solution.py:59
  66.6 0.0 collective-permute-done.6.refs_4_
  66.6 1.6 %collective-permute-start.10 = (bf16[1280,256]{1,0:T(8,128)(2,1)}, bf16[1280,256]{1,0:T(8,128)(2,1)S(1)}, u32[]{:S(2)}, u32[]{:S(2)}) collective-permute-start(bf16[1280,256]{1,0:T(8,128)(2,1)} %collective-permute-done.6.refs_4_), channel_id=1, source_target_pairs={{2,6},{3,1},{6,10},{7,3},{10,14},{11,7},{14,12},{15,11},{12,8},{13... | collective-permute-start | bytes 1966088 | tf_op jit(solution)/shard_map/ppermute | solution.py:230
  68.2 0.4 collective-permute-done.3.refs_5_
  68.6 2.0 %collective-permute-start.9 = (bf16[1280,256]{1,0:T(8,128)(2,1)}, bf16[1280,256]{1,0:T(8,128)(2,1)S(1)}, u32[]{:S(2)}, u32[]{:S(2)}) collective-permute-start(bf16[1280,256]{1,0:T(8,128)(2,1)} %collective-permute-done.3.refs_5_), channel_id=1, source_target_pairs={{2,6},{3,1},{6,10},{7,3},{10,14},{11,7},{14,12},{15,11},{12,8},{13... | collective-permute-start | bytes 1966088 | tf_op jit(solution)/shard_map/ppermute | solution.py:230
  70.5 0.0 copy-done.2
  70.5 0.0 copy-done.5
  70.5 0.0 copy-done.7
  70.5 2.3 %step.9 = (f32[320,256]{1,0:T(8,128)S(1)}, f32[320,256]{1,0:T(8,128)S(1)}) custom-call(s32[8]{0:T(128)S(1)} %dynamic-slice_bitcast_fusion.order_ref, bf16[160,32768]{1,0:T(8,128)(2,1)S(1)} %copy-done, bf16[160,32768]{1,0:T(8,128)(2,1)} %collective-permute-done.7.refs_1_.sib_ref, bf16[160,8192]{1,0:T(8,128)(2,1)S(1)} %copy-done.2, ...), custom_call_target="tpu_custom_call" | custom-call | flops 419430400 | bytes 4259840 | tf_op jit(solution)/shard_map/step/pallas_call | solution.py:59
  72.8 2.6 %step.10 = (f32[320,256]{1,0:T(8,128)S(1)}, f32[320,256]{1,0:T(8,128)S(1)}) custom-call(s32[8]{0:T(128)S(1)} %dynamic-slice_bitcast_fusion.order_ref, bf16[160,32768]{1,0:T(8,128)(2,1)S(1)} %copy-done, bf16[160,32768]{1,0:T(8,128)(2,1)} %collective-permute-done.7.refs_1_.sib_ref, bf16[160,8192]{1,0:T(8,128)(2,1)S(1)} %copy-done.2, ...), custom_call_target="tpu_custom_call" | custom-call | flops 419430400 | bytes 4259840 | tf_op jit(solution)/shard_map/step/pallas_call | solution.py:59
  75.5 1.9 %collective-permute-done.10.refs_4_ = bf16[1280,256]{1,0:T(8,128)(2,1)S(1)} collective-permute-done((bf16[1280,256]{1,0:T(8,128)(2,1)}, bf16[1280,256]{1,0:T(8,128)(2,1)S(1)}, u32[]{:S(2)}, u32[]{:S(2)}) %collective-permute-start.10) | collective-permute-done | bytes 655392 | tf_op jit(solution)/shard_map/ppermute | solution.py:230
  77.4 1.6 %collective-permute-start.12 = (bf16[1280,256]{1,0:T(8,128)(2,1)S(1)}, bf16[1280,256]{1,0:T(8,128)(2,1)S(1)}, u32[]{:S(2)}, u32[]{:S(2)}) collective-permute-start(bf16[1280,256]{1,0:T(8,128)(2,1)S(1)} %collective-permute-done.10.refs_4_), channel_id=1, source_target_pairs={{2,6},{3,1},{6,10},{7,3},{10,14},{11,7},{14,12},{15,11},{12,8},{13... | collective-permute-start | bytes 1966088 | tf_op jit(solution)/shard_map/ppermute | solution.py:230
  79.0 5.4 %collective-permute-done.9.refs_5_ = bf16[1280,256]{1,0:T(8,128)(2,1)S(1)} collective-permute-done((bf16[1280,256]{1,0:T(8,128)(2,1)}, bf16[1280,256]{1,0:T(8,128)(2,1)S(1)}, u32[]{:S(2)}, u32[]{:S(2)}) %collective-permute-start.9) | collective-permute-done | bytes 655392 | tf_op jit(solution)/shard_map/ppermute | solution.py:230
  84.4 1.6 %collective-permute-start.11 = (bf16[1280,256]{1,0:T(8,128)(2,1)S(1)}, bf16[1280,256]{1,0:T(8,128)(2,1)S(1)}, u32[]{:S(2)}, u32[]{:S(2)}) collective-permute-start(bf16[1280,256]{1,0:T(8,128)(2,1)S(1)} %collective-permute-done.9.refs_5_), channel_id=1, source_target_pairs={{2,6},{3,1},{6,10},{7,3},{10,14},{11,7},{14,12},{15,11},{12,8},{13... | collective-permute-start | bytes 1966088 | tf_op jit(solution)/shard_map/ppermute | solution.py:230
  86.0 2.6 %step.11 = (f32[320,256]{1,0:T(8,128)S(1)}, f32[320,256]{1,0:T(8,128)S(1)}) custom-call(s32[8]{0:T(128)S(1)} %dynamic-slice_bitcast_fusion.order_ref, bf16[160,32768]{1,0:T(8,128)(2,1)S(1)} %copy-done, bf16[160,32768]{1,0:T(8,128)(2,1)} %collective-permute-done.7.refs_1_.sib_ref, bf16[160,8192]{1,0:T(8,128)(2,1)S(1)} %copy-done.2, ...), custom_call_target="tpu_custom_call" | custom-call | flops 419430400 | bytes 4259840 | tf_op jit(solution)/shard_map/step/pallas_call | solution.py:59
  88.7 2.3 %step.12 = (f32[320,256]{1,0:T(8,128)S(1)}, f32[320,256]{1,0:T(8,128)S(1)}) custom-call(s32[8]{0:T(128)S(1)} %dynamic-slice_bitcast_fusion.order_ref, bf16[160,32768]{1,0:T(8,128)(2,1)S(1)} %copy-done, bf16[160,32768]{1,0:T(8,128)(2,1)} %collective-permute-done.7.refs_1_.sib_ref, bf16[160,8192]{1,0:T(8,128)(2,1)S(1)} %copy-done.2, ...), custom_call_target="tpu_custom_call" | custom-call | flops 419430400 | bytes 4259840 | tf_op jit(solution)/shard_map/step/pallas_call | solution.py:59
  91.0 0.5 collective-permute-done.12.refs_4_
  91.5 1.6 %collective-permute-start.14 = (bf16[1280,256]{1,0:T(8,128)(2,1)S(1)}, bf16[1280,256]{1,0:T(8,128)(2,1)S(1)}, u32[]{:S(2)}, u32[]{:S(2)}) collective-permute-start(bf16[1280,256]{1,0:T(8,128)(2,1)S(1)} %collective-permute-done.12.refs_4_), channel_id=1, source_target_pairs={{2,6},{3,1},{6,10},{7,3},{10,14},{11,7},{14,12},{15,11},{12,8},{13... | collective-permute-start | bytes 1966088 | tf_op jit(solution)/shard_map/ppermute | solution.py:230
  93.0 5.4 %collective-permute-done.11.refs_5_ = bf16[1280,256]{1,0:T(8,128)(2,1)S(1)} collective-permute-done((bf16[1280,256]{1,0:T(8,128)(2,1)S(1)}, bf16[1280,256]{1,0:T(8,128)(2,1)S(1)}, u32[]{:S(2)}, u32[]{:S(2)}) %collective-permute-start.11) | collective-permute-done | bytes 655392 | tf_op jit(solution)/shard_map/ppermute | solution.py:230
  98.5 1.6 %collective-permute-start.13 = (bf16[1280,256]{1,0:T(8,128)(2,1)S(1)}, bf16[1280,256]{1,0:T(8,128)(2,1)S(1)}, u32[]{:S(2)}, u32[]{:S(2)}) collective-permute-start(bf16[1280,256]{1,0:T(8,128)(2,1)S(1)} %collective-permute-done.11.refs_5_), channel_id=1, source_target_pairs={{2,6},{3,1},{6,10},{7,3},{10,14},{11,7},{14,12},{15,11},{12,8},{13... | collective-permute-start | bytes 1966088 | tf_op jit(solution)/shard_map/ppermute | solution.py:230
  100.1 2.3 %step.13 = (f32[320,256]{1,0:T(8,128)S(1)}, f32[320,256]{1,0:T(8,128)S(1)}) custom-call(s32[8]{0:T(128)S(1)} %dynamic-slice_bitcast_fusion.order_ref, bf16[160,32768]{1,0:T(8,128)(2,1)S(1)} %copy-done, bf16[160,32768]{1,0:T(8,128)(2,1)} %collective-permute-done.7.refs_1_.sib_ref, bf16[160,8192]{1,0:T(8,128)(2,1)S(1)} %copy-done.2, ...), custom_call_target="tpu_custom_call" | custom-call | flops 419430400 | bytes 4259840 | tf_op jit(solution)/shard_map/step/pallas_call | solution.py:59
  102.4 3.1 %collective-permute-done.14.refs_4_ = bf16[1280,256]{1,0:T(8,128)(2,1)S(1)} collective-permute-done((bf16[1280,256]{1,0:T(8,128)(2,1)S(1)}, bf16[1280,256]{1,0:T(8,128)(2,1)S(1)}, u32[]{:S(2)}, u32[]{:S(2)}) %collective-permute-start.14) | collective-permute-done | bytes 655392 | tf_op jit(solution)/shard_map/ppermute | solution.py:230
  105.5 1.6 %collective-permute-start.16 = (bf16[1280,256]{1,0:T(8,128)(2,1)S(1)}, bf16[1280,256]{1,0:T(8,128)(2,1)S(1)}, u32[]{:S(2)}, u32[]{:S(2)}) collective-permute-start(bf16[1280,256]{1,0:T(8,128)(2,1)S(1)} %collective-permute-done.14.refs_4_), channel_id=1, source_target_pairs={{2,6},{3,1},{6,10},{7,3},{10,14},{11,7},{14,12},{15,11},{12,8},{13... | collective-permute-start | bytes 1966088 | tf_op jit(solution)/shard_map/ppermute | solution.py:230
  107.1 5.4 %collective-permute-done.13.refs_5_ = bf16[1280,256]{1,0:T(8,128)(2,1)S(1)} collective-permute-done((bf16[1280,256]{1,0:T(8,128)(2,1)S(1)}, bf16[1280,256]{1,0:T(8,128)(2,1)S(1)}, u32[]{:S(2)}, u32[]{:S(2)}) %collective-permute-start.13) | collective-permute-done | bytes 655392 | tf_op jit(solution)/shard_map/ppermute | solution.py:230
  112.5 1.6 %collective-permute-start.15 = (bf16[1280,256]{1,0:T(8,128)(2,1)S(1)}, bf16[1280,256]{1,0:T(8,128)(2,1)S(1)}, u32[]{:S(2)}, u32[]{:S(2)}) collective-permute-start(bf16[1280,256]{1,0:T(8,128)(2,1)S(1)} %collective-permute-done.13.refs_5_), channel_id=1, source_target_pairs={{2,6},{3,1},{6,10},{7,3},{10,14},{11,7},{14,12},{15,11},{12,8},{13... | collective-permute-start | bytes 1966088 | tf_op jit(solution)/shard_map/ppermute | solution.py:230
  114.1 1.7 %window.1.window_ref = bf16[320,1280]{1,0:T(8,128)(2,1)S(1)} custom-call(s32[8]{0:T(128)S(1)} %dynamic-slice_bitcast_fusion.order_ref, bf16[160,32768]{1,0:T(8,128)(2,1)S(1)} %copy-done, bf16[160,32768]{1,0:T(8,128)(2,1)} %collective-permute-done.7.refs_1_.sib_ref), custom_call_target="tpu_custom_call" | custom-call | bytes 2129920 | tf_op jit(solution)/shard_map/window/pallas_call | solution.py:59
  115.8 2.3 %step.14 = (f32[320,256]{1,0:T(8,128)S(1)}, f32[320,256]{1,0:T(8,128)S(1)}) custom-call(s32[8]{0:T(128)S(1)} %dynamic-slice_bitcast_fusion.order_ref, bf16[160,32768]{1,0:T(8,128)(2,1)S(1)} %copy-done, bf16[160,32768]{1,0:T(8,128)(2,1)} %collective-permute-done.7.refs_1_.sib_ref, bf16[160,8192]{1,0:T(8,128)(2,1)S(1)} %copy-done.2, ...), custom_call_target="tpu_custom_call" | custom-call | flops 419430400 | bytes 4259840 | tf_op jit(solution)/shard_map/step/pallas_call | solution.py:59
  118.1 1.4 %collective-permute-done.16.refs_4_ = bf16[1280,256]{1,0:T(8,128)(2,1)S(1)} collective-permute-done((bf16[1280,256]{1,0:T(8,128)(2,1)S(1)}, bf16[1280,256]{1,0:T(8,128)(2,1)S(1)}, u32[]{:S(2)}, u32[]{:S(2)}) %collective-permute-start.16) | collective-permute-done | bytes 655392 | tf_op jit(solution)/shard_map/ppermute | solution.py:230
  119.6 2.0 %step.15 = (f32[320,256]{1,0:T(8,128)S(1)}, f32[320,256]{1,0:T(8,128)S(1)}) custom-call(s32[8]{0:T(128)S(1)} %dynamic-slice_bitcast_fusion.order_ref, bf16[160,32768]{1,0:T(8,128)(2,1)S(1)} %copy-done, bf16[160,32768]{1,0:T(8,128)(2,1)} %collective-permute-done.7.refs_1_.sib_ref, bf16[160,8192]{1,0:T(8,128)(2,1)S(1)} %copy-done.2, ...), custom_call_target="tpu_custom_call" | custom-call | flops 209715200 | bytes 3604480 | tf_op jit(solution)/shard_map/step/pallas_call | solution.py:59
  121.6 0.1 collective-permute-start.17
  121.7 0.0 copy-done.8
  121.7 0.0 copy-done.9
  121.7 0.5 collective-permute-start
  122.2 1.0 collective-permute-done
  123.3 3.3 %collective-permute-done.15.b_ref = bf16[1280,256]{1,0:T(8,128)(2,1)S(1)} collective-permute-done((bf16[1280,256]{1,0:T(8,128)(2,1)S(1)}, bf16[1280,256]{1,0:T(8,128)(2,1)S(1)}, u32[]{:S(2)}, u32[]{:S(2)}) %collective-permute-start.15) | collective-permute-done | bytes 655392 | tf_op jit(solution)/shard_map/ppermute | solution.py:230
  126.6 0.0 collective-permute-done.17.got_ref
  126.6 1.2 score.1
  127.8 11.3 %all_to_all.5 = f32[16,2,8]{2,1,0:T(2,128)S(1)} all-to-all(f32[16,2,8]{2,1,0:T(2,128)S(1)} %bitcast.9), channel_id=1, replica_groups=mesh['groups'=2,'dp'=16] {'dp'}, dimensions={0} | all-to-all | bytes 2048 | tf_op jit(solution)/shard_map/all_to_all | solution.py:251
  139.1 0.6 reduce_sum.9
  (9 shorter events, 0.0 us)
Async XLA Ops:
  0.0 57.2 %collective-permute-start.7 = (bf16[160,32768]{1,0:T(8,128)(2,1)}, bf16[160,32768]{1,0:T(8,128)(2,1)}, u32[]{:S(2)}, u32[]{:S(2)}) collective-permute-start(bf16[160,32768]{1,0:T(8,128)(2,1)} %refs_0_.15), channel_id=1, source_target_pairs={{0,1},{1,0},{2,3},{3,2},{4,5},{5,4},{6,7},{7,6},{8,9},{9,8},{10,11... | collective-permute-start | bytes 31457288 | tf_op jit(solution)/shard_map/ppermute | solution.py:216
  0.5 56.7 %collective-permute-start.8 = (bf16[160,8192]{1,0:T(8,128)(2,1)}, bf16[160,8192]{1,0:T(8,128)(2,1)S(1)}, u32[]{:S(2)}, u32[]{:S(2)}) collective-permute-start(bf16[160,8192]{1,0:T(8,128)(2,1)} %refs_2_.15), channel_id=1, source_target_pairs={{0,1},{1,0},{2,3},{3,2},{4,5},{5,4},{6,7},{7,6},{8,9},{9,8},{10,11... | collective-permute-start | bytes 7864328 | tf_op jit(solution)/shard_map/ppermute | solution.py:216
  21.5 11.9 %collective-permute-start.4 = (bf16[1280,256]{1,0:T(8,128)(2,1)}, bf16[1280,256]{1,0:T(8,128)(2,1)S(1)}, u32[]{:S(2)}, u32[]{:S(2)}) collective-permute-start(bf16[1280,256]{1,0:T(8,128)(2,1)} %join.1.refs_4_), channel_id=1, source_target_pairs={{2,6},{3,1},{6,10},{7,3},{10,14},{11,7},{14,12},{15,11},{12,8},{13... | collective-permute-start | bytes 1966088 | tf_op jit(solution)/shard_map/ppermute | solution.py:230
  25.6 14.7 %collective-permute-start.1 = (bf16[1280,256]{1,0:T(8,128)(2,1)S(1)}, bf16[1280,256]{1,0:T(8,128)(2,1)S(1)}, u32[]{:S(2)}, u32[]{:S(2)}) collective-permute-start(bf16[1280,256]{1,0:T(8,128)(2,1)S(1)} %slice.3.refs_5_), channel_id=1, source_target_pairs={{2,6},{3,1},{6,10},{7,3},{10,14},{11,7},{14,12},{15,11},{12,8},{13... | collective-permute-start | bytes 1966088 | tf_op jit(solution)/shard_map/ppermute | solution.py:230
  33.3 14.1 %collective-permute-start.5 = (bf16[1280,256]{1,0:T(8,128)(2,1)S(1)}, bf16[1280,256]{1,0:T(8,128)(2,1)}, u32[]{:S(2)}, u32[]{:S(2)}) collective-permute-start(bf16[1280,256]{1,0:T(8,128)(2,1)S(1)} %collective-permute-done.4.refs_4_), channel_id=1, source_target_pairs={{2,6},{3,1},{6,10},{7,3},{10,14},{11,7},{14,12},{15,11},{12,8},{13... | collective-permute-start | bytes 1966088 | tf_op jit(solution)/shard_map/ppermute | solution.py:230
  35.3 0.8 copy-start.4
  40.4 14.1 %collective-permute-start.2 = (bf16[1280,256]{1,0:T(8,128)(2,1)S(1)}, bf16[1280,256]{1,0:T(8,128)(2,1)}, u32[]{:S(2)}, u32[]{:S(2)}) collective-permute-start(bf16[1280,256]{1,0:T(8,128)(2,1)S(1)} %collective-permute-done.1.refs_5_), channel_id=1, source_target_pairs={{2,6},{3,1},{6,10},{7,3},{10,14},{11,7},{14,12},{15,11},{12,8},{13... | collective-permute-start | bytes 1966088 | tf_op jit(solution)/shard_map/ppermute | solution.py:230
  42.3 0.8 copy-start.6
  47.5 19.1 %collective-permute-start.6 = (bf16[1280,256]{1,0:T(8,128)(2,1)}, bf16[1280,256]{1,0:T(8,128)(2,1)}, u32[]{:S(2)}, u32[]{:S(2)}) collective-permute-start(bf16[1280,256]{1,0:T(8,128)(2,1)} %collective-permute-done.5.refs_4_), channel_id=1, source_target_pairs={{2,6},{3,1},{6,10},{7,3},{10,14},{11,7},{14,12},{15,11},{12,8},{13... | collective-permute-start | bytes 1966088 | tf_op jit(solution)/shard_map/ppermute | solution.py:230
  54.5 14.0 %collective-permute-start.3 = (bf16[1280,256]{1,0:T(8,128)(2,1)}, bf16[1280,256]{1,0:T(8,128)(2,1)}, u32[]{:S(2)}, u32[]{:S(2)}) collective-permute-start(bf16[1280,256]{1,0:T(8,128)(2,1)} %collective-permute-done.2.refs_5_), channel_id=1, source_target_pairs={{2,6},{3,1},{6,10},{7,3},{10,14},{11,7},{14,12},{15,11},{12,8},{13... | collective-permute-start | bytes 1966088 | tf_op jit(solution)/shard_map/ppermute | solution.py:230
  57.2 4.0 %copy-start = (bf16[160,32768]{1,0:T(8,128)(2,1)S(1)}, bf16[160,32768]{1,0:T(8,128)(2,1)}, u32[]{:S(2)}) copy-start(bf16[160,32768]{1,0:T(8,128)(2,1)} %refs_0_.15) | copy-start | bytes 31457284
  61.2 1.7 %copy-start.1 = (bf16[160,8192]{1,0:T(8,128)(2,1)S(1)}, bf16[160,8192]{1,0:T(8,128)(2,1)}, u32[]{:S(2)}) copy-start(bf16[160,8192]{1,0:T(8,128)(2,1)} %refs_2_.15) | copy-start | bytes 7864324
  62.9 1.1 copy-start.3
  64.0 6.5 %copy-start.2 = (bf16[160,8192]{1,0:T(8,128)(2,1)S(1)}, bf16[160,8192]{1,0:T(8,128)(2,1)}, u32[]{:S(2)}) copy-start(bf16[160,8192]{1,0:T(8,128)(2,1)} %refs_2_.15) | copy-start | bytes 7864324
  64.0 6.5 %copy-start.5 = (bf16[1280,256]{1,0:T(8,128)(2,1)S(1)}, bf16[1280,256]{1,0:T(8,128)(2,1)}, u32[]{:S(2)}) copy-start(bf16[1280,256]{1,0:T(8,128)(2,1)} %copy-done.4) | copy-start | bytes 1966084
  64.0 6.5 %copy-start.7 = (bf16[1280,256]{1,0:T(8,128)(2,1)S(1)}, bf16[1280,256]{1,0:T(8,128)(2,1)}, u32[]{:S(2)}) copy-start(bf16[1280,256]{1,0:T(8,128)(2,1)} %copy-done.6) | copy-start | bytes 1966084
  66.6 10.8 %collective-permute-start.10 = (bf16[1280,256]{1,0:T(8,128)(2,1)}, bf16[1280,256]{1,0:T(8,128)(2,1)S(1)}, u32[]{:S(2)}, u32[]{:S(2)}) collective-permute-start(bf16[1280,256]{1,0:T(8,128)(2,1)} %collective-permute-done.6.refs_4_), channel_id=1, source_target_pairs={{2,6},{3,1},{6,10},{7,3},{10,14},{11,7},{14,12},{15,11},{12,8},{13... | collective-permute-start | bytes 1966088 | tf_op jit(solution)/shard_map/ppermute | solution.py:230
  68.6 15.9 %collective-permute-start.9 = (bf16[1280,256]{1,0:T(8,128)(2,1)}, bf16[1280,256]{1,0:T(8,128)(2,1)S(1)}, u32[]{:S(2)}, u32[]{:S(2)}) collective-permute-start(bf16[1280,256]{1,0:T(8,128)(2,1)} %collective-permute-done.3.refs_5_), channel_id=1, source_target_pairs={{2,6},{3,1},{6,10},{7,3},{10,14},{11,7},{14,12},{15,11},{12,8},{13... | collective-permute-start | bytes 1966088 | tf_op jit(solution)/shard_map/ppermute | solution.py:230
  77.4 14.0 %collective-permute-start.12 = (bf16[1280,256]{1,0:T(8,128)(2,1)S(1)}, bf16[1280,256]{1,0:T(8,128)(2,1)S(1)}, u32[]{:S(2)}, u32[]{:S(2)}) collective-permute-start(bf16[1280,256]{1,0:T(8,128)(2,1)S(1)} %collective-permute-done.10.refs_4_), channel_id=1, source_target_pairs={{2,6},{3,1},{6,10},{7,3},{10,14},{11,7},{14,12},{15,11},{12,8},{13... | collective-permute-start | bytes 1966088 | tf_op jit(solution)/shard_map/ppermute | solution.py:230
  84.4 14.0 %collective-permute-start.11 = (bf16[1280,256]{1,0:T(8,128)(2,1)S(1)}, bf16[1280,256]{1,0:T(8,128)(2,1)S(1)}, u32[]{:S(2)}, u32[]{:S(2)}) collective-permute-start(bf16[1280,256]{1,0:T(8,128)(2,1)S(1)} %collective-permute-done.9.refs_5_), channel_id=1, source_target_pairs={{2,6},{3,1},{6,10},{7,3},{10,14},{11,7},{14,12},{15,11},{12,8},{13... | collective-permute-start | bytes 1966088 | tf_op jit(solution)/shard_map/ppermute | solution.py:230
  91.5 14.0 %collective-permute-start.14 = (bf16[1280,256]{1,0:T(8,128)(2,1)S(1)}, bf16[1280,256]{1,0:T(8,128)(2,1)S(1)}, u32[]{:S(2)}, u32[]{:S(2)}) collective-permute-start(bf16[1280,256]{1,0:T(8,128)(2,1)S(1)} %collective-permute-done.12.refs_4_), channel_id=1, source_target_pairs={{2,6},{3,1},{6,10},{7,3},{10,14},{11,7},{14,12},{15,11},{12,8},{13... | collective-permute-start | bytes 1966088 | tf_op jit(solution)/shard_map/ppermute | solution.py:230
  98.5 14.0 %collective-permute-start.13 = (bf16[1280,256]{1,0:T(8,128)(2,1)S(1)}, bf16[1280,256]{1,0:T(8,128)(2,1)S(1)}, u32[]{:S(2)}, u32[]{:S(2)}) collective-permute-start(bf16[1280,256]{1,0:T(8,128)(2,1)S(1)} %collective-permute-done.11.refs_5_), channel_id=1, source_target_pairs={{2,6},{3,1},{6,10},{7,3},{10,14},{11,7},{14,12},{15,11},{12,8},{13... | collective-permute-start | bytes 1966088 | tf_op jit(solution)/shard_map/ppermute | solution.py:230
  105.5 14.0 %collective-permute-start.16 = (bf16[1280,256]{1,0:T(8,128)(2,1)S(1)}, bf16[1280,256]{1,0:T(8,128)(2,1)S(1)}, u32[]{:S(2)}, u32[]{:S(2)}) collective-permute-start(bf16[1280,256]{1,0:T(8,128)(2,1)S(1)} %collective-permute-done.14.refs_4_), channel_id=1, source_target_pairs={{2,6},{3,1},{6,10},{7,3},{10,14},{11,7},{14,12},{15,11},{12,8},{13... | collective-permute-start | bytes 1966088 | tf_op jit(solution)/shard_map/ppermute | solution.py:230
  112.5 14.0 %collective-permute-start.15 = (bf16[1280,256]{1,0:T(8,128)(2,1)S(1)}, bf16[1280,256]{1,0:T(8,128)(2,1)S(1)}, u32[]{:S(2)}, u32[]{:S(2)}) collective-permute-start(bf16[1280,256]{1,0:T(8,128)(2,1)S(1)} %collective-permute-done.13.refs_5_), channel_id=1, source_target_pairs={{2,6},{3,1},{6,10},{7,3},{10,14},{11,7},{14,12},{15,11},{12,8},{13... | collective-permute-start | bytes 1966088 | tf_op jit(solution)/shard_map/ppermute | solution.py:230
  119.6 2.1 %copy-start.8 = (s32[2]{0:T(128)S(1)}, s32[2]{0:T(128)}, u32[]{:S(2)}) copy-start(s32[2]{0:T(128)} %seq_ref.1) | copy-start | bytes 28
  119.6 2.1 %copy-start.9 = (s32[2]{0:T(128)S(1)}, s32[2]{0:T(128)}, u32[]{:S(2)}) copy-start(s32[2]{0:T(128)} %len_ref.1) | copy-start | bytes 28
  121.6 5.0 %collective-permute-start.17 = (f32[320,256]{1,0:T(8,128)S(1)}, f32[320,256]{1,0:T(8,128)S(1)}, u32[]{:S(2)}, u32[]{:S(2)}) collective-permute-start(f32[320,256]{1,0:T(8,128)S(1)} %get-tuple-element.88.inn_ref), channel_id=1, source_target_pairs={{0,1},{1,0},{2,3},{3,2},{4,5},{5,4},{6,7},{7,6},{8,9},{9,8},{10,11... | collective-permute-start | bytes 983048 | tf_op jit(solution)/shard_map/ppermute | solution.py:244
  121.7 1.6 %collective-permute-start = (s32[2,2]{1,0:T(2,128)S(1)}, s32[2,2]{1,0:T(2,128)S(1)}, u32[]{:S(2)}, u32[]{:S(2)}) collective-permute-start(s32[2,2]{1,0:T(2,128)S(1)} %pad_add_fusion), channel_id=1, source_target_pairs={{0,1},{1,0},{2,3},{3,2},{4,5},{5,4},{6,7},{7,6},{8,9},{9,8},{10,11... | collective-permute-start | bytes 56 | tf_op jit(solution)/shard_map/ppermute | solution.py:215

commit v6 on v5

--- a/solution.py
+++ b/solution.py
@@ -110,13 +110,13 @@
     )
 
 
-def join_kernel(lead, in_ref, out_ref, joined_ref, sems):
+def join_kernel(in_ref, out_ref, a_ref, b_ref, sems):
     rows_in = in_ref.shape[0]
+    lead, rest = a_ref.shape[0] - rows_in, b_ref.shape[0]
     copies = [
-        pltpu.make_async_copy(in_ref, joined_ref.at[pl.ds(0, rows_in)], sems.at[0]),
-        pltpu.make_async_copy(
-            out_ref.at[pl.ds(0, lead)], joined_ref.at[pl.ds(rows_in, lead)], sems.at[1]
-        ),
+        pltpu.make_async_copy(in_ref, a_ref.at[pl.ds(0, rows_in)], sems.at[0]),
+        pltpu.make_async_copy(out_ref.at[pl.ds(0, lead)], a_ref.at[pl.ds(rows_in, lead)], sems.at[1]),
+        pltpu.make_async_copy(out_ref.at[pl.ds(lead, rest)], b_ref, sems.at[2]),
     ]
     for copy in copies:
         copy.start()
@@ -126,16 +126,17 @@
 
 def join(in_factors, out_factors, lead):
     rows_in, columns = in_factors.shape
-    anywhere = pl.BlockSpec(memory_space=pl.ANY)
+    heights = [rows_in + lead, out_factors.shape[0] - lead]
     return pl.pallas_call(
-        functools.partial(join_kernel, lead),
-        in_specs=[anywhere] * 2,
-        out_specs=anywhere,
-        out_shape=jax.ShapeDtypeStruct((rows_in + lead, columns), in_factors.dtype),
-        scratch_shapes=[pltpu.SemaphoreType.DMA((2,))],
+        join_kernel,
+        in_specs=[pl.BlockSpec(memory_space=pltpu.HBM)] * 2,
+        out_specs=[pl.BlockSpec(memory_space=pltpu.VMEM)] * 2,
+        out_shape=[jax.ShapeDtypeStruct((h, columns), in_factors.dtype) for h in heights],
+        scratch_shapes=[pltpu.SemaphoreType.DMA((3,))],
         cost_estimate=pl.CostEstimate(
-            flops=0, bytes_accessed=4 * (rows_in + lead) * columns, transcendentals=0
-        ),
+            flops=0, bytes_accessed=4 * sum(heights) * columns, transcendentals=0
+        ),
+        compiler_params=pltpu.CompilerParams(vmem_limit_bytes=4 << 20),
         name="join",
     )(in_factors, out_factors)
 
@@ -209,8 +210,10 @@
         every = lax.all_gather(in_factors, "dp", axis=0, tiled=True)
         own, rows_in = own[:1], 0
     lead = (rows - rows_in) // 2
-    first = join(in_factors, out_factors, lead) if rows_in else out_factors[:lead]
-    held = [(first, out_factors[lead:])]
+    if rows_in:
+        held = [join(in_factors, out_factors, lead)]
+    else:
+        held = [(out_factors[:lead], out_factors[lead:])]
 
     seq_sib, len_sib = lax.ppermute(jnp.stack([seq_slot, lengths]), "dp", swap)
     sib = [lax.ppermute(x, "dp", swap) for x in own]

time: 140 us -> 122 us (0.87)
  Pallas kernels: 42.9 us -> 22.4 us
  local copies, waits for them, and re-layouts: 10.3 us -> 12.2 us
    pallas_call x1, Pallas kernels: 21 us -> 0.44 us  [join(): pl.pallas_call(join_kernel, in_specs=[pl.BlockSpec(memory_space=pltpu.HBM...]
    unnamed x20 -> x26, local copies, waits for them, and re-layouts: 8.51 us -> 11.5 us
  transfers between devices with their start and end apart: 18 -> 18, of which waited for: 14 -> 14; matrix products, arithmetic and copies ran while one was open for 1% -> 1% of each run, Pallas kernels for 30% -> 17%
where the time goes in v6:
time: 122 us; the launch traced here: 121 us
  waiting for transfers between devices  47.8 us (39%)
  starting transfers between devices  26.6 us (22%)
  Pallas kernels  22.4 us (18%)
  local copies, waits for them, and re-layouts  12.2 us (10%)
  blocking collectives  11.3 us (9%)
    ppermute x14, waiting for transfers between devices, shards(): held.append((lax.ppermute(a, 'dp', pairs), lax.ppermute(b, 'dp', pairs)))  46.8 us
    ppermute x14, starting transfers between devices, shards(): held.append((lax.ppermute(a, 'dp', pairs), lax.ppermute(b, 'dp', pairs)))  25.5 us
    pallas_call x9, Pallas kernels, call(): pl.pallas_call(kernel, grid_spec=pltpu.PrefetchScalarGridSpec(num_scalar_...  20.8 us
    unnamed x26, local copies, waits for them, and re-layouts  11.5 us
    all_to_all x1, blocking collectives, shards(): lax.all_to_all(table.reshape(devices, slots, queries), 'dp', 0, 0, tiled=...  11.3 us
  transfers between devices with their start and end apart: 18, of which 14 were waited for; matrix products, arithmetic and copies ran while one was open for 1% of the time, Pallas kernels for 17%

profile of v6, /device:TPU:0, one launch (start us, length us, event | category | flops | bytes accessed | tf_op | source)
XLA Modules:
  0.0 121.1 jit_solution(16660413346001845181)
XLA Ops:
  0.0 0.5 collective-permute-start.7
  0.5 0.1 collective-permute-start.8
  0.5 1.2 %copy-done.3 = bf16[2048,256]{1,0:T(8,128)(2,1)S(1)} copy-done((bf16[2048,256]{1,0:T(8,128)(2,1)S(1)}, bf16[2048,256]{1,0:T(8,128)(2,1)}, u32[]{:S(2)}) %copy-start.3) | copy-done | bytes 1048600
  1.7 0.9 copy-done.10
  2.7 0.4 join.1
  3.1 3.0 %collective-permute-start.4 = (bf16[1280,256]{1,0:T(8,128)(2,1)S(1)}, bf16[1280,256]{1,0:T(8,128)(2,1)S(1)}, u32[]{:S(2)}, u32[]{:S(2)}) collective-permute-start(bf16[1280,256]{1,0:T(8,128)(2,1)S(1)} %get-tuple-element.50.refs_4_), channel_id=1, source_target_pairs={{2,6},{3,1},{6,10},{7,3},{10,14},{11,7},{14,12},{15,11},{12,8},{13... | collective-permute-start | bytes 1966088 | tf_op jit(solution)/shard_map/ppermute | solution.py:233
  6.2 1.6 %collective-permute-start.1 = (bf16[1280,256]{1,0:T(8,128)(2,1)S(1)}, bf16[1280,256]{1,0:T(8,128)(2,1)S(1)}, u32[]{:S(2)}, u32[]{:S(2)}) collective-permute-start(bf16[1280,256]{1,0:T(8,128)(2,1)S(1)} %get-tuple-element.49.refs_5_), channel_id=1, source_target_pairs={{2,6},{3,1},{6,10},{7,3},{10,14},{11,7},{14,12},{15,11},{12,8},{13... | collective-permute-start | bytes 1966088 | tf_op jit(solution)/shard_map/ppermute | solution.py:233
  7.7 0.9 copy-done.4
  8.6 6.2 %collective-permute-done.4.refs_4_ = bf16[1280,256]{1,0:T(8,128)(2,1)S(1)} collective-permute-done((bf16[1280,256]{1,0:T(8,128)(2,1)S(1)}, bf16[1280,256]{1,0:T(8,128)(2,1)S(1)}, u32[]{:S(2)}, u32[]{:S(2)}) %collective-permute-start.4) | collective-permute-done | bytes 655392 | tf_op jit(solution)/shard_map/ppermute | solution.py:233
  14.8 2.0 %collective-permute-start.5 = (bf16[1280,256]{1,0:T(8,128)(2,1)S(1)}, bf16[1280,256]{1,0:T(8,128)(2,1)}, u32[]{:S(2)}, u32[]{:S(2)}) collective-permute-start(bf16[1280,256]{1,0:T(8,128)(2,1)S(1)} %collective-permute-done.4.refs_4_), channel_id=1, source_target_pairs={{2,6},{3,1},{6,10},{7,3},{10,14},{11,7},{14,12},{15,11},{12,8},{13... | collective-permute-start | bytes 1966088 | tf_op jit(solution)/shard_map/ppermute | solution.py:233
  16.7 0.8 copy-done.6
  17.6 4.2 %collective-permute-done.1.refs_5_ = bf16[1280,256]{1,0:T(8,128)(2,1)S(1)} collective-permute-done((bf16[1280,256]{1,0:T(8,128)(2,1)S(1)}, bf16[1280,256]{1,0:T(8,128)(2,1)S(1)}, u32[]{:S(2)}, u32[]{:S(2)}) %collective-permute-start.1) | collective-permute-done | bytes 655392 | tf_op jit(solution)/shard_map/ppermute | solution.py:233
  21.8 2.0 %collective-permute-start.2 = (bf16[1280,256]{1,0:T(8,128)(2,1)S(1)}, bf16[1280,256]{1,0:T(8,128)(2,1)}, u32[]{:S(2)}, u32[]{:S(2)}) collective-permute-start(bf16[1280,256]{1,0:T(8,128)(2,1)S(1)} %collective-permute-done.1.refs_5_), channel_id=1, source_target_pairs={{2,6},{3,1},{6,10},{7,3},{10,14},{11,7},{14,12},{15,11},{12,8},{13... | collective-permute-start | bytes 1966088 | tf_op jit(solution)/shard_map/ppermute | solution.py:233
  23.8 0.9 copy-done.8
  24.6 4.3 %collective-permute-done.5.refs_4_ = bf16[1280,256]{1,0:T(8,128)(2,1)} collective-permute-done((bf16[1280,256]{1,0:T(8,128)(2,1)S(1)}, bf16[1280,256]{1,0:T(8,128)(2,1)}, u32[]{:S(2)}, u32[]{:S(2)}) %collective-permute-start.5) | collective-permute-done | bytes 655392 | tf_op jit(solution)/shard_map/ppermute | solution.py:233
  28.9 2.0 %collective-permute-start.6 = (bf16[1280,256]{1,0:T(8,128)(2,1)}, bf16[1280,256]{1,0:T(8,128)(2,1)}, u32[]{:S(2)}, u32[]{:S(2)}) collective-permute-start(bf16[1280,256]{1,0:T(8,128)(2,1)} %collective-permute-done.5.refs_4_), channel_id=1, source_target_pairs={{2,6},{3,1},{6,10},{7,3},{10,14},{11,7},{14,12},{15,11},{12,8},{13... | collective-permute-start | bytes 1966088 | tf_op jit(solution)/shard_map/ppermute | solution.py:233
  30.9 5.1 %collective-permute-done.2.refs_5_ = bf16[1280,256]{1,0:T(8,128)(2,1)} collective-permute-done((bf16[1280,256]{1,0:T(8,128)(2,1)S(1)}, bf16[1280,256]{1,0:T(8,128)(2,1)}, u32[]{:S(2)}, u32[]{:S(2)}) %collective-permute-start.2) | collective-permute-done | bytes 655392 | tf_op jit(solution)/shard_map/ppermute | solution.py:233
  35.9 2.0 %collective-permute-start.3 = (bf16[1280,256]{1,0:T(8,128)(2,1)}, bf16[1280,256]{1,0:T(8,128)(2,1)}, u32[]{:S(2)}, u32[]{:S(2)}) collective-permute-start(bf16[1280,256]{1,0:T(8,128)(2,1)} %collective-permute-done.2.refs_5_), channel_id=1, source_target_pairs={{2,6},{3,1},{6,10},{7,3},{10,14},{11,7},{14,12},{15,11},{12,8},{13... | collective-permute-start | bytes 1966088 | tf_op jit(solution)/shard_map/ppermute | solution.py:233
  37.9 0.7 dynamic-slice_bitcast_fusion.order_ref
  38.6 0.0 collective-permute-done.8.refs_3_
  38.6 0.0 collective-permute-done.7.refs_1_.sib_ref
  38.6 0.0 copy-start
  38.6 4.0 %copy-done = bf16[160,32768]{1,0:T(8,128)(2,1)S(1)} copy-done((bf16[160,32768]{1,0:T(8,128)(2,1)S(1)}, bf16[160,32768]{1,0:T(8,128)(2,1)}, u32[]{:S(2)}) %copy-start) | copy-done | bytes 10485784
  42.6 1.7 %copy-done.1 = bf16[160,8192]{1,0:T(8,128)(2,1)S(1)} copy-done((bf16[160,8192]{1,0:T(8,128)(2,1)S(1)}, bf16[160,8192]{1,0:T(8,128)(2,1)}, u32[]{:S(2)}) %copy-start.1) | copy-done | bytes 2621464
  44.3 1.1 copy-done.5
  45.4 2.6 %step.8 = (f32[320,256]{1,0:T(8,128)S(1)}, f32[320,256]{1,0:T(8,128)S(1)}) custom-call(s32[8]{0:T(128)S(1)} %dynamic-slice_bitcast_fusion.order_ref, bf16[160,32768]{1,0:T(8,128)(2,1)S(1)} %copy-done, bf16[160,32768]{1,0:T(8,128)(2,1)} %collective-permute-done.7.refs_1_.sib_ref, bf16[160,8192]{1,0:T(8,128)(2,1)S(1)} %copy-done.1, ...), custom_call_target="tpu_custom_call" | custom-call | flops 419430400 | bytes 3604480 | tf_op jit(solution)/shard_map/step/pallas_call | solution.py:59
  48.0 0.0 collective-permute-done.6.refs_4_
  48.0 1.6 %collective-permute-start.10 = (bf16[1280,256]{1,0:T(8,128)(2,1)}, bf16[1280,256]{1,0:T(8,128)(2,1)S(1)}, u32[]{:S(2)}, u32[]{:S(2)}) collective-permute-start(bf16[1280,256]{1,0:T(8,128)(2,1)} %collective-permute-done.6.refs_4_), channel_id=1, source_target_pairs={{2,6},{3,1},{6,10},{7,3},{10,14},{11,7},{14,12},{15,11},{12,8},{13... | collective-permute-start | bytes 1966088 | tf_op jit(solution)/shard_map/ppermute | solution.py:233
  49.6 0.4 collective-permute-done.3.refs_5_
  50.0 2.0 %collective-permute-start.9 = (bf16[1280,256]{1,0:T(8,128)(2,1)}, bf16[1280,256]{1,0:T(8,128)(2,1)S(1)}, u32[]{:S(2)}, u32[]{:S(2)}) collective-permute-start(bf16[1280,256]{1,0:T(8,128)(2,1)} %collective-permute-done.3.refs_5_), channel_id=1, source_target_pairs={{2,6},{3,1},{6,10},{7,3},{10,14},{11,7},{14,12},{15,11},{12,8},{13... | collective-permute-start | bytes 1966088 | tf_op jit(solution)/shard_map/ppermute | solution.py:233
  52.0 0.0 copy-done.2
  52.0 0.0 copy-done.7
  52.0 0.0 copy-done.9
  52.0 2.3 %step.9 = (f32[320,256]{1,0:T(8,128)S(1)}, f32[320,256]{1,0:T(8,128)S(1)}) custom-call(s32[8]{0:T(128)S(1)} %dynamic-slice_bitcast_fusion.order_ref, bf16[160,32768]{1,0:T(8,128)(2,1)S(1)} %copy-done, bf16[160,32768]{1,0:T(8,128)(2,1)} %collective-permute-done.7.refs_1_.sib_ref, bf16[160,8192]{1,0:T(8,128)(2,1)S(1)} %copy-done.2, ...), custom_call_target="tpu_custom_call" | custom-call | flops 419430400 | bytes 4259840 | tf_op jit(solution)/shard_map/step/pallas_call | solution.py:59
  54.3 2.6 %step.10 = (f32[320,256]{1,0:T(8,128)S(1)}, f32[320,256]{1,0:T(8,128)S(1)}) custom-call(s32[8]{0:T(128)S(1)} %dynamic-slice_bitcast_fusion.order_ref, bf16[160,32768]{1,0:T(8,128)(2,1)S(1)} %copy-done, bf16[160,32768]{1,0:T(8,128)(2,1)} %collective-permute-done.7.refs_1_.sib_ref, bf16[160,8192]{1,0:T(8,128)(2,1)S(1)} %copy-done.2, ...), custom_call_target="tpu_custom_call" | custom-call | flops 419430400 | bytes 4259840 | tf_op jit(solution)/shard_map/step/pallas_call | solution.py:59
  56.9 1.9 %collective-permute-done.10.refs_4_ = bf16[1280,256]{1,0:T(8,128)(2,1)S(1)} collective-permute-done((bf16[1280,256]{1,0:T(8,128)(2,1)}, bf16[1280,256]{1,0:T(8,128)(2,1)S(1)}, u32[]{:S(2)}, u32[]{:S(2)}) %collective-permute-start.10) | collective-permute-done | bytes 655392 | tf_op jit(solution)/shard_map/ppermute | solution.py:233
  58.9 1.6 %collective-permute-start.12 = (bf16[1280,256]{1,0:T(8,128)(2,1)S(1)}, bf16[1280,256]{1,0:T(8,128)(2,1)S(1)}, u32[]{:S(2)}, u32[]{:S(2)}) collective-permute-start(bf16[1280,256]{1,0:T(8,128)(2,1)S(1)} %collective-permute-done.10.refs_4_), channel_id=1, source_target_pairs={{2,6},{3,1},{6,10},{7,3},{10,14},{11,7},{14,12},{15,11},{12,8},{13... | collective-permute-start | bytes 1966088 | tf_op jit(solution)/shard_map/ppermute | solution.py:233
  60.4 5.4 %collective-permute-done.9.refs_5_ = bf16[1280,256]{1,0:T(8,128)(2,1)S(1)} collective-permute-done((bf16[1280,256]{1,0:T(8,128)(2,1)}, bf16[1280,256]{1,0:T(8,128)(2,1)S(1)}, u32[]{:S(2)}, u32[]{:S(2)}) %collective-permute-start.9) | collective-permute-done | bytes 655392 | tf_op jit(solution)/shard_map/ppermute | solution.py:233
  65.9 1.6 %collective-permute-start.11 = (bf16[1280,256]{1,0:T(8,128)(2,1)S(1)}, bf16[1280,256]{1,0:T(8,128)(2,1)S(1)}, u32[]{:S(2)}, u32[]{:S(2)}) collective-permute-start(bf16[1280,256]{1,0:T(8,128)(2,1)S(1)} %collective-permute-done.9.refs_5_), channel_id=1, source_target_pairs={{2,6},{3,1},{6,10},{7,3},{10,14},{11,7},{14,12},{15,11},{12,8},{13... | collective-permute-start | bytes 1966088 | tf_op jit(solution)/shard_map/ppermute | solution.py:233
  67.5 2.6 %step.11 = (f32[320,256]{1,0:T(8,128)S(1)}, f32[320,256]{1,0:T(8,128)S(1)}) custom-call(s32[8]{0:T(128)S(1)} %dynamic-slice_bitcast_fusion.order_ref, bf16[160,32768]{1,0:T(8,128)(2,1)S(1)} %copy-done, bf16[160,32768]{1,0:T(8,128)(2,1)} %collective-permute-done.7.refs_1_.sib_ref, bf16[160,8192]{1,0:T(8,128)(2,1)S(1)} %copy-done.2, ...), custom_call_target="tpu_custom_call" | custom-call | flops 419430400 | bytes 4259840 | tf_op jit(solution)/shard_map/step/pallas_call | solution.py:59
  70.1 2.3 %step.12 = (f32[320,256]{1,0:T(8,128)S(1)}, f32[320,256]{1,0:T(8,128)S(1)}) custom-call(s32[8]{0:T(128)S(1)} %dynamic-slice_bitcast_fusion.order_ref, bf16[160,32768]{1,0:T(8,128)(2,1)S(1)} %copy-done, bf16[160,32768]{1,0:T(8,128)(2,1)} %collective-permute-done.7.refs_1_.sib_ref, bf16[160,8192]{1,0:T(8,128)(2,1)S(1)} %copy-done.2, ...), custom_call_target="tpu_custom_call" | custom-call | flops 419430400 | bytes 4259840 | tf_op jit(solution)/shard_map/step/pallas_call | solution.py:59
  72.4 0.5 collective-permute-done.12.refs_4_
  72.9 1.6 %collective-permute-start.14 = (bf16[1280,256]{1,0:T(8,128)(2,1)S(1)}, bf16[1280,256]{1,0:T(8,128)(2,1)S(1)}, u32[]{:S(2)}, u32[]{:S(2)}) collective-permute-start(bf16[1280,256]{1,0:T(8,128)(2,1)S(1)} %collective-permute-done.12.refs_4_), channel_id=1, source_target_pairs={{2,6},{3,1},{6,10},{7,3},{10,14},{11,7},{14,12},{15,11},{12,8},{13... | collective-permute-start | bytes 1966088 | tf_op jit(solution)/shard_map/ppermute | solution.py:233
  74.5 5.4 %collective-permute-done.11.refs_5_ = bf16[1280,256]{1,0:T(8,128)(2,1)S(1)} collective-permute-done((bf16[1280,256]{1,0:T(8,128)(2,1)S(1)}, bf16[1280,256]{1,0:T(8,128)(2,1)S(1)}, u32[]{:S(2)}, u32[]{:S(2)}) %collective-permute-start.11) | collective-permute-done | bytes 655392 | tf_op jit(solution)/shard_map/ppermute | solution.py:233
  79.9 1.6 %collective-permute-start.13 = (bf16[1280,256]{1,0:T(8,128)(2,1)S(1)}, bf16[1280,256]{1,0:T(8,128)(2,1)S(1)}, u32[]{:S(2)}, u32[]{:S(2)}) collective-permute-start(bf16[1280,256]{1,0:T(8,128)(2,1)S(1)} %collective-permute-done.11.refs_5_), channel_id=1, source_target_pairs={{2,6},{3,1},{6,10},{7,3},{10,14},{11,7},{14,12},{15,11},{12,8},{13... | collective-permute-start | bytes 1966088 | tf_op jit(solution)/shard_map/ppermute | solution.py:233
  81.5 2.3 %step.13 = (f32[320,256]{1,0:T(8,128)S(1)}, f32[320,256]{1,0:T(8,128)S(1)}) custom-call(s32[8]{0:T(128)S(1)} %dynamic-slice_bitcast_fusion.order_ref, bf16[160,32768]{1,0:T(8,128)(2,1)S(1)} %copy-done, bf16[160,32768]{1,0:T(8,128)(2,1)} %collective-permute-done.7.refs_1_.sib_ref, bf16[160,8192]{1,0:T(8,128)(2,1)S(1)} %copy-done.2, ...), custom_call_target="tpu_custom_call" | custom-call | flops 419430400 | bytes 4259840 | tf_op jit(solution)/shard_map/step/pallas_call | solution.py:59
  83.8 3.1 %collective-permute-done.14.refs_4_ = bf16[1280,256]{1,0:T(8,128)(2,1)S(1)} collective-permute-done((bf16[1280,256]{1,0:T(8,128)(2,1)S(1)}, bf16[1280,256]{1,0:T(8,128)(2,1)S(1)}, u32[]{:S(2)}, u32[]{:S(2)}) %collective-permute-start.14) | collective-permute-done | bytes 655392 | tf_op jit(solution)/shard_map/ppermute | solution.py:233
  86.9 1.6 %collective-permute-start.16 = (bf16[1280,256]{1,0:T(8,128)(2,1)S(1)}, bf16[1280,256]{1,0:T(8,128)(2,1)S(1)}, u32[]{:S(2)}, u32[]{:S(2)}) collective-permute-start(bf16[1280,256]{1,0:T(8,128)(2,1)S(1)} %collective-permute-done.14.refs_4_), channel_id=1, source_target_pairs={{2,6},{3,1},{6,10},{7,3},{10,14},{11,7},{14,12},{15,11},{12,8},{13... | collective-permute-start | bytes 1966088 | tf_op jit(solution)/shard_map/ppermute | solution.py:233
  88.5 5.4 %collective-permute-done.13.refs_5_ = bf16[1280,256]{1,0:T(8,128)(2,1)S(1)} collective-permute-done((bf16[1280,256]{1,0:T(8,128)(2,1)S(1)}, bf16[1280,256]{1,0:T(8,128)(2,1)S(1)}, u32[]{:S(2)}, u32[]{:S(2)}) %collective-permute-start.13) | collective-permute-done | bytes 655392 | tf_op jit(solution)/shard_map/ppermute | solution.py:233
  94.0 1.6 %collective-permute-start.15 = (bf16[1280,256]{1,0:T(8,128)(2,1)S(1)}, bf16[1280,256]{1,0:T(8,128)(2,1)S(1)}, u32[]{:S(2)}, u32[]{:S(2)}) collective-permute-start(bf16[1280,256]{1,0:T(8,128)(2,1)S(1)} %collective-permute-done.13.refs_5_), channel_id=1, source_target_pairs={{2,6},{3,1},{6,10},{7,3},{10,14},{11,7},{14,12},{15,11},{12,8},{13... | collective-permute-start | bytes 1966088 | tf_op jit(solution)/shard_map/ppermute | solution.py:233
  95.5 1.7 %window.1.window_ref = bf16[320,1280]{1,0:T(8,128)(2,1)S(1)} custom-call(s32[8]{0:T(128)S(1)} %dynamic-slice_bitcast_fusion.order_ref, bf16[160,32768]{1,0:T(8,128)(2,1)S(1)} %copy-done, bf16[160,32768]{1,0:T(8,128)(2,1)} %collective-permute-done.7.refs_1_.sib_ref), custom_call_target="tpu_custom_call" | custom-call | bytes 2129920 | tf_op jit(solution)/shard_map/window/pallas_call | solution.py:59
  97.2 2.3 %step.14 = (f32[320,256]{1,0:T(8,128)S(1)}, f32[320,256]{1,0:T(8,128)S(1)}) custom-call(s32[8]{0:T(128)S(1)} %dynamic-slice_bitcast_fusion.order_ref, bf16[160,32768]{1,0:T(8,128)(2,1)S(1)} %copy-done, bf16[160,32768]{1,0:T(8,128)(2,1)} %collective-permute-done.7.refs_1_.sib_ref, bf16[160,8192]{1,0:T(8,128)(2,1)S(1)} %copy-done.2, ...), custom_call_target="tpu_custom_call" | custom-call | flops 419430400 | bytes 4259840 | tf_op jit(solution)/shard_map/step/pallas_call | solution.py:59
  99.5 1.4 %collective-permute-done.16.refs_4_ = bf16[1280,256]{1,0:T(8,128)(2,1)S(1)} collective-permute-done((bf16[1280,256]{1,0:T(8,128)(2,1)S(1)}, bf16[1280,256]{1,0:T(8,128)(2,1)S(1)}, u32[]{:S(2)}, u32[]{:S(2)}) %collective-permute-start.16) | collective-permute-done | bytes 655392 | tf_op jit(solution)/shard_map/ppermute | solution.py:233
  101.0 2.0 %step.15 = (f32[320,256]{1,0:T(8,128)S(1)}, f32[320,256]{1,0:T(8,128)S(1)}) custom-call(s32[8]{0:T(128)S(1)} %dynamic-slice_bitcast_fusion.order_ref, bf16[160,32768]{1,0:T(8,128)(2,1)S(1)} %copy-done, bf16[160,32768]{1,0:T(8,128)(2,1)} %collective-permute-done.7.refs_1_.sib_ref, bf16[160,8192]{1,0:T(8,128)(2,1)S(1)} %copy-done.2, ...), custom_call_target="tpu_custom_call" | custom-call | flops 209715200 | bytes 3604480 | tf_op jit(solution)/shard_map/step/pallas_call | solution.py:59
  103.0 0.1 collective-permute-start.17
  103.1 0.0 copy-done.11
  103.1 0.0 copy-done.12
  103.1 0.5 collective-permute-start
  103.7 1.0 collective-permute-done
  104.7 3.3 %collective-permute-done.15.b_ref = bf16[1280,256]{1,0:T(8,128)(2,1)S(1)} collective-permute-done((bf16[1280,256]{1,0:T(8,128)(2,1)S(1)}, bf16[1280,256]{1,0:T(8,128)(2,1)S(1)}, u32[]{:S(2)}, u32[]{:S(2)}) %collective-permute-start.15) | collective-permute-done | bytes 655392 | tf_op jit(solution)/shard_map/ppermute | solution.py:233
  108.0 0.0 collective-permute-done.17.got_ref
  108.0 1.2 %score.1 = f32[32,8]{1,0:T(8,128)S(1)} custom-call(s32[2]{0:T(128)S(1)} %copy-done.11, s32[2]{0:T(128)S(1)} %copy-done.12, s32[2]{0:T(128)S(1)} %get-tuple-element.94.seq_sib, s32[2]{0:T(128)S(1)} %get-tuple-element.93.len_sib, bf16[320,1280]{1,0:T(8,128)(2,1)S(1)} %window.1.window_ref, bf16[1280,256]{1,0:T(8,128)(2,1)S(1)} %collective-permute-done.15.b_ref, ...), custom_call_target="tpu_custom_call" | custom-call | flops 209715200 | bytes 2457600 | tf_op jit(solution)/shard_map/score/pallas_call | solution.py:182
  109.2 11.3 %all_to_all.5 = f32[16,2,8]{2,1,0:T(2,128)S(1)} all-to-all(f32[16,2,8]{2,1,0:T(2,128)S(1)} %bitcast.9), channel_id=1, replica_groups=mesh['groups'=2,'dp'=16] {'dp'}, dimensions={0} | all-to-all | bytes 2048 | tf_op jit(solution)/shard_map/all_to_all | solution.py:254
  120.5 0.6 reduce_sum.9
  (14 shorter events, 0.0 us)
Async XLA Ops:
  0.0 38.6 %collective-permute-start.7 = (bf16[160,32768]{1,0:T(8,128)(2,1)}, bf16[160,32768]{1,0:T(8,128)(2,1)}, u32[]{:S(2)}, u32[]{:S(2)}) collective-permute-start(bf16[160,32768]{1,0:T(8,128)(2,1)} %refs_0_.15), channel_id=1, source_target_pairs={{0,1},{1,0},{2,3},{3,2},{4,5},{5,4},{6,7},{7,6},{8,9},{9,8},{10,11... | collective-permute-start | bytes 31457288 | tf_op jit(solution)/shard_map/ppermute | solution.py:219
  0.5 38.1 %collective-permute-start.8 = (bf16[160,8192]{1,0:T(8,128)(2,1)}, bf16[160,8192]{1,0:T(8,128)(2,1)S(1)}, u32[]{:S(2)}, u32[]{:S(2)}) collective-permute-start(bf16[160,8192]{1,0:T(8,128)(2,1)} %refs_2_.15), channel_id=1, source_target_pairs={{0,1},{1,0},{2,3},{3,2},{4,5},{5,4},{6,7},{7,6},{8,9},{9,8},{10,11... | collective-permute-start | bytes 7864328 | tf_op jit(solution)/shard_map/ppermute | solution.py:219
  0.5 1.2 %copy-start.3 = (bf16[2048,256]{1,0:T(8,128)(2,1)S(1)}, bf16[2048,256]{1,0:T(8,128)(2,1)}, u32[]{:S(2)}) copy-start(bf16[2048,256]{1,0:T(8,128)(2,1)} %out_ref.1) | copy-start | bytes 3145732
  1.7 0.9 copy-start.10
  3.1 11.6 %collective-permute-start.4 = (bf16[1280,256]{1,0:T(8,128)(2,1)S(1)}, bf16[1280,256]{1,0:T(8,128)(2,1)S(1)}, u32[]{:S(2)}, u32[]{:S(2)}) collective-permute-start(bf16[1280,256]{1,0:T(8,128)(2,1)S(1)} %get-tuple-element.50.refs_4_), channel_id=1, source_target_pairs={{2,6},{3,1},{6,10},{7,3},{10,14},{11,7},{14,12},{15,11},{12,8},{13... | collective-permute-start | bytes 1966088 | tf_op jit(solution)/shard_map/ppermute | solution.py:233
  6.2 15.6 %collective-permute-start.1 = (bf16[1280,256]{1,0:T(8,128)(2,1)S(1)}, bf16[1280,256]{1,0:T(8,128)(2,1)S(1)}, u32[]{:S(2)}, u32[]{:S(2)}) collective-permute-start(bf16[1280,256]{1,0:T(8,128)(2,1)S(1)} %get-tuple-element.49.refs_5_), channel_id=1, source_target_pairs={{2,6},{3,1},{6,10},{7,3},{10,14},{11,7},{14,12},{15,11},{12,8},{13... | collective-permute-start | bytes 1966088 | tf_op jit(solution)/shard_map/ppermute | solution.py:233
  7.7 0.9 copy-start.4
  14.8 14.1 %collective-permute-start.5 = (bf16[1280,256]{1,0:T(8,128)(2,1)S(1)}, bf16[1280,256]{1,0:T(8,128)(2,1)}, u32[]{:S(2)}, u32[]{:S(2)}) collective-permute-start(bf16[1280,256]{1,0:T(8,128)(2,1)S(1)} %collective-permute-done.4.refs_4_), channel_id=1, source_target_pairs={{2,6},{3,1},{6,10},{7,3},{10,14},{11,7},{14,12},{15,11},{12,8},{13... | collective-permute-start | bytes 1966088 | tf_op jit(solution)/shard_map/ppermute | solution.py:233
  16.7 0.8 copy-start.6
  21.8 14.1 %collective-permute-start.2 = (bf16[1280,256]{1,0:T(8,128)(2,1)S(1)}, bf16[1280,256]{1,0:T(8,128)(2,1)}, u32[]{:S(2)}, u32[]{:S(2)}) collective-permute-start(bf16[1280,256]{1,0:T(8,128)(2,1)S(1)} %collective-permute-done.1.refs_5_), channel_id=1, source_target_pairs={{2,6},{3,1},{6,10},{7,3},{10,14},{11,7},{14,12},{15,11},{12,8},{13... | collective-permute-start | bytes 1966088 | tf_op jit(solution)/shard_map/ppermute | solution.py:233
  23.8 0.9 copy-start.8
  28.9 19.1 %collective-permute-start.6 = (bf16[1280,256]{1,0:T(8,128)(2,1)}, bf16[1280,256]{1,0:T(8,128)(2,1)}, u32[]{:S(2)}, u32[]{:S(2)}) collective-permute-start(bf16[1280,256]{1,0:T(8,128)(2,1)} %collective-permute-done.5.refs_4_), channel_id=1, source_target_pairs={{2,6},{3,1},{6,10},{7,3},{10,14},{11,7},{14,12},{15,11},{12,8},{13... | collective-permute-start | bytes 1966088 | tf_op jit(solution)/shard_map/ppermute | solution.py:233
  35.9 14.0 %collective-permute-start.3 = (bf16[1280,256]{1,0:T(8,128)(2,1)}, bf16[1280,256]{1,0:T(8,128)(2,1)}, u32[]{:S(2)}, u32[]{:S(2)}) collective-permute-start(bf16[1280,256]{1,0:T(8,128)(2,1)} %collective-permute-done.2.refs_5_), channel_id=1, source_target_pairs={{2,6},{3,1},{6,10},{7,3},{10,14},{11,7},{14,12},{15,11},{12,8},{13... | collective-permute-start | bytes 1966088 | tf_op jit(solution)/shard_map/ppermute | solution.py:233
  38.6 4.0 %copy-start = (bf16[160,32768]{1,0:T(8,128)(2,1)S(1)}, bf16[160,32768]{1,0:T(8,128)(2,1)}, u32[]{:S(2)}) copy-start(bf16[160,32768]{1,0:T(8,128)(2,1)} %refs_0_.15) | copy-start | bytes 31457284
  42.6 1.7 %copy-start.1 = (bf16[160,8192]{1,0:T(8,128)(2,1)S(1)}, bf16[160,8192]{1,0:T(8,128)(2,1)}, u32[]{:S(2)}) copy-start(bf16[160,8192]{1,0:T(8,128)(2,1)} %refs_2_.15) | copy-start | bytes 7864324
  44.3 1.1 copy-start.5
  45.4 6.5 %copy-start.2 = (bf16[160,8192]{1,0:T(8,128)(2,1)S(1)}, bf16[160,8192]{1,0:T(8,128)(2,1)}, u32[]{:S(2)}) copy-start(bf16[160,8192]{1,0:T(8,128)(2,1)} %refs_2_.15) | copy-start | bytes 7864324
  45.4 6.5 %copy-start.7 = (bf16[1280,256]{1,0:T(8,128)(2,1)S(1)}, bf16[1280,256]{1,0:T(8,128)(2,1)}, u32[]{:S(2)}) copy-start(bf16[1280,256]{1,0:T(8,128)(2,1)} %copy-done.6) | copy-start | bytes 1966084
  45.4 6.5 %copy-start.9 = (bf16[1280,256]{1,0:T(8,128)(2,1)S(1)}, bf16[1280,256]{1,0:T(8,128)(2,1)}, u32[]{:S(2)}) copy-start(bf16[1280,256]{1,0:T(8,128)(2,1)} %copy-done.8) | copy-start | bytes 1966084
  48.0 10.8 %collective-permute-start.10 = (bf16[1280,256]{1,0:T(8,128)(2,1)}, bf16[1280,256]{1,0:T(8,128)(2,1)S(1)}, u32[]{:S(2)}, u32[]{:S(2)}) collective-permute-start(bf16[1280,256]{1,0:T(8,128)(2,1)} %collective-permute-done.6.refs_4_), channel_id=1, source_target_pairs={{2,6},{3,1},{6,10},{7,3},{10,14},{11,7},{14,12},{15,11},{12,8},{13... | collective-permute-start | bytes 1966088 | tf_op jit(solution)/shard_map/ppermute | solution.py:233
  50.0 15.9 %collective-permute-start.9 = (bf16[1280,256]{1,0:T(8,128)(2,1)}, bf16[1280,256]{1,0:T(8,128)(2,1)S(1)}, u32[]{:S(2)}, u32[]{:S(2)}) collective-permute-start(bf16[1280,256]{1,0:T(8,128)(2,1)} %collective-permute-done.3.refs_5_), channel_id=1, source_target_pairs={{2,6},{3,1},{6,10},{7,3},{10,14},{11,7},{14,12},{15,11},{12,8},{13... | collective-permute-start | bytes 1966088 | tf_op jit(solution)/shard_map/ppermute | solution.py:233
  58.9 14.0 %collective-permute-start.12 = (bf16[1280,256]{1,0:T(8,128)(2,1)S(1)}, bf16[1280,256]{1,0:T(8,128)(2,1)S(1)}, u32[]{:S(2)}, u32[]{:S(2)}) collective-permute-start(bf16[1280,256]{1,0:T(8,128)(2,1)S(1)} %collective-permute-done.10.refs_4_), channel_id=1, source_target_pairs={{2,6},{3,1},{6,10},{7,3},{10,14},{11,7},{14,12},{15,11},{12,8},{13... | collective-permute-start | bytes 1966088 | tf_op jit(solution)/shard_map/ppermute | solution.py:233
  65.9 14.0 %collective-permute-start.11 = (bf16[1280,256]{1,0:T(8,128)(2,1)S(1)}, bf16[1280,256]{1,0:T(8,128)(2,1)S(1)}, u32[]{:S(2)}, u32[]{:S(2)}) collective-permute-start(bf16[1280,256]{1,0:T(8,128)(2,1)S(1)} %collective-permute-done.9.refs_5_), channel_id=1, source_target_pairs={{2,6},{3,1},{6,10},{7,3},{10,14},{11,7},{14,12},{15,11},{12,8},{13... | collective-permute-start | bytes 1966088 | tf_op jit(solution)/shard_map/ppermute | solution.py:233
  72.9 14.0 %collective-permute-start.14 = (bf16[1280,256]{1,0:T(8,128)(2,1)S(1)}, bf16[1280,256]{1,0:T(8,128)(2,1)S(1)}, u32[]{:S(2)}, u32[]{:S(2)}) collective-permute-start(bf16[1280,256]{1,0:T(8,128)(2,1)S(1)} %collective-permute-done.12.refs_4_), channel_id=1, source_target_pairs={{2,6},{3,1},{6,10},{7,3},{10,14},{11,7},{14,12},{15,11},{12,8},{13... | collective-permute-start | bytes 1966088 | tf_op jit(solution)/shard_map/ppermute | solution.py:233
  79.9 14.0 %collective-permute-start.13 = (bf16[1280,256]{1,0:T(8,128)(2,1)S(1)}, bf16[1280,256]{1,0:T(8,128)(2,1)S(1)}, u32[]{:S(2)}, u32[]{:S(2)}) collective-permute-start(bf16[1280,256]{1,0:T(8,128)(2,1)S(1)} %collective-permute-done.11.refs_5_), channel_id=1, source_target_pairs={{2,6},{3,1},{6,10},{7,3},{10,14},{11,7},{14,12},{15,11},{12,8},{13... | collective-permute-start | bytes 1966088 | tf_op jit(solution)/shard_map/ppermute | solution.py:233
  86.9 14.0 %collective-permute-start.16 = (bf16[1280,256]{1,0:T(8,128)(2,1)S(1)}, bf16[1280,256]{1,0:T(8,128)(2,1)S(1)}, u32[]{:S(2)}, u32[]{:S(2)}) collective-permute-start(bf16[1280,256]{1,0:T(8,128)(2,1)S(1)} %collective-permute-done.14.refs_4_), channel_id=1, source_target_pairs={{2,6},{3,1},{6,10},{7,3},{10,14},{11,7},{14,12},{15,11},{12,8},{13... | collective-permute-start | bytes 1966088 | tf_op jit(solution)/shard_map/ppermute | solution.py:233
  94.0 14.0 %collective-permute-start.15 = (bf16[1280,256]{1,0:T(8,128)(2,1)S(1)}, bf16[1280,256]{1,0:T(8,128)(2,1)S(1)}, u32[]{:S(2)}, u32[]{:S(2)}) collective-permute-start(bf16[1280,256]{1,0:T(8,128)(2,1)S(1)} %collective-permute-done.13.refs_5_), channel_id=1, source_target_pairs={{2,6},{3,1},{6,10},{7,3},{10,14},{11,7},{14,12},{15,11},{12,8},{13... | collective-permute-start | bytes 1966088 | tf_op jit(solution)/shard_map/ppermute | solution.py:233
  101.0 2.1 %copy-start.11 = (s32[2]{0:T(128)S(1)}, s32[2]{0:T(128)}, u32[]{:S(2)}) copy-start(s32[2]{0:T(128)} %seq_ref.1) | copy-start | bytes 28
  101.0 2.1 %copy-start.12 = (s32[2]{0:T(128)S(1)}, s32[2]{0:T(128)}, u32[]{:S(2)}) copy-start(s32[2]{0:T(128)} %len_ref.1) | copy-start | bytes 28
  103.0 5.0 %collective-permute-start.17 = (f32[320,256]{1,0:T(8,128)S(1)}, f32[320,256]{1,0:T(8,128)S(1)}, u32[]{:S(2)}, u32[]{:S(2)}) collective-permute-start(f32[320,256]{1,0:T(8,128)S(1)} %get-tuple-element.92.inn_ref), channel_id=1, source_target_pairs={{0,1},{1,0},{2,3},{3,2},{4,5},{5,4},{6,7},{7,6},{8,9},{9,8},{10,11... | collective-permute-start | bytes 983048 | tf_op jit(solution)/shard_map/ppermute | solution.py:247
  103.1 1.6 %collective-permute-start = (s32[2,2]{1,0:T(2,128)S(1)}, s32[2,2]{1,0:T(2,128)S(1)}, u32[]{:S(2)}, u32[]{:S(2)}) collective-permute-start(s32[2,2]{1,0:T(2,128)S(1)} %pad_add_fusion), channel_id=1, source_target_pairs={{0,1},{1,0},{2,3},{3,2},{4,5},{5,4},{6,7},{7,6},{8,9},{9,8},{10,11... | collective-permute-start | bytes 56 | tf_op jit(solution)/shard_map/ppermute | solution.py:218

commit v7 on v6

--- a/solution.py
+++ b/solution.py
@@ -12,7 +12,7 @@
 RANK = 32
 LEN = 80
 F32 = jnp.float32
-VMEM = 20 << 20
+VMEM = 52 << 20
 
 
 def ring_of(chips):
@@ -136,7 +136,6 @@
         cost_estimate=pl.CostEstimate(
             flops=0, bytes_accessed=4 * sum(heights) * columns, transcendentals=0
         ),
-        compiler_params=pltpu.CompilerParams(vmem_limit_bytes=4 << 20),
         name="join",
     )(in_factors, out_factors)
 
@@ -187,7 +186,7 @@
         cost_estimate=pl.CostEstimate(
             flops=2 * window.size * block.shape[1], bytes_accessed=size, transcendentals=0
         ),
-        compiler_params=pltpu.CompilerParams(vmem_limit_bytes=VMEM),
+        compiler_params=pltpu.CompilerParams(vmem_limit_bytes=16 << 20),
         name="score",
     )(*numbers, *arrays)
 

time: 122 us -> 121 us (level)
  local copies, waits for them, and re-layouts: 12.2 us -> 2.89 us
  Pallas kernels: 22.4 us -> 26.8 us
  starting transfers between devices: 26.6 us -> 28.3 us
  blocking collectives: 11.3 us -> 12.7 us
  waiting for transfers between devices: 47.8 us -> 49.1 us
    unnamed x26 -> x18, local copies, waits for them, and re-layouts: 11.5 us -> 2.19 us
    pallas_call x9, Pallas kernels: 20.8 us -> 23.2 us  [call(): pl.pallas_call(kernel, grid_spec=pltpu.PrefetchScalarGridSpec(num_scalar_...]
    pallas_call x1, Pallas kernels: 0.44 us -> 2.39 us  [join(): pl.pallas_call(join_kernel, in_specs=[pl.BlockSpec(memory_space=pltpu.HBM...]
    ppermute x14, starting transfers between devices: 25.5 us -> 27.2 us  [shards(): held.append((lax.ppermute(a, 'dp', pairs), lax.ppermute(b, 'dp', pairs)))]
    all_to_all x1, blocking collectives: 11.3 us -> 12.7 us  [shards(): lax.all_to_all(table.reshape(devices, slots, queries), 'dp', 0, 0, tiled=...]
    ppermute x14, waiting for transfers between devices: 46.8 us -> 48.1 us  [shards(): held.append((lax.ppermute(a, 'dp', pairs), lax.ppermute(b, 'dp', pairs)))]
  transfers between devices with their start and end apart: 18 -> 18, of which waited for: 14 -> 12; matrix products, arithmetic and copies ran while one was open for 1% -> 1% of each run, Pallas kernels for 17% -> 21%
where the time goes in v7:
time: 121 us
  waiting for transfers between devices  49.1 us (41%)
  starting transfers between devices  28.3 us (23%)
  Pallas kernels  26.8 us (22%)
  blocking collectives  12.7 us (10%)
  local copies, waits for them, and re-layouts  2.89 us (2%)
    ppermute x14, waiting for transfers between devices, shards(): held.append((lax.ppermute(a, 'dp', pairs), lax.ppermute(b, 'dp', pairs)))  48.1 us
    ppermute x14, starting transfers between devices, shards(): held.append((lax.ppermute(a, 'dp', pairs), lax.ppermute(b, 'dp', pairs)))  27.2 us
    pallas_call x9, Pallas kernels, call(): pl.pallas_call(kernel, grid_spec=pltpu.PrefetchScalarGridSpec(num_scalar_...  23.2 us
    all_to_all x1, blocking collectives, shards(): lax.all_to_all(table.reshape(devices, slots, queries), 'dp', 0, 0, tiled=...  12.7 us
  transfers between devices with their start and end apart: 18, of which 12 were waited for; matrix products, arithmetic and copies ran while one was open for 1% of the time, Pallas kernels for 21%

profile of v7, /device:TPU:0, one launch (start us, length us, event | category | flops | bytes accessed | tf_op | source)
XLA Modules:
  0.0 120.5 jit_solution(887620017434378203)
XLA Ops:
  0.0 0.5 collective-permute-start.7
  0.5 0.1 collective-permute-start.8
  0.5 2.4 %join.1 = (bf16[1280,256]{1,0:T(8,128)(2,1)}, bf16[1280,256]{1,0:T(8,128)(2,1)}) custom-call(bf16[512,256]{1,0:T(8,128)(2,1)} %in_ref.1, bf16[2048,256]{1,0:T(8,128)(2,1)} %out_ref.1), custom_call_target="tpu_custom_call" | custom-call | bytes 2621440 | tf_op jit(solution)/shard_map/join/pallas_call | solution.py:130
  2.9 3.0 %collective-permute-start.4 = (bf16[1280,256]{1,0:T(8,128)(2,1)}, bf16[1280,256]{1,0:T(8,128)(2,1)S(1)}, u32[]{:S(2)}, u32[]{:S(2)}) collective-permute-start(bf16[1280,256]{1,0:T(8,128)(2,1)} %get-tuple-element.50.refs_4_), channel_id=1, source_target_pairs={{2,6},{3,1},{6,10},{7,3},{10,14},{11,7},{14,12},{15,11},{12,8},{13... | collective-permute-start | bytes 1966088 | tf_op jit(solution)/shard_map/ppermute | solution.py:232
  5.9 1.6 %collective-permute-start.1 = (bf16[1280,256]{1,0:T(8,128)(2,1)}, bf16[1280,256]{1,0:T(8,128)(2,1)S(1)}, u32[]{:S(2)}, u32[]{:S(2)}) collective-permute-start(bf16[1280,256]{1,0:T(8,128)(2,1)} %get-tuple-element.49.refs_5_), channel_id=1, source_target_pairs={{2,6},{3,1},{6,10},{7,3},{10,14},{11,7},{14,12},{15,11},{12,8},{13... | collective-permute-start | bytes 1966088 | tf_op jit(solution)/shard_map/ppermute | solution.py:232
  7.5 7.3 %collective-permute-done.4.refs_4_ = bf16[1280,256]{1,0:T(8,128)(2,1)S(1)} collective-permute-done((bf16[1280,256]{1,0:T(8,128)(2,1)}, bf16[1280,256]{1,0:T(8,128)(2,1)S(1)}, u32[]{:S(2)}, u32[]{:S(2)}) %collective-permute-start.4) | collective-permute-done | bytes 655392 | tf_op jit(solution)/shard_map/ppermute | solution.py:232
  14.8 2.0 %collective-permute-start.5 = (bf16[1280,256]{1,0:T(8,128)(2,1)S(1)}, bf16[1280,256]{1,0:T(8,128)(2,1)S(1)}, u32[]{:S(2)}, u32[]{:S(2)}) collective-permute-start(bf16[1280,256]{1,0:T(8,128)(2,1)S(1)} %collective-permute-done.4.refs_4_), channel_id=1, source_target_pairs={{2,6},{3,1},{6,10},{7,3},{10,14},{11,7},{14,12},{15,11},{12,8},{13... | collective-permute-start | bytes 1966088 | tf_op jit(solution)/shard_map/ppermute | solution.py:232
  16.7 5.1 %collective-permute-done.1.refs_5_ = bf16[1280,256]{1,0:T(8,128)(2,1)S(1)} collective-permute-done((bf16[1280,256]{1,0:T(8,128)(2,1)}, bf16[1280,256]{1,0:T(8,128)(2,1)S(1)}, u32[]{:S(2)}, u32[]{:S(2)}) %collective-permute-start.1) | collective-permute-done | bytes 655392 | tf_op jit(solution)/shard_map/ppermute | solution.py:232
  21.8 0.0 copy-start.5
  21.8 2.0 %collective-permute-start.2 = (bf16[1280,256]{1,0:T(8,128)(2,1)S(1)}, bf16[1280,256]{1,0:T(8,128)(2,1)}, u32[]{:S(2)}, u32[]{:S(2)}) collective-permute-start(bf16[1280,256]{1,0:T(8,128)(2,1)S(1)} %collective-permute-done.1.refs_5_), channel_id=1, source_target_pairs={{2,6},{3,1},{6,10},{7,3},{10,14},{11,7},{14,12},{15,11},{12,8},{13... | collective-permute-start | bytes 1966088 | tf_op jit(solution)/shard_map/ppermute | solution.py:232
  23.8 5.1 %collective-permute-done.5.refs_4_ = bf16[1280,256]{1,0:T(8,128)(2,1)S(1)} collective-permute-done((bf16[1280,256]{1,0:T(8,128)(2,1)S(1)}, bf16[1280,256]{1,0:T(8,128)(2,1)S(1)}, u32[]{:S(2)}, u32[]{:S(2)}) %collective-permute-start.5) | collective-permute-done | bytes 655392 | tf_op jit(solution)/shard_map/ppermute | solution.py:232
  28.8 2.0 %collective-permute-start.6 = (bf16[1280,256]{1,0:T(8,128)(2,1)S(1)}, bf16[1280,256]{1,0:T(8,128)(2,1)S(1)}, u32[]{:S(2)}, u32[]{:S(2)}) collective-permute-start(bf16[1280,256]{1,0:T(8,128)(2,1)S(1)} %collective-permute-done.5.refs_4_), channel_id=1, source_target_pairs={{2,6},{3,1},{6,10},{7,3},{10,14},{11,7},{14,12},{15,11},{12,8},{13... | collective-permute-start | bytes 1966088 | tf_op jit(solution)/shard_map/ppermute | solution.py:232
  30.8 5.2 %collective-permute-done.2.refs_5_ = bf16[1280,256]{1,0:T(8,128)(2,1)} collective-permute-done((bf16[1280,256]{1,0:T(8,128)(2,1)S(1)}, bf16[1280,256]{1,0:T(8,128)(2,1)}, u32[]{:S(2)}, u32[]{:S(2)}) %collective-permute-start.2) | collective-permute-done | bytes 655392 | tf_op jit(solution)/shard_map/ppermute | solution.py:232
  35.9 2.0 %collective-permute-start.3 = (bf16[1280,256]{1,0:T(8,128)(2,1)}, bf16[1280,256]{1,0:T(8,128)(2,1)S(1)}, u32[]{:S(2)}, u32[]{:S(2)}) collective-permute-start(bf16[1280,256]{1,0:T(8,128)(2,1)} %collective-permute-done.2.refs_5_), channel_id=1, source_target_pairs={{2,6},{3,1},{6,10},{7,3},{10,14},{11,7},{14,12},{15,11},{12,8},{13... | collective-permute-start | bytes 1966088 | tf_op jit(solution)/shard_map/ppermute | solution.py:232
  37.9 0.7 dynamic-slice_bitcast_fusion.order_ref
  38.6 0.0 collective-permute-done.8.refs_3_
  38.6 0.0 collective-permute-done.7.refs_1_.sib_ref
  38.6 0.0 copy-start
  38.6 1.1 copy-done
  39.7 0.0 copy-start.1
  39.7 1.1 copy-done.1
  40.8 2.5 %step.8 = (f32[320,256]{1,0:T(8,128)S(1)}, f32[320,256]{1,0:T(8,128)S(1)}) custom-call(s32[8]{0:T(128)S(1)} %dynamic-slice_bitcast_fusion.order_ref, bf16[160,32768]{1,0:T(8,128)(2,1)} %refs_0_.15, bf16[160,32768]{1,0:T(8,128)(2,1)} %collective-permute-done.7.refs_1_.sib_ref, bf16[160,8192]{1,0:T(8,128)(2,1)} %refs_2_.15, ...), custom_call_target="tpu_custom_call" | custom-call | flops 419430400 | bytes 3604480 | tf_op jit(solution)/shard_map/step/pallas_call | solution.py:59
  43.3 0.0 copy-done.5
  43.3 0.0 collective-permute-done.6.refs_4_
  43.3 1.6 %collective-permute-start.10 = (bf16[1280,256]{1,0:T(8,128)(2,1)S(1)}, bf16[1280,256]{1,0:T(8,128)(2,1)S(1)}, u32[]{:S(2)}, u32[]{:S(2)}) collective-permute-start(bf16[1280,256]{1,0:T(8,128)(2,1)S(1)} %collective-permute-done.6.refs_4_), channel_id=1, source_target_pairs={{2,6},{3,1},{6,10},{7,3},{10,14},{11,7},{14,12},{15,11},{12,8},{13... | collective-permute-start | bytes 1966088 | tf_op jit(solution)/shard_map/ppermute | solution.py:232
  44.9 4.9 %collective-permute-done.3.refs_5_ = bf16[1280,256]{1,0:T(8,128)(2,1)S(1)} collective-permute-done((bf16[1280,256]{1,0:T(8,128)(2,1)}, bf16[1280,256]{1,0:T(8,128)(2,1)S(1)}, u32[]{:S(2)}, u32[]{:S(2)}) %collective-permute-start.3) | collective-permute-done | bytes 655392 | tf_op jit(solution)/shard_map/ppermute | solution.py:232
  49.9 0.0 copy-start.4
  49.9 2.0 %collective-permute-start.9 = (bf16[1280,256]{1,0:T(8,128)(2,1)S(1)}, bf16[1280,256]{1,0:T(8,128)(2,1)S(1)}, u32[]{:S(2)}, u32[]{:S(2)}) collective-permute-start(bf16[1280,256]{1,0:T(8,128)(2,1)S(1)} %collective-permute-done.3.refs_5_), channel_id=1, source_target_pairs={{2,6},{3,1},{6,10},{7,3},{10,14},{11,7},{14,12},{15,11},{12,8},{13... | collective-permute-start | bytes 1966088 | tf_op jit(solution)/shard_map/ppermute | solution.py:232
  51.8 2.7 %step.9 = (f32[320,256]{1,0:T(8,128)S(1)}, f32[320,256]{1,0:T(8,128)S(1)}) custom-call(s32[8]{0:T(128)S(1)} %dynamic-slice_bitcast_fusion.order_ref, bf16[160,32768]{1,0:T(8,128)(2,1)} %refs_0_.15, bf16[160,32768]{1,0:T(8,128)(2,1)} %collective-permute-done.7.refs_1_.sib_ref, bf16[160,8192]{1,0:T(8,128)(2,1)} %refs_2_.15, ...), custom_call_target="tpu_custom_call" | custom-call | flops 419430400 | bytes 4259840 | tf_op jit(solution)/shard_map/step/pallas_call | solution.py:59
  54.6 0.0 copy-done.4
  54.6 2.7 %step.10 = (f32[320,256]{1,0:T(8,128)S(1)}, f32[320,256]{1,0:T(8,128)S(1)}) custom-call(s32[8]{0:T(128)S(1)} %dynamic-slice_bitcast_fusion.order_ref, bf16[160,32768]{1,0:T(8,128)(2,1)} %refs_0_.15, bf16[160,32768]{1,0:T(8,128)(2,1)} %collective-permute-done.7.refs_1_.sib_ref, bf16[160,8192]{1,0:T(8,128)(2,1)} %refs_2_.15, ...), custom_call_target="tpu_custom_call" | custom-call | flops 419430400 | bytes 4259840 | tf_op jit(solution)/shard_map/step/pallas_call | solution.py:59
  57.3 0.0 collective-permute-done.10.refs_4_
  57.3 1.6 %collective-permute-start.12 = (bf16[1280,256]{1,0:T(8,128)(2,1)S(1)}, bf16[1280,256]{1,0:T(8,128)(2,1)S(1)}, u32[]{:S(2)}, u32[]{:S(2)}) collective-permute-start(bf16[1280,256]{1,0:T(8,128)(2,1)S(1)} %collective-permute-done.10.refs_4_), channel_id=1, source_target_pairs={{2,6},{3,1},{6,10},{7,3},{10,14},{11,7},{14,12},{15,11},{12,8},{13... | collective-permute-start | bytes 1966088 | tf_op jit(solution)/shard_map/ppermute | solution.py:232
  59.0 5.0 %collective-permute-done.9.refs_5_ = bf16[1280,256]{1,0:T(8,128)(2,1)S(1)} collective-permute-done((bf16[1280,256]{1,0:T(8,128)(2,1)S(1)}, bf16[1280,256]{1,0:T(8,128)(2,1)S(1)}, u32[]{:S(2)}, u32[]{:S(2)}) %collective-permute-start.9) | collective-permute-done | bytes 655392 | tf_op jit(solution)/shard_map/ppermute | solution.py:232
  63.9 0.0 copy-start.7
  63.9 2.0 %collective-permute-start.11 = (bf16[1280,256]{1,0:T(8,128)(2,1)S(1)}, bf16[1280,256]{1,0:T(8,128)(2,1)S(1)}, u32[]{:S(2)}, u32[]{:S(2)}) collective-permute-start(bf16[1280,256]{1,0:T(8,128)(2,1)S(1)} %collective-permute-done.9.refs_5_), channel_id=1, source_target_pairs={{2,6},{3,1},{6,10},{7,3},{10,14},{11,7},{14,12},{15,11},{12,8},{13... | collective-permute-start | bytes 1966088 | tf_op jit(solution)/shard_map/ppermute | solution.py:232
  65.9 2.7 %step.11 = (f32[320,256]{1,0:T(8,128)S(1)}, f32[320,256]{1,0:T(8,128)S(1)}) custom-call(s32[8]{0:T(128)S(1)} %dynamic-slice_bitcast_fusion.order_ref, bf16[160,32768]{1,0:T(8,128)(2,1)} %refs_0_.15, bf16[160,32768]{1,0:T(8,128)(2,1)} %collective-permute-done.7.refs_1_.sib_ref, bf16[160,8192]{1,0:T(8,128)(2,1)} %refs_2_.15, ...), custom_call_target="tpu_custom_call" | custom-call | flops 419430400 | bytes 4259840 | tf_op jit(solution)/shard_map/step/pallas_call | solution.py:59
  68.6 0.0 copy-done.7
  68.6 2.8 %step.12 = (f32[320,256]{1,0:T(8,128)S(1)}, f32[320,256]{1,0:T(8,128)S(1)}) custom-call(s32[8]{0:T(128)S(1)} %dynamic-slice_bitcast_fusion.order_ref, bf16[160,32768]{1,0:T(8,128)(2,1)} %refs_0_.15, bf16[160,32768]{1,0:T(8,128)(2,1)} %collective-permute-done.7.refs_1_.sib_ref, bf16[160,8192]{1,0:T(8,128)(2,1)} %refs_2_.15, ...), custom_call_target="tpu_custom_call" | custom-call | flops 419430400 | bytes 4259840 | tf_op jit(solution)/shard_map/step/pallas_call | solution.py:59
  71.4 0.0 collective-permute-done.12.refs_4_
  71.4 1.6 %collective-permute-start.14 = (bf16[1280,256]{1,0:T(8,128)(2,1)S(1)}, bf16[1280,256]{1,0:T(8,128)(2,1)S(1)}, u32[]{:S(2)}, u32[]{:S(2)}) collective-permute-start(bf16[1280,256]{1,0:T(8,128)(2,1)S(1)} %collective-permute-done.12.refs_4_), channel_id=1, source_target_pairs={{2,6},{3,1},{6,10},{7,3},{10,14},{11,7},{14,12},{15,11},{12,8},{13... | collective-permute-start | bytes 1966088 | tf_op jit(solution)/shard_map/ppermute | solution.py:232
  73.0 4.9 %collective-permute-done.11.refs_5_ = bf16[1280,256]{1,0:T(8,128)(2,1)S(1)} collective-permute-done((bf16[1280,256]{1,0:T(8,128)(2,1)S(1)}, bf16[1280,256]{1,0:T(8,128)(2,1)S(1)}, u32[]{:S(2)}, u32[]{:S(2)}) %collective-permute-start.11) | collective-permute-done | bytes 655392 | tf_op jit(solution)/shard_map/ppermute | solution.py:232
  78.0 2.0 %collective-permute-start.13 = (bf16[1280,256]{1,0:T(8,128)(2,1)S(1)}, bf16[1280,256]{1,0:T(8,128)(2,1)S(1)}, u32[]{:S(2)}, u32[]{:S(2)}) collective-permute-start(bf16[1280,256]{1,0:T(8,128)(2,1)S(1)} %collective-permute-done.11.refs_5_), channel_id=1, source_target_pairs={{2,6},{3,1},{6,10},{7,3},{10,14},{11,7},{14,12},{15,11},{12,8},{13... | collective-permute-start | bytes 1966088 | tf_op jit(solution)/shard_map/ppermute | solution.py:232
  79.9 0.0 copy-done.8
  79.9 2.8 %step.13 = (f32[320,256]{1,0:T(8,128)S(1)}, f32[320,256]{1,0:T(8,128)S(1)}) custom-call(s32[8]{0:T(128)S(1)} %dynamic-slice_bitcast_fusion.order_ref, bf16[160,32768]{1,0:T(8,128)(2,1)} %refs_0_.15, bf16[160,32768]{1,0:T(8,128)(2,1)} %collective-permute-done.7.refs_1_.sib_ref, bf16[160,8192]{1,0:T(8,128)(2,1)} %refs_2_.15, ...), custom_call_target="tpu_custom_call" | custom-call | flops 419430400 | bytes 4259840 | tf_op jit(solution)/shard_map/step/pallas_call | solution.py:59
  82.7 2.3 %collective-permute-done.14.refs_4_ = bf16[1280,256]{1,0:T(8,128)(2,1)S(1)} collective-permute-done((bf16[1280,256]{1,0:T(8,128)(2,1)S(1)}, bf16[1280,256]{1,0:T(8,128)(2,1)S(1)}, u32[]{:S(2)}, u32[]{:S(2)}) %collective-permute-start.14) | collective-permute-done | bytes 655392 | tf_op jit(solution)/shard_map/ppermute | solution.py:232
  85.0 2.0 %collective-permute-start.16 = (bf16[1280,256]{1,0:T(8,128)(2,1)S(1)}, bf16[1280,256]{1,0:T(8,128)(2,1)S(1)}, u32[]{:S(2)}, u32[]{:S(2)}) collective-permute-start(bf16[1280,256]{1,0:T(8,128)(2,1)S(1)} %collective-permute-done.14.refs_4_), channel_id=1, source_target_pairs={{2,6},{3,1},{6,10},{7,3},{10,14},{11,7},{14,12},{15,11},{12,8},{13... | collective-permute-start | bytes 1966088 | tf_op jit(solution)/shard_map/ppermute | solution.py:232
  87.0 5.1 %collective-permute-done.13.refs_5_ = bf16[1280,256]{1,0:T(8,128)(2,1)S(1)} collective-permute-done((bf16[1280,256]{1,0:T(8,128)(2,1)S(1)}, bf16[1280,256]{1,0:T(8,128)(2,1)S(1)}, u32[]{:S(2)}, u32[]{:S(2)}) %collective-permute-start.13) | collective-permute-done | bytes 655392 | tf_op jit(solution)/shard_map/ppermute | solution.py:232
  92.0 2.0 %collective-permute-start.15 = (bf16[1280,256]{1,0:T(8,128)(2,1)S(1)}, bf16[1280,256]{1,0:T(8,128)(2,1)S(1)}, u32[]{:S(2)}, u32[]{:S(2)}) collective-permute-start(bf16[1280,256]{1,0:T(8,128)(2,1)S(1)} %collective-permute-done.13.refs_5_), channel_id=1, source_target_pairs={{2,6},{3,1},{6,10},{7,3},{10,14},{11,7},{14,12},{15,11},{12,8},{13... | collective-permute-start | bytes 1966088 | tf_op jit(solution)/shard_map/ppermute | solution.py:232
  94.0 1.9 %window.1.window_ref = bf16[320,1280]{1,0:T(8,128)(2,1)S(1)} custom-call(s32[8]{0:T(128)S(1)} %dynamic-slice_bitcast_fusion.order_ref, bf16[160,32768]{1,0:T(8,128)(2,1)} %refs_0_.15, bf16[160,32768]{1,0:T(8,128)(2,1)} %collective-permute-done.7.refs_1_.sib_ref), custom_call_target="tpu_custom_call" | custom-call | bytes 2129920 | tf_op jit(solution)/shard_map/window/pallas_call | solution.py:59
  95.9 0.0 copy-done.6
  95.9 2.8 %step.14 = (f32[320,256]{1,0:T(8,128)S(1)}, f32[320,256]{1,0:T(8,128)S(1)}) custom-call(s32[8]{0:T(128)S(1)} %dynamic-slice_bitcast_fusion.order_ref, bf16[160,32768]{1,0:T(8,128)(2,1)} %refs_0_.15, bf16[160,32768]{1,0:T(8,128)(2,1)} %collective-permute-done.7.refs_1_.sib_ref, bf16[160,8192]{1,0:T(8,128)(2,1)} %refs_2_.15, ...), custom_call_target="tpu_custom_call" | custom-call | flops 419430400 | bytes 4259840 | tf_op jit(solution)/shard_map/step/pallas_call | solution.py:59
  98.6 0.4 collective-permute-done.16.refs_4_
  99.0 2.3 %step.15 = (f32[320,256]{1,0:T(8,128)S(1)}, f32[320,256]{1,0:T(8,128)S(1)}) custom-call(s32[8]{0:T(128)S(1)} %dynamic-slice_bitcast_fusion.order_ref, bf16[160,32768]{1,0:T(8,128)(2,1)} %refs_0_.15, bf16[160,32768]{1,0:T(8,128)(2,1)} %collective-permute-done.7.refs_1_.sib_ref, bf16[160,8192]{1,0:T(8,128)(2,1)} %refs_2_.15, ...), custom_call_target="tpu_custom_call" | custom-call | flops 209715200 | bytes 3604480 | tf_op jit(solution)/shard_map/step/pallas_call | solution.py:59
  101.3 0.1 collective-permute-start.17
  101.4 0.0 copy-done.2
  101.4 0.0 copy-done.3
  101.5 0.5 collective-permute-start
  102.0 1.0 collective-permute-done
  103.0 3.0 %collective-permute-done.15.b_ref = bf16[1280,256]{1,0:T(8,128)(2,1)S(1)} collective-permute-done((bf16[1280,256]{1,0:T(8,128)(2,1)S(1)}, bf16[1280,256]{1,0:T(8,128)(2,1)S(1)}, u32[]{:S(2)}, u32[]{:S(2)}) %collective-permute-start.15) | collective-permute-done | bytes 655392 | tf_op jit(solution)/shard_map/ppermute | solution.py:232
  106.1 0.0 collective-permute-done.17.got_ref
  106.1 1.2 %score.1 = f32[32,8]{1,0:T(8,128)S(1)} custom-call(s32[2]{0:T(128)S(1)} %copy-done.2, s32[2]{0:T(128)S(1)} %copy-done.3, s32[2]{0:T(128)S(1)} %get-tuple-element.94.seq_sib, s32[2]{0:T(128)S(1)} %get-tuple-element.93.len_sib, bf16[320,1280]{1,0:T(8,128)(2,1)S(1)} %window.1.window_ref, bf16[1280,256]{1,0:T(8,128)(2,1)S(1)} %collective-permute-done.15.b_ref, ...), custom_call_target="tpu_custom_call" | custom-call | flops 209715200 | bytes 2457600 | tf_op jit(solution)/shard_map/score/pallas_call | solution.py:181
  107.3 12.7 %all_to_all.5 = f32[16,2,8]{2,1,0:T(2,128)S(1)} all-to-all(f32[16,2,8]{2,1,0:T(2,128)S(1)} %bitcast.9), channel_id=1, replica_groups=mesh['groups'=2,'dp'=16] {'dp'}, dimensions={0} | all-to-all | bytes 2048 | tf_op jit(solution)/shard_map/all_to_all | solution.py:253
  120.0 0.6 reduce_sum.9
  (6 shorter events, 0.0 us)
Async XLA Ops:
  0.0 38.6 %collective-permute-start.7 = (bf16[160,32768]{1,0:T(8,128)(2,1)}, bf16[160,32768]{1,0:T(8,128)(2,1)}, u32[]{:S(2)}, u32[]{:S(2)}) collective-permute-start(bf16[160,32768]{1,0:T(8,128)(2,1)} %refs_0_.15), channel_id=1, source_target_pairs={{0,1},{1,0},{2,3},{3,2},{4,5},{5,4},{6,7},{7,6},{8,9},{9,8},{10,11... | collective-permute-start | bytes 31457288 | tf_op jit(solution)/shard_map/ppermute | solution.py:218
  0.5 38.1 %collective-permute-start.8 = (bf16[160,8192]{1,0:T(8,128)(2,1)}, bf16[160,8192]{1,0:T(8,128)(2,1)}, u32[]{:S(2)}, u32[]{:S(2)}) collective-permute-start(bf16[160,8192]{1,0:T(8,128)(2,1)} %refs_2_.15), channel_id=1, source_target_pairs={{0,1},{1,0},{2,3},{3,2},{4,5},{5,4},{6,7},{7,6},{8,9},{9,8},{10,11... | collective-permute-start | bytes 7864328 | tf_op jit(solution)/shard_map/ppermute | solution.py:218
  2.9 11.9 %collective-permute-start.4 = (bf16[1280,256]{1,0:T(8,128)(2,1)}, bf16[1280,256]{1,0:T(8,128)(2,1)S(1)}, u32[]{:S(2)}, u32[]{:S(2)}) collective-permute-start(bf16[1280,256]{1,0:T(8,128)(2,1)} %get-tuple-element.50.refs_4_), channel_id=1, source_target_pairs={{2,6},{3,1},{6,10},{7,3},{10,14},{11,7},{14,12},{15,11},{12,8},{13... | collective-permute-start | bytes 1966088 | tf_op jit(solution)/shard_map/ppermute | solution.py:232
  5.9 15.9 %collective-permute-start.1 = (bf16[1280,256]{1,0:T(8,128)(2,1)}, bf16[1280,256]{1,0:T(8,128)(2,1)S(1)}, u32[]{:S(2)}, u32[]{:S(2)}) collective-permute-start(bf16[1280,256]{1,0:T(8,128)(2,1)} %get-tuple-element.49.refs_5_), channel_id=1, source_target_pairs={{2,6},{3,1},{6,10},{7,3},{10,14},{11,7},{14,12},{15,11},{12,8},{13... | collective-permute-start | bytes 1966088 | tf_op jit(solution)/shard_map/ppermute | solution.py:232
  14.8 14.0 %collective-permute-start.5 = (bf16[1280,256]{1,0:T(8,128)(2,1)S(1)}, bf16[1280,256]{1,0:T(8,128)(2,1)S(1)}, u32[]{:S(2)}, u32[]{:S(2)}) collective-permute-start(bf16[1280,256]{1,0:T(8,128)(2,1)S(1)} %collective-permute-done.4.refs_4_), channel_id=1, source_target_pairs={{2,6},{3,1},{6,10},{7,3},{10,14},{11,7},{14,12},{15,11},{12,8},{13... | collective-permute-start | bytes 1966088 | tf_op jit(solution)/shard_map/ppermute | solution.py:232
  21.8 21.5 %copy-start.5 = (bf16[1280,256]{1,0:T(8,128)(2,1)}, bf16[1280,256]{1,0:T(8,128)(2,1)S(1)}, u32[]{:S(2)}) copy-start(bf16[1280,256]{1,0:T(8,128)(2,1)S(1)} %collective-permute-done.1.refs_5_) | copy-start | bytes 1966084
  21.8 14.1 %collective-permute-start.2 = (bf16[1280,256]{1,0:T(8,128)(2,1)S(1)}, bf16[1280,256]{1,0:T(8,128)(2,1)}, u32[]{:S(2)}, u32[]{:S(2)}) collective-permute-start(bf16[1280,256]{1,0:T(8,128)(2,1)S(1)} %collective-permute-done.1.refs_5_), channel_id=1, source_target_pairs={{2,6},{3,1},{6,10},{7,3},{10,14},{11,7},{14,12},{15,11},{12,8},{13... | collective-permute-start | bytes 1966088 | tf_op jit(solution)/shard_map/ppermute | solution.py:232
  28.8 14.5 %collective-permute-start.6 = (bf16[1280,256]{1,0:T(8,128)(2,1)S(1)}, bf16[1280,256]{1,0:T(8,128)(2,1)S(1)}, u32[]{:S(2)}, u32[]{:S(2)}) collective-permute-start(bf16[1280,256]{1,0:T(8,128)(2,1)S(1)} %collective-permute-done.5.refs_4_), channel_id=1, source_target_pairs={{2,6},{3,1},{6,10},{7,3},{10,14},{11,7},{14,12},{15,11},{12,8},{13... | collective-permute-start | bytes 1966088 | tf_op jit(solution)/shard_map/ppermute | solution.py:232
  35.9 13.9 %collective-permute-start.3 = (bf16[1280,256]{1,0:T(8,128)(2,1)}, bf16[1280,256]{1,0:T(8,128)(2,1)S(1)}, u32[]{:S(2)}, u32[]{:S(2)}) collective-permute-start(bf16[1280,256]{1,0:T(8,128)(2,1)} %collective-permute-done.2.refs_5_), channel_id=1, source_target_pairs={{2,6},{3,1},{6,10},{7,3},{10,14},{11,7},{14,12},{15,11},{12,8},{13... | collective-permute-start | bytes 1966088 | tf_op jit(solution)/shard_map/ppermute | solution.py:232
  38.6 1.1 copy-start
  39.7 1.1 copy-start.1
  43.3 14.0 %collective-permute-start.10 = (bf16[1280,256]{1,0:T(8,128)(2,1)S(1)}, bf16[1280,256]{1,0:T(8,128)(2,1)S(1)}, u32[]{:S(2)}, u32[]{:S(2)}) collective-permute-start(bf16[1280,256]{1,0:T(8,128)(2,1)S(1)} %collective-permute-done.6.refs_4_), channel_id=1, source_target_pairs={{2,6},{3,1},{6,10},{7,3},{10,14},{11,7},{14,12},{15,11},{12,8},{13... | collective-permute-start | bytes 1966088 | tf_op jit(solution)/shard_map/ppermute | solution.py:232
  49.9 4.7 %copy-start.4 = (bf16[1280,256]{1,0:T(8,128)(2,1)}, bf16[1280,256]{1,0:T(8,128)(2,1)S(1)}, u32[]{:S(2)}) copy-start(bf16[1280,256]{1,0:T(8,128)(2,1)S(1)} %collective-permute-done.3.refs_5_) | copy-start | bytes 1966084
  49.9 14.0 %collective-permute-start.9 = (bf16[1280,256]{1,0:T(8,128)(2,1)S(1)}, bf16[1280,256]{1,0:T(8,128)(2,1)S(1)}, u32[]{:S(2)}, u32[]{:S(2)}) collective-permute-start(bf16[1280,256]{1,0:T(8,128)(2,1)S(1)} %collective-permute-done.3.refs_5_), channel_id=1, source_target_pairs={{2,6},{3,1},{6,10},{7,3},{10,14},{11,7},{14,12},{15,11},{12,8},{13... | collective-permute-start | bytes 1966088 | tf_op jit(solution)/shard_map/ppermute | solution.py:232
  57.3 14.1 %collective-permute-start.12 = (bf16[1280,256]{1,0:T(8,128)(2,1)S(1)}, bf16[1280,256]{1,0:T(8,128)(2,1)S(1)}, u32[]{:S(2)}, u32[]{:S(2)}) collective-permute-start(bf16[1280,256]{1,0:T(8,128)(2,1)S(1)} %collective-permute-done.10.refs_4_), channel_id=1, source_target_pairs={{2,6},{3,1},{6,10},{7,3},{10,14},{11,7},{14,12},{15,11},{12,8},{13... | collective-permute-start | bytes 1966088 | tf_op jit(solution)/shard_map/ppermute | solution.py:232
  63.9 4.7 %copy-start.7 = (bf16[1280,256]{1,0:T(8,128)(2,1)}, bf16[1280,256]{1,0:T(8,128)(2,1)S(1)}, u32[]{:S(2)}) copy-start(bf16[1280,256]{1,0:T(8,128)(2,1)S(1)} %collective-permute-done.9.refs_5_) | copy-start | bytes 1966084
  63.9 14.0 %collective-permute-start.11 = (bf16[1280,256]{1,0:T(8,128)(2,1)S(1)}, bf16[1280,256]{1,0:T(8,128)(2,1)S(1)}, u32[]{:S(2)}, u32[]{:S(2)}) collective-permute-start(bf16[1280,256]{1,0:T(8,128)(2,1)S(1)} %collective-permute-done.9.refs_5_), channel_id=1, source_target_pairs={{2,6},{3,1},{6,10},{7,3},{10,14},{11,7},{14,12},{15,11},{12,8},{13... | collective-permute-start | bytes 1966088 | tf_op jit(solution)/shard_map/ppermute | solution.py:232
  71.4 13.6 %collective-permute-start.14 = (bf16[1280,256]{1,0:T(8,128)(2,1)S(1)}, bf16[1280,256]{1,0:T(8,128)(2,1)S(1)}, u32[]{:S(2)}, u32[]{:S(2)}) collective-permute-start(bf16[1280,256]{1,0:T(8,128)(2,1)S(1)} %collective-permute-done.12.refs_4_), channel_id=1, source_target_pairs={{2,6},{3,1},{6,10},{7,3},{10,14},{11,7},{14,12},{15,11},{12,8},{13... | collective-permute-start | bytes 1966088 | tf_op jit(solution)/shard_map/ppermute | solution.py:232
  78.0 2.0 %copy-start.8 = (bf16[1280,256]{1,0:T(8,128)(2,1)}, bf16[1280,256]{1,0:T(8,128)(2,1)S(1)}, u32[]{:S(2)}) copy-start(bf16[1280,256]{1,0:T(8,128)(2,1)S(1)} %collective-permute-done.11.refs_5_) | copy-start | bytes 1966084
  78.0 14.0 %collective-permute-start.13 = (bf16[1280,256]{1,0:T(8,128)(2,1)S(1)}, bf16[1280,256]{1,0:T(8,128)(2,1)S(1)}, u32[]{:S(2)}, u32[]{:S(2)}) collective-permute-start(bf16[1280,256]{1,0:T(8,128)(2,1)S(1)} %collective-permute-done.11.refs_5_), channel_id=1, source_target_pairs={{2,6},{3,1},{6,10},{7,3},{10,14},{11,7},{14,12},{15,11},{12,8},{13... | collective-permute-start | bytes 1966088 | tf_op jit(solution)/shard_map/ppermute | solution.py:232
  85.0 14.0 %collective-permute-start.16 = (bf16[1280,256]{1,0:T(8,128)(2,1)S(1)}, bf16[1280,256]{1,0:T(8,128)(2,1)S(1)}, u32[]{:S(2)}, u32[]{:S(2)}) collective-permute-start(bf16[1280,256]{1,0:T(8,128)(2,1)S(1)} %collective-permute-done.14.refs_4_), channel_id=1, source_target_pairs={{2,6},{3,1},{6,10},{7,3},{10,14},{11,7},{14,12},{15,11},{12,8},{13... | collective-permute-start | bytes 1966088 | tf_op jit(solution)/shard_map/ppermute | solution.py:232
  92.0 3.9 %copy-start.6 = (bf16[1280,256]{1,0:T(8,128)(2,1)}, bf16[1280,256]{1,0:T(8,128)(2,1)S(1)}, u32[]{:S(2)}) copy-start(bf16[1280,256]{1,0:T(8,128)(2,1)S(1)} %collective-permute-done.13.refs_5_) | copy-start | bytes 1966084
  92.0 14.0 %collective-permute-start.15 = (bf16[1280,256]{1,0:T(8,128)(2,1)S(1)}, bf16[1280,256]{1,0:T(8,128)(2,1)S(1)}, u32[]{:S(2)}, u32[]{:S(2)}) collective-permute-start(bf16[1280,256]{1,0:T(8,128)(2,1)S(1)} %collective-permute-done.13.refs_5_), channel_id=1, source_target_pairs={{2,6},{3,1},{6,10},{7,3},{10,14},{11,7},{14,12},{15,11},{12,8},{13... | collective-permute-start | bytes 1966088 | tf_op jit(solution)/shard_map/ppermute | solution.py:232
  99.0 2.4 %copy-start.2 = (s32[2]{0:T(128)S(1)}, s32[2]{0:T(128)}, u32[]{:S(2)}) copy-start(s32[2]{0:T(128)} %seq_ref.1) | copy-start | bytes 28
  99.0 2.4 %copy-start.3 = (s32[2]{0:T(128)S(1)}, s32[2]{0:T(128)}, u32[]{:S(2)}) copy-start(s32[2]{0:T(128)} %len_ref.1) | copy-start | bytes 28
  101.3 4.7 %collective-permute-start.17 = (f32[320,256]{1,0:T(8,128)S(1)}, f32[320,256]{1,0:T(8,128)S(1)}, u32[]{:S(2)}, u32[]{:S(2)}) collective-permute-start(f32[320,256]{1,0:T(8,128)S(1)} %get-tuple-element.92.inn_ref), channel_id=1, source_target_pairs={{0,1},{1,0},{2,3},{3,2},{4,5},{5,4},{6,7},{7,6},{8,9},{9,8},{10,11... | collective-permute-start | bytes 983048 | tf_op jit(solution)/shard_map/ppermute | solution.py:246
  101.5 1.6 %collective-permute-start = (s32[2,2]{1,0:T(2,128)S(1)}, s32[2,2]{1,0:T(2,128)S(1)}, u32[]{:S(2)}, u32[]{:S(2)}) collective-permute-start(s32[2,2]{1,0:T(2,128)S(1)} %pad_add_fusion), channel_id=1, source_target_pairs={{0,1},{1,0},{2,3},{3,2},{4,5},{5,4},{6,7},{7,6},{8,9},{9,8},{10,11... | collective-permute-start | bytes 56 | tf_op jit(solution)/shard_map/ppermute | solution.py:217

commit v8 on v7

--- a/solution.py
+++ b/solution.py
@@ -210,7 +210,9 @@
         own, rows_in = own[:1], 0
     lead = (rows - rows_in) // 2
     if rows_in:
-        held = [join(in_factors, out_factors, lead)]
+        held = [list(join(in_factors, out_factors, lead))]
+        *held[0], grads, acts = lax.optimization_barrier((*held[0], grads, acts))
+        own = [grads, acts]
     else:
         held = [(out_factors[:lead], out_factors[lead:])]
 

time: 121 us -> 121 us (level)
  transfers between devices with their start and end apart: 18 -> 18, of which waited for: 12 -> 12; matrix products, arithmetic and copies ran while one was open for 1% -> 1% of each run, Pallas kernels for 21% -> 19%
where the time goes in v8:
time: 121 us
  waiting for transfers between devices  49.1 us (41%)
  starting transfers between devices  28.3 us (23%)
  Pallas kernels  26.7 us (22%)
  blocking collectives  12.7 us (10%)
  local copies, waits for them, and re-layouts  2.89 us (2%)
    ppermute x14, waiting for transfers between devices, shards(): held.append((lax.ppermute(a, 'dp', pairs), lax.ppermute(b, 'dp', pairs)))  48.1 us
    ppermute x14, starting transfers between devices, shards(): held.append((lax.ppermute(a, 'dp', pairs), lax.ppermute(b, 'dp', pairs)))  27.1 us
    pallas_call x9, Pallas kernels, call(): pl.pallas_call(kernel, grid_spec=pltpu.PrefetchScalarGridSpec(num_scalar_...  23.1 us
    all_to_all x1, blocking collectives, shards(): lax.all_to_all(table.reshape(devices, slots, queries), 'dp', 0, 0, tiled=...  12.7 us
  transfers between devices with their start and end apart: 18, of which 12 were waited for; matrix products, arithmetic and copies ran while one was open for 1% of the time, Pallas kernels for 19%

profile of v8, /device:TPU:0, one launch (start us, length us, event | category | flops | bytes accessed | tf_op | source)
XLA Modules:
  0.0 120.5 jit_solution(14305589770943161449)
XLA Ops:
  0.0 2.4 %join.1 = (bf16[1280,256]{1,0:T(8,128)(2,1)}, bf16[1280,256]{1,0:T(8,128)(2,1)}) custom-call(bf16[512,256]{1,0:T(8,128)(2,1)} %in_ref.1, bf16[2048,256]{1,0:T(8,128)(2,1)} %out_ref.1), custom_call_target="tpu_custom_call" | custom-call | bytes 2621440 | tf_op jit(solution)/shard_map/join/pallas_call | solution.py:130
  2.4 0.5 collective-permute-start.7
  2.9 0.1 collective-permute-start.8
  3.0 2.9 %collective-permute-start.4 = (bf16[1280,256]{1,0:T(8,128)(2,1)}, bf16[1280,256]{1,0:T(8,128)(2,1)S(1)}, u32[]{:S(2)}, u32[]{:S(2)}) collective-permute-start(bf16[1280,256]{1,0:T(8,128)(2,1)} %get-tuple-element.56.refs_4_), channel_id=1, source_target_pairs={{2,6},{3,1},{6,10},{7,3},{10,14},{11,7},{14,12},{15,11},{12,8},{13... | collective-permute-start | bytes 1966088 | tf_op jit(solution)/shard_map/ppermute | solution.py:234
  5.9 1.6 %collective-permute-start.1 = (bf16[1280,256]{1,0:T(8,128)(2,1)}, bf16[1280,256]{1,0:T(8,128)(2,1)S(1)}, u32[]{:S(2)}, u32[]{:S(2)}) collective-permute-start(bf16[1280,256]{1,0:T(8,128)(2,1)} %get-tuple-element.55.refs_5_), channel_id=1, source_target_pairs={{2,6},{3,1},{6,10},{7,3},{10,14},{11,7},{14,12},{15,11},{12,8},{13... | collective-permute-start | bytes 1966088 | tf_op jit(solution)/shard_map/ppermute | solution.py:234
  7.5 7.3 %collective-permute-done.4.refs_4_ = bf16[1280,256]{1,0:T(8,128)(2,1)S(1)} collective-permute-done((bf16[1280,256]{1,0:T(8,128)(2,1)}, bf16[1280,256]{1,0:T(8,128)(2,1)S(1)}, u32[]{:S(2)}, u32[]{:S(2)}) %collective-permute-start.4) | collective-permute-done | bytes 655392 | tf_op jit(solution)/shard_map/ppermute | solution.py:234
  14.7 2.0 %collective-permute-start.5 = (bf16[1280,256]{1,0:T(8,128)(2,1)S(1)}, bf16[1280,256]{1,0:T(8,128)(2,1)S(1)}, u32[]{:S(2)}, u32[]{:S(2)}) collective-permute-start(bf16[1280,256]{1,0:T(8,128)(2,1)S(1)} %collective-permute-done.4.refs_4_), channel_id=1, source_target_pairs={{2,6},{3,1},{6,10},{7,3},{10,14},{11,7},{14,12},{15,11},{12,8},{13... | collective-permute-start | bytes 1966088 | tf_op jit(solution)/shard_map/ppermute | solution.py:234
  16.7 5.1 %collective-permute-done.1.refs_5_ = bf16[1280,256]{1,0:T(8,128)(2,1)S(1)} collective-permute-done((bf16[1280,256]{1,0:T(8,128)(2,1)}, bf16[1280,256]{1,0:T(8,128)(2,1)S(1)}, u32[]{:S(2)}, u32[]{:S(2)}) %collective-permute-start.1) | collective-permute-done | bytes 655392 | tf_op jit(solution)/shard_map/ppermute | solution.py:234
  21.8 0.0 copy-start.5
  21.8 2.0 %collective-permute-start.2 = (bf16[1280,256]{1,0:T(8,128)(2,1)S(1)}, bf16[1280,256]{1,0:T(8,128)(2,1)}, u32[]{:S(2)}, u32[]{:S(2)}) collective-permute-start(bf16[1280,256]{1,0:T(8,128)(2,1)S(1)} %collective-permute-done.1.refs_5_), channel_id=1, source_target_pairs={{2,6},{3,1},{6,10},{7,3},{10,14},{11,7},{14,12},{15,11},{12,8},{13... | collective-permute-start | bytes 1966088 | tf_op jit(solution)/shard_map/ppermute | solution.py:234
  23.7 5.1 %collective-permute-done.5.refs_4_ = bf16[1280,256]{1,0:T(8,128)(2,1)S(1)} collective-permute-done((bf16[1280,256]{1,0:T(8,128)(2,1)S(1)}, bf16[1280,256]{1,0:T(8,128)(2,1)S(1)}, u32[]{:S(2)}, u32[]{:S(2)}) %collective-permute-start.5) | collective-permute-done | bytes 655392 | tf_op jit(solution)/shard_map/ppermute | solution.py:234
  28.8 2.0 %collective-permute-start.6 = (bf16[1280,256]{1,0:T(8,128)(2,1)S(1)}, bf16[1280,256]{1,0:T(8,128)(2,1)S(1)}, u32[]{:S(2)}, u32[]{:S(2)}) collective-permute-start(bf16[1280,256]{1,0:T(8,128)(2,1)S(1)} %collective-permute-done.5.refs_4_), channel_id=1, source_target_pairs={{2,6},{3,1},{6,10},{7,3},{10,14},{11,7},{14,12},{15,11},{12,8},{13... | collective-permute-start | bytes 1966088 | tf_op jit(solution)/shard_map/ppermute | solution.py:234
  30.8 5.2 %collective-permute-done.2.refs_5_ = bf16[1280,256]{1,0:T(8,128)(2,1)} collective-permute-done((bf16[1280,256]{1,0:T(8,128)(2,1)S(1)}, bf16[1280,256]{1,0:T(8,128)(2,1)}, u32[]{:S(2)}, u32[]{:S(2)}) %collective-permute-start.2) | collective-permute-done | bytes 655392 | tf_op jit(solution)/shard_map/ppermute | solution.py:234
  35.9 2.0 %collective-permute-start.3 = (bf16[1280,256]{1,0:T(8,128)(2,1)}, bf16[1280,256]{1,0:T(8,128)(2,1)S(1)}, u32[]{:S(2)}, u32[]{:S(2)}) collective-permute-start(bf16[1280,256]{1,0:T(8,128)(2,1)} %collective-permute-done.2.refs_5_), channel_id=1, source_target_pairs={{2,6},{3,1},{6,10},{7,3},{10,14},{11,7},{14,12},{15,11},{12,8},{13... | collective-permute-start | bytes 1966088 | tf_op jit(solution)/shard_map/ppermute | solution.py:234
  37.9 0.7 dynamic-slice_bitcast_fusion.order_ref
  38.6 0.0 collective-permute-done.8.refs_3_
  38.6 0.0 collective-permute-done.7.refs_1_.sib_ref
  38.6 0.0 copy-start
  38.6 1.1 copy-done
  39.7 0.0 copy-start.1
  39.7 1.1 copy-done.1
  40.8 2.5 %step.8 = (f32[320,256]{1,0:T(8,128)S(1)}, f32[320,256]{1,0:T(8,128)S(1)}) custom-call(s32[8]{0:T(128)S(1)} %dynamic-slice_bitcast_fusion.order_ref, bf16[160,32768]{1,0:T(8,128)(2,1)} %refs_0_.7, bf16[160,32768]{1,0:T(8,128)(2,1)} %collective-permute-done.7.refs_1_.sib_ref, bf16[160,8192]{1,0:T(8,128)(2,1)} %refs_2_.7, ...), custom_call_target="tpu_custom_call" | custom-call | flops 419430400 | bytes 3604480 | tf_op jit(solution)/shard_map/step/pallas_call | solution.py:59
  43.3 0.0 copy-done.5
  43.3 0.0 collective-permute-done.6.refs_4_
  43.3 1.6 %collective-permute-start.10 = (bf16[1280,256]{1,0:T(8,128)(2,1)S(1)}, bf16[1280,256]{1,0:T(8,128)(2,1)S(1)}, u32[]{:S(2)}, u32[]{:S(2)}) collective-permute-start(bf16[1280,256]{1,0:T(8,128)(2,1)S(1)} %collective-permute-done.6.refs_4_), channel_id=1, source_target_pairs={{2,6},{3,1},{6,10},{7,3},{10,14},{11,7},{14,12},{15,11},{12,8},{13... | collective-permute-start | bytes 1966088 | tf_op jit(solution)/shard_map/ppermute | solution.py:234
  44.9 4.9 %collective-permute-done.3.refs_5_ = bf16[1280,256]{1,0:T(8,128)(2,1)S(1)} collective-permute-done((bf16[1280,256]{1,0:T(8,128)(2,1)}, bf16[1280,256]{1,0:T(8,128)(2,1)S(1)}, u32[]{:S(2)}, u32[]{:S(2)}) %collective-permute-start.3) | collective-permute-done | bytes 655392 | tf_op jit(solution)/shard_map/ppermute | solution.py:234
  49.9 0.0 copy-start.4
  49.9 2.0 %collective-permute-start.9 = (bf16[1280,256]{1,0:T(8,128)(2,1)S(1)}, bf16[1280,256]{1,0:T(8,128)(2,1)S(1)}, u32[]{:S(2)}, u32[]{:S(2)}) collective-permute-start(bf16[1280,256]{1,0:T(8,128)(2,1)S(1)} %collective-permute-done.3.refs_5_), channel_id=1, source_target_pairs={{2,6},{3,1},{6,10},{7,3},{10,14},{11,7},{14,12},{15,11},{12,8},{13... | collective-permute-start | bytes 1966088 | tf_op jit(solution)/shard_map/ppermute | solution.py:234
  51.8 2.7 %step.9 = (f32[320,256]{1,0:T(8,128)S(1)}, f32[320,256]{1,0:T(8,128)S(1)}) custom-call(s32[8]{0:T(128)S(1)} %dynamic-slice_bitcast_fusion.order_ref, bf16[160,32768]{1,0:T(8,128)(2,1)} %refs_0_.7, bf16[160,32768]{1,0:T(8,128)(2,1)} %collective-permute-done.7.refs_1_.sib_ref, bf16[160,8192]{1,0:T(8,128)(2,1)} %refs_2_.7, ...), custom_call_target="tpu_custom_call" | custom-call | flops 419430400 | bytes 4259840 | tf_op jit(solution)/shard_map/step/pallas_call | solution.py:59
  54.6 0.0 copy-done.4
  54.6 2.7 %step.10 = (f32[320,256]{1,0:T(8,128)S(1)}, f32[320,256]{1,0:T(8,128)S(1)}) custom-call(s32[8]{0:T(128)S(1)} %dynamic-slice_bitcast_fusion.order_ref, bf16[160,32768]{1,0:T(8,128)(2,1)} %refs_0_.7, bf16[160,32768]{1,0:T(8,128)(2,1)} %collective-permute-done.7.refs_1_.sib_ref, bf16[160,8192]{1,0:T(8,128)(2,1)} %refs_2_.7, ...), custom_call_target="tpu_custom_call" | custom-call | flops 419430400 | bytes 4259840 | tf_op jit(solution)/shard_map/step/pallas_call | solution.py:59
  57.3 0.0 collective-permute-done.10.refs_4_
  57.3 1.6 %collective-permute-start.12 = (bf16[1280,256]{1,0:T(8,128)(2,1)S(1)}, bf16[1280,256]{1,0:T(8,128)(2,1)S(1)}, u32[]{:S(2)}, u32[]{:S(2)}) collective-permute-start(bf16[1280,256]{1,0:T(8,128)(2,1)S(1)} %collective-permute-done.10.refs_4_), channel_id=1, source_target_pairs={{2,6},{3,1},{6,10},{7,3},{10,14},{11,7},{14,12},{15,11},{12,8},{13... | collective-permute-start | bytes 1966088 | tf_op jit(solution)/shard_map/ppermute | solution.py:234
  58.9 4.9 %collective-permute-done.9.refs_5_ = bf16[1280,256]{1,0:T(8,128)(2,1)S(1)} collective-permute-done((bf16[1280,256]{1,0:T(8,128)(2,1)S(1)}, bf16[1280,256]{1,0:T(8,128)(2,1)S(1)}, u32[]{:S(2)}, u32[]{:S(2)}) %collective-permute-start.9) | collective-permute-done | bytes 655392 | tf_op jit(solution)/shard_map/ppermute | solution.py:234
  63.9 0.0 copy-start.7
  63.9 2.0 %collective-permute-start.11 = (bf16[1280,256]{1,0:T(8,128)(2,1)S(1)}, bf16[1280,256]{1,0:T(8,128)(2,1)S(1)}, u32[]{:S(2)}, u32[]{:S(2)}) collective-permute-start(bf16[1280,256]{1,0:T(8,128)(2,1)S(1)} %collective-permute-done.9.refs_5_), channel_id=1, source_target_pairs={{2,6},{3,1},{6,10},{7,3},{10,14},{11,7},{14,12},{15,11},{12,8},{13... | collective-permute-start | bytes 1966088 | tf_op jit(solution)/shard_map/ppermute | solution.py:234
  65.9 2.7 %step.11 = (f32[320,256]{1,0:T(8,128)S(1)}, f32[320,256]{1,0:T(8,128)S(1)}) custom-call(s32[8]{0:T(128)S(1)} %dynamic-slice_bitcast_fusion.order_ref, bf16[160,32768]{1,0:T(8,128)(2,1)} %refs_0_.7, bf16[160,32768]{1,0:T(8,128)(2,1)} %collective-permute-done.7.refs_1_.sib_ref, bf16[160,8192]{1,0:T(8,128)(2,1)} %refs_2_.7, ...), custom_call_target="tpu_custom_call" | custom-call | flops 419430400 | bytes 4259840 | tf_op jit(solution)/shard_map/step/pallas_call | solution.py:59
  68.6 0.0 copy-done.7
  68.6 2.8 %step.12 = (f32[320,256]{1,0:T(8,128)S(1)}, f32[320,256]{1,0:T(8,128)S(1)}) custom-call(s32[8]{0:T(128)S(1)} %dynamic-slice_bitcast_fusion.order_ref, bf16[160,32768]{1,0:T(8,128)(2,1)} %refs_0_.7, bf16[160,32768]{1,0:T(8,128)(2,1)} %collective-permute-done.7.refs_1_.sib_ref, bf16[160,8192]{1,0:T(8,128)(2,1)} %refs_2_.7, ...), custom_call_target="tpu_custom_call" | custom-call | flops 419430400 | bytes 4259840 | tf_op jit(solution)/shard_map/step/pallas_call | solution.py:59
  71.4 0.0 collective-permute-done.12.refs_4_
  71.4 1.6 %collective-permute-start.14 = (bf16[1280,256]{1,0:T(8,128)(2,1)S(1)}, bf16[1280,256]{1,0:T(8,128)(2,1)S(1)}, u32[]{:S(2)}, u32[]{:S(2)}) collective-permute-start(bf16[1280,256]{1,0:T(8,128)(2,1)S(1)} %collective-permute-done.12.refs_4_), channel_id=1, source_target_pairs={{2,6},{3,1},{6,10},{7,3},{10,14},{11,7},{14,12},{15,11},{12,8},{13... | collective-permute-start | bytes 1966088 | tf_op jit(solution)/shard_map/ppermute | solution.py:234
  73.0 4.9 %collective-permute-done.11.refs_5_ = bf16[1280,256]{1,0:T(8,128)(2,1)S(1)} collective-permute-done((bf16[1280,256]{1,0:T(8,128)(2,1)S(1)}, bf16[1280,256]{1,0:T(8,128)(2,1)S(1)}, u32[]{:S(2)}, u32[]{:S(2)}) %collective-permute-start.11) | collective-permute-done | bytes 655392 | tf_op jit(solution)/shard_map/ppermute | solution.py:234
  77.9 2.0 %collective-permute-start.13 = (bf16[1280,256]{1,0:T(8,128)(2,1)S(1)}, bf16[1280,256]{1,0:T(8,128)(2,1)S(1)}, u32[]{:S(2)}, u32[]{:S(2)}) collective-permute-start(bf16[1280,256]{1,0:T(8,128)(2,1)S(1)} %collective-permute-done.11.refs_5_), channel_id=1, source_target_pairs={{2,6},{3,1},{6,10},{7,3},{10,14},{11,7},{14,12},{15,11},{12,8},{13... | collective-permute-start | bytes 1966088 | tf_op jit(solution)/shard_map/ppermute | solution.py:234
  79.9 0.0 copy-done.8
  79.9 2.8 %step.13 = (f32[320,256]{1,0:T(8,128)S(1)}, f32[320,256]{1,0:T(8,128)S(1)}) custom-call(s32[8]{0:T(128)S(1)} %dynamic-slice_bitcast_fusion.order_ref, bf16[160,32768]{1,0:T(8,128)(2,1)} %refs_0_.7, bf16[160,32768]{1,0:T(8,128)(2,1)} %collective-permute-done.7.refs_1_.sib_ref, bf16[160,8192]{1,0:T(8,128)(2,1)} %refs_2_.7, ...), custom_call_target="tpu_custom_call" | custom-call | flops 419430400 | bytes 4259840 | tf_op jit(solution)/shard_map/step/pallas_call | solution.py:59
  82.7 2.3 %collective-permute-done.14.refs_4_ = bf16[1280,256]{1,0:T(8,128)(2,1)S(1)} collective-permute-done((bf16[1280,256]{1,0:T(8,128)(2,1)S(1)}, bf16[1280,256]{1,0:T(8,128)(2,1)S(1)}, u32[]{:S(2)}, u32[]{:S(2)}) %collective-permute-start.14) | collective-permute-done | bytes 655392 | tf_op jit(solution)/shard_map/ppermute | solution.py:234
  85.0 2.0 %collective-permute-start.16 = (bf16[1280,256]{1,0:T(8,128)(2,1)S(1)}, bf16[1280,256]{1,0:T(8,128)(2,1)S(1)}, u32[]{:S(2)}, u32[]{:S(2)}) collective-permute-start(bf16[1280,256]{1,0:T(8,128)(2,1)S(1)} %collective-permute-done.14.refs_4_), channel_id=1, source_target_pairs={{2,6},{3,1},{6,10},{7,3},{10,14},{11,7},{14,12},{15,11},{12,8},{13... | collective-permute-start | bytes 1966088 | tf_op jit(solution)/shard_map/ppermute | solution.py:234
  86.9 5.1 %collective-permute-done.13.refs_5_ = bf16[1280,256]{1,0:T(8,128)(2,1)S(1)} collective-permute-done((bf16[1280,256]{1,0:T(8,128)(2,1)S(1)}, bf16[1280,256]{1,0:T(8,128)(2,1)S(1)}, u32[]{:S(2)}, u32[]{:S(2)}) %collective-permute-start.13) | collective-permute-done | bytes 655392 | tf_op jit(solution)/shard_map/ppermute | solution.py:234
  92.0 2.0 %collective-permute-start.15 = (bf16[1280,256]{1,0:T(8,128)(2,1)S(1)}, bf16[1280,256]{1,0:T(8,128)(2,1)S(1)}, u32[]{:S(2)}, u32[]{:S(2)}) collective-permute-start(bf16[1280,256]{1,0:T(8,128)(2,1)S(1)} %collective-permute-done.13.refs_5_), channel_id=1, source_target_pairs={{2,6},{3,1},{6,10},{7,3},{10,14},{11,7},{14,12},{15,11},{12,8},{13... | collective-permute-start | bytes 1966088 | tf_op jit(solution)/shard_map/ppermute | solution.py:234
  94.0 1.9 %window.1.window_ref = bf16[320,1280]{1,0:T(8,128)(2,1)S(1)} custom-call(s32[8]{0:T(128)S(1)} %dynamic-slice_bitcast_fusion.order_ref, bf16[160,32768]{1,0:T(8,128)(2,1)} %refs_0_.7, bf16[160,32768]{1,0:T(8,128)(2,1)} %collective-permute-done.7.refs_1_.sib_ref), custom_call_target="tpu_custom_call" | custom-call | bytes 2129920 | tf_op jit(solution)/shard_map/window/pallas_call | solution.py:59
  95.8 0.0 copy-done.6
  95.8 2.8 %step.14 = (f32[320,256]{1,0:T(8,128)S(1)}, f32[320,256]{1,0:T(8,128)S(1)}) custom-call(s32[8]{0:T(128)S(1)} %dynamic-slice_bitcast_fusion.order_ref, bf16[160,32768]{1,0:T(8,128)(2,1)} %refs_0_.7, bf16[160,32768]{1,0:T(8,128)(2,1)} %collective-permute-done.7.refs_1_.sib_ref, bf16[160,8192]{1,0:T(8,128)(2,1)} %refs_2_.7, ...), custom_call_target="tpu_custom_call" | custom-call | flops 419430400 | bytes 4259840 | tf_op jit(solution)/shard_map/step/pallas_call | solution.py:59
  98.6 0.4 collective-permute-done.16.refs_4_
  99.0 2.3 %step.15 = (f32[320,256]{1,0:T(8,128)S(1)}, f32[320,256]{1,0:T(8,128)S(1)}) custom-call(s32[8]{0:T(128)S(1)} %dynamic-slice_bitcast_fusion.order_ref, bf16[160,32768]{1,0:T(8,128)(2,1)} %refs_0_.7, bf16[160,32768]{1,0:T(8,128)(2,1)} %collective-permute-done.7.refs_1_.sib_ref, bf16[160,8192]{1,0:T(8,128)(2,1)} %refs_2_.7, ...), custom_call_target="tpu_custom_call" | custom-call | flops 209715200 | bytes 3604480 | tf_op jit(solution)/shard_map/step/pallas_call | solution.py:59
  101.3 0.1 collective-permute-start.17
  101.4 0.0 copy-done.2
  101.4 0.0 copy-done.3
  101.4 0.5 collective-permute-start
  102.0 1.0 collective-permute-done
  103.0 3.0 %collective-permute-done.15.b_ref = bf16[1280,256]{1,0:T(8,128)(2,1)S(1)} collective-permute-done((bf16[1280,256]{1,0:T(8,128)(2,1)S(1)}, bf16[1280,256]{1,0:T(8,128)(2,1)S(1)}, u32[]{:S(2)}, u32[]{:S(2)}) %collective-permute-start.15) | collective-permute-done | bytes 655392 | tf_op jit(solution)/shard_map/ppermute | solution.py:234
  106.0 0.0 collective-permute-done.17.got_ref
  106.0 1.2 %score.1 = f32[32,8]{1,0:T(8,128)S(1)} custom-call(s32[2]{0:T(128)S(1)} %copy-done.2, s32[2]{0:T(128)S(1)} %copy-done.3, s32[2]{0:T(128)S(1)} %get-tuple-element.102.seq_sib, s32[2]{0:T(128)S(1)} %get-tuple-element.101.len_sib, bf16[320,1280]{1,0:T(8,128)(2,1)S(1)} %window.1.window_ref, bf16[1280,256]{1,0:T(8,128)(2,1)S(1)} %collective-permute-done.15.b_ref, ...), custom_call_target="tpu_custom_call" | custom-call | flops 209715200 | bytes 2457600 | tf_op jit(solution)/shard_map/score/pallas_call | solution.py:181
  107.2 12.7 %all_to_all.5 = f32[16,2,8]{2,1,0:T(2,128)S(1)} all-to-all(f32[16,2,8]{2,1,0:T(2,128)S(1)} %bitcast.9), channel_id=1, replica_groups=mesh['groups'=2,'dp'=16] {'dp'}, dimensions={0} | all-to-all | bytes 2048 | tf_op jit(solution)/shard_map/all_to_all | solution.py:255
  119.9 0.6 reduce_sum.9
  (6 shorter events, 0.0 us)
Async XLA Ops:
  2.4 36.2 %collective-permute-start.7 = (bf16[160,32768]{1,0:T(8,128)(2,1)}, bf16[160,32768]{1,0:T(8,128)(2,1)}, u32[]{:S(2)}, u32[]{:S(2)}) collective-permute-start(bf16[160,32768]{1,0:T(8,128)(2,1)} %refs_0_.7), channel_id=1, source_target_pairs={{0,1},{1,0},{2,3},{3,2},{4,5},{5,4},{6,7},{7,6},{8,9},{9,8},{10,11... | collective-permute-start | bytes 31457288 | tf_op jit(solution)/shard_map/ppermute | solution.py:220
  2.9 35.7 %collective-permute-start.8 = (bf16[160,8192]{1,0:T(8,128)(2,1)}, bf16[160,8192]{1,0:T(8,128)(2,1)}, u32[]{:S(2)}, u32[]{:S(2)}) collective-permute-start(bf16[160,8192]{1,0:T(8,128)(2,1)} %refs_2_.7), channel_id=1, source_target_pairs={{0,1},{1,0},{2,3},{3,2},{4,5},{5,4},{6,7},{7,6},{8,9},{9,8},{10,11... | collective-permute-start | bytes 7864328 | tf_op jit(solution)/shard_map/ppermute | solution.py:220
  3.0 11.8 %collective-permute-start.4 = (bf16[1280,256]{1,0:T(8,128)(2,1)}, bf16[1280,256]{1,0:T(8,128)(2,1)S(1)}, u32[]{:S(2)}, u32[]{:S(2)}) collective-permute-start(bf16[1280,256]{1,0:T(8,128)(2,1)} %get-tuple-element.56.refs_4_), channel_id=1, source_target_pairs={{2,6},{3,1},{6,10},{7,3},{10,14},{11,7},{14,12},{15,11},{12,8},{13... | collective-permute-start | bytes 1966088 | tf_op jit(solution)/shard_map/ppermute | solution.py:234
  5.9 15.9 %collective-permute-start.1 = (bf16[1280,256]{1,0:T(8,128)(2,1)}, bf16[1280,256]{1,0:T(8,128)(2,1)S(1)}, u32[]{:S(2)}, u32[]{:S(2)}) collective-permute-start(bf16[1280,256]{1,0:T(8,128)(2,1)} %get-tuple-element.55.refs_5_), channel_id=1, source_target_pairs={{2,6},{3,1},{6,10},{7,3},{10,14},{11,7},{14,12},{15,11},{12,8},{13... | collective-permute-start | bytes 1966088 | tf_op jit(solution)/shard_map/ppermute | solution.py:234
  14.7 14.0 %collective-permute-start.5 = (bf16[1280,256]{1,0:T(8,128)(2,1)S(1)}, bf16[1280,256]{1,0:T(8,128)(2,1)S(1)}, u32[]{:S(2)}, u32[]{:S(2)}) collective-permute-start(bf16[1280,256]{1,0:T(8,128)(2,1)S(1)} %collective-permute-done.4.refs_4_), channel_id=1, source_target_pairs={{2,6},{3,1},{6,10},{7,3},{10,14},{11,7},{14,12},{15,11},{12,8},{13... | collective-permute-start | bytes 1966088 | tf_op jit(solution)/shard_map/ppermute | solution.py:234
  21.8 21.5 %copy-start.5 = (bf16[1280,256]{1,0:T(8,128)(2,1)}, bf16[1280,256]{1,0:T(8,128)(2,1)S(1)}, u32[]{:S(2)}) copy-start(bf16[1280,256]{1,0:T(8,128)(2,1)S(1)} %collective-permute-done.1.refs_5_) | copy-start | bytes 1966084
  21.8 14.1 %collective-permute-start.2 = (bf16[1280,256]{1,0:T(8,128)(2,1)S(1)}, bf16[1280,256]{1,0:T(8,128)(2,1)}, u32[]{:S(2)}, u32[]{:S(2)}) collective-permute-start(bf16[1280,256]{1,0:T(8,128)(2,1)S(1)} %collective-permute-done.1.refs_5_), channel_id=1, source_target_pairs={{2,6},{3,1},{6,10},{7,3},{10,14},{11,7},{14,12},{15,11},{12,8},{13... | collective-permute-start | bytes 1966088 | tf_op jit(solution)/shard_map/ppermute | solution.py:234
  28.8 14.5 %collective-permute-start.6 = (bf16[1280,256]{1,0:T(8,128)(2,1)S(1)}, bf16[1280,256]{1,0:T(8,128)(2,1)S(1)}, u32[]{:S(2)}, u32[]{:S(2)}) collective-permute-start(bf16[1280,256]{1,0:T(8,128)(2,1)S(1)} %collective-permute-done.5.refs_4_), channel_id=1, source_target_pairs={{2,6},{3,1},{6,10},{7,3},{10,14},{11,7},{14,12},{15,11},{12,8},{13... | collective-permute-start | bytes 1966088 | tf_op jit(solution)/shard_map/ppermute | solution.py:234
  35.9 13.9 %collective-permute-start.3 = (bf16[1280,256]{1,0:T(8,128)(2,1)}, bf16[1280,256]{1,0:T(8,128)(2,1)S(1)}, u32[]{:S(2)}, u32[]{:S(2)}) collective-permute-start(bf16[1280,256]{1,0:T(8,128)(2,1)} %collective-permute-done.2.refs_5_), channel_id=1, source_target_pairs={{2,6},{3,1},{6,10},{7,3},{10,14},{11,7},{14,12},{15,11},{12,8},{13... | collective-permute-start | bytes 1966088 | tf_op jit(solution)/shard_map/ppermute | solution.py:234
  38.6 1.1 copy-start
  39.7 1.1 copy-start.1
  43.3 14.0 %collective-permute-start.10 = (bf16[1280,256]{1,0:T(8,128)(2,1)S(1)}, bf16[1280,256]{1,0:T(8,128)(2,1)S(1)}, u32[]{:S(2)}, u32[]{:S(2)}) collective-permute-start(bf16[1280,256]{1,0:T(8,128)(2,1)S(1)} %collective-permute-done.6.refs_4_), channel_id=1, source_target_pairs={{2,6},{3,1},{6,10},{7,3},{10,14},{11,7},{14,12},{15,11},{12,8},{13... | collective-permute-start | bytes 1966088 | tf_op jit(solution)/shard_map/ppermute | solution.py:234
  49.9 4.7 %copy-start.4 = (bf16[1280,256]{1,0:T(8,128)(2,1)}, bf16[1280,256]{1,0:T(8,128)(2,1)S(1)}, u32[]{:S(2)}) copy-start(bf16[1280,256]{1,0:T(8,128)(2,1)S(1)} %collective-permute-done.3.refs_5_) | copy-start | bytes 1966084
  49.9 14.0 %collective-permute-start.9 = (bf16[1280,256]{1,0:T(8,128)(2,1)S(1)}, bf16[1280,256]{1,0:T(8,128)(2,1)S(1)}, u32[]{:S(2)}, u32[]{:S(2)}) collective-permute-start(bf16[1280,256]{1,0:T(8,128)(2,1)S(1)} %collective-permute-done.3.refs_5_), channel_id=1, source_target_pairs={{2,6},{3,1},{6,10},{7,3},{10,14},{11,7},{14,12},{15,11},{12,8},{13... | collective-permute-start | bytes 1966088 | tf_op jit(solution)/shard_map/ppermute | solution.py:234
  57.3 14.1 %collective-permute-start.12 = (bf16[1280,256]{1,0:T(8,128)(2,1)S(1)}, bf16[1280,256]{1,0:T(8,128)(2,1)S(1)}, u32[]{:S(2)}, u32[]{:S(2)}) collective-permute-start(bf16[1280,256]{1,0:T(8,128)(2,1)S(1)} %collective-permute-done.10.refs_4_), channel_id=1, source_target_pairs={{2,6},{3,1},{6,10},{7,3},{10,14},{11,7},{14,12},{15,11},{12,8},{13... | collective-permute-start | bytes 1966088 | tf_op jit(solution)/shard_map/ppermute | solution.py:234
  63.9 4.7 %copy-start.7 = (bf16[1280,256]{1,0:T(8,128)(2,1)}, bf16[1280,256]{1,0:T(8,128)(2,1)S(1)}, u32[]{:S(2)}) copy-start(bf16[1280,256]{1,0:T(8,128)(2,1)S(1)} %collective-permute-done.9.refs_5_) | copy-start | bytes 1966084
  63.9 14.0 %collective-permute-start.11 = (bf16[1280,256]{1,0:T(8,128)(2,1)S(1)}, bf16[1280,256]{1,0:T(8,128)(2,1)S(1)}, u32[]{:S(2)}, u32[]{:S(2)}) collective-permute-start(bf16[1280,256]{1,0:T(8,128)(2,1)S(1)} %collective-permute-done.9.refs_5_), channel_id=1, source_target_pairs={{2,6},{3,1},{6,10},{7,3},{10,14},{11,7},{14,12},{15,11},{12,8},{13... | collective-permute-start | bytes 1966088 | tf_op jit(solution)/shard_map/ppermute | solution.py:234
  71.4 13.6 %collective-permute-start.14 = (bf16[1280,256]{1,0:T(8,128)(2,1)S(1)}, bf16[1280,256]{1,0:T(8,128)(2,1)S(1)}, u32[]{:S(2)}, u32[]{:S(2)}) collective-permute-start(bf16[1280,256]{1,0:T(8,128)(2,1)S(1)} %collective-permute-done.12.refs_4_), channel_id=1, source_target_pairs={{2,6},{3,1},{6,10},{7,3},{10,14},{11,7},{14,12},{15,11},{12,8},{13... | collective-permute-start | bytes 1966088 | tf_op jit(solution)/shard_map/ppermute | solution.py:234
  77.9 2.0 %copy-start.8 = (bf16[1280,256]{1,0:T(8,128)(2,1)}, bf16[1280,256]{1,0:T(8,128)(2,1)S(1)}, u32[]{:S(2)}) copy-start(bf16[1280,256]{1,0:T(8,128)(2,1)S(1)} %collective-permute-done.11.refs_5_) | copy-start | bytes 1966084
  77.9 14.0 %collective-permute-start.13 = (bf16[1280,256]{1,0:T(8,128)(2,1)S(1)}, bf16[1280,256]{1,0:T(8,128)(2,1)S(1)}, u32[]{:S(2)}, u32[]{:S(2)}) collective-permute-start(bf16[1280,256]{1,0:T(8,128)(2,1)S(1)} %collective-permute-done.11.refs_5_), channel_id=1, source_target_pairs={{2,6},{3,1},{6,10},{7,3},{10,14},{11,7},{14,12},{15,11},{12,8},{13... | collective-permute-start | bytes 1966088 | tf_op jit(solution)/shard_map/ppermute | solution.py:234
  85.0 14.0 %collective-permute-start.16 = (bf16[1280,256]{1,0:T(8,128)(2,1)S(1)}, bf16[1280,256]{1,0:T(8,128)(2,1)S(1)}, u32[]{:S(2)}, u32[]{:S(2)}) collective-permute-start(bf16[1280,256]{1,0:T(8,128)(2,1)S(1)} %collective-permute-done.14.refs_4_), channel_id=1, source_target_pairs={{2,6},{3,1},{6,10},{7,3},{10,14},{11,7},{14,12},{15,11},{12,8},{13... | collective-permute-start | bytes 1966088 | tf_op jit(solution)/shard_map/ppermute | solution.py:234
  92.0 3.9 %copy-start.6 = (bf16[1280,256]{1,0:T(8,128)(2,1)}, bf16[1280,256]{1,0:T(8,128)(2,1)S(1)}, u32[]{:S(2)}) copy-start(bf16[1280,256]{1,0:T(8,128)(2,1)S(1)} %collective-permute-done.13.refs_5_) | copy-start | bytes 1966084
  92.0 14.0 %collective-permute-start.15 = (bf16[1280,256]{1,0:T(8,128)(2,1)S(1)}, bf16[1280,256]{1,0:T(8,128)(2,1)S(1)}, u32[]{:S(2)}, u32[]{:S(2)}) collective-permute-start(bf16[1280,256]{1,0:T(8,128)(2,1)S(1)} %collective-permute-done.13.refs_5_), channel_id=1, source_target_pairs={{2,6},{3,1},{6,10},{7,3},{10,14},{11,7},{14,12},{15,11},{12,8},{13... | collective-permute-start | bytes 1966088 | tf_op jit(solution)/shard_map/ppermute | solution.py:234
  99.0 2.4 %copy-start.2 = (s32[2]{0:T(128)S(1)}, s32[2]{0:T(128)}, u32[]{:S(2)}) copy-start(s32[2]{0:T(128)} %seq_ref.1) | copy-start | bytes 28
  99.0 2.4 %copy-start.3 = (s32[2]{0:T(128)S(1)}, s32[2]{0:T(128)}, u32[]{:S(2)}) copy-start(s32[2]{0:T(128)} %len_ref.1) | copy-start | bytes 28
  101.3 4.7 %collective-permute-start.17 = (f32[320,256]{1,0:T(8,128)S(1)}, f32[320,256]{1,0:T(8,128)S(1)}, u32[]{:S(2)}, u32[]{:S(2)}) collective-permute-start(f32[320,256]{1,0:T(8,128)S(1)} %get-tuple-element.100.inn_ref), channel_id=1, source_target_pairs={{0,1},{1,0},{2,3},{3,2},{4,5},{5,4},{6,7},{7,6},{8,9},{9,8},{10,11... | collective-permute-start | bytes 983048 | tf_op jit(solution)/shard_map/ppermute | solution.py:248
  101.4 1.6 %collective-permute-start = (s32[2,2]{1,0:T(2,128)S(1)}, s32[2,2]{1,0:T(2,128)S(1)}, u32[]{:S(2)}, u32[]{:S(2)}) collective-permute-start(s32[2,2]{1,0:T(2,128)S(1)} %pad_add_fusion), channel_id=1, source_target_pairs={{0,1},{1,0},{2,3},{3,2},{4,5},{5,4},{6,7},{7,6},{8,9},{9,8},{10,11... | collective-permute-start | bytes 56 | tf_op jit(solution)/shard_map/ppermute | solution.py:219

commit v9 on v7

--- a/solution.py
+++ b/solution.py
@@ -71,79 +71,42 @@
     )(order, *[x for x, _, _ in windows], *whole, *scalars)
 
 
-def step_kernel(lead, rows_in, with_b, summed, order_ref, *refs):
-    refs = list(refs)
-    own_g, sib_g = refs.pop(0), refs.pop(0)
-    own_a, sib_a = (refs.pop(0), refs.pop(0)) if rows_in else (None, None)
-    a_ref = refs.pop(0)
-    b_ref = refs.pop(0) if with_b else None
-    tokens = own_g.shape[0]
-    for k, (g, a) in enumerate(((own_g, own_a), (sib_g, sib_a))):
-        at = pl.ds(k * tokens, tokens)
-        out = dot(g[:, :lead], a_ref[rows_in:])
-        if with_b:
-            out += dot(g[:, lead:], b_ref[...])
-        if summed:
-            out += refs[0][at]
-        if rows_in:
-            inn = dot(a[...], a_ref[:rows_in])
-            if summed:
-                inn += refs[1][at]
-            refs[-1][at] = inn
-            refs[-2][at] = out
-        else:
-            refs[-1][at] = out
-
-
-def step(order, own, sib, blocks, totals, s, lead, rows, rows_in):
-    here = lambda i, o: (0, o[s])
-    windows = [(own[0], rows, here), (sib[0], rows, here)]
-    if rows_in:
-        windows += [(own[1], rows_in, here), (sib[1], rows_in, here)]
-    tokens, columns = own[0].shape[0], blocks[0].shape[1]
-    depth = sum(b.shape[0] for b in blocks)
+def step_kernel(pieces, kinds, count, summed, order_ref, *refs):
+    windows = {kind: refs[2 * i:2 * i + 2] for i, kind in enumerate(kinds)}
+    blocks, refs = refs[2 * len(kinds):2 * len(kinds) + count], refs[2 * len(kinds) + count:]
+    tokens = windows[kinds[0]][0].shape[0]
+    for i, kind in enumerate(kinds):
+        for k in range(2):
+            at = pl.ds(k * tokens, tokens)
+            total = refs[i][at] if summed else 0.0
+            for which, row, height, of, column in pieces:
+                if of == kind:
+                    window = windows[kind][k][:, column:column + height]
+                    total += dot(window, blocks[which][row:row + height])
+            refs[i - len(kinds)][at] = total
+
+
+def step(order, tokens_of, blocks, pieces, totals, s):
+    kinds = sorted({piece[3] for piece in pieces})
+    windows = []
+    for kind in kinds:
+        own, sib, width = tokens_of[kind]
+        windows += [(x, width, lambda i, o: (0, o[s])) for x in (own, sib)]
+    tokens, columns = windows[0][0].shape[0], blocks[0].shape[1]
+    summed = all(kind in totals for kind in kinds)
     shape = jax.ShapeDtypeStruct((2 * tokens, columns), F32)
-    return call(
-        functools.partial(step_kernel, lead, rows_in, len(blocks) > 1, bool(totals)),
-        order, windows, list(blocks) + list(totals), [],
-        [shape] * (2 if rows_in else 1), 4 * tokens * depth * columns, "step",
+    out = call(
+        functools.partial(step_kernel, pieces, kinds, len(blocks), summed),
+        order, windows, list(blocks) + ([totals[k] for k in kinds] if summed else []), [],
+        [shape] * len(kinds), 4 * tokens * sum(p[2] for p in pieces) * columns, "step",
     )
-
-
-def join_kernel(in_ref, out_ref, a_ref, b_ref, sems):
-    rows_in = in_ref.shape[0]
-    lead, rest = a_ref.shape[0] - rows_in, b_ref.shape[0]
-    copies = [
-        pltpu.make_async_copy(in_ref, a_ref.at[pl.ds(0, rows_in)], sems.at[0]),
-        pltpu.make_async_copy(out_ref.at[pl.ds(0, lead)], a_ref.at[pl.ds(rows_in, lead)], sems.at[1]),
-        pltpu.make_async_copy(out_ref.at[pl.ds(lead, rest)], b_ref, sems.at[2]),
-    ]
-    for copy in copies:
-        copy.start()
-    for copy in copies:
-        copy.wait()
-
-
-def join(in_factors, out_factors, lead):
-    rows_in, columns = in_factors.shape
-    heights = [rows_in + lead, out_factors.shape[0] - lead]
-    return pl.pallas_call(
-        join_kernel,
-        in_specs=[pl.BlockSpec(memory_space=pltpu.HBM)] * 2,
-        out_specs=[pl.BlockSpec(memory_space=pltpu.VMEM)] * 2,
-        out_shape=[jax.ShapeDtypeStruct((h, columns), in_factors.dtype) for h in heights],
-        scratch_shapes=[pltpu.SemaphoreType.DMA((3,))],
-        cost_estimate=pl.CostEstimate(
-            flops=0, bytes_accessed=4 * sum(heights) * columns, transcendentals=0
-        ),
-        name="join",
-    )(in_factors, out_factors)
+    return {**totals, **dict(zip(kinds, out))}
 
 
 def window_kernel(lead, order_ref, own_ref, sib_ref, out_ref):
     tokens = own_ref.shape[0]
-    out_ref[:tokens] = own_ref[:, lead:]
-    out_ref[tokens:] = sib_ref[:, lead:]
+    out_ref[:tokens] = own_ref[:, :lead]
+    out_ref[tokens:] = sib_ref[:, :lead]
 
 
 def score_kernel(seq_ref, len_ref, seq_sib, len_sib, window_ref, b_ref, out_ref, inn_ref, got_ref,
@@ -203,52 +166,75 @@
     pairs = ring_pairs(chips)
     swap = [(d, d ^ 1) for d in range(devices)]
 
-    own = [grads, acts]
+    send = lambda x: lax.ppermute(x, "dp", pairs)
+    across = lambda x: lax.ppermute(x, "dp", swap)
+
     every = None
     if rows_in % 128:
         every = lax.all_gather(in_factors, "dp", axis=0, tiled=True)
-        own, rows_in = own[:1], 0
+        rows_in = 0
     lead = (rows - rows_in) // 2
+    tokens_of = {"out": (grads, across(grads), rows)}
     if rows_in:
-        held = [join(in_factors, out_factors, lead)]
-    else:
-        held = [(out_factors[:lead], out_factors[lead:])]
-
-    seq_sib, len_sib = lax.ppermute(jnp.stack([seq_slot, lengths]), "dp", swap)
-    sib = [lax.ppermute(x, "dp", swap) for x in own]
-    totals, summed = [], 0
+        tokens_of["in"] = (acts, across(acts), rows_in)
+    slots_sib = across(jnp.stack([seq_slot, lengths]))
+
+    inside = [(1, 0, rows_in, "in", 0)] if rows_in else []
+    held = [[out_factors] + [in_factors] * (rows_in > 0)]
+    pieces = [[(0, 0, rows, "out", 0)] + inside]
+    came = send(out_factors)
+    late, early = came[lead:], came[:lead]
+    if rows_in:
+        early = jnp.concatenate([send(in_factors), early])
+    totals, summed = {}, 0
 
     def sum_to(k, totals, summed):
         for j in range(summed, k):
-            totals = step(mine, own, sib, held[j], totals, j, lead, rows, rows_in)
+            totals = step(mine, tokens_of, held[j], pieces[j], totals, j)
         return totals, max(k, summed)
 
-    for s in range(chips - 1):
-        a, b = held[s]
+    last = chips - 1
+    for s in range(1, chips):
+        held.append([late, early])
+        pieces.append([(0, 0, rows - lead, "out", lead), (1, rows_in, lead, "out", 0)] + inside)
+        if s == last:
+            break
         if s >= 3:
             totals, summed = sum_to(min(2 * s - 5, s), totals, summed)
-            a, *totals = lax.optimization_barrier((a, *totals))
-            b, *totals = lax.optimization_barrier((b, *totals))
-        held.append((lax.ppermute(a, "dp", pairs), lax.ppermute(b, "dp", pairs)))
-    s = chips - 1
+            late, totals = lax.optimization_barrier((late, totals))
+            early, totals = lax.optimization_barrier((early, totals))
+        late = send(late)
+        if s < last - 1:
+            early = send(early)
+        else:
+            inner, early = early[:rows_in], early[rows_in:]
+            if rows_in:
+                inner = send(inner)
+            early = send(early)
+
     window = call(
         functools.partial(window_kernel, lead), mine,
-        [(x, rows, lambda i, o: (0, o[s])) for x in (own[0], sib[0])], [], [],
-        [jax.ShapeDtypeStruct((2 * tokens, rows - lead), grads.dtype)], 0, "window",
+        [(x, rows, lambda i, o: (0, o[last])) for x in tokens_of["out"][:2]], [], [],
+        [jax.ShapeDtypeStruct((2 * tokens, lead), grads.dtype)], 0, "window",
     )[0]
-    totals[0], window = lax.optimization_barrier((totals[0], window))
-    totals, summed = sum_to(s, totals, summed)
-    a, b = held[s]
-    totals = step(mine, own, sib, [a], totals, s, lead, rows, rows_in)
-    if every is not None:
+    totals, window, slots_sib = lax.optimization_barrier((totals, window, slots_sib))
+    seq_sib, len_sib = slots_sib
+    totals, summed = sum_to(last, totals, summed)
+    totals = step(mine, tokens_of, [late], pieces[last][:1], totals, last)
+    if rows_in:
+        totals, inner = lax.optimization_barrier((totals, inner))
+        totals = step(mine, tokens_of, [inner], [(0, 0, rows_in, "in", 0)], totals, last)
+        inn = totals["in"]
+    else:
         inn = dot(acts, every)
-        totals = [totals[0], jnp.concatenate([inn, jnp.zeros_like(inn)])]
-    got = lax.ppermute(totals[1], "dp", swap)
+        inn = jnp.concatenate([inn, jnp.zeros_like(inn)])
+    got = across(inn)
 
     slots = lengths.shape[0]
     queries = columns // RANK
     table = score_table(
-        [seq_slot, lengths, seq_sib, len_sib], [window, b, *totals, got], slots * devices, queries
+        [seq_slot, lengths, seq_sib, len_sib], [window, early, totals["out"], inn, got],
+        slots * devices, queries,
     )
     got = lax.all_to_all(table.reshape(devices, slots, queries), "dp", 0, 0, tiled=True)
     return jnp.sum(got, axis=0)

time: 121 us -> 119 us (0.983)
  local copies, waits for them, and re-layouts: 2.89 us -> 0.85 us
  starting transfers between devices: 28.3 us -> 29.9 us
    pallas_call x1 -> x0, Pallas kernels: 2.39 us -> none  [join(): pl.pallas_call(join_kernel, in_specs=[pl.BlockSpec(memory_space=pltpu.HBM...]
    unnamed x18 -> x16, local copies, waits for them, and re-layouts: 2.19 us -> 0.04 us
    pallas_call x9 -> x10, Pallas kernels: 23.2 us -> 25.1 us  [call(): pl.pallas_call(kernel, grid_spec=pltpu.PrefetchScalarGridSpec(num_scalar_...]
    ppermute x18 -> x19, starting transfers between devices: 28.3 us -> 29.9 us  [the longest x15 29.2 us: shards(): send = lambda x: lax.ppermute(x, 'dp', pairs)]
    ppermute x18 -> x19, waiting for transfers between devices: 49.1 us -> 48.5 us  [the longest x15 48.3 us: shards(): send = lambda x: lax.ppermute(x, 'dp', pairs)]
  transfers between devices with their start and end apart: 18 -> 19, of which waited for: 12 -> 12; matrix products, arithmetic and copies ran while one was open for 1% -> 1% of each run, Pallas kernels for 21% -> 21%
where the time goes in v9:
time: 119 us
  waiting for transfers between devices  48.5 us (41%)
  starting transfers between devices  29.9 us (25%)
  Pallas kernels  26.2 us (22%)
  blocking collectives  12.5 us (11%)
    ppermute x15, waiting for transfers between devices, shards(): send = lambda x: lax.ppermute(x, 'dp', pairs)  48.3 us
    ppermute x15, starting transfers between devices, shards(): send = lambda x: lax.ppermute(x, 'dp', pairs)  29.2 us
    pallas_call x10, Pallas kernels, call(): pl.pallas_call(kernel, grid_spec=pltpu.PrefetchScalarGridSpec(num_scalar_...  25.1 us
    all_to_all x1, blocking collectives, shards(): lax.all_to_all(table.reshape(devices, slots, queries), 'dp', 0, 0, tiled=...  12.5 us
  transfers between devices with their start and end apart: 19, of which 12 were waited for; matrix products, arithmetic and copies ran while one was open for 1% of the time, Pallas kernels for 21%

profile of v9, /device:TPU:0, one launch (start us, length us, event | category | flops | bytes accessed | tf_op | source)
XLA Modules:
  0.0 118.9 jit_solution(8580098036660353404)
XLA Ops:
  0.0 0.0 copy-start
  0.0 0.5 collective-permute-start.7
  0.5 0.1 collective-permute-start.6
  0.5 2.9 %collective-permute-start.1 = (bf16[2048,256]{1,0:T(8,128)(2,1)}, bf16[2048,256]{1,0:T(8,128)(2,1)S(1)}, u32[]{:S(2)}, u32[]{:S(2)}) collective-permute-start(bf16[2048,256]{1,0:T(8,128)(2,1)} %refs_4_.1), channel_id=1, source_target_pairs={{2,6},{3,1},{6,10},{7,3},{10,14},{11,7},{14,12},{15,11},{12,8},{13... | collective-permute-start | bytes 3145736 | tf_op jit(solution)/shard_map/ppermute | solution.py:169
  3.5 1.6 %collective-permute-start = (bf16[512,256]{1,0:T(8,128)(2,1)}, bf16[512,256]{1,0:T(8,128)(2,1)S(1)}, u32[]{:S(2)}, u32[]{:S(2)}) collective-permute-start(bf16[512,256]{1,0:T(8,128)(2,1)} %refs_5_.1), channel_id=1, source_target_pairs={{2,6},{3,1},{6,10},{7,3},{10,14},{11,7},{14,12},{15,11},{12,8},{13... | collective-permute-start | bytes 786440 | tf_op jit(solution)/shard_map/ppermute | solution.py:169
  5.1 11.5 %collective-permute-done.1 = bf16[2048,256]{1,0:T(8,128)(2,1)S(1)} collective-permute-done((bf16[2048,256]{1,0:T(8,128)(2,1)}, bf16[2048,256]{1,0:T(8,128)(2,1)S(1)}, u32[]{:S(2)}, u32[]{:S(2)}) %collective-permute-start.1) | collective-permute-done | bytes 1048608 | tf_op jit(solution)/shard_map/ppermute | solution.py:169
  16.6 2.0 %collective-permute-start.4 = (bf16[1280,256]{1,0:T(8,128)(2,1)S(1)}, bf16[1280,256]{1,0:T(8,128)(2,1)S(1)}, u32[]{:S(2)}, u32[]{:S(2)}) collective-permute-start(bf16[1280,256]{1,0:T(8,128)(2,1)S(1)} %slice.17.refs_4_), channel_id=1, source_target_pairs={{2,6},{3,1},{6,10},{7,3},{10,14},{11,7},{14,12},{15,11},{12,8},{13... | collective-permute-start | bytes 1966088 | tf_op jit(solution)/shard_map/ppermute | solution.py:169
  18.6 0.7 collective-permute-done
  19.4 0.0 copy-start.4
  19.4 2.0 %collective-permute-start.2 = (bf16[1280,256]{1,0:T(8,128)(2,1)S(1)}, bf16[1280,256]{1,0:T(8,128)(2,1)}, u32[]{:S(2)}, u32[]{:S(2)}) collective-permute-start(bf16[1280,256]{1,0:T(8,128)(2,1)S(1)} %pad_maximum_fusion.refs_5_), channel_id=1, source_target_pairs={{2,6},{3,1},{6,10},{7,3},{10,14},{11,7},{14,12},{15,11},{12,8},{13... | collective-permute-start | bytes 1966088 | tf_op jit(solution)/shard_map/ppermute | solution.py:169
  21.4 5.8 %collective-permute-done.4.refs_4_ = bf16[1280,256]{1,0:T(8,128)(2,1)S(1)} collective-permute-done((bf16[1280,256]{1,0:T(8,128)(2,1)S(1)}, bf16[1280,256]{1,0:T(8,128)(2,1)S(1)}, u32[]{:S(2)}, u32[]{:S(2)}) %collective-permute-start.4) | collective-permute-done | bytes 655392 | tf_op jit(solution)/shard_map/ppermute | solution.py:169
  27.2 0.0 copy-done.4
  27.2 2.0 %collective-permute-start.5 = (bf16[1280,256]{1,0:T(8,128)(2,1)S(1)}, bf16[1280,256]{1,0:T(8,128)(2,1)S(1)}, u32[]{:S(2)}, u32[]{:S(2)}) collective-permute-start(bf16[1280,256]{1,0:T(8,128)(2,1)S(1)} %collective-permute-done.4.refs_4_), channel_id=1, source_target_pairs={{2,6},{3,1},{6,10},{7,3},{10,14},{11,7},{14,12},{15,11},{12,8},{13... | collective-permute-start | bytes 1966088 | tf_op jit(solution)/shard_map/ppermute | solution.py:169
  29.2 5.2 %collective-permute-done.2.refs_5_ = bf16[1280,256]{1,0:T(8,128)(2,1)} collective-permute-done((bf16[1280,256]{1,0:T(8,128)(2,1)S(1)}, bf16[1280,256]{1,0:T(8,128)(2,1)}, u32[]{:S(2)}, u32[]{:S(2)}) %collective-permute-start.2) | collective-permute-done | bytes 655392 | tf_op jit(solution)/shard_map/ppermute | solution.py:169
  34.3 2.0 %collective-permute-start.3 = (bf16[1280,256]{1,0:T(8,128)(2,1)}, bf16[1280,256]{1,0:T(8,128)(2,1)}, u32[]{:S(2)}, u32[]{:S(2)}) collective-permute-start(bf16[1280,256]{1,0:T(8,128)(2,1)} %collective-permute-done.2.refs_5_), channel_id=1, source_target_pairs={{2,6},{3,1},{6,10},{7,3},{10,14},{11,7},{14,12},{15,11},{12,8},{13... | collective-permute-start | bytes 1966088 | tf_op jit(solution)/shard_map/ppermute | solution.py:169
  36.3 0.7 dynamic-slice_bitcast_fusion.order_ref
  37.0 0.0 collective-permute-done.6.refs_1_
  37.0 0.0 collective-permute-done.7.refs_3_.sib_ref.refs_1_
  37.0 0.0 copy-done
  37.0 0.0 copy-done.1
  37.0 2.6 %step.9 = (f32[320,256]{1,0:T(8,128)S(1)}, f32[320,256]{1,0:T(8,128)S(1)}) custom-call(s32[8]{0:T(128)S(1)} %dynamic-slice_bitcast_fusion.order_ref, bf16[160,8192]{1,0:T(8,128)(2,1)} %refs_0_.17, bf16[160,8192]{1,0:T(8,128)(2,1)} %collective-permute-done.6.refs_1_, bf16[160,32768]{1,0:T(8,128)(2,1)} %refs_0_.16, ...), custom_call_target="tpu_custom_call" | custom-call | flops 419430400 | bytes 3604480 | tf_op jit(solution)/shard_map/step/pallas_call | solution.py:59
  39.6 1.6 %collective-permute-done.5.refs_4_ = bf16[1280,256]{1,0:T(8,128)(2,1)S(1)} collective-permute-done((bf16[1280,256]{1,0:T(8,128)(2,1)S(1)}, bf16[1280,256]{1,0:T(8,128)(2,1)S(1)}, u32[]{:S(2)}, u32[]{:S(2)}) %collective-permute-start.5) | collective-permute-done | bytes 655392 | tf_op jit(solution)/shard_map/ppermute | solution.py:169
  41.3 2.0 %collective-permute-start.9 = (bf16[1280,256]{1,0:T(8,128)(2,1)S(1)}, bf16[1280,256]{1,0:T(8,128)(2,1)S(1)}, u32[]{:S(2)}, u32[]{:S(2)}) collective-permute-start(bf16[1280,256]{1,0:T(8,128)(2,1)S(1)} %collective-permute-done.5.refs_4_), channel_id=1, source_target_pairs={{2,6},{3,1},{6,10},{7,3},{10,14},{11,7},{14,12},{15,11},{12,8},{13... | collective-permute-start | bytes 1966088 | tf_op jit(solution)/shard_map/ppermute | solution.py:169
  43.2 5.2 %collective-permute-done.3.refs_5_ = bf16[1280,256]{1,0:T(8,128)(2,1)} collective-permute-done((bf16[1280,256]{1,0:T(8,128)(2,1)}, bf16[1280,256]{1,0:T(8,128)(2,1)}, u32[]{:S(2)}, u32[]{:S(2)}) %collective-permute-start.3) | collective-permute-done | bytes 655392 | tf_op jit(solution)/shard_map/ppermute | solution.py:169
  48.4 2.0 %collective-permute-start.8 = (bf16[1280,256]{1,0:T(8,128)(2,1)}, bf16[1280,256]{1,0:T(8,128)(2,1)S(1)}, u32[]{:S(2)}, u32[]{:S(2)}) collective-permute-start(bf16[1280,256]{1,0:T(8,128)(2,1)} %collective-permute-done.3.refs_5_), channel_id=1, source_target_pairs={{2,6},{3,1},{6,10},{7,3},{10,14},{11,7},{14,12},{15,11},{12,8},{13... | collective-permute-start | bytes 1966088 | tf_op jit(solution)/shard_map/ppermute | solution.py:169
  50.4 2.8 %step.10 = (f32[320,256]{1,0:T(8,128)S(1)}, f32[320,256]{1,0:T(8,128)S(1)}) custom-call(s32[8]{0:T(128)S(1)} %dynamic-slice_bitcast_fusion.order_ref, bf16[160,8192]{1,0:T(8,128)(2,1)} %refs_0_.17, bf16[160,8192]{1,0:T(8,128)(2,1)} %collective-permute-done.6.refs_1_, bf16[160,32768]{1,0:T(8,128)(2,1)} %refs_0_.16, ...), custom_call_target="tpu_custom_call" | custom-call | flops 419430400 | bytes 4259840 | tf_op jit(solution)/shard_map/step/pallas_call | solution.py:59
  53.1 2.8 %step.11 = (f32[320,256]{1,0:T(8,128)S(1)}, f32[320,256]{1,0:T(8,128)S(1)}) custom-call(s32[8]{0:T(128)S(1)} %dynamic-slice_bitcast_fusion.order_ref, bf16[160,8192]{1,0:T(8,128)(2,1)} %refs_0_.17, bf16[160,8192]{1,0:T(8,128)(2,1)} %collective-permute-done.6.refs_1_, bf16[160,32768]{1,0:T(8,128)(2,1)} %refs_0_.16, ...), custom_call_target="tpu_custom_call" | custom-call | flops 419430400 | bytes 4259840 | tf_op jit(solution)/shard_map/step/pallas_call | solution.py:59
  55.9 0.0 collective-permute-done.9.refs_4_
  55.9 1.6 %collective-permute-start.11 = (bf16[1280,256]{1,0:T(8,128)(2,1)S(1)}, bf16[1280,256]{1,0:T(8,128)(2,1)S(1)}, u32[]{:S(2)}, u32[]{:S(2)}) collective-permute-start(bf16[1280,256]{1,0:T(8,128)(2,1)S(1)} %collective-permute-done.9.refs_4_), channel_id=1, source_target_pairs={{2,6},{3,1},{6,10},{7,3},{10,14},{11,7},{14,12},{15,11},{12,8},{13... | collective-permute-start | bytes 1966088 | tf_op jit(solution)/shard_map/ppermute | solution.py:169
  57.6 4.8 %collective-permute-done.8.refs_5_ = bf16[1280,256]{1,0:T(8,128)(2,1)S(1)} collective-permute-done((bf16[1280,256]{1,0:T(8,128)(2,1)}, bf16[1280,256]{1,0:T(8,128)(2,1)S(1)}, u32[]{:S(2)}, u32[]{:S(2)}) %collective-permute-start.8) | collective-permute-done | bytes 655392 | tf_op jit(solution)/shard_map/ppermute | solution.py:169
  62.3 2.0 %collective-permute-start.10 = (bf16[1280,256]{1,0:T(8,128)(2,1)S(1)}, bf16[1280,256]{1,0:T(8,128)(2,1)S(1)}, u32[]{:S(2)}, u32[]{:S(2)}) collective-permute-start(bf16[1280,256]{1,0:T(8,128)(2,1)S(1)} %collective-permute-done.8.refs_5_), channel_id=1, source_target_pairs={{2,6},{3,1},{6,10},{7,3},{10,14},{11,7},{14,12},{15,11},{12,8},{13... | collective-permute-start | bytes 1966088 | tf_op jit(solution)/shard_map/ppermute | solution.py:169
  64.3 2.8 %step.12 = (f32[320,256]{1,0:T(8,128)S(1)}, f32[320,256]{1,0:T(8,128)S(1)}) custom-call(s32[8]{0:T(128)S(1)} %dynamic-slice_bitcast_fusion.order_ref, bf16[160,8192]{1,0:T(8,128)(2,1)} %refs_0_.17, bf16[160,8192]{1,0:T(8,128)(2,1)} %collective-permute-done.6.refs_1_, bf16[160,32768]{1,0:T(8,128)(2,1)} %refs_0_.16, ...), custom_call_target="tpu_custom_call" | custom-call | flops 419430400 | bytes 4259840 | tf_op jit(solution)/shard_map/step/pallas_call | solution.py:59
  67.1 0.0 copy-done.6
  67.1 2.8 %step.13 = (f32[320,256]{1,0:T(8,128)S(1)}, f32[320,256]{1,0:T(8,128)S(1)}) custom-call(s32[8]{0:T(128)S(1)} %dynamic-slice_bitcast_fusion.order_ref, bf16[160,8192]{1,0:T(8,128)(2,1)} %refs_0_.17, bf16[160,8192]{1,0:T(8,128)(2,1)} %collective-permute-done.6.refs_1_, bf16[160,32768]{1,0:T(8,128)(2,1)} %refs_0_.16, ...), custom_call_target="tpu_custom_call" | custom-call | flops 419430400 | bytes 4259840 | tf_op jit(solution)/shard_map/step/pallas_call | solution.py:59
  69.9 0.0 collective-permute-done.11.refs_4_
  69.9 0.0 copy-start.2
  69.9 0.0 copy-start.3
  69.9 1.6 %collective-permute-start.13 = (bf16[1280,256]{1,0:T(8,128)(2,1)S(1)}, bf16[1280,256]{1,0:T(8,128)(2,1)S(1)}, u32[]{:S(2)}, u32[]{:S(2)}) collective-permute-start(bf16[1280,256]{1,0:T(8,128)(2,1)S(1)} %collective-permute-done.11.refs_4_), channel_id=1, source_target_pairs={{2,6},{3,1},{6,10},{7,3},{10,14},{11,7},{14,12},{15,11},{12,8},{13... | collective-permute-start | bytes 1966088 | tf_op jit(solution)/shard_map/ppermute | solution.py:169
  71.5 4.8 %collective-permute-done.10.refs_5_ = bf16[1280,256]{1,0:T(8,128)(2,1)S(1)} collective-permute-done((bf16[1280,256]{1,0:T(8,128)(2,1)S(1)}, bf16[1280,256]{1,0:T(8,128)(2,1)S(1)}, u32[]{:S(2)}, u32[]{:S(2)}) %collective-permute-start.10) | collective-permute-done | bytes 655392 | tf_op jit(solution)/shard_map/ppermute | solution.py:169
  76.4 2.0 %collective-permute-start.12 = (bf16[1280,256]{1,0:T(8,128)(2,1)S(1)}, bf16[1280,256]{1,0:T(8,128)(2,1)S(1)}, u32[]{:S(2)}, u32[]{:S(2)}) collective-permute-start(bf16[1280,256]{1,0:T(8,128)(2,1)S(1)} %collective-permute-done.10.refs_5_), channel_id=1, source_target_pairs={{2,6},{3,1},{6,10},{7,3},{10,14},{11,7},{14,12},{15,11},{12,8},{13... | collective-permute-start | bytes 1966088 | tf_op jit(solution)/shard_map/ppermute | solution.py:169
  78.3 0.0 copy-done.7
  78.3 2.8 %step.14 = (f32[320,256]{1,0:T(8,128)S(1)}, f32[320,256]{1,0:T(8,128)S(1)}) custom-call(s32[8]{0:T(128)S(1)} %dynamic-slice_bitcast_fusion.order_ref, bf16[160,8192]{1,0:T(8,128)(2,1)} %refs_0_.17, bf16[160,8192]{1,0:T(8,128)(2,1)} %collective-permute-done.6.refs_1_, bf16[160,32768]{1,0:T(8,128)(2,1)} %refs_0_.16, ...), custom_call_target="tpu_custom_call" | custom-call | flops 419430400 | bytes 4259840 | tf_op jit(solution)/shard_map/step/pallas_call | solution.py:59
  81.1 2.3 %collective-permute-done.13.refs_4_ = bf16[1280,256]{1,0:T(8,128)(2,1)S(1)} collective-permute-done((bf16[1280,256]{1,0:T(8,128)(2,1)S(1)}, bf16[1280,256]{1,0:T(8,128)(2,1)S(1)}, u32[]{:S(2)}, u32[]{:S(2)}) %collective-permute-start.13) | collective-permute-done | bytes 655392 | tf_op jit(solution)/shard_map/ppermute | solution.py:169
  83.4 2.0 %collective-permute-start.16 = (bf16[1280,256]{1,0:T(8,128)(2,1)S(1)}, bf16[1280,256]{1,0:T(8,128)(2,1)S(1)}, u32[]{:S(2)}, u32[]{:S(2)}) collective-permute-start(bf16[1280,256]{1,0:T(8,128)(2,1)S(1)} %collective-permute-done.13.refs_4_), channel_id=1, source_target_pairs={{2,6},{3,1},{6,10},{7,3},{10,14},{11,7},{14,12},{15,11},{12,8},{13... | collective-permute-start | bytes 1966088 | tf_op jit(solution)/shard_map/ppermute | solution.py:169
  85.4 5.1 %collective-permute-done.12.refs_5_ = bf16[1280,256]{1,0:T(8,128)(2,1)S(1)} collective-permute-done((bf16[1280,256]{1,0:T(8,128)(2,1)S(1)}, bf16[1280,256]{1,0:T(8,128)(2,1)S(1)}, u32[]{:S(2)}, u32[]{:S(2)}) %collective-permute-start.12) | collective-permute-done | bytes 655392 | tf_op jit(solution)/shard_map/ppermute | solution.py:169
  90.4 2.0 %collective-permute-start.17 = (bf16[512,256]{1,0:T(8,128)(2,1)S(1)}, bf16[512,256]{1,0:T(8,128)(2,1)S(1)}, u32[]{:S(2)}, u32[]{:S(2)}) collective-permute-start(bf16[512,256]{1,0:T(8,128)(2,1)S(1)} %slice.15), channel_id=1, source_target_pairs={{2,6},{3,1},{6,10},{7,3},{10,14},{11,7},{14,12},{15,11},{12,8},{13... | collective-permute-start | bytes 786440 | tf_op jit(solution)/shard_map/ppermute | solution.py:169
  92.5 0.0 copy-done.2
  92.5 0.0 copy-done.3
  92.5 0.1 collective-permute-start.14
  92.5 1.9 %window.1.window_ref = bf16[320,768]{1,0:T(8,128)(2,1)S(1)} custom-call(s32[8]{0:T(128)S(1)} %dynamic-slice_bitcast_fusion.order_ref, bf16[160,32768]{1,0:T(8,128)(2,1)} %refs_0_.16, bf16[160,32768]{1,0:T(8,128)(2,1)} %collective-permute-done.7.refs_3_.sib_ref.refs_1_), custom_call_target="tpu_custom_call" | custom-call | bytes 1802240 | tf_op jit(solution)/shard_map/window/pallas_call | solution.py:59
  94.4 0.0 copy-done.5
  94.5 0.0 collective-permute-done.14
  94.5 1.6 %collective-permute-start.15 = (bf16[768,256]{1,0:T(8,128)(2,1)S(1)}, bf16[768,256]{1,0:T(8,128)(2,1)S(1)}, u32[]{:S(2)}, u32[]{:S(2)}) collective-permute-start(bf16[768,256]{1,0:T(8,128)(2,1)S(1)} %slice.14), channel_id=1, source_target_pairs={{2,6},{3,1},{6,10},{7,3},{10,14},{11,7},{14,12},{15,11},{12,8},{13... | collective-permute-start | bytes 1179656 | tf_op jit(solution)/shard_map/ppermute | solution.py:169
  96.1 2.8 %step.15 = (f32[320,256]{1,0:T(8,128)S(1)}, f32[320,256]{1,0:T(8,128)S(1)}) custom-call(s32[8]{0:T(128)S(1)} %dynamic-slice_bitcast_fusion.order_ref, bf16[160,8192]{1,0:T(8,128)(2,1)} %refs_0_.17, bf16[160,8192]{1,0:T(8,128)(2,1)} %collective-permute-done.6.refs_1_, bf16[160,32768]{1,0:T(8,128)(2,1)} %refs_0_.16, ...), custom_call_target="tpu_custom_call" | custom-call | flops 419430400 | bytes 4259840 | tf_op jit(solution)/shard_map/step/pallas_call | solution.py:59
  98.9 0.0 collective-permute-done.16.refs_2_
  98.9 2.2 %step.16.out_ref = f32[320,256]{1,0:T(8,128)S(1)} custom-call(s32[8]{0:T(128)S(1)} %dynamic-slice_bitcast_fusion.order_ref, bf16[160,32768]{1,0:T(8,128)(2,1)} %refs_0_.16, bf16[160,32768]{1,0:T(8,128)(2,1)} %collective-permute-done.7.refs_3_.sib_ref.refs_1_, bf16[1280,256]{1,0:T(8,128)(2,1)S(1)} %collective-permute-done.16.refs_2_, ...), custom_call_target="tpu_custom_call" | custom-call | flops 209715200 | bytes 2621440 | tf_op jit(solution)/shard_map/step/pallas_call | solution.py:59
  101.1 0.0 collective-permute-done.17.refs_2_
  101.1 1.8 %step.17.inn_ref = f32[320,256]{1,0:T(8,128)S(1)} custom-call(s32[8]{0:T(128)S(1)} %dynamic-slice_bitcast_fusion.order_ref, bf16[160,8192]{1,0:T(8,128)(2,1)} %refs_0_.17, bf16[160,8192]{1,0:T(8,128)(2,1)} %collective-permute-done.6.refs_1_, bf16[512,256]{1,0:T(8,128)(2,1)S(1)} %collective-permute-done.17.refs_2_, f32[320,256]{1,0:T(8,128)S(1)} %get-tuple-element.94.refs_3_), custom_call_target="tpu_custom_call" | custom-call | flops 83886080 | bytes 1245184 | tf_op jit(solution)/shard_map/step/pallas_call | solution.py:59
  102.9 0.1 collective-permute-start.18
  103.0 1.4 %collective-permute-done.15.b_ref = bf16[768,256]{1,0:T(8,128)(2,1)S(1)} collective-permute-done((bf16[768,256]{1,0:T(8,128)(2,1)S(1)}, bf16[768,256]{1,0:T(8,128)(2,1)S(1)}, u32[]{:S(2)}, u32[]{:S(2)}) %collective-permute-start.15) | collective-permute-done | bytes 393248 | tf_op jit(solution)/shard_map/ppermute | solution.py:169
  104.5 0.2 collective-permute-done.18.got_ref
  104.6 1.1 score.1
  105.7 12.5 %all_to_all.5 = f32[16,2,8]{2,1,0:T(2,128)S(1)} all-to-all(f32[16,2,8]{2,1,0:T(2,128)S(1)} %bitcast.9), channel_id=1, replica_groups=mesh['groups'=2,'dp'=16] {'dp'}, dimensions={0} | all-to-all | bytes 2048 | tf_op jit(solution)/shard_map/all_to_all | solution.py:239
  118.3 0.6 reduce_sum.9
  (11 shorter events, 0.2 us)
Async XLA Ops:
  0.0 37.0 %copy-start = (bf16[2048,256]{1,0:T(8,128)(2,1)S(1)}, bf16[2048,256]{1,0:T(8,128)(2,1)}, u32[]{:S(2)}) copy-start(bf16[2048,256]{1,0:T(8,128)(2,1)} %refs_4_.1) | copy-start | bytes 3145732
  0.0 37.0 %copy-start.1 = (bf16[512,256]{1,0:T(8,128)(2,1)S(1)}, bf16[512,256]{1,0:T(8,128)(2,1)}, u32[]{:S(2)}) copy-start(bf16[512,256]{1,0:T(8,128)(2,1)} %refs_5_.1) | copy-start | bytes 786436
  0.0 37.0 %collective-permute-start.7 = (bf16[160,32768]{1,0:T(8,128)(2,1)}, bf16[160,32768]{1,0:T(8,128)(2,1)}, u32[]{:S(2)}, u32[]{:S(2)}) collective-permute-start(bf16[160,32768]{1,0:T(8,128)(2,1)} %refs_0_.16), channel_id=1, source_target_pairs={{0,1},{1,0},{2,3},{3,2},{4,5},{5,4},{6,7},{7,6},{8,9},{9,8},{10,11... | collective-permute-start | bytes 31457288 | tf_op jit(solution)/shard_map/ppermute | solution.py:170
  0.5 36.5 %collective-permute-start.6 = (bf16[160,8192]{1,0:T(8,128)(2,1)}, bf16[160,8192]{1,0:T(8,128)(2,1)}, u32[]{:S(2)}, u32[]{:S(2)}) collective-permute-start(bf16[160,8192]{1,0:T(8,128)(2,1)} %refs_0_.17), channel_id=1, source_target_pairs={{0,1},{1,0},{2,3},{3,2},{4,5},{5,4},{6,7},{7,6},{8,9},{9,8},{10,11... | collective-permute-start | bytes 7864328 | tf_op jit(solution)/shard_map/ppermute | solution.py:170
  0.5 16.0 %collective-permute-start.1 = (bf16[2048,256]{1,0:T(8,128)(2,1)}, bf16[2048,256]{1,0:T(8,128)(2,1)S(1)}, u32[]{:S(2)}, u32[]{:S(2)}) collective-permute-start(bf16[2048,256]{1,0:T(8,128)(2,1)} %refs_4_.1), channel_id=1, source_target_pairs={{2,6},{3,1},{6,10},{7,3},{10,14},{11,7},{14,12},{15,11},{12,8},{13... | collective-permute-start | bytes 3145736 | tf_op jit(solution)/shard_map/ppermute | solution.py:169
  3.5 15.9 %collective-permute-start = (bf16[512,256]{1,0:T(8,128)(2,1)}, bf16[512,256]{1,0:T(8,128)(2,1)S(1)}, u32[]{:S(2)}, u32[]{:S(2)}) collective-permute-start(bf16[512,256]{1,0:T(8,128)(2,1)} %refs_5_.1), channel_id=1, source_target_pairs={{2,6},{3,1},{6,10},{7,3},{10,14},{11,7},{14,12},{15,11},{12,8},{13... | collective-permute-start | bytes 786440 | tf_op jit(solution)/shard_map/ppermute | solution.py:169
  16.6 10.6 %collective-permute-start.4 = (bf16[1280,256]{1,0:T(8,128)(2,1)S(1)}, bf16[1280,256]{1,0:T(8,128)(2,1)S(1)}, u32[]{:S(2)}, u32[]{:S(2)}) collective-permute-start(bf16[1280,256]{1,0:T(8,128)(2,1)S(1)} %slice.17.refs_4_), channel_id=1, source_target_pairs={{2,6},{3,1},{6,10},{7,3},{10,14},{11,7},{14,12},{15,11},{12,8},{13... | collective-permute-start | bytes 1966088 | tf_op jit(solution)/shard_map/ppermute | solution.py:169
  19.4 7.8 %copy-start.4 = (bf16[1280,256]{1,0:T(8,128)(2,1)}, bf16[1280,256]{1,0:T(8,128)(2,1)S(1)}, u32[]{:S(2)}) copy-start(bf16[1280,256]{1,0:T(8,128)(2,1)S(1)} %pad_maximum_fusion.refs_5_) | copy-start | bytes 1966084
  19.4 14.9 %collective-permute-start.2 = (bf16[1280,256]{1,0:T(8,128)(2,1)S(1)}, bf16[1280,256]{1,0:T(8,128)(2,1)}, u32[]{:S(2)}, u32[]{:S(2)}) collective-permute-start(bf16[1280,256]{1,0:T(8,128)(2,1)S(1)} %pad_maximum_fusion.refs_5_), channel_id=1, source_target_pairs={{2,6},{3,1},{6,10},{7,3},{10,14},{11,7},{14,12},{15,11},{12,8},{13... | collective-permute-start | bytes 1966088 | tf_op jit(solution)/shard_map/ppermute | solution.py:169
  27.2 14.0 %collective-permute-start.5 = (bf16[1280,256]{1,0:T(8,128)(2,1)S(1)}, bf16[1280,256]{1,0:T(8,128)(2,1)S(1)}, u32[]{:S(2)}, u32[]{:S(2)}) collective-permute-start(bf16[1280,256]{1,0:T(8,128)(2,1)S(1)} %collective-permute-done.4.refs_4_), channel_id=1, source_target_pairs={{2,6},{3,1},{6,10},{7,3},{10,14},{11,7},{14,12},{15,11},{12,8},{13... | collective-permute-start | bytes 1966088 | tf_op jit(solution)/shard_map/ppermute | solution.py:169
  34.3 14.0 %collective-permute-start.3 = (bf16[1280,256]{1,0:T(8,128)(2,1)}, bf16[1280,256]{1,0:T(8,128)(2,1)}, u32[]{:S(2)}, u32[]{:S(2)}) collective-permute-start(bf16[1280,256]{1,0:T(8,128)(2,1)} %collective-permute-done.2.refs_5_), channel_id=1, source_target_pairs={{2,6},{3,1},{6,10},{7,3},{10,14},{11,7},{14,12},{15,11},{12,8},{13... | collective-permute-start | bytes 1966088 | tf_op jit(solution)/shard_map/ppermute | solution.py:169
  41.3 14.7 %collective-permute-start.9 = (bf16[1280,256]{1,0:T(8,128)(2,1)S(1)}, bf16[1280,256]{1,0:T(8,128)(2,1)S(1)}, u32[]{:S(2)}, u32[]{:S(2)}) collective-permute-start(bf16[1280,256]{1,0:T(8,128)(2,1)S(1)} %collective-permute-done.5.refs_4_), channel_id=1, source_target_pairs={{2,6},{3,1},{6,10},{7,3},{10,14},{11,7},{14,12},{15,11},{12,8},{13... | collective-permute-start | bytes 1966088 | tf_op jit(solution)/shard_map/ppermute | solution.py:169
  48.4 13.9 %collective-permute-start.8 = (bf16[1280,256]{1,0:T(8,128)(2,1)}, bf16[1280,256]{1,0:T(8,128)(2,1)S(1)}, u32[]{:S(2)}, u32[]{:S(2)}) collective-permute-start(bf16[1280,256]{1,0:T(8,128)(2,1)} %collective-permute-done.3.refs_5_), channel_id=1, source_target_pairs={{2,6},{3,1},{6,10},{7,3},{10,14},{11,7},{14,12},{15,11},{12,8},{13... | collective-permute-start | bytes 1966088 | tf_op jit(solution)/shard_map/ppermute | solution.py:169
  55.9 13.9 %collective-permute-start.11 = (bf16[1280,256]{1,0:T(8,128)(2,1)S(1)}, bf16[1280,256]{1,0:T(8,128)(2,1)S(1)}, u32[]{:S(2)}, u32[]{:S(2)}) collective-permute-start(bf16[1280,256]{1,0:T(8,128)(2,1)S(1)} %collective-permute-done.9.refs_4_), channel_id=1, source_target_pairs={{2,6},{3,1},{6,10},{7,3},{10,14},{11,7},{14,12},{15,11},{12,8},{13... | collective-permute-start | bytes 1966088 | tf_op jit(solution)/shard_map/ppermute | solution.py:169
  62.3 4.7 %copy-start.6 = (bf16[1280,256]{1,0:T(8,128)(2,1)}, bf16[1280,256]{1,0:T(8,128)(2,1)S(1)}, u32[]{:S(2)}) copy-start(bf16[1280,256]{1,0:T(8,128)(2,1)S(1)} %collective-permute-done.8.refs_5_) | copy-start | bytes 1966084
  62.3 14.0 %collective-permute-start.10 = (bf16[1280,256]{1,0:T(8,128)(2,1)S(1)}, bf16[1280,256]{1,0:T(8,128)(2,1)S(1)}, u32[]{:S(2)}, u32[]{:S(2)}) collective-permute-start(bf16[1280,256]{1,0:T(8,128)(2,1)S(1)} %collective-permute-done.8.refs_5_), channel_id=1, source_target_pairs={{2,6},{3,1},{6,10},{7,3},{10,14},{11,7},{14,12},{15,11},{12,8},{13... | collective-permute-start | bytes 1966088 | tf_op jit(solution)/shard_map/ppermute | solution.py:169
  69.9 22.6 %copy-start.2 = (s32[2]{0:T(128)S(1)}, s32[2]{0:T(128)}, u32[]{:S(2)}) copy-start(s32[2]{0:T(128)} %seq_ref.1) | copy-start | bytes 28
  69.9 22.6 %copy-start.3 = (s32[2]{0:T(128)S(1)}, s32[2]{0:T(128)}, u32[]{:S(2)}) copy-start(s32[2]{0:T(128)} %len_ref.1) | copy-start | bytes 28
  69.9 13.5 %collective-permute-start.13 = (bf16[1280,256]{1,0:T(8,128)(2,1)S(1)}, bf16[1280,256]{1,0:T(8,128)(2,1)S(1)}, u32[]{:S(2)}, u32[]{:S(2)}) collective-permute-start(bf16[1280,256]{1,0:T(8,128)(2,1)S(1)} %collective-permute-done.11.refs_4_), channel_id=1, source_target_pairs={{2,6},{3,1},{6,10},{7,3},{10,14},{11,7},{14,12},{15,11},{12,8},{13... | collective-permute-start | bytes 1966088 | tf_op jit(solution)/shard_map/ppermute | solution.py:169
  76.4 2.0 %copy-start.7 = (bf16[1280,256]{1,0:T(8,128)(2,1)}, bf16[1280,256]{1,0:T(8,128)(2,1)S(1)}, u32[]{:S(2)}) copy-start(bf16[1280,256]{1,0:T(8,128)(2,1)S(1)} %collective-permute-done.10.refs_5_) | copy-start | bytes 1966084
  76.4 14.0 %collective-permute-start.12 = (bf16[1280,256]{1,0:T(8,128)(2,1)S(1)}, bf16[1280,256]{1,0:T(8,128)(2,1)S(1)}, u32[]{:S(2)}, u32[]{:S(2)}) collective-permute-start(bf16[1280,256]{1,0:T(8,128)(2,1)S(1)} %collective-permute-done.10.refs_5_), channel_id=1, source_target_pairs={{2,6},{3,1},{6,10},{7,3},{10,14},{11,7},{14,12},{15,11},{12,8},{13... | collective-permute-start | bytes 1966088 | tf_op jit(solution)/shard_map/ppermute | solution.py:169
  83.4 15.5 %collective-permute-start.16 = (bf16[1280,256]{1,0:T(8,128)(2,1)S(1)}, bf16[1280,256]{1,0:T(8,128)(2,1)S(1)}, u32[]{:S(2)}, u32[]{:S(2)}) collective-permute-start(bf16[1280,256]{1,0:T(8,128)(2,1)S(1)} %collective-permute-done.13.refs_4_), channel_id=1, source_target_pairs={{2,6},{3,1},{6,10},{7,3},{10,14},{11,7},{14,12},{15,11},{12,8},{13... | collective-permute-start | bytes 1966088 | tf_op jit(solution)/shard_map/ppermute | solution.py:169
  90.4 4.0 %copy-start.5 = (bf16[1280,256]{1,0:T(8,128)(2,1)}, bf16[1280,256]{1,0:T(8,128)(2,1)S(1)}, u32[]{:S(2)}) copy-start(bf16[1280,256]{1,0:T(8,128)(2,1)S(1)} %collective-permute-done.12.refs_5_) | copy-start | bytes 1966084
  90.4 10.7 %collective-permute-start.17 = (bf16[512,256]{1,0:T(8,128)(2,1)S(1)}, bf16[512,256]{1,0:T(8,128)(2,1)S(1)}, u32[]{:S(2)}, u32[]{:S(2)}) collective-permute-start(bf16[512,256]{1,0:T(8,128)(2,1)S(1)} %slice.15), channel_id=1, source_target_pairs={{2,6},{3,1},{6,10},{7,3},{10,14},{11,7},{14,12},{15,11},{12,8},{13... | collective-permute-start | bytes 786440 | tf_op jit(solution)/shard_map/ppermute | solution.py:169
  92.5 2.0 %collective-permute-start.14 = (s32[2,2]{1,0:T(2,128)S(1)}, s32[2,2]{1,0:T(2,128)S(1)}, u32[]{:S(2)}, u32[]{:S(2)}) collective-permute-start(s32[2,2]{1,0:T(2,128)S(1)} %pad_add_fusion), channel_id=1, source_target_pairs={{0,1},{1,0},{2,3},{3,2},{4,5},{5,4},{6,7},{7,6},{8,9},{9,8},{10,11... | collective-permute-start | bytes 56 | tf_op jit(solution)/shard_map/ppermute | solution.py:170
  94.5 10.0 %collective-permute-start.15 = (bf16[768,256]{1,0:T(8,128)(2,1)S(1)}, bf16[768,256]{1,0:T(8,128)(2,1)S(1)}, u32[]{:S(2)}, u32[]{:S(2)}) collective-permute-start(bf16[768,256]{1,0:T(8,128)(2,1)S(1)} %slice.14), channel_id=1, source_target_pairs={{2,6},{3,1},{6,10},{7,3},{10,14},{11,7},{14,12},{15,11},{12,8},{13... | collective-permute-start | bytes 1179656 | tf_op jit(solution)/shard_map/ppermute | solution.py:169
  102.9 1.7 %collective-permute-start.18 = (f32[320,256]{1,0:T(8,128)S(1)}, f32[320,256]{1,0:T(8,128)S(1)}, u32[]{:S(2)}, u32[]{:S(2)}) collective-permute-start(f32[320,256]{1,0:T(8,128)S(1)} %step.17.inn_ref), channel_id=1, source_target_pairs={{0,1},{1,0},{2,3},{3,2},{4,5},{5,4},{6,7},{7,6},{8,9},{9,8},{10,11... | collective-permute-start | bytes 983048 | tf_op jit(solution)/shard_map/ppermute | solution.py:170

commit v10 on v9

--- a/solution.py
+++ b/solution.py
@@ -12,6 +12,7 @@
 RANK = 32
 LEN = 80
 F32 = jnp.float32
+PAD = 8
 VMEM = 52 << 20
 
 
@@ -109,49 +110,98 @@
     out_ref[tokens:] = sib_ref[:, :lead]
 
 
-def score_kernel(seq_ref, len_ref, seq_sib, len_sib, window_ref, b_ref, out_ref, inn_ref, got_ref,
-                 table_ref):
+def score_kernel(per_device, me_ref, seq_ref, len_ref, seq_sib, len_sib, window_ref, b_ref, out_ref,
+                 inn_ref, got_ref, *tables):
     columns = b_ref.shape[1]
     tokens = window_ref.shape[0] // 2
     queries = columns // RANK
-    column = lax.broadcasted_iota(jnp.int32, (columns, queries), 0) // RANK
-    query = lax.broadcasted_iota(jnp.int32, (columns, queries), 1)
+    shape = tables[0].shape
+    column = lax.broadcasted_iota(jnp.int32, (columns, shape[1]), 0) // RANK
+    query = lax.broadcasted_iota(jnp.int32, (columns, shape[1]), 1)
     fold = (column == query).astype(F32)
     position = lax.broadcasted_iota(jnp.int32, (LEN, columns), 0)
-    row = lax.broadcasted_iota(jnp.int32, table_ref.shape, 0)
+    row = lax.broadcasted_iota(jnp.int32, shape, 0)
     out = out_ref[...] + dot(window_ref[...], b_ref[...])
-    sums, slots = [], []
+    sums, seqs = [], []
     for k, (seq, lens) in enumerate(((seq_ref, len_ref), (seq_sib, len_sib))):
         mine, other = pl.ds(k * tokens, tokens), pl.ds((1 - k) * tokens, tokens)
         contrib = out[k * tokens:(k + 1) * tokens] * (inn_ref[mine] + got_ref[other])
         for i in range(tokens // LEN):
             kept = jnp.where(position < lens[i], contrib[i * LEN:(i + 1) * LEN], 0.0)
             sums.append(jnp.sum(kept, axis=0, keepdims=True))
-            slots.append(seq[i])
+            seqs.append(seq[i])
     scores = jnp.dot(
         jnp.concatenate(sums), fold, precision=lax.Precision.HIGHEST, preferred_element_type=F32
     ) * (1.0 / math.sqrt(RANK * LEN))
-    table = jnp.zeros(table_ref.shape, F32)
-    for i, slot in enumerate(slots):
-        table = jnp.where(row == slot, scores[i:i + 1], table)
-    table_ref[...] = table
-
-
-def score_table(numbers, arrays, rows, queries):
+    me = me_ref[0]
+    for t, table_ref in enumerate(tables):
+        table = jnp.zeros(shape, F32)
+        for i, seq in enumerate(seqs):
+            at = seq
+            if len(tables) == 2:
+                chips = shape[0] // PAD
+                owner = lax.div(seq, per_device)
+                ahead = lax.rem(lax.div(owner, 2) - lax.div(me, 2) + chips, chips)
+                at = ahead * PAD + lax.rem(seq, per_device)
+                same = lax.rem(owner + me, 2) == t
+                at = jnp.where(same, at, -1)
+            table = jnp.where(row == at, scores[i:i + 1], table)
+        table_ref[...] = table
+
+
+def score_tables(numbers, arrays, per_device, shape, count):
     smem, vmem = (pl.BlockSpec(memory_space=m) for m in (pltpu.SMEM, pltpu.VMEM))
     window, block = arrays[:2]
     size = sum(x.size * x.dtype.itemsize for x in arrays)
     return pl.pallas_call(
-        score_kernel,
+        functools.partial(score_kernel, per_device),
         in_specs=[smem] * len(numbers) + [vmem] * len(arrays),
-        out_specs=vmem,
-        out_shape=jax.ShapeDtypeStruct((rows, queries), F32),
+        out_specs=[vmem] * count,
+        out_shape=[jax.ShapeDtypeStruct(shape, F32)] * count,
         cost_estimate=pl.CostEstimate(
             flops=2 * window.size * block.shape[1], bytes_accessed=size, transcendentals=0
         ),
         compiler_params=pltpu.CompilerParams(vmem_limit_bytes=16 << 20),
         name="score",
     )(*numbers, *arrays)
+
+
+def deal_kernel(mine_ref, got_ref, *outs):
+    for k, out_ref in enumerate(outs):
+        at = pl.ds(k * PAD, PAD)
+        out_ref[...] = mine_ref[at] + got_ref[at]
+
+
+def gather_kernel(*refs):
+    total = refs[0][...]
+    for ref in refs[1:-1]:
+        total += ref[...]
+    rows, queries = refs[-1].shape
+    refs[-1][...] = total[:rows, :queries]
+
+
+def exchange(tables, rows, queries):
+    chips = lax.axis_size("dp") // 2
+    vmem = pl.BlockSpec(memory_space=pltpu.VMEM)
+    got = lax.ppermute(tables[1], "dp", [(d, d ^ 1) for d in range(2 * chips)])
+    parts = pl.pallas_call(
+        deal_kernel,
+        in_specs=[vmem] * 2,
+        out_specs=[vmem] * chips,
+        out_shape=[jax.ShapeDtypeStruct((PAD, tables[0].shape[1]), F32)] * chips,
+        name="deal",
+    )(tables[0], got)
+    parts = list(parts)
+    for k in range(1, chips):
+        ahead = [(d, (d + 2 * k) % (2 * chips)) for d in range(2 * chips)]
+        parts[k] = lax.ppermute(parts[k], "dp", ahead)
+    return pl.pallas_call(
+        gather_kernel,
+        in_specs=[vmem] * chips,
+        out_specs=vmem,
+        out_shape=jax.ShapeDtypeStruct((rows, queries), F32),
+        name="gather",
+    )(*parts)
 
 
 def shards(acts, grads, out_factors, in_factors, seq_slot, lengths):
@@ -232,10 +282,12 @@
 
     slots = lengths.shape[0]
     queries = columns // RANK
-    table = score_table(
-        [seq_slot, lengths, seq_sib, len_sib], [window, early, totals["out"], inn, got],
-        slots * devices, queries,
-    )
+    numbers = [jnp.reshape(me, (1,)), seq_slot, lengths, seq_sib, len_sib]
+    arrays = [window, early, totals["out"], inn, got]
+    if chips <= 8 and slots <= PAD:
+        tables = score_tables(numbers, arrays, slots, (chips * PAD, 128), 2)
+        return exchange(tables, slots, queries)
+    table = score_tables(numbers, arrays, slots, (slots * devices, queries), 1)[0]
     got = lax.all_to_all(table.reshape(devices, slots, queries), "dp", 0, 0, tiled=True)
     return jnp.sum(got, axis=0)
 

time: 119 us -> 127 us (1.067)
  starting transfers between devices: 29.9 us -> 42.6 us
  blocking collectives: 12.5 us -> 0 us
  waiting for transfers between devices: 48.5 us -> 52 us
  Pallas kernels: 26.2 us -> 28.9 us
  local copies, waits for them, and re-layouts: 0.85 us -> 2.61 us
    ppermute x0 -> x8, starting transfers between devices: none -> 12.7 us  [the longest x7 12.6 us: exchange(): parts[k] = lax.ppermute(parts[k], 'dp', ahead)]
    all_to_all x1 -> x0, blocking collectives: 12.5 us -> none  [shards(): lax.all_to_all(table.reshape(devices, slots, queries), 'dp', 0, 0, tiled=...]
    ppermute x0 -> x8, waiting for transfers between devices: none -> 3.45 us  [the longest x7 2.38 us: exchange(): parts[k] = lax.ppermute(parts[k], 'dp', ahead)]
    pallas_call x1 -> x3, Pallas kernels: 1.11 us -> 3.84 us  [the longest x1 1.4 us: exchange(): pl.pallas_call(deal_kernel, in_specs=[vmem] * 2, out_specs=[vmem] * chips...]
    unnamed x16 -> x34, local copies, waits for them, and re-layouts: 0.04 us -> 1.8 us
  transfers between devices with their start and end apart: 19 -> 27, of which waited for: 12 -> 15; matrix products, arithmetic and copies ran while one was open for 1% -> 1% of each run, Pallas kernels for 21% -> 20%
where the time goes in v10:
time: 127 us; the launch traced here: 126 us
  waiting for transfers between devices  52 us (41%)
  starting transfers between devices  42.6 us (34%)
  Pallas kernels  28.9 us (23%)
  local copies, waits for them, and re-layouts  2.61 us (2%)
    ppermute x15, waiting for transfers between devices, shards(): send = lambda x: lax.ppermute(x, 'dp', pairs)  48.3 us
    ppermute x15, starting transfers between devices, shards(): send = lambda x: lax.ppermute(x, 'dp', pairs)  29.2 us
    pallas_call x10, Pallas kernels, call(): pl.pallas_call(kernel, grid_spec=pltpu.PrefetchScalarGridSpec(num_scalar_...  25.1 us
    ppermute x7, starting transfers between devices, exchange(): parts[k] = lax.ppermute(parts[k], 'dp', ahead)  12.6 us
  transfers between devices with their start and end apart: 27, of which 15 were waited for; matrix products, arithmetic and copies ran while one was open for 1% of the time, Pallas kernels for 20%

profile of v10, /device:TPU:0, one launch (start us, length us, event | category | flops | bytes accessed | tf_op | source)
XLA Modules:
  0.0 126.4 jit_solution(7826821735031174399)
XLA Ops:
  0.0 0.5 collective-permute-start.7
  0.5 0.1 collective-permute-start.6
  0.5 2.9 %collective-permute-start.1 = (bf16[2048,256]{1,0:T(8,128)(2,1)}, bf16[2048,256]{1,0:T(8,128)(2,1)S(1)}, u32[]{:S(2)}, u32[]{:S(2)}) collective-permute-start(bf16[2048,256]{1,0:T(8,128)(2,1)} %refs_4_.1), channel_id=1, source_target_pairs={{2,6},{3,1},{6,10},{7,3},{10,14},{11,7},{14,12},{15,11},{12,8},{13... | collective-permute-start | bytes 3145736 | tf_op jit(solution)/shard_map/ppermute | solution.py:219
  3.5 1.6 %collective-permute-start = (bf16[512,256]{1,0:T(8,128)(2,1)}, bf16[512,256]{1,0:T(8,128)(2,1)S(1)}, u32[]{:S(2)}, u32[]{:S(2)}) collective-permute-start(bf16[512,256]{1,0:T(8,128)(2,1)} %refs_5_.1), channel_id=1, source_target_pairs={{2,6},{3,1},{6,10},{7,3},{10,14},{11,7},{14,12},{15,11},{12,8},{13... | collective-permute-start | bytes 786440 | tf_op jit(solution)/shard_map/ppermute | solution.py:219
  5.1 11.5 %collective-permute-done.1 = bf16[2048,256]{1,0:T(8,128)(2,1)S(1)} collective-permute-done((bf16[2048,256]{1,0:T(8,128)(2,1)}, bf16[2048,256]{1,0:T(8,128)(2,1)S(1)}, u32[]{:S(2)}, u32[]{:S(2)}) %collective-permute-start.1) | collective-permute-done | bytes 1048608 | tf_op jit(solution)/shard_map/ppermute | solution.py:219
  16.6 2.0 %collective-permute-start.4 = (bf16[1280,256]{1,0:T(8,128)(2,1)S(1)}, bf16[1280,256]{1,0:T(8,128)(2,1)S(1)}, u32[]{:S(2)}, u32[]{:S(2)}) collective-permute-start(bf16[1280,256]{1,0:T(8,128)(2,1)S(1)} %slice.17.refs_4_), channel_id=1, source_target_pairs={{2,6},{3,1},{6,10},{7,3},{10,14},{11,7},{14,12},{15,11},{12,8},{13... | collective-permute-start | bytes 1966088 | tf_op jit(solution)/shard_map/ppermute | solution.py:219
  18.6 0.7 collective-permute-done
  19.4 2.0 %collective-permute-start.2 = (bf16[1280,256]{1,0:T(8,128)(2,1)S(1)}, bf16[1280,256]{1,0:T(8,128)(2,1)}, u32[]{:S(2)}, u32[]{:S(2)}) collective-permute-start(bf16[1280,256]{1,0:T(8,128)(2,1)S(1)} %pad_maximum_fusion.refs_5_), channel_id=1, source_target_pairs={{2,6},{3,1},{6,10},{7,3},{10,14},{11,7},{14,12},{15,11},{12,8},{13... | collective-permute-start | bytes 1966088 | tf_op jit(solution)/shard_map/ppermute | solution.py:219
  21.4 5.8 %collective-permute-done.4.refs_4_ = bf16[1280,256]{1,0:T(8,128)(2,1)S(1)} collective-permute-done((bf16[1280,256]{1,0:T(8,128)(2,1)S(1)}, bf16[1280,256]{1,0:T(8,128)(2,1)S(1)}, u32[]{:S(2)}, u32[]{:S(2)}) %collective-permute-start.4) | collective-permute-done | bytes 655392 | tf_op jit(solution)/shard_map/ppermute | solution.py:219
  27.2 2.0 %collective-permute-start.5 = (bf16[1280,256]{1,0:T(8,128)(2,1)S(1)}, bf16[1280,256]{1,0:T(8,128)(2,1)S(1)}, u32[]{:S(2)}, u32[]{:S(2)}) collective-permute-start(bf16[1280,256]{1,0:T(8,128)(2,1)S(1)} %collective-permute-done.4.refs_4_), channel_id=1, source_target_pairs={{2,6},{3,1},{6,10},{7,3},{10,14},{11,7},{14,12},{15,11},{12,8},{13... | collective-permute-start | bytes 1966088 | tf_op jit(solution)/shard_map/ppermute | solution.py:219
  29.2 5.2 %collective-permute-done.2.refs_5_ = bf16[1280,256]{1,0:T(8,128)(2,1)} collective-permute-done((bf16[1280,256]{1,0:T(8,128)(2,1)S(1)}, bf16[1280,256]{1,0:T(8,128)(2,1)}, u32[]{:S(2)}, u32[]{:S(2)}) %collective-permute-start.2) | collective-permute-done | bytes 655392 | tf_op jit(solution)/shard_map/ppermute | solution.py:219
  34.3 2.0 %collective-permute-start.3 = (bf16[1280,256]{1,0:T(8,128)(2,1)}, bf16[1280,256]{1,0:T(8,128)(2,1)}, u32[]{:S(2)}, u32[]{:S(2)}) collective-permute-start(bf16[1280,256]{1,0:T(8,128)(2,1)} %collective-permute-done.2.refs_5_), channel_id=1, source_target_pairs={{2,6},{3,1},{6,10},{7,3},{10,14},{11,7},{14,12},{15,11},{12,8},{13... | collective-permute-start | bytes 1966088 | tf_op jit(solution)/shard_map/ppermute | solution.py:219
  36.3 0.7 dynamic-slice_bitcast_fusion.order_ref
  37.0 0.0 collective-permute-done.6.refs_1_
  37.0 0.0 collective-permute-done.7.refs_3_.sib_ref.refs_1_
  37.0 2.6 %step.9 = (f32[320,256]{1,0:T(8,128)S(1)}, f32[320,256]{1,0:T(8,128)S(1)}) custom-call(s32[8]{0:T(128)S(1)} %dynamic-slice_bitcast_fusion.order_ref, bf16[160,8192]{1,0:T(8,128)(2,1)} %refs_0_.17, bf16[160,8192]{1,0:T(8,128)(2,1)} %collective-permute-done.6.refs_1_, bf16[160,32768]{1,0:T(8,128)(2,1)} %refs_0_.16, ...), custom_call_target="tpu_custom_call" | custom-call | flops 419430400 | bytes 3604480 | tf_op jit(solution)/shard_map/step/pallas_call | solution.py:60
  39.6 1.6 %collective-permute-done.5.refs_4_ = bf16[1280,256]{1,0:T(8,128)(2,1)S(1)} collective-permute-done((bf16[1280,256]{1,0:T(8,128)(2,1)S(1)}, bf16[1280,256]{1,0:T(8,128)(2,1)S(1)}, u32[]{:S(2)}, u32[]{:S(2)}) %collective-permute-start.5) | collective-permute-done | bytes 655392 | tf_op jit(solution)/shard_map/ppermute | solution.py:219
  41.3 2.0 %collective-permute-start.9 = (bf16[1280,256]{1,0:T(8,128)(2,1)S(1)}, bf16[1280,256]{1,0:T(8,128)(2,1)S(1)}, u32[]{:S(2)}, u32[]{:S(2)}) collective-permute-start(bf16[1280,256]{1,0:T(8,128)(2,1)S(1)} %collective-permute-done.5.refs_4_), channel_id=1, source_target_pairs={{2,6},{3,1},{6,10},{7,3},{10,14},{11,7},{14,12},{15,11},{12,8},{13... | collective-permute-start | bytes 1966088 | tf_op jit(solution)/shard_map/ppermute | solution.py:219
  43.2 5.2 %collective-permute-done.3.refs_5_ = bf16[1280,256]{1,0:T(8,128)(2,1)} collective-permute-done((bf16[1280,256]{1,0:T(8,128)(2,1)}, bf16[1280,256]{1,0:T(8,128)(2,1)}, u32[]{:S(2)}, u32[]{:S(2)}) %collective-permute-start.3) | collective-permute-done | bytes 655392 | tf_op jit(solution)/shard_map/ppermute | solution.py:219
  48.4 2.0 %collective-permute-start.8 = (bf16[1280,256]{1,0:T(8,128)(2,1)}, bf16[1280,256]{1,0:T(8,128)(2,1)S(1)}, u32[]{:S(2)}, u32[]{:S(2)}) collective-permute-start(bf16[1280,256]{1,0:T(8,128)(2,1)} %collective-permute-done.3.refs_5_), channel_id=1, source_target_pairs={{2,6},{3,1},{6,10},{7,3},{10,14},{11,7},{14,12},{15,11},{12,8},{13... | collective-permute-start | bytes 1966088 | tf_op jit(solution)/shard_map/ppermute | solution.py:219
  50.4 2.8 %step.10 = (f32[320,256]{1,0:T(8,128)S(1)}, f32[320,256]{1,0:T(8,128)S(1)}) custom-call(s32[8]{0:T(128)S(1)} %dynamic-slice_bitcast_fusion.order_ref, bf16[160,8192]{1,0:T(8,128)(2,1)} %refs_0_.17, bf16[160,8192]{1,0:T(8,128)(2,1)} %collective-permute-done.6.refs_1_, bf16[160,32768]{1,0:T(8,128)(2,1)} %refs_0_.16, ...), custom_call_target="tpu_custom_call" | custom-call | flops 419430400 | bytes 4259840 | tf_op jit(solution)/shard_map/step/pallas_call | solution.py:60
  53.1 2.8 %step.11 = (f32[320,256]{1,0:T(8,128)S(1)}, f32[320,256]{1,0:T(8,128)S(1)}) custom-call(s32[8]{0:T(128)S(1)} %dynamic-slice_bitcast_fusion.order_ref, bf16[160,8192]{1,0:T(8,128)(2,1)} %refs_0_.17, bf16[160,8192]{1,0:T(8,128)(2,1)} %collective-permute-done.6.refs_1_, bf16[160,32768]{1,0:T(8,128)(2,1)} %refs_0_.16, ...), custom_call_target="tpu_custom_call" | custom-call | flops 419430400 | bytes 4259840 | tf_op jit(solution)/shard_map/step/pallas_call | solution.py:60
  55.9 0.0 collective-permute-done.9.refs_4_
  55.9 1.6 %collective-permute-start.11 = (bf16[1280,256]{1,0:T(8,128)(2,1)S(1)}, bf16[1280,256]{1,0:T(8,128)(2,1)S(1)}, u32[]{:S(2)}, u32[]{:S(2)}) collective-permute-start(bf16[1280,256]{1,0:T(8,128)(2,1)S(1)} %collective-permute-done.9.refs_4_), channel_id=1, source_target_pairs={{2,6},{3,1},{6,10},{7,3},{10,14},{11,7},{14,12},{15,11},{12,8},{13... | collective-permute-start | bytes 1966088 | tf_op jit(solution)/shard_map/ppermute | solution.py:219
  57.6 4.8 %collective-permute-done.8.refs_5_ = bf16[1280,256]{1,0:T(8,128)(2,1)S(1)} collective-permute-done((bf16[1280,256]{1,0:T(8,128)(2,1)}, bf16[1280,256]{1,0:T(8,128)(2,1)S(1)}, u32[]{:S(2)}, u32[]{:S(2)}) %collective-permute-start.8) | collective-permute-done | bytes 655392 | tf_op jit(solution)/shard_map/ppermute | solution.py:219
  62.3 2.0 %collective-permute-start.10 = (bf16[1280,256]{1,0:T(8,128)(2,1)S(1)}, bf16[1280,256]{1,0:T(8,128)(2,1)S(1)}, u32[]{:S(2)}, u32[]{:S(2)}) collective-permute-start(bf16[1280,256]{1,0:T(8,128)(2,1)S(1)} %collective-permute-done.8.refs_5_), channel_id=1, source_target_pairs={{2,6},{3,1},{6,10},{7,3},{10,14},{11,7},{14,12},{15,11},{12,8},{13... | collective-permute-start | bytes 1966088 | tf_op jit(solution)/shard_map/ppermute | solution.py:219
  64.3 2.8 %step.12 = (f32[320,256]{1,0:T(8,128)S(1)}, f32[320,256]{1,0:T(8,128)S(1)}) custom-call(s32[8]{0:T(128)S(1)} %dynamic-slice_bitcast_fusion.order_ref, bf16[160,8192]{1,0:T(8,128)(2,1)} %refs_0_.17, bf16[160,8192]{1,0:T(8,128)(2,1)} %collective-permute-done.6.refs_1_, bf16[160,32768]{1,0:T(8,128)(2,1)} %refs_0_.16, ...), custom_call_target="tpu_custom_call" | custom-call | flops 419430400 | bytes 4259840 | tf_op jit(solution)/shard_map/step/pallas_call | solution.py:60
  67.1 2.8 %step.13 = (f32[320,256]{1,0:T(8,128)S(1)}, f32[320,256]{1,0:T(8,128)S(1)}) custom-call(s32[8]{0:T(128)S(1)} %dynamic-slice_bitcast_fusion.order_ref, bf16[160,8192]{1,0:T(8,128)(2,1)} %refs_0_.17, bf16[160,8192]{1,0:T(8,128)(2,1)} %collective-permute-done.6.refs_1_, bf16[160,32768]{1,0:T(8,128)(2,1)} %refs_0_.16, ...), custom_call_target="tpu_custom_call" | custom-call | flops 419430400 | bytes 4259840 | tf_op jit(solution)/shard_map/step/pallas_call | solution.py:60
  69.9 0.0 copy-start.3
  69.9 0.0 copy-start.4
  69.9 1.6 %collective-permute-start.13 = (bf16[1280,256]{1,0:T(8,128)(2,1)S(1)}, bf16[1280,256]{1,0:T(8,128)(2,1)S(1)}, u32[]{:S(2)}, u32[]{:S(2)}) collective-permute-start(bf16[1280,256]{1,0:T(8,128)(2,1)S(1)} %collective-permute-done.11.refs_4_), channel_id=1, source_target_pairs={{2,6},{3,1},{6,10},{7,3},{10,14},{11,7},{14,12},{15,11},{12,8},{13... | collective-permute-start | bytes 1966088 | tf_op jit(solution)/shard_map/ppermute | solution.py:219
  71.5 4.8 %collective-permute-done.10.refs_5_ = bf16[1280,256]{1,0:T(8,128)(2,1)S(1)} collective-permute-done((bf16[1280,256]{1,0:T(8,128)(2,1)S(1)}, bf16[1280,256]{1,0:T(8,128)(2,1)S(1)}, u32[]{:S(2)}, u32[]{:S(2)}) %collective-permute-start.10) | collective-permute-done | bytes 655392 | tf_op jit(solution)/shard_map/ppermute | solution.py:219
  76.4 2.0 %collective-permute-start.12 = (bf16[1280,256]{1,0:T(8,128)(2,1)S(1)}, bf16[1280,256]{1,0:T(8,128)(2,1)S(1)}, u32[]{:S(2)}, u32[]{:S(2)}) collective-permute-start(bf16[1280,256]{1,0:T(8,128)(2,1)S(1)} %collective-permute-done.10.refs_5_), channel_id=1, source_target_pairs={{2,6},{3,1},{6,10},{7,3},{10,14},{11,7},{14,12},{15,11},{12,8},{13... | collective-permute-start | bytes 1966088 | tf_op jit(solution)/shard_map/ppermute | solution.py:219
  78.3 2.8 %step.14 = (f32[320,256]{1,0:T(8,128)S(1)}, f32[320,256]{1,0:T(8,128)S(1)}) custom-call(s32[8]{0:T(128)S(1)} %dynamic-slice_bitcast_fusion.order_ref, bf16[160,8192]{1,0:T(8,128)(2,1)} %refs_0_.17, bf16[160,8192]{1,0:T(8,128)(2,1)} %collective-permute-done.6.refs_1_, bf16[160,32768]{1,0:T(8,128)(2,1)} %refs_0_.16, ...), custom_call_target="tpu_custom_call" | custom-call | flops 419430400 | bytes 4259840 | tf_op jit(solution)/shard_map/step/pallas_call | solution.py:60
  81.1 2.3 %collective-permute-done.13.refs_4_ = bf16[1280,256]{1,0:T(8,128)(2,1)S(1)} collective-permute-done((bf16[1280,256]{1,0:T(8,128)(2,1)S(1)}, bf16[1280,256]{1,0:T(8,128)(2,1)S(1)}, u32[]{:S(2)}, u32[]{:S(2)}) %collective-permute-start.13) | collective-permute-done | bytes 655392 | tf_op jit(solution)/shard_map/ppermute | solution.py:219
  83.4 2.0 %collective-permute-start.16 = (bf16[1280,256]{1,0:T(8,128)(2,1)S(1)}, bf16[1280,256]{1,0:T(8,128)(2,1)S(1)}, u32[]{:S(2)}, u32[]{:S(2)}) collective-permute-start(bf16[1280,256]{1,0:T(8,128)(2,1)S(1)} %collective-permute-done.13.refs_4_), channel_id=1, source_target_pairs={{2,6},{3,1},{6,10},{7,3},{10,14},{11,7},{14,12},{15,11},{12,8},{13... | collective-permute-start | bytes 1966088 | tf_op jit(solution)/shard_map/ppermute | solution.py:219
  85.4 5.1 %collective-permute-done.12.refs_5_ = bf16[1280,256]{1,0:T(8,128)(2,1)S(1)} collective-permute-done((bf16[1280,256]{1,0:T(8,128)(2,1)S(1)}, bf16[1280,256]{1,0:T(8,128)(2,1)S(1)}, u32[]{:S(2)}, u32[]{:S(2)}) %collective-permute-start.12) | collective-permute-done | bytes 655392 | tf_op jit(solution)/shard_map/ppermute | solution.py:219
  90.4 2.0 %collective-permute-start.17 = (bf16[512,256]{1,0:T(8,128)(2,1)S(1)}, bf16[512,256]{1,0:T(8,128)(2,1)S(1)}, u32[]{:S(2)}, u32[]{:S(2)}) collective-permute-start(bf16[512,256]{1,0:T(8,128)(2,1)S(1)} %slice.15), channel_id=1, source_target_pairs={{2,6},{3,1},{6,10},{7,3},{10,14},{11,7},{14,12},{15,11},{12,8},{13... | collective-permute-start | bytes 786440 | tf_op jit(solution)/shard_map/ppermute | solution.py:219
  92.5 0.1 collective-permute-start.14
  92.5 1.9 %window.1.window_ref = bf16[320,768]{1,0:T(8,128)(2,1)S(1)} custom-call(s32[8]{0:T(128)S(1)} %dynamic-slice_bitcast_fusion.order_ref, bf16[160,32768]{1,0:T(8,128)(2,1)} %refs_0_.16, bf16[160,32768]{1,0:T(8,128)(2,1)} %collective-permute-done.7.refs_3_.sib_ref.refs_1_), custom_call_target="tpu_custom_call" | custom-call | bytes 1802240 | tf_op jit(solution)/shard_map/window/pallas_call | solution.py:60
  94.5 1.6 %collective-permute-start.15 = (bf16[768,256]{1,0:T(8,128)(2,1)S(1)}, bf16[768,256]{1,0:T(8,128)(2,1)S(1)}, u32[]{:S(2)}, u32[]{:S(2)}) collective-permute-start(bf16[768,256]{1,0:T(8,128)(2,1)S(1)} %slice.14), channel_id=1, source_target_pairs={{2,6},{3,1},{6,10},{7,3},{10,14},{11,7},{14,12},{15,11},{12,8},{13... | collective-permute-start | bytes 1179656 | tf_op jit(solution)/shard_map/ppermute | solution.py:219
  96.1 2.8 %step.15 = (f32[320,256]{1,0:T(8,128)S(1)}, f32[320,256]{1,0:T(8,128)S(1)}) custom-call(s32[8]{0:T(128)S(1)} %dynamic-slice_bitcast_fusion.order_ref, bf16[160,8192]{1,0:T(8,128)(2,1)} %refs_0_.17, bf16[160,8192]{1,0:T(8,128)(2,1)} %collective-permute-done.6.refs_1_, bf16[160,32768]{1,0:T(8,128)(2,1)} %refs_0_.16, ...), custom_call_target="tpu_custom_call" | custom-call | flops 419430400 | bytes 4259840 | tf_op jit(solution)/shard_map/step/pallas_call | solution.py:60
  98.9 2.2 %step.16.out_ref = f32[320,256]{1,0:T(8,128)S(1)} custom-call(s32[8]{0:T(128)S(1)} %dynamic-slice_bitcast_fusion.order_ref, bf16[160,32768]{1,0:T(8,128)(2,1)} %refs_0_.16, bf16[160,32768]{1,0:T(8,128)(2,1)} %collective-permute-done.7.refs_3_.sib_ref.refs_1_, bf16[1280,256]{1,0:T(8,128)(2,1)S(1)} %collective-permute-done.16.refs_2_, ...), custom_call_target="tpu_custom_call" | custom-call | flops 209715200 | bytes 2621440 | tf_op jit(solution)/shard_map/step/pallas_call | solution.py:60
  101.1 1.8 %step.17.inn_ref = f32[320,256]{1,0:T(8,128)S(1)} custom-call(s32[8]{0:T(128)S(1)} %dynamic-slice_bitcast_fusion.order_ref, bf16[160,8192]{1,0:T(8,128)(2,1)} %refs_0_.17, bf16[160,8192]{1,0:T(8,128)(2,1)} %collective-permute-done.6.refs_1_, bf16[512,256]{1,0:T(8,128)(2,1)S(1)} %collective-permute-done.17.refs_2_, f32[320,256]{1,0:T(8,128)S(1)} %get-tuple-element.104.refs_3_), custom_call_target="tpu_custom_call" | custom-call | flops 83886080 | bytes 1245184 | tf_op jit(solution)/shard_map/step/pallas_call | solution.py:60
  102.9 0.1 collective-permute-start.18
  103.0 1.4 %collective-permute-done.15.b_ref = bf16[768,256]{1,0:T(8,128)(2,1)S(1)} collective-permute-done((bf16[768,256]{1,0:T(8,128)(2,1)S(1)}, bf16[768,256]{1,0:T(8,128)(2,1)S(1)}, u32[]{:S(2)}, u32[]{:S(2)}) %collective-permute-start.15) | collective-permute-done | bytes 393248 | tf_op jit(solution)/shard_map/ppermute | solution.py:219
  104.5 0.2 collective-permute-done.18.got_ref
  104.6 1.1 score.1
  105.8 0.6 copy-done.2
  106.4 0.1 collective-permute-start.19
  106.5 1.1 collective-permute-done.19.got_ref
  107.6 0.6 copy-done.9
  108.2 1.4 %deal.1 = (f32[8,128]{1,0:T(8,128)}, f32[8,128]{1,0:T(8,128)}, f32[8,128]{1,0:T(8,128)}, f32[8,128]{1,0:T(8,128)}, f32[8,128]{1,0:T(8,128)}, /*index=5*/f32[8,12...) custom-call(f32[64,128]{1,0:T(8,128)} %copy-done.2, f32[64,128]{1,0:T(8,128)} %copy-done.9), custom_call_target="tpu_custom_call" | custom-call | tf_op jit(solution)/shard_map/deal/pallas_call | solution.py:187
  109.6 1.8 %collective-permute-start.20 = (f32[8,128]{1,0:T(8,128)}, f32[8,128]{1,0:T(8,128)S(1)}, u32[]{:S(2)}, u32[]{:S(2)}) collective-permute-start(f32[8,128]{1,0:T(8,128)} %get-tuple-element.108), channel_id=1, source_target_pairs={{0,2},{1,3},{2,4},{3,5},{4,6},{5,7},{6,8},{7,9},{8,10},{9,11},{10,... | collective-permute-start | bytes 12296 | tf_op jit(solution)/shard_map/ppermute | solution.py:197
  111.4 1.6 %collective-permute-start.21 = (f32[8,128]{1,0:T(8,128)}, f32[8,128]{1,0:T(8,128)S(1)}, u32[]{:S(2)}, u32[]{:S(2)}) collective-permute-start(f32[8,128]{1,0:T(8,128)} %get-tuple-element.109), channel_id=1, source_target_pairs={{0,4},{1,5},{2,6},{3,7},{4,8},{5,9},{6,10},{7,11},{8,12},{9,13},{1... | collective-permute-start | bytes 12296 | tf_op jit(solution)/shard_map/ppermute | solution.py:197
  113.0 2.5 %collective-permute-start.22 = (f32[8,128]{1,0:T(8,128)}, f32[8,128]{1,0:T(8,128)S(1)}, u32[]{:S(2)}, u32[]{:S(2)}) collective-permute-start(f32[8,128]{1,0:T(8,128)} %get-tuple-element.110), channel_id=1, source_target_pairs={{0,6},{1,7},{2,8},{3,9},{4,10},{5,11},{6,12},{7,13},{8,14},{9,15},... | collective-permute-start | bytes 12296 | tf_op jit(solution)/shard_map/ppermute | solution.py:197
  115.5 1.2 collective-permute-start.23
  116.7 2.6 %collective-permute-start.24 = (f32[8,128]{1,0:T(8,128)}, f32[8,128]{1,0:T(8,128)S(1)}, u32[]{:S(2)}, u32[]{:S(2)}) collective-permute-start(f32[8,128]{1,0:T(8,128)} %get-tuple-element.112), channel_id=1, source_target_pairs={{0,10},{1,11},{2,12},{3,13},{4,14},{5,15},{6,0},{7,1},{8,2},{9,3},... | collective-permute-start | bytes 12296 | tf_op jit(solution)/shard_map/ppermute | solution.py:197
  119.4 1.3 %collective-permute-start.25 = (f32[8,128]{1,0:T(8,128)}, f32[8,128]{1,0:T(8,128)S(1)}, u32[]{:S(2)}, u32[]{:S(2)}) collective-permute-start(f32[8,128]{1,0:T(8,128)} %get-tuple-element.113), channel_id=1, source_target_pairs={{0,12},{1,13},{2,14},{3,15},{4,0},{5,1},{6,2},{7,3},{8,4},{9,5},{1... | collective-permute-start | bytes 12296 | tf_op jit(solution)/shard_map/ppermute | solution.py:197
  120.8 1.4 %collective-permute-start.26 = (f32[8,128]{1,0:T(8,128)}, f32[8,128]{1,0:T(8,128)S(1)}, u32[]{:S(2)}, u32[]{:S(2)}) collective-permute-start(f32[8,128]{1,0:T(8,128)} %get-tuple-element.114), channel_id=1, source_target_pairs={{0,14},{1,15},{2,0},{3,1},{4,2},{5,3},{6,4},{7,5},{8,6},{9,7},{10,... | collective-permute-start | bytes 12296 | tf_op jit(solution)/shard_map/ppermute | solution.py:197
  122.2 1.0 collective-permute-done.25.refs_6_
  123.2 1.4 %collective-permute-done.26.refs_7_ = f32[8,128]{1,0:T(8,128)S(1)} collective-permute-done((f32[8,128]{1,0:T(8,128)}, f32[8,128]{1,0:T(8,128)S(1)}, u32[]{:S(2)}, u32[]{:S(2)}) %collective-permute-start.26) | collective-permute-done | bytes 4128 | tf_op jit(solution)/shard_map/ppermute | solution.py:197
  124.6 0.5 copy-done.16
  125.2 1.3 %gather.1 = f32[2,8]{1,0:T(2,128)} custom-call(f32[8,128]{1,0:T(8,128)} %get-tuple-element.107.refs_0_, f32[8,128]{1,0:T(8,128)} %copy-done.10, f32[8,128]{1,0:T(8,128)} %copy-done.11, f32[8,128]{1,0:T(8,128)} %copy-done.12, f32[8,128]{1,0:T(8,128)} %copy-done.13, f32[8,128]{1,0:T(8,128)} %copy-done.14, f32[8,128]{1,0:T(8,128)} %copy-done.15, ...), custom_call_target="tpu_custom_call" | custom-call | tf_op jit(solution)/shard_map/gather/pallas_call | solution.py:198
  (45 shorter events, 0.3 us)
Async XLA Ops:
  0.0 37.0 %copy-start = (bf16[2048,256]{1,0:T(8,128)(2,1)S(1)}, bf16[2048,256]{1,0:T(8,128)(2,1)}, u32[]{:S(2)}) copy-start(bf16[2048,256]{1,0:T(8,128)(2,1)} %refs_4_.1) | copy-start | bytes 3145732
  0.0 37.0 %copy-start.1 = (bf16[512,256]{1,0:T(8,128)(2,1)S(1)}, bf16[512,256]{1,0:T(8,128)(2,1)}, u32[]{:S(2)}) copy-start(bf16[512,256]{1,0:T(8,128)(2,1)} %refs_5_.1) | copy-start | bytes 786436
  0.0 37.0 %collective-permute-start.7 = (bf16[160,32768]{1,0:T(8,128)(2,1)}, bf16[160,32768]{1,0:T(8,128)(2,1)}, u32[]{:S(2)}, u32[]{:S(2)}) collective-permute-start(bf16[160,32768]{1,0:T(8,128)(2,1)} %refs_0_.16), channel_id=1, source_target_pairs={{0,1},{1,0},{2,3},{3,2},{4,5},{5,4},{6,7},{7,6},{8,9},{9,8},{10,11... | collective-permute-start | bytes 31457288 | tf_op jit(solution)/shard_map/ppermute | solution.py:220
  0.5 36.5 %collective-permute-start.6 = (bf16[160,8192]{1,0:T(8,128)(2,1)}, bf16[160,8192]{1,0:T(8,128)(2,1)}, u32[]{:S(2)}, u32[]{:S(2)}) collective-permute-start(bf16[160,8192]{1,0:T(8,128)(2,1)} %refs_0_.17), channel_id=1, source_target_pairs={{0,1},{1,0},{2,3},{3,2},{4,5},{5,4},{6,7},{7,6},{8,9},{9,8},{10,11... | collective-permute-start | bytes 7864328 | tf_op jit(solution)/shard_map/ppermute | solution.py:220
  0.5 16.0 %collective-permute-start.1 = (bf16[2048,256]{1,0:T(8,128)(2,1)}, bf16[2048,256]{1,0:T(8,128)(2,1)S(1)}, u32[]{:S(2)}, u32[]{:S(2)}) collective-permute-start(bf16[2048,256]{1,0:T(8,128)(2,1)} %refs_4_.1), channel_id=1, source_target_pairs={{2,6},{3,1},{6,10},{7,3},{10,14},{11,7},{14,12},{15,11},{12,8},{13... | collective-permute-start | bytes 3145736 | tf_op jit(solution)/shard_map/ppermute | solution.py:219
  3.5 15.9 %collective-permute-start = (bf16[512,256]{1,0:T(8,128)(2,1)}, bf16[512,256]{1,0:T(8,128)(2,1)S(1)}, u32[]{:S(2)}, u32[]{:S(2)}) collective-permute-start(bf16[512,256]{1,0:T(8,128)(2,1)} %refs_5_.1), channel_id=1, source_target_pairs={{2,6},{3,1},{6,10},{7,3},{10,14},{11,7},{14,12},{15,11},{12,8},{13... | collective-permute-start | bytes 786440 | tf_op jit(solution)/shard_map/ppermute | solution.py:219
  16.6 10.6 %collective-permute-start.4 = (bf16[1280,256]{1,0:T(8,128)(2,1)S(1)}, bf16[1280,256]{1,0:T(8,128)(2,1)S(1)}, u32[]{:S(2)}, u32[]{:S(2)}) collective-permute-start(bf16[1280,256]{1,0:T(8,128)(2,1)S(1)} %slice.17.refs_4_), channel_id=1, source_target_pairs={{2,6},{3,1},{6,10},{7,3},{10,14},{11,7},{14,12},{15,11},{12,8},{13... | collective-permute-start | bytes 1966088 | tf_op jit(solution)/shard_map/ppermute | solution.py:219
  19.4 7.8 %copy-start.5 = (bf16[1280,256]{1,0:T(8,128)(2,1)}, bf16[1280,256]{1,0:T(8,128)(2,1)S(1)}, u32[]{:S(2)}) copy-start(bf16[1280,256]{1,0:T(8,128)(2,1)S(1)} %pad_maximum_fusion.refs_5_) | copy-start | bytes 1966084
  19.4 14.9 %collective-permute-start.2 = (bf16[1280,256]{1,0:T(8,128)(2,1)S(1)}, bf16[1280,256]{1,0:T(8,128)(2,1)}, u32[]{:S(2)}, u32[]{:S(2)}) collective-permute-start(bf16[1280,256]{1,0:T(8,128)(2,1)S(1)} %pad_maximum_fusion.refs_5_), channel_id=1, source_target_pairs={{2,6},{3,1},{6,10},{7,3},{10,14},{11,7},{14,12},{15,11},{12,8},{13... | collective-permute-start | bytes 1966088 | tf_op jit(solution)/shard_map/ppermute | solution.py:219
  27.2 14.0 %collective-permute-start.5 = (bf16[1280,256]{1,0:T(8,128)(2,1)S(1)}, bf16[1280,256]{1,0:T(8,128)(2,1)S(1)}, u32[]{:S(2)}, u32[]{:S(2)}) collective-permute-start(bf16[1280,256]{1,0:T(8,128)(2,1)S(1)} %collective-permute-done.4.refs_4_), channel_id=1, source_target_pairs={{2,6},{3,1},{6,10},{7,3},{10,14},{11,7},{14,12},{15,11},{12,8},{13... | collective-permute-start | bytes 1966088 | tf_op jit(solution)/shard_map/ppermute | solution.py:219
  34.3 14.0 %collective-permute-start.3 = (bf16[1280,256]{1,0:T(8,128)(2,1)}, bf16[1280,256]{1,0:T(8,128)(2,1)}, u32[]{:S(2)}, u32[]{:S(2)}) collective-permute-start(bf16[1280,256]{1,0:T(8,128)(2,1)} %collective-permute-done.2.refs_5_), channel_id=1, source_target_pairs={{2,6},{3,1},{6,10},{7,3},{10,14},{11,7},{14,12},{15,11},{12,8},{13... | collective-permute-start | bytes 1966088 | tf_op jit(solution)/shard_map/ppermute | solution.py:219
  41.3 14.7 %collective-permute-start.9 = (bf16[1280,256]{1,0:T(8,128)(2,1)S(1)}, bf16[1280,256]{1,0:T(8,128)(2,1)S(1)}, u32[]{:S(2)}, u32[]{:S(2)}) collective-permute-start(bf16[1280,256]{1,0:T(8,128)(2,1)S(1)} %collective-permute-done.5.refs_4_), channel_id=1, source_target_pairs={{2,6},{3,1},{6,10},{7,3},{10,14},{11,7},{14,12},{15,11},{12,8},{13... | collective-permute-start | bytes 1966088 | tf_op jit(solution)/shard_map/ppermute | solution.py:219
  48.4 13.9 %collective-permute-start.8 = (bf16[1280,256]{1,0:T(8,128)(2,1)}, bf16[1280,256]{1,0:T(8,128)(2,1)S(1)}, u32[]{:S(2)}, u32[]{:S(2)}) collective-permute-start(bf16[1280,256]{1,0:T(8,128)(2,1)} %collective-permute-done.3.refs_5_), channel_id=1, source_target_pairs={{2,6},{3,1},{6,10},{7,3},{10,14},{11,7},{14,12},{15,11},{12,8},{13... | collective-permute-start | bytes 1966088 | tf_op jit(solution)/shard_map/ppermute | solution.py:219
  55.9 13.9 %collective-permute-start.11 = (bf16[1280,256]{1,0:T(8,128)(2,1)S(1)}, bf16[1280,256]{1,0:T(8,128)(2,1)S(1)}, u32[]{:S(2)}, u32[]{:S(2)}) collective-permute-start(bf16[1280,256]{1,0:T(8,128)(2,1)S(1)} %collective-permute-done.9.refs_4_), channel_id=1, source_target_pairs={{2,6},{3,1},{6,10},{7,3},{10,14},{11,7},{14,12},{15,11},{12,8},{13... | collective-permute-start | bytes 1966088 | tf_op jit(solution)/shard_map/ppermute | solution.py:219
  62.3 4.7 %copy-start.7 = (bf16[1280,256]{1,0:T(8,128)(2,1)}, bf16[1280,256]{1,0:T(8,128)(2,1)S(1)}, u32[]{:S(2)}) copy-start(bf16[1280,256]{1,0:T(8,128)(2,1)S(1)} %collective-permute-done.8.refs_5_) | copy-start | bytes 1966084
  62.3 14.0 %collective-permute-start.10 = (bf16[1280,256]{1,0:T(8,128)(2,1)S(1)}, bf16[1280,256]{1,0:T(8,128)(2,1)S(1)}, u32[]{:S(2)}, u32[]{:S(2)}) collective-permute-start(bf16[1280,256]{1,0:T(8,128)(2,1)S(1)} %collective-permute-done.8.refs_5_), channel_id=1, source_target_pairs={{2,6},{3,1},{6,10},{7,3},{10,14},{11,7},{14,12},{15,11},{12,8},{13... | collective-permute-start | bytes 1966088 | tf_op jit(solution)/shard_map/ppermute | solution.py:219
  69.9 22.6 %copy-start.3 = (s32[2]{0:T(128)S(1)}, s32[2]{0:T(128)}, u32[]{:S(2)}) copy-start(s32[2]{0:T(128)} %seq_ref.1) | copy-start | bytes 28
  69.9 22.6 %copy-start.4 = (s32[2]{0:T(128)S(1)}, s32[2]{0:T(128)}, u32[]{:S(2)}) copy-start(s32[2]{0:T(128)} %len_ref.1) | copy-start | bytes 28
  69.9 13.5 %collective-permute-start.13 = (bf16[1280,256]{1,0:T(8,128)(2,1)S(1)}, bf16[1280,256]{1,0:T(8,128)(2,1)S(1)}, u32[]{:S(2)}, u32[]{:S(2)}) collective-permute-start(bf16[1280,256]{1,0:T(8,128)(2,1)S(1)} %collective-permute-done.11.refs_4_), channel_id=1, source_target_pairs={{2,6},{3,1},{6,10},{7,3},{10,14},{11,7},{14,12},{15,11},{12,8},{13... | collective-permute-start | bytes 1966088 | tf_op jit(solution)/shard_map/ppermute | solution.py:219
  76.4 2.0 %copy-start.8 = (bf16[1280,256]{1,0:T(8,128)(2,1)}, bf16[1280,256]{1,0:T(8,128)(2,1)S(1)}, u32[]{:S(2)}) copy-start(bf16[1280,256]{1,0:T(8,128)(2,1)S(1)} %collective-permute-done.10.refs_5_) | copy-start | bytes 1966084
  76.4 14.0 %collective-permute-start.12 = (bf16[1280,256]{1,0:T(8,128)(2,1)S(1)}, bf16[1280,256]{1,0:T(8,128)(2,1)S(1)}, u32[]{:S(2)}, u32[]{:S(2)}) collective-permute-start(bf16[1280,256]{1,0:T(8,128)(2,1)S(1)} %collective-permute-done.10.refs_5_), channel_id=1, source_target_pairs={{2,6},{3,1},{6,10},{7,3},{10,14},{11,7},{14,12},{15,11},{12,8},{13... | collective-permute-start | bytes 1966088 | tf_op jit(solution)/shard_map/ppermute | solution.py:219
  83.4 15.5 %collective-permute-start.16 = (bf16[1280,256]{1,0:T(8,128)(2,1)S(1)}, bf16[1280,256]{1,0:T(8,128)(2,1)S(1)}, u32[]{:S(2)}, u32[]{:S(2)}) collective-permute-start(bf16[1280,256]{1,0:T(8,128)(2,1)S(1)} %collective-permute-done.13.refs_4_), channel_id=1, source_target_pairs={{2,6},{3,1},{6,10},{7,3},{10,14},{11,7},{14,12},{15,11},{12,8},{13... | collective-permute-start | bytes 1966088 | tf_op jit(solution)/shard_map/ppermute | solution.py:219
  90.4 4.0 %copy-start.6 = (bf16[1280,256]{1,0:T(8,128)(2,1)}, bf16[1280,256]{1,0:T(8,128)(2,1)S(1)}, u32[]{:S(2)}) copy-start(bf16[1280,256]{1,0:T(8,128)(2,1)S(1)} %collective-permute-done.12.refs_5_) | copy-start | bytes 1966084
  90.4 10.7 %collective-permute-start.17 = (bf16[512,256]{1,0:T(8,128)(2,1)S(1)}, bf16[512,256]{1,0:T(8,128)(2,1)S(1)}, u32[]{:S(2)}, u32[]{:S(2)}) collective-permute-start(bf16[512,256]{1,0:T(8,128)(2,1)S(1)} %slice.15), channel_id=1, source_target_pairs={{2,6},{3,1},{6,10},{7,3},{10,14},{11,7},{14,12},{15,11},{12,8},{13... | collective-permute-start | bytes 786440 | tf_op jit(solution)/shard_map/ppermute | solution.py:219
  92.5 2.0 %collective-permute-start.14 = (s32[2,2]{1,0:T(2,128)S(1)}, s32[2,2]{1,0:T(2,128)S(1)}, u32[]{:S(2)}, u32[]{:S(2)}) collective-permute-start(s32[2,2]{1,0:T(2,128)S(1)} %pad_add_fusion), channel_id=1, source_target_pairs={{0,1},{1,0},{2,3},{3,2},{4,5},{5,4},{6,7},{7,6},{8,9},{9,8},{10,11... | collective-permute-start | bytes 56 | tf_op jit(solution)/shard_map/ppermute | solution.py:220
  94.5 10.0 %collective-permute-start.15 = (bf16[768,256]{1,0:T(8,128)(2,1)S(1)}, bf16[768,256]{1,0:T(8,128)(2,1)S(1)}, u32[]{:S(2)}, u32[]{:S(2)}) collective-permute-start(bf16[768,256]{1,0:T(8,128)(2,1)S(1)} %slice.14), channel_id=1, source_target_pairs={{2,6},{3,1},{6,10},{7,3},{10,14},{11,7},{14,12},{15,11},{12,8},{13... | collective-permute-start | bytes 1179656 | tf_op jit(solution)/shard_map/ppermute | solution.py:219
  102.9 1.7 %collective-permute-start.18 = (f32[320,256]{1,0:T(8,128)S(1)}, f32[320,256]{1,0:T(8,128)S(1)}, u32[]{:S(2)}, u32[]{:S(2)}) collective-permute-start(f32[320,256]{1,0:T(8,128)S(1)} %step.17.inn_ref), channel_id=1, source_target_pairs={{0,1},{1,0},{2,3},{3,2},{4,5},{5,4},{6,7},{7,6},{8,9},{9,8},{10,11... | collective-permute-start | bytes 983048 | tf_op jit(solution)/shard_map/ppermute | solution.py:220
  105.8 0.6 copy-start.2
  106.4 1.2 collective-permute-start.19
  107.6 0.6 copy-start.9
  109.6 9.8 %collective-permute-start.20 = (f32[8,128]{1,0:T(8,128)}, f32[8,128]{1,0:T(8,128)S(1)}, u32[]{:S(2)}, u32[]{:S(2)}) collective-permute-start(f32[8,128]{1,0:T(8,128)} %get-tuple-element.108), channel_id=1, source_target_pairs={{0,2},{1,3},{2,4},{3,5},{4,6},{5,7},{6,8},{7,9},{8,10},{9,11},{10,... | collective-permute-start | bytes 12296 | tf_op jit(solution)/shard_map/ppermute | solution.py:197
  111.4 9.3 %collective-permute-start.21 = (f32[8,128]{1,0:T(8,128)}, f32[8,128]{1,0:T(8,128)S(1)}, u32[]{:S(2)}, u32[]{:S(2)}) collective-permute-start(f32[8,128]{1,0:T(8,128)} %get-tuple-element.109), channel_id=1, source_target_pairs={{0,4},{1,5},{2,6},{3,7},{4,8},{5,9},{6,10},{7,11},{8,12},{9,13},{1... | collective-permute-start | bytes 12296 | tf_op jit(solution)/shard_map/ppermute | solution.py:197
  113.0 9.2 %collective-permute-start.22 = (f32[8,128]{1,0:T(8,128)}, f32[8,128]{1,0:T(8,128)S(1)}, u32[]{:S(2)}, u32[]{:S(2)}) collective-permute-start(f32[8,128]{1,0:T(8,128)} %get-tuple-element.110), channel_id=1, source_target_pairs={{0,6},{1,7},{2,8},{3,9},{4,10},{5,11},{6,12},{7,13},{8,14},{9,15},... | collective-permute-start | bytes 12296 | tf_op jit(solution)/shard_map/ppermute | solution.py:197
  115.5 6.7 %collective-permute-start.23 = (f32[8,128]{1,0:T(8,128)}, f32[8,128]{1,0:T(8,128)S(1)}, u32[]{:S(2)}, u32[]{:S(2)}) collective-permute-start(f32[8,128]{1,0:T(8,128)} %get-tuple-element.111), channel_id=1, source_target_pairs={{0,8},{1,9},{2,10},{3,11},{4,12},{5,13},{6,14},{7,15},{8,0},{9,1},... | collective-permute-start | bytes 12296 | tf_op jit(solution)/shard_map/ppermute | solution.py:197
  116.7 5.4 %collective-permute-start.24 = (f32[8,128]{1,0:T(8,128)}, f32[8,128]{1,0:T(8,128)S(1)}, u32[]{:S(2)}, u32[]{:S(2)}) collective-permute-start(f32[8,128]{1,0:T(8,128)} %get-tuple-element.112), channel_id=1, source_target_pairs={{0,10},{1,11},{2,12},{3,13},{4,14},{5,15},{6,0},{7,1},{8,2},{9,3},... | collective-permute-start | bytes 12296 | tf_op jit(solution)/shard_map/ppermute | solution.py:197
  119.4 5.2 %copy-start.10 = (f32[8,128]{1,0:T(8,128)}, f32[8,128]{1,0:T(8,128)S(1)}, u32[]{:S(2)}) copy-start(f32[8,128]{1,0:T(8,128)S(1)} %collective-permute-done.20.refs_1_) | copy-start | bytes 12292
  119.4 3.8 %collective-permute-start.25 = (f32[8,128]{1,0:T(8,128)}, f32[8,128]{1,0:T(8,128)S(1)}, u32[]{:S(2)}, u32[]{:S(2)}) collective-permute-start(f32[8,128]{1,0:T(8,128)} %get-tuple-element.113), channel_id=1, source_target_pairs={{0,12},{1,13},{2,14},{3,15},{4,0},{5,1},{6,2},{7,3},{8,4},{9,5},{1... | collective-permute-start | bytes 12296 | tf_op jit(solution)/shard_map/ppermute | solution.py:197
  120.8 3.8 %copy-start.11 = (f32[8,128]{1,0:T(8,128)}, f32[8,128]{1,0:T(8,128)S(1)}, u32[]{:S(2)}) copy-start(f32[8,128]{1,0:T(8,128)S(1)} %collective-permute-done.21.refs_2_) | copy-start | bytes 12292
  120.8 3.8 %collective-permute-start.26 = (f32[8,128]{1,0:T(8,128)}, f32[8,128]{1,0:T(8,128)S(1)}, u32[]{:S(2)}, u32[]{:S(2)}) collective-permute-start(f32[8,128]{1,0:T(8,128)} %get-tuple-element.114), channel_id=1, source_target_pairs={{0,14},{1,15},{2,0},{3,1},{4,2},{5,3},{6,4},{7,5},{8,6},{9,7},{10,... | collective-permute-start | bytes 12296 | tf_op jit(solution)/shard_map/ppermute | solution.py:197
  122.2 2.4 %copy-start.12 = (f32[8,128]{1,0:T(8,128)}, f32[8,128]{1,0:T(8,128)S(1)}, u32[]{:S(2)}) copy-start(f32[8,128]{1,0:T(8,128)S(1)} %collective-permute-done.22.refs_3_) | copy-start | bytes 12292
  122.2 2.4 %copy-start.13 = (f32[8,128]{1,0:T(8,128)}, f32[8,128]{1,0:T(8,128)S(1)}, u32[]{:S(2)}) copy-start(f32[8,128]{1,0:T(8,128)S(1)} %collective-permute-done.23.refs_4_) | copy-start | bytes 12292
  122.2 2.4 %copy-start.14 = (f32[8,128]{1,0:T(8,128)}, f32[8,128]{1,0:T(8,128)S(1)}, u32[]{:S(2)}) copy-start(f32[8,128]{1,0:T(8,128)S(1)} %collective-permute-done.24.refs_5_) | copy-start | bytes 12292
  123.2 1.4 %copy-start.15 = (f32[8,128]{1,0:T(8,128)}, f32[8,128]{1,0:T(8,128)S(1)}, u32[]{:S(2)}) copy-start(f32[8,128]{1,0:T(8,128)S(1)} %collective-permute-done.25.refs_6_) | copy-start | bytes 12292
  124.6 0.6 copy-start.16

commit v11 on v9

--- a/solution.py
+++ b/solution.py
@@ -185,32 +185,27 @@
     came = send(out_factors)
     late, early = came[lead:], came[:lead]
     if rows_in:
+        turned = lax.ppermute(in_factors, "dp", [(j, i) for i, j in pairs])
         early = jnp.concatenate([send(in_factors), early])
-    totals, summed = {}, 0
+        early, turned = lax.optimization_barrier((early, turned))
+    totals, summed, last = {}, 0, chips - 1
 
     def sum_to(k, totals, summed):
         for j in range(summed, k):
             totals = step(mine, tokens_of, held[j], pieces[j], totals, j)
         return totals, max(k, summed)
 
-    last = chips - 1
     for s in range(1, chips):
         held.append([late, early])
         pieces.append([(0, 0, rows - lead, "out", lead), (1, rows_in, lead, "out", 0)] + inside)
         if s == last:
             break
-        if s >= 3:
-            totals, summed = sum_to(min(2 * s - 5, s), totals, summed)
+        if s >= 4:
+            totals, summed = sum_to(min(2 * s - 6, s), totals, summed)
             late, totals = lax.optimization_barrier((late, totals))
             early, totals = lax.optimization_barrier((early, totals))
         late = send(late)
-        if s < last - 1:
-            early = send(early)
-        else:
-            inner, early = early[:rows_in], early[rows_in:]
-            if rows_in:
-                inner = send(inner)
-            early = send(early)
+        early = send(early if s < last - 1 else early[rows_in:])
 
     window = call(
         functools.partial(window_kernel, lead), mine,
@@ -220,15 +215,14 @@
     totals, window, slots_sib = lax.optimization_barrier((totals, window, slots_sib))
     seq_sib, len_sib = slots_sib
     totals, summed = sum_to(last, totals, summed)
-    totals = step(mine, tokens_of, [late], pieces[last][:1], totals, last)
     if rows_in:
-        totals, inner = lax.optimization_barrier((totals, inner))
-        totals = step(mine, tokens_of, [inner], [(0, 0, rows_in, "in", 0)], totals, last)
+        totals = step(mine, tokens_of, [turned], [(0, 0, rows_in, "in", 0)], totals, last)
         inn = totals["in"]
     else:
         inn = dot(acts, every)
         inn = jnp.concatenate([inn, jnp.zeros_like(inn)])
     got = across(inn)
+    totals = step(mine, tokens_of, [late], pieces[last][:1], totals, last)
 
     slots = lengths.shape[0]
     queries = columns // RANK

time: 119 us -> 119 us (level)
  starting transfers between devices: 29.9 us -> 28.6 us
    ppermute x15 -> x14, starting transfers between devices: 29.2 us -> 26.6 us  [shards(): send = lambda x: lax.ppermute(x, 'dp', pairs)]
    ppermute x15 -> x14, waiting for transfers between devices: 48.3 us -> 49.2 us  [shards(): send = lambda x: lax.ppermute(x, 'dp', pairs)]
  transfers between devices with their start and end apart: 19 -> 19, of which waited for: 12 -> 9; matrix products, arithmetic and copies ran while one was open for 1% -> 1% of each run, Pallas kernels for 21% -> 21%
where the time goes in v11:
time: 119 us; the launch traced here: 118 us
  waiting for transfers between devices  49.2 us (41%)
  starting transfers between devices  28.6 us (24%)
  Pallas kernels  26.4 us (22%)
  blocking collectives  12.5 us (11%)
    ppermute x14, waiting for transfers between devices, shards(): send = lambda x: lax.ppermute(x, 'dp', pairs)  49.2 us
    ppermute x14, starting transfers between devices, shards(): send = lambda x: lax.ppermute(x, 'dp', pairs)  26.6 us
    pallas_call x10, Pallas kernels, call(): pl.pallas_call(kernel, grid_spec=pltpu.PrefetchScalarGridSpec(num_scalar_...  25.3 us
    all_to_all x1, blocking collectives, shards(): lax.all_to_all(table.reshape(devices, slots, queries), 'dp', 0, 0, tiled=...  12.5 us
  transfers between devices with their start and end apart: 19, of which 9 were waited for; matrix products, arithmetic and copies ran while one was open for 1% of the time, Pallas kernels for 21%

profile of v11, /device:TPU:0, one launch (start us, length us, event | category | flops | bytes accessed | tf_op | source)
XLA Modules:
  0.0 118.4 jit_solution(1931374065349017228)
XLA Ops:
  0.0 0.0 copy-start
  0.0 0.5 collective-permute-start.10
  0.5 2.6 %collective-permute-start.1 = (bf16[2048,256]{1,0:T(8,128)(2,1)}, bf16[2048,256]{1,0:T(8,128)(2,1)S(1)}, u32[]{:S(2)}, u32[]{:S(2)}) collective-permute-start(bf16[2048,256]{1,0:T(8,128)(2,1)} %refs_4_.1), channel_id=1, source_target_pairs={{2,6},{3,1},{6,10},{7,3},{10,14},{11,7},{14,12},{15,11},{12,8},{13... | collective-permute-start | bytes 3145736 | tf_op jit(solution)/shard_map/ppermute | solution.py:169
  3.0 0.2 collective-permute-start.9
  3.3 1.4 %collective-permute-start = (bf16[512,256]{1,0:T(8,128)(2,1)}, bf16[512,256]{1,0:T(8,128)(2,1)S(1)}, u32[]{:S(2)}, u32[]{:S(2)}) collective-permute-start(bf16[512,256]{1,0:T(8,128)(2,1)} %refs_5_.1), channel_id=1, source_target_pairs={{2,6},{3,1},{6,10},{7,3},{10,14},{11,7},{14,12},{15,11},{12,8},{13... | collective-permute-start | bytes 786440 | tf_op jit(solution)/shard_map/ppermute | solution.py:169
  4.6 0.7 collective-permute-start.2
  5.3 13.6 %collective-permute-done.1 = bf16[2048,256]{1,0:T(8,128)(2,1)S(1)} collective-permute-done((bf16[2048,256]{1,0:T(8,128)(2,1)}, bf16[2048,256]{1,0:T(8,128)(2,1)S(1)}, u32[]{:S(2)}, u32[]{:S(2)}) %collective-permute-start.1) | collective-permute-done | bytes 1048608 | tf_op jit(solution)/shard_map/ppermute | solution.py:169
  18.9 2.0 %collective-permute-start.6 = (bf16[1280,256]{1,0:T(8,128)(2,1)S(1)}, bf16[1280,256]{1,0:T(8,128)(2,1)S(1)}, u32[]{:S(2)}, u32[]{:S(2)}) collective-permute-start(bf16[1280,256]{1,0:T(8,128)(2,1)S(1)} %slice.13.refs_4_), channel_id=1, source_target_pairs={{2,6},{3,1},{6,10},{7,3},{10,14},{11,7},{14,12},{15,11},{12,8},{13... | collective-permute-start | bytes 1966088 | tf_op jit(solution)/shard_map/ppermute | solution.py:169
  21.0 0.7 collective-permute-done
  21.7 0.0 copy-start.4
  21.8 0.0 collective-permute-done.2.refs_2_
  21.8 2.0 %collective-permute-start.3 = (bf16[1280,256]{1,0:T(8,128)(2,1)S(1)}, bf16[1280,256]{1,0:T(8,128)(2,1)S(1)}, u32[]{:S(2)}, u32[]{:S(2)}) collective-permute-start(bf16[1280,256]{1,0:T(8,128)(2,1)S(1)} %pad_maximum_fusion.refs_5_), channel_id=1, source_target_pairs={{2,6},{3,1},{6,10},{7,3},{10,14},{11,7},{14,12},{15,11},{12,8},{13... | collective-permute-start | bytes 1966088 | tf_op jit(solution)/shard_map/ppermute | solution.py:169
  23.8 5.8 %collective-permute-done.6.refs_4_ = bf16[1280,256]{1,0:T(8,128)(2,1)S(1)} collective-permute-done((bf16[1280,256]{1,0:T(8,128)(2,1)S(1)}, bf16[1280,256]{1,0:T(8,128)(2,1)S(1)}, u32[]{:S(2)}, u32[]{:S(2)}) %collective-permute-start.6) | collective-permute-done | bytes 655392 | tf_op jit(solution)/shard_map/ppermute | solution.py:169
  29.6 2.0 %collective-permute-start.7 = (bf16[1280,256]{1,0:T(8,128)(2,1)S(1)}, bf16[1280,256]{1,0:T(8,128)(2,1)}, u32[]{:S(2)}, u32[]{:S(2)}) collective-permute-start(bf16[1280,256]{1,0:T(8,128)(2,1)S(1)} %collective-permute-done.6.refs_4_), channel_id=1, source_target_pairs={{2,6},{3,1},{6,10},{7,3},{10,14},{11,7},{14,12},{15,11},{12,8},{13... | collective-permute-start | bytes 1966088 | tf_op jit(solution)/shard_map/ppermute | solution.py:169
  31.5 5.1 %collective-permute-done.3.refs_5_ = bf16[1280,256]{1,0:T(8,128)(2,1)S(1)} collective-permute-done((bf16[1280,256]{1,0:T(8,128)(2,1)S(1)}, bf16[1280,256]{1,0:T(8,128)(2,1)S(1)}, u32[]{:S(2)}, u32[]{:S(2)}) %collective-permute-start.3) | collective-permute-done | bytes 655392 | tf_op jit(solution)/shard_map/ppermute | solution.py:169
  36.6 2.0 %collective-permute-start.4 = (bf16[1280,256]{1,0:T(8,128)(2,1)S(1)}, bf16[1280,256]{1,0:T(8,128)(2,1)}, u32[]{:S(2)}, u32[]{:S(2)}) collective-permute-start(bf16[1280,256]{1,0:T(8,128)(2,1)S(1)} %collective-permute-done.3.refs_5_), channel_id=1, source_target_pairs={{2,6},{3,1},{6,10},{7,3},{10,14},{11,7},{14,12},{15,11},{12,8},{13... | collective-permute-start | bytes 1966088 | tf_op jit(solution)/shard_map/ppermute | solution.py:169
  38.6 0.0 copy-done.4
  38.6 5.2 %collective-permute-done.7.refs_4_ = bf16[1280,256]{1,0:T(8,128)(2,1)} collective-permute-done((bf16[1280,256]{1,0:T(8,128)(2,1)S(1)}, bf16[1280,256]{1,0:T(8,128)(2,1)}, u32[]{:S(2)}, u32[]{:S(2)}) %collective-permute-start.7) | collective-permute-done | bytes 655392 | tf_op jit(solution)/shard_map/ppermute | solution.py:169
  43.7 0.0 copy-done.6
  43.7 2.0 %collective-permute-start.8 = (bf16[1280,256]{1,0:T(8,128)(2,1)}, bf16[1280,256]{1,0:T(8,128)(2,1)S(1)}, u32[]{:S(2)}, u32[]{:S(2)}) collective-permute-start(bf16[1280,256]{1,0:T(8,128)(2,1)} %collective-permute-done.7.refs_4_), channel_id=1, source_target_pairs={{2,6},{3,1},{6,10},{7,3},{10,14},{11,7},{14,12},{15,11},{12,8},{13... | collective-permute-start | bytes 1966088 | tf_op jit(solution)/shard_map/ppermute | solution.py:169
  45.7 5.1 %collective-permute-done.4.refs_5_ = bf16[1280,256]{1,0:T(8,128)(2,1)} collective-permute-done((bf16[1280,256]{1,0:T(8,128)(2,1)S(1)}, bf16[1280,256]{1,0:T(8,128)(2,1)}, u32[]{:S(2)}, u32[]{:S(2)}) %collective-permute-start.4) | collective-permute-done | bytes 655392 | tf_op jit(solution)/shard_map/ppermute | solution.py:169
  50.8 2.0 %collective-permute-start.5 = (bf16[1280,256]{1,0:T(8,128)(2,1)}, bf16[1280,256]{1,0:T(8,128)(2,1)}, u32[]{:S(2)}, u32[]{:S(2)}) collective-permute-start(bf16[1280,256]{1,0:T(8,128)(2,1)} %collective-permute-done.4.refs_5_), channel_id=1, source_target_pairs={{2,6},{3,1},{6,10},{7,3},{10,14},{11,7},{14,12},{15,11},{12,8},{13... | collective-permute-start | bytes 1966088 | tf_op jit(solution)/shard_map/ppermute | solution.py:169
  52.7 0.7 dynamic-slice_bitcast_fusion.order_ref
  53.4 0.0 collective-permute-done.9.refs_1_
  53.4 0.0 collective-permute-done.10.refs_3_.sib_ref.refs_1_
  53.4 0.0 copy-done
  53.4 0.0 copy-done.1
  53.4 2.6 %step.9 = (f32[320,256]{1,0:T(8,128)S(1)}, f32[320,256]{1,0:T(8,128)S(1)}) custom-call(s32[8]{0:T(128)S(1)} %dynamic-slice_bitcast_fusion.order_ref, bf16[160,8192]{1,0:T(8,128)(2,1)} %refs_0_.17, bf16[160,8192]{1,0:T(8,128)(2,1)} %collective-permute-done.9.refs_1_, bf16[160,32768]{1,0:T(8,128)(2,1)} %refs_0_.16, ...), custom_call_target="tpu_custom_call" | custom-call | flops 419430400 | bytes 3604480 | tf_op jit(solution)/shard_map/step/pallas_call | solution.py:59
  56.0 2.8 %step.10 = (f32[320,256]{1,0:T(8,128)S(1)}, f32[320,256]{1,0:T(8,128)S(1)}) custom-call(s32[8]{0:T(128)S(1)} %dynamic-slice_bitcast_fusion.order_ref, bf16[160,8192]{1,0:T(8,128)(2,1)} %refs_0_.17, bf16[160,8192]{1,0:T(8,128)(2,1)} %collective-permute-done.9.refs_1_, bf16[160,32768]{1,0:T(8,128)(2,1)} %refs_0_.16, ...), custom_call_target="tpu_custom_call" | custom-call | flops 419430400 | bytes 4259840 | tf_op jit(solution)/shard_map/step/pallas_call | solution.py:59
  58.8 0.0 collective-permute-done.8.refs_4_
  58.8 1.6 %collective-permute-start.12 = (bf16[1280,256]{1,0:T(8,128)(2,1)S(1)}, bf16[1280,256]{1,0:T(8,128)(2,1)S(1)}, u32[]{:S(2)}, u32[]{:S(2)}) collective-permute-start(bf16[1280,256]{1,0:T(8,128)(2,1)S(1)} %collective-permute-done.8.refs_4_), channel_id=1, source_target_pairs={{2,6},{3,1},{6,10},{7,3},{10,14},{11,7},{14,12},{15,11},{12,8},{13... | collective-permute-start | bytes 1966088 | tf_op jit(solution)/shard_map/ppermute | solution.py:169
  60.5 4.3 %collective-permute-done.5.refs_5_ = bf16[1280,256]{1,0:T(8,128)(2,1)} collective-permute-done((bf16[1280,256]{1,0:T(8,128)(2,1)}, bf16[1280,256]{1,0:T(8,128)(2,1)}, u32[]{:S(2)}, u32[]{:S(2)}) %collective-permute-start.5) | collective-permute-done | bytes 655392 | tf_op jit(solution)/shard_map/ppermute | solution.py:169
  64.8 2.0 %collective-permute-start.11 = (bf16[1280,256]{1,0:T(8,128)(2,1)}, bf16[1280,256]{1,0:T(8,128)(2,1)S(1)}, u32[]{:S(2)}, u32[]{:S(2)}) collective-permute-start(bf16[1280,256]{1,0:T(8,128)(2,1)} %collective-permute-done.5.refs_5_), channel_id=1, source_target_pairs={{2,6},{3,1},{6,10},{7,3},{10,14},{11,7},{14,12},{15,11},{12,8},{13... | collective-permute-start | bytes 1966088 | tf_op jit(solution)/shard_map/ppermute | solution.py:169
  66.8 2.8 %step.11 = (f32[320,256]{1,0:T(8,128)S(1)}, f32[320,256]{1,0:T(8,128)S(1)}) custom-call(s32[8]{0:T(128)S(1)} %dynamic-slice_bitcast_fusion.order_ref, bf16[160,8192]{1,0:T(8,128)(2,1)} %refs_0_.17, bf16[160,8192]{1,0:T(8,128)(2,1)} %collective-permute-done.9.refs_1_, bf16[160,32768]{1,0:T(8,128)(2,1)} %refs_0_.16, ...), custom_call_target="tpu_custom_call" | custom-call | flops 419430400 | bytes 4259840 | tf_op jit(solution)/shard_map/step/pallas_call | solution.py:59
  69.5 3.0 %step.12 = (f32[320,256]{1,0:T(8,128)S(1)}, f32[320,256]{1,0:T(8,128)S(1)}) custom-call(s32[8]{0:T(128)S(1)} %dynamic-slice_bitcast_fusion.order_ref, bf16[160,8192]{1,0:T(8,128)(2,1)} %refs_0_.17, bf16[160,8192]{1,0:T(8,128)(2,1)} %collective-permute-done.9.refs_1_, bf16[160,32768]{1,0:T(8,128)(2,1)} %refs_0_.16, ...), custom_call_target="tpu_custom_call" | custom-call | flops 419430400 | bytes 4259840 | tf_op jit(solution)/shard_map/step/pallas_call | solution.py:59
  72.5 0.0 collective-permute-done.12.refs_4_
  72.5 1.6 %collective-permute-start.14 = (bf16[1280,256]{1,0:T(8,128)(2,1)S(1)}, bf16[1280,256]{1,0:T(8,128)(2,1)S(1)}, u32[]{:S(2)}, u32[]{:S(2)}) collective-permute-start(bf16[1280,256]{1,0:T(8,128)(2,1)S(1)} %collective-permute-done.12.refs_4_), channel_id=1, source_target_pairs={{2,6},{3,1},{6,10},{7,3},{10,14},{11,7},{14,12},{15,11},{12,8},{13... | collective-permute-start | bytes 1966088 | tf_op jit(solution)/shard_map/ppermute | solution.py:169
  74.2 4.6 %collective-permute-done.11.refs_5_ = bf16[1280,256]{1,0:T(8,128)(2,1)S(1)} collective-permute-done((bf16[1280,256]{1,0:T(8,128)(2,1)}, bf16[1280,256]{1,0:T(8,128)(2,1)S(1)}, u32[]{:S(2)}, u32[]{:S(2)}) %collective-permute-start.11) | collective-permute-done | bytes 655392 | tf_op jit(solution)/shard_map/ppermute | solution.py:169
  78.7 2.0 %collective-permute-start.13 = (bf16[1280,256]{1,0:T(8,128)(2,1)S(1)}, bf16[1280,256]{1,0:T(8,128)(2,1)S(1)}, u32[]{:S(2)}, u32[]{:S(2)}) collective-permute-start(bf16[1280,256]{1,0:T(8,128)(2,1)S(1)} %collective-permute-done.11.refs_5_), channel_id=1, source_target_pairs={{2,6},{3,1},{6,10},{7,3},{10,14},{11,7},{14,12},{15,11},{12,8},{13... | collective-permute-start | bytes 1966088 | tf_op jit(solution)/shard_map/ppermute | solution.py:169
  80.7 2.8 %step.13 = (f32[320,256]{1,0:T(8,128)S(1)}, f32[320,256]{1,0:T(8,128)S(1)}) custom-call(s32[8]{0:T(128)S(1)} %dynamic-slice_bitcast_fusion.order_ref, bf16[160,8192]{1,0:T(8,128)(2,1)} %refs_0_.17, bf16[160,8192]{1,0:T(8,128)(2,1)} %collective-permute-done.9.refs_1_, bf16[160,32768]{1,0:T(8,128)(2,1)} %refs_0_.16, ...), custom_call_target="tpu_custom_call" | custom-call | flops 419430400 | bytes 4259840 | tf_op jit(solution)/shard_map/step/pallas_call | solution.py:59
  83.5 0.0 copy-done.7
  83.5 0.0 copy-start.2
  83.5 0.0 copy-start.3
  83.5 2.8 %step.14 = (f32[320,256]{1,0:T(8,128)S(1)}, f32[320,256]{1,0:T(8,128)S(1)}) custom-call(s32[8]{0:T(128)S(1)} %dynamic-slice_bitcast_fusion.order_ref, bf16[160,8192]{1,0:T(8,128)(2,1)} %refs_0_.17, bf16[160,8192]{1,0:T(8,128)(2,1)} %collective-permute-done.9.refs_1_, bf16[160,32768]{1,0:T(8,128)(2,1)} %refs_0_.16, ...), custom_call_target="tpu_custom_call" | custom-call | flops 419430400 | bytes 4259840 | tf_op jit(solution)/shard_map/step/pallas_call | solution.py:59
  86.3 0.0 collective-permute-done.14.refs_4_
  86.3 1.6 %collective-permute-start.17 = (bf16[1280,256]{1,0:T(8,128)(2,1)S(1)}, bf16[1280,256]{1,0:T(8,128)(2,1)S(1)}, u32[]{:S(2)}, u32[]{:S(2)}) collective-permute-start(bf16[1280,256]{1,0:T(8,128)(2,1)S(1)} %collective-permute-done.14.refs_4_), channel_id=1, source_target_pairs={{2,6},{3,1},{6,10},{7,3},{10,14},{11,7},{14,12},{15,11},{12,8},{13... | collective-permute-start | bytes 1966088 | tf_op jit(solution)/shard_map/ppermute | solution.py:169
  87.9 4.8 %collective-permute-done.13.refs_5_ = bf16[1280,256]{1,0:T(8,128)(2,1)S(1)} collective-permute-done((bf16[1280,256]{1,0:T(8,128)(2,1)S(1)}, bf16[1280,256]{1,0:T(8,128)(2,1)S(1)}, u32[]{:S(2)}, u32[]{:S(2)}) %collective-permute-start.13) | collective-permute-done | bytes 655392 | tf_op jit(solution)/shard_map/ppermute | solution.py:169
  92.8 2.0 %collective-permute-start.16 = (bf16[768,256]{1,0:T(8,128)(2,1)S(1)}, bf16[768,256]{1,0:T(8,128)(2,1)S(1)}, u32[]{:S(2)}, u32[]{:S(2)}) collective-permute-start(bf16[768,256]{1,0:T(8,128)(2,1)S(1)} %slice.11), channel_id=1, source_target_pairs={{2,6},{3,1},{6,10},{7,3},{10,14},{11,7},{14,12},{15,11},{12,8},{13... | collective-permute-start | bytes 1179656 | tf_op jit(solution)/shard_map/ppermute | solution.py:169
  94.8 0.0 copy-done.2
  94.8 0.0 copy-done.3
  94.8 0.1 collective-permute-start.15
  94.9 1.9 %window.1.window_ref = bf16[320,768]{1,0:T(8,128)(2,1)S(1)} custom-call(s32[8]{0:T(128)S(1)} %dynamic-slice_bitcast_fusion.order_ref, bf16[160,32768]{1,0:T(8,128)(2,1)} %refs_0_.16, bf16[160,32768]{1,0:T(8,128)(2,1)} %collective-permute-done.10.refs_3_.sib_ref.refs_1_), custom_call_target="tpu_custom_call" | custom-call | bytes 1802240 | tf_op jit(solution)/shard_map/window/pallas_call | solution.py:59
  96.8 0.0 copy-done.5
  96.8 0.0 collective-permute-done.15
  96.8 2.8 %step.15 = (f32[320,256]{1,0:T(8,128)S(1)}, f32[320,256]{1,0:T(8,128)S(1)}) custom-call(s32[8]{0:T(128)S(1)} %dynamic-slice_bitcast_fusion.order_ref, bf16[160,8192]{1,0:T(8,128)(2,1)} %refs_0_.17, bf16[160,8192]{1,0:T(8,128)(2,1)} %collective-permute-done.9.refs_1_, bf16[160,32768]{1,0:T(8,128)(2,1)} %refs_0_.16, ...), custom_call_target="tpu_custom_call" | custom-call | flops 419430400 | bytes 4259840 | tf_op jit(solution)/shard_map/step/pallas_call | solution.py:59
  99.6 1.8 %step.17.inn_ref = f32[320,256]{1,0:T(8,128)S(1)} custom-call(s32[8]{0:T(128)S(1)} %dynamic-slice_bitcast_fusion.order_ref, bf16[160,8192]{1,0:T(8,128)(2,1)} %refs_0_.17, bf16[160,8192]{1,0:T(8,128)(2,1)} %collective-permute-done.9.refs_1_, bf16[512,256]{1,0:T(8,128)(2,1)S(1)} %collective-permute-done.2.refs_2_, f32[320,256]{1,0:T(8,128)S(1)} %get-tuple-element.80.refs_3_), custom_call_target="tpu_custom_call" | custom-call | flops 83886080 | bytes 1245184 | tf_op jit(solution)/shard_map/step/pallas_call | solution.py:59
  101.4 0.6 collective-permute-start.18
  101.9 0.0 collective-permute-done.17.refs_2_
  102.0 2.2 %step.16.out_ref = f32[320,256]{1,0:T(8,128)S(1)} custom-call(s32[8]{0:T(128)S(1)} %dynamic-slice_bitcast_fusion.order_ref, bf16[160,32768]{1,0:T(8,128)(2,1)} %refs_0_.16, bf16[160,32768]{1,0:T(8,128)(2,1)} %collective-permute-done.10.refs_3_.sib_ref.refs_1_, bf16[1280,256]{1,0:T(8,128)(2,1)S(1)} %collective-permute-done.17.refs_2_, ...), custom_call_target="tpu_custom_call" | custom-call | flops 209715200 | bytes 2621440 | tf_op jit(solution)/shard_map/step/pallas_call | solution.py:59
  104.2 0.0 collective-permute-done.18.got_ref
  104.2 0.0 collective-permute-done.16.b_ref
  104.2 1.1 score.1
  105.3 12.5 %all_to_all.5 = f32[16,2,8]{2,1,0:T(2,128)S(1)} all-to-all(f32[16,2,8]{2,1,0:T(2,128)S(1)} %bitcast.9), channel_id=1, replica_groups=mesh['groups'=2,'dp'=16] {'dp'}, dimensions={0} | all-to-all | bytes 2048 | tf_op jit(solution)/shard_map/all_to_all | solution.py:233
  117.8 0.6 reduce_sum.9
  (10 shorter events, 0.2 us)
Async XLA Ops:
  0.0 53.4 %copy-start = (bf16[2048,256]{1,0:T(8,128)(2,1)S(1)}, bf16[2048,256]{1,0:T(8,128)(2,1)}, u32[]{:S(2)}) copy-start(bf16[2048,256]{1,0:T(8,128)(2,1)} %refs_4_.1) | copy-start | bytes 3145732
  0.0 53.4 %copy-start.1 = (bf16[512,256]{1,0:T(8,128)(2,1)S(1)}, bf16[512,256]{1,0:T(8,128)(2,1)}, u32[]{:S(2)}) copy-start(bf16[512,256]{1,0:T(8,128)(2,1)} %refs_5_.1) | copy-start | bytes 786436
  0.0 53.4 %collective-permute-start.10 = (bf16[160,32768]{1,0:T(8,128)(2,1)}, bf16[160,32768]{1,0:T(8,128)(2,1)}, u32[]{:S(2)}, u32[]{:S(2)}) collective-permute-start(bf16[160,32768]{1,0:T(8,128)(2,1)} %refs_0_.16), channel_id=1, source_target_pairs={{0,1},{1,0},{2,3},{3,2},{4,5},{5,4},{6,7},{7,6},{8,9},{9,8},{10,11... | collective-permute-start | bytes 31457288 | tf_op jit(solution)/shard_map/ppermute | solution.py:170
  0.5 18.4 %collective-permute-start.1 = (bf16[2048,256]{1,0:T(8,128)(2,1)}, bf16[2048,256]{1,0:T(8,128)(2,1)S(1)}, u32[]{:S(2)}, u32[]{:S(2)}) collective-permute-start(bf16[2048,256]{1,0:T(8,128)(2,1)} %refs_4_.1), channel_id=1, source_target_pairs={{2,6},{3,1},{6,10},{7,3},{10,14},{11,7},{14,12},{15,11},{12,8},{13... | collective-permute-start | bytes 3145736 | tf_op jit(solution)/shard_map/ppermute | solution.py:169
  3.0 50.4 %collective-permute-start.9 = (bf16[160,8192]{1,0:T(8,128)(2,1)}, bf16[160,8192]{1,0:T(8,128)(2,1)}, u32[]{:S(2)}, u32[]{:S(2)}) collective-permute-start(bf16[160,8192]{1,0:T(8,128)(2,1)} %refs_0_.17), channel_id=1, source_target_pairs={{0,1},{1,0},{2,3},{3,2},{4,5},{5,4},{6,7},{7,6},{8,9},{9,8},{10,11... | collective-permute-start | bytes 7864328 | tf_op jit(solution)/shard_map/ppermute | solution.py:170
  3.3 18.4 %collective-permute-start = (bf16[512,256]{1,0:T(8,128)(2,1)}, bf16[512,256]{1,0:T(8,128)(2,1)S(1)}, u32[]{:S(2)}, u32[]{:S(2)}) collective-permute-start(bf16[512,256]{1,0:T(8,128)(2,1)} %refs_5_.1), channel_id=1, source_target_pairs={{2,6},{3,1},{6,10},{7,3},{10,14},{11,7},{14,12},{15,11},{12,8},{13... | collective-permute-start | bytes 786440 | tf_op jit(solution)/shard_map/ppermute | solution.py:169
  4.6 17.1 %collective-permute-start.2 = (bf16[512,256]{1,0:T(8,128)(2,1)}, bf16[512,256]{1,0:T(8,128)(2,1)S(1)}, u32[]{:S(2)}, u32[]{:S(2)}) collective-permute-start(bf16[512,256]{1,0:T(8,128)(2,1)} %refs_5_.1), channel_id=1, source_target_pairs={{6,2},{1,3},{10,6},{3,7},{14,10},{7,11},{12,14},{11,15},{8,12},{15... | collective-permute-start | bytes 786440 | tf_op jit(solution)/shard_map/ppermute | solution.py:188
  18.9 10.6 %collective-permute-start.6 = (bf16[1280,256]{1,0:T(8,128)(2,1)S(1)}, bf16[1280,256]{1,0:T(8,128)(2,1)S(1)}, u32[]{:S(2)}, u32[]{:S(2)}) collective-permute-start(bf16[1280,256]{1,0:T(8,128)(2,1)S(1)} %slice.13.refs_4_), channel_id=1, source_target_pairs={{2,6},{3,1},{6,10},{7,3},{10,14},{11,7},{14,12},{15,11},{12,8},{13... | collective-permute-start | bytes 1966088 | tf_op jit(solution)/shard_map/ppermute | solution.py:169
  21.7 16.8 %copy-start.4 = (bf16[1280,256]{1,0:T(8,128)(2,1)}, bf16[1280,256]{1,0:T(8,128)(2,1)S(1)}, u32[]{:S(2)}) copy-start(bf16[1280,256]{1,0:T(8,128)(2,1)S(1)} %pad_maximum_fusion.refs_5_) | copy-start | bytes 1966084
  21.8 14.8 %collective-permute-start.3 = (bf16[1280,256]{1,0:T(8,128)(2,1)S(1)}, bf16[1280,256]{1,0:T(8,128)(2,1)S(1)}, u32[]{:S(2)}, u32[]{:S(2)}) collective-permute-start(bf16[1280,256]{1,0:T(8,128)(2,1)S(1)} %pad_maximum_fusion.refs_5_), channel_id=1, source_target_pairs={{2,6},{3,1},{6,10},{7,3},{10,14},{11,7},{14,12},{15,11},{12,8},{13... | collective-permute-start | bytes 1966088 | tf_op jit(solution)/shard_map/ppermute | solution.py:169
  29.6 14.1 %collective-permute-start.7 = (bf16[1280,256]{1,0:T(8,128)(2,1)S(1)}, bf16[1280,256]{1,0:T(8,128)(2,1)}, u32[]{:S(2)}, u32[]{:S(2)}) collective-permute-start(bf16[1280,256]{1,0:T(8,128)(2,1)S(1)} %collective-permute-done.6.refs_4_), channel_id=1, source_target_pairs={{2,6},{3,1},{6,10},{7,3},{10,14},{11,7},{14,12},{15,11},{12,8},{13... | collective-permute-start | bytes 1966088 | tf_op jit(solution)/shard_map/ppermute | solution.py:169
  36.6 7.1 %copy-start.6 = (bf16[1280,256]{1,0:T(8,128)(2,1)}, bf16[1280,256]{1,0:T(8,128)(2,1)S(1)}, u32[]{:S(2)}) copy-start(bf16[1280,256]{1,0:T(8,128)(2,1)S(1)} %collective-permute-done.3.refs_5_) | copy-start | bytes 1966084
  36.6 14.1 %collective-permute-start.4 = (bf16[1280,256]{1,0:T(8,128)(2,1)S(1)}, bf16[1280,256]{1,0:T(8,128)(2,1)}, u32[]{:S(2)}, u32[]{:S(2)}) collective-permute-start(bf16[1280,256]{1,0:T(8,128)(2,1)S(1)} %collective-permute-done.3.refs_5_), channel_id=1, source_target_pairs={{2,6},{3,1},{6,10},{7,3},{10,14},{11,7},{14,12},{15,11},{12,8},{13... | collective-permute-start | bytes 1966088 | tf_op jit(solution)/shard_map/ppermute | solution.py:169
  43.7 15.1 %collective-permute-start.8 = (bf16[1280,256]{1,0:T(8,128)(2,1)}, bf16[1280,256]{1,0:T(8,128)(2,1)S(1)}, u32[]{:S(2)}, u32[]{:S(2)}) collective-permute-start(bf16[1280,256]{1,0:T(8,128)(2,1)} %collective-permute-done.7.refs_4_), channel_id=1, source_target_pairs={{2,6},{3,1},{6,10},{7,3},{10,14},{11,7},{14,12},{15,11},{12,8},{13... | collective-permute-start | bytes 1966088 | tf_op jit(solution)/shard_map/ppermute | solution.py:169
  50.8 14.0 %collective-permute-start.5 = (bf16[1280,256]{1,0:T(8,128)(2,1)}, bf16[1280,256]{1,0:T(8,128)(2,1)}, u32[]{:S(2)}, u32[]{:S(2)}) collective-permute-start(bf16[1280,256]{1,0:T(8,128)(2,1)} %collective-permute-done.4.refs_5_), channel_id=1, source_target_pairs={{2,6},{3,1},{6,10},{7,3},{10,14},{11,7},{14,12},{15,11},{12,8},{13... | collective-permute-start | bytes 1966088 | tf_op jit(solution)/shard_map/ppermute | solution.py:169
  58.8 13.7 %collective-permute-start.12 = (bf16[1280,256]{1,0:T(8,128)(2,1)S(1)}, bf16[1280,256]{1,0:T(8,128)(2,1)S(1)}, u32[]{:S(2)}, u32[]{:S(2)}) collective-permute-start(bf16[1280,256]{1,0:T(8,128)(2,1)S(1)} %collective-permute-done.8.refs_4_), channel_id=1, source_target_pairs={{2,6},{3,1},{6,10},{7,3},{10,14},{11,7},{14,12},{15,11},{12,8},{13... | collective-permute-start | bytes 1966088 | tf_op jit(solution)/shard_map/ppermute | solution.py:169
  64.8 13.9 %collective-permute-start.11 = (bf16[1280,256]{1,0:T(8,128)(2,1)}, bf16[1280,256]{1,0:T(8,128)(2,1)S(1)}, u32[]{:S(2)}, u32[]{:S(2)}) collective-permute-start(bf16[1280,256]{1,0:T(8,128)(2,1)} %collective-permute-done.5.refs_5_), channel_id=1, source_target_pairs={{2,6},{3,1},{6,10},{7,3},{10,14},{11,7},{14,12},{15,11},{12,8},{13... | collective-permute-start | bytes 1966088 | tf_op jit(solution)/shard_map/ppermute | solution.py:169
  72.5 13.8 %collective-permute-start.14 = (bf16[1280,256]{1,0:T(8,128)(2,1)S(1)}, bf16[1280,256]{1,0:T(8,128)(2,1)S(1)}, u32[]{:S(2)}, u32[]{:S(2)}) collective-permute-start(bf16[1280,256]{1,0:T(8,128)(2,1)S(1)} %collective-permute-done.12.refs_4_), channel_id=1, source_target_pairs={{2,6},{3,1},{6,10},{7,3},{10,14},{11,7},{14,12},{15,11},{12,8},{13... | collective-permute-start | bytes 1966088 | tf_op jit(solution)/shard_map/ppermute | solution.py:169
  78.7 4.7 %copy-start.7 = (bf16[1280,256]{1,0:T(8,128)(2,1)}, bf16[1280,256]{1,0:T(8,128)(2,1)S(1)}, u32[]{:S(2)}) copy-start(bf16[1280,256]{1,0:T(8,128)(2,1)S(1)} %collective-permute-done.11.refs_5_) | copy-start | bytes 1966084
  78.7 14.0 %collective-permute-start.13 = (bf16[1280,256]{1,0:T(8,128)(2,1)S(1)}, bf16[1280,256]{1,0:T(8,128)(2,1)S(1)}, u32[]{:S(2)}, u32[]{:S(2)}) collective-permute-start(bf16[1280,256]{1,0:T(8,128)(2,1)S(1)} %collective-permute-done.11.refs_5_), channel_id=1, source_target_pairs={{2,6},{3,1},{6,10},{7,3},{10,14},{11,7},{14,12},{15,11},{12,8},{13... | collective-permute-start | bytes 1966088 | tf_op jit(solution)/shard_map/ppermute | solution.py:169
  83.5 11.3 %copy-start.2 = (s32[2]{0:T(128)S(1)}, s32[2]{0:T(128)}, u32[]{:S(2)}) copy-start(s32[2]{0:T(128)} %seq_ref.1) | copy-start | bytes 28
  83.5 11.3 %copy-start.3 = (s32[2]{0:T(128)S(1)}, s32[2]{0:T(128)}, u32[]{:S(2)}) copy-start(s32[2]{0:T(128)} %len_ref.1) | copy-start | bytes 28
  86.3 15.6 %collective-permute-start.17 = (bf16[1280,256]{1,0:T(8,128)(2,1)S(1)}, bf16[1280,256]{1,0:T(8,128)(2,1)S(1)}, u32[]{:S(2)}, u32[]{:S(2)}) collective-permute-start(bf16[1280,256]{1,0:T(8,128)(2,1)S(1)} %collective-permute-done.14.refs_4_), channel_id=1, source_target_pairs={{2,6},{3,1},{6,10},{7,3},{10,14},{11,7},{14,12},{15,11},{12,8},{13... | collective-permute-start | bytes 1966088 | tf_op jit(solution)/shard_map/ppermute | solution.py:169
  92.8 4.0 %copy-start.5 = (bf16[1280,256]{1,0:T(8,128)(2,1)}, bf16[1280,256]{1,0:T(8,128)(2,1)S(1)}, u32[]{:S(2)}) copy-start(bf16[1280,256]{1,0:T(8,128)(2,1)S(1)} %collective-permute-done.13.refs_5_) | copy-start | bytes 1966084
  92.8 11.4 %collective-permute-start.16 = (bf16[768,256]{1,0:T(8,128)(2,1)S(1)}, bf16[768,256]{1,0:T(8,128)(2,1)S(1)}, u32[]{:S(2)}, u32[]{:S(2)}) collective-permute-start(bf16[768,256]{1,0:T(8,128)(2,1)S(1)} %slice.11), channel_id=1, source_target_pairs={{2,6},{3,1},{6,10},{7,3},{10,14},{11,7},{14,12},{15,11},{12,8},{13... | collective-permute-start | bytes 1179656 | tf_op jit(solution)/shard_map/ppermute | solution.py:169
  94.8 2.0 %collective-permute-start.15 = (s32[2,2]{1,0:T(2,128)S(1)}, s32[2,2]{1,0:T(2,128)S(1)}, u32[]{:S(2)}, u32[]{:S(2)}) collective-permute-start(s32[2,2]{1,0:T(2,128)S(1)} %pad_add_fusion), channel_id=1, source_target_pairs={{0,1},{1,0},{2,3},{3,2},{4,5},{5,4},{6,7},{7,6},{8,9},{9,8},{10,11... | collective-permute-start | bytes 56 | tf_op jit(solution)/shard_map/ppermute | solution.py:170
  101.4 2.8 %collective-permute-start.18 = (f32[320,256]{1,0:T(8,128)S(1)}, f32[320,256]{1,0:T(8,128)S(1)}, u32[]{:S(2)}, u32[]{:S(2)}) collective-permute-start(f32[320,256]{1,0:T(8,128)S(1)} %step.17.inn_ref), channel_id=1, source_target_pairs={{0,1},{1,0},{2,3},{3,2},{4,5},{5,4},{6,7},{7,6},{8,9},{9,8},{10,11... | collective-permute-start | bytes 983048 | tf_op jit(solution)/shard_map/ppermute | solution.py:170

commit v12 on v11

--- a/solution.py
+++ b/solution.py
@@ -185,7 +185,9 @@
     came = send(out_factors)
     late, early = came[lead:], came[:lead]
     if rows_in:
-        turned = lax.ppermute(in_factors, "dp", [(j, i) for i, j in pairs])
+        came, turned = lax.optimization_barrier((came, in_factors))
+        turned = lax.ppermute(turned, "dp", [(j, i) for i, j in pairs])
+        late, early = came[lead:], came[:lead]
         early = jnp.concatenate([send(in_factors), early])
         early, turned = lax.optimization_barrier((early, turned))
     totals, summed, last = {}, 0, chips - 1

time: 119 us -> 118 us (level)
    ppermute x1, waiting for transfers between devices: 0.01 us -> 6.23 us  [shards(): turned = lax.ppermute(turned, 'dp', [(j, i) for i, j in pairs])]
    ppermute x14, waiting for transfers between devices: 49.2 us -> 43.3 us  [shards(): send = lambda x: lax.ppermute(x, 'dp', pairs)]
    ppermute x14, starting transfers between devices: 26.6 us -> 24.4 us  [shards(): send = lambda x: lax.ppermute(x, 'dp', pairs)]
    ppermute x1, starting transfers between devices: 0.67 us -> 2.02 us  [shards(): turned = lax.ppermute(turned, 'dp', [(j, i) for i, j in pairs])]
  transfers between devices with their start and end apart: 19 -> 19, of which waited for: 9 -> 10; matrix products, arithmetic and copies ran while one was open for 1% -> 1% of each run, Pallas kernels for 21% -> 21%
where the time goes in v12:
time: 118 us
  waiting for transfers between devices  49.5 us (42%)
  starting transfers between devices  27.7 us (23%)
  Pallas kernels  26.4 us (22%)
  blocking collectives  12.5 us (11%)
    ppermute x14, waiting for transfers between devices, shards(): send = lambda x: lax.ppermute(x, 'dp', pairs)  43.3 us
    pallas_call x10, Pallas kernels, call(): pl.pallas_call(kernel, grid_spec=pltpu.PrefetchScalarGridSpec(num_scalar_...  25.3 us
    ppermute x14, starting transfers between devices, shards(): send = lambda x: lax.ppermute(x, 'dp', pairs)  24.4 us
    all_to_all x1, blocking collectives, shards(): lax.all_to_all(table.reshape(devices, slots, queries), 'dp', 0, 0, tiled=...  12.5 us
    ppermute x1, waiting for transfers between devices, shards(): turned = lax.ppermute(turned, 'dp', [(j, i) for i, j in pairs])  6.23 us
  transfers between devices with their start and end apart: 19, of which 10 were waited for; matrix products, arithmetic and copies ran while one was open for 1% of the time, Pallas kernels for 21%

profile of v12, /device:TPU:0, one launch (start us, length us, event | category | flops | bytes accessed | tf_op | source)
XLA Modules:
  0.0 117.9 jit_solution(5239479098163794415)
XLA Ops:
  0.0 0.0 copy-start
  0.0 0.5 collective-permute-start.10
  0.5 2.6 %collective-permute-start.1 = (bf16[2048,256]{1,0:T(8,128)(2,1)}, bf16[2048,256]{1,0:T(8,128)(2,1)S(1)}, u32[]{:S(2)}, u32[]{:S(2)}) collective-permute-start(bf16[2048,256]{1,0:T(8,128)(2,1)} %refs_4_.1), channel_id=1, source_target_pairs={{2,6},{3,1},{6,10},{7,3},{10,14},{11,7},{14,12},{15,11},{12,8},{13... | collective-permute-start | bytes 3145736 | tf_op jit(solution)/shard_map/ppermute | solution.py:169
  3.0 0.2 collective-permute-start.9
  3.3 1.4 %collective-permute-start = (bf16[512,256]{1,0:T(8,128)(2,1)}, bf16[512,256]{1,0:T(8,128)(2,1)S(1)}, u32[]{:S(2)}, u32[]{:S(2)}) collective-permute-start(bf16[512,256]{1,0:T(8,128)(2,1)} %refs_5_.1), channel_id=1, source_target_pairs={{2,6},{3,1},{6,10},{7,3},{10,14},{11,7},{14,12},{15,11},{12,8},{13... | collective-permute-start | bytes 786440 | tf_op jit(solution)/shard_map/ppermute | solution.py:169
  4.6 11.5 %collective-permute-done.1 = bf16[2048,256]{1,0:T(8,128)(2,1)S(1)} collective-permute-done((bf16[2048,256]{1,0:T(8,128)(2,1)}, bf16[2048,256]{1,0:T(8,128)(2,1)S(1)}, u32[]{:S(2)}, u32[]{:S(2)}) %collective-permute-start.1) | collective-permute-done | bytes 1048608 | tf_op jit(solution)/shard_map/ppermute | solution.py:169
  16.1 2.0 %collective-permute-start.2 = (bf16[512,256]{1,0:T(8,128)(2,1)}, bf16[512,256]{1,0:T(8,128)(2,1)S(1)}, u32[]{:S(2)}, u32[]{:S(2)}) collective-permute-start(bf16[512,256]{1,0:T(8,128)(2,1)} %refs_5_.1), channel_id=1, source_target_pairs={{6,2},{1,3},{10,6},{3,7},{14,10},{7,11},{12,14},{11,15},{8,12},{15... | collective-permute-start | bytes 786440 | tf_op jit(solution)/shard_map/ppermute | solution.py:189
  18.2 0.1 collective-permute-start.6
  18.3 0.7 collective-permute-done
  19.0 0.0 copy-start.4
  19.0 6.2 %collective-permute-done.2.refs_2_ = bf16[512,256]{1,0:T(8,128)(2,1)S(1)} collective-permute-done((bf16[512,256]{1,0:T(8,128)(2,1)}, bf16[512,256]{1,0:T(8,128)(2,1)S(1)}, u32[]{:S(2)}, u32[]{:S(2)}) %collective-permute-start.2) | collective-permute-done | bytes 262176 | tf_op jit(solution)/shard_map/ppermute | solution.py:189
  25.2 2.2 %collective-permute-start.3 = (bf16[1280,256]{1,0:T(8,128)(2,1)S(1)}, bf16[1280,256]{1,0:T(8,128)(2,1)S(1)}, u32[]{:S(2)}, u32[]{:S(2)}) collective-permute-start(bf16[1280,256]{1,0:T(8,128)(2,1)S(1)} %pad_maximum_fusion.refs_5_), channel_id=1, source_target_pairs={{2,6},{3,1},{6,10},{7,3},{10,14},{11,7},{14,12},{15,11},{12,8},{13... | collective-permute-start | bytes 1966088 | tf_op jit(solution)/shard_map/ppermute | solution.py:169
  27.4 1.4 %collective-permute-done.6.refs_4_ = bf16[1280,256]{1,0:T(8,128)(2,1)S(1)} collective-permute-done((bf16[1280,256]{1,0:T(8,128)(2,1)S(1)}, bf16[1280,256]{1,0:T(8,128)(2,1)S(1)}, u32[]{:S(2)}, u32[]{:S(2)}) %collective-permute-start.6) | collective-permute-done | bytes 655392 | tf_op jit(solution)/shard_map/ppermute | solution.py:169
  28.8 1.9 %collective-permute-start.7 = (bf16[1280,256]{1,0:T(8,128)(2,1)S(1)}, bf16[1280,256]{1,0:T(8,128)(2,1)}, u32[]{:S(2)}, u32[]{:S(2)}) collective-permute-start(bf16[1280,256]{1,0:T(8,128)(2,1)S(1)} %collective-permute-done.6.refs_4_), channel_id=1, source_target_pairs={{2,6},{3,1},{6,10},{7,3},{10,14},{11,7},{14,12},{15,11},{12,8},{13... | collective-permute-start | bytes 1966088 | tf_op jit(solution)/shard_map/ppermute | solution.py:169
  30.7 5.4 %collective-permute-done.3.refs_5_ = bf16[1280,256]{1,0:T(8,128)(2,1)S(1)} collective-permute-done((bf16[1280,256]{1,0:T(8,128)(2,1)S(1)}, bf16[1280,256]{1,0:T(8,128)(2,1)S(1)}, u32[]{:S(2)}, u32[]{:S(2)}) %collective-permute-start.3) | collective-permute-done | bytes 655392 | tf_op jit(solution)/shard_map/ppermute | solution.py:169
  36.1 1.9 %collective-permute-start.4 = (bf16[1280,256]{1,0:T(8,128)(2,1)S(1)}, bf16[1280,256]{1,0:T(8,128)(2,1)}, u32[]{:S(2)}, u32[]{:S(2)}) collective-permute-start(bf16[1280,256]{1,0:T(8,128)(2,1)S(1)} %collective-permute-done.3.refs_5_), channel_id=1, source_target_pairs={{2,6},{3,1},{6,10},{7,3},{10,14},{11,7},{14,12},{15,11},{12,8},{13... | collective-permute-start | bytes 1966088 | tf_op jit(solution)/shard_map/ppermute | solution.py:169
  38.0 0.0 copy-done.4
  38.0 5.2 %collective-permute-done.7.refs_4_ = bf16[1280,256]{1,0:T(8,128)(2,1)} collective-permute-done((bf16[1280,256]{1,0:T(8,128)(2,1)S(1)}, bf16[1280,256]{1,0:T(8,128)(2,1)}, u32[]{:S(2)}, u32[]{:S(2)}) %collective-permute-start.7) | collective-permute-done | bytes 655392 | tf_op jit(solution)/shard_map/ppermute | solution.py:169
  43.2 0.0 copy-done.6
  43.2 1.9 %collective-permute-start.8 = (bf16[1280,256]{1,0:T(8,128)(2,1)}, bf16[1280,256]{1,0:T(8,128)(2,1)S(1)}, u32[]{:S(2)}, u32[]{:S(2)}) collective-permute-start(bf16[1280,256]{1,0:T(8,128)(2,1)} %collective-permute-done.7.refs_4_), channel_id=1, source_target_pairs={{2,6},{3,1},{6,10},{7,3},{10,14},{11,7},{14,12},{15,11},{12,8},{13... | collective-permute-start | bytes 1966088 | tf_op jit(solution)/shard_map/ppermute | solution.py:169
  45.2 5.1 %collective-permute-done.4.refs_5_ = bf16[1280,256]{1,0:T(8,128)(2,1)} collective-permute-done((bf16[1280,256]{1,0:T(8,128)(2,1)S(1)}, bf16[1280,256]{1,0:T(8,128)(2,1)}, u32[]{:S(2)}, u32[]{:S(2)}) %collective-permute-start.4) | collective-permute-done | bytes 655392 | tf_op jit(solution)/shard_map/ppermute | solution.py:169
  50.3 1.9 %collective-permute-start.5 = (bf16[1280,256]{1,0:T(8,128)(2,1)}, bf16[1280,256]{1,0:T(8,128)(2,1)}, u32[]{:S(2)}, u32[]{:S(2)}) collective-permute-start(bf16[1280,256]{1,0:T(8,128)(2,1)} %collective-permute-done.4.refs_5_), channel_id=1, source_target_pairs={{2,6},{3,1},{6,10},{7,3},{10,14},{11,7},{14,12},{15,11},{12,8},{13... | collective-permute-start | bytes 1966088 | tf_op jit(solution)/shard_map/ppermute | solution.py:169
  52.2 0.7 dynamic-slice_bitcast_fusion.order_ref
  52.9 0.0 collective-permute-done.9.refs_1_
  52.9 0.0 collective-permute-done.10.refs_3_.sib_ref.refs_1_
  52.9 0.0 copy-done
  52.9 0.0 copy-done.1
  52.9 2.6 %step.9 = (f32[320,256]{1,0:T(8,128)S(1)}, f32[320,256]{1,0:T(8,128)S(1)}) custom-call(s32[8]{0:T(128)S(1)} %dynamic-slice_bitcast_fusion.order_ref, bf16[160,8192]{1,0:T(8,128)(2,1)} %refs_0_.17, bf16[160,8192]{1,0:T(8,128)(2,1)} %collective-permute-done.9.refs_1_, bf16[160,32768]{1,0:T(8,128)(2,1)} %refs_0_.16, ...), custom_call_target="tpu_custom_call" | custom-call | flops 419430400 | bytes 3604480 | tf_op jit(solution)/shard_map/step/pallas_call | solution.py:59
  55.5 2.8 %step.10 = (f32[320,256]{1,0:T(8,128)S(1)}, f32[320,256]{1,0:T(8,128)S(1)}) custom-call(s32[8]{0:T(128)S(1)} %dynamic-slice_bitcast_fusion.order_ref, bf16[160,8192]{1,0:T(8,128)(2,1)} %refs_0_.17, bf16[160,8192]{1,0:T(8,128)(2,1)} %collective-permute-done.9.refs_1_, bf16[160,32768]{1,0:T(8,128)(2,1)} %refs_0_.16, ...), custom_call_target="tpu_custom_call" | custom-call | flops 419430400 | bytes 4259840 | tf_op jit(solution)/shard_map/step/pallas_call | solution.py:59
  58.3 0.0 collective-permute-done.8.refs_4_
  58.3 1.6 %collective-permute-start.12 = (bf16[1280,256]{1,0:T(8,128)(2,1)S(1)}, bf16[1280,256]{1,0:T(8,128)(2,1)S(1)}, u32[]{:S(2)}, u32[]{:S(2)}) collective-permute-start(bf16[1280,256]{1,0:T(8,128)(2,1)S(1)} %collective-permute-done.8.refs_4_), channel_id=1, source_target_pairs={{2,6},{3,1},{6,10},{7,3},{10,14},{11,7},{14,12},{15,11},{12,8},{13... | collective-permute-start | bytes 1966088 | tf_op jit(solution)/shard_map/ppermute | solution.py:169
  59.9 4.4 %collective-permute-done.5.refs_5_ = bf16[1280,256]{1,0:T(8,128)(2,1)} collective-permute-done((bf16[1280,256]{1,0:T(8,128)(2,1)}, bf16[1280,256]{1,0:T(8,128)(2,1)}, u32[]{:S(2)}, u32[]{:S(2)}) %collective-permute-start.5) | collective-permute-done | bytes 655392 | tf_op jit(solution)/shard_map/ppermute | solution.py:169
  64.3 1.9 %collective-permute-start.11 = (bf16[1280,256]{1,0:T(8,128)(2,1)}, bf16[1280,256]{1,0:T(8,128)(2,1)S(1)}, u32[]{:S(2)}, u32[]{:S(2)}) collective-permute-start(bf16[1280,256]{1,0:T(8,128)(2,1)} %collective-permute-done.5.refs_5_), channel_id=1, source_target_pairs={{2,6},{3,1},{6,10},{7,3},{10,14},{11,7},{14,12},{15,11},{12,8},{13... | collective-permute-start | bytes 1966088 | tf_op jit(solution)/shard_map/ppermute | solution.py:169
  66.2 2.8 %step.11 = (f32[320,256]{1,0:T(8,128)S(1)}, f32[320,256]{1,0:T(8,128)S(1)}) custom-call(s32[8]{0:T(128)S(1)} %dynamic-slice_bitcast_fusion.order_ref, bf16[160,8192]{1,0:T(8,128)(2,1)} %refs_0_.17, bf16[160,8192]{1,0:T(8,128)(2,1)} %collective-permute-done.9.refs_1_, bf16[160,32768]{1,0:T(8,128)(2,1)} %refs_0_.16, ...), custom_call_target="tpu_custom_call" | custom-call | flops 419430400 | bytes 4259840 | tf_op jit(solution)/shard_map/step/pallas_call | solution.py:59
  69.0 3.0 %step.12 = (f32[320,256]{1,0:T(8,128)S(1)}, f32[320,256]{1,0:T(8,128)S(1)}) custom-call(s32[8]{0:T(128)S(1)} %dynamic-slice_bitcast_fusion.order_ref, bf16[160,8192]{1,0:T(8,128)(2,1)} %refs_0_.17, bf16[160,8192]{1,0:T(8,128)(2,1)} %collective-permute-done.9.refs_1_, bf16[160,32768]{1,0:T(8,128)(2,1)} %refs_0_.16, ...), custom_call_target="tpu_custom_call" | custom-call | flops 419430400 | bytes 4259840 | tf_op jit(solution)/shard_map/step/pallas_call | solution.py:59
  72.0 0.0 collective-permute-done.12.refs_4_
  72.0 1.6 %collective-permute-start.14 = (bf16[1280,256]{1,0:T(8,128)(2,1)S(1)}, bf16[1280,256]{1,0:T(8,128)(2,1)S(1)}, u32[]{:S(2)}, u32[]{:S(2)}) collective-permute-start(bf16[1280,256]{1,0:T(8,128)(2,1)S(1)} %collective-permute-done.12.refs_4_), channel_id=1, source_target_pairs={{2,6},{3,1},{6,10},{7,3},{10,14},{11,7},{14,12},{15,11},{12,8},{13... | collective-permute-start | bytes 1966088 | tf_op jit(solution)/shard_map/ppermute | solution.py:169
  73.6 4.6 %collective-permute-done.11.refs_5_ = bf16[1280,256]{1,0:T(8,128)(2,1)S(1)} collective-permute-done((bf16[1280,256]{1,0:T(8,128)(2,1)}, bf16[1280,256]{1,0:T(8,128)(2,1)S(1)}, u32[]{:S(2)}, u32[]{:S(2)}) %collective-permute-start.11) | collective-permute-done | bytes 655392 | tf_op jit(solution)/shard_map/ppermute | solution.py:169
  78.3 1.9 %collective-permute-start.13 = (bf16[1280,256]{1,0:T(8,128)(2,1)S(1)}, bf16[1280,256]{1,0:T(8,128)(2,1)S(1)}, u32[]{:S(2)}, u32[]{:S(2)}) collective-permute-start(bf16[1280,256]{1,0:T(8,128)(2,1)S(1)} %collective-permute-done.11.refs_5_), channel_id=1, source_target_pairs={{2,6},{3,1},{6,10},{7,3},{10,14},{11,7},{14,12},{15,11},{12,8},{13... | collective-permute-start | bytes 1966088 | tf_op jit(solution)/shard_map/ppermute | solution.py:169
  80.2 2.8 %step.13 = (f32[320,256]{1,0:T(8,128)S(1)}, f32[320,256]{1,0:T(8,128)S(1)}) custom-call(s32[8]{0:T(128)S(1)} %dynamic-slice_bitcast_fusion.order_ref, bf16[160,8192]{1,0:T(8,128)(2,1)} %refs_0_.17, bf16[160,8192]{1,0:T(8,128)(2,1)} %collective-permute-done.9.refs_1_, bf16[160,32768]{1,0:T(8,128)(2,1)} %refs_0_.16, ...), custom_call_target="tpu_custom_call" | custom-call | flops 419430400 | bytes 4259840 | tf_op jit(solution)/shard_map/step/pallas_call | solution.py:59
  82.9 0.0 copy-done.7
  82.9 0.0 copy-start.2
  83.0 0.0 copy-start.3
  83.0 2.8 %step.14 = (f32[320,256]{1,0:T(8,128)S(1)}, f32[320,256]{1,0:T(8,128)S(1)}) custom-call(s32[8]{0:T(128)S(1)} %dynamic-slice_bitcast_fusion.order_ref, bf16[160,8192]{1,0:T(8,128)(2,1)} %refs_0_.17, bf16[160,8192]{1,0:T(8,128)(2,1)} %collective-permute-done.9.refs_1_, bf16[160,32768]{1,0:T(8,128)(2,1)} %refs_0_.16, ...), custom_call_target="tpu_custom_call" | custom-call | flops 419430400 | bytes 4259840 | tf_op jit(solution)/shard_map/step/pallas_call | solution.py:59
  85.8 0.0 collective-permute-done.14.refs_4_
  85.8 1.6 %collective-permute-start.17 = (bf16[1280,256]{1,0:T(8,128)(2,1)S(1)}, bf16[1280,256]{1,0:T(8,128)(2,1)S(1)}, u32[]{:S(2)}, u32[]{:S(2)}) collective-permute-start(bf16[1280,256]{1,0:T(8,128)(2,1)S(1)} %collective-permute-done.14.refs_4_), channel_id=1, source_target_pairs={{2,6},{3,1},{6,10},{7,3},{10,14},{11,7},{14,12},{15,11},{12,8},{13... | collective-permute-start | bytes 1966088 | tf_op jit(solution)/shard_map/ppermute | solution.py:169
  87.4 4.9 %collective-permute-done.13.refs_5_ = bf16[1280,256]{1,0:T(8,128)(2,1)S(1)} collective-permute-done((bf16[1280,256]{1,0:T(8,128)(2,1)S(1)}, bf16[1280,256]{1,0:T(8,128)(2,1)S(1)}, u32[]{:S(2)}, u32[]{:S(2)}) %collective-permute-start.13) | collective-permute-done | bytes 655392 | tf_op jit(solution)/shard_map/ppermute | solution.py:169
  92.3 2.0 %collective-permute-start.16 = (bf16[768,256]{1,0:T(8,128)(2,1)S(1)}, bf16[768,256]{1,0:T(8,128)(2,1)S(1)}, u32[]{:S(2)}, u32[]{:S(2)}) collective-permute-start(bf16[768,256]{1,0:T(8,128)(2,1)S(1)} %slice.11), channel_id=1, source_target_pairs={{2,6},{3,1},{6,10},{7,3},{10,14},{11,7},{14,12},{15,11},{12,8},{13... | collective-permute-start | bytes 1179656 | tf_op jit(solution)/shard_map/ppermute | solution.py:169
  94.3 0.0 copy-done.2
  94.3 0.0 copy-done.3
  94.3 0.1 collective-permute-start.15
  94.4 1.9 %window.1.window_ref = bf16[320,768]{1,0:T(8,128)(2,1)S(1)} custom-call(s32[8]{0:T(128)S(1)} %dynamic-slice_bitcast_fusion.order_ref, bf16[160,32768]{1,0:T(8,128)(2,1)} %refs_0_.16, bf16[160,32768]{1,0:T(8,128)(2,1)} %collective-permute-done.10.refs_3_.sib_ref.refs_1_), custom_call_target="tpu_custom_call" | custom-call | bytes 1802240 | tf_op jit(solution)/shard_map/window/pallas_call | solution.py:59
  96.2 0.0 copy-done.5
  96.3 0.0 collective-permute-done.15
  96.3 2.8 %step.15 = (f32[320,256]{1,0:T(8,128)S(1)}, f32[320,256]{1,0:T(8,128)S(1)}) custom-call(s32[8]{0:T(128)S(1)} %dynamic-slice_bitcast_fusion.order_ref, bf16[160,8192]{1,0:T(8,128)(2,1)} %refs_0_.17, bf16[160,8192]{1,0:T(8,128)(2,1)} %collective-permute-done.9.refs_1_, bf16[160,32768]{1,0:T(8,128)(2,1)} %refs_0_.16, ...), custom_call_target="tpu_custom_call" | custom-call | flops 419430400 | bytes 4259840 | tf_op jit(solution)/shard_map/step/pallas_call | solution.py:59
  99.1 1.8 %step.17.inn_ref = f32[320,256]{1,0:T(8,128)S(1)} custom-call(s32[8]{0:T(128)S(1)} %dynamic-slice_bitcast_fusion.order_ref, bf16[160,8192]{1,0:T(8,128)(2,1)} %refs_0_.17, bf16[160,8192]{1,0:T(8,128)(2,1)} %collective-permute-done.9.refs_1_, bf16[512,256]{1,0:T(8,128)(2,1)S(1)} %collective-permute-done.2.refs_2_, f32[320,256]{1,0:T(8,128)S(1)} %get-tuple-element.84.refs_3_), custom_call_target="tpu_custom_call" | custom-call | flops 83886080 | bytes 1245184 | tf_op jit(solution)/shard_map/step/pallas_call | solution.py:59
  100.8 0.6 collective-permute-start.18
  101.4 0.0 collective-permute-done.17.refs_2_
  101.4 2.2 %step.16.out_ref = f32[320,256]{1,0:T(8,128)S(1)} custom-call(s32[8]{0:T(128)S(1)} %dynamic-slice_bitcast_fusion.order_ref, bf16[160,32768]{1,0:T(8,128)(2,1)} %refs_0_.16, bf16[160,32768]{1,0:T(8,128)(2,1)} %collective-permute-done.10.refs_3_.sib_ref.refs_1_, bf16[1280,256]{1,0:T(8,128)(2,1)S(1)} %collective-permute-done.17.refs_2_, ...), custom_call_target="tpu_custom_call" | custom-call | flops 209715200 | bytes 2621440 | tf_op jit(solution)/shard_map/step/pallas_call | solution.py:59
  103.6 0.0 collective-permute-done.18.got_ref
  103.6 0.0 collective-permute-done.16.b_ref
  103.7 1.1 score.1
  104.8 12.5 %all_to_all.5 = f32[16,2,8]{2,1,0:T(2,128)S(1)} all-to-all(f32[16,2,8]{2,1,0:T(2,128)S(1)} %bitcast.9), channel_id=1, replica_groups=mesh['groups'=2,'dp'=16] {'dp'}, dimensions={0} | all-to-all | bytes 2048 | tf_op jit(solution)/shard_map/all_to_all | solution.py:235
  117.3 0.6 reduce_sum.9
  (10 shorter events, 0.2 us)
Async XLA Ops:
  0.0 52.9 %copy-start = (bf16[2048,256]{1,0:T(8,128)(2,1)S(1)}, bf16[2048,256]{1,0:T(8,128)(2,1)}, u32[]{:S(2)}) copy-start(bf16[2048,256]{1,0:T(8,128)(2,1)} %refs_4_.1) | copy-start | bytes 3145732
  0.0 52.9 %copy-start.1 = (bf16[512,256]{1,0:T(8,128)(2,1)S(1)}, bf16[512,256]{1,0:T(8,128)(2,1)}, u32[]{:S(2)}) copy-start(bf16[512,256]{1,0:T(8,128)(2,1)} %refs_5_.1) | copy-start | bytes 786436
  0.0 52.9 %collective-permute-start.10 = (bf16[160,32768]{1,0:T(8,128)(2,1)}, bf16[160,32768]{1,0:T(8,128)(2,1)}, u32[]{:S(2)}, u32[]{:S(2)}) collective-permute-start(bf16[160,32768]{1,0:T(8,128)(2,1)} %refs_0_.16), channel_id=1, source_target_pairs={{0,1},{1,0},{2,3},{3,2},{4,5},{5,4},{6,7},{7,6},{8,9},{9,8},{10,11... | collective-permute-start | bytes 31457288 | tf_op jit(solution)/shard_map/ppermute | solution.py:170
  0.5 15.6 %collective-permute-start.1 = (bf16[2048,256]{1,0:T(8,128)(2,1)}, bf16[2048,256]{1,0:T(8,128)(2,1)S(1)}, u32[]{:S(2)}, u32[]{:S(2)}) collective-permute-start(bf16[2048,256]{1,0:T(8,128)(2,1)} %refs_4_.1), channel_id=1, source_target_pairs={{2,6},{3,1},{6,10},{7,3},{10,14},{11,7},{14,12},{15,11},{12,8},{13... | collective-permute-start | bytes 3145736 | tf_op jit(solution)/shard_map/ppermute | solution.py:169
  3.0 49.8 %collective-permute-start.9 = (bf16[160,8192]{1,0:T(8,128)(2,1)}, bf16[160,8192]{1,0:T(8,128)(2,1)}, u32[]{:S(2)}, u32[]{:S(2)}) collective-permute-start(bf16[160,8192]{1,0:T(8,128)(2,1)} %refs_0_.17), channel_id=1, source_target_pairs={{0,1},{1,0},{2,3},{3,2},{4,5},{5,4},{6,7},{7,6},{8,9},{9,8},{10,11... | collective-permute-start | bytes 7864328 | tf_op jit(solution)/shard_map/ppermute | solution.py:170
  3.3 15.7 %collective-permute-start = (bf16[512,256]{1,0:T(8,128)(2,1)}, bf16[512,256]{1,0:T(8,128)(2,1)S(1)}, u32[]{:S(2)}, u32[]{:S(2)}) collective-permute-start(bf16[512,256]{1,0:T(8,128)(2,1)} %refs_5_.1), channel_id=1, source_target_pairs={{2,6},{3,1},{6,10},{7,3},{10,14},{11,7},{14,12},{15,11},{12,8},{13... | collective-permute-start | bytes 786440 | tf_op jit(solution)/shard_map/ppermute | solution.py:169
  16.1 9.2 %collective-permute-start.2 = (bf16[512,256]{1,0:T(8,128)(2,1)}, bf16[512,256]{1,0:T(8,128)(2,1)S(1)}, u32[]{:S(2)}, u32[]{:S(2)}) collective-permute-start(bf16[512,256]{1,0:T(8,128)(2,1)} %refs_5_.1), channel_id=1, source_target_pairs={{6,2},{1,3},{10,6},{3,7},{14,10},{7,11},{12,14},{11,15},{8,12},{15... | collective-permute-start | bytes 786440 | tf_op jit(solution)/shard_map/ppermute | solution.py:189
  18.2 10.6 %collective-permute-start.6 = (bf16[1280,256]{1,0:T(8,128)(2,1)S(1)}, bf16[1280,256]{1,0:T(8,128)(2,1)S(1)}, u32[]{:S(2)}, u32[]{:S(2)}) collective-permute-start(bf16[1280,256]{1,0:T(8,128)(2,1)S(1)} %slice.10.refs_4_), channel_id=1, source_target_pairs={{2,6},{3,1},{6,10},{7,3},{10,14},{11,7},{14,12},{15,11},{12,8},{13... | collective-permute-start | bytes 1966088 | tf_op jit(solution)/shard_map/ppermute | solution.py:169
  19.0 19.0 %copy-start.4 = (bf16[1280,256]{1,0:T(8,128)(2,1)}, bf16[1280,256]{1,0:T(8,128)(2,1)S(1)}, u32[]{:S(2)}) copy-start(bf16[1280,256]{1,0:T(8,128)(2,1)S(1)} %pad_maximum_fusion.refs_5_) | copy-start | bytes 1966084
  25.2 10.9 %collective-permute-start.3 = (bf16[1280,256]{1,0:T(8,128)(2,1)S(1)}, bf16[1280,256]{1,0:T(8,128)(2,1)S(1)}, u32[]{:S(2)}, u32[]{:S(2)}) collective-permute-start(bf16[1280,256]{1,0:T(8,128)(2,1)S(1)} %pad_maximum_fusion.refs_5_), channel_id=1, source_target_pairs={{2,6},{3,1},{6,10},{7,3},{10,14},{11,7},{14,12},{15,11},{12,8},{13... | collective-permute-start | bytes 1966088 | tf_op jit(solution)/shard_map/ppermute | solution.py:169
  28.8 14.4 %collective-permute-start.7 = (bf16[1280,256]{1,0:T(8,128)(2,1)S(1)}, bf16[1280,256]{1,0:T(8,128)(2,1)}, u32[]{:S(2)}, u32[]{:S(2)}) collective-permute-start(bf16[1280,256]{1,0:T(8,128)(2,1)S(1)} %collective-permute-done.6.refs_4_), channel_id=1, source_target_pairs={{2,6},{3,1},{6,10},{7,3},{10,14},{11,7},{14,12},{15,11},{12,8},{13... | collective-permute-start | bytes 1966088 | tf_op jit(solution)/shard_map/ppermute | solution.py:169
  36.1 7.1 %copy-start.6 = (bf16[1280,256]{1,0:T(8,128)(2,1)}, bf16[1280,256]{1,0:T(8,128)(2,1)S(1)}, u32[]{:S(2)}) copy-start(bf16[1280,256]{1,0:T(8,128)(2,1)S(1)} %collective-permute-done.3.refs_5_) | copy-start | bytes 1966084
  36.1 14.1 %collective-permute-start.4 = (bf16[1280,256]{1,0:T(8,128)(2,1)S(1)}, bf16[1280,256]{1,0:T(8,128)(2,1)}, u32[]{:S(2)}, u32[]{:S(2)}) collective-permute-start(bf16[1280,256]{1,0:T(8,128)(2,1)S(1)} %collective-permute-done.3.refs_5_), channel_id=1, source_target_pairs={{2,6},{3,1},{6,10},{7,3},{10,14},{11,7},{14,12},{15,11},{12,8},{13... | collective-permute-start | bytes 1966088 | tf_op jit(solution)/shard_map/ppermute | solution.py:169
  43.2 15.0 %collective-permute-start.8 = (bf16[1280,256]{1,0:T(8,128)(2,1)}, bf16[1280,256]{1,0:T(8,128)(2,1)S(1)}, u32[]{:S(2)}, u32[]{:S(2)}) collective-permute-start(bf16[1280,256]{1,0:T(8,128)(2,1)} %collective-permute-done.7.refs_4_), channel_id=1, source_target_pairs={{2,6},{3,1},{6,10},{7,3},{10,14},{11,7},{14,12},{15,11},{12,8},{13... | collective-permute-start | bytes 1966088 | tf_op jit(solution)/shard_map/ppermute | solution.py:169
  50.3 14.0 %collective-permute-start.5 = (bf16[1280,256]{1,0:T(8,128)(2,1)}, bf16[1280,256]{1,0:T(8,128)(2,1)}, u32[]{:S(2)}, u32[]{:S(2)}) collective-permute-start(bf16[1280,256]{1,0:T(8,128)(2,1)} %collective-permute-done.4.refs_5_), channel_id=1, source_target_pairs={{2,6},{3,1},{6,10},{7,3},{10,14},{11,7},{14,12},{15,11},{12,8},{13... | collective-permute-start | bytes 1966088 | tf_op jit(solution)/shard_map/ppermute | solution.py:169
  58.3 13.7 %collective-permute-start.12 = (bf16[1280,256]{1,0:T(8,128)(2,1)S(1)}, bf16[1280,256]{1,0:T(8,128)(2,1)S(1)}, u32[]{:S(2)}, u32[]{:S(2)}) collective-permute-start(bf16[1280,256]{1,0:T(8,128)(2,1)S(1)} %collective-permute-done.8.refs_4_), channel_id=1, source_target_pairs={{2,6},{3,1},{6,10},{7,3},{10,14},{11,7},{14,12},{15,11},{12,8},{13... | collective-permute-start | bytes 1966088 | tf_op jit(solution)/shard_map/ppermute | solution.py:169
  64.3 13.9 %collective-permute-start.11 = (bf16[1280,256]{1,0:T(8,128)(2,1)}, bf16[1280,256]{1,0:T(8,128)(2,1)S(1)}, u32[]{:S(2)}, u32[]{:S(2)}) collective-permute-start(bf16[1280,256]{1,0:T(8,128)(2,1)} %collective-permute-done.5.refs_5_), channel_id=1, source_target_pairs={{2,6},{3,1},{6,10},{7,3},{10,14},{11,7},{14,12},{15,11},{12,8},{13... | collective-permute-start | bytes 1966088 | tf_op jit(solution)/shard_map/ppermute | solution.py:169
  72.0 13.8 %collective-permute-start.14 = (bf16[1280,256]{1,0:T(8,128)(2,1)S(1)}, bf16[1280,256]{1,0:T(8,128)(2,1)S(1)}, u32[]{:S(2)}, u32[]{:S(2)}) collective-permute-start(bf16[1280,256]{1,0:T(8,128)(2,1)S(1)} %collective-permute-done.12.refs_4_), channel_id=1, source_target_pairs={{2,6},{3,1},{6,10},{7,3},{10,14},{11,7},{14,12},{15,11},{12,8},{13... | collective-permute-start | bytes 1966088 | tf_op jit(solution)/shard_map/ppermute | solution.py:169
  78.2 4.7 %copy-start.7 = (bf16[1280,256]{1,0:T(8,128)(2,1)}, bf16[1280,256]{1,0:T(8,128)(2,1)S(1)}, u32[]{:S(2)}) copy-start(bf16[1280,256]{1,0:T(8,128)(2,1)S(1)} %collective-permute-done.11.refs_5_) | copy-start | bytes 1966084
  78.3 14.0 %collective-permute-start.13 = (bf16[1280,256]{1,0:T(8,128)(2,1)S(1)}, bf16[1280,256]{1,0:T(8,128)(2,1)S(1)}, u32[]{:S(2)}, u32[]{:S(2)}) collective-permute-start(bf16[1280,256]{1,0:T(8,128)(2,1)S(1)} %collective-permute-done.11.refs_5_), channel_id=1, source_target_pairs={{2,6},{3,1},{6,10},{7,3},{10,14},{11,7},{14,12},{15,11},{12,8},{13... | collective-permute-start | bytes 1966088 | tf_op jit(solution)/shard_map/ppermute | solution.py:169
  82.9 11.3 %copy-start.2 = (s32[2]{0:T(128)S(1)}, s32[2]{0:T(128)}, u32[]{:S(2)}) copy-start(s32[2]{0:T(128)} %seq_ref.1) | copy-start | bytes 28
  83.0 11.3 %copy-start.3 = (s32[2]{0:T(128)S(1)}, s32[2]{0:T(128)}, u32[]{:S(2)}) copy-start(s32[2]{0:T(128)} %len_ref.1) | copy-start | bytes 28
  85.8 15.6 %collective-permute-start.17 = (bf16[1280,256]{1,0:T(8,128)(2,1)S(1)}, bf16[1280,256]{1,0:T(8,128)(2,1)S(1)}, u32[]{:S(2)}, u32[]{:S(2)}) collective-permute-start(bf16[1280,256]{1,0:T(8,128)(2,1)S(1)} %collective-permute-done.14.refs_4_), channel_id=1, source_target_pairs={{2,6},{3,1},{6,10},{7,3},{10,14},{11,7},{14,12},{15,11},{12,8},{13... | collective-permute-start | bytes 1966088 | tf_op jit(solution)/shard_map/ppermute | solution.py:169
  92.3 4.0 %copy-start.5 = (bf16[1280,256]{1,0:T(8,128)(2,1)}, bf16[1280,256]{1,0:T(8,128)(2,1)S(1)}, u32[]{:S(2)}) copy-start(bf16[1280,256]{1,0:T(8,128)(2,1)S(1)} %collective-permute-done.13.refs_5_) | copy-start | bytes 1966084
  92.3 11.3 %collective-permute-start.16 = (bf16[768,256]{1,0:T(8,128)(2,1)S(1)}, bf16[768,256]{1,0:T(8,128)(2,1)S(1)}, u32[]{:S(2)}, u32[]{:S(2)}) collective-permute-start(bf16[768,256]{1,0:T(8,128)(2,1)S(1)} %slice.11), channel_id=1, source_target_pairs={{2,6},{3,1},{6,10},{7,3},{10,14},{11,7},{14,12},{15,11},{12,8},{13... | collective-permute-start | bytes 1179656 | tf_op jit(solution)/shard_map/ppermute | solution.py:169
  94.3 2.0 %collective-permute-start.15 = (s32[2,2]{1,0:T(2,128)S(1)}, s32[2,2]{1,0:T(2,128)S(1)}, u32[]{:S(2)}, u32[]{:S(2)}) collective-permute-start(s32[2,2]{1,0:T(2,128)S(1)} %pad_add_fusion), channel_id=1, source_target_pairs={{0,1},{1,0},{2,3},{3,2},{4,5},{5,4},{6,7},{7,6},{8,9},{9,8},{10,11... | collective-permute-start | bytes 56 | tf_op jit(solution)/shard_map/ppermute | solution.py:170
  100.8 2.8 %collective-permute-start.18 = (f32[320,256]{1,0:T(8,128)S(1)}, f32[320,256]{1,0:T(8,128)S(1)}, u32[]{:S(2)}, u32[]{:S(2)}) collective-permute-start(f32[320,256]{1,0:T(8,128)S(1)} %step.17.inn_ref), channel_id=1, source_target_pairs={{0,1},{1,0},{2,3},{3,2},{4,5},{5,4},{6,7},{7,6},{8,9},{9,8},{10,11... | collective-permute-start | bytes 983048 | tf_op jit(solution)/shard_map/ppermute | solution.py:170

commit v13 on v12

--- a/solution.py
+++ b/solution.py
@@ -154,7 +154,7 @@
     )(*numbers, *arrays)
 
 
-def shards(acts, grads, out_factors, in_factors, seq_slot, lengths):
+def ring_shards(acts, grads, out_factors, in_factors, seq_slot, lengths):
     devices = lax.axis_size("dp")
     chips = devices // 2
     me = lax.axis_index("dp")
@@ -236,6 +236,247 @@
     return jnp.sum(got, axis=0)
 
 
+EXTRA = 8
+MIDDLE = {0: 1, 7: 6, 3: 2, 4: 5}
+INTERIOR = {1: 6, 6: 1, 2: 5, 5: 2}
+LANE = {0: 0, 7: 1, 3: 1, 4: 0}
+
+
+class Links:
+    def __init__(self):
+        ring = ring_of(8)
+        at = lambda place, core: 2 * ring[place] + core
+        self.ring = ring_pairs(8)
+        self.back = [(j, i) for i, j in self.ring]
+        self.inward = [(at(q, c), at(m, c)) for q, m in MIDDLE.items() for c in (0, 1)]
+        out = [(at(q, LANE[q]), at(m, LANE[q])) for q, m in MIDDLE.items()]
+        self.relieved = [pair for pair in self.ring if pair not in out]
+        self.near = [(at(INTERIOR[m], LANE[q]), at(m, LANE[q])) for q, m in MIDDLE.items()]
+        self.far = [(at(INTERIOR[m], 1 - LANE[q]), at(m, 1 - LANE[q])) for q, m in MIDDLE.items()]
+        flag = np.zeros((16, 1), np.int32)
+        flag[[j for _, j in self.near]] = 1
+        self.table = np.concatenate([block_orders(8), flag], axis=1)
+        blocks = block_orders(8)
+        for i, j in self.inward:
+            at_hand = blocks[j, 0] if flag[j] else blocks[dict((y, x) for x, y in self.far)[j], 1]
+            assert blocks[i, 7] == at_hand
+        for i, j in self.near:
+            assert all(blocks[i, s - 2] == blocks[j, s + 1] for s in (2, 3, 4, 5, 6))
+        for i, j in self.far:
+            assert blocks[i, 2] == blocks[j, 7]
+
+
+FLAG = 8
+
+
+def turned_kernel(count, order_ref, *refs):
+    windows, blocks = refs[:2 * count], refs[2 * count:3 * count]
+    total_ref, seq_ref, len_ref, out_ref = refs[3 * count:]
+    tokens = windows[0].shape[0]
+    for k in range(2):
+        at = pl.ds(k * tokens, tokens)
+        total = total_ref[at]
+        for w in range(count):
+            total += dot(windows[2 * w + k][...], blocks[w][...])
+        out_ref[at] = total
+    held = seq_ref.shape[0]
+    lane = lax.broadcasted_iota(jnp.int32, (EXTRA, out_ref.shape[1]), 1)
+    numbers = jnp.zeros(lane.shape, F32)
+    for i in range(held):
+        numbers = jnp.where(lane == i, seq_ref[i].astype(F32), numbers)
+        numbers = jnp.where(lane == held + i, len_ref[i].astype(F32), numbers)
+    out_ref[2 * tokens:] = numbers
+
+
+def masked_kernel(order_ref, own_ref, got_ref, out_ref):
+    tokens = (own_ref.shape[0] - EXTRA) // 2
+    columns = own_ref.shape[1]
+    held = tokens // LEN
+    position = lax.broadcasted_iota(jnp.int32, (LEN, columns), 0).astype(F32)
+    for k, (mine, other) in enumerate(((own_ref, got_ref), (got_ref, own_ref))):
+        for i in range(held):
+            at, across = pl.ds(i * LEN, LEN), pl.ds(tokens + i * LEN, LEN)
+            length = mine[2 * tokens:2 * tokens + 1, held + i:held + i + 1]
+            out_ref[pl.ds(k * tokens + i * LEN, LEN)] = jnp.where(
+                position < length, mine[at] + other[across], 0.0
+            )
+    lane = lax.broadcasted_iota(jnp.int32, (EXTRA, columns), 1)
+    numbers = jnp.zeros(lane.shape, F32)
+    for k, ref in enumerate((own_ref, got_ref)):
+        for i in range(held):
+            slot = ref[2 * tokens:2 * tokens + 1, i:i + 1]
+            numbers = jnp.where(lane == k * held + i, slot, numbers)
+    out_ref[2 * tokens:] = numbers
+
+
+def cut_kernel(order_ref, own_ref, sib_ref, *outs):
+    tokens = own_ref.shape[0]
+    start = 0
+    for out_ref in outs:
+        width = out_ref.shape[1]
+        out_ref[:tokens] = own_ref[:, start:start + width]
+        out_ref[tokens:] = sib_ref[:, start:start + width]
+        start += width
+
+
+def job_kernel(order_ref, first_ref, second_ref, own_ref, far_ref, out_ref):
+    rows, half = far_ref.shape[0], first_ref.shape[1]
+    own = jnp.full(far_ref.shape, order_ref[FLAG], jnp.int32) == 1
+    block = jnp.where(own, own_ref[:rows], far_ref[...])
+    out_ref[...] = dot(first_ref[...], block[:half]) + dot(second_ref[...], block[half:])
+
+
+def finish_kernel(window_ref, block_ref, total_ref, inn_ref, job_ref, job_inn_ref, table_ref):
+    height, columns = total_ref.shape
+    queries = columns // RANK
+    column = lax.broadcasted_iota(jnp.int32, (columns, queries), 0) // RANK
+    query = lax.broadcasted_iota(jnp.int32, (columns, queries), 1)
+    fold = (column == query).astype(F32)
+    row = lax.broadcasted_iota(jnp.int32, table_ref.shape, 0).astype(F32)
+    sums, slots = [], []
+    out = total_ref[...] + dot(window_ref[...], block_ref[...])
+    for got, inn in ((out, inn_ref), (job_ref[...], job_inn_ref)):
+        contrib = got * inn[:height]
+        for i in range(height // LEN):
+            sums.append(jnp.sum(contrib[i * LEN:(i + 1) * LEN], axis=0, keepdims=True))
+            slots.append(inn[height:height + 1, i:i + 1])
+    scores = jnp.dot(
+        jnp.concatenate(sums), fold, precision=lax.Precision.HIGHEST, preferred_element_type=F32
+    ) * (1.0 / math.sqrt(RANK * LEN))
+    table = jnp.zeros(table_ref.shape, F32)
+    for i, slot in enumerate(slots):
+        table += jnp.where(row == slot, scores[i:i + 1], 0.0)
+    table_ref[...] = table
+
+
+def ring8_shards(acts, grads, out_factors, in_factors, seq_slot, lengths):
+    devices = lax.axis_size("dp")
+    links = Links()
+    order = lax.dynamic_index_in_dim(
+        jnp.asarray(links.table), lax.axis_index("dp"), keepdims=False
+    )
+    tokens = grads.shape[0]
+    rows, columns = out_factors.shape
+    ins = in_factors.shape[0]
+    lead = rows // 2
+    send = lambda x, pairs=links.ring: lax.ppermute(x, "dp", pairs)
+    swap = lambda x: send(x, [(d, d ^ 1) for d in range(devices)])
+    tie = lax.optimization_barrier
+
+    tokens_of = {"out": (grads, swap(grads), rows), "in": (acts, swap(acts), ins)}
+    g1, g2, window = call(
+        cut_kernel, order, [(x, rows, lambda i, o: (0, o[7])) for x in tokens_of["out"][:2]],
+        [], [],
+        [jax.ShapeDtypeStruct((2 * tokens, w), grads.dtype) for w in (lead // 2, lead // 2, rows - lead)],
+        0, "cut",
+    )
+
+    came = send(out_factors)
+    late, early = [None, came[lead:]], [out_factors[:lead], came[:lead]]
+    ahead, back = [None, send(in_factors)], [None, send(in_factors, links.back)]
+
+    pieces = [[(0, 0, rows, "out", 0), (1, 0, ins, "in", 0)]]
+    pieces += [
+        [(0, 0, rows - lead, "out", lead), (1, 0, lead, "out", 0), (2, 0, ins, "in", 0)]
+    ] * 4
+    pieces += [[(0, 0, rows - lead, "out", lead), (1, 0, lead, "out", 0)]] * 2
+    totals = {}
+
+    def add(*stages):
+        nonlocal totals
+        for k in stages:
+            blocks = [late[k], early[k]] + ahead[k:k + 1] if k else [out_factors, in_factors]
+            totals = step(order, tokens_of, blocks, pieces[k], totals, k)
+
+    def hold(k, *others):
+        nonlocal totals
+        late[k], totals = tie((late[k], totals))
+        early[k], totals, others = tie((early[k], totals, others))
+        return others
+
+    def hop(k):
+        late.append(send(late[k]))
+        if k == 1:
+            early.append(send(early[k]))
+        else:
+            early.append(send(early[k], links.relieved) + send(early[k - 2], links.near))
+        if k <= 3:
+            ahead.append(send(ahead[k]))
+        if k <= 2:
+            back.append(send(back[k], links.back))
+
+    hop(1)
+    far = send(early[1], links.far)
+    hop(2)
+    missing = send(early[2], links.far)
+
+    add(0)
+    g1, g2, ahead[2], back[2] = hold(3, g1, g2, ahead[2], back[2])
+    hop(3)
+    g1 = send(g1, links.inward)
+
+    add(1, 2)
+    g1, far, ahead[3], back[3] = hold(4, g1, far, ahead[3], back[3])
+    hop(4)
+    g2 = send(g2, links.inward)
+
+    add(3, 4)
+    inn = call(
+        functools.partial(turned_kernel, 3), order,
+        [
+            (x, ins, functools.partial(lambda i, o, k: (0, o[k]), k=8 - k))
+            for k in (1, 2, 3) for x in tokens_of["in"][:2]
+        ],
+        back[1:] + [totals["in"]], [seq_slot, lengths],
+        [jax.ShapeDtypeStruct((2 * tokens + EXTRA, columns), F32)],
+        12 * tokens * ins * columns, "turned",
+    )[0]
+    g2, inn, missing = hold(5, g2, inn, missing)
+    hop(5)
+    near = send(early[4], links.near)
+    inn = call(
+        masked_kernel, order, [], [inn, swap(inn)], [],
+        [jax.ShapeDtypeStruct(inn.shape, F32)], 0, "masked",
+    )[0]
+
+    job = call(
+        job_kernel, order, [], [g1, g2, out_factors, far], [],
+        [jax.ShapeDtypeStruct((2 * tokens, columns), F32)],
+        4 * tokens * lead * columns, "job",
+    )[0]
+    add(5)
+    late[6], totals, inn, job, window = tie((late[6], totals, inn, job, window))
+    last = send(late[6])
+    job_inn = send(inn, links.inward)
+    totals = step(
+        order, tokens_of, [missing + near], [(0, 0, lead, "out", 0)], totals, 7
+    )
+    add(6)
+
+    slots = lengths.shape[0]
+    queries = columns // RANK
+    arrays = [window, last, totals["out"], inn, job, job_inn]
+    table = pl.pallas_call(
+        finish_kernel,
+        in_specs=[pl.BlockSpec(memory_space=pltpu.VMEM)] * len(arrays),
+        out_specs=pl.BlockSpec(memory_space=pltpu.VMEM),
+        out_shape=jax.ShapeDtypeStruct((slots * devices, queries), F32),
+        cost_estimate=pl.CostEstimate(
+            flops=2 * window.size * columns, bytes_accessed=8 << 20, transcendentals=0
+        ),
+        compiler_params=pltpu.CompilerParams(vmem_limit_bytes=16 << 20),
+        name="finish",
+    )(*arrays)
+    got = lax.all_to_all(table.reshape(devices, slots, queries), "dp", 0, 0, tiled=True)
+    return jnp.sum(got, axis=0)
+
+
+def shards(acts, grads, out_factors, in_factors, seq_slot, lengths):
+    small = lax.axis_size("dp") == 16 and in_factors.shape[0] % 128 == 0
+    run = ring8_shards if small else ring_shards
+    return run(acts, grads, out_factors, in_factors, seq_slot, lengths)
+
+
 def solution(mesh):
     return jax.shard_map(
         shards,

time: 118 us -> 141 us (1.19)
  starting transfers between devices: 27.7 us -> 50.1 us
  waiting for transfers between devices: 49.5 us -> 38.9 us
  local copies, waits for them, and re-layouts: 0.83 us -> 4.85 us
  Pallas kernels: 26.4 us -> 28.6 us
  blocking collectives: 12.5 us -> 14.5 us
  other arithmetic: 0.64 us -> 2.5 us
    ppermute x19 -> x32, starting transfers between devices: 27.7 us -> 50.1 us  [ring8_shards(): send = lambda x, pairs=links.ring: lax.ppermute(x, 'dp', pairs)]
    ppermute x19 -> x32, waiting for transfers between devices: 49.5 us -> 38.9 us  [ring8_shards(): send = lambda x, pairs=links.ring: lax.ppermute(x, 'dp', pairs)]
    pallas_call x10 -> x12, Pallas kernels: 25.3 us -> 28 us  [call(): pl.pallas_call(kernel, grid_spec=pltpu.PrefetchScalarGridSpec(num_scalar_...]
    unnamed x16 -> x26, local copies, waits for them, and re-layouts: 0.04 us -> 2.22 us
    all_to_all x1, blocking collectives: 12.5 us -> 14.5 us  [ring8_shards(): lax.all_to_all(table.reshape(devices, slots, queries), 'dp', 0, 0, tiled=...]
    add x0 -> x5, other arithmetic: none -> 1.91 us  [the longest x4 1.77 us: hop(): send(early[k], links.relieved) + send(early[k - 2], links.near)]
    slice x3 -> x2, local copies, waits for them, and re-layouts: 0.1 us -> 1.94 us  [ring8_shards(): late, early = ([None, came[lead:]], [out_factors[:lead], came[:lead]])]
  transfers between devices with their start and end apart: 19 -> 32, of which waited for: 10 -> 7; matrix products, arithmetic and copies ran while one was open for 1% -> 3% of each run, Pallas kernels for 21% -> 20%
where the time goes in v13:
time: 141 us; the launch traced here: 140 us
  starting transfers between devices  50.1 us (36%)
  waiting for transfers between devices  38.9 us (28%)
  Pallas kernels  28.6 us (20%)
  blocking collectives  14.5 us (10%)
  local copies, waits for them, and re-layouts  4.85 us (3%)
  other arithmetic  2.5 us (2%)
    ppermute x32, starting transfers between devices, ring8_shards(): send = lambda x, pairs=links.ring: lax.ppermute(x, 'dp', pairs)  50.1 us
    ppermute x32, waiting for transfers between devices, ring8_shards(): send = lambda x, pairs=links.ring: lax.ppermute(x, 'dp', pairs)  38.9 us
    pallas_call x12, Pallas kernels, call(): pl.pallas_call(kernel, grid_spec=pltpu.PrefetchScalarGridSpec(num_scalar_...  28 us
    all_to_all x1, blocking collectives, ring8_shards(): lax.all_to_all(table.reshape(devices, slots, queries), 'dp', 0, 0, tiled=...  14.5 us
  transfers between devices with their start and end apart: 32, of which 7 were waited for; matrix products, arithmetic and copies ran while one was open for 3% of the time, Pallas kernels for 20%

profile of v13, /device:TPU:0, one launch (start us, length us, event | category | flops | bytes accessed | tf_op | source)
XLA Modules:
  0.0 140.1 jit_solution(8309680424047750097)
XLA Ops:
  0.0 0.5 collective-permute-start.4
  0.5 0.1 collective-permute-start.3
  0.5 3.0 %collective-permute-start = (bf16[2048,256]{1,0:T(8,128)(2,1)}, bf16[2048,256]{1,0:T(8,128)(2,1)S(1)}, u32[]{:S(2)}, u32[]{:S(2)}) collective-permute-start(bf16[2048,256]{1,0:T(8,128)(2,1)} %own_ref.3), channel_id=1, source_target_pairs={{2,6},{3,1},{6,10},{7,3},{10,14},{11,7},{14,12},{15,11},{12,8},{13... | collective-permute-start | bytes 3145736 | tf_op jit(solution)/shard_map/ppermute | solution.py:362
  3.5 13.0 %collective-permute-done = bf16[2048,256]{1,0:T(8,128)(2,1)S(1)} collective-permute-done((bf16[2048,256]{1,0:T(8,128)(2,1)}, bf16[2048,256]{1,0:T(8,128)(2,1)S(1)}, u32[]{:S(2)}, u32[]{:S(2)}) %collective-permute-start) | collective-permute-done | bytes 1048608 | tf_op jit(solution)/shard_map/ppermute | solution.py:362
  16.5 0.1 fusion
  16.6 2.0 %collective-permute-start.1 = (bf16[1024,256]{1,0:T(8,128)(2,1)S(1)}, bf16[1024,256]{1,0:T(8,128)(2,1)}, u32[]{:S(2)}, u32[]{:S(2)}) collective-permute-start(bf16[1024,256]{1,0:T(8,128)(2,1)S(1)} %get-tuple-element.96.refs_4_), channel_id=1, source_target_pairs={{2,6},{3,1},{6,10},{7,3},{10,14},{11,7},{14,12},{15,11},{12,8},{13... | collective-permute-start | bytes 1572872 | tf_op jit(solution)/shard_map/ppermute | solution.py:362
  18.6 1.6 %collective-permute-start.9 = (bf16[512,256]{1,0:T(8,128)(2,1)}, bf16[512,256]{1,0:T(8,128)(2,1)S(1)}, u32[]{:S(2)}, u32[]{:S(2)}) collective-permute-start(bf16[512,256]{1,0:T(8,128)(2,1)} %refs_5_.1), channel_id=1, source_target_pairs={{2,6},{3,1},{6,10},{7,3},{10,14},{11,7},{14,12},{15,11},{12,8},{13... | collective-permute-start | bytes 786440 | tf_op jit(solution)/shard_map/ppermute | solution.py:362
  20.2 1.6 %collective-permute-start.6 = (bf16[1024,256]{1,0:T(8,128)(2,1)S(1)}, bf16[1024,256]{1,0:T(8,128)(2,1)}, u32[]{:S(2)}, u32[]{:S(2)}) collective-permute-start(bf16[1024,256]{1,0:T(8,128)(2,1)S(1)} %get-tuple-element.95.refs_5_), channel_id=1, source_target_pairs={{2,6},{3,1},{6,10},{7,3},{10,14},{11,7},{14,12},{15,11},{12,8},{13... | collective-permute-start | bytes 1572872 | tf_op jit(solution)/shard_map/ppermute | solution.py:362
  21.8 6.9 %collective-permute-done.9.refs_6_ = bf16[512,256]{1,0:T(8,128)(2,1)S(1)} collective-permute-done((bf16[512,256]{1,0:T(8,128)(2,1)}, bf16[512,256]{1,0:T(8,128)(2,1)S(1)}, u32[]{:S(2)}, u32[]{:S(2)}) %collective-permute-start.9) | collective-permute-done | bytes 262176 | tf_op jit(solution)/shard_map/ppermute | solution.py:362
  28.7 2.0 %collective-permute-start.11 = (bf16[512,256]{1,0:T(8,128)(2,1)}, bf16[512,256]{1,0:T(8,128)(2,1)S(1)}, u32[]{:S(2)}, u32[]{:S(2)}) collective-permute-start(bf16[512,256]{1,0:T(8,128)(2,1)} %refs_5_.1), channel_id=1, source_target_pairs={{6,2},{1,3},{10,6},{3,7},{14,10},{7,11},{12,14},{11,15},{8,12},{15... | collective-permute-start | bytes 786440 | tf_op jit(solution)/shard_map/ppermute | solution.py:362
  30.7 0.0 collective-permute-start.2
  30.7 1.9 %slice.11 = bf16[1024,256]{1,0:T(8,128)(2,1)} slice(bf16[2048,256]{1,0:T(8,128)(2,1)} %own_ref.3), slice={[0:1024], [0:256]} | slice | bytes 1048576 | tf_op jit(solution)/shard_map/slice | solution.py:375
  32.6 5.6 %collective-permute-done.11.refs_6_ = bf16[512,256]{1,0:T(8,128)(2,1)S(1)} collective-permute-done((bf16[512,256]{1,0:T(8,128)(2,1)}, bf16[512,256]{1,0:T(8,128)(2,1)S(1)}, u32[]{:S(2)}, u32[]{:S(2)}) %collective-permute-start.11) | collective-permute-done | bytes 262176 | tf_op jit(solution)/shard_map/ppermute | solution.py:362
  38.1 1.5 %collective-permute-start.8 = (bf16[1024,256]{1,0:T(8,128)(2,1)}, bf16[1024,256]{1,0:T(8,128)(2,1)}, u32[]{:S(2)}, u32[]{:S(2)}) collective-permute-start(bf16[1024,256]{1,0:T(8,128)(2,1)} %slice.11), channel_id=1, source_target_pairs={{4,6},{7,5},{9,11},{10,8},{20,22},{23,21},{25,27},{26,24}} | collective-permute-start | bytes 1572872 | tf_op jit(solution)/shard_map/ppermute | solution.py:362
  39.6 3.9 %collective-permute-start.7 = (bf16[1024,256]{1,0:T(8,128)(2,1)}, bf16[1024,256]{1,0:T(8,128)(2,1)}, u32[]{:S(2)}, u32[]{:S(2)}) collective-permute-start(bf16[1024,256]{1,0:T(8,128)(2,1)} %collective-permute-done.6.refs_5_), channel_id=1, source_target_pairs={{3,1},{6,10},{7,3},{10,14},{11,7},{14,12},{13,15},{8,4},{9,13},{4,... | collective-permute-start | bytes 1572872 | tf_op jit(solution)/shard_map/ppermute | solution.py:362
  43.5 0.1 collective-permute-start.10
  43.6 2.9 %collective-permute-start.12 = (bf16[512,256]{1,0:T(8,128)(2,1)S(1)}, bf16[512,256]{1,0:T(8,128)(2,1)S(1)}, u32[]{:S(2)}, u32[]{:S(2)}) collective-permute-start(bf16[512,256]{1,0:T(8,128)(2,1)S(1)} %collective-permute-done.11.refs_6_), channel_id=1, source_target_pairs={{6,2},{1,3},{10,6},{3,7},{14,10},{7,11},{12,14},{11,15},{8,12},{15... | collective-permute-start | bytes 786440 | tf_op jit(solution)/shard_map/ppermute | solution.py:362
  46.4 0.7 dynamic-slice_bitcast_fusion.order_ref
  47.1 1.2 copy-done
  48.4 0.9 copy-done.1
  49.3 2.6 %step.8 = (f32[320,256]{1,0:T(8,128)S(1)}, f32[320,256]{1,0:T(8,128)S(1)}) custom-call(s32[9]{0:T(128)S(1)} %dynamic-slice_bitcast_fusion.order_ref, bf16[160,8192]{1,0:T(8,128)(2,1)} %refs_4_.3, bf16[160,8192]{1,0:T(8,128)(2,1)} %copy-done.4, bf16[160,32768]{1,0:T(8,128)(2,1)} %refs_0_.17, ...), custom_call_target="tpu_custom_call" | custom-call | flops 419430400 | bytes 3604480 | tf_op jit(solution)/shard_map/step/pallas_call | solution.py:59
  51.9 2.8 %collective-permute-start.5 = (bf16[1024,256]{1,0:T(8,128)(2,1)}, bf16[1024,256]{1,0:T(8,128)(2,1)S(1)}, u32[]{:S(2)}, u32[]{:S(2)}) collective-permute-start(bf16[1024,256]{1,0:T(8,128)(2,1)} %collective-permute-done.2.refs_4_), channel_id=1, source_target_pairs={{2,6},{3,1},{6,10},{7,3},{10,14},{11,7},{14,12},{15,11},{12,8},{13... | collective-permute-start | bytes 1572872 | tf_op jit(solution)/shard_map/ppermute | solution.py:362
  54.7 0.7 collective-permute-start.15
  55.4 3.8 %collective-permute-done.10.refs_6_ = bf16[512,256]{1,0:T(8,128)(2,1)S(1)} collective-permute-done((bf16[512,256]{1,0:T(8,128)(2,1)S(1)}, bf16[512,256]{1,0:T(8,128)(2,1)S(1)}, u32[]{:S(2)}, u32[]{:S(2)}) %collective-permute-start.10) | collective-permute-done | bytes 262176 | tf_op jit(solution)/shard_map/ppermute | solution.py:362
  59.2 1.3 add.20.refs_5_
  60.6 1.9 %cut.1 = (bf16[320,512]{1,0:T(8,128)(2,1)S(1)}, bf16[320,512]{1,0:T(8,128)(2,1)S(1)}, bf16[320,1024]{1,0:T(8,128)(2,1)S(1)}) custom-call(s32[9]{0:T(128)S(1)} %dynamic-slice_bitcast_fusion.order_ref, bf16[160,32768]{1,0:T(8,128)(2,1)} %refs_0_.17, bf16[160,32768]{1,0:T(8,128)(2,1)} %collective-permute-done.4.refs_3_.sib_ref.refs_1_), custom_call_target="tpu_custom_call" | custom-call | bytes 2621440 | tf_op jit(solution)/shard_map/cut/pallas_call | solution.py:59
  62.5 1.9 %collective-permute-start.14 = (bf16[1024,256]{1,0:T(8,128)(2,1)S(1)}, bf16[1024,256]{1,0:T(8,128)(2,1)S(1)}, u32[]{:S(2)}, u32[]{:S(2)}) collective-permute-start(bf16[1024,256]{1,0:T(8,128)(2,1)S(1)} %add.20.refs_5_), channel_id=1, source_target_pairs={{3,1},{6,10},{7,3},{10,14},{11,7},{14,12},{13,15},{8,4},{9,13},{4,... | collective-permute-start | bytes 1572872 | tf_op jit(solution)/shard_map/ppermute | solution.py:362
  64.4 0.7 collective-permute-start.17
  65.2 2.5 %collective-permute-done.18.refs_6_ = bf16[512,256]{1,0:T(8,128)(2,1)S(1)} collective-permute-done((bf16[512,256]{1,0:T(8,128)(2,1)S(1)}, bf16[512,256]{1,0:T(8,128)(2,1)S(1)}, u32[]{:S(2)}, u32[]{:S(2)}) %collective-permute-start.18) | collective-permute-done | bytes 262176 | tf_op jit(solution)/shard_map/ppermute | solution.py:362
  67.6 2.2 %collective-permute-start.16 = (bf16[320,512]{1,0:T(8,128)(2,1)S(1)}, bf16[320,512]{1,0:T(8,128)(2,1)S(1)}, u32[]{:S(2)}, u32[]{:S(2)}) collective-permute-start(bf16[320,512]{1,0:T(8,128)(2,1)S(1)} %get-tuple-element.68), channel_id=1, source_target_pairs={{2,6},{3,7},{0,4},{1,5},{14,10},{15,11},{12,8},{13,9},{18,22},{19,... | collective-permute-start | bytes 983048 | tf_op jit(solution)/shard_map/ppermute | solution.py:362
  69.9 0.1 collective-permute-start.19
  70.0 2.9 %step.9 = (f32[320,256]{1,0:T(8,128)S(1)}, f32[320,256]{1,0:T(8,128)S(1)}) custom-call(s32[9]{0:T(128)S(1)} %dynamic-slice_bitcast_fusion.order_ref, bf16[160,8192]{1,0:T(8,128)(2,1)} %refs_4_.3, bf16[160,8192]{1,0:T(8,128)(2,1)} %copy-done.4, bf16[160,32768]{1,0:T(8,128)(2,1)} %refs_0_.17, ...), custom_call_target="tpu_custom_call" | custom-call | flops 419430400 | bytes 4259840 | tf_op jit(solution)/shard_map/step/pallas_call | solution.py:59
  72.9 2.9 %step.10 = (f32[320,256]{1,0:T(8,128)S(1)}, f32[320,256]{1,0:T(8,128)S(1)}) custom-call(s32[9]{0:T(128)S(1)} %dynamic-slice_bitcast_fusion.order_ref, bf16[160,8192]{1,0:T(8,128)(2,1)} %refs_4_.3, bf16[160,8192]{1,0:T(8,128)(2,1)} %copy-done.4, bf16[160,32768]{1,0:T(8,128)(2,1)} %refs_0_.17, ...), custom_call_target="tpu_custom_call" | custom-call | flops 419430400 | bytes 4259840 | tf_op jit(solution)/shard_map/step/pallas_call | solution.py:59
  75.8 2.5 %collective-permute-start.13 = (bf16[1024,256]{1,0:T(8,128)(2,1)S(1)}, bf16[1024,256]{1,0:T(8,128)(2,1)S(1)}, u32[]{:S(2)}, u32[]{:S(2)}) collective-permute-start(bf16[1024,256]{1,0:T(8,128)(2,1)S(1)} %collective-permute-done.5.refs_4_), channel_id=1, source_target_pairs={{2,6},{3,1},{6,10},{7,3},{10,14},{11,7},{14,12},{15,11},{12,8},{13... | collective-permute-start | bytes 1572872 | tf_op jit(solution)/shard_map/ppermute | solution.py:362
  78.3 2.0 %collective-permute-start.20 = (bf16[512,256]{1,0:T(8,128)(2,1)S(1)}, bf16[512,256]{1,0:T(8,128)(2,1)S(1)}, u32[]{:S(2)}, u32[]{:S(2)}) collective-permute-start(bf16[512,256]{1,0:T(8,128)(2,1)S(1)} %collective-permute-done.18.refs_6_), channel_id=1, source_target_pairs={{2,6},{3,1},{6,10},{7,3},{10,14},{11,7},{14,12},{15,11},{12,8},{13... | collective-permute-start | bytes 786440 | tf_op jit(solution)/shard_map/ppermute | solution.py:362
  80.3 0.2 add.21.refs_5_
  80.5 0.7 collective-permute-start.23
  81.2 2.3 %collective-permute-start.22 = (bf16[1024,256]{1,0:T(8,128)(2,1)S(1)}, bf16[1024,256]{1,0:T(8,128)(2,1)S(1)}, u32[]{:S(2)}, u32[]{:S(2)}) collective-permute-start(bf16[1024,256]{1,0:T(8,128)(2,1)S(1)} %add.21.refs_5_), channel_id=1, source_target_pairs={{3,1},{6,10},{7,3},{10,14},{11,7},{14,12},{13,15},{8,4},{9,13},{4,... | collective-permute-start | bytes 1572872 | tf_op jit(solution)/shard_map/ppermute | solution.py:362
  83.5 0.7 collective-permute-start.25
  84.2 3.6 %collective-permute-done.20.refs_6_ = bf16[512,256]{1,0:T(8,128)(2,1)S(1)} collective-permute-done((bf16[512,256]{1,0:T(8,128)(2,1)S(1)}, bf16[512,256]{1,0:T(8,128)(2,1)S(1)}, u32[]{:S(2)}, u32[]{:S(2)}) %collective-permute-start.20) | collective-permute-done | bytes 262176 | tf_op jit(solution)/shard_map/ppermute | solution.py:362
  87.8 3.8 %collective-permute-start.24 = (bf16[320,512]{1,0:T(8,128)(2,1)S(1)}, bf16[320,512]{1,0:T(8,128)(2,1)S(1)}, u32[]{:S(2)}, u32[]{:S(2)}) collective-permute-start(bf16[320,512]{1,0:T(8,128)(2,1)S(1)} %get-tuple-element.79), channel_id=1, source_target_pairs={{2,6},{3,7},{0,4},{1,5},{14,10},{15,11},{12,8},{13,9},{18,22},{19,... | collective-permute-start | bytes 983048 | tf_op jit(solution)/shard_map/ppermute | solution.py:362
  91.6 2.9 %step.11 = (f32[320,256]{1,0:T(8,128)S(1)}, f32[320,256]{1,0:T(8,128)S(1)}) custom-call(s32[9]{0:T(128)S(1)} %dynamic-slice_bitcast_fusion.order_ref, bf16[160,8192]{1,0:T(8,128)(2,1)} %refs_4_.3, bf16[160,8192]{1,0:T(8,128)(2,1)} %copy-done.4, bf16[160,32768]{1,0:T(8,128)(2,1)} %refs_0_.17, ...), custom_call_target="tpu_custom_call" | custom-call | flops 419430400 | bytes 4259840 | tf_op jit(solution)/shard_map/step/pallas_call | solution.py:59
  94.5 0.0 copy-start.3
  94.6 2.9 %step.12 = (f32[320,256]{1,0:T(8,128)S(1)}, f32[320,256]{1,0:T(8,128)S(1)}) custom-call(s32[9]{0:T(128)S(1)} %dynamic-slice_bitcast_fusion.order_ref, bf16[160,8192]{1,0:T(8,128)(2,1)} %refs_4_.3, bf16[160,8192]{1,0:T(8,128)(2,1)} %copy-done.4, bf16[160,32768]{1,0:T(8,128)(2,1)} %refs_0_.17, ...), custom_call_target="tpu_custom_call" | custom-call | flops 419430400 | bytes 4259840 | tf_op jit(solution)/shard_map/step/pallas_call | solution.py:59
  97.5 3.4 %collective-permute-start.21 = (bf16[1024,256]{1,0:T(8,128)(2,1)S(1)}, bf16[1024,256]{1,0:T(8,128)(2,1)S(1)}, u32[]{:S(2)}, u32[]{:S(2)}) collective-permute-start(bf16[1024,256]{1,0:T(8,128)(2,1)S(1)} %collective-permute-done.13.refs_2_), channel_id=1, source_target_pairs={{2,6},{3,1},{6,10},{7,3},{10,14},{11,7},{14,12},{15,11},{12,8},{13... | collective-permute-start | bytes 1572872 | tf_op jit(solution)/shard_map/ppermute | solution.py:362
  100.9 2.3 %turned.1.own_ref = f32[328,256]{1,0:T(8,128)S(1)} custom-call(s32[9]{0:T(128)S(1)} %dynamic-slice_bitcast_fusion.order_ref, bf16[160,8192]{1,0:T(8,128)(2,1)} %refs_4_.3, bf16[160,8192]{1,0:T(8,128)(2,1)} %copy-done.4, bf16[160,8192]{1,0:T(8,128)(2,1)} %refs_4_.3, bf16[160,8192]{1,0:T(8,128)(2,1)} %copy-done.4, bf16[160,8192]{1,0:T(8,128)(2,1)} %refs_4_.3, ...), custom_call_target="tpu_custom_call" | custom-call | flops 251658240 | bytes 2433024 | tf_op jit(solution)/shard_map/turned/pallas_call | solution.py:59
  103.2 0.2 add.22.refs_3_
  103.4 0.1 collective-permute-start.26
  103.5 0.7 collective-permute-start.29
  104.2 0.7 collective-permute-start.30
  104.9 1.9 %collective-permute-start.28 = (bf16[1024,256]{1,0:T(8,128)(2,1)S(1)}, bf16[1024,256]{1,0:T(8,128)(2,1)S(1)}, u32[]{:S(2)}, u32[]{:S(2)}) collective-permute-start(bf16[1024,256]{1,0:T(8,128)(2,1)S(1)} %add.22.refs_3_), channel_id=1, source_target_pairs={{3,1},{6,10},{7,3},{10,14},{11,7},{14,12},{13,15},{8,4},{9,13},{4,... | collective-permute-start | bytes 1572872 | tf_op jit(solution)/shard_map/ppermute | solution.py:362
  106.8 2.1 %job.1.job_ref = f32[320,256]{1,0:T(8,128)S(1)} custom-call(s32[9]{0:T(128)S(1)} %dynamic-slice_bitcast_fusion.order_ref, bf16[320,512]{1,0:T(8,128)(2,1)S(1)} %collective-permute-done.16.first_ref, bf16[320,512]{1,0:T(8,128)(2,1)S(1)} %collective-permute-done.24.second_ref, bf16[2048,256]{1,0:T(8,128)(2,1)} %own_ref.3, ...), custom_call_target="tpu_custom_call" | custom-call | flops 167772160 | bytes 2555904 | tf_op jit(solution)/shard_map/job/pallas_call | solution.py:59
  109.0 2.4 %step.13.refs_3_ = f32[320,256]{1,0:T(8,128)S(1)} custom-call(s32[9]{0:T(128)S(1)} %dynamic-slice_bitcast_fusion.order_ref, bf16[160,32768]{1,0:T(8,128)(2,1)} %refs_0_.17, bf16[160,32768]{1,0:T(8,128)(2,1)} %collective-permute-done.4.refs_3_.sib_ref.refs_1_, bf16[1024,256]{1,0:T(8,128)(2,1)S(1)} %collective-permute-done.13.refs_2_, ...), custom_call_target="tpu_custom_call" | custom-call | flops 335544320 | bytes 3014656 | tf_op jit(solution)/shard_map/step/pallas_call | solution.py:59
  111.3 0.6 masked.1.inn_ref
  112.0 0.1 collective-permute-start.27
  112.1 3.9 %collective-permute-start.31 = (f32[328,256]{1,0:T(8,128)S(1)}, f32[328,256]{1,0:T(8,128)S(1)}, u32[]{:S(2)}, u32[]{:S(2)}) collective-permute-start(f32[328,256]{1,0:T(8,128)S(1)} %masked.1.inn_ref), channel_id=1, source_target_pairs={{2,6},{3,7},{0,4},{1,5},{14,10},{15,11},{12,8},{13,9},{18,22},{19,... | collective-permute-start | bytes 1007624 | tf_op jit(solution)/shard_map/ppermute | solution.py:362
  116.0 0.1 add.24.refs_2_
  116.2 0.1 add.23.refs_3_
  116.3 2.2 %step.14.refs_4_ = f32[320,256]{1,0:T(8,128)S(1)} custom-call(s32[9]{0:T(128)S(1)} %dynamic-slice_bitcast_fusion.order_ref, bf16[160,32768]{1,0:T(8,128)(2,1)} %refs_0_.17, bf16[160,32768]{1,0:T(8,128)(2,1)} %collective-permute-done.4.refs_3_.sib_ref.refs_1_, bf16[1024,256]{1,0:T(8,128)(2,1)S(1)} %add.24.refs_2_, f32[320,256]{1,0:T(8,128)S(1)} %step.13.refs_3_), custom_call_target="tpu_custom_call" | custom-call | flops 167772160 | bytes 2490368 | tf_op jit(solution)/shard_map/step/pallas_call | solution.py:59
  118.5 2.4 %step.15.total_ref = f32[320,256]{1,0:T(8,128)S(1)} custom-call(s32[9]{0:T(128)S(1)} %dynamic-slice_bitcast_fusion.order_ref, bf16[160,32768]{1,0:T(8,128)(2,1)} %refs_0_.17, bf16[160,32768]{1,0:T(8,128)(2,1)} %collective-permute-done.4.refs_3_.sib_ref.refs_1_, bf16[1024,256]{1,0:T(8,128)(2,1)S(1)} %collective-permute-done.21.refs_2_, ...), custom_call_target="tpu_custom_call" | custom-call | flops 335544320 | bytes 3014656 | tf_op jit(solution)/shard_map/step/pallas_call | solution.py:59
  120.9 3.4 %collective-permute-done.31.job_inn_ref = f32[328,256]{1,0:T(8,128)S(1)} collective-permute-done((f32[328,256]{1,0:T(8,128)S(1)}, f32[328,256]{1,0:T(8,128)S(1)}, u32[]{:S(2)}, u32[]{:S(2)}) %collective-permute-start.31) | collective-permute-done | bytes 335904 | tf_op jit(solution)/shard_map/ppermute | solution.py:362
  124.3 0.7 finish.1
  125.0 14.5 %all_to_all.5 = f32[16,2,8]{2,1,0:T(2,128)S(1)} all-to-all(f32[16,2,8]{2,1,0:T(2,128)S(1)} %bitcast.3), channel_id=1, replica_groups=mesh['groups'=2,'dp'=16] {'dp'}, dimensions={0} | all-to-all | bytes 2048 | tf_op jit(solution)/shard_map/all_to_all | solution.py:470
  139.5 0.6 reduce_sum.9
  (49 shorter events, 0.1 us)
Async XLA Ops:
  0.0 43.6 %collective-permute-start.4 = (bf16[160,32768]{1,0:T(8,128)(2,1)}, bf16[160,32768]{1,0:T(8,128)(2,1)}, u32[]{:S(2)}, u32[]{:S(2)}) collective-permute-start(bf16[160,32768]{1,0:T(8,128)(2,1)} %refs_0_.17), channel_id=1, source_target_pairs={{0,1},{1,0},{2,3},{3,2},{4,5},{5,4},{6,7},{7,6},{8,9},{9,8},{10,11... | collective-permute-start | bytes 31457288 | tf_op jit(solution)/shard_map/ppermute | solution.py:362
  0.5 43.0 %collective-permute-start.3 = (bf16[160,8192]{1,0:T(8,128)(2,1)}, bf16[160,8192]{1,0:T(8,128)(2,1)S(1)}, u32[]{:S(2)}, u32[]{:S(2)}) collective-permute-start(bf16[160,8192]{1,0:T(8,128)(2,1)} %refs_4_.3), channel_id=1, source_target_pairs={{0,1},{1,0},{2,3},{3,2},{4,5},{5,4},{6,7},{7,6},{8,9},{9,8},{10,11... | collective-permute-start | bytes 7864328 | tf_op jit(solution)/shard_map/ppermute | solution.py:362
  0.5 16.0 %collective-permute-start = (bf16[2048,256]{1,0:T(8,128)(2,1)}, bf16[2048,256]{1,0:T(8,128)(2,1)S(1)}, u32[]{:S(2)}, u32[]{:S(2)}) collective-permute-start(bf16[2048,256]{1,0:T(8,128)(2,1)} %own_ref.3), channel_id=1, source_target_pairs={{2,6},{3,1},{6,10},{7,3},{10,14},{11,7},{14,12},{15,11},{12,8},{13... | collective-permute-start | bytes 3145736 | tf_op jit(solution)/shard_map/ppermute | solution.py:362
  16.6 21.5 %copy-start.9 = (bf16[1024,256]{1,0:T(8,128)(2,1)}, bf16[1024,256]{1,0:T(8,128)(2,1)S(1)}, u32[]{:S(2)}) copy-start(bf16[1024,256]{1,0:T(8,128)(2,1)S(1)} %get-tuple-element.95.refs_5_) | copy-start | bytes 1572868
  16.6 23.0 %copy-start.11 = (bf16[1024,256]{1,0:T(8,128)(2,1)}, bf16[1024,256]{1,0:T(8,128)(2,1)S(1)}, u32[]{:S(2)}) copy-start(bf16[1024,256]{1,0:T(8,128)(2,1)S(1)} %get-tuple-element.96.refs_4_) | copy-start | bytes 1572868
  16.6 14.1 %collective-permute-start.1 = (bf16[1024,256]{1,0:T(8,128)(2,1)S(1)}, bf16[1024,256]{1,0:T(8,128)(2,1)}, u32[]{:S(2)}, u32[]{:S(2)}) collective-permute-start(bf16[1024,256]{1,0:T(8,128)(2,1)S(1)} %get-tuple-element.96.refs_4_), channel_id=1, source_target_pairs={{2,6},{3,1},{6,10},{7,3},{10,14},{11,7},{14,12},{15,11},{12,8},{13... | collective-permute-start | bytes 1572872 | tf_op jit(solution)/shard_map/ppermute | solution.py:362
  18.6 10.0 %collective-permute-start.9 = (bf16[512,256]{1,0:T(8,128)(2,1)}, bf16[512,256]{1,0:T(8,128)(2,1)S(1)}, u32[]{:S(2)}, u32[]{:S(2)}) collective-permute-start(bf16[512,256]{1,0:T(8,128)(2,1)} %refs_5_.1), channel_id=1, source_target_pairs={{2,6},{3,1},{6,10},{7,3},{10,14},{11,7},{14,12},{15,11},{12,8},{13... | collective-permute-start | bytes 786440 | tf_op jit(solution)/shard_map/ppermute | solution.py:362
  20.2 19.4 %collective-permute-start.6 = (bf16[1024,256]{1,0:T(8,128)(2,1)S(1)}, bf16[1024,256]{1,0:T(8,128)(2,1)}, u32[]{:S(2)}, u32[]{:S(2)}) collective-permute-start(bf16[1024,256]{1,0:T(8,128)(2,1)S(1)} %get-tuple-element.95.refs_5_), channel_id=1, source_target_pairs={{2,6},{3,1},{6,10},{7,3},{10,14},{11,7},{14,12},{15,11},{12,8},{13... | collective-permute-start | bytes 1572872 | tf_op jit(solution)/shard_map/ppermute | solution.py:362
  28.7 9.5 %collective-permute-start.11 = (bf16[512,256]{1,0:T(8,128)(2,1)}, bf16[512,256]{1,0:T(8,128)(2,1)S(1)}, u32[]{:S(2)}, u32[]{:S(2)}) collective-permute-start(bf16[512,256]{1,0:T(8,128)(2,1)} %refs_5_.1), channel_id=1, source_target_pairs={{6,2},{1,3},{10,6},{3,7},{14,10},{7,11},{12,14},{11,15},{8,12},{15... | collective-permute-start | bytes 786440 | tf_op jit(solution)/shard_map/ppermute | solution.py:362
  30.7 21.2 %collective-permute-start.2 = (bf16[1024,256]{1,0:T(8,128)(2,1)}, bf16[1024,256]{1,0:T(8,128)(2,1)}, u32[]{:S(2)}, u32[]{:S(2)}) collective-permute-start(bf16[1024,256]{1,0:T(8,128)(2,1)} %collective-permute-done.1.refs_4_), channel_id=1, source_target_pairs={{2,6},{3,1},{6,10},{7,3},{10,14},{11,7},{14,12},{15,11},{12,8},{13... | collective-permute-start | bytes 1572872 | tf_op jit(solution)/shard_map/ppermute | solution.py:362
  38.1 16.6 %collective-permute-start.8 = (bf16[1024,256]{1,0:T(8,128)(2,1)}, bf16[1024,256]{1,0:T(8,128)(2,1)}, u32[]{:S(2)}, u32[]{:S(2)}) collective-permute-start(bf16[1024,256]{1,0:T(8,128)(2,1)} %slice.11), channel_id=1, source_target_pairs={{4,6},{7,5},{9,11},{10,8},{20,22},{23,21},{25,27},{26,24}} | collective-permute-start | bytes 1572872 | tf_op jit(solution)/shard_map/ppermute | solution.py:362
  39.6 19.6 %collective-permute-start.7 = (bf16[1024,256]{1,0:T(8,128)(2,1)}, bf16[1024,256]{1,0:T(8,128)(2,1)}, u32[]{:S(2)}, u32[]{:S(2)}) collective-permute-start(bf16[1024,256]{1,0:T(8,128)(2,1)} %collective-permute-done.6.refs_5_), channel_id=1, source_target_pairs={{3,1},{6,10},{7,3},{10,14},{11,7},{14,12},{13,15},{8,4},{9,13},{4,... | collective-permute-start | bytes 1572872 | tf_op jit(solution)/shard_map/ppermute | solution.py:362
  43.5 3.7 %copy-start.4 = (bf16[160,8192]{1,0:T(8,128)(2,1)}, bf16[160,8192]{1,0:T(8,128)(2,1)S(1)}, u32[]{:S(2)}) copy-start(bf16[160,8192]{1,0:T(8,128)(2,1)S(1)} %collective-permute-done.3.refs_1_.refs_3_.refs_5_) | copy-start | bytes 7864324
  43.5 15.7 %collective-permute-start.10 = (bf16[512,256]{1,0:T(8,128)(2,1)S(1)}, bf16[512,256]{1,0:T(8,128)(2,1)S(1)}, u32[]{:S(2)}, u32[]{:S(2)}) collective-permute-start(bf16[512,256]{1,0:T(8,128)(2,1)S(1)} %collective-permute-done.9.refs_6_), channel_id=1, source_target_pairs={{2,6},{3,1},{6,10},{7,3},{10,14},{11,7},{14,12},{15,11},{12,8},{13... | collective-permute-start | bytes 786440 | tf_op jit(solution)/shard_map/ppermute | solution.py:362
  43.6 18.9 %collective-permute-start.12 = (bf16[512,256]{1,0:T(8,128)(2,1)S(1)}, bf16[512,256]{1,0:T(8,128)(2,1)S(1)}, u32[]{:S(2)}, u32[]{:S(2)}) collective-permute-start(bf16[512,256]{1,0:T(8,128)(2,1)S(1)} %collective-permute-done.11.refs_6_), channel_id=1, source_target_pairs={{6,2},{1,3},{10,6},{3,7},{14,10},{7,11},{12,14},{11,15},{8,12},{15... | collective-permute-start | bytes 786440 | tf_op jit(solution)/shard_map/ppermute | solution.py:362
  47.1 1.2 copy-start
  48.4 0.9 copy-start.1
  49.3 5.4 %copy-start.10 = (bf16[1024,256]{1,0:T(8,128)(2,1)S(1)}, bf16[1024,256]{1,0:T(8,128)(2,1)}, u32[]{:S(2)}) copy-start(bf16[1024,256]{1,0:T(8,128)(2,1)} %copy-done.9) | copy-start | bytes 1572868
  51.9 18.0 %collective-permute-start.5 = (bf16[1024,256]{1,0:T(8,128)(2,1)}, bf16[1024,256]{1,0:T(8,128)(2,1)S(1)}, u32[]{:S(2)}, u32[]{:S(2)}) collective-permute-start(bf16[1024,256]{1,0:T(8,128)(2,1)} %collective-permute-done.2.refs_4_), channel_id=1, source_target_pairs={{2,6},{3,1},{6,10},{7,3},{10,14},{11,7},{14,12},{15,11},{12,8},{13... | collective-permute-start | bytes 1572872 | tf_op jit(solution)/shard_map/ppermute | solution.py:362
  54.7 21.0 %collective-permute-start.15 = (bf16[1024,256]{1,0:T(8,128)(2,1)S(1)}, bf16[1024,256]{1,0:T(8,128)(2,1)S(1)}, u32[]{:S(2)}, u32[]{:S(2)}) collective-permute-start(bf16[1024,256]{1,0:T(8,128)(2,1)S(1)} %copy-done.10), channel_id=1, source_target_pairs={{4,6},{7,5},{9,11},{10,8},{20,22},{23,21},{25,27},{26,24}} | collective-permute-start | bytes 1572872 | tf_op jit(solution)/shard_map/ppermute | solution.py:362
  59.2 8.4 %collective-permute-start.18 = (bf16[512,256]{1,0:T(8,128)(2,1)S(1)}, bf16[512,256]{1,0:T(8,128)(2,1)S(1)}, u32[]{:S(2)}, u32[]{:S(2)}) collective-permute-start(bf16[512,256]{1,0:T(8,128)(2,1)S(1)} %collective-permute-done.10.refs_6_), channel_id=1, source_target_pairs={{2,6},{3,1},{6,10},{7,3},{10,14},{11,7},{14,12},{15,11},{12,8},{13... | collective-permute-start | bytes 786440 | tf_op jit(solution)/shard_map/ppermute | solution.py:362
  60.6 1.9 %copy-start.5 = (bf16[1024,256]{1,0:T(8,128)(2,1)}, bf16[1024,256]{1,0:T(8,128)(2,1)S(1)}, u32[]{:S(2)}) copy-start(bf16[1024,256]{1,0:T(8,128)(2,1)S(1)} %add.20.refs_5_) | copy-start | bytes 1572868
  62.5 15.8 %collective-permute-start.14 = (bf16[1024,256]{1,0:T(8,128)(2,1)S(1)}, bf16[1024,256]{1,0:T(8,128)(2,1)S(1)}, u32[]{:S(2)}, u32[]{:S(2)}) collective-permute-start(bf16[1024,256]{1,0:T(8,128)(2,1)S(1)} %add.20.refs_5_), channel_id=1, source_target_pairs={{3,1},{6,10},{7,3},{10,14},{11,7},{14,12},{13,15},{8,4},{9,13},{4,... | collective-permute-start | bytes 1572872 | tf_op jit(solution)/shard_map/ppermute | solution.py:362
  64.4 16.8 %collective-permute-start.17 = (bf16[1024,256]{1,0:T(8,128)(2,1)S(1)}, bf16[1024,256]{1,0:T(8,128)(2,1)S(1)}, u32[]{:S(2)}, u32[]{:S(2)}) collective-permute-start(bf16[1024,256]{1,0:T(8,128)(2,1)S(1)} %copy-done.10), channel_id=1, source_target_pairs={{5,7},{6,4},{8,10},{11,9},{21,23},{22,20},{24,26},{27,25}} | collective-permute-start | bytes 1572872 | tf_op jit(solution)/shard_map/ppermute | solution.py:362
  67.6 13.6 %collective-permute-start.16 = (bf16[320,512]{1,0:T(8,128)(2,1)S(1)}, bf16[320,512]{1,0:T(8,128)(2,1)S(1)}, u32[]{:S(2)}, u32[]{:S(2)}) collective-permute-start(bf16[320,512]{1,0:T(8,128)(2,1)S(1)} %get-tuple-element.68), channel_id=1, source_target_pairs={{2,6},{3,7},{0,4},{1,5},{14,10},{15,11},{12,8},{13,9},{18,22},{19,... | collective-permute-start | bytes 983048 | tf_op jit(solution)/shard_map/ppermute | solution.py:362
  69.9 5.9 %copy-start.12 = (bf16[1024,256]{1,0:T(8,128)(2,1)}, bf16[1024,256]{1,0:T(8,128)(2,1)S(1)}, u32[]{:S(2)}) copy-start(bf16[1024,256]{1,0:T(8,128)(2,1)S(1)} %collective-permute-done.5.refs_4_) | copy-start | bytes 1572868
  69.9 10.6 %collective-permute-start.19 = (bf16[512,256]{1,0:T(8,128)(2,1)S(1)}, bf16[512,256]{1,0:T(8,128)(2,1)S(1)}, u32[]{:S(2)}, u32[]{:S(2)}) collective-permute-start(bf16[512,256]{1,0:T(8,128)(2,1)S(1)} %collective-permute-done.12.refs_7_), channel_id=1, source_target_pairs={{6,2},{1,3},{10,6},{3,7},{14,10},{7,11},{12,14},{11,15},{8,12},{15... | collective-permute-start | bytes 786440 | tf_op jit(solution)/shard_map/ppermute | solution.py:362
  75.8 21.7 %collective-permute-start.13 = (bf16[1024,256]{1,0:T(8,128)(2,1)S(1)}, bf16[1024,256]{1,0:T(8,128)(2,1)S(1)}, u32[]{:S(2)}, u32[]{:S(2)}) collective-permute-start(bf16[1024,256]{1,0:T(8,128)(2,1)S(1)} %collective-permute-done.5.refs_4_), channel_id=1, source_target_pairs={{2,6},{3,1},{6,10},{7,3},{10,14},{11,7},{14,12},{15,11},{12,8},{13... | collective-permute-start | bytes 1572872 | tf_op jit(solution)/shard_map/ppermute | solution.py:362
  78.3 9.5 %collective-permute-start.20 = (bf16[512,256]{1,0:T(8,128)(2,1)S(1)}, bf16[512,256]{1,0:T(8,128)(2,1)S(1)}, u32[]{:S(2)}, u32[]{:S(2)}) collective-permute-start(bf16[512,256]{1,0:T(8,128)(2,1)S(1)} %collective-permute-done.18.refs_6_), channel_id=1, source_target_pairs={{2,6},{3,1},{6,10},{7,3},{10,14},{11,7},{14,12},{15,11},{12,8},{13... | collective-permute-start | bytes 786440 | tf_op jit(solution)/shard_map/ppermute | solution.py:362
  80.5 14.0 %copy-start.7 = (bf16[1024,256]{1,0:T(8,128)(2,1)}, bf16[1024,256]{1,0:T(8,128)(2,1)S(1)}, u32[]{:S(2)}) copy-start(bf16[1024,256]{1,0:T(8,128)(2,1)S(1)} %add.21.refs_5_) | copy-start | bytes 1572868
  80.5 22.7 %collective-permute-start.23 = (bf16[1024,256]{1,0:T(8,128)(2,1)}, bf16[1024,256]{1,0:T(8,128)(2,1)S(1)}, u32[]{:S(2)}, u32[]{:S(2)}) collective-permute-start(bf16[1024,256]{1,0:T(8,128)(2,1)} %collective-permute-done.6.refs_5_), channel_id=1, source_target_pairs={{4,6},{7,5},{9,11},{10,8},{20,22},{23,21},{25,27},{26,24}} | collective-permute-start | bytes 1572872 | tf_op jit(solution)/shard_map/ppermute | solution.py:362
  81.2 22.0 %collective-permute-start.22 = (bf16[1024,256]{1,0:T(8,128)(2,1)S(1)}, bf16[1024,256]{1,0:T(8,128)(2,1)S(1)}, u32[]{:S(2)}, u32[]{:S(2)}) collective-permute-start(bf16[1024,256]{1,0:T(8,128)(2,1)S(1)} %add.21.refs_5_), channel_id=1, source_target_pairs={{3,1},{6,10},{7,3},{10,14},{11,7},{14,12},{13,15},{8,4},{9,13},{4,... | collective-permute-start | bytes 1572872 | tf_op jit(solution)/shard_map/ppermute | solution.py:362
  83.5 19.8 %collective-permute-start.25 = (bf16[1024,256]{1,0:T(8,128)(2,1)}, bf16[1024,256]{1,0:T(8,128)(2,1)S(1)}, u32[]{:S(2)}, u32[]{:S(2)}) collective-permute-start(bf16[1024,256]{1,0:T(8,128)(2,1)} %collective-permute-done.6.refs_5_), channel_id=1, source_target_pairs={{5,7},{6,4},{8,10},{11,9},{21,23},{22,20},{24,26},{27,25}} | collective-permute-start | bytes 1572872 | tf_op jit(solution)/shard_map/ppermute | solution.py:362
  87.8 15.5 %collective-permute-start.24 = (bf16[320,512]{1,0:T(8,128)(2,1)S(1)}, bf16[320,512]{1,0:T(8,128)(2,1)S(1)}, u32[]{:S(2)}, u32[]{:S(2)}) collective-permute-start(bf16[320,512]{1,0:T(8,128)(2,1)S(1)} %get-tuple-element.79), channel_id=1, source_target_pairs={{2,6},{3,7},{0,4},{1,5},{14,10},{15,11},{12,8},{13,9},{18,22},{19,... | collective-permute-start | bytes 983048 | tf_op jit(solution)/shard_map/ppermute | solution.py:362
  94.5 6.4 %copy-start.2 = (s32[2]{0:T(128)S(1)}, s32[2]{0:T(128)}, u32[]{:S(2)}) copy-start(s32[2]{0:T(128)} %refs_10_.1) | copy-start | bytes 28
  94.5 6.4 %copy-start.3 = (s32[2]{0:T(128)S(1)}, s32[2]{0:T(128)}, u32[]{:S(2)}) copy-start(s32[2]{0:T(128)} %refs_11_.1) | copy-start | bytes 28
  97.5 6.0 %copy-start.6 = (bf16[1024,256]{1,0:T(8,128)(2,1)S(1)}, bf16[1024,256]{1,0:T(8,128)(2,1)}, u32[]{:S(2)}) copy-start(bf16[1024,256]{1,0:T(8,128)(2,1)} %copy-done.5) | copy-start | bytes 1572868
  97.5 6.7 %copy-start.8 = (bf16[1024,256]{1,0:T(8,128)(2,1)S(1)}, bf16[1024,256]{1,0:T(8,128)(2,1)}, u32[]{:S(2)}) copy-start(bf16[1024,256]{1,0:T(8,128)(2,1)} %copy-done.7) | copy-start | bytes 1572868
  97.5 14.5 %collective-permute-start.21 = (bf16[1024,256]{1,0:T(8,128)(2,1)S(1)}, bf16[1024,256]{1,0:T(8,128)(2,1)S(1)}, u32[]{:S(2)}, u32[]{:S(2)}) collective-permute-start(bf16[1024,256]{1,0:T(8,128)(2,1)S(1)} %collective-permute-done.13.refs_2_), channel_id=1, source_target_pairs={{2,6},{3,1},{6,10},{7,3},{10,14},{11,7},{14,12},{15,11},{12,8},{13... | collective-permute-start | bytes 1572872 | tf_op jit(solution)/shard_map/ppermute | solution.py:362
  103.4 7.9 %collective-permute-start.26 = (f32[328,256]{1,0:T(8,128)S(1)}, f32[328,256]{1,0:T(8,128)S(1)}, u32[]{:S(2)}, u32[]{:S(2)}) collective-permute-start(f32[328,256]{1,0:T(8,128)S(1)} %turned.1.own_ref), channel_id=1, source_target_pairs={{0,1},{1,0},{2,3},{3,2},{4,5},{5,4},{6,7},{7,6},{8,9},{9,8},{10,11... | collective-permute-start | bytes 1007624 | tf_op jit(solution)/shard_map/ppermute | solution.py:362
  103.5 12.7 %collective-permute-start.29 = (bf16[1024,256]{1,0:T(8,128)(2,1)S(1)}, bf16[1024,256]{1,0:T(8,128)(2,1)S(1)}, u32[]{:S(2)}, u32[]{:S(2)}) collective-permute-start(bf16[1024,256]{1,0:T(8,128)(2,1)S(1)} %copy-done.6), channel_id=1, source_target_pairs={{4,6},{7,5},{9,11},{10,8},{20,22},{23,21},{25,27},{26,24}} | collective-permute-start | bytes 1572872 | tf_op jit(solution)/shard_map/ppermute | solution.py:362
  104.2 11.8 %collective-permute-start.30 = (bf16[1024,256]{1,0:T(8,128)(2,1)S(1)}, bf16[1024,256]{1,0:T(8,128)(2,1)S(1)}, u32[]{:S(2)}, u32[]{:S(2)}) collective-permute-start(bf16[1024,256]{1,0:T(8,128)(2,1)S(1)} %copy-done.8), channel_id=1, source_target_pairs={{4,6},{7,5},{9,11},{10,8},{20,22},{23,21},{25,27},{26,24}} | collective-permute-start | bytes 1572872 | tf_op jit(solution)/shard_map/ppermute | solution.py:362
  104.9 11.3 %collective-permute-start.28 = (bf16[1024,256]{1,0:T(8,128)(2,1)S(1)}, bf16[1024,256]{1,0:T(8,128)(2,1)S(1)}, u32[]{:S(2)}, u32[]{:S(2)}) collective-permute-start(bf16[1024,256]{1,0:T(8,128)(2,1)S(1)} %add.22.refs_3_), channel_id=1, source_target_pairs={{3,1},{6,10},{7,3},{10,14},{11,7},{14,12},{13,15},{8,4},{9,13},{4,... | collective-permute-start | bytes 1572872 | tf_op jit(solution)/shard_map/ppermute | solution.py:362
  112.0 12.3 %collective-permute-start.27 = (bf16[1024,256]{1,0:T(8,128)(2,1)S(1)}, bf16[1024,256]{1,0:T(8,128)(2,1)S(1)}, u32[]{:S(2)}, u32[]{:S(2)}) collective-permute-start(bf16[1024,256]{1,0:T(8,128)(2,1)S(1)} %collective-permute-done.21.refs_2_), channel_id=1, source_target_pairs={{2,6},{3,1},{6,10},{7,3},{10,14},{11,7},{14,12},{15,11},{12,8},{13... | collective-permute-start | bytes 1572872 | tf_op jit(solution)/shard_map/ppermute | solution.py:362
  112.1 12.2 %collective-permute-start.31 = (f32[328,256]{1,0:T(8,128)S(1)}, f32[328,256]{1,0:T(8,128)S(1)}, u32[]{:S(2)}, u32[]{:S(2)}) collective-permute-start(f32[328,256]{1,0:T(8,128)S(1)} %masked.1.inn_ref), channel_id=1, source_target_pairs={{2,6},{3,7},{0,4},{1,5},{14,10},{15,11},{12,8},{13,9},{18,22},{19,... | collective-permute-start | bytes 1007624 | tf_op jit(solution)/shard_map/ppermute | solution.py:362

commit v14 on v12

--- a/solution.py
+++ b/solution.py
@@ -109,41 +109,76 @@
     out_ref[tokens:] = sib_ref[:, :lead]
 
 
-def score_kernel(seq_ref, len_ref, seq_sib, len_sib, window_ref, b_ref, out_ref, inn_ref, got_ref,
-                 table_ref):
-    columns = b_ref.shape[1]
-    tokens = window_ref.shape[0] // 2
+EXTRA = 8
+
+
+def turned_kernel(count, order_ref, *refs):
+    windows, blocks = refs[:2 * count], refs[2 * count:3 * count]
+    total_ref, seq_ref, len_ref, out_ref = refs[3 * count:]
+    tokens = windows[0].shape[0]
+    for k in range(2):
+        at = pl.ds(k * tokens, tokens)
+        total = total_ref[at]
+        for w in range(count):
+            total += dot(windows[2 * w + k][...], blocks[w][...])
+        out_ref[at] = total
+    held = seq_ref.shape[0]
+    lane = lax.broadcasted_iota(jnp.int32, (EXTRA, out_ref.shape[1]), 1)
+    numbers = jnp.zeros(lane.shape, F32)
+    for i in range(held):
+        numbers = jnp.where(lane == i, seq_ref[i].astype(F32), numbers)
+        numbers = jnp.where(lane == held + i, len_ref[i].astype(F32), numbers)
+    out_ref[2 * tokens:] = numbers
+
+
+def masked_kernel(order_ref, own_ref, got_ref, out_ref):
+    tokens = (own_ref.shape[0] - EXTRA) // 2
+    columns = own_ref.shape[1]
+    held = tokens // LEN
+    position = lax.broadcasted_iota(jnp.int32, (LEN, columns), 0).astype(F32)
+    for k, (mine, other) in enumerate(((own_ref, got_ref), (got_ref, own_ref))):
+        for i in range(held):
+            at, across = pl.ds(i * LEN, LEN), pl.ds(tokens + i * LEN, LEN)
+            length = mine[2 * tokens:2 * tokens + 1, held + i:held + i + 1]
+            out_ref[pl.ds(k * tokens + i * LEN, LEN)] = jnp.where(
+                position < length, mine[at] + other[across], 0.0
+            )
+    lane = lax.broadcasted_iota(jnp.int32, (EXTRA, columns), 1)
+    numbers = jnp.zeros(lane.shape, F32)
+    for k, ref in enumerate((own_ref, got_ref)):
+        for i in range(held):
+            slot = ref[2 * tokens:2 * tokens + 1, i:i + 1]
+            numbers = jnp.where(lane == k * held + i, slot, numbers)
+    out_ref[2 * tokens:] = numbers
+
+
+def score_kernel(window_ref, block_ref, total_ref, inn_ref, table_ref):
+    height, columns = total_ref.shape
     queries = columns // RANK
     column = lax.broadcasted_iota(jnp.int32, (columns, queries), 0) // RANK
     query = lax.broadcasted_iota(jnp.int32, (columns, queries), 1)
     fold = (column == query).astype(F32)
-    position = lax.broadcasted_iota(jnp.int32, (LEN, columns), 0)
-    row = lax.broadcasted_iota(jnp.int32, table_ref.shape, 0)
-    out = out_ref[...] + dot(window_ref[...], b_ref[...])
-    sums, slots = [], []
-    for k, (seq, lens) in enumerate(((seq_ref, len_ref), (seq_sib, len_sib))):
-        mine, other = pl.ds(k * tokens, tokens), pl.ds((1 - k) * tokens, tokens)
-        contrib = out[k * tokens:(k + 1) * tokens] * (inn_ref[mine] + got_ref[other])
-        for i in range(tokens // LEN):
-            kept = jnp.where(position < lens[i], contrib[i * LEN:(i + 1) * LEN], 0.0)
-            sums.append(jnp.sum(kept, axis=0, keepdims=True))
-            slots.append(seq[i])
+    row = lax.broadcasted_iota(jnp.int32, table_ref.shape, 0).astype(F32)
+    contrib = (total_ref[...] + dot(window_ref[...], block_ref[...])) * inn_ref[:height]
+    count = height // LEN
+    sums = [jnp.sum(contrib[i * LEN:(i + 1) * LEN], axis=0, keepdims=True) for i in range(count)]
     scores = jnp.dot(
         jnp.concatenate(sums), fold, precision=lax.Precision.HIGHEST, preferred_element_type=F32
     ) * (1.0 / math.sqrt(RANK * LEN))
     table = jnp.zeros(table_ref.shape, F32)
-    for i, slot in enumerate(slots):
+    for i in range(count):
+        slot = inn_ref[height:height + 1, i:i + 1]
         table = jnp.where(row == slot, scores[i:i + 1], table)
     table_ref[...] = table
 
 
-def score_table(numbers, arrays, rows, queries):
-    smem, vmem = (pl.BlockSpec(memory_space=m) for m in (pltpu.SMEM, pltpu.VMEM))
+def score_table(arrays, rows, queries):
+    vmem = pl.BlockSpec(memory_space=pltpu.VMEM)
     window, block = arrays[:2]
     size = sum(x.size * x.dtype.itemsize for x in arrays)
     return pl.pallas_call(
         score_kernel,
-        in_specs=[smem] * len(numbers) + [vmem] * len(arrays),
+        in_specs=[vmem] * len(arrays),
         out_specs=vmem,
         out_shape=jax.ShapeDtypeStruct((rows, queries), F32),
         cost_estimate=pl.CostEstimate(
@@ -151,7 +186,7 @@
         ),
         compiler_params=pltpu.CompilerParams(vmem_limit_bytes=16 << 20),
         name="score",
-    )(*numbers, *arrays)
+    )(*arrays)
 
 
 def shards(acts, grads, out_factors, in_factors, seq_slot, lengths):
@@ -177,7 +212,6 @@
     tokens_of = {"out": (grads, across(grads), rows)}
     if rows_in:
         tokens_of["in"] = (acts, across(acts), rows_in)
-    slots_sib = across(jnp.stack([seq_slot, lengths]))
 
     inside = [(1, 0, rows_in, "in", 0)] if rows_in else []
     held = [[out_factors] + [in_factors] * (rows_in > 0)]
@@ -214,24 +248,29 @@
         [(x, rows, lambda i, o: (0, o[last])) for x in tokens_of["out"][:2]], [], [],
         [jax.ShapeDtypeStruct((2 * tokens, lead), grads.dtype)], 0, "window",
     )[0]
-    totals, window, slots_sib = lax.optimization_barrier((totals, window, slots_sib))
-    seq_sib, len_sib = slots_sib
+    totals, window = lax.optimization_barrier((totals, window))
     totals, summed = sum_to(last, totals, summed)
+    slots = lengths.shape[0]
+    height = (2 * tokens + EXTRA, columns)
     if rows_in:
-        totals = step(mine, tokens_of, [turned], [(0, 0, rows_in, "in", 0)], totals, last)
-        inn = totals["in"]
+        inn = call(
+            functools.partial(turned_kernel, 1), mine,
+            [(x, rows_in, lambda i, o: (0, o[last])) for x in tokens_of["in"][:2]],
+            [turned, totals["in"]], [seq_slot, lengths],
+            [jax.ShapeDtypeStruct(height, F32)], 4 * tokens * rows_in * columns, "turned",
+        )[0]
     else:
-        inn = dot(acts, every)
-        inn = jnp.concatenate([inn, jnp.zeros_like(inn)])
-    got = across(inn)
+        numbers = jnp.concatenate([seq_slot, lengths]).astype(F32)
+        inn = jnp.zeros(height, F32).at[:tokens].set(dot(acts, every))
+        inn = inn.at[2 * tokens, :2 * slots].set(numbers)
+    inn = call(
+        masked_kernel, mine, [], [inn, across(inn)], [],
+        [jax.ShapeDtypeStruct(height, F32)], 0, "masked",
+    )[0]
     totals = step(mine, tokens_of, [late], pieces[last][:1], totals, last)
 
-    slots = lengths.shape[0]
     queries = columns // RANK
-    table = score_table(
-        [seq_slot, lengths, seq_sib, len_sib], [window, early, totals["out"], inn, got],
-        slots * devices, queries,
-    )
+    table = score_table([window, early, totals["out"], inn], slots * devices, queries)
     got = lax.all_to_all(table.reshape(devices, slots, queries), "dp", 0, 0, tiled=True)
     return jnp.sum(got, axis=0)
 

time: 118 us -> 119 us (level)
  waiting for transfers between devices: 49.5 us -> 54.6 us
  starting transfers between devices: 27.7 us -> 24 us
  blocking collectives: 12.5 us -> 11.3 us
    ppermute x1, waiting for transfers between devices: 6.23 us -> 8.65 us  [shards(): turned = lax.ppermute(turned, 'dp', [(j, i) for i, j in pairs])]
    ppermute x1, starting transfers between devices: 2.02 us -> 0.12 us  [shards(): turned = lax.ppermute(turned, 'dp', [(j, i) for i, j in pairs])]
    ppermute x4 -> x3, waiting for transfers between devices: 0.01 us -> 1.63 us  [shards(): across = lambda x: lax.ppermute(x, 'dp', swap)]
    ppermute x14, starting transfers between devices: 24.4 us -> 23.1 us  [shards(): send = lambda x: lax.ppermute(x, 'dp', pairs)]
    all_to_all x1, blocking collectives: 12.5 us -> 11.3 us  [shards(): lax.all_to_all(table.reshape(devices, slots, queries), 'dp', 0, 0, tiled=...]
    pallas_call x10 -> x11, Pallas kernels: 25.3 us -> 25.9 us  [call(): pl.pallas_call(kernel, grid_spec=pltpu.PrefetchScalarGridSpec(num_scalar_...]
  transfers between devices with their start and end apart: 19 -> 18, of which waited for: 10 -> 12; matrix products, arithmetic and copies ran while one was open for 1% -> 1% of each run, Pallas kernels for 21% -> 22%
where the time goes in v14:
time: 119 us; the launch traced here: 118 us
  waiting for transfers between devices  54.6 us (46%)
  Pallas kernels  26.5 us (22%)
  starting transfers between devices  24 us (20%)
  blocking collectives  11.3 us (9%)
    ppermute x14, waiting for transfers between devices, shards(): send = lambda x: lax.ppermute(x, 'dp', pairs)  44.3 us
    pallas_call x11, Pallas kernels, call(): pl.pallas_call(kernel, grid_spec=pltpu.PrefetchScalarGridSpec(num_scalar_...  25.9 us
    ppermute x14, starting transfers between devices, shards(): send = lambda x: lax.ppermute(x, 'dp', pairs)  23.1 us
    all_to_all x1, blocking collectives, shards(): lax.all_to_all(table.reshape(devices, slots, queries), 'dp', 0, 0, tiled=...  11.3 us
    ppermute x1, waiting for transfers between devices, shards(): turned = lax.ppermute(turned, 'dp', [(j, i) for i, j in pairs])  8.65 us
  transfers between devices with their start and end apart: 18, of which 12 were waited for; matrix products, arithmetic and copies ran while one was open for 1% of the time, Pallas kernels for 22%

profile of v14, /device:TPU:0, one launch (start us, length us, event | category | flops | bytes accessed | tf_op | source)
XLA Modules:
  0.0 118.0 jit_solution(16698795703705056703)
XLA Ops:
  0.0 0.0 copy-start
  0.0 0.5 collective-permute-start.10
  0.5 2.6 %collective-permute-start.1 = (bf16[2048,256]{1,0:T(8,128)(2,1)}, bf16[2048,256]{1,0:T(8,128)(2,1)S(1)}, u32[]{:S(2)}, u32[]{:S(2)}) collective-permute-start(bf16[2048,256]{1,0:T(8,128)(2,1)} %refs_4_.2), channel_id=1, source_target_pairs={{2,6},{3,1},{6,10},{7,3},{10,14},{11,7},{14,12},{15,11},{12,8},{13... | collective-permute-start | bytes 3145736 | tf_op jit(solution)/shard_map/ppermute | solution.py:204
  3.0 0.2 collective-permute-start.9
  3.3 1.4 %collective-permute-start = (bf16[512,256]{1,0:T(8,128)(2,1)}, bf16[512,256]{1,0:T(8,128)(2,1)S(1)}, u32[]{:S(2)}, u32[]{:S(2)}) collective-permute-start(bf16[512,256]{1,0:T(8,128)(2,1)} %refs_5_.2), channel_id=1, source_target_pairs={{2,6},{3,1},{6,10},{7,3},{10,14},{11,7},{14,12},{15,11},{12,8},{13... | collective-permute-start | bytes 786440 | tf_op jit(solution)/shard_map/ppermute | solution.py:204
  4.6 11.5 %collective-permute-done.1 = bf16[2048,256]{1,0:T(8,128)(2,1)S(1)} collective-permute-done((bf16[2048,256]{1,0:T(8,128)(2,1)}, bf16[2048,256]{1,0:T(8,128)(2,1)S(1)}, u32[]{:S(2)}, u32[]{:S(2)}) %collective-permute-start.1) | collective-permute-done | bytes 1048608 | tf_op jit(solution)/shard_map/ppermute | solution.py:204
  16.1 2.0 %collective-permute-start.6 = (bf16[1280,256]{1,0:T(8,128)(2,1)S(1)}, bf16[1280,256]{1,0:T(8,128)(2,1)S(1)}, u32[]{:S(2)}, u32[]{:S(2)}) collective-permute-start(bf16[1280,256]{1,0:T(8,128)(2,1)S(1)} %slice.10.refs_4_), channel_id=1, source_target_pairs={{2,6},{3,1},{6,10},{7,3},{10,14},{11,7},{14,12},{15,11},{12,8},{13... | collective-permute-start | bytes 1966088 | tf_op jit(solution)/shard_map/ppermute | solution.py:204
  18.1 0.1 collective-permute-start.2
  18.3 0.6 collective-permute-done
  18.9 0.0 copy-start.4
  18.9 8.6 %collective-permute-done.2.refs_2_ = bf16[512,256]{1,0:T(8,128)(2,1)S(1)} collective-permute-done((bf16[512,256]{1,0:T(8,128)(2,1)}, bf16[512,256]{1,0:T(8,128)(2,1)S(1)}, u32[]{:S(2)}, u32[]{:S(2)}) %collective-permute-start.2) | collective-permute-done | bytes 262176 | tf_op jit(solution)/shard_map/ppermute | solution.py:223
  27.6 1.6 %collective-permute-start.3 = (bf16[1280,256]{1,0:T(8,128)(2,1)S(1)}, bf16[1280,256]{1,0:T(8,128)(2,1)S(1)}, u32[]{:S(2)}, u32[]{:S(2)}) collective-permute-start(bf16[1280,256]{1,0:T(8,128)(2,1)S(1)} %pad_maximum_fusion.refs_5_), channel_id=1, source_target_pairs={{2,6},{3,1},{6,10},{7,3},{10,14},{11,7},{14,12},{15,11},{12,8},{13... | collective-permute-start | bytes 1966088 | tf_op jit(solution)/shard_map/ppermute | solution.py:204
  29.2 0.4 collective-permute-done.6.refs_4_
  29.6 1.2 %collective-permute-start.7 = (bf16[1280,256]{1,0:T(8,128)(2,1)S(1)}, bf16[1280,256]{1,0:T(8,128)(2,1)}, u32[]{:S(2)}, u32[]{:S(2)}) collective-permute-start(bf16[1280,256]{1,0:T(8,128)(2,1)S(1)} %collective-permute-done.6.refs_4_), channel_id=1, source_target_pairs={{2,6},{3,1},{6,10},{7,3},{10,14},{11,7},{14,12},{15,11},{12,8},{13... | collective-permute-start | bytes 1966088 | tf_op jit(solution)/shard_map/ppermute | solution.py:204
  30.8 7.4 %collective-permute-done.3.refs_5_ = bf16[1280,256]{1,0:T(8,128)(2,1)S(1)} collective-permute-done((bf16[1280,256]{1,0:T(8,128)(2,1)S(1)}, bf16[1280,256]{1,0:T(8,128)(2,1)S(1)}, u32[]{:S(2)}, u32[]{:S(2)}) %collective-permute-start.3) | collective-permute-done | bytes 655392 | tf_op jit(solution)/shard_map/ppermute | solution.py:204
  38.2 0.0 copy-start.6
  38.2 1.6 %collective-permute-start.4 = (bf16[1280,256]{1,0:T(8,128)(2,1)S(1)}, bf16[1280,256]{1,0:T(8,128)(2,1)}, u32[]{:S(2)}, u32[]{:S(2)}) collective-permute-start(bf16[1280,256]{1,0:T(8,128)(2,1)S(1)} %collective-permute-done.3.refs_5_), channel_id=1, source_target_pairs={{2,6},{3,1},{6,10},{7,3},{10,14},{11,7},{14,12},{15,11},{12,8},{13... | collective-permute-start | bytes 1966088 | tf_op jit(solution)/shard_map/ppermute | solution.py:204
  39.8 0.0 copy-done.4
  39.8 5.5 %collective-permute-done.7.refs_4_ = bf16[1280,256]{1,0:T(8,128)(2,1)} collective-permute-done((bf16[1280,256]{1,0:T(8,128)(2,1)S(1)}, bf16[1280,256]{1,0:T(8,128)(2,1)}, u32[]{:S(2)}, u32[]{:S(2)}) %collective-permute-start.7) | collective-permute-done | bytes 655392 | tf_op jit(solution)/shard_map/ppermute | solution.py:204
  45.3 0.0 copy-done.6
  45.3 1.6 %collective-permute-start.8 = (bf16[1280,256]{1,0:T(8,128)(2,1)}, bf16[1280,256]{1,0:T(8,128)(2,1)S(1)}, u32[]{:S(2)}, u32[]{:S(2)}) collective-permute-start(bf16[1280,256]{1,0:T(8,128)(2,1)} %collective-permute-done.7.refs_4_), channel_id=1, source_target_pairs={{2,6},{3,1},{6,10},{7,3},{10,14},{11,7},{14,12},{15,11},{12,8},{13... | collective-permute-start | bytes 1966088 | tf_op jit(solution)/shard_map/ppermute | solution.py:204
  46.9 5.4 %collective-permute-done.4.refs_5_ = bf16[1280,256]{1,0:T(8,128)(2,1)} collective-permute-done((bf16[1280,256]{1,0:T(8,128)(2,1)S(1)}, bf16[1280,256]{1,0:T(8,128)(2,1)}, u32[]{:S(2)}, u32[]{:S(2)}) %collective-permute-start.4) | collective-permute-done | bytes 655392 | tf_op jit(solution)/shard_map/ppermute | solution.py:204
  52.3 1.6 %collective-permute-start.5 = (bf16[1280,256]{1,0:T(8,128)(2,1)}, bf16[1280,256]{1,0:T(8,128)(2,1)}, u32[]{:S(2)}, u32[]{:S(2)}) collective-permute-start(bf16[1280,256]{1,0:T(8,128)(2,1)} %collective-permute-done.4.refs_5_), channel_id=1, source_target_pairs={{2,6},{3,1},{6,10},{7,3},{10,14},{11,7},{14,12},{15,11},{12,8},{13... | collective-permute-start | bytes 1966088 | tf_op jit(solution)/shard_map/ppermute | solution.py:204
  53.9 0.7 dynamic-slice_bitcast_fusion.order_ref
  54.6 0.0 collective-permute-done.9.refs_1_
  54.6 0.0 collective-permute-done.10.refs_3_.sib_ref.refs_1_
  54.6 0.0 copy-done
  54.6 0.0 copy-done.1
  54.6 2.6 %step.8 = (f32[320,256]{1,0:T(8,128)S(1)}, f32[320,256]{1,0:T(8,128)S(1)}) custom-call(s32[8]{0:T(128)S(1)} %dynamic-slice_bitcast_fusion.order_ref, bf16[160,8192]{1,0:T(8,128)(2,1)} %refs_0_.17, bf16[160,8192]{1,0:T(8,128)(2,1)} %collective-permute-done.9.refs_1_, bf16[160,32768]{1,0:T(8,128)(2,1)} %refs_0_.16, ...), custom_call_target="tpu_custom_call" | custom-call | flops 419430400 | bytes 3604480 | tf_op jit(solution)/shard_map/step/pallas_call | solution.py:59
  57.2 2.8 %step.9 = (f32[320,256]{1,0:T(8,128)S(1)}, f32[320,256]{1,0:T(8,128)S(1)}) custom-call(s32[8]{0:T(128)S(1)} %dynamic-slice_bitcast_fusion.order_ref, bf16[160,8192]{1,0:T(8,128)(2,1)} %refs_0_.17, bf16[160,8192]{1,0:T(8,128)(2,1)} %collective-permute-done.9.refs_1_, bf16[160,32768]{1,0:T(8,128)(2,1)} %refs_0_.16, ...), custom_call_target="tpu_custom_call" | custom-call | flops 419430400 | bytes 4259840 | tf_op jit(solution)/shard_map/step/pallas_call | solution.py:59
  60.0 0.0 collective-permute-done.8.refs_4_
  60.0 1.6 %collective-permute-start.12 = (bf16[1280,256]{1,0:T(8,128)(2,1)S(1)}, bf16[1280,256]{1,0:T(8,128)(2,1)S(1)}, u32[]{:S(2)}, u32[]{:S(2)}) collective-permute-start(bf16[1280,256]{1,0:T(8,128)(2,1)S(1)} %collective-permute-done.8.refs_4_), channel_id=1, source_target_pairs={{2,6},{3,1},{6,10},{7,3},{10,14},{11,7},{14,12},{15,11},{12,8},{13... | collective-permute-start | bytes 1966088 | tf_op jit(solution)/shard_map/ppermute | solution.py:204
  61.7 4.7 %collective-permute-done.5.refs_5_ = bf16[1280,256]{1,0:T(8,128)(2,1)} collective-permute-done((bf16[1280,256]{1,0:T(8,128)(2,1)}, bf16[1280,256]{1,0:T(8,128)(2,1)}, u32[]{:S(2)}, u32[]{:S(2)}) %collective-permute-start.5) | collective-permute-done | bytes 655392 | tf_op jit(solution)/shard_map/ppermute | solution.py:204
  66.4 1.6 %collective-permute-start.11 = (bf16[1280,256]{1,0:T(8,128)(2,1)}, bf16[1280,256]{1,0:T(8,128)(2,1)S(1)}, u32[]{:S(2)}, u32[]{:S(2)}) collective-permute-start(bf16[1280,256]{1,0:T(8,128)(2,1)} %collective-permute-done.5.refs_5_), channel_id=1, source_target_pairs={{2,6},{3,1},{6,10},{7,3},{10,14},{11,7},{14,12},{15,11},{12,8},{13... | collective-permute-start | bytes 1966088 | tf_op jit(solution)/shard_map/ppermute | solution.py:204
  68.0 2.8 %step.10 = (f32[320,256]{1,0:T(8,128)S(1)}, f32[320,256]{1,0:T(8,128)S(1)}) custom-call(s32[8]{0:T(128)S(1)} %dynamic-slice_bitcast_fusion.order_ref, bf16[160,8192]{1,0:T(8,128)(2,1)} %refs_0_.17, bf16[160,8192]{1,0:T(8,128)(2,1)} %collective-permute-done.9.refs_1_, bf16[160,32768]{1,0:T(8,128)(2,1)} %refs_0_.16, ...), custom_call_target="tpu_custom_call" | custom-call | flops 419430400 | bytes 4259840 | tf_op jit(solution)/shard_map/step/pallas_call | solution.py:59
  70.7 3.0 %step.11 = (f32[320,256]{1,0:T(8,128)S(1)}, f32[320,256]{1,0:T(8,128)S(1)}) custom-call(s32[8]{0:T(128)S(1)} %dynamic-slice_bitcast_fusion.order_ref, bf16[160,8192]{1,0:T(8,128)(2,1)} %refs_0_.17, bf16[160,8192]{1,0:T(8,128)(2,1)} %collective-permute-done.9.refs_1_, bf16[160,32768]{1,0:T(8,128)(2,1)} %refs_0_.16, ...), custom_call_target="tpu_custom_call" | custom-call | flops 419430400 | bytes 4259840 | tf_op jit(solution)/shard_map/step/pallas_call | solution.py:59
  73.7 0.0 collective-permute-done.12.refs_4_
  73.7 1.6 %collective-permute-start.14 = (bf16[1280,256]{1,0:T(8,128)(2,1)S(1)}, bf16[1280,256]{1,0:T(8,128)(2,1)S(1)}, u32[]{:S(2)}, u32[]{:S(2)}) collective-permute-start(bf16[1280,256]{1,0:T(8,128)(2,1)S(1)} %collective-permute-done.12.refs_4_), channel_id=1, source_target_pairs={{2,6},{3,1},{6,10},{7,3},{10,14},{11,7},{14,12},{15,11},{12,8},{13... | collective-permute-start | bytes 1966088 | tf_op jit(solution)/shard_map/ppermute | solution.py:204
  75.4 5.0 %collective-permute-done.11.refs_5_ = bf16[1280,256]{1,0:T(8,128)(2,1)S(1)} collective-permute-done((bf16[1280,256]{1,0:T(8,128)(2,1)}, bf16[1280,256]{1,0:T(8,128)(2,1)S(1)}, u32[]{:S(2)}, u32[]{:S(2)}) %collective-permute-start.11) | collective-permute-done | bytes 655392 | tf_op jit(solution)/shard_map/ppermute | solution.py:204
  80.3 1.6 %collective-permute-start.13 = (bf16[1280,256]{1,0:T(8,128)(2,1)S(1)}, bf16[1280,256]{1,0:T(8,128)(2,1)S(1)}, u32[]{:S(2)}, u32[]{:S(2)}) collective-permute-start(bf16[1280,256]{1,0:T(8,128)(2,1)S(1)} %collective-permute-done.11.refs_5_), channel_id=1, source_target_pairs={{2,6},{3,1},{6,10},{7,3},{10,14},{11,7},{14,12},{15,11},{12,8},{13... | collective-permute-start | bytes 1966088 | tf_op jit(solution)/shard_map/ppermute | solution.py:204
  81.9 2.8 %step.12 = (f32[320,256]{1,0:T(8,128)S(1)}, f32[320,256]{1,0:T(8,128)S(1)}) custom-call(s32[8]{0:T(128)S(1)} %dynamic-slice_bitcast_fusion.order_ref, bf16[160,8192]{1,0:T(8,128)(2,1)} %refs_0_.17, bf16[160,8192]{1,0:T(8,128)(2,1)} %collective-permute-done.9.refs_1_, bf16[160,32768]{1,0:T(8,128)(2,1)} %refs_0_.16, ...), custom_call_target="tpu_custom_call" | custom-call | flops 419430400 | bytes 4259840 | tf_op jit(solution)/shard_map/step/pallas_call | solution.py:59
  84.7 0.0 copy-done.7
  84.7 2.8 %step.13 = (f32[320,256]{1,0:T(8,128)S(1)}, f32[320,256]{1,0:T(8,128)S(1)}) custom-call(s32[8]{0:T(128)S(1)} %dynamic-slice_bitcast_fusion.order_ref, bf16[160,8192]{1,0:T(8,128)(2,1)} %refs_0_.17, bf16[160,8192]{1,0:T(8,128)(2,1)} %collective-permute-done.9.refs_1_, bf16[160,32768]{1,0:T(8,128)(2,1)} %refs_0_.16, ...), custom_call_target="tpu_custom_call" | custom-call | flops 419430400 | bytes 4259840 | tf_op jit(solution)/shard_map/step/pallas_call | solution.py:59
  87.5 0.0 collective-permute-done.14.refs_4_
  87.5 1.6 %collective-permute-start.16 = (bf16[1280,256]{1,0:T(8,128)(2,1)S(1)}, bf16[1280,256]{1,0:T(8,128)(2,1)S(1)}, u32[]{:S(2)}, u32[]{:S(2)}) collective-permute-start(bf16[1280,256]{1,0:T(8,128)(2,1)S(1)} %collective-permute-done.14.refs_4_), channel_id=1, source_target_pairs={{2,6},{3,1},{6,10},{7,3},{10,14},{11,7},{14,12},{15,11},{12,8},{13... | collective-permute-start | bytes 1966088 | tf_op jit(solution)/shard_map/ppermute | solution.py:204
  89.1 1.9 %window.1.window_ref = bf16[320,768]{1,0:T(8,128)(2,1)S(1)} custom-call(s32[8]{0:T(128)S(1)} %dynamic-slice_bitcast_fusion.order_ref, bf16[160,32768]{1,0:T(8,128)(2,1)} %refs_0_.16, bf16[160,32768]{1,0:T(8,128)(2,1)} %collective-permute-done.10.refs_3_.sib_ref.refs_1_), custom_call_target="tpu_custom_call" | custom-call | bytes 1802240 | tf_op jit(solution)/shard_map/window/pallas_call | solution.py:59
  91.0 3.4 %collective-permute-done.13.refs_5_ = bf16[1280,256]{1,0:T(8,128)(2,1)S(1)} collective-permute-done((bf16[1280,256]{1,0:T(8,128)(2,1)S(1)}, bf16[1280,256]{1,0:T(8,128)(2,1)S(1)}, u32[]{:S(2)}, u32[]{:S(2)}) %collective-permute-start.13) | collective-permute-done | bytes 655392 | tf_op jit(solution)/shard_map/ppermute | solution.py:204
  94.4 0.0 copy-start.2
  94.4 0.0 copy-start.3
  94.4 1.6 %collective-permute-start.15 = (bf16[768,256]{1,0:T(8,128)(2,1)S(1)}, bf16[768,256]{1,0:T(8,128)(2,1)S(1)}, u32[]{:S(2)}, u32[]{:S(2)}) collective-permute-start(bf16[768,256]{1,0:T(8,128)(2,1)S(1)} %slice.11), channel_id=1, source_target_pairs={{2,6},{3,1},{6,10},{7,3},{10,14},{11,7},{14,12},{15,11},{12,8},{13... | collective-permute-start | bytes 1179656 | tf_op jit(solution)/shard_map/ppermute | solution.py:204
  96.0 0.0 copy-done.5
  96.0 2.8 %step.14 = (f32[320,256]{1,0:T(8,128)S(1)}, f32[320,256]{1,0:T(8,128)S(1)}) custom-call(s32[8]{0:T(128)S(1)} %dynamic-slice_bitcast_fusion.order_ref, bf16[160,8192]{1,0:T(8,128)(2,1)} %refs_0_.17, bf16[160,8192]{1,0:T(8,128)(2,1)} %collective-permute-done.9.refs_1_, bf16[160,32768]{1,0:T(8,128)(2,1)} %refs_0_.16, ...), custom_call_target="tpu_custom_call" | custom-call | flops 419430400 | bytes 4259840 | tf_op jit(solution)/shard_map/step/pallas_call | solution.py:59
  98.8 0.0 copy-done.2
  98.8 0.0 copy-done.3
  98.9 1.8 %turned.1.own_ref = f32[328,256]{1,0:T(8,128)S(1)} custom-call(s32[8]{0:T(128)S(1)} %dynamic-slice_bitcast_fusion.order_ref, bf16[160,8192]{1,0:T(8,128)(2,1)} %refs_0_.17, bf16[160,8192]{1,0:T(8,128)(2,1)} %collective-permute-done.9.refs_1_, bf16[512,256]{1,0:T(8,128)(2,1)S(1)} %collective-permute-done.2.refs_2_, f32[320,256]{1,0:T(8,128)S(1)} %get-tuple-element.82.refs_3_, ...), custom_call_target="tpu_custom_call" | custom-call | flops 83886080 | bytes 1253376 | tf_op jit(solution)/shard_map/turned/pallas_call | solution.py:59
  100.7 0.1 collective-permute-start.17
  100.7 1.6 %collective-permute-done.17.got_ref = f32[328,256]{1,0:T(8,128)S(1)} collective-permute-done((f32[328,256]{1,0:T(8,128)S(1)}, f32[328,256]{1,0:T(8,128)S(1)}, u32[]{:S(2)}, u32[]{:S(2)}) %collective-permute-start.17) | collective-permute-done | bytes 335904 | tf_op jit(solution)/shard_map/ppermute | solution.py:205
  102.4 0.6 masked.1.inn_ref
  103.0 0.0 collective-permute-done.16.refs_2_
  103.0 2.2 %step.15.total_ref = f32[320,256]{1,0:T(8,128)S(1)} custom-call(s32[8]{0:T(128)S(1)} %dynamic-slice_bitcast_fusion.order_ref, bf16[160,32768]{1,0:T(8,128)(2,1)} %refs_0_.16, bf16[160,32768]{1,0:T(8,128)(2,1)} %collective-permute-done.10.refs_3_.sib_ref.refs_1_, bf16[1280,256]{1,0:T(8,128)(2,1)S(1)} %collective-permute-done.16.refs_2_, ...), custom_call_target="tpu_custom_call" | custom-call | flops 209715200 | bytes 2621440 | tf_op jit(solution)/shard_map/step/pallas_call | solution.py:59
  105.2 0.4 collective-permute-done.15.block_ref
  105.6 0.6 score.1
  106.2 11.3 %all_to_all.5 = f32[16,2,8]{2,1,0:T(2,128)S(1)} all-to-all(f32[16,2,8]{2,1,0:T(2,128)S(1)} %bitcast.3), channel_id=1, replica_groups=mesh['groups'=2,'dp'=16] {'dp'}, dimensions={0} | all-to-all | bytes 2048 | tf_op jit(solution)/shard_map/all_to_all | solution.py:274
  117.4 0.6 reduce_sum.9
  (7 shorter events, 0.1 us)
Async XLA Ops:
  0.0 54.6 %copy-start = (bf16[2048,256]{1,0:T(8,128)(2,1)S(1)}, bf16[2048,256]{1,0:T(8,128)(2,1)}, u32[]{:S(2)}) copy-start(bf16[2048,256]{1,0:T(8,128)(2,1)} %refs_4_.2) | copy-start | bytes 3145732
  0.0 54.6 %copy-start.1 = (bf16[512,256]{1,0:T(8,128)(2,1)S(1)}, bf16[512,256]{1,0:T(8,128)(2,1)}, u32[]{:S(2)}) copy-start(bf16[512,256]{1,0:T(8,128)(2,1)} %refs_5_.2) | copy-start | bytes 786436
  0.0 54.6 %collective-permute-start.10 = (bf16[160,32768]{1,0:T(8,128)(2,1)}, bf16[160,32768]{1,0:T(8,128)(2,1)}, u32[]{:S(2)}, u32[]{:S(2)}) collective-permute-start(bf16[160,32768]{1,0:T(8,128)(2,1)} %refs_0_.16), channel_id=1, source_target_pairs={{0,1},{1,0},{2,3},{3,2},{4,5},{5,4},{6,7},{7,6},{8,9},{9,8},{10,11... | collective-permute-start | bytes 31457288 | tf_op jit(solution)/shard_map/ppermute | solution.py:205
  0.5 15.6 %collective-permute-start.1 = (bf16[2048,256]{1,0:T(8,128)(2,1)}, bf16[2048,256]{1,0:T(8,128)(2,1)S(1)}, u32[]{:S(2)}, u32[]{:S(2)}) collective-permute-start(bf16[2048,256]{1,0:T(8,128)(2,1)} %refs_4_.2), channel_id=1, source_target_pairs={{2,6},{3,1},{6,10},{7,3},{10,14},{11,7},{14,12},{15,11},{12,8},{13... | collective-permute-start | bytes 3145736 | tf_op jit(solution)/shard_map/ppermute | solution.py:204
  3.0 51.6 %collective-permute-start.9 = (bf16[160,8192]{1,0:T(8,128)(2,1)}, bf16[160,8192]{1,0:T(8,128)(2,1)}, u32[]{:S(2)}, u32[]{:S(2)}) collective-permute-start(bf16[160,8192]{1,0:T(8,128)(2,1)} %refs_0_.17), channel_id=1, source_target_pairs={{0,1},{1,0},{2,3},{3,2},{4,5},{5,4},{6,7},{7,6},{8,9},{9,8},{10,11... | collective-permute-start | bytes 7864328 | tf_op jit(solution)/shard_map/ppermute | solution.py:205
  3.3 15.6 %collective-permute-start = (bf16[512,256]{1,0:T(8,128)(2,1)}, bf16[512,256]{1,0:T(8,128)(2,1)S(1)}, u32[]{:S(2)}, u32[]{:S(2)}) collective-permute-start(bf16[512,256]{1,0:T(8,128)(2,1)} %refs_5_.2), channel_id=1, source_target_pairs={{2,6},{3,1},{6,10},{7,3},{10,14},{11,7},{14,12},{15,11},{12,8},{13... | collective-permute-start | bytes 786440 | tf_op jit(solution)/shard_map/ppermute | solution.py:204
  16.1 13.4 %collective-permute-start.6 = (bf16[1280,256]{1,0:T(8,128)(2,1)S(1)}, bf16[1280,256]{1,0:T(8,128)(2,1)S(1)}, u32[]{:S(2)}, u32[]{:S(2)}) collective-permute-start(bf16[1280,256]{1,0:T(8,128)(2,1)S(1)} %slice.10.refs_4_), channel_id=1, source_target_pairs={{2,6},{3,1},{6,10},{7,3},{10,14},{11,7},{14,12},{15,11},{12,8},{13... | collective-permute-start | bytes 1966088 | tf_op jit(solution)/shard_map/ppermute | solution.py:204
  18.1 9.5 %collective-permute-start.2 = (bf16[512,256]{1,0:T(8,128)(2,1)}, bf16[512,256]{1,0:T(8,128)(2,1)S(1)}, u32[]{:S(2)}, u32[]{:S(2)}) collective-permute-start(bf16[512,256]{1,0:T(8,128)(2,1)} %refs_5_.2), channel_id=1, source_target_pairs={{6,2},{1,3},{10,6},{3,7},{14,10},{7,11},{12,14},{11,15},{8,12},{15... | collective-permute-start | bytes 786440 | tf_op jit(solution)/shard_map/ppermute | solution.py:223
  18.9 20.8 %copy-start.4 = (bf16[1280,256]{1,0:T(8,128)(2,1)}, bf16[1280,256]{1,0:T(8,128)(2,1)S(1)}, u32[]{:S(2)}) copy-start(bf16[1280,256]{1,0:T(8,128)(2,1)S(1)} %pad_maximum_fusion.refs_5_) | copy-start | bytes 1966084
  27.6 10.6 %collective-permute-start.3 = (bf16[1280,256]{1,0:T(8,128)(2,1)S(1)}, bf16[1280,256]{1,0:T(8,128)(2,1)S(1)}, u32[]{:S(2)}, u32[]{:S(2)}) collective-permute-start(bf16[1280,256]{1,0:T(8,128)(2,1)S(1)} %pad_maximum_fusion.refs_5_), channel_id=1, source_target_pairs={{2,6},{3,1},{6,10},{7,3},{10,14},{11,7},{14,12},{15,11},{12,8},{13... | collective-permute-start | bytes 1966088 | tf_op jit(solution)/shard_map/ppermute | solution.py:204
  29.6 15.7 %collective-permute-start.7 = (bf16[1280,256]{1,0:T(8,128)(2,1)S(1)}, bf16[1280,256]{1,0:T(8,128)(2,1)}, u32[]{:S(2)}, u32[]{:S(2)}) collective-permute-start(bf16[1280,256]{1,0:T(8,128)(2,1)S(1)} %collective-permute-done.6.refs_4_), channel_id=1, source_target_pairs={{2,6},{3,1},{6,10},{7,3},{10,14},{11,7},{14,12},{15,11},{12,8},{13... | collective-permute-start | bytes 1966088 | tf_op jit(solution)/shard_map/ppermute | solution.py:204
  38.2 7.1 %copy-start.6 = (bf16[1280,256]{1,0:T(8,128)(2,1)}, bf16[1280,256]{1,0:T(8,128)(2,1)S(1)}, u32[]{:S(2)}) copy-start(bf16[1280,256]{1,0:T(8,128)(2,1)S(1)} %collective-permute-done.3.refs_5_) | copy-start | bytes 1966084
  38.2 14.1 %collective-permute-start.4 = (bf16[1280,256]{1,0:T(8,128)(2,1)S(1)}, bf16[1280,256]{1,0:T(8,128)(2,1)}, u32[]{:S(2)}, u32[]{:S(2)}) collective-permute-start(bf16[1280,256]{1,0:T(8,128)(2,1)S(1)} %collective-permute-done.3.refs_5_), channel_id=1, source_target_pairs={{2,6},{3,1},{6,10},{7,3},{10,14},{11,7},{14,12},{15,11},{12,8},{13... | collective-permute-start | bytes 1966088 | tf_op jit(solution)/shard_map/ppermute | solution.py:204
  45.3 14.7 %collective-permute-start.8 = (bf16[1280,256]{1,0:T(8,128)(2,1)}, bf16[1280,256]{1,0:T(8,128)(2,1)S(1)}, u32[]{:S(2)}, u32[]{:S(2)}) collective-permute-start(bf16[1280,256]{1,0:T(8,128)(2,1)} %collective-permute-done.7.refs_4_), channel_id=1, source_target_pairs={{2,6},{3,1},{6,10},{7,3},{10,14},{11,7},{14,12},{15,11},{12,8},{13... | collective-permute-start | bytes 1966088 | tf_op jit(solution)/shard_map/ppermute | solution.py:204
  52.3 14.0 %collective-permute-start.5 = (bf16[1280,256]{1,0:T(8,128)(2,1)}, bf16[1280,256]{1,0:T(8,128)(2,1)}, u32[]{:S(2)}, u32[]{:S(2)}) collective-permute-start(bf16[1280,256]{1,0:T(8,128)(2,1)} %collective-permute-done.4.refs_5_), channel_id=1, source_target_pairs={{2,6},{3,1},{6,10},{7,3},{10,14},{11,7},{14,12},{15,11},{12,8},{13... | collective-permute-start | bytes 1966088 | tf_op jit(solution)/shard_map/ppermute | solution.py:204
  60.0 13.7 %collective-permute-start.12 = (bf16[1280,256]{1,0:T(8,128)(2,1)S(1)}, bf16[1280,256]{1,0:T(8,128)(2,1)S(1)}, u32[]{:S(2)}, u32[]{:S(2)}) collective-permute-start(bf16[1280,256]{1,0:T(8,128)(2,1)S(1)} %collective-permute-done.8.refs_4_), channel_id=1, source_target_pairs={{2,6},{3,1},{6,10},{7,3},{10,14},{11,7},{14,12},{15,11},{12,8},{13... | collective-permute-start | bytes 1966088 | tf_op jit(solution)/shard_map/ppermute | solution.py:204
  66.4 13.9 %collective-permute-start.11 = (bf16[1280,256]{1,0:T(8,128)(2,1)}, bf16[1280,256]{1,0:T(8,128)(2,1)S(1)}, u32[]{:S(2)}, u32[]{:S(2)}) collective-permute-start(bf16[1280,256]{1,0:T(8,128)(2,1)} %collective-permute-done.5.refs_5_), channel_id=1, source_target_pairs={{2,6},{3,1},{6,10},{7,3},{10,14},{11,7},{14,12},{15,11},{12,8},{13... | collective-permute-start | bytes 1966088 | tf_op jit(solution)/shard_map/ppermute | solution.py:204
  73.7 13.7 %collective-permute-start.14 = (bf16[1280,256]{1,0:T(8,128)(2,1)S(1)}, bf16[1280,256]{1,0:T(8,128)(2,1)S(1)}, u32[]{:S(2)}, u32[]{:S(2)}) collective-permute-start(bf16[1280,256]{1,0:T(8,128)(2,1)S(1)} %collective-permute-done.12.refs_4_), channel_id=1, source_target_pairs={{2,6},{3,1},{6,10},{7,3},{10,14},{11,7},{14,12},{15,11},{12,8},{13... | collective-permute-start | bytes 1966088 | tf_op jit(solution)/shard_map/ppermute | solution.py:204
  80.3 4.4 %copy-start.7 = (bf16[1280,256]{1,0:T(8,128)(2,1)}, bf16[1280,256]{1,0:T(8,128)(2,1)S(1)}, u32[]{:S(2)}) copy-start(bf16[1280,256]{1,0:T(8,128)(2,1)S(1)} %collective-permute-done.11.refs_5_) | copy-start | bytes 1966084
  80.3 14.0 %collective-permute-start.13 = (bf16[1280,256]{1,0:T(8,128)(2,1)S(1)}, bf16[1280,256]{1,0:T(8,128)(2,1)S(1)}, u32[]{:S(2)}, u32[]{:S(2)}) collective-permute-start(bf16[1280,256]{1,0:T(8,128)(2,1)S(1)} %collective-permute-done.11.refs_5_), channel_id=1, source_target_pairs={{2,6},{3,1},{6,10},{7,3},{10,14},{11,7},{14,12},{15,11},{12,8},{13... | collective-permute-start | bytes 1966088 | tf_op jit(solution)/shard_map/ppermute | solution.py:204
  87.5 15.5 %collective-permute-start.16 = (bf16[1280,256]{1,0:T(8,128)(2,1)S(1)}, bf16[1280,256]{1,0:T(8,128)(2,1)S(1)}, u32[]{:S(2)}, u32[]{:S(2)}) collective-permute-start(bf16[1280,256]{1,0:T(8,128)(2,1)S(1)} %collective-permute-done.14.refs_4_), channel_id=1, source_target_pairs={{2,6},{3,1},{6,10},{7,3},{10,14},{11,7},{14,12},{15,11},{12,8},{13... | collective-permute-start | bytes 1966088 | tf_op jit(solution)/shard_map/ppermute | solution.py:204
  94.4 1.7 %copy-start.5 = (bf16[1280,256]{1,0:T(8,128)(2,1)}, bf16[1280,256]{1,0:T(8,128)(2,1)S(1)}, u32[]{:S(2)}) copy-start(bf16[1280,256]{1,0:T(8,128)(2,1)S(1)} %collective-permute-done.13.refs_5_) | copy-start | bytes 1966084
  94.4 4.4 %copy-start.2 = (s32[2]{0:T(128)S(1)}, s32[2]{0:T(128)}, u32[]{:S(2)}) copy-start(s32[2]{0:T(128)} %refs_4_.3) | copy-start | bytes 28
  94.4 4.4 %copy-start.3 = (s32[2]{0:T(128)S(1)}, s32[2]{0:T(128)}, u32[]{:S(2)}) copy-start(s32[2]{0:T(128)} %refs_5_.3) | copy-start | bytes 28
  94.4 11.2 %collective-permute-start.15 = (bf16[768,256]{1,0:T(8,128)(2,1)S(1)}, bf16[768,256]{1,0:T(8,128)(2,1)S(1)}, u32[]{:S(2)}, u32[]{:S(2)}) collective-permute-start(bf16[768,256]{1,0:T(8,128)(2,1)S(1)} %slice.11), channel_id=1, source_target_pairs={{2,6},{3,1},{6,10},{7,3},{10,14},{11,7},{14,12},{15,11},{12,8},{13... | collective-permute-start | bytes 1179656 | tf_op jit(solution)/shard_map/ppermute | solution.py:204
  100.7 1.7 %collective-permute-start.17 = (f32[328,256]{1,0:T(8,128)S(1)}, f32[328,256]{1,0:T(8,128)S(1)}, u32[]{:S(2)}, u32[]{:S(2)}) collective-permute-start(f32[328,256]{1,0:T(8,128)S(1)} %turned.1.own_ref), channel_id=1, source_target_pairs={{0,1},{1,0},{2,3},{3,2},{4,5},{5,4},{6,7},{7,6},{8,9},{9,8},{10,11... | collective-permute-start | bytes 1007624 | tf_op jit(solution)/shard_map/ppermute | solution.py:205

commit v15 on v14

--- a/solution.py
+++ b/solution.py
@@ -222,8 +222,8 @@
         came, turned = lax.optimization_barrier((came, in_factors))
         turned = lax.ppermute(turned, "dp", [(j, i) for i, j in pairs])
         late, early = came[lead:], came[:lead]
-        early = jnp.concatenate([send(in_factors), early])
-        early, turned = lax.optimization_barrier((early, turned))
+        inner, turned = lax.optimization_barrier((send(in_factors), turned))
+        early = jnp.concatenate([inner, early])
     totals, summed, last = {}, 0, chips - 1
 
     def sum_to(k, totals, summed):

time: 119 us -> 118 us (level)
  waiting for transfers between devices: 54.6 us -> 49.4 us
  starting transfers between devices: 24 us -> 27.2 us
  blocking collectives: 11.3 us -> 12.7 us
    ppermute x14, waiting for transfers between devices: 44.3 us -> 41.5 us  [shards(): send = lambda x: lax.ppermute(x, 'dp', pairs)]
    ppermute x1, waiting for transfers between devices: 8.65 us -> 6.32 us  [shards(): turned = lax.ppermute(turned, 'dp', [(j, i) for i, j in pairs])]
    ppermute x1, starting transfers between devices: 0.12 us -> 2.02 us  [shards(): turned = lax.ppermute(turned, 'dp', [(j, i) for i, j in pairs])]
    all_to_all x1, blocking collectives: 11.3 us -> 12.7 us  [shards(): lax.all_to_all(table.reshape(devices, slots, queries), 'dp', 0, 0, tiled=...]
    ppermute x14, starting transfers between devices: 23.1 us -> 24.4 us  [shards(): send = lambda x: lax.ppermute(x, 'dp', pairs)]
  transfers between devices with their start and end apart: 18 -> 18, of which waited for: 12 -> 11; matrix products, arithmetic and copies ran while one was open for 1% -> 1% of each run, Pallas kernels for 22% -> 22%
where the time goes in v15:
time: 118 us; the launch traced here: 117 us
  waiting for transfers between devices  49.4 us (42%)
  starting transfers between devices  27.2 us (23%)
  Pallas kernels  26.5 us (22%)
  blocking collectives  12.7 us (11%)
    ppermute x14, waiting for transfers between devices, shards(): send = lambda x: lax.ppermute(x, 'dp', pairs)  41.5 us
    pallas_call x11, Pallas kernels, call(): pl.pallas_call(kernel, grid_spec=pltpu.PrefetchScalarGridSpec(num_scalar_...  25.9 us
    ppermute x14, starting transfers between devices, shards(): send = lambda x: lax.ppermute(x, 'dp', pairs)  24.4 us
    all_to_all x1, blocking collectives, shards(): lax.all_to_all(table.reshape(devices, slots, queries), 'dp', 0, 0, tiled=...  12.7 us
    ppermute x1, waiting for transfers between devices, shards(): turned = lax.ppermute(turned, 'dp', [(j, i) for i, j in pairs])  6.32 us
  transfers between devices with their start and end apart: 18, of which 11 were waited for; matrix products, arithmetic and copies ran while one was open for 1% of the time, Pallas kernels for 22%

profile of v15, /device:TPU:0, one launch (start us, length us, event | category | flops | bytes accessed | tf_op | source)
XLA Modules:
  0.0 117.4 jit_solution(14867716003938041699)
XLA Ops:
  0.0 0.0 copy-start
  0.0 0.0 copy-start.1
  0.0 0.5 collective-permute-start.10
  0.5 2.6 %collective-permute-start.1 = (bf16[2048,256]{1,0:T(8,128)(2,1)}, bf16[2048,256]{1,0:T(8,128)(2,1)S(1)}, u32[]{:S(2)}, u32[]{:S(2)}) collective-permute-start(bf16[2048,256]{1,0:T(8,128)(2,1)} %refs_4_.2), channel_id=1, source_target_pairs={{2,6},{3,1},{6,10},{7,3},{10,14},{11,7},{14,12},{15,11},{12,8},{13... | collective-permute-start | bytes 3145736 | tf_op jit(solution)/shard_map/ppermute | solution.py:204
  3.0 0.2 collective-permute-start.9
  3.3 1.4 %collective-permute-start = (bf16[512,256]{1,0:T(8,128)(2,1)}, bf16[512,256]{1,0:T(8,128)(2,1)S(1)}, u32[]{:S(2)}, u32[]{:S(2)}) collective-permute-start(bf16[512,256]{1,0:T(8,128)(2,1)} %refs_5_.2), channel_id=1, source_target_pairs={{2,6},{3,1},{6,10},{7,3},{10,14},{11,7},{14,12},{15,11},{12,8},{13... | collective-permute-start | bytes 786440 | tf_op jit(solution)/shard_map/ppermute | solution.py:204
  4.6 11.5 %collective-permute-done.1 = bf16[2048,256]{1,0:T(8,128)(2,1)S(1)} collective-permute-done((bf16[2048,256]{1,0:T(8,128)(2,1)}, bf16[2048,256]{1,0:T(8,128)(2,1)S(1)}, u32[]{:S(2)}, u32[]{:S(2)}) %collective-permute-start.1) | collective-permute-done | bytes 1048608 | tf_op jit(solution)/shard_map/ppermute | solution.py:204
  16.1 2.0 %collective-permute-start.2 = (bf16[512,256]{1,0:T(8,128)(2,1)}, bf16[512,256]{1,0:T(8,128)(2,1)S(1)}, u32[]{:S(2)}, u32[]{:S(2)}) collective-permute-start(bf16[512,256]{1,0:T(8,128)(2,1)} %refs_5_.2), channel_id=1, source_target_pairs={{6,2},{1,3},{10,6},{3,7},{14,10},{7,11},{12,14},{11,15},{8,12},{15... | collective-permute-start | bytes 786440 | tf_op jit(solution)/shard_map/ppermute | solution.py:223
  18.1 0.1 collective-permute-start.6
  18.3 0.7 collective-permute-done
  19.0 6.3 %collective-permute-done.2.refs_2_ = bf16[512,256]{1,0:T(8,128)(2,1)S(1)} collective-permute-done((bf16[512,256]{1,0:T(8,128)(2,1)}, bf16[512,256]{1,0:T(8,128)(2,1)S(1)}, u32[]{:S(2)}, u32[]{:S(2)}) %collective-permute-start.2) | collective-permute-done | bytes 262176 | tf_op jit(solution)/shard_map/ppermute | solution.py:223
  25.3 0.0 copy-start.4
  25.3 2.2 %collective-permute-start.3 = (bf16[1280,256]{1,0:T(8,128)(2,1)S(1)}, bf16[1280,256]{1,0:T(8,128)(2,1)S(1)}, u32[]{:S(2)}, u32[]{:S(2)}) collective-permute-start(bf16[1280,256]{1,0:T(8,128)(2,1)S(1)} %pad_maximum_fusion.refs_5_), channel_id=1, source_target_pairs={{2,6},{3,1},{6,10},{7,3},{10,14},{11,7},{14,12},{15,11},{12,8},{13... | collective-permute-start | bytes 1966088 | tf_op jit(solution)/shard_map/ppermute | solution.py:204
  27.5 1.2 %collective-permute-done.6.refs_4_ = bf16[1280,256]{1,0:T(8,128)(2,1)S(1)} collective-permute-done((bf16[1280,256]{1,0:T(8,128)(2,1)S(1)}, bf16[1280,256]{1,0:T(8,128)(2,1)S(1)}, u32[]{:S(2)}, u32[]{:S(2)}) %collective-permute-start.6) | collective-permute-done | bytes 655392 | tf_op jit(solution)/shard_map/ppermute | solution.py:204
  28.8 1.9 %collective-permute-start.7 = (bf16[1280,256]{1,0:T(8,128)(2,1)S(1)}, bf16[1280,256]{1,0:T(8,128)(2,1)}, u32[]{:S(2)}, u32[]{:S(2)}) collective-permute-start(bf16[1280,256]{1,0:T(8,128)(2,1)S(1)} %collective-permute-done.6.refs_4_), channel_id=1, source_target_pairs={{2,6},{3,1},{6,10},{7,3},{10,14},{11,7},{14,12},{15,11},{12,8},{13... | collective-permute-start | bytes 1966088 | tf_op jit(solution)/shard_map/ppermute | solution.py:204
  30.7 5.5 %collective-permute-done.3.refs_5_ = bf16[1280,256]{1,0:T(8,128)(2,1)S(1)} collective-permute-done((bf16[1280,256]{1,0:T(8,128)(2,1)S(1)}, bf16[1280,256]{1,0:T(8,128)(2,1)S(1)}, u32[]{:S(2)}, u32[]{:S(2)}) %collective-permute-start.3) | collective-permute-done | bytes 655392 | tf_op jit(solution)/shard_map/ppermute | solution.py:204
  36.2 1.9 %collective-permute-start.4 = (bf16[1280,256]{1,0:T(8,128)(2,1)S(1)}, bf16[1280,256]{1,0:T(8,128)(2,1)}, u32[]{:S(2)}, u32[]{:S(2)}) collective-permute-start(bf16[1280,256]{1,0:T(8,128)(2,1)S(1)} %collective-permute-done.3.refs_5_), channel_id=1, source_target_pairs={{2,6},{3,1},{6,10},{7,3},{10,14},{11,7},{14,12},{15,11},{12,8},{13... | collective-permute-start | bytes 1966088 | tf_op jit(solution)/shard_map/ppermute | solution.py:204
  38.1 0.0 copy-done.4
  38.1 5.2 %collective-permute-done.7.refs_4_ = bf16[1280,256]{1,0:T(8,128)(2,1)} collective-permute-done((bf16[1280,256]{1,0:T(8,128)(2,1)S(1)}, bf16[1280,256]{1,0:T(8,128)(2,1)}, u32[]{:S(2)}, u32[]{:S(2)}) %collective-permute-start.7) | collective-permute-done | bytes 655392 | tf_op jit(solution)/shard_map/ppermute | solution.py:204
  43.4 0.0 copy-done.6
  43.4 1.9 %collective-permute-start.8 = (bf16[1280,256]{1,0:T(8,128)(2,1)}, bf16[1280,256]{1,0:T(8,128)(2,1)S(1)}, u32[]{:S(2)}, u32[]{:S(2)}) collective-permute-start(bf16[1280,256]{1,0:T(8,128)(2,1)} %collective-permute-done.7.refs_4_), channel_id=1, source_target_pairs={{2,6},{3,1},{6,10},{7,3},{10,14},{11,7},{14,12},{15,11},{12,8},{13... | collective-permute-start | bytes 1966088 | tf_op jit(solution)/shard_map/ppermute | solution.py:204
  45.3 5.1 %collective-permute-done.4.refs_5_ = bf16[1280,256]{1,0:T(8,128)(2,1)} collective-permute-done((bf16[1280,256]{1,0:T(8,128)(2,1)S(1)}, bf16[1280,256]{1,0:T(8,128)(2,1)}, u32[]{:S(2)}, u32[]{:S(2)}) %collective-permute-start.4) | collective-permute-done | bytes 655392 | tf_op jit(solution)/shard_map/ppermute | solution.py:204
  50.4 1.9 %collective-permute-start.5 = (bf16[1280,256]{1,0:T(8,128)(2,1)}, bf16[1280,256]{1,0:T(8,128)(2,1)}, u32[]{:S(2)}, u32[]{:S(2)}) collective-permute-start(bf16[1280,256]{1,0:T(8,128)(2,1)} %collective-permute-done.4.refs_5_), channel_id=1, source_target_pairs={{2,6},{3,1},{6,10},{7,3},{10,14},{11,7},{14,12},{15,11},{12,8},{13... | collective-permute-start | bytes 1966088 | tf_op jit(solution)/shard_map/ppermute | solution.py:204
  52.3 0.7 dynamic-slice_bitcast_fusion.order_ref
  53.0 0.0 collective-permute-done.9.refs_1_
  53.0 0.0 collective-permute-done.10.refs_3_.sib_ref.refs_1_
  53.0 0.0 copy-done
  53.0 0.0 copy-done.1
  53.0 2.6 %step.8 = (f32[320,256]{1,0:T(8,128)S(1)}, f32[320,256]{1,0:T(8,128)S(1)}) custom-call(s32[8]{0:T(128)S(1)} %dynamic-slice_bitcast_fusion.order_ref, bf16[160,8192]{1,0:T(8,128)(2,1)} %refs_0_.17, bf16[160,8192]{1,0:T(8,128)(2,1)} %collective-permute-done.9.refs_1_, bf16[160,32768]{1,0:T(8,128)(2,1)} %refs_0_.16, ...), custom_call_target="tpu_custom_call" | custom-call | flops 419430400 | bytes 3604480 | tf_op jit(solution)/shard_map/step/pallas_call | solution.py:59
  55.6 2.8 %step.9 = (f32[320,256]{1,0:T(8,128)S(1)}, f32[320,256]{1,0:T(8,128)S(1)}) custom-call(s32[8]{0:T(128)S(1)} %dynamic-slice_bitcast_fusion.order_ref, bf16[160,8192]{1,0:T(8,128)(2,1)} %refs_0_.17, bf16[160,8192]{1,0:T(8,128)(2,1)} %collective-permute-done.9.refs_1_, bf16[160,32768]{1,0:T(8,128)(2,1)} %refs_0_.16, ...), custom_call_target="tpu_custom_call" | custom-call | flops 419430400 | bytes 4259840 | tf_op jit(solution)/shard_map/step/pallas_call | solution.py:59
  58.4 0.0 collective-permute-done.8.refs_4_
  58.4 1.6 %collective-permute-start.12 = (bf16[1280,256]{1,0:T(8,128)(2,1)S(1)}, bf16[1280,256]{1,0:T(8,128)(2,1)S(1)}, u32[]{:S(2)}, u32[]{:S(2)}) collective-permute-start(bf16[1280,256]{1,0:T(8,128)(2,1)S(1)} %collective-permute-done.8.refs_4_), channel_id=1, source_target_pairs={{2,6},{3,1},{6,10},{7,3},{10,14},{11,7},{14,12},{15,11},{12,8},{13... | collective-permute-start | bytes 1966088 | tf_op jit(solution)/shard_map/ppermute | solution.py:204
  60.0 4.4 %collective-permute-done.5.refs_5_ = bf16[1280,256]{1,0:T(8,128)(2,1)} collective-permute-done((bf16[1280,256]{1,0:T(8,128)(2,1)}, bf16[1280,256]{1,0:T(8,128)(2,1)}, u32[]{:S(2)}, u32[]{:S(2)}) %collective-permute-start.5) | collective-permute-done | bytes 655392 | tf_op jit(solution)/shard_map/ppermute | solution.py:204
  64.4 1.9 %collective-permute-start.11 = (bf16[1280,256]{1,0:T(8,128)(2,1)}, bf16[1280,256]{1,0:T(8,128)(2,1)S(1)}, u32[]{:S(2)}, u32[]{:S(2)}) collective-permute-start(bf16[1280,256]{1,0:T(8,128)(2,1)} %collective-permute-done.5.refs_5_), channel_id=1, source_target_pairs={{2,6},{3,1},{6,10},{7,3},{10,14},{11,7},{14,12},{15,11},{12,8},{13... | collective-permute-start | bytes 1966088 | tf_op jit(solution)/shard_map/ppermute | solution.py:204
  66.3 2.8 %step.10 = (f32[320,256]{1,0:T(8,128)S(1)}, f32[320,256]{1,0:T(8,128)S(1)}) custom-call(s32[8]{0:T(128)S(1)} %dynamic-slice_bitcast_fusion.order_ref, bf16[160,8192]{1,0:T(8,128)(2,1)} %refs_0_.17, bf16[160,8192]{1,0:T(8,128)(2,1)} %collective-permute-done.9.refs_1_, bf16[160,32768]{1,0:T(8,128)(2,1)} %refs_0_.16, ...), custom_call_target="tpu_custom_call" | custom-call | flops 419430400 | bytes 4259840 | tf_op jit(solution)/shard_map/step/pallas_call | solution.py:59
  69.1 3.0 %step.11 = (f32[320,256]{1,0:T(8,128)S(1)}, f32[320,256]{1,0:T(8,128)S(1)}) custom-call(s32[8]{0:T(128)S(1)} %dynamic-slice_bitcast_fusion.order_ref, bf16[160,8192]{1,0:T(8,128)(2,1)} %refs_0_.17, bf16[160,8192]{1,0:T(8,128)(2,1)} %collective-permute-done.9.refs_1_, bf16[160,32768]{1,0:T(8,128)(2,1)} %refs_0_.16, ...), custom_call_target="tpu_custom_call" | custom-call | flops 419430400 | bytes 4259840 | tf_op jit(solution)/shard_map/step/pallas_call | solution.py:59
  72.1 0.0 collective-permute-done.12.refs_4_
  72.1 1.6 %collective-permute-start.14 = (bf16[1280,256]{1,0:T(8,128)(2,1)S(1)}, bf16[1280,256]{1,0:T(8,128)(2,1)S(1)}, u32[]{:S(2)}, u32[]{:S(2)}) collective-permute-start(bf16[1280,256]{1,0:T(8,128)(2,1)S(1)} %collective-permute-done.12.refs_4_), channel_id=1, source_target_pairs={{2,6},{3,1},{6,10},{7,3},{10,14},{11,7},{14,12},{15,11},{12,8},{13... | collective-permute-start | bytes 1966088 | tf_op jit(solution)/shard_map/ppermute | solution.py:204
  73.7 4.6 %collective-permute-done.11.refs_5_ = bf16[1280,256]{1,0:T(8,128)(2,1)S(1)} collective-permute-done((bf16[1280,256]{1,0:T(8,128)(2,1)}, bf16[1280,256]{1,0:T(8,128)(2,1)S(1)}, u32[]{:S(2)}, u32[]{:S(2)}) %collective-permute-start.11) | collective-permute-done | bytes 655392 | tf_op jit(solution)/shard_map/ppermute | solution.py:204
  78.4 1.9 %collective-permute-start.13 = (bf16[1280,256]{1,0:T(8,128)(2,1)S(1)}, bf16[1280,256]{1,0:T(8,128)(2,1)S(1)}, u32[]{:S(2)}, u32[]{:S(2)}) collective-permute-start(bf16[1280,256]{1,0:T(8,128)(2,1)S(1)} %collective-permute-done.11.refs_5_), channel_id=1, source_target_pairs={{2,6},{3,1},{6,10},{7,3},{10,14},{11,7},{14,12},{15,11},{12,8},{13... | collective-permute-start | bytes 1966088 | tf_op jit(solution)/shard_map/ppermute | solution.py:204
  80.3 2.8 %step.12 = (f32[320,256]{1,0:T(8,128)S(1)}, f32[320,256]{1,0:T(8,128)S(1)}) custom-call(s32[8]{0:T(128)S(1)} %dynamic-slice_bitcast_fusion.order_ref, bf16[160,8192]{1,0:T(8,128)(2,1)} %refs_0_.17, bf16[160,8192]{1,0:T(8,128)(2,1)} %collective-permute-done.9.refs_1_, bf16[160,32768]{1,0:T(8,128)(2,1)} %refs_0_.16, ...), custom_call_target="tpu_custom_call" | custom-call | flops 419430400 | bytes 4259840 | tf_op jit(solution)/shard_map/step/pallas_call | solution.py:59
  83.0 0.0 copy-done.7
  83.1 2.8 %step.13 = (f32[320,256]{1,0:T(8,128)S(1)}, f32[320,256]{1,0:T(8,128)S(1)}) custom-call(s32[8]{0:T(128)S(1)} %dynamic-slice_bitcast_fusion.order_ref, bf16[160,8192]{1,0:T(8,128)(2,1)} %refs_0_.17, bf16[160,8192]{1,0:T(8,128)(2,1)} %collective-permute-done.9.refs_1_, bf16[160,32768]{1,0:T(8,128)(2,1)} %refs_0_.16, ...), custom_call_target="tpu_custom_call" | custom-call | flops 419430400 | bytes 4259840 | tf_op jit(solution)/shard_map/step/pallas_call | solution.py:59
  85.8 0.0 collective-permute-done.14.refs_4_
  85.9 1.6 %collective-permute-start.16 = (bf16[1280,256]{1,0:T(8,128)(2,1)S(1)}, bf16[1280,256]{1,0:T(8,128)(2,1)S(1)}, u32[]{:S(2)}, u32[]{:S(2)}) collective-permute-start(bf16[1280,256]{1,0:T(8,128)(2,1)S(1)} %collective-permute-done.14.refs_4_), channel_id=1, source_target_pairs={{2,6},{3,1},{6,10},{7,3},{10,14},{11,7},{14,12},{15,11},{12,8},{13... | collective-permute-start | bytes 1966088 | tf_op jit(solution)/shard_map/ppermute | solution.py:204
  87.5 1.9 %window.1.window_ref = bf16[320,768]{1,0:T(8,128)(2,1)S(1)} custom-call(s32[8]{0:T(128)S(1)} %dynamic-slice_bitcast_fusion.order_ref, bf16[160,32768]{1,0:T(8,128)(2,1)} %refs_0_.16, bf16[160,32768]{1,0:T(8,128)(2,1)} %collective-permute-done.10.refs_3_.sib_ref.refs_1_), custom_call_target="tpu_custom_call" | custom-call | bytes 1802240 | tf_op jit(solution)/shard_map/window/pallas_call | solution.py:59
  89.3 3.1 %collective-permute-done.13.refs_5_ = bf16[1280,256]{1,0:T(8,128)(2,1)S(1)} collective-permute-done((bf16[1280,256]{1,0:T(8,128)(2,1)S(1)}, bf16[1280,256]{1,0:T(8,128)(2,1)S(1)}, u32[]{:S(2)}, u32[]{:S(2)}) %collective-permute-start.13) | collective-permute-done | bytes 655392 | tf_op jit(solution)/shard_map/ppermute | solution.py:204
  92.4 0.0 copy-start.2
  92.5 0.0 copy-start.3
  92.5 2.0 %collective-permute-start.15 = (bf16[768,256]{1,0:T(8,128)(2,1)S(1)}, bf16[768,256]{1,0:T(8,128)(2,1)S(1)}, u32[]{:S(2)}, u32[]{:S(2)}) collective-permute-start(bf16[768,256]{1,0:T(8,128)(2,1)S(1)} %slice.11), channel_id=1, source_target_pairs={{2,6},{3,1},{6,10},{7,3},{10,14},{11,7},{14,12},{15,11},{12,8},{13... | collective-permute-start | bytes 1179656 | tf_op jit(solution)/shard_map/ppermute | solution.py:204
  94.4 0.0 copy-done.5
  94.4 2.8 %step.14 = (f32[320,256]{1,0:T(8,128)S(1)}, f32[320,256]{1,0:T(8,128)S(1)}) custom-call(s32[8]{0:T(128)S(1)} %dynamic-slice_bitcast_fusion.order_ref, bf16[160,8192]{1,0:T(8,128)(2,1)} %refs_0_.17, bf16[160,8192]{1,0:T(8,128)(2,1)} %collective-permute-done.9.refs_1_, bf16[160,32768]{1,0:T(8,128)(2,1)} %refs_0_.16, ...), custom_call_target="tpu_custom_call" | custom-call | flops 419430400 | bytes 4259840 | tf_op jit(solution)/shard_map/step/pallas_call | solution.py:59
  97.2 0.0 copy-done.2
  97.2 0.0 copy-done.3
  97.2 1.8 %turned.1.own_ref = f32[328,256]{1,0:T(8,128)S(1)} custom-call(s32[8]{0:T(128)S(1)} %dynamic-slice_bitcast_fusion.order_ref, bf16[160,8192]{1,0:T(8,128)(2,1)} %refs_0_.17, bf16[160,8192]{1,0:T(8,128)(2,1)} %collective-permute-done.9.refs_1_, bf16[512,256]{1,0:T(8,128)(2,1)S(1)} %collective-permute-done.2.refs_2_, f32[320,256]{1,0:T(8,128)S(1)} %get-tuple-element.82.refs_3_, ...), custom_call_target="tpu_custom_call" | custom-call | flops 83886080 | bytes 1253376 | tf_op jit(solution)/shard_map/turned/pallas_call | solution.py:59
  99.0 0.1 collective-permute-start.17
  99.1 1.6 %collective-permute-done.17.got_ref = f32[328,256]{1,0:T(8,128)S(1)} collective-permute-done((f32[328,256]{1,0:T(8,128)S(1)}, f32[328,256]{1,0:T(8,128)S(1)}, u32[]{:S(2)}, u32[]{:S(2)}) %collective-permute-start.17) | collective-permute-done | bytes 335904 | tf_op jit(solution)/shard_map/ppermute | solution.py:205
  100.7 0.6 masked.1.inn_ref
  101.4 0.0 collective-permute-done.16.refs_2_
  101.4 2.2 %step.15.total_ref = f32[320,256]{1,0:T(8,128)S(1)} custom-call(s32[8]{0:T(128)S(1)} %dynamic-slice_bitcast_fusion.order_ref, bf16[160,32768]{1,0:T(8,128)(2,1)} %refs_0_.16, bf16[160,32768]{1,0:T(8,128)(2,1)} %collective-permute-done.10.refs_3_.sib_ref.refs_1_, bf16[1280,256]{1,0:T(8,128)(2,1)S(1)} %collective-permute-done.16.refs_2_, ...), custom_call_target="tpu_custom_call" | custom-call | flops 209715200 | bytes 2621440 | tf_op jit(solution)/shard_map/step/pallas_call | solution.py:59
  103.6 0.0 collective-permute-done.15.block_ref
  103.6 0.6 score.1
  104.2 12.7 %all_to_all.5 = f32[16,2,8]{2,1,0:T(2,128)S(1)} all-to-all(f32[16,2,8]{2,1,0:T(2,128)S(1)} %bitcast.3), channel_id=1, replica_groups=mesh['groups'=2,'dp'=16] {'dp'}, dimensions={0} | all-to-all | bytes 2048 | tf_op jit(solution)/shard_map/all_to_all | solution.py:274
  116.9 0.6 reduce_sum.9
  (7 shorter events, 0.1 us)
Async XLA Ops:
  0.0 53.0 %copy-start = (bf16[2048,256]{1,0:T(8,128)(2,1)S(1)}, bf16[2048,256]{1,0:T(8,128)(2,1)}, u32[]{:S(2)}) copy-start(bf16[2048,256]{1,0:T(8,128)(2,1)} %refs_4_.2) | copy-start | bytes 3145732
  0.0 53.0 %copy-start.1 = (bf16[512,256]{1,0:T(8,128)(2,1)S(1)}, bf16[512,256]{1,0:T(8,128)(2,1)}, u32[]{:S(2)}) copy-start(bf16[512,256]{1,0:T(8,128)(2,1)} %refs_5_.2) | copy-start | bytes 786436
  0.0 53.0 %collective-permute-start.10 = (bf16[160,32768]{1,0:T(8,128)(2,1)}, bf16[160,32768]{1,0:T(8,128)(2,1)}, u32[]{:S(2)}, u32[]{:S(2)}) collective-permute-start(bf16[160,32768]{1,0:T(8,128)(2,1)} %refs_0_.16), channel_id=1, source_target_pairs={{0,1},{1,0},{2,3},{3,2},{4,5},{5,4},{6,7},{7,6},{8,9},{9,8},{10,11... | collective-permute-start | bytes 31457288 | tf_op jit(solution)/shard_map/ppermute | solution.py:205
  0.5 15.6 %collective-permute-start.1 = (bf16[2048,256]{1,0:T(8,128)(2,1)}, bf16[2048,256]{1,0:T(8,128)(2,1)S(1)}, u32[]{:S(2)}, u32[]{:S(2)}) collective-permute-start(bf16[2048,256]{1,0:T(8,128)(2,1)} %refs_4_.2), channel_id=1, source_target_pairs={{2,6},{3,1},{6,10},{7,3},{10,14},{11,7},{14,12},{15,11},{12,8},{13... | collective-permute-start | bytes 3145736 | tf_op jit(solution)/shard_map/ppermute | solution.py:204
  3.0 49.9 %collective-permute-start.9 = (bf16[160,8192]{1,0:T(8,128)(2,1)}, bf16[160,8192]{1,0:T(8,128)(2,1)}, u32[]{:S(2)}, u32[]{:S(2)}) collective-permute-start(bf16[160,8192]{1,0:T(8,128)(2,1)} %refs_0_.17), channel_id=1, source_target_pairs={{0,1},{1,0},{2,3},{3,2},{4,5},{5,4},{6,7},{7,6},{8,9},{9,8},{10,11... | collective-permute-start | bytes 7864328 | tf_op jit(solution)/shard_map/ppermute | solution.py:205
  3.3 15.7 %collective-permute-start = (bf16[512,256]{1,0:T(8,128)(2,1)}, bf16[512,256]{1,0:T(8,128)(2,1)S(1)}, u32[]{:S(2)}, u32[]{:S(2)}) collective-permute-start(bf16[512,256]{1,0:T(8,128)(2,1)} %refs_5_.2), channel_id=1, source_target_pairs={{2,6},{3,1},{6,10},{7,3},{10,14},{11,7},{14,12},{15,11},{12,8},{13... | collective-permute-start | bytes 786440 | tf_op jit(solution)/shard_map/ppermute | solution.py:204
  16.1 9.2 %collective-permute-start.2 = (bf16[512,256]{1,0:T(8,128)(2,1)}, bf16[512,256]{1,0:T(8,128)(2,1)S(1)}, u32[]{:S(2)}, u32[]{:S(2)}) collective-permute-start(bf16[512,256]{1,0:T(8,128)(2,1)} %refs_5_.2), channel_id=1, source_target_pairs={{6,2},{1,3},{10,6},{3,7},{14,10},{7,11},{12,14},{11,15},{8,12},{15... | collective-permute-start | bytes 786440 | tf_op jit(solution)/shard_map/ppermute | solution.py:223
  18.1 10.6 %collective-permute-start.6 = (bf16[1280,256]{1,0:T(8,128)(2,1)S(1)}, bf16[1280,256]{1,0:T(8,128)(2,1)S(1)}, u32[]{:S(2)}, u32[]{:S(2)}) collective-permute-start(bf16[1280,256]{1,0:T(8,128)(2,1)S(1)} %slice.10.refs_4_), channel_id=1, source_target_pairs={{2,6},{3,1},{6,10},{7,3},{10,14},{11,7},{14,12},{15,11},{12,8},{13... | collective-permute-start | bytes 1966088 | tf_op jit(solution)/shard_map/ppermute | solution.py:204
  25.3 12.8 %copy-start.4 = (bf16[1280,256]{1,0:T(8,128)(2,1)}, bf16[1280,256]{1,0:T(8,128)(2,1)S(1)}, u32[]{:S(2)}) copy-start(bf16[1280,256]{1,0:T(8,128)(2,1)S(1)} %pad_maximum_fusion.refs_5_) | copy-start | bytes 1966084
  25.3 10.9 %collective-permute-start.3 = (bf16[1280,256]{1,0:T(8,128)(2,1)S(1)}, bf16[1280,256]{1,0:T(8,128)(2,1)S(1)}, u32[]{:S(2)}, u32[]{:S(2)}) collective-permute-start(bf16[1280,256]{1,0:T(8,128)(2,1)S(1)} %pad_maximum_fusion.refs_5_), channel_id=1, source_target_pairs={{2,6},{3,1},{6,10},{7,3},{10,14},{11,7},{14,12},{15,11},{12,8},{13... | collective-permute-start | bytes 1966088 | tf_op jit(solution)/shard_map/ppermute | solution.py:204
  28.8 14.6 %collective-permute-start.7 = (bf16[1280,256]{1,0:T(8,128)(2,1)S(1)}, bf16[1280,256]{1,0:T(8,128)(2,1)}, u32[]{:S(2)}, u32[]{:S(2)}) collective-permute-start(bf16[1280,256]{1,0:T(8,128)(2,1)S(1)} %collective-permute-done.6.refs_4_), channel_id=1, source_target_pairs={{2,6},{3,1},{6,10},{7,3},{10,14},{11,7},{14,12},{15,11},{12,8},{13... | collective-permute-start | bytes 1966088 | tf_op jit(solution)/shard_map/ppermute | solution.py:204
  36.2 7.1 %copy-start.6 = (bf16[1280,256]{1,0:T(8,128)(2,1)}, bf16[1280,256]{1,0:T(8,128)(2,1)S(1)}, u32[]{:S(2)}) copy-start(bf16[1280,256]{1,0:T(8,128)(2,1)S(1)} %collective-permute-done.3.refs_5_) | copy-start | bytes 1966084
  36.2 14.1 %collective-permute-start.4 = (bf16[1280,256]{1,0:T(8,128)(2,1)S(1)}, bf16[1280,256]{1,0:T(8,128)(2,1)}, u32[]{:S(2)}, u32[]{:S(2)}) collective-permute-start(bf16[1280,256]{1,0:T(8,128)(2,1)S(1)} %collective-permute-done.3.refs_5_), channel_id=1, source_target_pairs={{2,6},{3,1},{6,10},{7,3},{10,14},{11,7},{14,12},{15,11},{12,8},{13... | collective-permute-start | bytes 1966088 | tf_op jit(solution)/shard_map/ppermute | solution.py:204
  43.4 15.0 %collective-permute-start.8 = (bf16[1280,256]{1,0:T(8,128)(2,1)}, bf16[1280,256]{1,0:T(8,128)(2,1)S(1)}, u32[]{:S(2)}, u32[]{:S(2)}) collective-permute-start(bf16[1280,256]{1,0:T(8,128)(2,1)} %collective-permute-done.7.refs_4_), channel_id=1, source_target_pairs={{2,6},{3,1},{6,10},{7,3},{10,14},{11,7},{14,12},{15,11},{12,8},{13... | collective-permute-start | bytes 1966088 | tf_op jit(solution)/shard_map/ppermute | solution.py:204
  50.4 14.0 %collective-permute-start.5 = (bf16[1280,256]{1,0:T(8,128)(2,1)}, bf16[1280,256]{1,0:T(8,128)(2,1)}, u32[]{:S(2)}, u32[]{:S(2)}) collective-permute-start(bf16[1280,256]{1,0:T(8,128)(2,1)} %collective-permute-done.4.refs_5_), channel_id=1, source_target_pairs={{2,6},{3,1},{6,10},{7,3},{10,14},{11,7},{14,12},{15,11},{12,8},{13... | collective-permute-start | bytes 1966088 | tf_op jit(solution)/shard_map/ppermute | solution.py:204
  58.4 13.7 %collective-permute-start.12 = (bf16[1280,256]{1,0:T(8,128)(2,1)S(1)}, bf16[1280,256]{1,0:T(8,128)(2,1)S(1)}, u32[]{:S(2)}, u32[]{:S(2)}) collective-permute-start(bf16[1280,256]{1,0:T(8,128)(2,1)S(1)} %collective-permute-done.8.refs_4_), channel_id=1, source_target_pairs={{2,6},{3,1},{6,10},{7,3},{10,14},{11,7},{14,12},{15,11},{12,8},{13... | collective-permute-start | bytes 1966088 | tf_op jit(solution)/shard_map/ppermute | solution.py:204
  64.4 13.9 %collective-permute-start.11 = (bf16[1280,256]{1,0:T(8,128)(2,1)}, bf16[1280,256]{1,0:T(8,128)(2,1)S(1)}, u32[]{:S(2)}, u32[]{:S(2)}) collective-permute-start(bf16[1280,256]{1,0:T(8,128)(2,1)} %collective-permute-done.5.refs_5_), channel_id=1, source_target_pairs={{2,6},{3,1},{6,10},{7,3},{10,14},{11,7},{14,12},{15,11},{12,8},{13... | collective-permute-start | bytes 1966088 | tf_op jit(solution)/shard_map/ppermute | solution.py:204
  72.1 13.8 %collective-permute-start.14 = (bf16[1280,256]{1,0:T(8,128)(2,1)S(1)}, bf16[1280,256]{1,0:T(8,128)(2,1)S(1)}, u32[]{:S(2)}, u32[]{:S(2)}) collective-permute-start(bf16[1280,256]{1,0:T(8,128)(2,1)S(1)} %collective-permute-done.12.refs_4_), channel_id=1, source_target_pairs={{2,6},{3,1},{6,10},{7,3},{10,14},{11,7},{14,12},{15,11},{12,8},{13... | collective-permute-start | bytes 1966088 | tf_op jit(solution)/shard_map/ppermute | solution.py:204
  78.4 4.7 %copy-start.7 = (bf16[1280,256]{1,0:T(8,128)(2,1)}, bf16[1280,256]{1,0:T(8,128)(2,1)S(1)}, u32[]{:S(2)}) copy-start(bf16[1280,256]{1,0:T(8,128)(2,1)S(1)} %collective-permute-done.11.refs_5_) | copy-start | bytes 1966084
  78.4 14.0 %collective-permute-start.13 = (bf16[1280,256]{1,0:T(8,128)(2,1)S(1)}, bf16[1280,256]{1,0:T(8,128)(2,1)S(1)}, u32[]{:S(2)}, u32[]{:S(2)}) collective-permute-start(bf16[1280,256]{1,0:T(8,128)(2,1)S(1)} %collective-permute-done.11.refs_5_), channel_id=1, source_target_pairs={{2,6},{3,1},{6,10},{7,3},{10,14},{11,7},{14,12},{15,11},{12,8},{13... | collective-permute-start | bytes 1966088 | tf_op jit(solution)/shard_map/ppermute | solution.py:204
  85.9 15.5 %collective-permute-start.16 = (bf16[1280,256]{1,0:T(8,128)(2,1)S(1)}, bf16[1280,256]{1,0:T(8,128)(2,1)S(1)}, u32[]{:S(2)}, u32[]{:S(2)}) collective-permute-start(bf16[1280,256]{1,0:T(8,128)(2,1)S(1)} %collective-permute-done.14.refs_4_), channel_id=1, source_target_pairs={{2,6},{3,1},{6,10},{7,3},{10,14},{11,7},{14,12},{15,11},{12,8},{13... | collective-permute-start | bytes 1966088 | tf_op jit(solution)/shard_map/ppermute | solution.py:204
  92.4 2.0 %copy-start.5 = (bf16[1280,256]{1,0:T(8,128)(2,1)}, bf16[1280,256]{1,0:T(8,128)(2,1)S(1)}, u32[]{:S(2)}) copy-start(bf16[1280,256]{1,0:T(8,128)(2,1)S(1)} %collective-permute-done.13.refs_5_) | copy-start | bytes 1966084
  92.4 4.8 %copy-start.2 = (s32[2]{0:T(128)S(1)}, s32[2]{0:T(128)}, u32[]{:S(2)}) copy-start(s32[2]{0:T(128)} %refs_4_.3) | copy-start | bytes 28
  92.5 4.8 %copy-start.3 = (s32[2]{0:T(128)S(1)}, s32[2]{0:T(128)}, u32[]{:S(2)}) copy-start(s32[2]{0:T(128)} %refs_5_.3) | copy-start | bytes 28
  92.5 11.2 %collective-permute-start.15 = (bf16[768,256]{1,0:T(8,128)(2,1)S(1)}, bf16[768,256]{1,0:T(8,128)(2,1)S(1)}, u32[]{:S(2)}, u32[]{:S(2)}) collective-permute-start(bf16[768,256]{1,0:T(8,128)(2,1)S(1)} %slice.11), channel_id=1, source_target_pairs={{2,6},{3,1},{6,10},{7,3},{10,14},{11,7},{14,12},{15,11},{12,8},{13... | collective-permute-start | bytes 1179656 | tf_op jit(solution)/shard_map/ppermute | solution.py:204
  99.0 1.7 %collective-permute-start.17 = (f32[328,256]{1,0:T(8,128)S(1)}, f32[328,256]{1,0:T(8,128)S(1)}, u32[]{:S(2)}, u32[]{:S(2)}) collective-permute-start(f32[328,256]{1,0:T(8,128)S(1)} %turned.1.own_ref), channel_id=1, source_target_pairs={{0,1},{1,0},{2,3},{3,2},{4,5},{5,4},{6,7},{7,6},{8,9},{9,8},{10,11... | collective-permute-start | bytes 1007624 | tf_op jit(solution)/shard_map/ppermute | solution.py:205

commit v16 on v15

--- a/solution.py
+++ b/solution.py
@@ -271,8 +271,15 @@
 
     queries = columns // RANK
     table = score_table([window, early, totals["out"], inn], slots * devices, queries)
-    got = lax.all_to_all(table.reshape(devices, slots, queries), "dp", 0, 0, tiled=True)
-    return jnp.sum(got, axis=0)
+    groups = [list(range(core, devices, 2)) for core in (0, 1)]
+    got = lax.all_to_all(
+        table.reshape(chips, 2 * slots, queries), "dp", 0, 0, axis_index_groups=groups, tiled=True
+    )
+    got = jnp.sum(got, axis=0)
+    first = me % 2 == 0
+    keep = jnp.where(first, got[:slots], got[slots:])
+    give = jnp.where(first, got[slots:], got[:slots])
+    return keep + across(give)
 
 
 def solution(mesh):

time: 118 us -> 120 us (1.017)
  blocking collectives: 12.7 us -> 0 us
  waiting for transfers between devices: 49.4 us -> 57.1 us
  starting transfers between devices: 27.2 us -> 33.5 us
    all_to_all x1 -> x0, blocking collectives: 12.7 us -> none  [shards(): lax.all_to_all(table.reshape(devices, slots, queries), 'dp', 0, 0, tiled=...]
    all_to_all x0 -> x1, waiting for transfers between devices: none -> 6.58 us  [shards(): lax.all_to_all(table.reshape(chips, 2 * slots, queries), 'dp', 0, 0, axis...]
    all_to_all x0 -> x1, starting transfers between devices: none -> 6.25 us  [shards(): lax.all_to_all(table.reshape(chips, 2 * slots, queries), 'dp', 0, 0, axis...]
    ppermute x3 -> x4, waiting for transfers between devices: 1.63 us -> 2.76 us  [shards(): across = lambda x: lax.ppermute(x, 'dp', swap)]
  transfers between devices with their start and end apart: 18 -> 20, of which waited for: 11 -> 13; matrix products, arithmetic and copies ran while one was open for 1% -> 1% of each run, Pallas kernels for 22% -> 22%
where the time goes in v16:
time: 120 us; the launch traced here: 119 us
  waiting for transfers between devices  57.1 us (48%)
  starting transfers between devices  33.5 us (28%)
  Pallas kernels  27.1 us (23%)
    ppermute x14, waiting for transfers between devices, shards(): send = lambda x: lax.ppermute(x, 'dp', pairs)  41.5 us
    pallas_call x11, Pallas kernels, call(): pl.pallas_call(kernel, grid_spec=pltpu.PrefetchScalarGridSpec(num_scalar_...  25.9 us
    ppermute x14, starting transfers between devices, shards(): send = lambda x: lax.ppermute(x, 'dp', pairs)  24.4 us
    all_to_all x1, waiting for transfers between devices, shards(): lax.all_to_all(table.reshape(chips, 2 * slots, queries), 'dp', 0, 0, axis...  6.58 us
    ppermute x1, waiting for transfers between devices, shards(): turned = lax.ppermute(turned, 'dp', [(j, i) for i, j in pairs])  6.32 us
    all_to_all x1, starting transfers between devices, shards(): lax.all_to_all(table.reshape(chips, 2 * slots, queries), 'dp', 0, 0, axis...  6.25 us
    ppermute x4, waiting for transfers between devices, shards(): across = lambda x: lax.ppermute(x, 'dp', swap)  2.76 us
  transfers between devices with their start and end apart: 20, of which 13 were waited for; matrix products, arithmetic and copies ran while one was open for 1% of the time, Pallas kernels for 22%

profile of v16, /device:TPU:0, one launch (start us, length us, event | category | flops | bytes accessed | tf_op | source)
XLA Modules:
  0.0 119.5 jit_solution(13770760840510554291)
XLA Ops:
  0.0 0.5 collective-permute-start.10
  0.5 2.6 %collective-permute-start.1 = (bf16[2048,256]{1,0:T(8,128)(2,1)}, bf16[2048,256]{1,0:T(8,128)(2,1)S(1)}, u32[]{:S(2)}, u32[]{:S(2)}) collective-permute-start(bf16[2048,256]{1,0:T(8,128)(2,1)} %refs_4_.2), channel_id=1, source_target_pairs={{2,6},{3,1},{6,10},{7,3},{10,14},{11,7},{14,12},{15,11},{12,8},{13... | collective-permute-start | bytes 3145736 | tf_op jit(solution)/shard_map/ppermute | solution.py:204
  3.0 0.2 collective-permute-start.9
  3.3 1.4 %collective-permute-start = (bf16[512,256]{1,0:T(8,128)(2,1)}, bf16[512,256]{1,0:T(8,128)(2,1)S(1)}, u32[]{:S(2)}, u32[]{:S(2)}) collective-permute-start(bf16[512,256]{1,0:T(8,128)(2,1)} %refs_5_.2), channel_id=1, source_target_pairs={{2,6},{3,1},{6,10},{7,3},{10,14},{11,7},{14,12},{15,11},{12,8},{13... | collective-permute-start | bytes 786440 | tf_op jit(solution)/shard_map/ppermute | solution.py:204
  4.6 11.5 %collective-permute-done.1 = bf16[2048,256]{1,0:T(8,128)(2,1)S(1)} collective-permute-done((bf16[2048,256]{1,0:T(8,128)(2,1)}, bf16[2048,256]{1,0:T(8,128)(2,1)S(1)}, u32[]{:S(2)}, u32[]{:S(2)}) %collective-permute-start.1) | collective-permute-done | bytes 1048608 | tf_op jit(solution)/shard_map/ppermute | solution.py:204
  16.1 2.0 %collective-permute-start.2 = (bf16[512,256]{1,0:T(8,128)(2,1)}, bf16[512,256]{1,0:T(8,128)(2,1)S(1)}, u32[]{:S(2)}, u32[]{:S(2)}) collective-permute-start(bf16[512,256]{1,0:T(8,128)(2,1)} %refs_5_.2), channel_id=1, source_target_pairs={{6,2},{1,3},{10,6},{3,7},{14,10},{7,11},{12,14},{11,15},{8,12},{15... | collective-permute-start | bytes 786440 | tf_op jit(solution)/shard_map/ppermute | solution.py:223
  18.1 0.1 collective-permute-start.6
  18.3 0.7 collective-permute-done
  19.0 6.3 %collective-permute-done.2.refs_2_ = bf16[512,256]{1,0:T(8,128)(2,1)S(1)} collective-permute-done((bf16[512,256]{1,0:T(8,128)(2,1)}, bf16[512,256]{1,0:T(8,128)(2,1)S(1)}, u32[]{:S(2)}, u32[]{:S(2)}) %collective-permute-start.2) | collective-permute-done | bytes 262176 | tf_op jit(solution)/shard_map/ppermute | solution.py:223
  25.3 0.0 copy-start.4
  25.3 2.2 %collective-permute-start.3 = (bf16[1280,256]{1,0:T(8,128)(2,1)S(1)}, bf16[1280,256]{1,0:T(8,128)(2,1)S(1)}, u32[]{:S(2)}, u32[]{:S(2)}) collective-permute-start(bf16[1280,256]{1,0:T(8,128)(2,1)S(1)} %pad_maximum_fusion.refs_5_), channel_id=1, source_target_pairs={{2,6},{3,1},{6,10},{7,3},{10,14},{11,7},{14,12},{15,11},{12,8},{13... | collective-permute-start | bytes 1966088 | tf_op jit(solution)/shard_map/ppermute | solution.py:204
  27.5 1.2 %collective-permute-done.6.refs_4_ = bf16[1280,256]{1,0:T(8,128)(2,1)S(1)} collective-permute-done((bf16[1280,256]{1,0:T(8,128)(2,1)S(1)}, bf16[1280,256]{1,0:T(8,128)(2,1)S(1)}, u32[]{:S(2)}, u32[]{:S(2)}) %collective-permute-start.6) | collective-permute-done | bytes 655392 | tf_op jit(solution)/shard_map/ppermute | solution.py:204
  28.8 1.9 %collective-permute-start.7 = (bf16[1280,256]{1,0:T(8,128)(2,1)S(1)}, bf16[1280,256]{1,0:T(8,128)(2,1)}, u32[]{:S(2)}, u32[]{:S(2)}) collective-permute-start(bf16[1280,256]{1,0:T(8,128)(2,1)S(1)} %collective-permute-done.6.refs_4_), channel_id=1, source_target_pairs={{2,6},{3,1},{6,10},{7,3},{10,14},{11,7},{14,12},{15,11},{12,8},{13... | collective-permute-start | bytes 1966088 | tf_op jit(solution)/shard_map/ppermute | solution.py:204
  30.7 5.5 %collective-permute-done.3.refs_5_ = bf16[1280,256]{1,0:T(8,128)(2,1)S(1)} collective-permute-done((bf16[1280,256]{1,0:T(8,128)(2,1)S(1)}, bf16[1280,256]{1,0:T(8,128)(2,1)S(1)}, u32[]{:S(2)}, u32[]{:S(2)}) %collective-permute-start.3) | collective-permute-done | bytes 655392 | tf_op jit(solution)/shard_map/ppermute | solution.py:204
  36.2 1.9 %collective-permute-start.4 = (bf16[1280,256]{1,0:T(8,128)(2,1)S(1)}, bf16[1280,256]{1,0:T(8,128)(2,1)}, u32[]{:S(2)}, u32[]{:S(2)}) collective-permute-start(bf16[1280,256]{1,0:T(8,128)(2,1)S(1)} %collective-permute-done.3.refs_5_), channel_id=1, source_target_pairs={{2,6},{3,1},{6,10},{7,3},{10,14},{11,7},{14,12},{15,11},{12,8},{13... | collective-permute-start | bytes 1966088 | tf_op jit(solution)/shard_map/ppermute | solution.py:204
  38.1 0.0 copy-done.4
  38.1 5.2 %collective-permute-done.7.refs_4_ = bf16[1280,256]{1,0:T(8,128)(2,1)} collective-permute-done((bf16[1280,256]{1,0:T(8,128)(2,1)S(1)}, bf16[1280,256]{1,0:T(8,128)(2,1)}, u32[]{:S(2)}, u32[]{:S(2)}) %collective-permute-start.7) | collective-permute-done | bytes 655392 | tf_op jit(solution)/shard_map/ppermute | solution.py:204
  43.4 0.0 copy-done.6
  43.4 1.9 %collective-permute-start.8 = (bf16[1280,256]{1,0:T(8,128)(2,1)}, bf16[1280,256]{1,0:T(8,128)(2,1)S(1)}, u32[]{:S(2)}, u32[]{:S(2)}) collective-permute-start(bf16[1280,256]{1,0:T(8,128)(2,1)} %collective-permute-done.7.refs_4_), channel_id=1, source_target_pairs={{2,6},{3,1},{6,10},{7,3},{10,14},{11,7},{14,12},{15,11},{12,8},{13... | collective-permute-start | bytes 1966088 | tf_op jit(solution)/shard_map/ppermute | solution.py:204
  45.3 5.1 %collective-permute-done.4.refs_5_ = bf16[1280,256]{1,0:T(8,128)(2,1)} collective-permute-done((bf16[1280,256]{1,0:T(8,128)(2,1)S(1)}, bf16[1280,256]{1,0:T(8,128)(2,1)}, u32[]{:S(2)}, u32[]{:S(2)}) %collective-permute-start.4) | collective-permute-done | bytes 655392 | tf_op jit(solution)/shard_map/ppermute | solution.py:204
  50.4 1.9 %collective-permute-start.5 = (bf16[1280,256]{1,0:T(8,128)(2,1)}, bf16[1280,256]{1,0:T(8,128)(2,1)}, u32[]{:S(2)}, u32[]{:S(2)}) collective-permute-start(bf16[1280,256]{1,0:T(8,128)(2,1)} %collective-permute-done.4.refs_5_), channel_id=1, source_target_pairs={{2,6},{3,1},{6,10},{7,3},{10,14},{11,7},{14,12},{15,11},{12,8},{13... | collective-permute-start | bytes 1966088 | tf_op jit(solution)/shard_map/ppermute | solution.py:204
  52.3 0.7 dynamic-slice_bitcast_fusion.order_ref
  53.0 0.0 collective-permute-done.9.refs_1_
  53.0 0.0 collective-permute-done.10.refs_3_.sib_ref.refs_1_
  53.0 0.0 copy-done
  53.0 0.0 copy-done.1
  53.0 2.6 %step.8 = (f32[320,256]{1,0:T(8,128)S(1)}, f32[320,256]{1,0:T(8,128)S(1)}) custom-call(s32[8]{0:T(128)S(1)} %dynamic-slice_bitcast_fusion.order_ref, bf16[160,8192]{1,0:T(8,128)(2,1)} %refs_0_.17, bf16[160,8192]{1,0:T(8,128)(2,1)} %collective-permute-done.9.refs_1_, bf16[160,32768]{1,0:T(8,128)(2,1)} %refs_0_.16, ...), custom_call_target="tpu_custom_call" | custom-call | flops 419430400 | bytes 3604480 | tf_op jit(solution)/shard_map/step/pallas_call | solution.py:59
  55.6 2.8 %step.9 = (f32[320,256]{1,0:T(8,128)S(1)}, f32[320,256]{1,0:T(8,128)S(1)}) custom-call(s32[8]{0:T(128)S(1)} %dynamic-slice_bitcast_fusion.order_ref, bf16[160,8192]{1,0:T(8,128)(2,1)} %refs_0_.17, bf16[160,8192]{1,0:T(8,128)(2,1)} %collective-permute-done.9.refs_1_, bf16[160,32768]{1,0:T(8,128)(2,1)} %refs_0_.16, ...), custom_call_target="tpu_custom_call" | custom-call | flops 419430400 | bytes 4259840 | tf_op jit(solution)/shard_map/step/pallas_call | solution.py:59
  58.4 0.0 collective-permute-done.8.refs_4_
  58.4 1.6 %collective-permute-start.12 = (bf16[1280,256]{1,0:T(8,128)(2,1)S(1)}, bf16[1280,256]{1,0:T(8,128)(2,1)S(1)}, u32[]{:S(2)}, u32[]{:S(2)}) collective-permute-start(bf16[1280,256]{1,0:T(8,128)(2,1)S(1)} %collective-permute-done.8.refs_4_), channel_id=1, source_target_pairs={{2,6},{3,1},{6,10},{7,3},{10,14},{11,7},{14,12},{15,11},{12,8},{13... | collective-permute-start | bytes 1966088 | tf_op jit(solution)/shard_map/ppermute | solution.py:204
  60.0 4.4 %collective-permute-done.5.refs_5_ = bf16[1280,256]{1,0:T(8,128)(2,1)} collective-permute-done((bf16[1280,256]{1,0:T(8,128)(2,1)}, bf16[1280,256]{1,0:T(8,128)(2,1)}, u32[]{:S(2)}, u32[]{:S(2)}) %collective-permute-start.5) | collective-permute-done | bytes 655392 | tf_op jit(solution)/shard_map/ppermute | solution.py:204
  64.4 1.9 %collective-permute-start.11 = (bf16[1280,256]{1,0:T(8,128)(2,1)}, bf16[1280,256]{1,0:T(8,128)(2,1)S(1)}, u32[]{:S(2)}, u32[]{:S(2)}) collective-permute-start(bf16[1280,256]{1,0:T(8,128)(2,1)} %collective-permute-done.5.refs_5_), channel_id=1, source_target_pairs={{2,6},{3,1},{6,10},{7,3},{10,14},{11,7},{14,12},{15,11},{12,8},{13... | collective-permute-start | bytes 1966088 | tf_op jit(solution)/shard_map/ppermute | solution.py:204
  66.3 2.8 %step.10 = (f32[320,256]{1,0:T(8,128)S(1)}, f32[320,256]{1,0:T(8,128)S(1)}) custom-call(s32[8]{0:T(128)S(1)} %dynamic-slice_bitcast_fusion.order_ref, bf16[160,8192]{1,0:T(8,128)(2,1)} %refs_0_.17, bf16[160,8192]{1,0:T(8,128)(2,1)} %collective-permute-done.9.refs_1_, bf16[160,32768]{1,0:T(8,128)(2,1)} %refs_0_.16, ...), custom_call_target="tpu_custom_call" | custom-call | flops 419430400 | bytes 4259840 | tf_op jit(solution)/shard_map/step/pallas_call | solution.py:59
  69.1 3.0 %step.11 = (f32[320,256]{1,0:T(8,128)S(1)}, f32[320,256]{1,0:T(8,128)S(1)}) custom-call(s32[8]{0:T(128)S(1)} %dynamic-slice_bitcast_fusion.order_ref, bf16[160,8192]{1,0:T(8,128)(2,1)} %refs_0_.17, bf16[160,8192]{1,0:T(8,128)(2,1)} %collective-permute-done.9.refs_1_, bf16[160,32768]{1,0:T(8,128)(2,1)} %refs_0_.16, ...), custom_call_target="tpu_custom_call" | custom-call | flops 419430400 | bytes 4259840 | tf_op jit(solution)/shard_map/step/pallas_call | solution.py:59
  72.1 0.0 collective-permute-done.12.refs_4_
  72.1 1.6 %collective-permute-start.14 = (bf16[1280,256]{1,0:T(8,128)(2,1)S(1)}, bf16[1280,256]{1,0:T(8,128)(2,1)S(1)}, u32[]{:S(2)}, u32[]{:S(2)}) collective-permute-start(bf16[1280,256]{1,0:T(8,128)(2,1)S(1)} %collective-permute-done.12.refs_4_), channel_id=1, source_target_pairs={{2,6},{3,1},{6,10},{7,3},{10,14},{11,7},{14,12},{15,11},{12,8},{13... | collective-permute-start | bytes 1966088 | tf_op jit(solution)/shard_map/ppermute | solution.py:204
  73.7 4.6 %collective-permute-done.11.refs_5_ = bf16[1280,256]{1,0:T(8,128)(2,1)S(1)} collective-permute-done((bf16[1280,256]{1,0:T(8,128)(2,1)}, bf16[1280,256]{1,0:T(8,128)(2,1)S(1)}, u32[]{:S(2)}, u32[]{:S(2)}) %collective-permute-start.11) | collective-permute-done | bytes 655392 | tf_op jit(solution)/shard_map/ppermute | solution.py:204
  78.4 1.9 %collective-permute-start.13 = (bf16[1280,256]{1,0:T(8,128)(2,1)S(1)}, bf16[1280,256]{1,0:T(8,128)(2,1)S(1)}, u32[]{:S(2)}, u32[]{:S(2)}) collective-permute-start(bf16[1280,256]{1,0:T(8,128)(2,1)S(1)} %collective-permute-done.11.refs_5_), channel_id=1, source_target_pairs={{2,6},{3,1},{6,10},{7,3},{10,14},{11,7},{14,12},{15,11},{12,8},{13... | collective-permute-start | bytes 1966088 | tf_op jit(solution)/shard_map/ppermute | solution.py:204
  80.3 2.8 %step.12 = (f32[320,256]{1,0:T(8,128)S(1)}, f32[320,256]{1,0:T(8,128)S(1)}) custom-call(s32[8]{0:T(128)S(1)} %dynamic-slice_bitcast_fusion.order_ref, bf16[160,8192]{1,0:T(8,128)(2,1)} %refs_0_.17, bf16[160,8192]{1,0:T(8,128)(2,1)} %collective-permute-done.9.refs_1_, bf16[160,32768]{1,0:T(8,128)(2,1)} %refs_0_.16, ...), custom_call_target="tpu_custom_call" | custom-call | flops 419430400 | bytes 4259840 | tf_op jit(solution)/shard_map/step/pallas_call | solution.py:59
  83.0 0.0 copy-done.7
  83.1 2.8 %step.13 = (f32[320,256]{1,0:T(8,128)S(1)}, f32[320,256]{1,0:T(8,128)S(1)}) custom-call(s32[8]{0:T(128)S(1)} %dynamic-slice_bitcast_fusion.order_ref, bf16[160,8192]{1,0:T(8,128)(2,1)} %refs_0_.17, bf16[160,8192]{1,0:T(8,128)(2,1)} %collective-permute-done.9.refs_1_, bf16[160,32768]{1,0:T(8,128)(2,1)} %refs_0_.16, ...), custom_call_target="tpu_custom_call" | custom-call | flops 419430400 | bytes 4259840 | tf_op jit(solution)/shard_map/step/pallas_call | solution.py:59
  85.8 0.0 collective-permute-done.14.refs_4_
  85.9 1.6 %collective-permute-start.16 = (bf16[1280,256]{1,0:T(8,128)(2,1)S(1)}, bf16[1280,256]{1,0:T(8,128)(2,1)S(1)}, u32[]{:S(2)}, u32[]{:S(2)}) collective-permute-start(bf16[1280,256]{1,0:T(8,128)(2,1)S(1)} %collective-permute-done.14.refs_4_), channel_id=1, source_target_pairs={{2,6},{3,1},{6,10},{7,3},{10,14},{11,7},{14,12},{15,11},{12,8},{13... | collective-permute-start | bytes 1966088 | tf_op jit(solution)/shard_map/ppermute | solution.py:204
  87.5 1.9 %window.1.window_ref = bf16[320,768]{1,0:T(8,128)(2,1)S(1)} custom-call(s32[8]{0:T(128)S(1)} %dynamic-slice_bitcast_fusion.order_ref, bf16[160,32768]{1,0:T(8,128)(2,1)} %refs_0_.16, bf16[160,32768]{1,0:T(8,128)(2,1)} %collective-permute-done.10.refs_3_.sib_ref.refs_1_), custom_call_target="tpu_custom_call" | custom-call | bytes 1802240 | tf_op jit(solution)/shard_map/window/pallas_call | solution.py:59
  89.3 3.1 %collective-permute-done.13.refs_5_ = bf16[1280,256]{1,0:T(8,128)(2,1)S(1)} collective-permute-done((bf16[1280,256]{1,0:T(8,128)(2,1)S(1)}, bf16[1280,256]{1,0:T(8,128)(2,1)S(1)}, u32[]{:S(2)}, u32[]{:S(2)}) %collective-permute-start.13) | collective-permute-done | bytes 655392 | tf_op jit(solution)/shard_map/ppermute | solution.py:204
  92.4 0.0 copy-start.2
  92.5 0.0 copy-start.3
  92.5 2.0 %collective-permute-start.15 = (bf16[768,256]{1,0:T(8,128)(2,1)S(1)}, bf16[768,256]{1,0:T(8,128)(2,1)S(1)}, u32[]{:S(2)}, u32[]{:S(2)}) collective-permute-start(bf16[768,256]{1,0:T(8,128)(2,1)S(1)} %slice.19), channel_id=1, source_target_pairs={{2,6},{3,1},{6,10},{7,3},{10,14},{11,7},{14,12},{15,11},{12,8},{13... | collective-permute-start | bytes 1179656 | tf_op jit(solution)/shard_map/ppermute | solution.py:204
  94.4 0.0 copy-done.5
  94.4 2.8 %step.14 = (f32[320,256]{1,0:T(8,128)S(1)}, f32[320,256]{1,0:T(8,128)S(1)}) custom-call(s32[8]{0:T(128)S(1)} %dynamic-slice_bitcast_fusion.order_ref, bf16[160,8192]{1,0:T(8,128)(2,1)} %refs_0_.17, bf16[160,8192]{1,0:T(8,128)(2,1)} %collective-permute-done.9.refs_1_, bf16[160,32768]{1,0:T(8,128)(2,1)} %refs_0_.16, ...), custom_call_target="tpu_custom_call" | custom-call | flops 419430400 | bytes 4259840 | tf_op jit(solution)/shard_map/step/pallas_call | solution.py:59
  97.2 0.0 copy-done.2
  97.2 1.8 %turned.1.own_ref = f32[328,256]{1,0:T(8,128)S(1)} custom-call(s32[8]{0:T(128)S(1)} %dynamic-slice_bitcast_fusion.order_ref, bf16[160,8192]{1,0:T(8,128)(2,1)} %refs_0_.17, bf16[160,8192]{1,0:T(8,128)(2,1)} %collective-permute-done.9.refs_1_, bf16[512,256]{1,0:T(8,128)(2,1)S(1)} %collective-permute-done.2.refs_2_, f32[320,256]{1,0:T(8,128)S(1)} %get-tuple-element.82.refs_3_, ...), custom_call_target="tpu_custom_call" | custom-call | flops 83886080 | bytes 1253376 | tf_op jit(solution)/shard_map/turned/pallas_call | solution.py:59
  99.0 0.1 collective-permute-start.17
  99.1 1.6 %collective-permute-done.17.got_ref = f32[328,256]{1,0:T(8,128)S(1)} collective-permute-done((f32[328,256]{1,0:T(8,128)S(1)}, f32[328,256]{1,0:T(8,128)S(1)}, u32[]{:S(2)}, u32[]{:S(2)}) %collective-permute-start.17) | collective-permute-done | bytes 335904 | tf_op jit(solution)/shard_map/ppermute | solution.py:205
  100.7 0.6 masked.1.inn_ref
  101.4 0.0 collective-permute-done.16.refs_2_
  101.4 2.2 %step.15.total_ref = f32[320,256]{1,0:T(8,128)S(1)} custom-call(s32[8]{0:T(128)S(1)} %dynamic-slice_bitcast_fusion.order_ref, bf16[160,32768]{1,0:T(8,128)(2,1)} %refs_0_.16, bf16[160,32768]{1,0:T(8,128)(2,1)} %collective-permute-done.10.refs_3_.sib_ref.refs_1_, bf16[1280,256]{1,0:T(8,128)(2,1)S(1)} %collective-permute-done.16.refs_2_, ...), custom_call_target="tpu_custom_call" | custom-call | flops 209715200 | bytes 2621440 | tf_op jit(solution)/shard_map/step/pallas_call | solution.py:59
  103.6 0.0 collective-permute-done.15.block_ref
  103.6 1.2 score.1
  104.8 6.2 %all-to-all-start = ((f32[8,4,8]{2,1,0:T(4,128)}), f32[8,4,8]{2,1,0:T(4,128)S(1)}, u32[]{:S(2)}, u32[]{:S(2)}) async-start(f32[8,4,8]{2,1,0:T(4,128)} %bitcast.1), calls=%async_computation | async-start | bytes 32768 | tf_op jit(solution)/shard_map/all_to_all | solution.py:275
  111.1 6.6 %all-to-all-done = f32[8,4,8]{2,1,0:T(4,128)S(1)} async-done(((f32[8,4,8]{2,1,0:T(4,128)}), f32[8,4,8]{2,1,0:T(4,128)S(1)}, u32[]{:S(2)}, u32[]{:S(2)}) %all-to-all-start) | async-done | bytes 1056 | tf_op jit(solution)/shard_map/all_to_all | solution.py:275
  117.7 0.1 collective-permute-start.18
  117.8 1.1 collective-permute-done.18
  118.9 0.6 select_add_fusion
  (12 shorter events, 0.2 us)
Async XLA Ops:
  0.0 53.0 %copy-start = (bf16[2048,256]{1,0:T(8,128)(2,1)S(1)}, bf16[2048,256]{1,0:T(8,128)(2,1)}, u32[]{:S(2)}) copy-start(bf16[2048,256]{1,0:T(8,128)(2,1)} %refs_4_.2) | copy-start | bytes 3145732
  0.0 53.0 %copy-start.1 = (bf16[512,256]{1,0:T(8,128)(2,1)S(1)}, bf16[512,256]{1,0:T(8,128)(2,1)}, u32[]{:S(2)}) copy-start(bf16[512,256]{1,0:T(8,128)(2,1)} %refs_5_.2) | copy-start | bytes 786436
  0.0 53.0 %collective-permute-start.10 = (bf16[160,32768]{1,0:T(8,128)(2,1)}, bf16[160,32768]{1,0:T(8,128)(2,1)}, u32[]{:S(2)}, u32[]{:S(2)}) collective-permute-start(bf16[160,32768]{1,0:T(8,128)(2,1)} %refs_0_.16), channel_id=1, source_target_pairs={{0,1},{1,0},{2,3},{3,2},{4,5},{5,4},{6,7},{7,6},{8,9},{9,8},{10,11... | collective-permute-start | bytes 31457288 | tf_op jit(solution)/shard_map/ppermute | solution.py:205
  0.5 15.6 %collective-permute-start.1 = (bf16[2048,256]{1,0:T(8,128)(2,1)}, bf16[2048,256]{1,0:T(8,128)(2,1)S(1)}, u32[]{:S(2)}, u32[]{:S(2)}) collective-permute-start(bf16[2048,256]{1,0:T(8,128)(2,1)} %refs_4_.2), channel_id=1, source_target_pairs={{2,6},{3,1},{6,10},{7,3},{10,14},{11,7},{14,12},{15,11},{12,8},{13... | collective-permute-start | bytes 3145736 | tf_op jit(solution)/shard_map/ppermute | solution.py:204
  3.0 49.9 %collective-permute-start.9 = (bf16[160,8192]{1,0:T(8,128)(2,1)}, bf16[160,8192]{1,0:T(8,128)(2,1)}, u32[]{:S(2)}, u32[]{:S(2)}) collective-permute-start(bf16[160,8192]{1,0:T(8,128)(2,1)} %refs_0_.17), channel_id=1, source_target_pairs={{0,1},{1,0},{2,3},{3,2},{4,5},{5,4},{6,7},{7,6},{8,9},{9,8},{10,11... | collective-permute-start | bytes 7864328 | tf_op jit(solution)/shard_map/ppermute | solution.py:205
  3.3 15.7 %collective-permute-start = (bf16[512,256]{1,0:T(8,128)(2,1)}, bf16[512,256]{1,0:T(8,128)(2,1)S(1)}, u32[]{:S(2)}, u32[]{:S(2)}) collective-permute-start(bf16[512,256]{1,0:T(8,128)(2,1)} %refs_5_.2), channel_id=1, source_target_pairs={{2,6},{3,1},{6,10},{7,3},{10,14},{11,7},{14,12},{15,11},{12,8},{13... | collective-permute-start | bytes 786440 | tf_op jit(solution)/shard_map/ppermute | solution.py:204
  16.1 9.2 %collective-permute-start.2 = (bf16[512,256]{1,0:T(8,128)(2,1)}, bf16[512,256]{1,0:T(8,128)(2,1)S(1)}, u32[]{:S(2)}, u32[]{:S(2)}) collective-permute-start(bf16[512,256]{1,0:T(8,128)(2,1)} %refs_5_.2), channel_id=1, source_target_pairs={{6,2},{1,3},{10,6},{3,7},{14,10},{7,11},{12,14},{11,15},{8,12},{15... | collective-permute-start | bytes 786440 | tf_op jit(solution)/shard_map/ppermute | solution.py:223
  18.1 10.6 %collective-permute-start.6 = (bf16[1280,256]{1,0:T(8,128)(2,1)S(1)}, bf16[1280,256]{1,0:T(8,128)(2,1)S(1)}, u32[]{:S(2)}, u32[]{:S(2)}) collective-permute-start(bf16[1280,256]{1,0:T(8,128)(2,1)S(1)} %slice.18.refs_4_), channel_id=1, source_target_pairs={{2,6},{3,1},{6,10},{7,3},{10,14},{11,7},{14,12},{15,11},{12,8},{13... | collective-permute-start | bytes 1966088 | tf_op jit(solution)/shard_map/ppermute | solution.py:204
  25.3 12.8 %copy-start.4 = (bf16[1280,256]{1,0:T(8,128)(2,1)}, bf16[1280,256]{1,0:T(8,128)(2,1)S(1)}, u32[]{:S(2)}) copy-start(bf16[1280,256]{1,0:T(8,128)(2,1)S(1)} %pad_maximum_fusion.refs_5_) | copy-start | bytes 1966084
  25.3 10.9 %collective-permute-start.3 = (bf16[1280,256]{1,0:T(8,128)(2,1)S(1)}, bf16[1280,256]{1,0:T(8,128)(2,1)S(1)}, u32[]{:S(2)}, u32[]{:S(2)}) collective-permute-start(bf16[1280,256]{1,0:T(8,128)(2,1)S(1)} %pad_maximum_fusion.refs_5_), channel_id=1, source_target_pairs={{2,6},{3,1},{6,10},{7,3},{10,14},{11,7},{14,12},{15,11},{12,8},{13... | collective-permute-start | bytes 1966088 | tf_op jit(solution)/shard_map/ppermute | solution.py:204
  28.8 14.6 %collective-permute-start.7 = (bf16[1280,256]{1,0:T(8,128)(2,1)S(1)}, bf16[1280,256]{1,0:T(8,128)(2,1)}, u32[]{:S(2)}, u32[]{:S(2)}) collective-permute-start(bf16[1280,256]{1,0:T(8,128)(2,1)S(1)} %collective-permute-done.6.refs_4_), channel_id=1, source_target_pairs={{2,6},{3,1},{6,10},{7,3},{10,14},{11,7},{14,12},{15,11},{12,8},{13... | collective-permute-start | bytes 1966088 | tf_op jit(solution)/shard_map/ppermute | solution.py:204
  36.2 7.1 %copy-start.6 = (bf16[1280,256]{1,0:T(8,128)(2,1)}, bf16[1280,256]{1,0:T(8,128)(2,1)S(1)}, u32[]{:S(2)}) copy-start(bf16[1280,256]{1,0:T(8,128)(2,1)S(1)} %collective-permute-done.3.refs_5_) | copy-start | bytes 1966084
  36.2 14.1 %collective-permute-start.4 = (bf16[1280,256]{1,0:T(8,128)(2,1)S(1)}, bf16[1280,256]{1,0:T(8,128)(2,1)}, u32[]{:S(2)}, u32[]{:S(2)}) collective-permute-start(bf16[1280,256]{1,0:T(8,128)(2,1)S(1)} %collective-permute-done.3.refs_5_), channel_id=1, source_target_pairs={{2,6},{3,1},{6,10},{7,3},{10,14},{11,7},{14,12},{15,11},{12,8},{13... | collective-permute-start | bytes 1966088 | tf_op jit(solution)/shard_map/ppermute | solution.py:204
  43.4 15.0 %collective-permute-start.8 = (bf16[1280,256]{1,0:T(8,128)(2,1)}, bf16[1280,256]{1,0:T(8,128)(2,1)S(1)}, u32[]{:S(2)}, u32[]{:S(2)}) collective-permute-start(bf16[1280,256]{1,0:T(8,128)(2,1)} %collective-permute-done.7.refs_4_), channel_id=1, source_target_pairs={{2,6},{3,1},{6,10},{7,3},{10,14},{11,7},{14,12},{15,11},{12,8},{13... | collective-permute-start | bytes 1966088 | tf_op jit(solution)/shard_map/ppermute | solution.py:204
  50.4 14.0 %collective-permute-start.5 = (bf16[1280,256]{1,0:T(8,128)(2,1)}, bf16[1280,256]{1,0:T(8,128)(2,1)}, u32[]{:S(2)}, u32[]{:S(2)}) collective-permute-start(bf16[1280,256]{1,0:T(8,128)(2,1)} %collective-permute-done.4.refs_5_), channel_id=1, source_target_pairs={{2,6},{3,1},{6,10},{7,3},{10,14},{11,7},{14,12},{15,11},{12,8},{13... | collective-permute-start | bytes 1966088 | tf_op jit(solution)/shard_map/ppermute | solution.py:204
  58.4 13.7 %collective-permute-start.12 = (bf16[1280,256]{1,0:T(8,128)(2,1)S(1)}, bf16[1280,256]{1,0:T(8,128)(2,1)S(1)}, u32[]{:S(2)}, u32[]{:S(2)}) collective-permute-start(bf16[1280,256]{1,0:T(8,128)(2,1)S(1)} %collective-permute-done.8.refs_4_), channel_id=1, source_target_pairs={{2,6},{3,1},{6,10},{7,3},{10,14},{11,7},{14,12},{15,11},{12,8},{13... | collective-permute-start | bytes 1966088 | tf_op jit(solution)/shard_map/ppermute | solution.py:204
  64.4 13.9 %collective-permute-start.11 = (bf16[1280,256]{1,0:T(8,128)(2,1)}, bf16[1280,256]{1,0:T(8,128)(2,1)S(1)}, u32[]{:S(2)}, u32[]{:S(2)}) collective-permute-start(bf16[1280,256]{1,0:T(8,128)(2,1)} %collective-permute-done.5.refs_5_), channel_id=1, source_target_pairs={{2,6},{3,1},{6,10},{7,3},{10,14},{11,7},{14,12},{15,11},{12,8},{13... | collective-permute-start | bytes 1966088 | tf_op jit(solution)/shard_map/ppermute | solution.py:204
  72.1 13.8 %collective-permute-start.14 = (bf16[1280,256]{1,0:T(8,128)(2,1)S(1)}, bf16[1280,256]{1,0:T(8,128)(2,1)S(1)}, u32[]{:S(2)}, u32[]{:S(2)}) collective-permute-start(bf16[1280,256]{1,0:T(8,128)(2,1)S(1)} %collective-permute-done.12.refs_4_), channel_id=1, source_target_pairs={{2,6},{3,1},{6,10},{7,3},{10,14},{11,7},{14,12},{15,11},{12,8},{13... | collective-permute-start | bytes 1966088 | tf_op jit(solution)/shard_map/ppermute | solution.py:204
  78.4 4.7 %copy-start.7 = (bf16[1280,256]{1,0:T(8,128)(2,1)}, bf16[1280,256]{1,0:T(8,128)(2,1)S(1)}, u32[]{:S(2)}) copy-start(bf16[1280,256]{1,0:T(8,128)(2,1)S(1)} %collective-permute-done.11.refs_5_) | copy-start | bytes 1966084
  78.4 14.0 %collective-permute-start.13 = (bf16[1280,256]{1,0:T(8,128)(2,1)S(1)}, bf16[1280,256]{1,0:T(8,128)(2,1)S(1)}, u32[]{:S(2)}, u32[]{:S(2)}) collective-permute-start(bf16[1280,256]{1,0:T(8,128)(2,1)S(1)} %collective-permute-done.11.refs_5_), channel_id=1, source_target_pairs={{2,6},{3,1},{6,10},{7,3},{10,14},{11,7},{14,12},{15,11},{12,8},{13... | collective-permute-start | bytes 1966088 | tf_op jit(solution)/shard_map/ppermute | solution.py:204
  85.9 15.5 %collective-permute-start.16 = (bf16[1280,256]{1,0:T(8,128)(2,1)S(1)}, bf16[1280,256]{1,0:T(8,128)(2,1)S(1)}, u32[]{:S(2)}, u32[]{:S(2)}) collective-permute-start(bf16[1280,256]{1,0:T(8,128)(2,1)S(1)} %collective-permute-done.14.refs_4_), channel_id=1, source_target_pairs={{2,6},{3,1},{6,10},{7,3},{10,14},{11,7},{14,12},{15,11},{12,8},{13... | collective-permute-start | bytes 1966088 | tf_op jit(solution)/shard_map/ppermute | solution.py:204
  92.4 2.0 %copy-start.5 = (bf16[1280,256]{1,0:T(8,128)(2,1)}, bf16[1280,256]{1,0:T(8,128)(2,1)S(1)}, u32[]{:S(2)}) copy-start(bf16[1280,256]{1,0:T(8,128)(2,1)S(1)} %collective-permute-done.13.refs_5_) | copy-start | bytes 1966084
  92.4 4.8 %copy-start.2 = (s32[2]{0:T(128)S(1)}, s32[2]{0:T(128)}, u32[]{:S(2)}) copy-start(s32[2]{0:T(128)} %refs_4_.3) | copy-start | bytes 28
  92.5 4.8 %copy-start.3 = (s32[2]{0:T(128)S(1)}, s32[2]{0:T(128)}, u32[]{:S(2)}) copy-start(s32[2]{0:T(128)} %refs_5_.3) | copy-start | bytes 28
  92.5 11.2 %collective-permute-start.15 = (bf16[768,256]{1,0:T(8,128)(2,1)S(1)}, bf16[768,256]{1,0:T(8,128)(2,1)S(1)}, u32[]{:S(2)}, u32[]{:S(2)}) collective-permute-start(bf16[768,256]{1,0:T(8,128)(2,1)S(1)} %slice.19), channel_id=1, source_target_pairs={{2,6},{3,1},{6,10},{7,3},{10,14},{11,7},{14,12},{15,11},{12,8},{13... | collective-permute-start | bytes 1179656 | tf_op jit(solution)/shard_map/ppermute | solution.py:204
  99.0 1.7 %collective-permute-start.17 = (f32[328,256]{1,0:T(8,128)S(1)}, f32[328,256]{1,0:T(8,128)S(1)}, u32[]{:S(2)}, u32[]{:S(2)}) collective-permute-start(f32[328,256]{1,0:T(8,128)S(1)} %turned.1.own_ref), channel_id=1, source_target_pairs={{0,1},{1,0},{2,3},{3,2},{4,5},{5,4},{6,7},{7,6},{8,9},{9,8},{10,11... | collective-permute-start | bytes 1007624 | tf_op jit(solution)/shard_map/ppermute | solution.py:205
  104.8 12.8 %all-to-all-start = ((f32[8,4,8]{2,1,0:T(4,128)}), f32[8,4,8]{2,1,0:T(4,128)S(1)}, u32[]{:S(2)}, u32[]{:S(2)}) async-start(f32[8,4,8]{2,1,0:T(4,128)} %bitcast.1), calls=%async_computation | async-start | bytes 32768 | tf_op jit(solution)/shard_map/all_to_all | solution.py:275
  117.7 1.2 %collective-permute-start.18 = (f32[2,8]{1,0:T(2,128)S(1)}, f32[2,8]{1,0:T(2,128)S(1)}, u32[]{:S(2)}, u32[]{:S(2)}) collective-permute-start(f32[2,8]{1,0:T(2,128)S(1)} %broadcast_select_fusion), channel_id=1, source_target_pairs={{0,1},{1,0},{2,3},{3,2},{4,5},{5,4},{6,7},{7,6},{8,9},{9,8},{10,11... | collective-permute-start | bytes 200 | tf_op jit(solution)/shard_map/ppermute | solution.py:205

commit v17 on v15

--- a/solution.py
+++ b/solution.py
@@ -271,8 +271,19 @@
 
     queries = columns // RANK
     table = score_table([window, early, totals["out"], inn], slots * devices, queries)
-    got = lax.all_to_all(table.reshape(devices, slots, queries), "dp", 0, 0, tiled=True)
-    return jnp.sum(got, axis=0)
+    if devices & (devices - 1):
+        got = lax.all_to_all(table.reshape(devices, slots, queries), "dp", 0, 0, tiled=True)
+        return jnp.sum(got, axis=0)
+    bit = devices // 2
+    while bit:
+        upper = lax.rem(lax.div(me, bit), 2) == 1
+        low, high = table[:bit * slots], table[bit * slots:]
+        give = lax.ppermute(
+            jnp.where(upper, low, high), "dp", [(d, d ^ bit) for d in range(devices)]
+        )
+        table = jnp.where(upper, high, low) + give
+        bit //= 2
+    return table
 
 
 def solution(mesh):

time: 118 us -> 119 us (level)
  blocking collectives: 12.7 us -> 0 us
  waiting for transfers between devices: 49.4 us -> 57 us
  starting transfers between devices: 27.2 us -> 32.6 us
    all_to_all x1 -> x0, blocking collectives: 12.7 us -> none  [shards(): lax.all_to_all(table.reshape(devices, slots, queries), 'dp', 0, 0, tiled=...]
    ppermute x0 -> x4, waiting for transfers between devices: none -> 7.68 us  [shards(): lax.ppermute(jnp.where(upper, low, high), 'dp', [(d, d ^ bit) for d in ra...]
    ppermute x0 -> x4, starting transfers between devices: none -> 5.45 us  [shards(): lax.ppermute(jnp.where(upper, low, high), 'dp', [(d, d ^ bit) for d in ra...]
  transfers between devices with their start and end apart: 18 -> 22, of which waited for: 11 -> 15; matrix products, arithmetic and copies ran while one was open for 1% -> 1% of each run, Pallas kernels for 22% -> 22%
where the time goes in v17:
time: 119 us
  waiting for transfers between devices  57 us (48%)
  starting transfers between devices  32.6 us (27%)
  Pallas kernels  26.5 us (22%)
  local copies, waits for them, and re-layouts  1.61 us (1%)
    ppermute x14, waiting for transfers between devices, shards(): send = lambda x: lax.ppermute(x, 'dp', pairs)  41.4 us
    pallas_call x11, Pallas kernels, call(): pl.pallas_call(kernel, grid_spec=pltpu.PrefetchScalarGridSpec(num_scalar_...  26 us
    ppermute x14, starting transfers between devices, shards(): send = lambda x: lax.ppermute(x, 'dp', pairs)  24.4 us
    ppermute x4, waiting for transfers between devices, shards(): lax.ppermute(jnp.where(upper, low, high), 'dp', [(d, d ^ bit) for d in ra...  7.68 us
    ppermute x1, waiting for transfers between devices, shards(): turned = lax.ppermute(turned, 'dp', [(j, i) for i, j in pairs])  6.32 us
    ppermute x4, starting transfers between devices, shards(): lax.ppermute(jnp.where(upper, low, high), 'dp', [(d, d ^ bit) for d in ra...  5.45 us
  transfers between devices with their start and end apart: 22, of which 15 were waited for; matrix products, arithmetic and copies ran while one was open for 1% of the time, Pallas kernels for 22%

profile of v17, /device:TPU:0, one launch (start us, length us, event | category | flops | bytes accessed | tf_op | source)
XLA Modules:
  0.0 118.7 jit_solution(14288465498259575613)
XLA Ops:
  0.0 0.5 collective-permute-start.10
  0.5 2.6 %collective-permute-start.1 = (bf16[2048,256]{1,0:T(8,128)(2,1)}, bf16[2048,256]{1,0:T(8,128)(2,1)S(1)}, u32[]{:S(2)}, u32[]{:S(2)}) collective-permute-start(bf16[2048,256]{1,0:T(8,128)(2,1)} %refs_4_.2), channel_id=1, source_target_pairs={{2,6},{3,1},{6,10},{7,3},{10,14},{11,7},{14,12},{15,11},{12,8},{13... | collective-permute-start | bytes 3145736 | tf_op jit(solution)/shard_map/ppermute | solution.py:204
  3.0 0.2 collective-permute-start.9
  3.3 1.4 %collective-permute-start = (bf16[512,256]{1,0:T(8,128)(2,1)}, bf16[512,256]{1,0:T(8,128)(2,1)S(1)}, u32[]{:S(2)}, u32[]{:S(2)}) collective-permute-start(bf16[512,256]{1,0:T(8,128)(2,1)} %refs_5_.2), channel_id=1, source_target_pairs={{2,6},{3,1},{6,10},{7,3},{10,14},{11,7},{14,12},{15,11},{12,8},{13... | collective-permute-start | bytes 786440 | tf_op jit(solution)/shard_map/ppermute | solution.py:204
  4.6 11.5 %collective-permute-done.1 = bf16[2048,256]{1,0:T(8,128)(2,1)S(1)} collective-permute-done((bf16[2048,256]{1,0:T(8,128)(2,1)}, bf16[2048,256]{1,0:T(8,128)(2,1)S(1)}, u32[]{:S(2)}, u32[]{:S(2)}) %collective-permute-start.1) | collective-permute-done | bytes 1048608 | tf_op jit(solution)/shard_map/ppermute | solution.py:204
  16.1 2.0 %collective-permute-start.2 = (bf16[512,256]{1,0:T(8,128)(2,1)}, bf16[512,256]{1,0:T(8,128)(2,1)S(1)}, u32[]{:S(2)}, u32[]{:S(2)}) collective-permute-start(bf16[512,256]{1,0:T(8,128)(2,1)} %refs_5_.2), channel_id=1, source_target_pairs={{6,2},{1,3},{10,6},{3,7},{14,10},{7,11},{12,14},{11,15},{8,12},{15... | collective-permute-start | bytes 786440 | tf_op jit(solution)/shard_map/ppermute | solution.py:223
  18.1 0.1 collective-permute-start.6
  18.3 0.7 collective-permute-done
  19.0 6.3 %collective-permute-done.2.refs_2_ = bf16[512,256]{1,0:T(8,128)(2,1)S(1)} collective-permute-done((bf16[512,256]{1,0:T(8,128)(2,1)}, bf16[512,256]{1,0:T(8,128)(2,1)S(1)}, u32[]{:S(2)}, u32[]{:S(2)}) %collective-permute-start.2) | collective-permute-done | bytes 262176 | tf_op jit(solution)/shard_map/ppermute | solution.py:223
  25.3 0.0 copy-start.4
  25.3 2.2 %collective-permute-start.3 = (bf16[1280,256]{1,0:T(8,128)(2,1)S(1)}, bf16[1280,256]{1,0:T(8,128)(2,1)S(1)}, u32[]{:S(2)}, u32[]{:S(2)}) collective-permute-start(bf16[1280,256]{1,0:T(8,128)(2,1)S(1)} %pad_maximum_fusion.refs_5_), channel_id=1, source_target_pairs={{2,6},{3,1},{6,10},{7,3},{10,14},{11,7},{14,12},{15,11},{12,8},{13... | collective-permute-start | bytes 1966088 | tf_op jit(solution)/shard_map/ppermute | solution.py:204
  27.5 1.2 %collective-permute-done.6.refs_4_ = bf16[1280,256]{1,0:T(8,128)(2,1)S(1)} collective-permute-done((bf16[1280,256]{1,0:T(8,128)(2,1)S(1)}, bf16[1280,256]{1,0:T(8,128)(2,1)S(1)}, u32[]{:S(2)}, u32[]{:S(2)}) %collective-permute-start.6) | collective-permute-done | bytes 655392 | tf_op jit(solution)/shard_map/ppermute | solution.py:204
  28.8 1.9 %collective-permute-start.7 = (bf16[1280,256]{1,0:T(8,128)(2,1)S(1)}, bf16[1280,256]{1,0:T(8,128)(2,1)}, u32[]{:S(2)}, u32[]{:S(2)}) collective-permute-start(bf16[1280,256]{1,0:T(8,128)(2,1)S(1)} %collective-permute-done.6.refs_4_), channel_id=1, source_target_pairs={{2,6},{3,1},{6,10},{7,3},{10,14},{11,7},{14,12},{15,11},{12,8},{13... | collective-permute-start | bytes 1966088 | tf_op jit(solution)/shard_map/ppermute | solution.py:204
  30.7 5.5 %collective-permute-done.3.refs_5_ = bf16[1280,256]{1,0:T(8,128)(2,1)S(1)} collective-permute-done((bf16[1280,256]{1,0:T(8,128)(2,1)S(1)}, bf16[1280,256]{1,0:T(8,128)(2,1)S(1)}, u32[]{:S(2)}, u32[]{:S(2)}) %collective-permute-start.3) | collective-permute-done | bytes 655392 | tf_op jit(solution)/shard_map/ppermute | solution.py:204
  36.2 1.9 %collective-permute-start.4 = (bf16[1280,256]{1,0:T(8,128)(2,1)S(1)}, bf16[1280,256]{1,0:T(8,128)(2,1)}, u32[]{:S(2)}, u32[]{:S(2)}) collective-permute-start(bf16[1280,256]{1,0:T(8,128)(2,1)S(1)} %collective-permute-done.3.refs_5_), channel_id=1, source_target_pairs={{2,6},{3,1},{6,10},{7,3},{10,14},{11,7},{14,12},{15,11},{12,8},{13... | collective-permute-start | bytes 1966088 | tf_op jit(solution)/shard_map/ppermute | solution.py:204
  38.1 0.0 copy-done.4
  38.1 5.2 %collective-permute-done.7.refs_4_ = bf16[1280,256]{1,0:T(8,128)(2,1)} collective-permute-done((bf16[1280,256]{1,0:T(8,128)(2,1)S(1)}, bf16[1280,256]{1,0:T(8,128)(2,1)}, u32[]{:S(2)}, u32[]{:S(2)}) %collective-permute-start.7) | collective-permute-done | bytes 655392 | tf_op jit(solution)/shard_map/ppermute | solution.py:204
  43.4 0.0 copy-done.6
  43.4 1.9 %collective-permute-start.8 = (bf16[1280,256]{1,0:T(8,128)(2,1)}, bf16[1280,256]{1,0:T(8,128)(2,1)S(1)}, u32[]{:S(2)}, u32[]{:S(2)}) collective-permute-start(bf16[1280,256]{1,0:T(8,128)(2,1)} %collective-permute-done.7.refs_4_), channel_id=1, source_target_pairs={{2,6},{3,1},{6,10},{7,3},{10,14},{11,7},{14,12},{15,11},{12,8},{13... | collective-permute-start | bytes 1966088 | tf_op jit(solution)/shard_map/ppermute | solution.py:204
  45.3 5.1 %collective-permute-done.4.refs_5_ = bf16[1280,256]{1,0:T(8,128)(2,1)} collective-permute-done((bf16[1280,256]{1,0:T(8,128)(2,1)S(1)}, bf16[1280,256]{1,0:T(8,128)(2,1)}, u32[]{:S(2)}, u32[]{:S(2)}) %collective-permute-start.4) | collective-permute-done | bytes 655392 | tf_op jit(solution)/shard_map/ppermute | solution.py:204
  50.4 1.9 %collective-permute-start.5 = (bf16[1280,256]{1,0:T(8,128)(2,1)}, bf16[1280,256]{1,0:T(8,128)(2,1)}, u32[]{:S(2)}, u32[]{:S(2)}) collective-permute-start(bf16[1280,256]{1,0:T(8,128)(2,1)} %collective-permute-done.4.refs_5_), channel_id=1, source_target_pairs={{2,6},{3,1},{6,10},{7,3},{10,14},{11,7},{14,12},{15,11},{12,8},{13... | collective-permute-start | bytes 1966088 | tf_op jit(solution)/shard_map/ppermute | solution.py:204
  52.3 0.7 dynamic-slice_bitcast_fusion.order_ref
  53.0 0.0 collective-permute-done.9.refs_1_
  53.0 0.0 collective-permute-done.10.refs_3_.sib_ref.refs_1_
  53.0 0.0 copy-done
  53.0 2.6 %step.8 = (f32[320,256]{1,0:T(8,128)S(1)}, f32[320,256]{1,0:T(8,128)S(1)}) custom-call(s32[8]{0:T(128)S(1)} %dynamic-slice_bitcast_fusion.order_ref, bf16[160,8192]{1,0:T(8,128)(2,1)} %refs_0_.17, bf16[160,8192]{1,0:T(8,128)(2,1)} %collective-permute-done.9.refs_1_, bf16[160,32768]{1,0:T(8,128)(2,1)} %refs_0_.16, ...), custom_call_target="tpu_custom_call" | custom-call | flops 419430400 | bytes 3604480 | tf_op jit(solution)/shard_map/step/pallas_call | solution.py:59
  55.6 2.8 %step.9 = (f32[320,256]{1,0:T(8,128)S(1)}, f32[320,256]{1,0:T(8,128)S(1)}) custom-call(s32[8]{0:T(128)S(1)} %dynamic-slice_bitcast_fusion.order_ref, bf16[160,8192]{1,0:T(8,128)(2,1)} %refs_0_.17, bf16[160,8192]{1,0:T(8,128)(2,1)} %collective-permute-done.9.refs_1_, bf16[160,32768]{1,0:T(8,128)(2,1)} %refs_0_.16, ...), custom_call_target="tpu_custom_call" | custom-call | flops 419430400 | bytes 4259840 | tf_op jit(solution)/shard_map/step/pallas_call | solution.py:59
  58.4 0.0 collective-permute-done.8.refs_4_
  58.4 1.6 %collective-permute-start.12 = (bf16[1280,256]{1,0:T(8,128)(2,1)S(1)}, bf16[1280,256]{1,0:T(8,128)(2,1)S(1)}, u32[]{:S(2)}, u32[]{:S(2)}) collective-permute-start(bf16[1280,256]{1,0:T(8,128)(2,1)S(1)} %collective-permute-done.8.refs_4_), channel_id=1, source_target_pairs={{2,6},{3,1},{6,10},{7,3},{10,14},{11,7},{14,12},{15,11},{12,8},{13... | collective-permute-start | bytes 1966088 | tf_op jit(solution)/shard_map/ppermute | solution.py:204
  60.0 4.4 %collective-permute-done.5.refs_5_ = bf16[1280,256]{1,0:T(8,128)(2,1)} collective-permute-done((bf16[1280,256]{1,0:T(8,128)(2,1)}, bf16[1280,256]{1,0:T(8,128)(2,1)}, u32[]{:S(2)}, u32[]{:S(2)}) %collective-permute-start.5) | collective-permute-done | bytes 655392 | tf_op jit(solution)/shard_map/ppermute | solution.py:204
  64.4 1.9 %collective-permute-start.11 = (bf16[1280,256]{1,0:T(8,128)(2,1)}, bf16[1280,256]{1,0:T(8,128)(2,1)S(1)}, u32[]{:S(2)}, u32[]{:S(2)}) collective-permute-start(bf16[1280,256]{1,0:T(8,128)(2,1)} %collective-permute-done.5.refs_5_), channel_id=1, source_target_pairs={{2,6},{3,1},{6,10},{7,3},{10,14},{11,7},{14,12},{15,11},{12,8},{13... | collective-permute-start | bytes 1966088 | tf_op jit(solution)/shard_map/ppermute | solution.py:204
  66.3 2.8 %step.10 = (f32[320,256]{1,0:T(8,128)S(1)}, f32[320,256]{1,0:T(8,128)S(1)}) custom-call(s32[8]{0:T(128)S(1)} %dynamic-slice_bitcast_fusion.order_ref, bf16[160,8192]{1,0:T(8,128)(2,1)} %refs_0_.17, bf16[160,8192]{1,0:T(8,128)(2,1)} %collective-permute-done.9.refs_1_, bf16[160,32768]{1,0:T(8,128)(2,1)} %refs_0_.16, ...), custom_call_target="tpu_custom_call" | custom-call | flops 419430400 | bytes 4259840 | tf_op jit(solution)/shard_map/step/pallas_call | solution.py:59
  69.1 3.0 %step.11 = (f32[320,256]{1,0:T(8,128)S(1)}, f32[320,256]{1,0:T(8,128)S(1)}) custom-call(s32[8]{0:T(128)S(1)} %dynamic-slice_bitcast_fusion.order_ref, bf16[160,8192]{1,0:T(8,128)(2,1)} %refs_0_.17, bf16[160,8192]{1,0:T(8,128)(2,1)} %collective-permute-done.9.refs_1_, bf16[160,32768]{1,0:T(8,128)(2,1)} %refs_0_.16, ...), custom_call_target="tpu_custom_call" | custom-call | flops 419430400 | bytes 4259840 | tf_op jit(solution)/shard_map/step/pallas_call | solution.py:59
  72.1 0.0 collective-permute-done.12.refs_4_
  72.1 1.6 %collective-permute-start.14 = (bf16[1280,256]{1,0:T(8,128)(2,1)S(1)}, bf16[1280,256]{1,0:T(8,128)(2,1)S(1)}, u32[]{:S(2)}, u32[]{:S(2)}) collective-permute-start(bf16[1280,256]{1,0:T(8,128)(2,1)S(1)} %collective-permute-done.12.refs_4_), channel_id=1, source_target_pairs={{2,6},{3,1},{6,10},{7,3},{10,14},{11,7},{14,12},{15,11},{12,8},{13... | collective-permute-start | bytes 1966088 | tf_op jit(solution)/shard_map/ppermute | solution.py:204
  73.7 4.6 %collective-permute-done.11.refs_5_ = bf16[1280,256]{1,0:T(8,128)(2,1)S(1)} collective-permute-done((bf16[1280,256]{1,0:T(8,128)(2,1)}, bf16[1280,256]{1,0:T(8,128)(2,1)S(1)}, u32[]{:S(2)}, u32[]{:S(2)}) %collective-permute-start.11) | collective-permute-done | bytes 655392 | tf_op jit(solution)/shard_map/ppermute | solution.py:204
  78.4 1.9 %collective-permute-start.13 = (bf16[1280,256]{1,0:T(8,128)(2,1)S(1)}, bf16[1280,256]{1,0:T(8,128)(2,1)S(1)}, u32[]{:S(2)}, u32[]{:S(2)}) collective-permute-start(bf16[1280,256]{1,0:T(8,128)(2,1)S(1)} %collective-permute-done.11.refs_5_), channel_id=1, source_target_pairs={{2,6},{3,1},{6,10},{7,3},{10,14},{11,7},{14,12},{15,11},{12,8},{13... | collective-permute-start | bytes 1966088 | tf_op jit(solution)/shard_map/ppermute | solution.py:204
  80.3 2.8 %step.12 = (f32[320,256]{1,0:T(8,128)S(1)}, f32[320,256]{1,0:T(8,128)S(1)}) custom-call(s32[8]{0:T(128)S(1)} %dynamic-slice_bitcast_fusion.order_ref, bf16[160,8192]{1,0:T(8,128)(2,1)} %refs_0_.17, bf16[160,8192]{1,0:T(8,128)(2,1)} %collective-permute-done.9.refs_1_, bf16[160,32768]{1,0:T(8,128)(2,1)} %refs_0_.16, ...), custom_call_target="tpu_custom_call" | custom-call | flops 419430400 | bytes 4259840 | tf_op jit(solution)/shard_map/step/pallas_call | solution.py:59
  83.1 2.8 %step.13 = (f32[320,256]{1,0:T(8,128)S(1)}, f32[320,256]{1,0:T(8,128)S(1)}) custom-call(s32[8]{0:T(128)S(1)} %dynamic-slice_bitcast_fusion.order_ref, bf16[160,8192]{1,0:T(8,128)(2,1)} %refs_0_.17, bf16[160,8192]{1,0:T(8,128)(2,1)} %collective-permute-done.9.refs_1_, bf16[160,32768]{1,0:T(8,128)(2,1)} %refs_0_.16, ...), custom_call_target="tpu_custom_call" | custom-call | flops 419430400 | bytes 4259840 | tf_op jit(solution)/shard_map/step/pallas_call | solution.py:59
  85.8 0.0 collective-permute-done.14.refs_4_
  85.9 1.6 %collective-permute-start.16 = (bf16[1280,256]{1,0:T(8,128)(2,1)S(1)}, bf16[1280,256]{1,0:T(8,128)(2,1)S(1)}, u32[]{:S(2)}, u32[]{:S(2)}) collective-permute-start(bf16[1280,256]{1,0:T(8,128)(2,1)S(1)} %collective-permute-done.14.refs_4_), channel_id=1, source_target_pairs={{2,6},{3,1},{6,10},{7,3},{10,14},{11,7},{14,12},{15,11},{12,8},{13... | collective-permute-start | bytes 1966088 | tf_op jit(solution)/shard_map/ppermute | solution.py:204
  87.5 1.9 %window.1.window_ref = bf16[320,768]{1,0:T(8,128)(2,1)S(1)} custom-call(s32[8]{0:T(128)S(1)} %dynamic-slice_bitcast_fusion.order_ref, bf16[160,32768]{1,0:T(8,128)(2,1)} %refs_0_.16, bf16[160,32768]{1,0:T(8,128)(2,1)} %collective-permute-done.10.refs_3_.sib_ref.refs_1_), custom_call_target="tpu_custom_call" | custom-call | bytes 1802240 | tf_op jit(solution)/shard_map/window/pallas_call | solution.py:59
  89.3 3.1 %collective-permute-done.13.refs_5_ = bf16[1280,256]{1,0:T(8,128)(2,1)S(1)} collective-permute-done((bf16[1280,256]{1,0:T(8,128)(2,1)S(1)}, bf16[1280,256]{1,0:T(8,128)(2,1)S(1)}, u32[]{:S(2)}, u32[]{:S(2)}) %collective-permute-start.13) | collective-permute-done | bytes 655392 | tf_op jit(solution)/shard_map/ppermute | solution.py:204
  92.4 0.8 slice.35
  93.2 1.9 %collective-permute-start.15 = (bf16[768,256]{1,0:T(8,128)(2,1)}, bf16[768,256]{1,0:T(8,128)(2,1)S(1)}, u32[]{:S(2)}, u32[]{:S(2)}) collective-permute-start(bf16[768,256]{1,0:T(8,128)(2,1)} %slice.35), channel_id=1, source_target_pairs={{2,6},{3,1},{6,10},{7,3},{10,14},{11,7},{14,12},{15,11},{12,8},{13... | collective-permute-start | bytes 1179656 | tf_op jit(solution)/shard_map/ppermute | solution.py:204
  95.1 0.0 copy-done.5
  95.1 2.8 %step.14 = (f32[320,256]{1,0:T(8,128)S(1)}, f32[320,256]{1,0:T(8,128)S(1)}) custom-call(s32[8]{0:T(128)S(1)} %dynamic-slice_bitcast_fusion.order_ref, bf16[160,8192]{1,0:T(8,128)(2,1)} %refs_0_.17, bf16[160,8192]{1,0:T(8,128)(2,1)} %collective-permute-done.9.refs_1_, bf16[160,32768]{1,0:T(8,128)(2,1)} %refs_0_.16, ...), custom_call_target="tpu_custom_call" | custom-call | flops 419430400 | bytes 4259840 | tf_op jit(solution)/shard_map/step/pallas_call | solution.py:59
  98.0 1.8 %turned.1.own_ref = f32[328,256]{1,0:T(8,128)S(1)} custom-call(s32[8]{0:T(128)S(1)} %dynamic-slice_bitcast_fusion.order_ref, bf16[160,8192]{1,0:T(8,128)(2,1)} %refs_0_.17, bf16[160,8192]{1,0:T(8,128)(2,1)} %collective-permute-done.9.refs_1_, bf16[512,256]{1,0:T(8,128)(2,1)S(1)} %collective-permute-done.2.refs_2_, f32[320,256]{1,0:T(8,128)S(1)} %get-tuple-element.82.refs_3_, ...), custom_call_target="tpu_custom_call" | custom-call | flops 83886080 | bytes 1253376 | tf_op jit(solution)/shard_map/turned/pallas_call | solution.py:59
  99.8 0.1 collective-permute-start.17
  99.9 1.6 %collective-permute-done.17.got_ref = f32[328,256]{1,0:T(8,128)S(1)} collective-permute-done((f32[328,256]{1,0:T(8,128)S(1)}, f32[328,256]{1,0:T(8,128)S(1)}, u32[]{:S(2)}, u32[]{:S(2)}) %collective-permute-start.17) | collective-permute-done | bytes 335904 | tf_op jit(solution)/shard_map/ppermute | solution.py:205
  101.5 0.6 masked.1.inn_ref
  102.1 0.0 collective-permute-done.16.refs_2_
  102.1 2.2 %step.15.total_ref = f32[320,256]{1,0:T(8,128)S(1)} custom-call(s32[8]{0:T(128)S(1)} %dynamic-slice_bitcast_fusion.order_ref, bf16[160,32768]{1,0:T(8,128)(2,1)} %refs_0_.16, bf16[160,32768]{1,0:T(8,128)(2,1)} %collective-permute-done.10.refs_3_.sib_ref.refs_1_, bf16[1280,256]{1,0:T(8,128)(2,1)S(1)} %collective-permute-done.16.refs_2_, ...), custom_call_target="tpu_custom_call" | custom-call | flops 209715200 | bytes 2621440 | tf_op jit(solution)/shard_map/step/pallas_call | solution.py:59
  104.3 0.0 collective-permute-done.15.block_ref
  104.4 0.6 score.1
  104.9 2.4 %collective-permute-start.18 = (f32[16,8]{1,0:T(8,128)S(1)}, f32[16,8]{1,0:T(8,128)S(1)}, u32[]{:S(2)}, u32[]{:S(2)}) collective-permute-start(f32[16,8]{1,0:T(8,128)S(1)} %slice_select_fusion), channel_id=1, source_target_pairs={{0,8},{1,9},{2,10},{3,11},{4,12},{5,13},{6,14},{7,15},{8,0},{9,1},... | collective-permute-start | bytes 1544 | tf_op jit(solution)/shard_map/ppermute | solution.py:281
  107.3 2.3 %collective-permute-done.18 = f32[16,8]{1,0:T(8,128)S(1)} collective-permute-done((f32[16,8]{1,0:T(8,128)S(1)}, f32[16,8]{1,0:T(8,128)S(1)}, u32[]{:S(2)}, u32[]{:S(2)}) %collective-permute-start.18) | collective-permute-done | bytes 544 | tf_op jit(solution)/shard_map/ppermute | solution.py:281
  109.6 1.4 %collective-permute-start.19 = (f32[8,8]{1,0:T(8,128)S(1)}, f32[8,8]{1,0:T(8,128)S(1)}, u32[]{:S(2)}, u32[]{:S(2)}) collective-permute-start(f32[8,8]{1,0:T(8,128)S(1)} %slice_select_fusion.1), channel_id=1, source_target_pairs={{0,4},{1,5},{2,6},{3,7},{4,0},{5,1},{6,2},{7,3},{8,12},{9,13},{10,... | collective-permute-start | bytes 776 | tf_op jit(solution)/shard_map/ppermute | solution.py:281
  110.9 2.3 %collective-permute-done.19 = f32[8,8]{1,0:T(8,128)S(1)} collective-permute-done((f32[8,8]{1,0:T(8,128)S(1)}, f32[8,8]{1,0:T(8,128)S(1)}, u32[]{:S(2)}, u32[]{:S(2)}) %collective-permute-start.19) | collective-permute-done | bytes 288 | tf_op jit(solution)/shard_map/ppermute | solution.py:281
  113.2 1.6 %collective-permute-start.20 = (f32[4,8]{1,0:T(4,128)S(1)}, f32[4,8]{1,0:T(4,128)S(1)}, u32[]{:S(2)}, u32[]{:S(2)}) collective-permute-start(f32[4,8]{1,0:T(4,128)S(1)} %slice_select_fusion.2), channel_id=1, source_target_pairs={{0,2},{1,3},{2,0},{3,1},{4,6},{5,7},{6,4},{7,5},{8,10},{9,11},{10,... | collective-permute-start | bytes 392 | tf_op jit(solution)/shard_map/ppermute | solution.py:281
  114.9 2.0 %collective-permute-done.20 = f32[4,8]{1,0:T(4,128)S(1)} collective-permute-done((f32[4,8]{1,0:T(4,128)S(1)}, f32[4,8]{1,0:T(4,128)S(1)}, u32[]{:S(2)}, u32[]{:S(2)}) %collective-permute-start.20) | collective-permute-done | bytes 160 | tf_op jit(solution)/shard_map/ppermute | solution.py:281
  116.9 0.1 collective-permute-start.21
  117.0 1.1 collective-permute-done.21
  118.1 0.6 select_add_fusion.3
  (21 shorter events, 0.2 us)
Async XLA Ops:
  0.0 53.0 %copy-start = (bf16[2048,256]{1,0:T(8,128)(2,1)S(1)}, bf16[2048,256]{1,0:T(8,128)(2,1)}, u32[]{:S(2)}) copy-start(bf16[2048,256]{1,0:T(8,128)(2,1)} %refs_4_.2) | copy-start | bytes 3145732
  0.0 53.0 %copy-start.1 = (bf16[512,256]{1,0:T(8,128)(2,1)S(1)}, bf16[512,256]{1,0:T(8,128)(2,1)}, u32[]{:S(2)}) copy-start(bf16[512,256]{1,0:T(8,128)(2,1)} %refs_5_.2) | copy-start | bytes 786436
  0.0 53.0 %collective-permute-start.10 = (bf16[160,32768]{1,0:T(8,128)(2,1)}, bf16[160,32768]{1,0:T(8,128)(2,1)}, u32[]{:S(2)}, u32[]{:S(2)}) collective-permute-start(bf16[160,32768]{1,0:T(8,128)(2,1)} %refs_0_.16), channel_id=1, source_target_pairs={{0,1},{1,0},{2,3},{3,2},{4,5},{5,4},{6,7},{7,6},{8,9},{9,8},{10,11... | collective-permute-start | bytes 31457288 | tf_op jit(solution)/shard_map/ppermute | solution.py:205
  0.5 15.6 %collective-permute-start.1 = (bf16[2048,256]{1,0:T(8,128)(2,1)}, bf16[2048,256]{1,0:T(8,128)(2,1)S(1)}, u32[]{:S(2)}, u32[]{:S(2)}) collective-permute-start(bf16[2048,256]{1,0:T(8,128)(2,1)} %refs_4_.2), channel_id=1, source_target_pairs={{2,6},{3,1},{6,10},{7,3},{10,14},{11,7},{14,12},{15,11},{12,8},{13... | collective-permute-start | bytes 3145736 | tf_op jit(solution)/shard_map/ppermute | solution.py:204
  3.0 49.9 %collective-permute-start.9 = (bf16[160,8192]{1,0:T(8,128)(2,1)}, bf16[160,8192]{1,0:T(8,128)(2,1)}, u32[]{:S(2)}, u32[]{:S(2)}) collective-permute-start(bf16[160,8192]{1,0:T(8,128)(2,1)} %refs_0_.17), channel_id=1, source_target_pairs={{0,1},{1,0},{2,3},{3,2},{4,5},{5,4},{6,7},{7,6},{8,9},{9,8},{10,11... | collective-permute-start | bytes 7864328 | tf_op jit(solution)/shard_map/ppermute | solution.py:205
  3.3 15.7 %collective-permute-start = (bf16[512,256]{1,0:T(8,128)(2,1)}, bf16[512,256]{1,0:T(8,128)(2,1)S(1)}, u32[]{:S(2)}, u32[]{:S(2)}) collective-permute-start(bf16[512,256]{1,0:T(8,128)(2,1)} %refs_5_.2), channel_id=1, source_target_pairs={{2,6},{3,1},{6,10},{7,3},{10,14},{11,7},{14,12},{15,11},{12,8},{13... | collective-permute-start | bytes 786440 | tf_op jit(solution)/shard_map/ppermute | solution.py:204
  16.1 9.2 %collective-permute-start.2 = (bf16[512,256]{1,0:T(8,128)(2,1)}, bf16[512,256]{1,0:T(8,128)(2,1)S(1)}, u32[]{:S(2)}, u32[]{:S(2)}) collective-permute-start(bf16[512,256]{1,0:T(8,128)(2,1)} %refs_5_.2), channel_id=1, source_target_pairs={{6,2},{1,3},{10,6},{3,7},{14,10},{7,11},{12,14},{11,15},{8,12},{15... | collective-permute-start | bytes 786440 | tf_op jit(solution)/shard_map/ppermute | solution.py:223
  18.1 10.6 %collective-permute-start.6 = (bf16[1280,256]{1,0:T(8,128)(2,1)S(1)}, bf16[1280,256]{1,0:T(8,128)(2,1)S(1)}, u32[]{:S(2)}, u32[]{:S(2)}) collective-permute-start(bf16[1280,256]{1,0:T(8,128)(2,1)S(1)} %slice.34.refs_4_), channel_id=1, source_target_pairs={{2,6},{3,1},{6,10},{7,3},{10,14},{11,7},{14,12},{15,11},{12,8},{13... | collective-permute-start | bytes 1966088 | tf_op jit(solution)/shard_map/ppermute | solution.py:204
  25.3 12.8 %copy-start.4 = (bf16[1280,256]{1,0:T(8,128)(2,1)}, bf16[1280,256]{1,0:T(8,128)(2,1)S(1)}, u32[]{:S(2)}) copy-start(bf16[1280,256]{1,0:T(8,128)(2,1)S(1)} %pad_maximum_fusion.refs_5_) | copy-start | bytes 1966084
  25.3 10.9 %collective-permute-start.3 = (bf16[1280,256]{1,0:T(8,128)(2,1)S(1)}, bf16[1280,256]{1,0:T(8,128)(2,1)S(1)}, u32[]{:S(2)}, u32[]{:S(2)}) collective-permute-start(bf16[1280,256]{1,0:T(8,128)(2,1)S(1)} %pad_maximum_fusion.refs_5_), channel_id=1, source_target_pairs={{2,6},{3,1},{6,10},{7,3},{10,14},{11,7},{14,12},{15,11},{12,8},{13... | collective-permute-start | bytes 1966088 | tf_op jit(solution)/shard_map/ppermute | solution.py:204
  28.8 14.6 %collective-permute-start.7 = (bf16[1280,256]{1,0:T(8,128)(2,1)S(1)}, bf16[1280,256]{1,0:T(8,128)(2,1)}, u32[]{:S(2)}, u32[]{:S(2)}) collective-permute-start(bf16[1280,256]{1,0:T(8,128)(2,1)S(1)} %collective-permute-done.6.refs_4_), channel_id=1, source_target_pairs={{2,6},{3,1},{6,10},{7,3},{10,14},{11,7},{14,12},{15,11},{12,8},{13... | collective-permute-start | bytes 1966088 | tf_op jit(solution)/shard_map/ppermute | solution.py:204
  36.2 7.1 %copy-start.6 = (bf16[1280,256]{1,0:T(8,128)(2,1)}, bf16[1280,256]{1,0:T(8,128)(2,1)S(1)}, u32[]{:S(2)}) copy-start(bf16[1280,256]{1,0:T(8,128)(2,1)S(1)} %collective-permute-done.3.refs_5_) | copy-start | bytes 1966084
  36.2 14.1 %collective-permute-start.4 = (bf16[1280,256]{1,0:T(8,128)(2,1)S(1)}, bf16[1280,256]{1,0:T(8,128)(2,1)}, u32[]{:S(2)}, u32[]{:S(2)}) collective-permute-start(bf16[1280,256]{1,0:T(8,128)(2,1)S(1)} %collective-permute-done.3.refs_5_), channel_id=1, source_target_pairs={{2,6},{3,1},{6,10},{7,3},{10,14},{11,7},{14,12},{15,11},{12,8},{13... | collective-permute-start | bytes 1966088 | tf_op jit(solution)/shard_map/ppermute | solution.py:204
  43.4 15.0 %collective-permute-start.8 = (bf16[1280,256]{1,0:T(8,128)(2,1)}, bf16[1280,256]{1,0:T(8,128)(2,1)S(1)}, u32[]{:S(2)}, u32[]{:S(2)}) collective-permute-start(bf16[1280,256]{1,0:T(8,128)(2,1)} %collective-permute-done.7.refs_4_), channel_id=1, source_target_pairs={{2,6},{3,1},{6,10},{7,3},{10,14},{11,7},{14,12},{15,11},{12,8},{13... | collective-permute-start | bytes 1966088 | tf_op jit(solution)/shard_map/ppermute | solution.py:204
  50.4 14.0 %collective-permute-start.5 = (bf16[1280,256]{1,0:T(8,128)(2,1)}, bf16[1280,256]{1,0:T(8,128)(2,1)}, u32[]{:S(2)}, u32[]{:S(2)}) collective-permute-start(bf16[1280,256]{1,0:T(8,128)(2,1)} %collective-permute-done.4.refs_5_), channel_id=1, source_target_pairs={{2,6},{3,1},{6,10},{7,3},{10,14},{11,7},{14,12},{15,11},{12,8},{13... | collective-permute-start | bytes 1966088 | tf_op jit(solution)/shard_map/ppermute | solution.py:204
  58.4 13.7 %collective-permute-start.12 = (bf16[1280,256]{1,0:T(8,128)(2,1)S(1)}, bf16[1280,256]{1,0:T(8,128)(2,1)S(1)}, u32[]{:S(2)}, u32[]{:S(2)}) collective-permute-start(bf16[1280,256]{1,0:T(8,128)(2,1)S(1)} %collective-permute-done.8.refs_4_), channel_id=1, source_target_pairs={{2,6},{3,1},{6,10},{7,3},{10,14},{11,7},{14,12},{15,11},{12,8},{13... | collective-permute-start | bytes 1966088 | tf_op jit(solution)/shard_map/ppermute | solution.py:204
  64.4 13.9 %collective-permute-start.11 = (bf16[1280,256]{1,0:T(8,128)(2,1)}, bf16[1280,256]{1,0:T(8,128)(2,1)S(1)}, u32[]{:S(2)}, u32[]{:S(2)}) collective-permute-start(bf16[1280,256]{1,0:T(8,128)(2,1)} %collective-permute-done.5.refs_5_), channel_id=1, source_target_pairs={{2,6},{3,1},{6,10},{7,3},{10,14},{11,7},{14,12},{15,11},{12,8},{13... | collective-permute-start | bytes 1966088 | tf_op jit(solution)/shard_map/ppermute | solution.py:204
  72.1 13.8 %collective-permute-start.14 = (bf16[1280,256]{1,0:T(8,128)(2,1)S(1)}, bf16[1280,256]{1,0:T(8,128)(2,1)S(1)}, u32[]{:S(2)}, u32[]{:S(2)}) collective-permute-start(bf16[1280,256]{1,0:T(8,128)(2,1)S(1)} %collective-permute-done.12.refs_4_), channel_id=1, source_target_pairs={{2,6},{3,1},{6,10},{7,3},{10,14},{11,7},{14,12},{15,11},{12,8},{13... | collective-permute-start | bytes 1966088 | tf_op jit(solution)/shard_map/ppermute | solution.py:204
  78.4 4.7 %copy-start.7 = (bf16[1280,256]{1,0:T(8,128)(2,1)}, bf16[1280,256]{1,0:T(8,128)(2,1)S(1)}, u32[]{:S(2)}) copy-start(bf16[1280,256]{1,0:T(8,128)(2,1)S(1)} %collective-permute-done.11.refs_5_) | copy-start | bytes 1966084
  78.4 14.0 %collective-permute-start.13 = (bf16[1280,256]{1,0:T(8,128)(2,1)S(1)}, bf16[1280,256]{1,0:T(8,128)(2,1)S(1)}, u32[]{:S(2)}, u32[]{:S(2)}) collective-permute-start(bf16[1280,256]{1,0:T(8,128)(2,1)S(1)} %collective-permute-done.11.refs_5_), channel_id=1, source_target_pairs={{2,6},{3,1},{6,10},{7,3},{10,14},{11,7},{14,12},{15,11},{12,8},{13... | collective-permute-start | bytes 1966088 | tf_op jit(solution)/shard_map/ppermute | solution.py:204
  85.9 16.3 %collective-permute-start.16 = (bf16[1280,256]{1,0:T(8,128)(2,1)S(1)}, bf16[1280,256]{1,0:T(8,128)(2,1)S(1)}, u32[]{:S(2)}, u32[]{:S(2)}) collective-permute-start(bf16[1280,256]{1,0:T(8,128)(2,1)S(1)} %collective-permute-done.14.refs_4_), channel_id=1, source_target_pairs={{2,6},{3,1},{6,10},{7,3},{10,14},{11,7},{14,12},{15,11},{12,8},{13... | collective-permute-start | bytes 1966088 | tf_op jit(solution)/shard_map/ppermute | solution.py:204
  92.4 2.7 %copy-start.5 = (bf16[1280,256]{1,0:T(8,128)(2,1)}, bf16[1280,256]{1,0:T(8,128)(2,1)S(1)}, u32[]{:S(2)}) copy-start(bf16[1280,256]{1,0:T(8,128)(2,1)S(1)} %collective-permute-done.13.refs_5_) | copy-start | bytes 1966084
  93.2 4.7 %copy-start.2 = (s32[2]{0:T(128)S(1)}, s32[2]{0:T(128)}, u32[]{:S(2)}) copy-start(s32[2]{0:T(128)} %refs_4_.3) | copy-start | bytes 28
  93.2 4.7 %copy-start.3 = (s32[2]{0:T(128)S(1)}, s32[2]{0:T(128)}, u32[]{:S(2)}) copy-start(s32[2]{0:T(128)} %refs_5_.3) | copy-start | bytes 28
  93.2 11.1 %collective-permute-start.15 = (bf16[768,256]{1,0:T(8,128)(2,1)}, bf16[768,256]{1,0:T(8,128)(2,1)S(1)}, u32[]{:S(2)}, u32[]{:S(2)}) collective-permute-start(bf16[768,256]{1,0:T(8,128)(2,1)} %slice.35), channel_id=1, source_target_pairs={{2,6},{3,1},{6,10},{7,3},{10,14},{11,7},{14,12},{15,11},{12,8},{13... | collective-permute-start | bytes 1179656 | tf_op jit(solution)/shard_map/ppermute | solution.py:204
  99.8 1.7 %collective-permute-start.17 = (f32[328,256]{1,0:T(8,128)S(1)}, f32[328,256]{1,0:T(8,128)S(1)}, u32[]{:S(2)}, u32[]{:S(2)}) collective-permute-start(f32[328,256]{1,0:T(8,128)S(1)} %turned.1.own_ref), channel_id=1, source_target_pairs={{0,1},{1,0},{2,3},{3,2},{4,5},{5,4},{6,7},{7,6},{8,9},{9,8},{10,11... | collective-permute-start | bytes 1007624 | tf_op jit(solution)/shard_map/ppermute | solution.py:205
  104.9 4.6 %collective-permute-start.18 = (f32[16,8]{1,0:T(8,128)S(1)}, f32[16,8]{1,0:T(8,128)S(1)}, u32[]{:S(2)}, u32[]{:S(2)}) collective-permute-start(f32[16,8]{1,0:T(8,128)S(1)} %slice_select_fusion), channel_id=1, source_target_pairs={{0,8},{1,9},{2,10},{3,11},{4,12},{5,13},{6,14},{7,15},{8,0},{9,1},... | collective-permute-start | bytes 1544 | tf_op jit(solution)/shard_map/ppermute | solution.py:281
  109.6 3.7 %collective-permute-start.19 = (f32[8,8]{1,0:T(8,128)S(1)}, f32[8,8]{1,0:T(8,128)S(1)}, u32[]{:S(2)}, u32[]{:S(2)}) collective-permute-start(f32[8,8]{1,0:T(8,128)S(1)} %slice_select_fusion.1), channel_id=1, source_target_pairs={{0,4},{1,5},{2,6},{3,7},{4,0},{5,1},{6,2},{7,3},{8,12},{9,13},{10,... | collective-permute-start | bytes 776 | tf_op jit(solution)/shard_map/ppermute | solution.py:281
  113.2 3.6 %collective-permute-start.20 = (f32[4,8]{1,0:T(4,128)S(1)}, f32[4,8]{1,0:T(4,128)S(1)}, u32[]{:S(2)}, u32[]{:S(2)}) collective-permute-start(f32[4,8]{1,0:T(4,128)S(1)} %slice_select_fusion.2), channel_id=1, source_target_pairs={{0,2},{1,3},{2,0},{3,1},{4,6},{5,7},{6,4},{7,5},{8,10},{9,11},{10,... | collective-permute-start | bytes 392 | tf_op jit(solution)/shard_map/ppermute | solution.py:281
  116.9 1.2 %collective-permute-start.21 = (f32[2,8]{1,0:T(2,128)S(1)}, f32[2,8]{1,0:T(2,128)S(1)}, u32[]{:S(2)}, u32[]{:S(2)}) collective-permute-start(f32[2,8]{1,0:T(2,128)S(1)} %broadcast_select_fusion), channel_id=1, source_target_pairs={{0,1},{1,0},{2,3},{3,2},{4,5},{5,4},{6,7},{7,6},{8,9},{9,8},{10,11... | collective-permute-start | bytes 200 | tf_op jit(solution)/shard_map/ppermute | solution.py:281

commit v18 on v15

--- a/solution.py
+++ b/solution.py
@@ -109,6 +109,7 @@
     out_ref[tokens:] = sib_ref[:, :lead]
 
 
+TILE = 8
 EXTRA = 8
 
 
@@ -152,13 +153,15 @@
     out_ref[2 * tokens:] = numbers
 
 
-def score_kernel(window_ref, block_ref, total_ref, inn_ref, table_ref):
+def score_kernel(per_device, window_ref, block_ref, total_ref, inn_ref, table_ref):
     height, columns = total_ref.shape
-    queries = columns // RANK
-    column = lax.broadcasted_iota(jnp.int32, (columns, queries), 0) // RANK
-    query = lax.broadcasted_iota(jnp.int32, (columns, queries), 1)
+    lanes = table_ref.shape[1]
+    column = lax.broadcasted_iota(jnp.int32, (columns, lanes), 0) // RANK
+    query = lax.broadcasted_iota(jnp.int32, (columns, lanes), 1)
     fold = (column == query).astype(F32)
-    row = lax.broadcasted_iota(jnp.int32, table_ref.shape, 0).astype(F32)
+    at = lax.broadcasted_iota(jnp.int32, table_ref.shape, 0)
+    within = lax.rem(at, TILE)
+    row = jnp.where(within < per_device, lax.div(at, TILE) * per_device + within, -1).astype(F32)
     contrib = (total_ref[...] + dot(window_ref[...], block_ref[...])) * inn_ref[:height]
     count = height // LEN
     sums = [jnp.sum(contrib[i * LEN:(i + 1) * LEN], axis=0, keepdims=True) for i in range(count)]
@@ -172,15 +175,15 @@
     table_ref[...] = table
 
 
-def score_table(arrays, rows, queries):
+def score_table(arrays, per_device, devices):
     vmem = pl.BlockSpec(memory_space=pltpu.VMEM)
     window, block = arrays[:2]
     size = sum(x.size * x.dtype.itemsize for x in arrays)
     return pl.pallas_call(
-        score_kernel,
+        functools.partial(score_kernel, per_device),
         in_specs=[vmem] * len(arrays),
         out_specs=vmem,
-        out_shape=jax.ShapeDtypeStruct((rows, queries), F32),
+        out_shape=jax.ShapeDtypeStruct((devices * TILE, 128), F32),
         cost_estimate=pl.CostEstimate(
             flops=2 * window.size * block.shape[1], bytes_accessed=size, transcendentals=0
         ),
@@ -270,9 +273,9 @@
     totals = step(mine, tokens_of, [late], pieces[last][:1], totals, last)
 
     queries = columns // RANK
-    table = score_table([window, early, totals["out"], inn], slots * devices, queries)
-    got = lax.all_to_all(table.reshape(devices, slots, queries), "dp", 0, 0, tiled=True)
-    return jnp.sum(got, axis=0)
+    table = score_table([window, early, totals["out"], inn], slots, devices)
+    got = lax.all_to_all(table.reshape(devices, TILE, -1), "dp", 0, 0, tiled=True)
+    return jnp.sum(got[:, :slots, :queries], axis=0)
 
 
 def solution(mesh):

time: 118 us -> 118 us (level)
  no operation moved by 1% of the time
where the time goes in v18:
time: 118 us
  waiting for transfers between devices  49.4 us (42%)
  starting transfers between devices  27.2 us (23%)
  Pallas kernels  26.5 us (22%)
  blocking collectives  13.1 us (11%)
    ppermute x14, waiting for transfers between devices, shards(): send = lambda x: lax.ppermute(x, 'dp', pairs)  41.5 us
    pallas_call x11, Pallas kernels, call(): pl.pallas_call(kernel, grid_spec=pltpu.PrefetchScalarGridSpec(num_scalar_...  25.9 us
    ppermute x14, starting transfers between devices, shards(): send = lambda x: lax.ppermute(x, 'dp', pairs)  24.4 us
    all_to_all x1, blocking collectives, shards(): lax.all_to_all(table.reshape(devices, TILE, -1), 'dp', 0, 0, tiled=True)  13.1 us
    ppermute x1, waiting for transfers between devices, shards(): turned = lax.ppermute(turned, 'dp', [(j, i) for i, j in pairs])  6.32 us
  transfers between devices with their start and end apart: 18, of which 11 were waited for; matrix products, arithmetic and copies ran while one was open for 1% of the time, Pallas kernels for 22%

profile of v18, /device:TPU:0, one launch (start us, length us, event | category | flops | bytes accessed | tf_op | source)
XLA Modules:
  0.0 117.9 jit_solution(10220229237737012353)
XLA Ops:
  0.0 0.0 copy-start
  0.0 0.0 copy-start.1
  0.0 0.5 collective-permute-start.10
  0.5 2.6 %collective-permute-start.1 = (bf16[2048,256]{1,0:T(8,128)(2,1)}, bf16[2048,256]{1,0:T(8,128)(2,1)S(1)}, u32[]{:S(2)}, u32[]{:S(2)}) collective-permute-start(bf16[2048,256]{1,0:T(8,128)(2,1)} %refs_4_.2), channel_id=1, source_target_pairs={{2,6},{3,1},{6,10},{7,3},{10,14},{11,7},{14,12},{15,11},{12,8},{13... | collective-permute-start | bytes 3145736 | tf_op jit(solution)/shard_map/ppermute | solution.py:207
  3.0 0.2 collective-permute-start.9
  3.3 1.4 %collective-permute-start = (bf16[512,256]{1,0:T(8,128)(2,1)}, bf16[512,256]{1,0:T(8,128)(2,1)S(1)}, u32[]{:S(2)}, u32[]{:S(2)}) collective-permute-start(bf16[512,256]{1,0:T(8,128)(2,1)} %refs_5_.2), channel_id=1, source_target_pairs={{2,6},{3,1},{6,10},{7,3},{10,14},{11,7},{14,12},{15,11},{12,8},{13... | collective-permute-start | bytes 786440 | tf_op jit(solution)/shard_map/ppermute | solution.py:207
  4.6 11.5 %collective-permute-done.1 = bf16[2048,256]{1,0:T(8,128)(2,1)S(1)} collective-permute-done((bf16[2048,256]{1,0:T(8,128)(2,1)}, bf16[2048,256]{1,0:T(8,128)(2,1)S(1)}, u32[]{:S(2)}, u32[]{:S(2)}) %collective-permute-start.1) | collective-permute-done | bytes 1048608 | tf_op jit(solution)/shard_map/ppermute | solution.py:207
  16.1 2.0 %collective-permute-start.2 = (bf16[512,256]{1,0:T(8,128)(2,1)}, bf16[512,256]{1,0:T(8,128)(2,1)S(1)}, u32[]{:S(2)}, u32[]{:S(2)}) collective-permute-start(bf16[512,256]{1,0:T(8,128)(2,1)} %refs_5_.2), channel_id=1, source_target_pairs={{6,2},{1,3},{10,6},{3,7},{14,10},{7,11},{12,14},{11,15},{8,12},{15... | collective-permute-start | bytes 786440 | tf_op jit(solution)/shard_map/ppermute | solution.py:226
  18.1 0.1 collective-permute-start.6
  18.3 0.7 collective-permute-done
  19.0 6.3 %collective-permute-done.2.refs_2_ = bf16[512,256]{1,0:T(8,128)(2,1)S(1)} collective-permute-done((bf16[512,256]{1,0:T(8,128)(2,1)}, bf16[512,256]{1,0:T(8,128)(2,1)S(1)}, u32[]{:S(2)}, u32[]{:S(2)}) %collective-permute-start.2) | collective-permute-done | bytes 262176 | tf_op jit(solution)/shard_map/ppermute | solution.py:226
  25.3 0.0 copy-start.4
  25.3 2.2 %collective-permute-start.3 = (bf16[1280,256]{1,0:T(8,128)(2,1)S(1)}, bf16[1280,256]{1,0:T(8,128)(2,1)S(1)}, u32[]{:S(2)}, u32[]{:S(2)}) collective-permute-start(bf16[1280,256]{1,0:T(8,128)(2,1)S(1)} %pad_maximum_fusion.refs_5_), channel_id=1, source_target_pairs={{2,6},{3,1},{6,10},{7,3},{10,14},{11,7},{14,12},{15,11},{12,8},{13... | collective-permute-start | bytes 1966088 | tf_op jit(solution)/shard_map/ppermute | solution.py:207
  27.5 1.2 %collective-permute-done.6.refs_4_ = bf16[1280,256]{1,0:T(8,128)(2,1)S(1)} collective-permute-done((bf16[1280,256]{1,0:T(8,128)(2,1)S(1)}, bf16[1280,256]{1,0:T(8,128)(2,1)S(1)}, u32[]{:S(2)}, u32[]{:S(2)}) %collective-permute-start.6) | collective-permute-done | bytes 655392 | tf_op jit(solution)/shard_map/ppermute | solution.py:207
  28.8 1.9 %collective-permute-start.7 = (bf16[1280,256]{1,0:T(8,128)(2,1)S(1)}, bf16[1280,256]{1,0:T(8,128)(2,1)}, u32[]{:S(2)}, u32[]{:S(2)}) collective-permute-start(bf16[1280,256]{1,0:T(8,128)(2,1)S(1)} %collective-permute-done.6.refs_4_), channel_id=1, source_target_pairs={{2,6},{3,1},{6,10},{7,3},{10,14},{11,7},{14,12},{15,11},{12,8},{13... | collective-permute-start | bytes 1966088 | tf_op jit(solution)/shard_map/ppermute | solution.py:207
  30.7 5.5 %collective-permute-done.3.refs_5_ = bf16[1280,256]{1,0:T(8,128)(2,1)S(1)} collective-permute-done((bf16[1280,256]{1,0:T(8,128)(2,1)S(1)}, bf16[1280,256]{1,0:T(8,128)(2,1)S(1)}, u32[]{:S(2)}, u32[]{:S(2)}) %collective-permute-start.3) | collective-permute-done | bytes 655392 | tf_op jit(solution)/shard_map/ppermute | solution.py:207
  36.2 1.9 %collective-permute-start.4 = (bf16[1280,256]{1,0:T(8,128)(2,1)S(1)}, bf16[1280,256]{1,0:T(8,128)(2,1)}, u32[]{:S(2)}, u32[]{:S(2)}) collective-permute-start(bf16[1280,256]{1,0:T(8,128)(2,1)S(1)} %collective-permute-done.3.refs_5_), channel_id=1, source_target_pairs={{2,6},{3,1},{6,10},{7,3},{10,14},{11,7},{14,12},{15,11},{12,8},{13... | collective-permute-start | bytes 1966088 | tf_op jit(solution)/shard_map/ppermute | solution.py:207
  38.1 0.0 copy-done.4
  38.1 5.2 %collective-permute-done.7.refs_4_ = bf16[1280,256]{1,0:T(8,128)(2,1)} collective-permute-done((bf16[1280,256]{1,0:T(8,128)(2,1)S(1)}, bf16[1280,256]{1,0:T(8,128)(2,1)}, u32[]{:S(2)}, u32[]{:S(2)}) %collective-permute-start.7) | collective-permute-done | bytes 655392 | tf_op jit(solution)/shard_map/ppermute | solution.py:207
  43.4 0.0 copy-done.6
  43.4 1.9 %collective-permute-start.8 = (bf16[1280,256]{1,0:T(8,128)(2,1)}, bf16[1280,256]{1,0:T(8,128)(2,1)S(1)}, u32[]{:S(2)}, u32[]{:S(2)}) collective-permute-start(bf16[1280,256]{1,0:T(8,128)(2,1)} %collective-permute-done.7.refs_4_), channel_id=1, source_target_pairs={{2,6},{3,1},{6,10},{7,3},{10,14},{11,7},{14,12},{15,11},{12,8},{13... | collective-permute-start | bytes 1966088 | tf_op jit(solution)/shard_map/ppermute | solution.py:207
  45.3 5.1 %collective-permute-done.4.refs_5_ = bf16[1280,256]{1,0:T(8,128)(2,1)} collective-permute-done((bf16[1280,256]{1,0:T(8,128)(2,1)S(1)}, bf16[1280,256]{1,0:T(8,128)(2,1)}, u32[]{:S(2)}, u32[]{:S(2)}) %collective-permute-start.4) | collective-permute-done | bytes 655392 | tf_op jit(solution)/shard_map/ppermute | solution.py:207
  50.4 1.9 %collective-permute-start.5 = (bf16[1280,256]{1,0:T(8,128)(2,1)}, bf16[1280,256]{1,0:T(8,128)(2,1)}, u32[]{:S(2)}, u32[]{:S(2)}) collective-permute-start(bf16[1280,256]{1,0:T(8,128)(2,1)} %collective-permute-done.4.refs_5_), channel_id=1, source_target_pairs={{2,6},{3,1},{6,10},{7,3},{10,14},{11,7},{14,12},{15,11},{12,8},{13... | collective-permute-start | bytes 1966088 | tf_op jit(solution)/shard_map/ppermute | solution.py:207
  52.3 0.7 dynamic-slice_bitcast_fusion.order_ref
  53.0 0.0 collective-permute-done.9.refs_1_
  53.0 0.0 collective-permute-done.10.refs_3_.sib_ref.refs_1_
  53.0 0.0 copy-done
  53.0 0.0 copy-done.1
  53.0 2.6 %step.8 = (f32[320,256]{1,0:T(8,128)S(1)}, f32[320,256]{1,0:T(8,128)S(1)}) custom-call(s32[8]{0:T(128)S(1)} %dynamic-slice_bitcast_fusion.order_ref, bf16[160,8192]{1,0:T(8,128)(2,1)} %refs_0_.17, bf16[160,8192]{1,0:T(8,128)(2,1)} %collective-permute-done.9.refs_1_, bf16[160,32768]{1,0:T(8,128)(2,1)} %refs_0_.16, ...), custom_call_target="tpu_custom_call" | custom-call | flops 419430400 | bytes 3604480 | tf_op jit(solution)/shard_map/step/pallas_call | solution.py:59
  55.6 2.8 %step.9 = (f32[320,256]{1,0:T(8,128)S(1)}, f32[320,256]{1,0:T(8,128)S(1)}) custom-call(s32[8]{0:T(128)S(1)} %dynamic-slice_bitcast_fusion.order_ref, bf16[160,8192]{1,0:T(8,128)(2,1)} %refs_0_.17, bf16[160,8192]{1,0:T(8,128)(2,1)} %collective-permute-done.9.refs_1_, bf16[160,32768]{1,0:T(8,128)(2,1)} %refs_0_.16, ...), custom_call_target="tpu_custom_call" | custom-call | flops 419430400 | bytes 4259840 | tf_op jit(solution)/shard_map/step/pallas_call | solution.py:59
  58.4 0.0 collective-permute-done.8.refs_4_
  58.4 1.6 %collective-permute-start.12 = (bf16[1280,256]{1,0:T(8,128)(2,1)S(1)}, bf16[1280,256]{1,0:T(8,128)(2,1)S(1)}, u32[]{:S(2)}, u32[]{:S(2)}) collective-permute-start(bf16[1280,256]{1,0:T(8,128)(2,1)S(1)} %collective-permute-done.8.refs_4_), channel_id=1, source_target_pairs={{2,6},{3,1},{6,10},{7,3},{10,14},{11,7},{14,12},{15,11},{12,8},{13... | collective-permute-start | bytes 1966088 | tf_op jit(solution)/shard_map/ppermute | solution.py:207
  60.0 4.4 %collective-permute-done.5.refs_5_ = bf16[1280,256]{1,0:T(8,128)(2,1)} collective-permute-done((bf16[1280,256]{1,0:T(8,128)(2,1)}, bf16[1280,256]{1,0:T(8,128)(2,1)}, u32[]{:S(2)}, u32[]{:S(2)}) %collective-permute-start.5) | collective-permute-done | bytes 655392 | tf_op jit(solution)/shard_map/ppermute | solution.py:207
  64.4 1.9 %collective-permute-start.11 = (bf16[1280,256]{1,0:T(8,128)(2,1)}, bf16[1280,256]{1,0:T(8,128)(2,1)S(1)}, u32[]{:S(2)}, u32[]{:S(2)}) collective-permute-start(bf16[1280,256]{1,0:T(8,128)(2,1)} %collective-permute-done.5.refs_5_), channel_id=1, source_target_pairs={{2,6},{3,1},{6,10},{7,3},{10,14},{11,7},{14,12},{15,11},{12,8},{13... | collective-permute-start | bytes 1966088 | tf_op jit(solution)/shard_map/ppermute | solution.py:207
  66.3 2.8 %step.10 = (f32[320,256]{1,0:T(8,128)S(1)}, f32[320,256]{1,0:T(8,128)S(1)}) custom-call(s32[8]{0:T(128)S(1)} %dynamic-slice_bitcast_fusion.order_ref, bf16[160,8192]{1,0:T(8,128)(2,1)} %refs_0_.17, bf16[160,8192]{1,0:T(8,128)(2,1)} %collective-permute-done.9.refs_1_, bf16[160,32768]{1,0:T(8,128)(2,1)} %refs_0_.16, ...), custom_call_target="tpu_custom_call" | custom-call | flops 419430400 | bytes 4259840 | tf_op jit(solution)/shard_map/step/pallas_call | solution.py:59
  69.1 3.0 %step.11 = (f32[320,256]{1,0:T(8,128)S(1)}, f32[320,256]{1,0:T(8,128)S(1)}) custom-call(s32[8]{0:T(128)S(1)} %dynamic-slice_bitcast_fusion.order_ref, bf16[160,8192]{1,0:T(8,128)(2,1)} %refs_0_.17, bf16[160,8192]{1,0:T(8,128)(2,1)} %collective-permute-done.9.refs_1_, bf16[160,32768]{1,0:T(8,128)(2,1)} %refs_0_.16, ...), custom_call_target="tpu_custom_call" | custom-call | flops 419430400 | bytes 4259840 | tf_op jit(solution)/shard_map/step/pallas_call | solution.py:59
  72.1 0.0 collective-permute-done.12.refs_4_
  72.1 1.6 %collective-permute-start.14 = (bf16[1280,256]{1,0:T(8,128)(2,1)S(1)}, bf16[1280,256]{1,0:T(8,128)(2,1)S(1)}, u32[]{:S(2)}, u32[]{:S(2)}) collective-permute-start(bf16[1280,256]{1,0:T(8,128)(2,1)S(1)} %collective-permute-done.12.refs_4_), channel_id=1, source_target_pairs={{2,6},{3,1},{6,10},{7,3},{10,14},{11,7},{14,12},{15,11},{12,8},{13... | collective-permute-start | bytes 1966088 | tf_op jit(solution)/shard_map/ppermute | solution.py:207
  73.7 4.6 %collective-permute-done.11.refs_5_ = bf16[1280,256]{1,0:T(8,128)(2,1)S(1)} collective-permute-done((bf16[1280,256]{1,0:T(8,128)(2,1)}, bf16[1280,256]{1,0:T(8,128)(2,1)S(1)}, u32[]{:S(2)}, u32[]{:S(2)}) %collective-permute-start.11) | collective-permute-done | bytes 655392 | tf_op jit(solution)/shard_map/ppermute | solution.py:207
  78.4 1.9 %collective-permute-start.13 = (bf16[1280,256]{1,0:T(8,128)(2,1)S(1)}, bf16[1280,256]{1,0:T(8,128)(2,1)S(1)}, u32[]{:S(2)}, u32[]{:S(2)}) collective-permute-start(bf16[1280,256]{1,0:T(8,128)(2,1)S(1)} %collective-permute-done.11.refs_5_), channel_id=1, source_target_pairs={{2,6},{3,1},{6,10},{7,3},{10,14},{11,7},{14,12},{15,11},{12,8},{13... | collective-permute-start | bytes 1966088 | tf_op jit(solution)/shard_map/ppermute | solution.py:207
  80.3 2.8 %step.12 = (f32[320,256]{1,0:T(8,128)S(1)}, f32[320,256]{1,0:T(8,128)S(1)}) custom-call(s32[8]{0:T(128)S(1)} %dynamic-slice_bitcast_fusion.order_ref, bf16[160,8192]{1,0:T(8,128)(2,1)} %refs_0_.17, bf16[160,8192]{1,0:T(8,128)(2,1)} %collective-permute-done.9.refs_1_, bf16[160,32768]{1,0:T(8,128)(2,1)} %refs_0_.16, ...), custom_call_target="tpu_custom_call" | custom-call | flops 419430400 | bytes 4259840 | tf_op jit(solution)/shard_map/step/pallas_call | solution.py:59
  83.0 0.0 copy-done.7
  83.1 2.8 %step.13 = (f32[320,256]{1,0:T(8,128)S(1)}, f32[320,256]{1,0:T(8,128)S(1)}) custom-call(s32[8]{0:T(128)S(1)} %dynamic-slice_bitcast_fusion.order_ref, bf16[160,8192]{1,0:T(8,128)(2,1)} %refs_0_.17, bf16[160,8192]{1,0:T(8,128)(2,1)} %collective-permute-done.9.refs_1_, bf16[160,32768]{1,0:T(8,128)(2,1)} %refs_0_.16, ...), custom_call_target="tpu_custom_call" | custom-call | flops 419430400 | bytes 4259840 | tf_op jit(solution)/shard_map/step/pallas_call | solution.py:59
  85.8 0.0 collective-permute-done.14.refs_4_
  85.9 1.6 %collective-permute-start.16 = (bf16[1280,256]{1,0:T(8,128)(2,1)S(1)}, bf16[1280,256]{1,0:T(8,128)(2,1)S(1)}, u32[]{:S(2)}, u32[]{:S(2)}) collective-permute-start(bf16[1280,256]{1,0:T(8,128)(2,1)S(1)} %collective-permute-done.14.refs_4_), channel_id=1, source_target_pairs={{2,6},{3,1},{6,10},{7,3},{10,14},{11,7},{14,12},{15,11},{12,8},{13... | collective-permute-start | bytes 1966088 | tf_op jit(solution)/shard_map/ppermute | solution.py:207
  87.5 1.9 %window.1.window_ref = bf16[320,768]{1,0:T(8,128)(2,1)S(1)} custom-call(s32[8]{0:T(128)S(1)} %dynamic-slice_bitcast_fusion.order_ref, bf16[160,32768]{1,0:T(8,128)(2,1)} %refs_0_.16, bf16[160,32768]{1,0:T(8,128)(2,1)} %collective-permute-done.10.refs_3_.sib_ref.refs_1_), custom_call_target="tpu_custom_call" | custom-call | bytes 1802240 | tf_op jit(solution)/shard_map/window/pallas_call | solution.py:59
  89.3 3.1 %collective-permute-done.13.refs_5_ = bf16[1280,256]{1,0:T(8,128)(2,1)S(1)} collective-permute-done((bf16[1280,256]{1,0:T(8,128)(2,1)S(1)}, bf16[1280,256]{1,0:T(8,128)(2,1)S(1)}, u32[]{:S(2)}, u32[]{:S(2)}) %collective-permute-start.13) | collective-permute-done | bytes 655392 | tf_op jit(solution)/shard_map/ppermute | solution.py:207
  92.4 0.0 copy-start.2
  92.5 0.0 copy-start.3
  92.5 2.0 %collective-permute-start.15 = (bf16[768,256]{1,0:T(8,128)(2,1)S(1)}, bf16[768,256]{1,0:T(8,128)(2,1)S(1)}, u32[]{:S(2)}, u32[]{:S(2)}) collective-permute-start(bf16[768,256]{1,0:T(8,128)(2,1)S(1)} %slice.14), channel_id=1, source_target_pairs={{2,6},{3,1},{6,10},{7,3},{10,14},{11,7},{14,12},{15,11},{12,8},{13... | collective-permute-start | bytes 1179656 | tf_op jit(solution)/shard_map/ppermute | solution.py:207
  94.4 0.0 copy-done.5
  94.4 2.8 %step.14 = (f32[320,256]{1,0:T(8,128)S(1)}, f32[320,256]{1,0:T(8,128)S(1)}) custom-call(s32[8]{0:T(128)S(1)} %dynamic-slice_bitcast_fusion.order_ref, bf16[160,8192]{1,0:T(8,128)(2,1)} %refs_0_.17, bf16[160,8192]{1,0:T(8,128)(2,1)} %collective-permute-done.9.refs_1_, bf16[160,32768]{1,0:T(8,128)(2,1)} %refs_0_.16, ...), custom_call_target="tpu_custom_call" | custom-call | flops 419430400 | bytes 4259840 | tf_op jit(solution)/shard_map/step/pallas_call | solution.py:59
  97.2 0.0 copy-done.2
  97.2 0.0 copy-done.3
  97.2 1.8 %turned.1.own_ref = f32[328,256]{1,0:T(8,128)S(1)} custom-call(s32[8]{0:T(128)S(1)} %dynamic-slice_bitcast_fusion.order_ref, bf16[160,8192]{1,0:T(8,128)(2,1)} %refs_0_.17, bf16[160,8192]{1,0:T(8,128)(2,1)} %collective-permute-done.9.refs_1_, bf16[512,256]{1,0:T(8,128)(2,1)S(1)} %collective-permute-done.2.refs_2_, f32[320,256]{1,0:T(8,128)S(1)} %get-tuple-element.82.refs_3_, ...), custom_call_target="tpu_custom_call" | custom-call | flops 83886080 | bytes 1253376 | tf_op jit(solution)/shard_map/turned/pallas_call | solution.py:59
  99.0 0.1 collective-permute-start.17
  99.1 1.6 %collective-permute-done.17.got_ref = f32[328,256]{1,0:T(8,128)S(1)} collective-permute-done((f32[328,256]{1,0:T(8,128)S(1)}, f32[328,256]{1,0:T(8,128)S(1)}, u32[]{:S(2)}, u32[]{:S(2)}) %collective-permute-start.17) | collective-permute-done | bytes 335904 | tf_op jit(solution)/shard_map/ppermute | solution.py:208
  100.7 0.6 masked.1.inn_ref
  101.4 0.0 collective-permute-done.16.refs_2_
  101.4 2.2 %step.15.total_ref = f32[320,256]{1,0:T(8,128)S(1)} custom-call(s32[8]{0:T(128)S(1)} %dynamic-slice_bitcast_fusion.order_ref, bf16[160,32768]{1,0:T(8,128)(2,1)} %refs_0_.16, bf16[160,32768]{1,0:T(8,128)(2,1)} %collective-permute-done.10.refs_3_.sib_ref.refs_1_, bf16[1280,256]{1,0:T(8,128)(2,1)S(1)} %collective-permute-done.16.refs_2_, ...), custom_call_target="tpu_custom_call" | custom-call | flops 209715200 | bytes 2621440 | tf_op jit(solution)/shard_map/step/pallas_call | solution.py:59
  103.6 0.0 collective-permute-done.15.block_ref
  103.6 0.6 score.1
  104.2 13.1 %all_to_all.5 = f32[16,8,128]{2,1,0:T(8,128)S(1)} all-to-all(f32[16,8,128]{2,1,0:T(8,128)S(1)} %bitcast.3), channel_id=1, replica_groups=mesh['groups'=2,'dp'=16] {'dp'}, dimensions={0} | all-to-all | bytes 131072 | tf_op jit(solution)/shard_map/all_to_all | solution.py:277
  117.3 0.6 slice_reduce_fusion
  (7 shorter events, 0.1 us)
Async XLA Ops:
  0.0 53.0 %copy-start = (bf16[2048,256]{1,0:T(8,128)(2,1)S(1)}, bf16[2048,256]{1,0:T(8,128)(2,1)}, u32[]{:S(2)}) copy-start(bf16[2048,256]{1,0:T(8,128)(2,1)} %refs_4_.2) | copy-start | bytes 3145732
  0.0 53.0 %copy-start.1 = (bf16[512,256]{1,0:T(8,128)(2,1)S(1)}, bf16[512,256]{1,0:T(8,128)(2,1)}, u32[]{:S(2)}) copy-start(bf16[512,256]{1,0:T(8,128)(2,1)} %refs_5_.2) | copy-start | bytes 786436
  0.0 53.0 %collective-permute-start.10 = (bf16[160,32768]{1,0:T(8,128)(2,1)}, bf16[160,32768]{1,0:T(8,128)(2,1)}, u32[]{:S(2)}, u32[]{:S(2)}) collective-permute-start(bf16[160,32768]{1,0:T(8,128)(2,1)} %refs_0_.16), channel_id=1, source_target_pairs={{0,1},{1,0},{2,3},{3,2},{4,5},{5,4},{6,7},{7,6},{8,9},{9,8},{10,11... | collective-permute-start | bytes 31457288 | tf_op jit(solution)/shard_map/ppermute | solution.py:208
  0.5 15.6 %collective-permute-start.1 = (bf16[2048,256]{1,0:T(8,128)(2,1)}, bf16[2048,256]{1,0:T(8,128)(2,1)S(1)}, u32[]{:S(2)}, u32[]{:S(2)}) collective-permute-start(bf16[2048,256]{1,0:T(8,128)(2,1)} %refs_4_.2), channel_id=1, source_target_pairs={{2,6},{3,1},{6,10},{7,3},{10,14},{11,7},{14,12},{15,11},{12,8},{13... | collective-permute-start | bytes 3145736 | tf_op jit(solution)/shard_map/ppermute | solution.py:207
  3.0 49.9 %collective-permute-start.9 = (bf16[160,8192]{1,0:T(8,128)(2,1)}, bf16[160,8192]{1,0:T(8,128)(2,1)}, u32[]{:S(2)}, u32[]{:S(2)}) collective-permute-start(bf16[160,8192]{1,0:T(8,128)(2,1)} %refs_0_.17), channel_id=1, source_target_pairs={{0,1},{1,0},{2,3},{3,2},{4,5},{5,4},{6,7},{7,6},{8,9},{9,8},{10,11... | collective-permute-start | bytes 7864328 | tf_op jit(solution)/shard_map/ppermute | solution.py:208
  3.3 15.7 %collective-permute-start = (bf16[512,256]{1,0:T(8,128)(2,1)}, bf16[512,256]{1,0:T(8,128)(2,1)S(1)}, u32[]{:S(2)}, u32[]{:S(2)}) collective-permute-start(bf16[512,256]{1,0:T(8,128)(2,1)} %refs_5_.2), channel_id=1, source_target_pairs={{2,6},{3,1},{6,10},{7,3},{10,14},{11,7},{14,12},{15,11},{12,8},{13... | collective-permute-start | bytes 786440 | tf_op jit(solution)/shard_map/ppermute | solution.py:207
  16.1 9.2 %collective-permute-start.2 = (bf16[512,256]{1,0:T(8,128)(2,1)}, bf16[512,256]{1,0:T(8,128)(2,1)S(1)}, u32[]{:S(2)}, u32[]{:S(2)}) collective-permute-start(bf16[512,256]{1,0:T(8,128)(2,1)} %refs_5_.2), channel_id=1, source_target_pairs={{6,2},{1,3},{10,6},{3,7},{14,10},{7,11},{12,14},{11,15},{8,12},{15... | collective-permute-start | bytes 786440 | tf_op jit(solution)/shard_map/ppermute | solution.py:226
  18.1 10.6 %collective-permute-start.6 = (bf16[1280,256]{1,0:T(8,128)(2,1)S(1)}, bf16[1280,256]{1,0:T(8,128)(2,1)S(1)}, u32[]{:S(2)}, u32[]{:S(2)}) collective-permute-start(bf16[1280,256]{1,0:T(8,128)(2,1)S(1)} %slice.13.refs_4_), channel_id=1, source_target_pairs={{2,6},{3,1},{6,10},{7,3},{10,14},{11,7},{14,12},{15,11},{12,8},{13... | collective-permute-start | bytes 1966088 | tf_op jit(solution)/shard_map/ppermute | solution.py:207
  25.3 12.8 %copy-start.4 = (bf16[1280,256]{1,0:T(8,128)(2,1)}, bf16[1280,256]{1,0:T(8,128)(2,1)S(1)}, u32[]{:S(2)}) copy-start(bf16[1280,256]{1,0:T(8,128)(2,1)S(1)} %pad_maximum_fusion.refs_5_) | copy-start | bytes 1966084
  25.3 10.9 %collective-permute-start.3 = (bf16[1280,256]{1,0:T(8,128)(2,1)S(1)}, bf16[1280,256]{1,0:T(8,128)(2,1)S(1)}, u32[]{:S(2)}, u32[]{:S(2)}) collective-permute-start(bf16[1280,256]{1,0:T(8,128)(2,1)S(1)} %pad_maximum_fusion.refs_5_), channel_id=1, source_target_pairs={{2,6},{3,1},{6,10},{7,3},{10,14},{11,7},{14,12},{15,11},{12,8},{13... | collective-permute-start | bytes 1966088 | tf_op jit(solution)/shard_map/ppermute | solution.py:207
  28.8 14.6 %collective-permute-start.7 = (bf16[1280,256]{1,0:T(8,128)(2,1)S(1)}, bf16[1280,256]{1,0:T(8,128)(2,1)}, u32[]{:S(2)}, u32[]{:S(2)}) collective-permute-start(bf16[1280,256]{1,0:T(8,128)(2,1)S(1)} %collective-permute-done.6.refs_4_), channel_id=1, source_target_pairs={{2,6},{3,1},{6,10},{7,3},{10,14},{11,7},{14,12},{15,11},{12,8},{13... | collective-permute-start | bytes 1966088 | tf_op jit(solution)/shard_map/ppermute | solution.py:207
  36.2 7.1 %copy-start.6 = (bf16[1280,256]{1,0:T(8,128)(2,1)}, bf16[1280,256]{1,0:T(8,128)(2,1)S(1)}, u32[]{:S(2)}) copy-start(bf16[1280,256]{1,0:T(8,128)(2,1)S(1)} %collective-permute-done.3.refs_5_) | copy-start | bytes 1966084
  36.2 14.1 %collective-permute-start.4 = (bf16[1280,256]{1,0:T(8,128)(2,1)S(1)}, bf16[1280,256]{1,0:T(8,128)(2,1)}, u32[]{:S(2)}, u32[]{:S(2)}) collective-permute-start(bf16[1280,256]{1,0:T(8,128)(2,1)S(1)} %collective-permute-done.3.refs_5_), channel_id=1, source_target_pairs={{2,6},{3,1},{6,10},{7,3},{10,14},{11,7},{14,12},{15,11},{12,8},{13... | collective-permute-start | bytes 1966088 | tf_op jit(solution)/shard_map/ppermute | solution.py:207
  43.4 15.0 %collective-permute-start.8 = (bf16[1280,256]{1,0:T(8,128)(2,1)}, bf16[1280,256]{1,0:T(8,128)(2,1)S(1)}, u32[]{:S(2)}, u32[]{:S(2)}) collective-permute-start(bf16[1280,256]{1,0:T(8,128)(2,1)} %collective-permute-done.7.refs_4_), channel_id=1, source_target_pairs={{2,6},{3,1},{6,10},{7,3},{10,14},{11,7},{14,12},{15,11},{12,8},{13... | collective-permute-start | bytes 1966088 | tf_op jit(solution)/shard_map/ppermute | solution.py:207
  50.4 14.0 %collective-permute-start.5 = (bf16[1280,256]{1,0:T(8,128)(2,1)}, bf16[1280,256]{1,0:T(8,128)(2,1)}, u32[]{:S(2)}, u32[]{:S(2)}) collective-permute-start(bf16[1280,256]{1,0:T(8,128)(2,1)} %collective-permute-done.4.refs_5_), channel_id=1, source_target_pairs={{2,6},{3,1},{6,10},{7,3},{10,14},{11,7},{14,12},{15,11},{12,8},{13... | collective-permute-start | bytes 1966088 | tf_op jit(solution)/shard_map/ppermute | solution.py:207
  58.4 13.7 %collective-permute-start.12 = (bf16[1280,256]{1,0:T(8,128)(2,1)S(1)}, bf16[1280,256]{1,0:T(8,128)(2,1)S(1)}, u32[]{:S(2)}, u32[]{:S(2)}) collective-permute-start(bf16[1280,256]{1,0:T(8,128)(2,1)S(1)} %collective-permute-done.8.refs_4_), channel_id=1, source_target_pairs={{2,6},{3,1},{6,10},{7,3},{10,14},{11,7},{14,12},{15,11},{12,8},{13... | collective-permute-start | bytes 1966088 | tf_op jit(solution)/shard_map/ppermute | solution.py:207
  64.4 13.9 %collective-permute-start.11 = (bf16[1280,256]{1,0:T(8,128)(2,1)}, bf16[1280,256]{1,0:T(8,128)(2,1)S(1)}, u32[]{:S(2)}, u32[]{:S(2)}) collective-permute-start(bf16[1280,256]{1,0:T(8,128)(2,1)} %collective-permute-done.5.refs_5_), channel_id=1, source_target_pairs={{2,6},{3,1},{6,10},{7,3},{10,14},{11,7},{14,12},{15,11},{12,8},{13... | collective-permute-start | bytes 1966088 | tf_op jit(solution)/shard_map/ppermute | solution.py:207
  72.1 13.8 %collective-permute-start.14 = (bf16[1280,256]{1,0:T(8,128)(2,1)S(1)}, bf16[1280,256]{1,0:T(8,128)(2,1)S(1)}, u32[]{:S(2)}, u32[]{:S(2)}) collective-permute-start(bf16[1280,256]{1,0:T(8,128)(2,1)S(1)} %collective-permute-done.12.refs_4_), channel_id=1, source_target_pairs={{2,6},{3,1},{6,10},{7,3},{10,14},{11,7},{14,12},{15,11},{12,8},{13... | collective-permute-start | bytes 1966088 | tf_op jit(solution)/shard_map/ppermute | solution.py:207
  78.4 4.7 %copy-start.7 = (bf16[1280,256]{1,0:T(8,128)(2,1)}, bf16[1280,256]{1,0:T(8,128)(2,1)S(1)}, u32[]{:S(2)}) copy-start(bf16[1280,256]{1,0:T(8,128)(2,1)S(1)} %collective-permute-done.11.refs_5_) | copy-start | bytes 1966084
  78.4 14.0 %collective-permute-start.13 = (bf16[1280,256]{1,0:T(8,128)(2,1)S(1)}, bf16[1280,256]{1,0:T(8,128)(2,1)S(1)}, u32[]{:S(2)}, u32[]{:S(2)}) collective-permute-start(bf16[1280,256]{1,0:T(8,128)(2,1)S(1)} %collective-permute-done.11.refs_5_), channel_id=1, source_target_pairs={{2,6},{3,1},{6,10},{7,3},{10,14},{11,7},{14,12},{15,11},{12,8},{13... | collective-permute-start | bytes 1966088 | tf_op jit(solution)/shard_map/ppermute | solution.py:207
  85.9 15.5 %collective-permute-start.16 = (bf16[1280,256]{1,0:T(8,128)(2,1)S(1)}, bf16[1280,256]{1,0:T(8,128)(2,1)S(1)}, u32[]{:S(2)}, u32[]{:S(2)}) collective-permute-start(bf16[1280,256]{1,0:T(8,128)(2,1)S(1)} %collective-permute-done.14.refs_4_), channel_id=1, source_target_pairs={{2,6},{3,1},{6,10},{7,3},{10,14},{11,7},{14,12},{15,11},{12,8},{13... | collective-permute-start | bytes 1966088 | tf_op jit(solution)/shard_map/ppermute | solution.py:207
  92.4 2.0 %copy-start.5 = (bf16[1280,256]{1,0:T(8,128)(2,1)}, bf16[1280,256]{1,0:T(8,128)(2,1)S(1)}, u32[]{:S(2)}) copy-start(bf16[1280,256]{1,0:T(8,128)(2,1)S(1)} %collective-permute-done.13.refs_5_) | copy-start | bytes 1966084
  92.4 4.8 %copy-start.2 = (s32[2]{0:T(128)S(1)}, s32[2]{0:T(128)}, u32[]{:S(2)}) copy-start(s32[2]{0:T(128)} %refs_4_.3) | copy-start | bytes 28
  92.5 4.8 %copy-start.3 = (s32[2]{0:T(128)S(1)}, s32[2]{0:T(128)}, u32[]{:S(2)}) copy-start(s32[2]{0:T(128)} %refs_5_.3) | copy-start | bytes 28
  92.5 11.2 %collective-permute-start.15 = (bf16[768,256]{1,0:T(8,128)(2,1)S(1)}, bf16[768,256]{1,0:T(8,128)(2,1)S(1)}, u32[]{:S(2)}, u32[]{:S(2)}) collective-permute-start(bf16[768,256]{1,0:T(8,128)(2,1)S(1)} %slice.14), channel_id=1, source_target_pairs={{2,6},{3,1},{6,10},{7,3},{10,14},{11,7},{14,12},{15,11},{12,8},{13... | collective-permute-start | bytes 1179656 | tf_op jit(solution)/shard_map/ppermute | solution.py:207
  99.0 1.7 %collective-permute-start.17 = (f32[328,256]{1,0:T(8,128)S(1)}, f32[328,256]{1,0:T(8,128)S(1)}, u32[]{:S(2)}, u32[]{:S(2)}) collective-permute-start(f32[328,256]{1,0:T(8,128)S(1)} %turned.1.own_ref), channel_id=1, source_target_pairs={{0,1},{1,0},{2,3},{3,2},{4,5},{5,4},{6,7},{7,6},{8,9},{9,8},{10,11... | collective-permute-start | bytes 1007624 | tf_op jit(solution)/shard_map/ppermute | solution.py:208

commit v19 on v15

--- a/solution.py
+++ b/solution.py
@@ -152,13 +152,15 @@
     out_ref[2 * tokens:] = numbers
 
 
-def score_kernel(window_ref, block_ref, total_ref, inn_ref, table_ref):
+def score_kernel(per_device, window_ref, block_ref, total_ref, inn_ref, table_ref):
     height, columns = total_ref.shape
     queries = columns // RANK
     column = lax.broadcasted_iota(jnp.int32, (columns, queries), 0) // RANK
     query = lax.broadcasted_iota(jnp.int32, (columns, queries), 1)
     fold = (column == query).astype(F32)
-    row = lax.broadcasted_iota(jnp.int32, table_ref.shape, 0).astype(F32)
+    row = lax.broadcasted_iota(jnp.int32, table_ref.shape, 0)
+    owner = table_ref.shape[0] // per_device - 1 - lax.div(row, per_device)
+    row = (owner * per_device + lax.rem(row, per_device)).astype(F32)
     contrib = (total_ref[...] + dot(window_ref[...], block_ref[...])) * inn_ref[:height]
     count = height // LEN
     sums = [jnp.sum(contrib[i * LEN:(i + 1) * LEN], axis=0, keepdims=True) for i in range(count)]
@@ -172,12 +174,12 @@
     table_ref[...] = table
 
 
-def score_table(arrays, rows, queries):
+def score_table(arrays, per_device, rows, queries):
     vmem = pl.BlockSpec(memory_space=pltpu.VMEM)
     window, block = arrays[:2]
     size = sum(x.size * x.dtype.itemsize for x in arrays)
     return pl.pallas_call(
-        score_kernel,
+        functools.partial(score_kernel, per_device),
         in_specs=[vmem] * len(arrays),
         out_specs=vmem,
         out_shape=jax.ShapeDtypeStruct((rows, queries), F32),
@@ -270,8 +272,11 @@
     totals = step(mine, tokens_of, [late], pieces[last][:1], totals, last)
 
     queries = columns // RANK
-    table = score_table([window, early, totals["out"], inn], slots * devices, queries)
-    got = lax.all_to_all(table.reshape(devices, slots, queries), "dp", 0, 0, tiled=True)
+    table = score_table([window, early, totals["out"], inn], slots, slots * devices, queries)
+    groups = [list(reversed(range(devices)))]
+    got = lax.all_to_all(
+        table.reshape(devices, slots, queries), "dp", 0, 0, axis_index_groups=groups, tiled=True
+    )
     return jnp.sum(got, axis=0)
 
 

time: 118 us -> 114 us (0.966)
  blocking collectives: 12.7 us -> 9.17 us
    all_to_all x1, blocking collectives: 12.7 us -> 9.17 us  [shards(): lax.all_to_all(table.reshape(devices, slots, queries), 'dp', 0, 0, axis_i...]
  transfers between devices with their start and end apart: 18 -> 18, of which waited for: 11 -> 11; matrix products, arithmetic and copies ran while one was open for 1% -> 1% of each run, Pallas kernels for 22% -> 23%
where the time goes in v19:
time: 114 us
  waiting for transfers between devices  49.4 us (43%)
  starting transfers between devices  27.2 us (24%)
  Pallas kernels  26.5 us (23%)
  blocking collectives  9.17 us (8%)
    ppermute x14, waiting for transfers between devices, shards(): send = lambda x: lax.ppermute(x, 'dp', pairs)  41.5 us
    pallas_call x11, Pallas kernels, call(): pl.pallas_call(kernel, grid_spec=pltpu.PrefetchScalarGridSpec(num_scalar_...  25.9 us
    ppermute x14, starting transfers between devices, shards(): send = lambda x: lax.ppermute(x, 'dp', pairs)  24.4 us
    all_to_all x1, blocking collectives, shards(): lax.all_to_all(table.reshape(devices, slots, queries), 'dp', 0, 0, axis_i...  9.17 us
    ppermute x1, waiting for transfers between devices, shards(): turned = lax.ppermute(turned, 'dp', [(j, i) for i, j in pairs])  6.32 us
  transfers between devices with their start and end apart: 18, of which 11 were waited for; matrix products, arithmetic and copies ran while one was open for 1% of the time, Pallas kernels for 23%

profile of v19, /device:TPU:0, one launch (start us, length us, event | category | flops | bytes accessed | tf_op | source)
XLA Modules:
  0.0 114.0 jit_solution(15761940219326211357)
XLA Ops:
  0.0 0.0 copy-start
  0.0 0.0 copy-start.1
  0.0 0.5 collective-permute-start.10
  0.5 2.6 %collective-permute-start.1 = (bf16[2048,256]{1,0:T(8,128)(2,1)}, bf16[2048,256]{1,0:T(8,128)(2,1)S(1)}, u32[]{:S(2)}, u32[]{:S(2)}) collective-permute-start(bf16[2048,256]{1,0:T(8,128)(2,1)} %refs_4_.2), channel_id=1, source_target_pairs={{2,6},{3,1},{6,10},{7,3},{10,14},{11,7},{14,12},{15,11},{12,8},{13... | collective-permute-start | bytes 3145736 | tf_op jit(solution)/shard_map/ppermute | solution.py:206
  3.0 0.2 collective-permute-start.9
  3.3 1.4 %collective-permute-start = (bf16[512,256]{1,0:T(8,128)(2,1)}, bf16[512,256]{1,0:T(8,128)(2,1)S(1)}, u32[]{:S(2)}, u32[]{:S(2)}) collective-permute-start(bf16[512,256]{1,0:T(8,128)(2,1)} %refs_5_.2), channel_id=1, source_target_pairs={{2,6},{3,1},{6,10},{7,3},{10,14},{11,7},{14,12},{15,11},{12,8},{13... | collective-permute-start | bytes 786440 | tf_op jit(solution)/shard_map/ppermute | solution.py:206
  4.6 11.5 %collective-permute-done.1 = bf16[2048,256]{1,0:T(8,128)(2,1)S(1)} collective-permute-done((bf16[2048,256]{1,0:T(8,128)(2,1)}, bf16[2048,256]{1,0:T(8,128)(2,1)S(1)}, u32[]{:S(2)}, u32[]{:S(2)}) %collective-permute-start.1) | collective-permute-done | bytes 1048608 | tf_op jit(solution)/shard_map/ppermute | solution.py:206
  16.1 2.0 %collective-permute-start.2 = (bf16[512,256]{1,0:T(8,128)(2,1)}, bf16[512,256]{1,0:T(8,128)(2,1)S(1)}, u32[]{:S(2)}, u32[]{:S(2)}) collective-permute-start(bf16[512,256]{1,0:T(8,128)(2,1)} %refs_5_.2), channel_id=1, source_target_pairs={{6,2},{1,3},{10,6},{3,7},{14,10},{7,11},{12,14},{11,15},{8,12},{15... | collective-permute-start | bytes 786440 | tf_op jit(solution)/shard_map/ppermute | solution.py:225
  18.1 0.1 collective-permute-start.6
  18.3 0.7 collective-permute-done
  19.0 6.3 %collective-permute-done.2.refs_2_ = bf16[512,256]{1,0:T(8,128)(2,1)S(1)} collective-permute-done((bf16[512,256]{1,0:T(8,128)(2,1)}, bf16[512,256]{1,0:T(8,128)(2,1)S(1)}, u32[]{:S(2)}, u32[]{:S(2)}) %collective-permute-start.2) | collective-permute-done | bytes 262176 | tf_op jit(solution)/shard_map/ppermute | solution.py:225
  25.3 0.0 copy-start.4
  25.3 2.2 %collective-permute-start.3 = (bf16[1280,256]{1,0:T(8,128)(2,1)S(1)}, bf16[1280,256]{1,0:T(8,128)(2,1)S(1)}, u32[]{:S(2)}, u32[]{:S(2)}) collective-permute-start(bf16[1280,256]{1,0:T(8,128)(2,1)S(1)} %pad_maximum_fusion.refs_5_), channel_id=1, source_target_pairs={{2,6},{3,1},{6,10},{7,3},{10,14},{11,7},{14,12},{15,11},{12,8},{13... | collective-permute-start | bytes 1966088 | tf_op jit(solution)/shard_map/ppermute | solution.py:206
  27.5 1.2 %collective-permute-done.6.refs_4_ = bf16[1280,256]{1,0:T(8,128)(2,1)S(1)} collective-permute-done((bf16[1280,256]{1,0:T(8,128)(2,1)S(1)}, bf16[1280,256]{1,0:T(8,128)(2,1)S(1)}, u32[]{:S(2)}, u32[]{:S(2)}) %collective-permute-start.6) | collective-permute-done | bytes 655392 | tf_op jit(solution)/shard_map/ppermute | solution.py:206
  28.8 1.9 %collective-permute-start.7 = (bf16[1280,256]{1,0:T(8,128)(2,1)S(1)}, bf16[1280,256]{1,0:T(8,128)(2,1)}, u32[]{:S(2)}, u32[]{:S(2)}) collective-permute-start(bf16[1280,256]{1,0:T(8,128)(2,1)S(1)} %collective-permute-done.6.refs_4_), channel_id=1, source_target_pairs={{2,6},{3,1},{6,10},{7,3},{10,14},{11,7},{14,12},{15,11},{12,8},{13... | collective-permute-start | bytes 1966088 | tf_op jit(solution)/shard_map/ppermute | solution.py:206
  30.7 5.5 %collective-permute-done.3.refs_5_ = bf16[1280,256]{1,0:T(8,128)(2,1)S(1)} collective-permute-done((bf16[1280,256]{1,0:T(8,128)(2,1)S(1)}, bf16[1280,256]{1,0:T(8,128)(2,1)S(1)}, u32[]{:S(2)}, u32[]{:S(2)}) %collective-permute-start.3) | collective-permute-done | bytes 655392 | tf_op jit(solution)/shard_map/ppermute | solution.py:206
  36.2 1.9 %collective-permute-start.4 = (bf16[1280,256]{1,0:T(8,128)(2,1)S(1)}, bf16[1280,256]{1,0:T(8,128)(2,1)}, u32[]{:S(2)}, u32[]{:S(2)}) collective-permute-start(bf16[1280,256]{1,0:T(8,128)(2,1)S(1)} %collective-permute-done.3.refs_5_), channel_id=1, source_target_pairs={{2,6},{3,1},{6,10},{7,3},{10,14},{11,7},{14,12},{15,11},{12,8},{13... | collective-permute-start | bytes 1966088 | tf_op jit(solution)/shard_map/ppermute | solution.py:206
  38.1 0.0 copy-done.4
  38.1 5.2 %collective-permute-done.7.refs_4_ = bf16[1280,256]{1,0:T(8,128)(2,1)} collective-permute-done((bf16[1280,256]{1,0:T(8,128)(2,1)S(1)}, bf16[1280,256]{1,0:T(8,128)(2,1)}, u32[]{:S(2)}, u32[]{:S(2)}) %collective-permute-start.7) | collective-permute-done | bytes 655392 | tf_op jit(solution)/shard_map/ppermute | solution.py:206
  43.4 0.0 copy-done.6
  43.4 1.9 %collective-permute-start.8 = (bf16[1280,256]{1,0:T(8,128)(2,1)}, bf16[1280,256]{1,0:T(8,128)(2,1)S(1)}, u32[]{:S(2)}, u32[]{:S(2)}) collective-permute-start(bf16[1280,256]{1,0:T(8,128)(2,1)} %collective-permute-done.7.refs_4_), channel_id=1, source_target_pairs={{2,6},{3,1},{6,10},{7,3},{10,14},{11,7},{14,12},{15,11},{12,8},{13... | collective-permute-start | bytes 1966088 | tf_op jit(solution)/shard_map/ppermute | solution.py:206
  45.3 5.1 %collective-permute-done.4.refs_5_ = bf16[1280,256]{1,0:T(8,128)(2,1)} collective-permute-done((bf16[1280,256]{1,0:T(8,128)(2,1)S(1)}, bf16[1280,256]{1,0:T(8,128)(2,1)}, u32[]{:S(2)}, u32[]{:S(2)}) %collective-permute-start.4) | collective-permute-done | bytes 655392 | tf_op jit(solution)/shard_map/ppermute | solution.py:206
  50.4 1.9 %collective-permute-start.5 = (bf16[1280,256]{1,0:T(8,128)(2,1)}, bf16[1280,256]{1,0:T(8,128)(2,1)}, u32[]{:S(2)}, u32[]{:S(2)}) collective-permute-start(bf16[1280,256]{1,0:T(8,128)(2,1)} %collective-permute-done.4.refs_5_), channel_id=1, source_target_pairs={{2,6},{3,1},{6,10},{7,3},{10,14},{11,7},{14,12},{15,11},{12,8},{13... | collective-permute-start | bytes 1966088 | tf_op jit(solution)/shard_map/ppermute | solution.py:206
  52.3 0.7 dynamic-slice_bitcast_fusion.order_ref
  53.0 0.0 collective-permute-done.9.refs_1_
  53.0 0.0 collective-permute-done.10.refs_3_.sib_ref.refs_1_
  53.0 0.0 copy-done
  53.0 0.0 copy-done.1
  53.0 2.6 %step.8 = (f32[320,256]{1,0:T(8,128)S(1)}, f32[320,256]{1,0:T(8,128)S(1)}) custom-call(s32[8]{0:T(128)S(1)} %dynamic-slice_bitcast_fusion.order_ref, bf16[160,8192]{1,0:T(8,128)(2,1)} %refs_0_.17, bf16[160,8192]{1,0:T(8,128)(2,1)} %collective-permute-done.9.refs_1_, bf16[160,32768]{1,0:T(8,128)(2,1)} %refs_0_.16, ...), custom_call_target="tpu_custom_call" | custom-call | flops 419430400 | bytes 3604480 | tf_op jit(solution)/shard_map/step/pallas_call | solution.py:59
  55.6 2.8 %step.9 = (f32[320,256]{1,0:T(8,128)S(1)}, f32[320,256]{1,0:T(8,128)S(1)}) custom-call(s32[8]{0:T(128)S(1)} %dynamic-slice_bitcast_fusion.order_ref, bf16[160,8192]{1,0:T(8,128)(2,1)} %refs_0_.17, bf16[160,8192]{1,0:T(8,128)(2,1)} %collective-permute-done.9.refs_1_, bf16[160,32768]{1,0:T(8,128)(2,1)} %refs_0_.16, ...), custom_call_target="tpu_custom_call" | custom-call | flops 419430400 | bytes 4259840 | tf_op jit(solution)/shard_map/step/pallas_call | solution.py:59
  58.4 0.0 collective-permute-done.8.refs_4_
  58.4 1.6 %collective-permute-start.12 = (bf16[1280,256]{1,0:T(8,128)(2,1)S(1)}, bf16[1280,256]{1,0:T(8,128)(2,1)S(1)}, u32[]{:S(2)}, u32[]{:S(2)}) collective-permute-start(bf16[1280,256]{1,0:T(8,128)(2,1)S(1)} %collective-permute-done.8.refs_4_), channel_id=1, source_target_pairs={{2,6},{3,1},{6,10},{7,3},{10,14},{11,7},{14,12},{15,11},{12,8},{13... | collective-permute-start | bytes 1966088 | tf_op jit(solution)/shard_map/ppermute | solution.py:206
  60.0 4.4 %collective-permute-done.5.refs_5_ = bf16[1280,256]{1,0:T(8,128)(2,1)} collective-permute-done((bf16[1280,256]{1,0:T(8,128)(2,1)}, bf16[1280,256]{1,0:T(8,128)(2,1)}, u32[]{:S(2)}, u32[]{:S(2)}) %collective-permute-start.5) | collective-permute-done | bytes 655392 | tf_op jit(solution)/shard_map/ppermute | solution.py:206
  64.4 1.9 %collective-permute-start.11 = (bf16[1280,256]{1,0:T(8,128)(2,1)}, bf16[1280,256]{1,0:T(8,128)(2,1)S(1)}, u32[]{:S(2)}, u32[]{:S(2)}) collective-permute-start(bf16[1280,256]{1,0:T(8,128)(2,1)} %collective-permute-done.5.refs_5_), channel_id=1, source_target_pairs={{2,6},{3,1},{6,10},{7,3},{10,14},{11,7},{14,12},{15,11},{12,8},{13... | collective-permute-start | bytes 1966088 | tf_op jit(solution)/shard_map/ppermute | solution.py:206
  66.3 2.8 %step.10 = (f32[320,256]{1,0:T(8,128)S(1)}, f32[320,256]{1,0:T(8,128)S(1)}) custom-call(s32[8]{0:T(128)S(1)} %dynamic-slice_bitcast_fusion.order_ref, bf16[160,8192]{1,0:T(8,128)(2,1)} %refs_0_.17, bf16[160,8192]{1,0:T(8,128)(2,1)} %collective-permute-done.9.refs_1_, bf16[160,32768]{1,0:T(8,128)(2,1)} %refs_0_.16, ...), custom_call_target="tpu_custom_call" | custom-call | flops 419430400 | bytes 4259840 | tf_op jit(solution)/shard_map/step/pallas_call | solution.py:59
  69.1 3.0 %step.11 = (f32[320,256]{1,0:T(8,128)S(1)}, f32[320,256]{1,0:T(8,128)S(1)}) custom-call(s32[8]{0:T(128)S(1)} %dynamic-slice_bitcast_fusion.order_ref, bf16[160,8192]{1,0:T(8,128)(2,1)} %refs_0_.17, bf16[160,8192]{1,0:T(8,128)(2,1)} %collective-permute-done.9.refs_1_, bf16[160,32768]{1,0:T(8,128)(2,1)} %refs_0_.16, ...), custom_call_target="tpu_custom_call" | custom-call | flops 419430400 | bytes 4259840 | tf_op jit(solution)/shard_map/step/pallas_call | solution.py:59
  72.1 0.0 collective-permute-done.12.refs_4_
  72.1 1.6 %collective-permute-start.14 = (bf16[1280,256]{1,0:T(8,128)(2,1)S(1)}, bf16[1280,256]{1,0:T(8,128)(2,1)S(1)}, u32[]{:S(2)}, u32[]{:S(2)}) collective-permute-start(bf16[1280,256]{1,0:T(8,128)(2,1)S(1)} %collective-permute-done.12.refs_4_), channel_id=1, source_target_pairs={{2,6},{3,1},{6,10},{7,3},{10,14},{11,7},{14,12},{15,11},{12,8},{13... | collective-permute-start | bytes 1966088 | tf_op jit(solution)/shard_map/ppermute | solution.py:206
  73.7 4.6 %collective-permute-done.11.refs_5_ = bf16[1280,256]{1,0:T(8,128)(2,1)S(1)} collective-permute-done((bf16[1280,256]{1,0:T(8,128)(2,1)}, bf16[1280,256]{1,0:T(8,128)(2,1)S(1)}, u32[]{:S(2)}, u32[]{:S(2)}) %collective-permute-start.11) | collective-permute-done | bytes 655392 | tf_op jit(solution)/shard_map/ppermute | solution.py:206
  78.4 1.9 %collective-permute-start.13 = (bf16[1280,256]{1,0:T(8,128)(2,1)S(1)}, bf16[1280,256]{1,0:T(8,128)(2,1)S(1)}, u32[]{:S(2)}, u32[]{:S(2)}) collective-permute-start(bf16[1280,256]{1,0:T(8,128)(2,1)S(1)} %collective-permute-done.11.refs_5_), channel_id=1, source_target_pairs={{2,6},{3,1},{6,10},{7,3},{10,14},{11,7},{14,12},{15,11},{12,8},{13... | collective-permute-start | bytes 1966088 | tf_op jit(solution)/shard_map/ppermute | solution.py:206
  80.3 2.8 %step.12 = (f32[320,256]{1,0:T(8,128)S(1)}, f32[320,256]{1,0:T(8,128)S(1)}) custom-call(s32[8]{0:T(128)S(1)} %dynamic-slice_bitcast_fusion.order_ref, bf16[160,8192]{1,0:T(8,128)(2,1)} %refs_0_.17, bf16[160,8192]{1,0:T(8,128)(2,1)} %collective-permute-done.9.refs_1_, bf16[160,32768]{1,0:T(8,128)(2,1)} %refs_0_.16, ...), custom_call_target="tpu_custom_call" | custom-call | flops 419430400 | bytes 4259840 | tf_op jit(solution)/shard_map/step/pallas_call | solution.py:59
  83.0 0.0 copy-done.7
  83.1 2.8 %step.13 = (f32[320,256]{1,0:T(8,128)S(1)}, f32[320,256]{1,0:T(8,128)S(1)}) custom-call(s32[8]{0:T(128)S(1)} %dynamic-slice_bitcast_fusion.order_ref, bf16[160,8192]{1,0:T(8,128)(2,1)} %refs_0_.17, bf16[160,8192]{1,0:T(8,128)(2,1)} %collective-permute-done.9.refs_1_, bf16[160,32768]{1,0:T(8,128)(2,1)} %refs_0_.16, ...), custom_call_target="tpu_custom_call" | custom-call | flops 419430400 | bytes 4259840 | tf_op jit(solution)/shard_map/step/pallas_call | solution.py:59
  85.8 0.0 collective-permute-done.14.refs_4_
  85.9 1.6 %collective-permute-start.16 = (bf16[1280,256]{1,0:T(8,128)(2,1)S(1)}, bf16[1280,256]{1,0:T(8,128)(2,1)S(1)}, u32[]{:S(2)}, u32[]{:S(2)}) collective-permute-start(bf16[1280,256]{1,0:T(8,128)(2,1)S(1)} %collective-permute-done.14.refs_4_), channel_id=1, source_target_pairs={{2,6},{3,1},{6,10},{7,3},{10,14},{11,7},{14,12},{15,11},{12,8},{13... | collective-permute-start | bytes 1966088 | tf_op jit(solution)/shard_map/ppermute | solution.py:206
  87.5 1.9 %window.1.window_ref = bf16[320,768]{1,0:T(8,128)(2,1)S(1)} custom-call(s32[8]{0:T(128)S(1)} %dynamic-slice_bitcast_fusion.order_ref, bf16[160,32768]{1,0:T(8,128)(2,1)} %refs_0_.16, bf16[160,32768]{1,0:T(8,128)(2,1)} %collective-permute-done.10.refs_3_.sib_ref.refs_1_), custom_call_target="tpu_custom_call" | custom-call | bytes 1802240 | tf_op jit(solution)/shard_map/window/pallas_call | solution.py:59
  89.3 3.1 %collective-permute-done.13.refs_5_ = bf16[1280,256]{1,0:T(8,128)(2,1)S(1)} collective-permute-done((bf16[1280,256]{1,0:T(8,128)(2,1)S(1)}, bf16[1280,256]{1,0:T(8,128)(2,1)S(1)}, u32[]{:S(2)}, u32[]{:S(2)}) %collective-permute-start.13) | collective-permute-done | bytes 655392 | tf_op jit(solution)/shard_map/ppermute | solution.py:206
  92.4 0.0 copy-start.2
  92.5 0.0 copy-start.3
  92.5 2.0 %collective-permute-start.15 = (bf16[768,256]{1,0:T(8,128)(2,1)S(1)}, bf16[768,256]{1,0:T(8,128)(2,1)S(1)}, u32[]{:S(2)}, u32[]{:S(2)}) collective-permute-start(bf16[768,256]{1,0:T(8,128)(2,1)S(1)} %slice.11), channel_id=1, source_target_pairs={{2,6},{3,1},{6,10},{7,3},{10,14},{11,7},{14,12},{15,11},{12,8},{13... | collective-permute-start | bytes 1179656 | tf_op jit(solution)/shard_map/ppermute | solution.py:206
  94.4 0.0 copy-done.5
  94.4 2.8 %step.14 = (f32[320,256]{1,0:T(8,128)S(1)}, f32[320,256]{1,0:T(8,128)S(1)}) custom-call(s32[8]{0:T(128)S(1)} %dynamic-slice_bitcast_fusion.order_ref, bf16[160,8192]{1,0:T(8,128)(2,1)} %refs_0_.17, bf16[160,8192]{1,0:T(8,128)(2,1)} %collective-permute-done.9.refs_1_, bf16[160,32768]{1,0:T(8,128)(2,1)} %refs_0_.16, ...), custom_call_target="tpu_custom_call" | custom-call | flops 419430400 | bytes 4259840 | tf_op jit(solution)/shard_map/step/pallas_call | solution.py:59
  97.2 0.0 copy-done.2
  97.2 0.0 copy-done.3
  97.2 1.8 %turned.1.own_ref = f32[328,256]{1,0:T(8,128)S(1)} custom-call(s32[8]{0:T(128)S(1)} %dynamic-slice_bitcast_fusion.order_ref, bf16[160,8192]{1,0:T(8,128)(2,1)} %refs_0_.17, bf16[160,8192]{1,0:T(8,128)(2,1)} %collective-permute-done.9.refs_1_, bf16[512,256]{1,0:T(8,128)(2,1)S(1)} %collective-permute-done.2.refs_2_, f32[320,256]{1,0:T(8,128)S(1)} %get-tuple-element.82.refs_3_, ...), custom_call_target="tpu_custom_call" | custom-call | flops 83886080 | bytes 1253376 | tf_op jit(solution)/shard_map/turned/pallas_call | solution.py:59
  99.0 0.1 collective-permute-start.17
  99.1 1.6 %collective-permute-done.17.got_ref = f32[328,256]{1,0:T(8,128)S(1)} collective-permute-done((f32[328,256]{1,0:T(8,128)S(1)}, f32[328,256]{1,0:T(8,128)S(1)}, u32[]{:S(2)}, u32[]{:S(2)}) %collective-permute-start.17) | collective-permute-done | bytes 335904 | tf_op jit(solution)/shard_map/ppermute | solution.py:207
  100.7 0.6 masked.1.inn_ref
  101.4 0.0 collective-permute-done.16.refs_2_
  101.4 2.2 %step.15.total_ref = f32[320,256]{1,0:T(8,128)S(1)} custom-call(s32[8]{0:T(128)S(1)} %dynamic-slice_bitcast_fusion.order_ref, bf16[160,32768]{1,0:T(8,128)(2,1)} %refs_0_.16, bf16[160,32768]{1,0:T(8,128)(2,1)} %collective-permute-done.10.refs_3_.sib_ref.refs_1_, bf16[1280,256]{1,0:T(8,128)(2,1)S(1)} %collective-permute-done.16.refs_2_, ...), custom_call_target="tpu_custom_call" | custom-call | flops 209715200 | bytes 2621440 | tf_op jit(solution)/shard_map/step/pallas_call | solution.py:59
  103.6 0.0 collective-permute-done.15.block_ref
  103.6 0.6 score.1
  104.2 9.2 %all_to_all.5 = f32[16,2,8]{2,1,0:T(2,128)S(1)} all-to-all(f32[16,2,8]{2,1,0:T(2,128)S(1)} %bitcast.3), channel_id=1, replica_groups={{15,14,13,12,11,10,9,8,7,6,5,4,3,2,1,0},{31,30,29,28,27,26,25,24,23,22,..., dimensions={0} | all-to-all | bytes 2048 | tf_op jit(solution)/shard_map/all_to_all | solution.py:277
  113.4 0.6 reduce_sum.9
  (7 shorter events, 0.1 us)
Async XLA Ops:
  0.0 53.0 %copy-start = (bf16[2048,256]{1,0:T(8,128)(2,1)S(1)}, bf16[2048,256]{1,0:T(8,128)(2,1)}, u32[]{:S(2)}) copy-start(bf16[2048,256]{1,0:T(8,128)(2,1)} %refs_4_.2) | copy-start | bytes 3145732
  0.0 53.0 %copy-start.1 = (bf16[512,256]{1,0:T(8,128)(2,1)S(1)}, bf16[512,256]{1,0:T(8,128)(2,1)}, u32[]{:S(2)}) copy-start(bf16[512,256]{1,0:T(8,128)(2,1)} %refs_5_.2) | copy-start | bytes 786436
  0.0 53.0 %collective-permute-start.10 = (bf16[160,32768]{1,0:T(8,128)(2,1)}, bf16[160,32768]{1,0:T(8,128)(2,1)}, u32[]{:S(2)}, u32[]{:S(2)}) collective-permute-start(bf16[160,32768]{1,0:T(8,128)(2,1)} %refs_0_.16), channel_id=1, source_target_pairs={{0,1},{1,0},{2,3},{3,2},{4,5},{5,4},{6,7},{7,6},{8,9},{9,8},{10,11... | collective-permute-start | bytes 31457288 | tf_op jit(solution)/shard_map/ppermute | solution.py:207
  0.5 15.6 %collective-permute-start.1 = (bf16[2048,256]{1,0:T(8,128)(2,1)}, bf16[2048,256]{1,0:T(8,128)(2,1)S(1)}, u32[]{:S(2)}, u32[]{:S(2)}) collective-permute-start(bf16[2048,256]{1,0:T(8,128)(2,1)} %refs_4_.2), channel_id=1, source_target_pairs={{2,6},{3,1},{6,10},{7,3},{10,14},{11,7},{14,12},{15,11},{12,8},{13... | collective-permute-start | bytes 3145736 | tf_op jit(solution)/shard_map/ppermute | solution.py:206
  3.0 49.9 %collective-permute-start.9 = (bf16[160,8192]{1,0:T(8,128)(2,1)}, bf16[160,8192]{1,0:T(8,128)(2,1)}, u32[]{:S(2)}, u32[]{:S(2)}) collective-permute-start(bf16[160,8192]{1,0:T(8,128)(2,1)} %refs_0_.17), channel_id=1, source_target_pairs={{0,1},{1,0},{2,3},{3,2},{4,5},{5,4},{6,7},{7,6},{8,9},{9,8},{10,11... | collective-permute-start | bytes 7864328 | tf_op jit(solution)/shard_map/ppermute | solution.py:207
  3.3 15.7 %collective-permute-start = (bf16[512,256]{1,0:T(8,128)(2,1)}, bf16[512,256]{1,0:T(8,128)(2,1)S(1)}, u32[]{:S(2)}, u32[]{:S(2)}) collective-permute-start(bf16[512,256]{1,0:T(8,128)(2,1)} %refs_5_.2), channel_id=1, source_target_pairs={{2,6},{3,1},{6,10},{7,3},{10,14},{11,7},{14,12},{15,11},{12,8},{13... | collective-permute-start | bytes 786440 | tf_op jit(solution)/shard_map/ppermute | solution.py:206
  16.1 9.2 %collective-permute-start.2 = (bf16[512,256]{1,0:T(8,128)(2,1)}, bf16[512,256]{1,0:T(8,128)(2,1)S(1)}, u32[]{:S(2)}, u32[]{:S(2)}) collective-permute-start(bf16[512,256]{1,0:T(8,128)(2,1)} %refs_5_.2), channel_id=1, source_target_pairs={{6,2},{1,3},{10,6},{3,7},{14,10},{7,11},{12,14},{11,15},{8,12},{15... | collective-permute-start | bytes 786440 | tf_op jit(solution)/shard_map/ppermute | solution.py:225
  18.1 10.6 %collective-permute-start.6 = (bf16[1280,256]{1,0:T(8,128)(2,1)S(1)}, bf16[1280,256]{1,0:T(8,128)(2,1)S(1)}, u32[]{:S(2)}, u32[]{:S(2)}) collective-permute-start(bf16[1280,256]{1,0:T(8,128)(2,1)S(1)} %slice.10.refs_4_), channel_id=1, source_target_pairs={{2,6},{3,1},{6,10},{7,3},{10,14},{11,7},{14,12},{15,11},{12,8},{13... | collective-permute-start | bytes 1966088 | tf_op jit(solution)/shard_map/ppermute | solution.py:206
  25.3 12.8 %copy-start.4 = (bf16[1280,256]{1,0:T(8,128)(2,1)}, bf16[1280,256]{1,0:T(8,128)(2,1)S(1)}, u32[]{:S(2)}) copy-start(bf16[1280,256]{1,0:T(8,128)(2,1)S(1)} %pad_maximum_fusion.refs_5_) | copy-start | bytes 1966084
  25.3 10.9 %collective-permute-start.3 = (bf16[1280,256]{1,0:T(8,128)(2,1)S(1)}, bf16[1280,256]{1,0:T(8,128)(2,1)S(1)}, u32[]{:S(2)}, u32[]{:S(2)}) collective-permute-start(bf16[1280,256]{1,0:T(8,128)(2,1)S(1)} %pad_maximum_fusion.refs_5_), channel_id=1, source_target_pairs={{2,6},{3,1},{6,10},{7,3},{10,14},{11,7},{14,12},{15,11},{12,8},{13... | collective-permute-start | bytes 1966088 | tf_op jit(solution)/shard_map/ppermute | solution.py:206
  28.8 14.6 %collective-permute-start.7 = (bf16[1280,256]{1,0:T(8,128)(2,1)S(1)}, bf16[1280,256]{1,0:T(8,128)(2,1)}, u32[]{:S(2)}, u32[]{:S(2)}) collective-permute-start(bf16[1280,256]{1,0:T(8,128)(2,1)S(1)} %collective-permute-done.6.refs_4_), channel_id=1, source_target_pairs={{2,6},{3,1},{6,10},{7,3},{10,14},{11,7},{14,12},{15,11},{12,8},{13... | collective-permute-start | bytes 1966088 | tf_op jit(solution)/shard_map/ppermute | solution.py:206
  36.2 7.1 %copy-start.6 = (bf16[1280,256]{1,0:T(8,128)(2,1)}, bf16[1280,256]{1,0:T(8,128)(2,1)S(1)}, u32[]{:S(2)}) copy-start(bf16[1280,256]{1,0:T(8,128)(2,1)S(1)} %collective-permute-done.3.refs_5_) | copy-start | bytes 1966084
  36.2 14.1 %collective-permute-start.4 = (bf16[1280,256]{1,0:T(8,128)(2,1)S(1)}, bf16[1280,256]{1,0:T(8,128)(2,1)}, u32[]{:S(2)}, u32[]{:S(2)}) collective-permute-start(bf16[1280,256]{1,0:T(8,128)(2,1)S(1)} %collective-permute-done.3.refs_5_), channel_id=1, source_target_pairs={{2,6},{3,1},{6,10},{7,3},{10,14},{11,7},{14,12},{15,11},{12,8},{13... | collective-permute-start | bytes 1966088 | tf_op jit(solution)/shard_map/ppermute | solution.py:206
  43.4 15.0 %collective-permute-start.8 = (bf16[1280,256]{1,0:T(8,128)(2,1)}, bf16[1280,256]{1,0:T(8,128)(2,1)S(1)}, u32[]{:S(2)}, u32[]{:S(2)}) collective-permute-start(bf16[1280,256]{1,0:T(8,128)(2,1)} %collective-permute-done.7.refs_4_), channel_id=1, source_target_pairs={{2,6},{3,1},{6,10},{7,3},{10,14},{11,7},{14,12},{15,11},{12,8},{13... | collective-permute-start | bytes 1966088 | tf_op jit(solution)/shard_map/ppermute | solution.py:206
  50.4 14.0 %collective-permute-start.5 = (bf16[1280,256]{1,0:T(8,128)(2,1)}, bf16[1280,256]{1,0:T(8,128)(2,1)}, u32[]{:S(2)}, u32[]{:S(2)}) collective-permute-start(bf16[1280,256]{1,0:T(8,128)(2,1)} %collective-permute-done.4.refs_5_), channel_id=1, source_target_pairs={{2,6},{3,1},{6,10},{7,3},{10,14},{11,7},{14,12},{15,11},{12,8},{13... | collective-permute-start | bytes 1966088 | tf_op jit(solution)/shard_map/ppermute | solution.py:206
  58.4 13.7 %collective-permute-start.12 = (bf16[1280,256]{1,0:T(8,128)(2,1)S(1)}, bf16[1280,256]{1,0:T(8,128)(2,1)S(1)}, u32[]{:S(2)}, u32[]{:S(2)}) collective-permute-start(bf16[1280,256]{1,0:T(8,128)(2,1)S(1)} %collective-permute-done.8.refs_4_), channel_id=1, source_target_pairs={{2,6},{3,1},{6,10},{7,3},{10,14},{11,7},{14,12},{15,11},{12,8},{13... | collective-permute-start | bytes 1966088 | tf_op jit(solution)/shard_map/ppermute | solution.py:206
  64.4 13.9 %collective-permute-start.11 = (bf16[1280,256]{1,0:T(8,128)(2,1)}, bf16[1280,256]{1,0:T(8,128)(2,1)S(1)}, u32[]{:S(2)}, u32[]{:S(2)}) collective-permute-start(bf16[1280,256]{1,0:T(8,128)(2,1)} %collective-permute-done.5.refs_5_), channel_id=1, source_target_pairs={{2,6},{3,1},{6,10},{7,3},{10,14},{11,7},{14,12},{15,11},{12,8},{13... | collective-permute-start | bytes 1966088 | tf_op jit(solution)/shard_map/ppermute | solution.py:206
  72.1 13.8 %collective-permute-start.14 = (bf16[1280,256]{1,0:T(8,128)(2,1)S(1)}, bf16[1280,256]{1,0:T(8,128)(2,1)S(1)}, u32[]{:S(2)}, u32[]{:S(2)}) collective-permute-start(bf16[1280,256]{1,0:T(8,128)(2,1)S(1)} %collective-permute-done.12.refs_4_), channel_id=1, source_target_pairs={{2,6},{3,1},{6,10},{7,3},{10,14},{11,7},{14,12},{15,11},{12,8},{13... | collective-permute-start | bytes 1966088 | tf_op jit(solution)/shard_map/ppermute | solution.py:206
  78.4 4.7 %copy-start.7 = (bf16[1280,256]{1,0:T(8,128)(2,1)}, bf16[1280,256]{1,0:T(8,128)(2,1)S(1)}, u32[]{:S(2)}) copy-start(bf16[1280,256]{1,0:T(8,128)(2,1)S(1)} %collective-permute-done.11.refs_5_) | copy-start | bytes 1966084
  78.4 14.0 %collective-permute-start.13 = (bf16[1280,256]{1,0:T(8,128)(2,1)S(1)}, bf16[1280,256]{1,0:T(8,128)(2,1)S(1)}, u32[]{:S(2)}, u32[]{:S(2)}) collective-permute-start(bf16[1280,256]{1,0:T(8,128)(2,1)S(1)} %collective-permute-done.11.refs_5_), channel_id=1, source_target_pairs={{2,6},{3,1},{6,10},{7,3},{10,14},{11,7},{14,12},{15,11},{12,8},{13... | collective-permute-start | bytes 1966088 | tf_op jit(solution)/shard_map/ppermute | solution.py:206
  85.9 15.5 %collective-permute-start.16 = (bf16[1280,256]{1,0:T(8,128)(2,1)S(1)}, bf16[1280,256]{1,0:T(8,128)(2,1)S(1)}, u32[]{:S(2)}, u32[]{:S(2)}) collective-permute-start(bf16[1280,256]{1,0:T(8,128)(2,1)S(1)} %collective-permute-done.14.refs_4_), channel_id=1, source_target_pairs={{2,6},{3,1},{6,10},{7,3},{10,14},{11,7},{14,12},{15,11},{12,8},{13... | collective-permute-start | bytes 1966088 | tf_op jit(solution)/shard_map/ppermute | solution.py:206
  92.4 2.0 %copy-start.5 = (bf16[1280,256]{1,0:T(8,128)(2,1)}, bf16[1280,256]{1,0:T(8,128)(2,1)S(1)}, u32[]{:S(2)}) copy-start(bf16[1280,256]{1,0:T(8,128)(2,1)S(1)} %collective-permute-done.13.refs_5_) | copy-start | bytes 1966084
  92.4 4.8 %copy-start.2 = (s32[2]{0:T(128)S(1)}, s32[2]{0:T(128)}, u32[]{:S(2)}) copy-start(s32[2]{0:T(128)} %refs_4_.3) | copy-start | bytes 28
  92.5 4.8 %copy-start.3 = (s32[2]{0:T(128)S(1)}, s32[2]{0:T(128)}, u32[]{:S(2)}) copy-start(s32[2]{0:T(128)} %refs_5_.3) | copy-start | bytes 28
  92.5 11.2 %collective-permute-start.15 = (bf16[768,256]{1,0:T(8,128)(2,1)S(1)}, bf16[768,256]{1,0:T(8,128)(2,1)S(1)}, u32[]{:S(2)}, u32[]{:S(2)}) collective-permute-start(bf16[768,256]{1,0:T(8,128)(2,1)S(1)} %slice.11), channel_id=1, source_target_pairs={{2,6},{3,1},{6,10},{7,3},{10,14},{11,7},{14,12},{15,11},{12,8},{13... | collective-permute-start | bytes 1179656 | tf_op jit(solution)/shard_map/ppermute | solution.py:206
  99.0 1.7 %collective-permute-start.17 = (f32[328,256]{1,0:T(8,128)S(1)}, f32[328,256]{1,0:T(8,128)S(1)}, u32[]{:S(2)}, u32[]{:S(2)}) collective-permute-start(f32[328,256]{1,0:T(8,128)S(1)} %turned.1.own_ref), channel_id=1, source_target_pairs={{0,1},{1,0},{2,3},{3,2},{4,5},{5,4},{6,7},{7,6},{8,9},{9,8},{10,11... | collective-permute-start | bytes 1007624 | tf_op jit(solution)/shard_map/ppermute | solution.py:207

commit v20 on v19

--- a/solution.py
+++ b/solution.py
@@ -226,6 +226,8 @@
         late, early = came[lead:], came[:lead]
         inner, turned = lax.optimization_barrier((send(in_factors), turned))
         early = jnp.concatenate([inner, early])
+        backward = [(j, i) for i, j in pairs]
+        turned = [turned, lax.ppermute(turned, "dp", backward)]
     totals, summed, last = {}, 0, chips - 1
 
     def sum_to(k, totals, summed):
@@ -235,15 +237,19 @@
 
     for s in range(1, chips):
         held.append([late, early])
-        pieces.append([(0, 0, rows - lead, "out", lead), (1, rows_in, lead, "out", 0)] + inside)
+        top = rows_in if s < last - 1 else 0
+        pieces.append([(0, 0, rows - lead, "out", lead), (1, top, lead, "out", 0)])
+        pieces[s] += inside if top else []
         if s == last:
             break
         if s >= 4:
             totals, summed = sum_to(min(2 * s - 6, s), totals, summed)
             late, totals = lax.optimization_barrier((late, totals))
             early, totals = lax.optimization_barrier((early, totals))
+        if s == 3 and rows_in:
+            early, turned = lax.optimization_barrier((early, turned))
         late = send(late)
-        early = send(early if s < last - 1 else early[rows_in:])
+        early = send(early[rows_in:] if s == last - 2 else early)
 
     window = call(
         functools.partial(window_kernel, lead), mine,
@@ -256,10 +262,13 @@
     height = (2 * tokens + EXTRA, columns)
     if rows_in:
         inn = call(
-            functools.partial(turned_kernel, 1), mine,
-            [(x, rows_in, lambda i, o: (0, o[last])) for x in tokens_of["in"][:2]],
-            [turned, totals["in"]], [seq_slot, lengths],
-            [jax.ShapeDtypeStruct(height, F32)], 4 * tokens * rows_in * columns, "turned",
+            functools.partial(turned_kernel, 2), mine,
+            [
+                (x, rows_in, functools.partial(lambda i, o, k: (0, o[k]), k=last - k))
+                for k in (0, 1) for x in tokens_of["in"][:2]
+            ],
+            turned + [totals["in"]], [seq_slot, lengths],
+            [jax.ShapeDtypeStruct(height, F32)], 8 * tokens * rows_in * columns, "turned",
         )[0]
     else:
         numbers = jnp.concatenate([seq_slot, lengths]).astype(F32)

time: 114 us -> 114 us (level)
    ppermute x0 -> x1, waiting for transfers between devices: none -> 9.22 us  [shards(): turned = [turned, lax.ppermute(turned, 'dp', backward)]]
    ppermute x14, waiting for transfers between devices: 41.5 us -> 34.1 us  [shards(): send = lambda x: lax.ppermute(x, 'dp', pairs)]
    ppermute x3, waiting for transfers between devices: 1.63 us -> 0.01 us  [shards(): across = lambda x: lax.ppermute(x, 'dp', swap)]
  transfers between devices with their start and end apart: 18 -> 19, of which waited for: 11 -> 10; matrix products, arithmetic and copies ran while one was open for 1% -> 1% of each run, Pallas kernels for 23% -> 23%
where the time goes in v20:
time: 114 us
  waiting for transfers between devices  49.7 us (44%)
  starting transfers between devices  27 us (24%)
  Pallas kernels  26.5 us (23%)
  blocking collectives  9.1 us (8%)
    ppermute x14, waiting for transfers between devices, shards(): send = lambda x: lax.ppermute(x, 'dp', pairs)  34.1 us
    pallas_call x11, Pallas kernels, call(): pl.pallas_call(kernel, grid_spec=pltpu.PrefetchScalarGridSpec(num_scalar_...  25.9 us
    ppermute x14, starting transfers between devices, shards(): send = lambda x: lax.ppermute(x, 'dp', pairs)  24.1 us
    ppermute x1, waiting for transfers between devices, shards(): turned = [turned, lax.ppermute(turned, 'dp', backward)]  9.22 us
    all_to_all x1, blocking collectives, shards(): lax.all_to_all(table.reshape(devices, slots, queries), 'dp', 0, 0, axis_i...  9.1 us
    ppermute x1, waiting for transfers between devices, shards(): turned = lax.ppermute(turned, 'dp', [(j, i) for i, j in pairs])  6.32 us
  transfers between devices with their start and end apart: 19, of which 10 were waited for; matrix products, arithmetic and copies ran while one was open for 1% of the time, Pallas kernels for 23%

profile of v20, /device:TPU:0, one launch (start us, length us, event | category | flops | bytes accessed | tf_op | source)
XLA Modules:
  0.0 114.0 jit_solution(11445521128205105542)
XLA Ops:
  0.0 0.0 copy-start
  0.0 0.5 collective-permute-start.11
  0.5 2.6 %collective-permute-start.1 = (bf16[2048,256]{1,0:T(8,128)(2,1)}, bf16[2048,256]{1,0:T(8,128)(2,1)S(1)}, u32[]{:S(2)}, u32[]{:S(2)}) collective-permute-start(bf16[2048,256]{1,0:T(8,128)(2,1)} %refs_4_.1), channel_id=1, source_target_pairs={{2,6},{3,1},{6,10},{7,3},{10,14},{11,7},{14,12},{15,11},{12,8},{13... | collective-permute-start | bytes 3145736 | tf_op jit(solution)/shard_map/ppermute | solution.py:206
  3.0 0.2 collective-permute-start.10
  3.3 1.4 %collective-permute-start = (bf16[512,256]{1,0:T(8,128)(2,1)}, bf16[512,256]{1,0:T(8,128)(2,1)S(1)}, u32[]{:S(2)}, u32[]{:S(2)}) collective-permute-start(bf16[512,256]{1,0:T(8,128)(2,1)} %refs_5_.1), channel_id=1, source_target_pairs={{2,6},{3,1},{6,10},{7,3},{10,14},{11,7},{14,12},{15,11},{12,8},{13... | collective-permute-start | bytes 786440 | tf_op jit(solution)/shard_map/ppermute | solution.py:206
  4.6 11.5 %collective-permute-done.1 = bf16[2048,256]{1,0:T(8,128)(2,1)S(1)} collective-permute-done((bf16[2048,256]{1,0:T(8,128)(2,1)}, bf16[2048,256]{1,0:T(8,128)(2,1)S(1)}, u32[]{:S(2)}, u32[]{:S(2)}) %collective-permute-start.1) | collective-permute-done | bytes 1048608 | tf_op jit(solution)/shard_map/ppermute | solution.py:206
  16.1 2.0 %collective-permute-start.2 = (bf16[512,256]{1,0:T(8,128)(2,1)}, bf16[512,256]{1,0:T(8,128)(2,1)S(1)}, u32[]{:S(2)}, u32[]{:S(2)}) collective-permute-start(bf16[512,256]{1,0:T(8,128)(2,1)} %refs_5_.1), channel_id=1, source_target_pairs={{6,2},{1,3},{10,6},{3,7},{14,10},{7,11},{12,14},{11,15},{8,12},{15... | collective-permute-start | bytes 786440 | tf_op jit(solution)/shard_map/ppermute | solution.py:225
  18.1 0.1 collective-permute-start.7
  18.3 0.7 collective-permute-done
  19.0 6.3 %collective-permute-done.2.refs_4_ = bf16[512,256]{1,0:T(8,128)(2,1)S(1)} collective-permute-done((bf16[512,256]{1,0:T(8,128)(2,1)}, bf16[512,256]{1,0:T(8,128)(2,1)S(1)}, u32[]{:S(2)}, u32[]{:S(2)}) %collective-permute-start.2) | collective-permute-done | bytes 262176 | tf_op jit(solution)/shard_map/ppermute | solution.py:225
  25.3 0.0 copy-start.4
  25.3 2.2 %collective-permute-start.3 = (bf16[1280,256]{1,0:T(8,128)(2,1)S(1)}, bf16[1280,256]{1,0:T(8,128)(2,1)}, u32[]{:S(2)}, u32[]{:S(2)}) collective-permute-start(bf16[1280,256]{1,0:T(8,128)(2,1)S(1)} %pad_maximum_fusion.refs_5_), channel_id=1, source_target_pairs={{2,6},{3,1},{6,10},{7,3},{10,14},{11,7},{14,12},{15,11},{12,8},{13... | collective-permute-start | bytes 1966088 | tf_op jit(solution)/shard_map/ppermute | solution.py:206
  27.5 1.2 %collective-permute-done.7.refs_4_ = bf16[1280,256]{1,0:T(8,128)(2,1)S(1)} collective-permute-done((bf16[1280,256]{1,0:T(8,128)(2,1)S(1)}, bf16[1280,256]{1,0:T(8,128)(2,1)S(1)}, u32[]{:S(2)}, u32[]{:S(2)}) %collective-permute-start.7) | collective-permute-done | bytes 655392 | tf_op jit(solution)/shard_map/ppermute | solution.py:206
  28.8 1.9 %collective-permute-start.8 = (bf16[1280,256]{1,0:T(8,128)(2,1)S(1)}, bf16[1280,256]{1,0:T(8,128)(2,1)}, u32[]{:S(2)}, u32[]{:S(2)}) collective-permute-start(bf16[1280,256]{1,0:T(8,128)(2,1)S(1)} %collective-permute-done.7.refs_4_), channel_id=1, source_target_pairs={{2,6},{3,1},{6,10},{7,3},{10,14},{11,7},{14,12},{15,11},{12,8},{13... | collective-permute-start | bytes 1966088 | tf_op jit(solution)/shard_map/ppermute | solution.py:206
  30.7 5.7 %collective-permute-done.3.refs_5_ = bf16[1280,256]{1,0:T(8,128)(2,1)} collective-permute-done((bf16[1280,256]{1,0:T(8,128)(2,1)S(1)}, bf16[1280,256]{1,0:T(8,128)(2,1)}, u32[]{:S(2)}, u32[]{:S(2)}) %collective-permute-start.3) | collective-permute-done | bytes 655392 | tf_op jit(solution)/shard_map/ppermute | solution.py:206
  36.3 1.9 %collective-permute-start.4 = (bf16[1280,256]{1,0:T(8,128)(2,1)}, bf16[1280,256]{1,0:T(8,128)(2,1)}, u32[]{:S(2)}, u32[]{:S(2)}) collective-permute-start(bf16[1280,256]{1,0:T(8,128)(2,1)} %collective-permute-done.3.refs_5_), channel_id=1, source_target_pairs={{2,6},{3,1},{6,10},{7,3},{10,14},{11,7},{14,12},{15,11},{12,8},{13... | collective-permute-start | bytes 1966088 | tf_op jit(solution)/shard_map/ppermute | solution.py:206
  38.2 0.0 copy-done.4
  38.2 5.1 %collective-permute-done.8.refs_4_ = bf16[1280,256]{1,0:T(8,128)(2,1)} collective-permute-done((bf16[1280,256]{1,0:T(8,128)(2,1)S(1)}, bf16[1280,256]{1,0:T(8,128)(2,1)}, u32[]{:S(2)}, u32[]{:S(2)}) %collective-permute-start.8) | collective-permute-done | bytes 655392 | tf_op jit(solution)/shard_map/ppermute | solution.py:206
  43.4 1.9 %collective-permute-start.9 = (bf16[1280,256]{1,0:T(8,128)(2,1)}, bf16[1280,256]{1,0:T(8,128)(2,1)S(1)}, u32[]{:S(2)}, u32[]{:S(2)}) collective-permute-start(bf16[1280,256]{1,0:T(8,128)(2,1)} %collective-permute-done.8.refs_4_), channel_id=1, source_target_pairs={{2,6},{3,1},{6,10},{7,3},{10,14},{11,7},{14,12},{15,11},{12,8},{13... | collective-permute-start | bytes 1966088 | tf_op jit(solution)/shard_map/ppermute | solution.py:206
  45.3 0.1 collective-permute-start.5
  45.4 9.2 %collective-permute-done.5.refs_5_ = bf16[512,256]{1,0:T(8,128)(2,1)} collective-permute-done((bf16[512,256]{1,0:T(8,128)(2,1)S(1)}, bf16[512,256]{1,0:T(8,128)(2,1)}, u32[]{:S(2)}, u32[]{:S(2)}) %collective-permute-start.5) | collective-permute-done | bytes 262176 | tf_op jit(solution)/shard_map/ppermute | solution.py:230
  54.6 0.0 collective-permute-done.4.refs_5_
  54.6 1.6 %collective-permute-start.6 = (bf16[1280,256]{1,0:T(8,128)(2,1)}, bf16[1280,256]{1,0:T(8,128)(2,1)S(1)}, u32[]{:S(2)}, u32[]{:S(2)}) collective-permute-start(bf16[1280,256]{1,0:T(8,128)(2,1)} %collective-permute-done.4.refs_5_), channel_id=1, source_target_pairs={{2,6},{3,1},{6,10},{7,3},{10,14},{11,7},{14,12},{15,11},{12,8},{13... | collective-permute-start | bytes 1966088 | tf_op jit(solution)/shard_map/ppermute | solution.py:206
  56.2 0.7 dynamic-slice_bitcast_fusion.order_ref
  56.9 0.0 collective-permute-done.10.refs_1_.refs_3_
  56.9 0.0 collective-permute-done.11.refs_3_.sib_ref.refs_1_
  56.9 0.0 copy-done
  56.9 0.0 copy-done.1
  56.9 2.6 %step.8 = (f32[320,256]{1,0:T(8,128)S(1)}, f32[320,256]{1,0:T(8,128)S(1)}) custom-call(s32[8]{0:T(128)S(1)} %dynamic-slice_bitcast_fusion.order_ref, bf16[160,8192]{1,0:T(8,128)(2,1)} %refs_2_.13, bf16[160,8192]{1,0:T(8,128)(2,1)} %collective-permute-done.10.refs_1_.refs_3_, bf16[160,32768]{1,0:T(8,128)(2,1)} %refs_0_.16, ...), custom_call_target="tpu_custom_call" | custom-call | flops 419430400 | bytes 3604480 | tf_op jit(solution)/shard_map/step/pallas_call | solution.py:59
  59.5 2.8 %step.9 = (f32[320,256]{1,0:T(8,128)S(1)}, f32[320,256]{1,0:T(8,128)S(1)}) custom-call(s32[8]{0:T(128)S(1)} %dynamic-slice_bitcast_fusion.order_ref, bf16[160,8192]{1,0:T(8,128)(2,1)} %refs_2_.13, bf16[160,8192]{1,0:T(8,128)(2,1)} %collective-permute-done.10.refs_1_.refs_3_, bf16[160,32768]{1,0:T(8,128)(2,1)} %refs_0_.16, ...), custom_call_target="tpu_custom_call" | custom-call | flops 419430400 | bytes 4259840 | tf_op jit(solution)/shard_map/step/pallas_call | solution.py:59
  62.3 0.0 collective-permute-done.9.refs_4_
  62.3 1.6 %collective-permute-start.13 = (bf16[1280,256]{1,0:T(8,128)(2,1)S(1)}, bf16[1280,256]{1,0:T(8,128)(2,1)S(1)}, u32[]{:S(2)}, u32[]{:S(2)}) collective-permute-start(bf16[1280,256]{1,0:T(8,128)(2,1)S(1)} %collective-permute-done.9.refs_4_), channel_id=1, source_target_pairs={{2,6},{3,1},{6,10},{7,3},{10,14},{11,7},{14,12},{15,11},{12,8},{13... | collective-permute-start | bytes 1966088 | tf_op jit(solution)/shard_map/ppermute | solution.py:206
  63.9 3.2 %collective-permute-done.6.refs_5_ = bf16[1280,256]{1,0:T(8,128)(2,1)S(1)} collective-permute-done((bf16[1280,256]{1,0:T(8,128)(2,1)}, bf16[1280,256]{1,0:T(8,128)(2,1)S(1)}, u32[]{:S(2)}, u32[]{:S(2)}) %collective-permute-start.6) | collective-permute-done | bytes 655392 | tf_op jit(solution)/shard_map/ppermute | solution.py:206
  67.1 1.9 %collective-permute-start.12 = (bf16[1280,256]{1,0:T(8,128)(2,1)S(1)}, bf16[1280,256]{1,0:T(8,128)(2,1)S(1)}, u32[]{:S(2)}, u32[]{:S(2)}) collective-permute-start(bf16[1280,256]{1,0:T(8,128)(2,1)S(1)} %collective-permute-done.6.refs_5_), channel_id=1, source_target_pairs={{2,6},{3,1},{6,10},{7,3},{10,14},{11,7},{14,12},{15,11},{12,8},{13... | collective-permute-start | bytes 1966088 | tf_op jit(solution)/shard_map/ppermute | solution.py:206
  69.0 2.8 %step.10 = (f32[320,256]{1,0:T(8,128)S(1)}, f32[320,256]{1,0:T(8,128)S(1)}) custom-call(s32[8]{0:T(128)S(1)} %dynamic-slice_bitcast_fusion.order_ref, bf16[160,8192]{1,0:T(8,128)(2,1)} %refs_2_.13, bf16[160,8192]{1,0:T(8,128)(2,1)} %collective-permute-done.10.refs_1_.refs_3_, bf16[160,32768]{1,0:T(8,128)(2,1)} %refs_0_.16, ...), custom_call_target="tpu_custom_call" | custom-call | flops 419430400 | bytes 4259840 | tf_op jit(solution)/shard_map/step/pallas_call | solution.py:59
  71.8 0.0 copy-done.6
  71.8 3.0 %step.11 = (f32[320,256]{1,0:T(8,128)S(1)}, f32[320,256]{1,0:T(8,128)S(1)}) custom-call(s32[8]{0:T(128)S(1)} %dynamic-slice_bitcast_fusion.order_ref, bf16[160,8192]{1,0:T(8,128)(2,1)} %refs_2_.13, bf16[160,8192]{1,0:T(8,128)(2,1)} %collective-permute-done.10.refs_1_.refs_3_, bf16[160,32768]{1,0:T(8,128)(2,1)} %refs_0_.16, ...), custom_call_target="tpu_custom_call" | custom-call | flops 419430400 | bytes 4259840 | tf_op jit(solution)/shard_map/step/pallas_call | solution.py:59
  74.8 0.0 collective-permute-done.13.refs_4_
  74.8 1.6 %collective-permute-start.15 = (bf16[1280,256]{1,0:T(8,128)(2,1)S(1)}, bf16[1280,256]{1,0:T(8,128)(2,1)S(1)}, u32[]{:S(2)}, u32[]{:S(2)}) collective-permute-start(bf16[1280,256]{1,0:T(8,128)(2,1)S(1)} %collective-permute-done.13.refs_4_), channel_id=1, source_target_pairs={{2,6},{3,1},{6,10},{7,3},{10,14},{11,7},{14,12},{15,11},{12,8},{13... | collective-permute-start | bytes 1966088 | tf_op jit(solution)/shard_map/ppermute | solution.py:206
  76.4 4.7 %collective-permute-done.12.refs_5_ = bf16[1280,256]{1,0:T(8,128)(2,1)S(1)} collective-permute-done((bf16[1280,256]{1,0:T(8,128)(2,1)S(1)}, bf16[1280,256]{1,0:T(8,128)(2,1)S(1)}, u32[]{:S(2)}, u32[]{:S(2)}) %collective-permute-start.12) | collective-permute-done | bytes 655392 | tf_op jit(solution)/shard_map/ppermute | solution.py:206
  81.2 2.0 %collective-permute-start.14 = (bf16[768,256]{1,0:T(8,128)(2,1)S(1)}, bf16[768,256]{1,0:T(8,128)(2,1)S(1)}, u32[]{:S(2)}, u32[]{:S(2)}) collective-permute-start(bf16[768,256]{1,0:T(8,128)(2,1)S(1)} %slice.11), channel_id=1, source_target_pairs={{2,6},{3,1},{6,10},{7,3},{10,14},{11,7},{14,12},{15,11},{12,8},{13... | collective-permute-start | bytes 1179656 | tf_op jit(solution)/shard_map/ppermute | solution.py:206
  83.2 2.8 %step.12 = (f32[320,256]{1,0:T(8,128)S(1)}, f32[320,256]{1,0:T(8,128)S(1)}) custom-call(s32[8]{0:T(128)S(1)} %dynamic-slice_bitcast_fusion.order_ref, bf16[160,8192]{1,0:T(8,128)(2,1)} %refs_2_.13, bf16[160,8192]{1,0:T(8,128)(2,1)} %collective-permute-done.10.refs_1_.refs_3_, bf16[160,32768]{1,0:T(8,128)(2,1)} %refs_0_.16, ...), custom_call_target="tpu_custom_call" | custom-call | flops 419430400 | bytes 4259840 | tf_op jit(solution)/shard_map/step/pallas_call | solution.py:59
  85.9 0.0 copy-done.5
  85.9 2.8 %step.13 = (f32[320,256]{1,0:T(8,128)S(1)}, f32[320,256]{1,0:T(8,128)S(1)}) custom-call(s32[8]{0:T(128)S(1)} %dynamic-slice_bitcast_fusion.order_ref, bf16[160,8192]{1,0:T(8,128)(2,1)} %refs_2_.13, bf16[160,8192]{1,0:T(8,128)(2,1)} %collective-permute-done.10.refs_1_.refs_3_, bf16[160,32768]{1,0:T(8,128)(2,1)} %refs_0_.16, ...), custom_call_target="tpu_custom_call" | custom-call | flops 419430400 | bytes 4259840 | tf_op jit(solution)/shard_map/step/pallas_call | solution.py:59
  88.7 0.0 collective-permute-done.15.refs_2_
  88.7 0.0 copy-start.2
  88.8 0.0 copy-start.3
  88.8 1.6 %collective-permute-start.17 = (bf16[1280,256]{1,0:T(8,128)(2,1)S(1)}, bf16[1280,256]{1,0:T(8,128)(2,1)S(1)}, u32[]{:S(2)}, u32[]{:S(2)}) collective-permute-start(bf16[1280,256]{1,0:T(8,128)(2,1)S(1)} %collective-permute-done.15.refs_2_), channel_id=1, source_target_pairs={{2,6},{3,1},{6,10},{7,3},{10,14},{11,7},{14,12},{15,11},{12,8},{13... | collective-permute-start | bytes 1966088 | tf_op jit(solution)/shard_map/ppermute | solution.py:206
  90.4 2.0 %collective-permute-done.14.refs_3_ = bf16[768,256]{1,0:T(8,128)(2,1)S(1)} collective-permute-done((bf16[768,256]{1,0:T(8,128)(2,1)S(1)}, bf16[768,256]{1,0:T(8,128)(2,1)S(1)}, u32[]{:S(2)}, u32[]{:S(2)}) %collective-permute-start.14) | collective-permute-done | bytes 393248 | tf_op jit(solution)/shard_map/ppermute | solution.py:206
  92.4 1.9 %collective-permute-start.16 = (bf16[768,256]{1,0:T(8,128)(2,1)S(1)}, bf16[768,256]{1,0:T(8,128)(2,1)S(1)}, u32[]{:S(2)}, u32[]{:S(2)}) collective-permute-start(bf16[768,256]{1,0:T(8,128)(2,1)S(1)} %collective-permute-done.14.refs_3_), channel_id=1, source_target_pairs={{2,6},{3,1},{6,10},{7,3},{10,14},{11,7},{14,12},{15,11},{12,8},{13... | collective-permute-start | bytes 1179656 | tf_op jit(solution)/shard_map/ppermute | solution.py:206
  94.3 1.9 %window.1.window_ref = bf16[320,768]{1,0:T(8,128)(2,1)S(1)} custom-call(s32[8]{0:T(128)S(1)} %dynamic-slice_bitcast_fusion.order_ref, bf16[160,32768]{1,0:T(8,128)(2,1)} %refs_0_.16, bf16[160,32768]{1,0:T(8,128)(2,1)} %collective-permute-done.11.refs_3_.sib_ref.refs_1_), custom_call_target="tpu_custom_call" | custom-call | bytes 1802240 | tf_op jit(solution)/shard_map/window/pallas_call | solution.py:59
  96.2 0.0 copy-done.2
  96.2 0.0 copy-done.3
  96.2 2.2 %turned.1.own_ref = f32[328,256]{1,0:T(8,128)S(1)} custom-call(s32[8]{0:T(128)S(1)} %dynamic-slice_bitcast_fusion.order_ref, bf16[160,8192]{1,0:T(8,128)(2,1)} %refs_2_.13, bf16[160,8192]{1,0:T(8,128)(2,1)} %collective-permute-done.10.refs_1_.refs_3_, bf16[160,8192]{1,0:T(8,128)(2,1)} %refs_2_.13, bf16[160,8192]{1,0:T(8,128)(2,1)} %collective-permute-done.10.refs_1_.refs_3_, ...), custom_call_target="tpu_custom_call" | custom-call | flops 167772160 | bytes 1843200 | tf_op jit(solution)/shard_map/turned/pallas_call | solution.py:59
  98.4 0.1 collective-permute-start.18
  98.5 2.3 %step.14.refs_3_ = f32[320,256]{1,0:T(8,128)S(1)} custom-call(s32[8]{0:T(128)S(1)} %dynamic-slice_bitcast_fusion.order_ref, bf16[160,32768]{1,0:T(8,128)(2,1)} %refs_0_.16, bf16[160,32768]{1,0:T(8,128)(2,1)} %collective-permute-done.11.refs_3_.sib_ref.refs_1_, bf16[1280,256]{1,0:T(8,128)(2,1)S(1)} %collective-permute-done.15.refs_2_, ...), custom_call_target="tpu_custom_call" | custom-call | flops 335544320 | bytes 3014656 | tf_op jit(solution)/shard_map/step/pallas_call | solution.py:59
  100.8 0.0 collective-permute-done.18.got_ref
  100.8 0.6 masked.1.inn_ref
  101.5 0.0 collective-permute-done.17.refs_2_
  101.5 2.2 %step.15.total_ref = f32[320,256]{1,0:T(8,128)S(1)} custom-call(s32[8]{0:T(128)S(1)} %dynamic-slice_bitcast_fusion.order_ref, bf16[160,32768]{1,0:T(8,128)(2,1)} %refs_0_.16, bf16[160,32768]{1,0:T(8,128)(2,1)} %collective-permute-done.11.refs_3_.sib_ref.refs_1_, bf16[1280,256]{1,0:T(8,128)(2,1)S(1)} %collective-permute-done.17.refs_2_, ...), custom_call_target="tpu_custom_call" | custom-call | flops 209715200 | bytes 2621440 | tf_op jit(solution)/shard_map/step/pallas_call | solution.py:59
  103.7 0.0 collective-permute-done.16.block_ref
  103.7 0.6 score.1
  104.3 9.1 %all_to_all.5 = f32[16,2,8]{2,1,0:T(2,128)S(1)} all-to-all(f32[16,2,8]{2,1,0:T(2,128)S(1)} %bitcast.3), channel_id=1, replica_groups={{15,14,13,12,11,10,9,8,7,6,5,4,3,2,1,0},{31,30,29,28,27,26,25,24,23,22,..., dimensions={0} | all-to-all | bytes 2048 | tf_op jit(solution)/shard_map/all_to_all | solution.py:286
  113.4 0.6 reduce_sum.9
  (7 shorter events, 0.1 us)
Async XLA Ops:
  0.0 56.9 %copy-start = (bf16[2048,256]{1,0:T(8,128)(2,1)S(1)}, bf16[2048,256]{1,0:T(8,128)(2,1)}, u32[]{:S(2)}) copy-start(bf16[2048,256]{1,0:T(8,128)(2,1)} %refs_4_.1) | copy-start | bytes 3145732
  0.0 56.9 %copy-start.1 = (bf16[512,256]{1,0:T(8,128)(2,1)S(1)}, bf16[512,256]{1,0:T(8,128)(2,1)}, u32[]{:S(2)}) copy-start(bf16[512,256]{1,0:T(8,128)(2,1)} %refs_5_.1) | copy-start | bytes 786436
  0.0 56.9 %collective-permute-start.11 = (bf16[160,32768]{1,0:T(8,128)(2,1)}, bf16[160,32768]{1,0:T(8,128)(2,1)}, u32[]{:S(2)}, u32[]{:S(2)}) collective-permute-start(bf16[160,32768]{1,0:T(8,128)(2,1)} %refs_0_.16), channel_id=1, source_target_pairs={{0,1},{1,0},{2,3},{3,2},{4,5},{5,4},{6,7},{7,6},{8,9},{9,8},{10,11... | collective-permute-start | bytes 31457288 | tf_op jit(solution)/shard_map/ppermute | solution.py:207
  0.5 15.6 %collective-permute-start.1 = (bf16[2048,256]{1,0:T(8,128)(2,1)}, bf16[2048,256]{1,0:T(8,128)(2,1)S(1)}, u32[]{:S(2)}, u32[]{:S(2)}) collective-permute-start(bf16[2048,256]{1,0:T(8,128)(2,1)} %refs_4_.1), channel_id=1, source_target_pairs={{2,6},{3,1},{6,10},{7,3},{10,14},{11,7},{14,12},{15,11},{12,8},{13... | collective-permute-start | bytes 3145736 | tf_op jit(solution)/shard_map/ppermute | solution.py:206
  3.0 53.8 %collective-permute-start.10 = (bf16[160,8192]{1,0:T(8,128)(2,1)}, bf16[160,8192]{1,0:T(8,128)(2,1)}, u32[]{:S(2)}, u32[]{:S(2)}) collective-permute-start(bf16[160,8192]{1,0:T(8,128)(2,1)} %refs_2_.13), channel_id=1, source_target_pairs={{0,1},{1,0},{2,3},{3,2},{4,5},{5,4},{6,7},{7,6},{8,9},{9,8},{10,11... | collective-permute-start | bytes 7864328 | tf_op jit(solution)/shard_map/ppermute | solution.py:207
  3.3 15.7 %collective-permute-start = (bf16[512,256]{1,0:T(8,128)(2,1)}, bf16[512,256]{1,0:T(8,128)(2,1)S(1)}, u32[]{:S(2)}, u32[]{:S(2)}) collective-permute-start(bf16[512,256]{1,0:T(8,128)(2,1)} %refs_5_.1), channel_id=1, source_target_pairs={{2,6},{3,1},{6,10},{7,3},{10,14},{11,7},{14,12},{15,11},{12,8},{13... | collective-permute-start | bytes 786440 | tf_op jit(solution)/shard_map/ppermute | solution.py:206
  16.1 9.2 %collective-permute-start.2 = (bf16[512,256]{1,0:T(8,128)(2,1)}, bf16[512,256]{1,0:T(8,128)(2,1)S(1)}, u32[]{:S(2)}, u32[]{:S(2)}) collective-permute-start(bf16[512,256]{1,0:T(8,128)(2,1)} %refs_5_.1), channel_id=1, source_target_pairs={{6,2},{1,3},{10,6},{3,7},{14,10},{7,11},{12,14},{11,15},{8,12},{15... | collective-permute-start | bytes 786440 | tf_op jit(solution)/shard_map/ppermute | solution.py:225
  18.1 10.6 %collective-permute-start.7 = (bf16[1280,256]{1,0:T(8,128)(2,1)S(1)}, bf16[1280,256]{1,0:T(8,128)(2,1)S(1)}, u32[]{:S(2)}, u32[]{:S(2)}) collective-permute-start(bf16[1280,256]{1,0:T(8,128)(2,1)S(1)} %slice.10.refs_4_), channel_id=1, source_target_pairs={{2,6},{3,1},{6,10},{7,3},{10,14},{11,7},{14,12},{15,11},{12,8},{13... | collective-permute-start | bytes 1966088 | tf_op jit(solution)/shard_map/ppermute | solution.py:206
  25.3 12.9 %copy-start.4 = (bf16[1280,256]{1,0:T(8,128)(2,1)}, bf16[1280,256]{1,0:T(8,128)(2,1)S(1)}, u32[]{:S(2)}) copy-start(bf16[1280,256]{1,0:T(8,128)(2,1)S(1)} %pad_maximum_fusion.refs_5_) | copy-start | bytes 1966084
  25.3 11.0 %collective-permute-start.3 = (bf16[1280,256]{1,0:T(8,128)(2,1)S(1)}, bf16[1280,256]{1,0:T(8,128)(2,1)}, u32[]{:S(2)}, u32[]{:S(2)}) collective-permute-start(bf16[1280,256]{1,0:T(8,128)(2,1)S(1)} %pad_maximum_fusion.refs_5_), channel_id=1, source_target_pairs={{2,6},{3,1},{6,10},{7,3},{10,14},{11,7},{14,12},{15,11},{12,8},{13... | collective-permute-start | bytes 1966088 | tf_op jit(solution)/shard_map/ppermute | solution.py:206
  28.8 14.6 %collective-permute-start.8 = (bf16[1280,256]{1,0:T(8,128)(2,1)S(1)}, bf16[1280,256]{1,0:T(8,128)(2,1)}, u32[]{:S(2)}, u32[]{:S(2)}) collective-permute-start(bf16[1280,256]{1,0:T(8,128)(2,1)S(1)} %collective-permute-done.7.refs_4_), channel_id=1, source_target_pairs={{2,6},{3,1},{6,10},{7,3},{10,14},{11,7},{14,12},{15,11},{12,8},{13... | collective-permute-start | bytes 1966088 | tf_op jit(solution)/shard_map/ppermute | solution.py:206
  36.3 18.3 %collective-permute-start.4 = (bf16[1280,256]{1,0:T(8,128)(2,1)}, bf16[1280,256]{1,0:T(8,128)(2,1)}, u32[]{:S(2)}, u32[]{:S(2)}) collective-permute-start(bf16[1280,256]{1,0:T(8,128)(2,1)} %collective-permute-done.3.refs_5_), channel_id=1, source_target_pairs={{2,6},{3,1},{6,10},{7,3},{10,14},{11,7},{14,12},{15,11},{12,8},{13... | collective-permute-start | bytes 1966088 | tf_op jit(solution)/shard_map/ppermute | solution.py:206
  43.4 18.9 %collective-permute-start.9 = (bf16[1280,256]{1,0:T(8,128)(2,1)}, bf16[1280,256]{1,0:T(8,128)(2,1)S(1)}, u32[]{:S(2)}, u32[]{:S(2)}) collective-permute-start(bf16[1280,256]{1,0:T(8,128)(2,1)} %collective-permute-done.8.refs_4_), channel_id=1, source_target_pairs={{2,6},{3,1},{6,10},{7,3},{10,14},{11,7},{14,12},{15,11},{12,8},{13... | collective-permute-start | bytes 1966088 | tf_op jit(solution)/shard_map/ppermute | solution.py:206
  45.3 9.3 %collective-permute-start.5 = (bf16[512,256]{1,0:T(8,128)(2,1)S(1)}, bf16[512,256]{1,0:T(8,128)(2,1)}, u32[]{:S(2)}, u32[]{:S(2)}) collective-permute-start(bf16[512,256]{1,0:T(8,128)(2,1)S(1)} %collective-permute-done.2.refs_4_), channel_id=1, source_target_pairs={{6,2},{1,3},{10,6},{3,7},{14,10},{7,11},{12,14},{11,15},{8,12},{15... | collective-permute-start | bytes 786440 | tf_op jit(solution)/shard_map/ppermute | solution.py:230
  54.6 12.5 %collective-permute-start.6 = (bf16[1280,256]{1,0:T(8,128)(2,1)}, bf16[1280,256]{1,0:T(8,128)(2,1)S(1)}, u32[]{:S(2)}, u32[]{:S(2)}) collective-permute-start(bf16[1280,256]{1,0:T(8,128)(2,1)} %collective-permute-done.4.refs_5_), channel_id=1, source_target_pairs={{2,6},{3,1},{6,10},{7,3},{10,14},{11,7},{14,12},{15,11},{12,8},{13... | collective-permute-start | bytes 1966088 | tf_op jit(solution)/shard_map/ppermute | solution.py:206
  62.3 12.5 %collective-permute-start.13 = (bf16[1280,256]{1,0:T(8,128)(2,1)S(1)}, bf16[1280,256]{1,0:T(8,128)(2,1)S(1)}, u32[]{:S(2)}, u32[]{:S(2)}) collective-permute-start(bf16[1280,256]{1,0:T(8,128)(2,1)S(1)} %collective-permute-done.9.refs_4_), channel_id=1, source_target_pairs={{2,6},{3,1},{6,10},{7,3},{10,14},{11,7},{14,12},{15,11},{12,8},{13... | collective-permute-start | bytes 1966088 | tf_op jit(solution)/shard_map/ppermute | solution.py:206
  67.1 4.7 %copy-start.6 = (bf16[1280,256]{1,0:T(8,128)(2,1)}, bf16[1280,256]{1,0:T(8,128)(2,1)S(1)}, u32[]{:S(2)}) copy-start(bf16[1280,256]{1,0:T(8,128)(2,1)S(1)} %collective-permute-done.6.refs_5_) | copy-start | bytes 1966084
  67.1 14.0 %collective-permute-start.12 = (bf16[1280,256]{1,0:T(8,128)(2,1)S(1)}, bf16[1280,256]{1,0:T(8,128)(2,1)S(1)}, u32[]{:S(2)}, u32[]{:S(2)}) collective-permute-start(bf16[1280,256]{1,0:T(8,128)(2,1)S(1)} %collective-permute-done.6.refs_5_), channel_id=1, source_target_pairs={{2,6},{3,1},{6,10},{7,3},{10,14},{11,7},{14,12},{15,11},{12,8},{13... | collective-permute-start | bytes 1966088 | tf_op jit(solution)/shard_map/ppermute | solution.py:206
  74.8 13.9 %collective-permute-start.15 = (bf16[1280,256]{1,0:T(8,128)(2,1)S(1)}, bf16[1280,256]{1,0:T(8,128)(2,1)S(1)}, u32[]{:S(2)}, u32[]{:S(2)}) collective-permute-start(bf16[1280,256]{1,0:T(8,128)(2,1)S(1)} %collective-permute-done.13.refs_4_), channel_id=1, source_target_pairs={{2,6},{3,1},{6,10},{7,3},{10,14},{11,7},{14,12},{15,11},{12,8},{13... | collective-permute-start | bytes 1966088 | tf_op jit(solution)/shard_map/ppermute | solution.py:206
  81.2 4.8 %copy-start.5 = (bf16[1280,256]{1,0:T(8,128)(2,1)}, bf16[1280,256]{1,0:T(8,128)(2,1)S(1)}, u32[]{:S(2)}) copy-start(bf16[1280,256]{1,0:T(8,128)(2,1)S(1)} %collective-permute-done.12.refs_5_) | copy-start | bytes 1966084
  81.2 11.2 %collective-permute-start.14 = (bf16[768,256]{1,0:T(8,128)(2,1)S(1)}, bf16[768,256]{1,0:T(8,128)(2,1)S(1)}, u32[]{:S(2)}, u32[]{:S(2)}) collective-permute-start(bf16[768,256]{1,0:T(8,128)(2,1)S(1)} %slice.11), channel_id=1, source_target_pairs={{2,6},{3,1},{6,10},{7,3},{10,14},{11,7},{14,12},{15,11},{12,8},{13... | collective-permute-start | bytes 1179656 | tf_op jit(solution)/shard_map/ppermute | solution.py:206
  88.7 7.4 %copy-start.2 = (s32[2]{0:T(128)S(1)}, s32[2]{0:T(128)}, u32[]{:S(2)}) copy-start(s32[2]{0:T(128)} %refs_7_.1) | copy-start | bytes 28
  88.8 7.4 %copy-start.3 = (s32[2]{0:T(128)S(1)}, s32[2]{0:T(128)}, u32[]{:S(2)}) copy-start(s32[2]{0:T(128)} %refs_8_.1) | copy-start | bytes 28
  88.8 12.7 %collective-permute-start.17 = (bf16[1280,256]{1,0:T(8,128)(2,1)S(1)}, bf16[1280,256]{1,0:T(8,128)(2,1)S(1)}, u32[]{:S(2)}, u32[]{:S(2)}) collective-permute-start(bf16[1280,256]{1,0:T(8,128)(2,1)S(1)} %collective-permute-done.15.refs_2_), channel_id=1, source_target_pairs={{2,6},{3,1},{6,10},{7,3},{10,14},{11,7},{14,12},{15,11},{12,8},{13... | collective-permute-start | bytes 1966088 | tf_op jit(solution)/shard_map/ppermute | solution.py:206
  92.4 11.3 %collective-permute-start.16 = (bf16[768,256]{1,0:T(8,128)(2,1)S(1)}, bf16[768,256]{1,0:T(8,128)(2,1)S(1)}, u32[]{:S(2)}, u32[]{:S(2)}) collective-permute-start(bf16[768,256]{1,0:T(8,128)(2,1)S(1)} %collective-permute-done.14.refs_3_), channel_id=1, source_target_pairs={{2,6},{3,1},{6,10},{7,3},{10,14},{11,7},{14,12},{15,11},{12,8},{13... | collective-permute-start | bytes 1179656 | tf_op jit(solution)/shard_map/ppermute | solution.py:206
  98.4 2.4 %collective-permute-start.18 = (f32[328,256]{1,0:T(8,128)S(1)}, f32[328,256]{1,0:T(8,128)S(1)}, u32[]{:S(2)}, u32[]{:S(2)}) collective-permute-start(f32[328,256]{1,0:T(8,128)S(1)} %turned.1.own_ref), channel_id=1, source_target_pairs={{0,1},{1,0},{2,3},{3,2},{4,5},{5,4},{6,7},{7,6},{8,9},{9,8},{10,11... | collective-permute-start | bytes 1007624 | tf_op jit(solution)/shard_map/ppermute | solution.py:207

commit v21 on v20

--- a/solution.py
+++ b/solution.py
@@ -235,6 +235,12 @@
             totals = step(mine, tokens_of, held[j], pieces[j], totals, j)
         return totals, max(k, summed)
 
+    window = call(
+        functools.partial(window_kernel, lead), mine,
+        [(x, rows, lambda i, o: (0, o[last])) for x in tokens_of["out"][:2]], [], [],
+        [jax.ShapeDtypeStruct((2 * tokens, lead), grads.dtype)], 0, "window",
+    )[0]
+
     for s in range(1, chips):
         held.append([late, early])
         top = rows_in if s < last - 1 else 0
@@ -249,14 +255,10 @@
         if s == 3 and rows_in:
             early, turned = lax.optimization_barrier((early, turned))
         late = send(late)
+        if s == last - 1:
+            early, window = lax.optimization_barrier((early, window))
         early = send(early[rows_in:] if s == last - 2 else early)
 
-    window = call(
-        functools.partial(window_kernel, lead), mine,
-        [(x, rows, lambda i, o: (0, o[last])) for x in tokens_of["out"][:2]], [], [],
-        [jax.ShapeDtypeStruct((2 * tokens, lead), grads.dtype)], 0, "window",
-    )[0]
-    totals, window = lax.optimization_barrier((totals, window))
     totals, summed = sum_to(last, totals, summed)
     slots = lengths.shape[0]
     height = (2 * tokens + EXTRA, columns)

time: 114 us -> 114 us (level)
  transfers between devices with their start and end apart: 19 -> 19, of which waited for: 10 -> 11; matrix products, arithmetic and copies ran while one was open for 1% -> 1% of each run, Pallas kernels for 23% -> 23%
where the time goes in v21:
time: 114 us
  waiting for transfers between devices  49.7 us (44%)
  starting transfers between devices  27 us (24%)
  Pallas kernels  26.4 us (23%)
  blocking collectives  9.17 us (8%)
    ppermute x14, waiting for transfers between devices, shards(): send = lambda x: lax.ppermute(x, 'dp', pairs)  34.1 us
    pallas_call x11, Pallas kernels, call(): pl.pallas_call(kernel, grid_spec=pltpu.PrefetchScalarGridSpec(num_scalar_...  25.9 us
    ppermute x14, starting transfers between devices, shards(): send = lambda x: lax.ppermute(x, 'dp', pairs)  24.1 us
    ppermute x1, waiting for transfers between devices, shards(): turned = [turned, lax.ppermute(turned, 'dp', backward)]  9.22 us
    all_to_all x1, blocking collectives, shards(): lax.all_to_all(table.reshape(devices, slots, queries), 'dp', 0, 0, axis_i...  9.17 us
    ppermute x1, waiting for transfers between devices, shards(): turned = lax.ppermute(turned, 'dp', [(j, i) for i, j in pairs])  6.32 us
  transfers between devices with their start and end apart: 19, of which 11 were waited for; matrix products, arithmetic and copies ran while one was open for 1% of the time, Pallas kernels for 23%

profile of v21, /device:TPU:0, one launch (start us, length us, event | category | flops | bytes accessed | tf_op | source)
XLA Modules:
  0.0 114.0 jit_solution(16244857894438284833)
XLA Ops:
  0.0 0.0 copy-start
  0.0 0.5 collective-permute-start.11
  0.5 2.6 %collective-permute-start.1 = (bf16[2048,256]{1,0:T(8,128)(2,1)}, bf16[2048,256]{1,0:T(8,128)(2,1)S(1)}, u32[]{:S(2)}, u32[]{:S(2)}) collective-permute-start(bf16[2048,256]{1,0:T(8,128)(2,1)} %refs_4_.1), channel_id=1, source_target_pairs={{2,6},{3,1},{6,10},{7,3},{10,14},{11,7},{14,12},{15,11},{12,8},{13... | collective-permute-start | bytes 3145736 | tf_op jit(solution)/shard_map/ppermute | solution.py:206
  3.0 0.2 collective-permute-start.10
  3.3 1.4 %collective-permute-start = (bf16[512,256]{1,0:T(8,128)(2,1)}, bf16[512,256]{1,0:T(8,128)(2,1)S(1)}, u32[]{:S(2)}, u32[]{:S(2)}) collective-permute-start(bf16[512,256]{1,0:T(8,128)(2,1)} %refs_5_.1), channel_id=1, source_target_pairs={{2,6},{3,1},{6,10},{7,3},{10,14},{11,7},{14,12},{15,11},{12,8},{13... | collective-permute-start | bytes 786440 | tf_op jit(solution)/shard_map/ppermute | solution.py:206
  4.6 11.5 %collective-permute-done.1 = bf16[2048,256]{1,0:T(8,128)(2,1)S(1)} collective-permute-done((bf16[2048,256]{1,0:T(8,128)(2,1)}, bf16[2048,256]{1,0:T(8,128)(2,1)S(1)}, u32[]{:S(2)}, u32[]{:S(2)}) %collective-permute-start.1) | collective-permute-done | bytes 1048608 | tf_op jit(solution)/shard_map/ppermute | solution.py:206
  16.1 2.0 %collective-permute-start.2 = (bf16[512,256]{1,0:T(8,128)(2,1)}, bf16[512,256]{1,0:T(8,128)(2,1)S(1)}, u32[]{:S(2)}, u32[]{:S(2)}) collective-permute-start(bf16[512,256]{1,0:T(8,128)(2,1)} %refs_5_.1), channel_id=1, source_target_pairs={{6,2},{1,3},{10,6},{3,7},{14,10},{7,11},{12,14},{11,15},{8,12},{15... | collective-permute-start | bytes 786440 | tf_op jit(solution)/shard_map/ppermute | solution.py:225
  18.1 0.1 collective-permute-start.7
  18.3 0.7 collective-permute-done
  19.0 6.3 %collective-permute-done.2.refs_4_ = bf16[512,256]{1,0:T(8,128)(2,1)S(1)} collective-permute-done((bf16[512,256]{1,0:T(8,128)(2,1)}, bf16[512,256]{1,0:T(8,128)(2,1)S(1)}, u32[]{:S(2)}, u32[]{:S(2)}) %collective-permute-start.2) | collective-permute-done | bytes 262176 | tf_op jit(solution)/shard_map/ppermute | solution.py:225
  25.3 0.0 copy-start.4
  25.3 2.2 %collective-permute-start.3 = (bf16[1280,256]{1,0:T(8,128)(2,1)S(1)}, bf16[1280,256]{1,0:T(8,128)(2,1)}, u32[]{:S(2)}, u32[]{:S(2)}) collective-permute-start(bf16[1280,256]{1,0:T(8,128)(2,1)S(1)} %pad_maximum_fusion.refs_5_), channel_id=1, source_target_pairs={{2,6},{3,1},{6,10},{7,3},{10,14},{11,7},{14,12},{15,11},{12,8},{13... | collective-permute-start | bytes 1966088 | tf_op jit(solution)/shard_map/ppermute | solution.py:206
  27.5 1.2 %collective-permute-done.7.refs_4_ = bf16[1280,256]{1,0:T(8,128)(2,1)S(1)} collective-permute-done((bf16[1280,256]{1,0:T(8,128)(2,1)S(1)}, bf16[1280,256]{1,0:T(8,128)(2,1)S(1)}, u32[]{:S(2)}, u32[]{:S(2)}) %collective-permute-start.7) | collective-permute-done | bytes 655392 | tf_op jit(solution)/shard_map/ppermute | solution.py:206
  28.8 1.9 %collective-permute-start.8 = (bf16[1280,256]{1,0:T(8,128)(2,1)S(1)}, bf16[1280,256]{1,0:T(8,128)(2,1)}, u32[]{:S(2)}, u32[]{:S(2)}) collective-permute-start(bf16[1280,256]{1,0:T(8,128)(2,1)S(1)} %collective-permute-done.7.refs_4_), channel_id=1, source_target_pairs={{2,6},{3,1},{6,10},{7,3},{10,14},{11,7},{14,12},{15,11},{12,8},{13... | collective-permute-start | bytes 1966088 | tf_op jit(solution)/shard_map/ppermute | solution.py:206
  30.7 5.7 %collective-permute-done.3.refs_5_ = bf16[1280,256]{1,0:T(8,128)(2,1)} collective-permute-done((bf16[1280,256]{1,0:T(8,128)(2,1)S(1)}, bf16[1280,256]{1,0:T(8,128)(2,1)}, u32[]{:S(2)}, u32[]{:S(2)}) %collective-permute-start.3) | collective-permute-done | bytes 655392 | tf_op jit(solution)/shard_map/ppermute | solution.py:206
  36.3 1.9 %collective-permute-start.4 = (bf16[1280,256]{1,0:T(8,128)(2,1)}, bf16[1280,256]{1,0:T(8,128)(2,1)}, u32[]{:S(2)}, u32[]{:S(2)}) collective-permute-start(bf16[1280,256]{1,0:T(8,128)(2,1)} %collective-permute-done.3.refs_5_), channel_id=1, source_target_pairs={{2,6},{3,1},{6,10},{7,3},{10,14},{11,7},{14,12},{15,11},{12,8},{13... | collective-permute-start | bytes 1966088 | tf_op jit(solution)/shard_map/ppermute | solution.py:206
  38.2 0.0 copy-done.4
  38.2 5.1 %collective-permute-done.8.refs_4_ = bf16[1280,256]{1,0:T(8,128)(2,1)} collective-permute-done((bf16[1280,256]{1,0:T(8,128)(2,1)S(1)}, bf16[1280,256]{1,0:T(8,128)(2,1)}, u32[]{:S(2)}, u32[]{:S(2)}) %collective-permute-start.8) | collective-permute-done | bytes 655392 | tf_op jit(solution)/shard_map/ppermute | solution.py:206
  43.4 1.9 %collective-permute-start.9 = (bf16[1280,256]{1,0:T(8,128)(2,1)}, bf16[1280,256]{1,0:T(8,128)(2,1)S(1)}, u32[]{:S(2)}, u32[]{:S(2)}) collective-permute-start(bf16[1280,256]{1,0:T(8,128)(2,1)} %collective-permute-done.8.refs_4_), channel_id=1, source_target_pairs={{2,6},{3,1},{6,10},{7,3},{10,14},{11,7},{14,12},{15,11},{12,8},{13... | collective-permute-start | bytes 1966088 | tf_op jit(solution)/shard_map/ppermute | solution.py:206
  45.3 0.1 collective-permute-start.5
  45.4 9.2 %collective-permute-done.5.refs_5_ = bf16[512,256]{1,0:T(8,128)(2,1)} collective-permute-done((bf16[512,256]{1,0:T(8,128)(2,1)S(1)}, bf16[512,256]{1,0:T(8,128)(2,1)}, u32[]{:S(2)}, u32[]{:S(2)}) %collective-permute-start.5) | collective-permute-done | bytes 262176 | tf_op jit(solution)/shard_map/ppermute | solution.py:230
  54.6 0.0 collective-permute-done.4.refs_5_
  54.6 1.6 %collective-permute-start.6 = (bf16[1280,256]{1,0:T(8,128)(2,1)}, bf16[1280,256]{1,0:T(8,128)(2,1)S(1)}, u32[]{:S(2)}, u32[]{:S(2)}) collective-permute-start(bf16[1280,256]{1,0:T(8,128)(2,1)} %collective-permute-done.4.refs_5_), channel_id=1, source_target_pairs={{2,6},{3,1},{6,10},{7,3},{10,14},{11,7},{14,12},{15,11},{12,8},{13... | collective-permute-start | bytes 1966088 | tf_op jit(solution)/shard_map/ppermute | solution.py:206
  56.2 0.7 dynamic-slice_bitcast_fusion.order_ref
  56.9 0.0 collective-permute-done.10.refs_1_.refs_3_
  56.9 0.0 collective-permute-done.11.refs_3_.sib_ref.refs_1_
  56.9 0.0 copy-done
  56.9 0.0 copy-done.1
  56.9 2.6 %step.8 = (f32[320,256]{1,0:T(8,128)S(1)}, f32[320,256]{1,0:T(8,128)S(1)}) custom-call(s32[8]{0:T(128)S(1)} %dynamic-slice_bitcast_fusion.order_ref, bf16[160,8192]{1,0:T(8,128)(2,1)} %refs_2_.13, bf16[160,8192]{1,0:T(8,128)(2,1)} %collective-permute-done.10.refs_1_.refs_3_, bf16[160,32768]{1,0:T(8,128)(2,1)} %refs_0_.16, ...), custom_call_target="tpu_custom_call" | custom-call | flops 419430400 | bytes 3604480 | tf_op jit(solution)/shard_map/step/pallas_call | solution.py:59
  59.5 2.8 %step.9 = (f32[320,256]{1,0:T(8,128)S(1)}, f32[320,256]{1,0:T(8,128)S(1)}) custom-call(s32[8]{0:T(128)S(1)} %dynamic-slice_bitcast_fusion.order_ref, bf16[160,8192]{1,0:T(8,128)(2,1)} %refs_2_.13, bf16[160,8192]{1,0:T(8,128)(2,1)} %collective-permute-done.10.refs_1_.refs_3_, bf16[160,32768]{1,0:T(8,128)(2,1)} %refs_0_.16, ...), custom_call_target="tpu_custom_call" | custom-call | flops 419430400 | bytes 4259840 | tf_op jit(solution)/shard_map/step/pallas_call | solution.py:59
  62.3 0.0 collective-permute-done.9.refs_4_
  62.3 1.6 %collective-permute-start.13 = (bf16[1280,256]{1,0:T(8,128)(2,1)S(1)}, bf16[1280,256]{1,0:T(8,128)(2,1)S(1)}, u32[]{:S(2)}, u32[]{:S(2)}) collective-permute-start(bf16[1280,256]{1,0:T(8,128)(2,1)S(1)} %collective-permute-done.9.refs_4_), channel_id=1, source_target_pairs={{2,6},{3,1},{6,10},{7,3},{10,14},{11,7},{14,12},{15,11},{12,8},{13... | collective-permute-start | bytes 1966088 | tf_op jit(solution)/shard_map/ppermute | solution.py:206
  63.9 3.2 %collective-permute-done.6.refs_5_ = bf16[1280,256]{1,0:T(8,128)(2,1)S(1)} collective-permute-done((bf16[1280,256]{1,0:T(8,128)(2,1)}, bf16[1280,256]{1,0:T(8,128)(2,1)S(1)}, u32[]{:S(2)}, u32[]{:S(2)}) %collective-permute-start.6) | collective-permute-done | bytes 655392 | tf_op jit(solution)/shard_map/ppermute | solution.py:206
  67.1 1.9 %collective-permute-start.12 = (bf16[1280,256]{1,0:T(8,128)(2,1)S(1)}, bf16[1280,256]{1,0:T(8,128)(2,1)S(1)}, u32[]{:S(2)}, u32[]{:S(2)}) collective-permute-start(bf16[1280,256]{1,0:T(8,128)(2,1)S(1)} %collective-permute-done.6.refs_5_), channel_id=1, source_target_pairs={{2,6},{3,1},{6,10},{7,3},{10,14},{11,7},{14,12},{15,11},{12,8},{13... | collective-permute-start | bytes 1966088 | tf_op jit(solution)/shard_map/ppermute | solution.py:206
  69.0 2.8 %step.10 = (f32[320,256]{1,0:T(8,128)S(1)}, f32[320,256]{1,0:T(8,128)S(1)}) custom-call(s32[8]{0:T(128)S(1)} %dynamic-slice_bitcast_fusion.order_ref, bf16[160,8192]{1,0:T(8,128)(2,1)} %refs_2_.13, bf16[160,8192]{1,0:T(8,128)(2,1)} %collective-permute-done.10.refs_1_.refs_3_, bf16[160,32768]{1,0:T(8,128)(2,1)} %refs_0_.16, ...), custom_call_target="tpu_custom_call" | custom-call | flops 419430400 | bytes 4259840 | tf_op jit(solution)/shard_map/step/pallas_call | solution.py:59
  71.8 0.0 copy-done.6
  71.8 3.0 %step.11 = (f32[320,256]{1,0:T(8,128)S(1)}, f32[320,256]{1,0:T(8,128)S(1)}) custom-call(s32[8]{0:T(128)S(1)} %dynamic-slice_bitcast_fusion.order_ref, bf16[160,8192]{1,0:T(8,128)(2,1)} %refs_2_.13, bf16[160,8192]{1,0:T(8,128)(2,1)} %collective-permute-done.10.refs_1_.refs_3_, bf16[160,32768]{1,0:T(8,128)(2,1)} %refs_0_.16, ...), custom_call_target="tpu_custom_call" | custom-call | flops 419430400 | bytes 4259840 | tf_op jit(solution)/shard_map/step/pallas_call | solution.py:59
  74.8 0.0 collective-permute-done.13.refs_4_
  74.8 1.6 %collective-permute-start.15 = (bf16[1280,256]{1,0:T(8,128)(2,1)S(1)}, bf16[1280,256]{1,0:T(8,128)(2,1)S(1)}, u32[]{:S(2)}, u32[]{:S(2)}) collective-permute-start(bf16[1280,256]{1,0:T(8,128)(2,1)S(1)} %collective-permute-done.13.refs_4_), channel_id=1, source_target_pairs={{2,6},{3,1},{6,10},{7,3},{10,14},{11,7},{14,12},{15,11},{12,8},{13... | collective-permute-start | bytes 1966088 | tf_op jit(solution)/shard_map/ppermute | solution.py:206
  76.4 4.7 %collective-permute-done.12.refs_5_ = bf16[1280,256]{1,0:T(8,128)(2,1)S(1)} collective-permute-done((bf16[1280,256]{1,0:T(8,128)(2,1)S(1)}, bf16[1280,256]{1,0:T(8,128)(2,1)S(1)}, u32[]{:S(2)}, u32[]{:S(2)}) %collective-permute-start.12) | collective-permute-done | bytes 655392 | tf_op jit(solution)/shard_map/ppermute | solution.py:206
  81.2 2.0 %collective-permute-start.14 = (bf16[768,256]{1,0:T(8,128)(2,1)S(1)}, bf16[768,256]{1,0:T(8,128)(2,1)S(1)}, u32[]{:S(2)}, u32[]{:S(2)}) collective-permute-start(bf16[768,256]{1,0:T(8,128)(2,1)S(1)} %slice.11), channel_id=1, source_target_pairs={{2,6},{3,1},{6,10},{7,3},{10,14},{11,7},{14,12},{15,11},{12,8},{13... | collective-permute-start | bytes 1179656 | tf_op jit(solution)/shard_map/ppermute | solution.py:206
  83.2 2.8 %step.12 = (f32[320,256]{1,0:T(8,128)S(1)}, f32[320,256]{1,0:T(8,128)S(1)}) custom-call(s32[8]{0:T(128)S(1)} %dynamic-slice_bitcast_fusion.order_ref, bf16[160,8192]{1,0:T(8,128)(2,1)} %refs_2_.13, bf16[160,8192]{1,0:T(8,128)(2,1)} %collective-permute-done.10.refs_1_.refs_3_, bf16[160,32768]{1,0:T(8,128)(2,1)} %refs_0_.16, ...), custom_call_target="tpu_custom_call" | custom-call | flops 419430400 | bytes 4259840 | tf_op jit(solution)/shard_map/step/pallas_call | solution.py:59
  85.9 0.0 copy-done.5
  85.9 2.8 %step.13 = (f32[320,256]{1,0:T(8,128)S(1)}, f32[320,256]{1,0:T(8,128)S(1)}) custom-call(s32[8]{0:T(128)S(1)} %dynamic-slice_bitcast_fusion.order_ref, bf16[160,8192]{1,0:T(8,128)(2,1)} %refs_2_.13, bf16[160,8192]{1,0:T(8,128)(2,1)} %collective-permute-done.10.refs_1_.refs_3_, bf16[160,32768]{1,0:T(8,128)(2,1)} %refs_0_.16, ...), custom_call_target="tpu_custom_call" | custom-call | flops 419430400 | bytes 4259840 | tf_op jit(solution)/shard_map/step/pallas_call | solution.py:59
  88.7 0.0 collective-permute-done.15.refs_2_
  88.7 0.0 copy-start.2
  88.8 0.0 copy-start.3
  88.8 1.6 %collective-permute-start.17 = (bf16[1280,256]{1,0:T(8,128)(2,1)S(1)}, bf16[1280,256]{1,0:T(8,128)(2,1)S(1)}, u32[]{:S(2)}, u32[]{:S(2)}) collective-permute-start(bf16[1280,256]{1,0:T(8,128)(2,1)S(1)} %collective-permute-done.15.refs_2_), channel_id=1, source_target_pairs={{2,6},{3,1},{6,10},{7,3},{10,14},{11,7},{14,12},{15,11},{12,8},{13... | collective-permute-start | bytes 1966088 | tf_op jit(solution)/shard_map/ppermute | solution.py:206
  90.4 1.9 %window.1.window_ref = bf16[320,768]{1,0:T(8,128)(2,1)S(1)} custom-call(s32[8]{0:T(128)S(1)} %dynamic-slice_bitcast_fusion.order_ref, bf16[160,32768]{1,0:T(8,128)(2,1)} %refs_0_.16, bf16[160,32768]{1,0:T(8,128)(2,1)} %collective-permute-done.11.refs_3_.sib_ref.refs_1_), custom_call_target="tpu_custom_call" | custom-call | bytes 1802240 | tf_op jit(solution)/shard_map/window/pallas_call | solution.py:59
  92.3 0.1 collective-permute-done.14.refs_3_
  92.4 1.9 %collective-permute-start.16 = (bf16[768,256]{1,0:T(8,128)(2,1)S(1)}, bf16[768,256]{1,0:T(8,128)(2,1)S(1)}, u32[]{:S(2)}, u32[]{:S(2)}) collective-permute-start(bf16[768,256]{1,0:T(8,128)(2,1)S(1)} %collective-permute-done.14.refs_3_), channel_id=1, source_target_pairs={{2,6},{3,1},{6,10},{7,3},{10,14},{11,7},{14,12},{15,11},{12,8},{13... | collective-permute-start | bytes 1179656 | tf_op jit(solution)/shard_map/ppermute | solution.py:206
  94.3 0.0 copy-done.2
  94.3 0.0 copy-done.3
  94.3 2.2 %turned.1.own_ref = f32[328,256]{1,0:T(8,128)S(1)} custom-call(s32[8]{0:T(128)S(1)} %dynamic-slice_bitcast_fusion.order_ref, bf16[160,8192]{1,0:T(8,128)(2,1)} %refs_2_.13, bf16[160,8192]{1,0:T(8,128)(2,1)} %collective-permute-done.10.refs_1_.refs_3_, bf16[160,8192]{1,0:T(8,128)(2,1)} %refs_2_.13, bf16[160,8192]{1,0:T(8,128)(2,1)} %collective-permute-done.10.refs_1_.refs_3_, ...), custom_call_target="tpu_custom_call" | custom-call | flops 167772160 | bytes 1843200 | tf_op jit(solution)/shard_map/turned/pallas_call | solution.py:59
  96.5 0.1 collective-permute-start.18
  96.6 2.4 %step.14.refs_3_ = f32[320,256]{1,0:T(8,128)S(1)} custom-call(s32[8]{0:T(128)S(1)} %dynamic-slice_bitcast_fusion.order_ref, bf16[160,32768]{1,0:T(8,128)(2,1)} %refs_0_.16, bf16[160,32768]{1,0:T(8,128)(2,1)} %collective-permute-done.11.refs_3_.sib_ref.refs_1_, bf16[1280,256]{1,0:T(8,128)(2,1)S(1)} %collective-permute-done.15.refs_2_, ...), custom_call_target="tpu_custom_call" | custom-call | flops 335544320 | bytes 3014656 | tf_op jit(solution)/shard_map/step/pallas_call | solution.py:59
  98.9 0.0 collective-permute-done.18.got_ref
  98.9 0.6 masked.1.inn_ref
  99.6 0.0 collective-permute-done.17.refs_2_
  99.6 2.2 %step.15.total_ref = f32[320,256]{1,0:T(8,128)S(1)} custom-call(s32[8]{0:T(128)S(1)} %dynamic-slice_bitcast_fusion.order_ref, bf16[160,32768]{1,0:T(8,128)(2,1)} %refs_0_.16, bf16[160,32768]{1,0:T(8,128)(2,1)} %collective-permute-done.11.refs_3_.sib_ref.refs_1_, bf16[1280,256]{1,0:T(8,128)(2,1)S(1)} %collective-permute-done.17.refs_2_, ...), custom_call_target="tpu_custom_call" | custom-call | flops 209715200 | bytes 2621440 | tf_op jit(solution)/shard_map/step/pallas_call | solution.py:59
  101.8 1.8 %collective-permute-done.16.block_ref = bf16[768,256]{1,0:T(8,128)(2,1)S(1)} collective-permute-done((bf16[768,256]{1,0:T(8,128)(2,1)S(1)}, bf16[768,256]{1,0:T(8,128)(2,1)S(1)}, u32[]{:S(2)}, u32[]{:S(2)}) %collective-permute-start.16) | collective-permute-done | bytes 393248 | tf_op jit(solution)/shard_map/ppermute | solution.py:206
  103.6 0.6 score.1
  104.2 9.2 %all_to_all.5 = f32[16,2,8]{2,1,0:T(2,128)S(1)} all-to-all(f32[16,2,8]{2,1,0:T(2,128)S(1)} %bitcast.3), channel_id=1, replica_groups={{15,14,13,12,11,10,9,8,7,6,5,4,3,2,1,0},{31,30,29,28,27,26,25,24,23,22,..., dimensions={0} | all-to-all | bytes 2048 | tf_op jit(solution)/shard_map/all_to_all | solution.py:288
  113.4 0.6 reduce_sum.9
  (7 shorter events, 0.1 us)
Async XLA Ops:
  0.0 56.9 %copy-start = (bf16[2048,256]{1,0:T(8,128)(2,1)S(1)}, bf16[2048,256]{1,0:T(8,128)(2,1)}, u32[]{:S(2)}) copy-start(bf16[2048,256]{1,0:T(8,128)(2,1)} %refs_4_.1) | copy-start | bytes 3145732
  0.0 56.9 %copy-start.1 = (bf16[512,256]{1,0:T(8,128)(2,1)S(1)}, bf16[512,256]{1,0:T(8,128)(2,1)}, u32[]{:S(2)}) copy-start(bf16[512,256]{1,0:T(8,128)(2,1)} %refs_5_.1) | copy-start | bytes 786436
  0.0 56.9 %collective-permute-start.11 = (bf16[160,32768]{1,0:T(8,128)(2,1)}, bf16[160,32768]{1,0:T(8,128)(2,1)}, u32[]{:S(2)}, u32[]{:S(2)}) collective-permute-start(bf16[160,32768]{1,0:T(8,128)(2,1)} %refs_0_.16), channel_id=1, source_target_pairs={{0,1},{1,0},{2,3},{3,2},{4,5},{5,4},{6,7},{7,6},{8,9},{9,8},{10,11... | collective-permute-start | bytes 31457288 | tf_op jit(solution)/shard_map/ppermute | solution.py:207
  0.5 15.6 %collective-permute-start.1 = (bf16[2048,256]{1,0:T(8,128)(2,1)}, bf16[2048,256]{1,0:T(8,128)(2,1)S(1)}, u32[]{:S(2)}, u32[]{:S(2)}) collective-permute-start(bf16[2048,256]{1,0:T(8,128)(2,1)} %refs_4_.1), channel_id=1, source_target_pairs={{2,6},{3,1},{6,10},{7,3},{10,14},{11,7},{14,12},{15,11},{12,8},{13... | collective-permute-start | bytes 3145736 | tf_op jit(solution)/shard_map/ppermute | solution.py:206
  3.0 53.8 %collective-permute-start.10 = (bf16[160,8192]{1,0:T(8,128)(2,1)}, bf16[160,8192]{1,0:T(8,128)(2,1)}, u32[]{:S(2)}, u32[]{:S(2)}) collective-permute-start(bf16[160,8192]{1,0:T(8,128)(2,1)} %refs_2_.13), channel_id=1, source_target_pairs={{0,1},{1,0},{2,3},{3,2},{4,5},{5,4},{6,7},{7,6},{8,9},{9,8},{10,11... | collective-permute-start | bytes 7864328 | tf_op jit(solution)/shard_map/ppermute | solution.py:207
  3.3 15.7 %collective-permute-start = (bf16[512,256]{1,0:T(8,128)(2,1)}, bf16[512,256]{1,0:T(8,128)(2,1)S(1)}, u32[]{:S(2)}, u32[]{:S(2)}) collective-permute-start(bf16[512,256]{1,0:T(8,128)(2,1)} %refs_5_.1), channel_id=1, source_target_pairs={{2,6},{3,1},{6,10},{7,3},{10,14},{11,7},{14,12},{15,11},{12,8},{13... | collective-permute-start | bytes 786440 | tf_op jit(solution)/shard_map/ppermute | solution.py:206
  16.1 9.2 %collective-permute-start.2 = (bf16[512,256]{1,0:T(8,128)(2,1)}, bf16[512,256]{1,0:T(8,128)(2,1)S(1)}, u32[]{:S(2)}, u32[]{:S(2)}) collective-permute-start(bf16[512,256]{1,0:T(8,128)(2,1)} %refs_5_.1), channel_id=1, source_target_pairs={{6,2},{1,3},{10,6},{3,7},{14,10},{7,11},{12,14},{11,15},{8,12},{15... | collective-permute-start | bytes 786440 | tf_op jit(solution)/shard_map/ppermute | solution.py:225
  18.1 10.6 %collective-permute-start.7 = (bf16[1280,256]{1,0:T(8,128)(2,1)S(1)}, bf16[1280,256]{1,0:T(8,128)(2,1)S(1)}, u32[]{:S(2)}, u32[]{:S(2)}) collective-permute-start(bf16[1280,256]{1,0:T(8,128)(2,1)S(1)} %slice.10.refs_4_), channel_id=1, source_target_pairs={{2,6},{3,1},{6,10},{7,3},{10,14},{11,7},{14,12},{15,11},{12,8},{13... | collective-permute-start | bytes 1966088 | tf_op jit(solution)/shard_map/ppermute | solution.py:206
  25.3 12.9 %copy-start.4 = (bf16[1280,256]{1,0:T(8,128)(2,1)}, bf16[1280,256]{1,0:T(8,128)(2,1)S(1)}, u32[]{:S(2)}) copy-start(bf16[1280,256]{1,0:T(8,128)(2,1)S(1)} %pad_maximum_fusion.refs_5_) | copy-start | bytes 1966084
  25.3 11.0 %collective-permute-start.3 = (bf16[1280,256]{1,0:T(8,128)(2,1)S(1)}, bf16[1280,256]{1,0:T(8,128)(2,1)}, u32[]{:S(2)}, u32[]{:S(2)}) collective-permute-start(bf16[1280,256]{1,0:T(8,128)(2,1)S(1)} %pad_maximum_fusion.refs_5_), channel_id=1, source_target_pairs={{2,6},{3,1},{6,10},{7,3},{10,14},{11,7},{14,12},{15,11},{12,8},{13... | collective-permute-start | bytes 1966088 | tf_op jit(solution)/shard_map/ppermute | solution.py:206
  28.8 14.6 %collective-permute-start.8 = (bf16[1280,256]{1,0:T(8,128)(2,1)S(1)}, bf16[1280,256]{1,0:T(8,128)(2,1)}, u32[]{:S(2)}, u32[]{:S(2)}) collective-permute-start(bf16[1280,256]{1,0:T(8,128)(2,1)S(1)} %collective-permute-done.7.refs_4_), channel_id=1, source_target_pairs={{2,6},{3,1},{6,10},{7,3},{10,14},{11,7},{14,12},{15,11},{12,8},{13... | collective-permute-start | bytes 1966088 | tf_op jit(solution)/shard_map/ppermute | solution.py:206
  36.3 18.3 %collective-permute-start.4 = (bf16[1280,256]{1,0:T(8,128)(2,1)}, bf16[1280,256]{1,0:T(8,128)(2,1)}, u32[]{:S(2)}, u32[]{:S(2)}) collective-permute-start(bf16[1280,256]{1,0:T(8,128)(2,1)} %collective-permute-done.3.refs_5_), channel_id=1, source_target_pairs={{2,6},{3,1},{6,10},{7,3},{10,14},{11,7},{14,12},{15,11},{12,8},{13... | collective-permute-start | bytes 1966088 | tf_op jit(solution)/shard_map/ppermute | solution.py:206
  43.4 18.9 %collective-permute-start.9 = (bf16[1280,256]{1,0:T(8,128)(2,1)}, bf16[1280,256]{1,0:T(8,128)(2,1)S(1)}, u32[]{:S(2)}, u32[]{:S(2)}) collective-permute-start(bf16[1280,256]{1,0:T(8,128)(2,1)} %collective-permute-done.8.refs_4_), channel_id=1, source_target_pairs={{2,6},{3,1},{6,10},{7,3},{10,14},{11,7},{14,12},{15,11},{12,8},{13... | collective-permute-start | bytes 1966088 | tf_op jit(solution)/shard_map/ppermute | solution.py:206
  45.3 9.3 %collective-permute-start.5 = (bf16[512,256]{1,0:T(8,128)(2,1)S(1)}, bf16[512,256]{1,0:T(8,128)(2,1)}, u32[]{:S(2)}, u32[]{:S(2)}) collective-permute-start(bf16[512,256]{1,0:T(8,128)(2,1)S(1)} %collective-permute-done.2.refs_4_), channel_id=1, source_target_pairs={{6,2},{1,3},{10,6},{3,7},{14,10},{7,11},{12,14},{11,15},{8,12},{15... | collective-permute-start | bytes 786440 | tf_op jit(solution)/shard_map/ppermute | solution.py:230
  54.6 12.5 %collective-permute-start.6 = (bf16[1280,256]{1,0:T(8,128)(2,1)}, bf16[1280,256]{1,0:T(8,128)(2,1)S(1)}, u32[]{:S(2)}, u32[]{:S(2)}) collective-permute-start(bf16[1280,256]{1,0:T(8,128)(2,1)} %collective-permute-done.4.refs_5_), channel_id=1, source_target_pairs={{2,6},{3,1},{6,10},{7,3},{10,14},{11,7},{14,12},{15,11},{12,8},{13... | collective-permute-start | bytes 1966088 | tf_op jit(solution)/shard_map/ppermute | solution.py:206
  62.3 12.5 %collective-permute-start.13 = (bf16[1280,256]{1,0:T(8,128)(2,1)S(1)}, bf16[1280,256]{1,0:T(8,128)(2,1)S(1)}, u32[]{:S(2)}, u32[]{:S(2)}) collective-permute-start(bf16[1280,256]{1,0:T(8,128)(2,1)S(1)} %collective-permute-done.9.refs_4_), channel_id=1, source_target_pairs={{2,6},{3,1},{6,10},{7,3},{10,14},{11,7},{14,12},{15,11},{12,8},{13... | collective-permute-start | bytes 1966088 | tf_op jit(solution)/shard_map/ppermute | solution.py:206
  67.1 4.7 %copy-start.6 = (bf16[1280,256]{1,0:T(8,128)(2,1)}, bf16[1280,256]{1,0:T(8,128)(2,1)S(1)}, u32[]{:S(2)}) copy-start(bf16[1280,256]{1,0:T(8,128)(2,1)S(1)} %collective-permute-done.6.refs_5_) | copy-start | bytes 1966084
  67.1 14.0 %collective-permute-start.12 = (bf16[1280,256]{1,0:T(8,128)(2,1)S(1)}, bf16[1280,256]{1,0:T(8,128)(2,1)S(1)}, u32[]{:S(2)}, u32[]{:S(2)}) collective-permute-start(bf16[1280,256]{1,0:T(8,128)(2,1)S(1)} %collective-permute-done.6.refs_5_), channel_id=1, source_target_pairs={{2,6},{3,1},{6,10},{7,3},{10,14},{11,7},{14,12},{15,11},{12,8},{13... | collective-permute-start | bytes 1966088 | tf_op jit(solution)/shard_map/ppermute | solution.py:206
  74.8 13.9 %collective-permute-start.15 = (bf16[1280,256]{1,0:T(8,128)(2,1)S(1)}, bf16[1280,256]{1,0:T(8,128)(2,1)S(1)}, u32[]{:S(2)}, u32[]{:S(2)}) collective-permute-start(bf16[1280,256]{1,0:T(8,128)(2,1)S(1)} %collective-permute-done.13.refs_4_), channel_id=1, source_target_pairs={{2,6},{3,1},{6,10},{7,3},{10,14},{11,7},{14,12},{15,11},{12,8},{13... | collective-permute-start | bytes 1966088 | tf_op jit(solution)/shard_map/ppermute | solution.py:206
  81.2 4.8 %copy-start.5 = (bf16[1280,256]{1,0:T(8,128)(2,1)}, bf16[1280,256]{1,0:T(8,128)(2,1)S(1)}, u32[]{:S(2)}) copy-start(bf16[1280,256]{1,0:T(8,128)(2,1)S(1)} %collective-permute-done.12.refs_5_) | copy-start | bytes 1966084
  81.2 11.2 %collective-permute-start.14 = (bf16[768,256]{1,0:T(8,128)(2,1)S(1)}, bf16[768,256]{1,0:T(8,128)(2,1)S(1)}, u32[]{:S(2)}, u32[]{:S(2)}) collective-permute-start(bf16[768,256]{1,0:T(8,128)(2,1)S(1)} %slice.11), channel_id=1, source_target_pairs={{2,6},{3,1},{6,10},{7,3},{10,14},{11,7},{14,12},{15,11},{12,8},{13... | collective-permute-start | bytes 1179656 | tf_op jit(solution)/shard_map/ppermute | solution.py:206
  88.7 5.6 %copy-start.2 = (s32[2]{0:T(128)S(1)}, s32[2]{0:T(128)}, u32[]{:S(2)}) copy-start(s32[2]{0:T(128)} %refs_7_.1) | copy-start | bytes 28
  88.8 5.6 %copy-start.3 = (s32[2]{0:T(128)S(1)}, s32[2]{0:T(128)}, u32[]{:S(2)}) copy-start(s32[2]{0:T(128)} %refs_8_.1) | copy-start | bytes 28
  88.8 10.8 %collective-permute-start.17 = (bf16[1280,256]{1,0:T(8,128)(2,1)S(1)}, bf16[1280,256]{1,0:T(8,128)(2,1)S(1)}, u32[]{:S(2)}, u32[]{:S(2)}) collective-permute-start(bf16[1280,256]{1,0:T(8,128)(2,1)S(1)} %collective-permute-done.15.refs_2_), channel_id=1, source_target_pairs={{2,6},{3,1},{6,10},{7,3},{10,14},{11,7},{14,12},{15,11},{12,8},{13... | collective-permute-start | bytes 1966088 | tf_op jit(solution)/shard_map/ppermute | solution.py:206
  92.4 11.2 %collective-permute-start.16 = (bf16[768,256]{1,0:T(8,128)(2,1)S(1)}, bf16[768,256]{1,0:T(8,128)(2,1)S(1)}, u32[]{:S(2)}, u32[]{:S(2)}) collective-permute-start(bf16[768,256]{1,0:T(8,128)(2,1)S(1)} %collective-permute-done.14.refs_3_), channel_id=1, source_target_pairs={{2,6},{3,1},{6,10},{7,3},{10,14},{11,7},{14,12},{15,11},{12,8},{13... | collective-permute-start | bytes 1179656 | tf_op jit(solution)/shard_map/ppermute | solution.py:206
  96.5 2.4 %collective-permute-start.18 = (f32[328,256]{1,0:T(8,128)S(1)}, f32[328,256]{1,0:T(8,128)S(1)}, u32[]{:S(2)}, u32[]{:S(2)}) collective-permute-start(f32[328,256]{1,0:T(8,128)S(1)} %turned.1.own_ref), channel_id=1, source_target_pairs={{0,1},{1,0},{2,3},{3,2},{4,5},{5,4},{6,7},{7,6},{8,9},{9,8},{10,11... | collective-permute-start | bytes 1007624 | tf_op jit(solution)/shard_map/ppermute | solution.py:207

commit v22 on v21

--- a/solution.py
+++ b/solution.py
@@ -252,7 +252,7 @@
             totals, summed = sum_to(min(2 * s - 6, s), totals, summed)
             late, totals = lax.optimization_barrier((late, totals))
             early, totals = lax.optimization_barrier((early, totals))
-        if s == 3 and rows_in:
+        if s == 4 and rows_in:
             early, turned = lax.optimization_barrier((early, turned))
         late = send(late)
         if s == last - 1:

time: 114 us -> 114 us (level)
    ppermute x1, waiting for transfers between devices: 9.22 us -> 2.16 us  [shards(): turned = [turned, lax.ppermute(turned, 'dp', backward)]]
    ppermute x14, waiting for transfers between devices: 34.1 us -> 40.9 us  [shards(): send = lambda x: lax.ppermute(x, 'dp', pairs)]
  transfers between devices with their start and end apart: 19 -> 19, of which waited for: 11 -> 12; matrix products, arithmetic and copies ran while one was open for 1% -> 1% of each run, Pallas kernels for 23% -> 23%
where the time goes in v22:
time: 114 us
  waiting for transfers between devices  49.4 us (43%)
  starting transfers between devices  27.4 us (24%)
  Pallas kernels  26.3 us (23%)
  blocking collectives  9.17 us (8%)
    ppermute x14, waiting for transfers between devices, shards(): send = lambda x: lax.ppermute(x, 'dp', pairs)  40.9 us
    pallas_call x11, Pallas kernels, call(): pl.pallas_call(kernel, grid_spec=pltpu.PrefetchScalarGridSpec(num_scalar_...  25.8 us
    ppermute x14, starting transfers between devices, shards(): send = lambda x: lax.ppermute(x, 'dp', pairs)  24.2 us
    all_to_all x1, blocking collectives, shards(): lax.all_to_all(table.reshape(devices, slots, queries), 'dp', 0, 0, axis_i...  9.17 us
    ppermute x1, waiting for transfers between devices, shards(): turned = lax.ppermute(turned, 'dp', [(j, i) for i, j in pairs])  6.32 us
  transfers between devices with their start and end apart: 19, of which 12 were waited for; matrix products, arithmetic and copies ran while one was open for 1% of the time, Pallas kernels for 23%

profile of v22, /device:TPU:0, one launch (start us, length us, event | category | flops | bytes accessed | tf_op | source)
XLA Modules:
  0.0 114.0 jit_solution(11622650789580022143)
XLA Ops:
  0.0 0.0 copy-start
  0.0 0.5 collective-permute-start.10
  0.5 2.6 %collective-permute-start.1 = (bf16[2048,256]{1,0:T(8,128)(2,1)}, bf16[2048,256]{1,0:T(8,128)(2,1)S(1)}, u32[]{:S(2)}, u32[]{:S(2)}) collective-permute-start(bf16[2048,256]{1,0:T(8,128)(2,1)} %refs_4_.1), channel_id=1, source_target_pairs={{2,6},{3,1},{6,10},{7,3},{10,14},{11,7},{14,12},{15,11},{12,8},{13... | collective-permute-start | bytes 3145736 | tf_op jit(solution)/shard_map/ppermute | solution.py:206
  3.0 0.2 collective-permute-start.9
  3.3 1.4 %collective-permute-start = (bf16[512,256]{1,0:T(8,128)(2,1)}, bf16[512,256]{1,0:T(8,128)(2,1)S(1)}, u32[]{:S(2)}, u32[]{:S(2)}) collective-permute-start(bf16[512,256]{1,0:T(8,128)(2,1)} %refs_5_.1), channel_id=1, source_target_pairs={{2,6},{3,1},{6,10},{7,3},{10,14},{11,7},{14,12},{15,11},{12,8},{13... | collective-permute-start | bytes 786440 | tf_op jit(solution)/shard_map/ppermute | solution.py:206
  4.6 11.5 %collective-permute-done.1 = bf16[2048,256]{1,0:T(8,128)(2,1)S(1)} collective-permute-done((bf16[2048,256]{1,0:T(8,128)(2,1)}, bf16[2048,256]{1,0:T(8,128)(2,1)S(1)}, u32[]{:S(2)}, u32[]{:S(2)}) %collective-permute-start.1) | collective-permute-done | bytes 1048608 | tf_op jit(solution)/shard_map/ppermute | solution.py:206
  16.1 2.0 %collective-permute-start.2 = (bf16[512,256]{1,0:T(8,128)(2,1)}, bf16[512,256]{1,0:T(8,128)(2,1)S(1)}, u32[]{:S(2)}, u32[]{:S(2)}) collective-permute-start(bf16[512,256]{1,0:T(8,128)(2,1)} %refs_5_.1), channel_id=1, source_target_pairs={{6,2},{1,3},{10,6},{3,7},{14,10},{7,11},{12,14},{11,15},{8,12},{15... | collective-permute-start | bytes 786440 | tf_op jit(solution)/shard_map/ppermute | solution.py:225
  18.1 0.1 collective-permute-start.6
  18.3 0.7 collective-permute-done
  19.0 6.3 %collective-permute-done.2.refs_4_ = bf16[512,256]{1,0:T(8,128)(2,1)S(1)} collective-permute-done((bf16[512,256]{1,0:T(8,128)(2,1)}, bf16[512,256]{1,0:T(8,128)(2,1)S(1)}, u32[]{:S(2)}, u32[]{:S(2)}) %collective-permute-start.2) | collective-permute-done | bytes 262176 | tf_op jit(solution)/shard_map/ppermute | solution.py:225
  25.3 0.0 copy-start.4
  25.3 2.2 %collective-permute-start.3 = (bf16[1280,256]{1,0:T(8,128)(2,1)S(1)}, bf16[1280,256]{1,0:T(8,128)(2,1)}, u32[]{:S(2)}, u32[]{:S(2)}) collective-permute-start(bf16[1280,256]{1,0:T(8,128)(2,1)S(1)} %pad_maximum_fusion.refs_5_), channel_id=1, source_target_pairs={{2,6},{3,1},{6,10},{7,3},{10,14},{11,7},{14,12},{15,11},{12,8},{13... | collective-permute-start | bytes 1966088 | tf_op jit(solution)/shard_map/ppermute | solution.py:206
  27.5 1.2 %collective-permute-done.6.refs_4_ = bf16[1280,256]{1,0:T(8,128)(2,1)S(1)} collective-permute-done((bf16[1280,256]{1,0:T(8,128)(2,1)S(1)}, bf16[1280,256]{1,0:T(8,128)(2,1)S(1)}, u32[]{:S(2)}, u32[]{:S(2)}) %collective-permute-start.6) | collective-permute-done | bytes 655392 | tf_op jit(solution)/shard_map/ppermute | solution.py:206
  28.8 1.9 %collective-permute-start.7 = (bf16[1280,256]{1,0:T(8,128)(2,1)S(1)}, bf16[1280,256]{1,0:T(8,128)(2,1)}, u32[]{:S(2)}, u32[]{:S(2)}) collective-permute-start(bf16[1280,256]{1,0:T(8,128)(2,1)S(1)} %collective-permute-done.6.refs_4_), channel_id=1, source_target_pairs={{2,6},{3,1},{6,10},{7,3},{10,14},{11,7},{14,12},{15,11},{12,8},{13... | collective-permute-start | bytes 1966088 | tf_op jit(solution)/shard_map/ppermute | solution.py:206
  30.7 5.7 %collective-permute-done.3.refs_5_ = bf16[1280,256]{1,0:T(8,128)(2,1)} collective-permute-done((bf16[1280,256]{1,0:T(8,128)(2,1)S(1)}, bf16[1280,256]{1,0:T(8,128)(2,1)}, u32[]{:S(2)}, u32[]{:S(2)}) %collective-permute-start.3) | collective-permute-done | bytes 655392 | tf_op jit(solution)/shard_map/ppermute | solution.py:206
  36.3 1.9 %collective-permute-start.4 = (bf16[1280,256]{1,0:T(8,128)(2,1)}, bf16[1280,256]{1,0:T(8,128)(2,1)}, u32[]{:S(2)}, u32[]{:S(2)}) collective-permute-start(bf16[1280,256]{1,0:T(8,128)(2,1)} %collective-permute-done.3.refs_5_), channel_id=1, source_target_pairs={{2,6},{3,1},{6,10},{7,3},{10,14},{11,7},{14,12},{15,11},{12,8},{13... | collective-permute-start | bytes 1966088 | tf_op jit(solution)/shard_map/ppermute | solution.py:206
  38.2 0.0 copy-done.4
  38.2 5.1 %collective-permute-done.7.refs_4_ = bf16[1280,256]{1,0:T(8,128)(2,1)} collective-permute-done((bf16[1280,256]{1,0:T(8,128)(2,1)S(1)}, bf16[1280,256]{1,0:T(8,128)(2,1)}, u32[]{:S(2)}, u32[]{:S(2)}) %collective-permute-start.7) | collective-permute-done | bytes 655392 | tf_op jit(solution)/shard_map/ppermute | solution.py:206
  43.4 1.9 %collective-permute-start.8 = (bf16[1280,256]{1,0:T(8,128)(2,1)}, bf16[1280,256]{1,0:T(8,128)(2,1)S(1)}, u32[]{:S(2)}, u32[]{:S(2)}) collective-permute-start(bf16[1280,256]{1,0:T(8,128)(2,1)} %collective-permute-done.7.refs_4_), channel_id=1, source_target_pairs={{2,6},{3,1},{6,10},{7,3},{10,14},{11,7},{14,12},{15,11},{12,8},{13... | collective-permute-start | bytes 1966088 | tf_op jit(solution)/shard_map/ppermute | solution.py:206
  45.3 5.1 %collective-permute-done.4.refs_5_ = bf16[1280,256]{1,0:T(8,128)(2,1)} collective-permute-done((bf16[1280,256]{1,0:T(8,128)(2,1)}, bf16[1280,256]{1,0:T(8,128)(2,1)}, u32[]{:S(2)}, u32[]{:S(2)}) %collective-permute-start.4) | collective-permute-done | bytes 655392 | tf_op jit(solution)/shard_map/ppermute | solution.py:206
  50.4 1.9 %collective-permute-start.5 = (bf16[1280,256]{1,0:T(8,128)(2,1)}, bf16[1280,256]{1,0:T(8,128)(2,1)S(1)}, u32[]{:S(2)}, u32[]{:S(2)}) collective-permute-start(bf16[1280,256]{1,0:T(8,128)(2,1)} %collective-permute-done.4.refs_5_), channel_id=1, source_target_pairs={{2,6},{3,1},{6,10},{7,3},{10,14},{11,7},{14,12},{15,11},{12,8},{13... | collective-permute-start | bytes 1966088 | tf_op jit(solution)/shard_map/ppermute | solution.py:206
  52.3 0.7 dynamic-slice_bitcast_fusion.order_ref
  53.0 0.0 collective-permute-done.9.refs_1_.refs_3_
  53.0 0.0 collective-permute-done.10.refs_3_.sib_ref.refs_1_
  53.0 0.0 copy-done
  53.0 0.0 copy-done.1
  53.0 2.6 %step.8 = (f32[320,256]{1,0:T(8,128)S(1)}, f32[320,256]{1,0:T(8,128)S(1)}) custom-call(s32[8]{0:T(128)S(1)} %dynamic-slice_bitcast_fusion.order_ref, bf16[160,8192]{1,0:T(8,128)(2,1)} %refs_2_.13, bf16[160,8192]{1,0:T(8,128)(2,1)} %collective-permute-done.9.refs_1_.refs_3_, bf16[160,32768]{1,0:T(8,128)(2,1)} %refs_0_.16, ...), custom_call_target="tpu_custom_call" | custom-call | flops 419430400 | bytes 3604480 | tf_op jit(solution)/shard_map/step/pallas_call | solution.py:59
  55.6 2.8 %step.9 = (f32[320,256]{1,0:T(8,128)S(1)}, f32[320,256]{1,0:T(8,128)S(1)}) custom-call(s32[8]{0:T(128)S(1)} %dynamic-slice_bitcast_fusion.order_ref, bf16[160,8192]{1,0:T(8,128)(2,1)} %refs_2_.13, bf16[160,8192]{1,0:T(8,128)(2,1)} %collective-permute-done.9.refs_1_.refs_3_, bf16[160,32768]{1,0:T(8,128)(2,1)} %refs_0_.16, ...), custom_call_target="tpu_custom_call" | custom-call | flops 419430400 | bytes 4259840 | tf_op jit(solution)/shard_map/step/pallas_call | solution.py:59
  58.4 0.0 collective-permute-done.8.refs_4_
  58.4 1.6 %collective-permute-start.13 = (bf16[1280,256]{1,0:T(8,128)(2,1)S(1)}, bf16[1280,256]{1,0:T(8,128)(2,1)S(1)}, u32[]{:S(2)}, u32[]{:S(2)}) collective-permute-start(bf16[1280,256]{1,0:T(8,128)(2,1)S(1)} %collective-permute-done.8.refs_4_), channel_id=1, source_target_pairs={{2,6},{3,1},{6,10},{7,3},{10,14},{11,7},{14,12},{15,11},{12,8},{13... | collective-permute-start | bytes 1966088 | tf_op jit(solution)/shard_map/ppermute | solution.py:206
  60.0 0.4 collective-permute-start.11
  60.5 6.6 %collective-permute-done.5.refs_5_ = bf16[1280,256]{1,0:T(8,128)(2,1)S(1)} collective-permute-done((bf16[1280,256]{1,0:T(8,128)(2,1)}, bf16[1280,256]{1,0:T(8,128)(2,1)S(1)}, u32[]{:S(2)}, u32[]{:S(2)}) %collective-permute-start.5) | collective-permute-done | bytes 655392 | tf_op jit(solution)/shard_map/ppermute | solution.py:206
  67.1 2.2 %collective-permute-done.11.refs_5_ = bf16[512,256]{1,0:T(8,128)(2,1)S(1)} collective-permute-done((bf16[512,256]{1,0:T(8,128)(2,1)S(1)}, bf16[512,256]{1,0:T(8,128)(2,1)S(1)}, u32[]{:S(2)}, u32[]{:S(2)}) %collective-permute-start.11) | collective-permute-done | bytes 262176 | tf_op jit(solution)/shard_map/ppermute | solution.py:230
  69.3 1.6 %collective-permute-start.12 = (bf16[1280,256]{1,0:T(8,128)(2,1)S(1)}, bf16[1280,256]{1,0:T(8,128)(2,1)S(1)}, u32[]{:S(2)}, u32[]{:S(2)}) collective-permute-start(bf16[1280,256]{1,0:T(8,128)(2,1)S(1)} %collective-permute-done.5.refs_5_), channel_id=1, source_target_pairs={{2,6},{3,1},{6,10},{7,3},{10,14},{11,7},{14,12},{15,11},{12,8},{13... | collective-permute-start | bytes 1966088 | tf_op jit(solution)/shard_map/ppermute | solution.py:206
  70.8 2.8 %step.10 = (f32[320,256]{1,0:T(8,128)S(1)}, f32[320,256]{1,0:T(8,128)S(1)}) custom-call(s32[8]{0:T(128)S(1)} %dynamic-slice_bitcast_fusion.order_ref, bf16[160,8192]{1,0:T(8,128)(2,1)} %refs_2_.13, bf16[160,8192]{1,0:T(8,128)(2,1)} %collective-permute-done.9.refs_1_.refs_3_, bf16[160,32768]{1,0:T(8,128)(2,1)} %refs_0_.16, ...), custom_call_target="tpu_custom_call" | custom-call | flops 419430400 | bytes 4259840 | tf_op jit(solution)/shard_map/step/pallas_call | solution.py:59
  73.6 0.0 copy-done.6
  73.6 3.0 %step.11 = (f32[320,256]{1,0:T(8,128)S(1)}, f32[320,256]{1,0:T(8,128)S(1)}) custom-call(s32[8]{0:T(128)S(1)} %dynamic-slice_bitcast_fusion.order_ref, bf16[160,8192]{1,0:T(8,128)(2,1)} %refs_2_.13, bf16[160,8192]{1,0:T(8,128)(2,1)} %collective-permute-done.9.refs_1_.refs_3_, bf16[160,32768]{1,0:T(8,128)(2,1)} %refs_0_.16, ...), custom_call_target="tpu_custom_call" | custom-call | flops 419430400 | bytes 4259840 | tf_op jit(solution)/shard_map/step/pallas_call | solution.py:59
  76.6 0.0 collective-permute-done.13.refs_4_
  76.6 1.7 %collective-permute-start.15 = (bf16[1280,256]{1,0:T(8,128)(2,1)S(1)}, bf16[1280,256]{1,0:T(8,128)(2,1)S(1)}, u32[]{:S(2)}, u32[]{:S(2)}) collective-permute-start(bf16[1280,256]{1,0:T(8,128)(2,1)S(1)} %collective-permute-done.13.refs_4_), channel_id=1, source_target_pairs={{2,6},{3,1},{6,10},{7,3},{10,14},{11,7},{14,12},{15,11},{12,8},{13... | collective-permute-start | bytes 1966088 | tf_op jit(solution)/shard_map/ppermute | solution.py:206
  78.3 2.9 %collective-permute-done.12.refs_5_ = bf16[1280,256]{1,0:T(8,128)(2,1)S(1)} collective-permute-done((bf16[1280,256]{1,0:T(8,128)(2,1)S(1)}, bf16[1280,256]{1,0:T(8,128)(2,1)S(1)}, u32[]{:S(2)}, u32[]{:S(2)}) %collective-permute-start.12) | collective-permute-done | bytes 655392 | tf_op jit(solution)/shard_map/ppermute | solution.py:206
  81.2 2.0 %collective-permute-start.14 = (bf16[768,256]{1,0:T(8,128)(2,1)S(1)}, bf16[768,256]{1,0:T(8,128)(2,1)S(1)}, u32[]{:S(2)}, u32[]{:S(2)}) collective-permute-start(bf16[768,256]{1,0:T(8,128)(2,1)S(1)} %slice.11), channel_id=1, source_target_pairs={{2,6},{3,1},{6,10},{7,3},{10,14},{11,7},{14,12},{15,11},{12,8},{13... | collective-permute-start | bytes 1179656 | tf_op jit(solution)/shard_map/ppermute | solution.py:206
  83.2 2.8 %step.12 = (f32[320,256]{1,0:T(8,128)S(1)}, f32[320,256]{1,0:T(8,128)S(1)}) custom-call(s32[8]{0:T(128)S(1)} %dynamic-slice_bitcast_fusion.order_ref, bf16[160,8192]{1,0:T(8,128)(2,1)} %refs_2_.13, bf16[160,8192]{1,0:T(8,128)(2,1)} %collective-permute-done.9.refs_1_.refs_3_, bf16[160,32768]{1,0:T(8,128)(2,1)} %refs_0_.16, ...), custom_call_target="tpu_custom_call" | custom-call | flops 419430400 | bytes 4259840 | tf_op jit(solution)/shard_map/step/pallas_call | solution.py:59
  85.9 0.0 copy-done.5
  85.9 2.8 %step.13 = (f32[320,256]{1,0:T(8,128)S(1)}, f32[320,256]{1,0:T(8,128)S(1)}) custom-call(s32[8]{0:T(128)S(1)} %dynamic-slice_bitcast_fusion.order_ref, bf16[160,8192]{1,0:T(8,128)(2,1)} %refs_2_.13, bf16[160,8192]{1,0:T(8,128)(2,1)} %collective-permute-done.9.refs_1_.refs_3_, bf16[160,32768]{1,0:T(8,128)(2,1)} %refs_0_.16, ...), custom_call_target="tpu_custom_call" | custom-call | flops 419430400 | bytes 4259840 | tf_op jit(solution)/shard_map/step/pallas_call | solution.py:59
  88.7 0.0 collective-permute-done.15.refs_2_
  88.7 0.0 copy-start.2
  88.8 0.0 copy-start.3
  88.8 1.6 %collective-permute-start.17 = (bf16[1280,256]{1,0:T(8,128)(2,1)S(1)}, bf16[1280,256]{1,0:T(8,128)(2,1)S(1)}, u32[]{:S(2)}, u32[]{:S(2)}) collective-permute-start(bf16[1280,256]{1,0:T(8,128)(2,1)S(1)} %collective-permute-done.15.refs_2_), channel_id=1, source_target_pairs={{2,6},{3,1},{6,10},{7,3},{10,14},{11,7},{14,12},{15,11},{12,8},{13... | collective-permute-start | bytes 1966088 | tf_op jit(solution)/shard_map/ppermute | solution.py:206
  90.4 1.9 %window.1.window_ref = bf16[320,768]{1,0:T(8,128)(2,1)S(1)} custom-call(s32[8]{0:T(128)S(1)} %dynamic-slice_bitcast_fusion.order_ref, bf16[160,32768]{1,0:T(8,128)(2,1)} %refs_0_.16, bf16[160,32768]{1,0:T(8,128)(2,1)} %collective-permute-done.10.refs_3_.sib_ref.refs_1_), custom_call_target="tpu_custom_call" | custom-call | bytes 1802240 | tf_op jit(solution)/shard_map/window/pallas_call | solution.py:59
  92.3 0.1 collective-permute-done.14.refs_3_
  92.4 1.9 %collective-permute-start.16 = (bf16[768,256]{1,0:T(8,128)(2,1)S(1)}, bf16[768,256]{1,0:T(8,128)(2,1)S(1)}, u32[]{:S(2)}, u32[]{:S(2)}) collective-permute-start(bf16[768,256]{1,0:T(8,128)(2,1)S(1)} %collective-permute-done.14.refs_3_), channel_id=1, source_target_pairs={{2,6},{3,1},{6,10},{7,3},{10,14},{11,7},{14,12},{15,11},{12,8},{13... | collective-permute-start | bytes 1179656 | tf_op jit(solution)/shard_map/ppermute | solution.py:206
  94.3 0.0 copy-done.2
  94.3 0.0 copy-done.3
  94.3 2.0 %turned.1.own_ref = f32[328,256]{1,0:T(8,128)S(1)} custom-call(s32[8]{0:T(128)S(1)} %dynamic-slice_bitcast_fusion.order_ref, bf16[160,8192]{1,0:T(8,128)(2,1)} %refs_2_.13, bf16[160,8192]{1,0:T(8,128)(2,1)} %collective-permute-done.9.refs_1_.refs_3_, bf16[160,8192]{1,0:T(8,128)(2,1)} %refs_2_.13, bf16[160,8192]{1,0:T(8,128)(2,1)} %collective-permute-done.9.refs_1_.refs_3_, ...), custom_call_target="tpu_custom_call" | custom-call | flops 167772160 | bytes 1843200 | tf_op jit(solution)/shard_map/turned/pallas_call | solution.py:59
  96.4 0.1 collective-permute-start.18
  96.5 2.4 %step.14.refs_3_ = f32[320,256]{1,0:T(8,128)S(1)} custom-call(s32[8]{0:T(128)S(1)} %dynamic-slice_bitcast_fusion.order_ref, bf16[160,32768]{1,0:T(8,128)(2,1)} %refs_0_.16, bf16[160,32768]{1,0:T(8,128)(2,1)} %collective-permute-done.10.refs_3_.sib_ref.refs_1_, bf16[1280,256]{1,0:T(8,128)(2,1)S(1)} %collective-permute-done.15.refs_2_, ...), custom_call_target="tpu_custom_call" | custom-call | flops 335544320 | bytes 3014656 | tf_op jit(solution)/shard_map/step/pallas_call | solution.py:59
  98.8 0.0 collective-permute-done.18.got_ref
  98.8 0.6 masked.1.inn_ref
  99.5 0.0 collective-permute-done.17.refs_2_
  99.5 2.2 %step.15.total_ref = f32[320,256]{1,0:T(8,128)S(1)} custom-call(s32[8]{0:T(128)S(1)} %dynamic-slice_bitcast_fusion.order_ref, bf16[160,32768]{1,0:T(8,128)(2,1)} %refs_0_.16, bf16[160,32768]{1,0:T(8,128)(2,1)} %collective-permute-done.10.refs_3_.sib_ref.refs_1_, bf16[1280,256]{1,0:T(8,128)(2,1)S(1)} %collective-permute-done.17.refs_2_, ...), custom_call_target="tpu_custom_call" | custom-call | flops 209715200 | bytes 2621440 | tf_op jit(solution)/shard_map/step/pallas_call | solution.py:59
  101.7 1.9 %collective-permute-done.16.block_ref = bf16[768,256]{1,0:T(8,128)(2,1)S(1)} collective-permute-done((bf16[768,256]{1,0:T(8,128)(2,1)S(1)}, bf16[768,256]{1,0:T(8,128)(2,1)S(1)}, u32[]{:S(2)}, u32[]{:S(2)}) %collective-permute-start.16) | collective-permute-done | bytes 393248 | tf_op jit(solution)/shard_map/ppermute | solution.py:206
  103.6 0.6 score.1
  104.2 9.2 %all_to_all.5 = f32[16,2,8]{2,1,0:T(2,128)S(1)} all-to-all(f32[16,2,8]{2,1,0:T(2,128)S(1)} %bitcast.3), channel_id=1, replica_groups={{15,14,13,12,11,10,9,8,7,6,5,4,3,2,1,0},{31,30,29,28,27,26,25,24,23,22,..., dimensions={0} | all-to-all | bytes 2048 | tf_op jit(solution)/shard_map/all_to_all | solution.py:288
  113.4 0.6 reduce_sum.9
  (7 shorter events, 0.1 us)
Async XLA Ops:
  0.0 53.0 %copy-start = (bf16[2048,256]{1,0:T(8,128)(2,1)S(1)}, bf16[2048,256]{1,0:T(8,128)(2,1)}, u32[]{:S(2)}) copy-start(bf16[2048,256]{1,0:T(8,128)(2,1)} %refs_4_.1) | copy-start | bytes 3145732
  0.0 53.0 %copy-start.1 = (bf16[512,256]{1,0:T(8,128)(2,1)S(1)}, bf16[512,256]{1,0:T(8,128)(2,1)}, u32[]{:S(2)}) copy-start(bf16[512,256]{1,0:T(8,128)(2,1)} %refs_5_.1) | copy-start | bytes 786436
  0.0 53.0 %collective-permute-start.10 = (bf16[160,32768]{1,0:T(8,128)(2,1)}, bf16[160,32768]{1,0:T(8,128)(2,1)}, u32[]{:S(2)}, u32[]{:S(2)}) collective-permute-start(bf16[160,32768]{1,0:T(8,128)(2,1)} %refs_0_.16), channel_id=1, source_target_pairs={{0,1},{1,0},{2,3},{3,2},{4,5},{5,4},{6,7},{7,6},{8,9},{9,8},{10,11... | collective-permute-start | bytes 31457288 | tf_op jit(solution)/shard_map/ppermute | solution.py:207
  0.5 15.6 %collective-permute-start.1 = (bf16[2048,256]{1,0:T(8,128)(2,1)}, bf16[2048,256]{1,0:T(8,128)(2,1)S(1)}, u32[]{:S(2)}, u32[]{:S(2)}) collective-permute-start(bf16[2048,256]{1,0:T(8,128)(2,1)} %refs_4_.1), channel_id=1, source_target_pairs={{2,6},{3,1},{6,10},{7,3},{10,14},{11,7},{14,12},{15,11},{12,8},{13... | collective-permute-start | bytes 3145736 | tf_op jit(solution)/shard_map/ppermute | solution.py:206
  3.0 49.9 %collective-permute-start.9 = (bf16[160,8192]{1,0:T(8,128)(2,1)}, bf16[160,8192]{1,0:T(8,128)(2,1)}, u32[]{:S(2)}, u32[]{:S(2)}) collective-permute-start(bf16[160,8192]{1,0:T(8,128)(2,1)} %refs_2_.13), channel_id=1, source_target_pairs={{0,1},{1,0},{2,3},{3,2},{4,5},{5,4},{6,7},{7,6},{8,9},{9,8},{10,11... | collective-permute-start | bytes 7864328 | tf_op jit(solution)/shard_map/ppermute | solution.py:207
  3.3 15.7 %collective-permute-start = (bf16[512,256]{1,0:T(8,128)(2,1)}, bf16[512,256]{1,0:T(8,128)(2,1)S(1)}, u32[]{:S(2)}, u32[]{:S(2)}) collective-permute-start(bf16[512,256]{1,0:T(8,128)(2,1)} %refs_5_.1), channel_id=1, source_target_pairs={{2,6},{3,1},{6,10},{7,3},{10,14},{11,7},{14,12},{15,11},{12,8},{13... | collective-permute-start | bytes 786440 | tf_op jit(solution)/shard_map/ppermute | solution.py:206
  16.1 9.2 %collective-permute-start.2 = (bf16[512,256]{1,0:T(8,128)(2,1)}, bf16[512,256]{1,0:T(8,128)(2,1)S(1)}, u32[]{:S(2)}, u32[]{:S(2)}) collective-permute-start(bf16[512,256]{1,0:T(8,128)(2,1)} %refs_5_.1), channel_id=1, source_target_pairs={{6,2},{1,3},{10,6},{3,7},{14,10},{7,11},{12,14},{11,15},{8,12},{15... | collective-permute-start | bytes 786440 | tf_op jit(solution)/shard_map/ppermute | solution.py:225
  18.1 10.6 %collective-permute-start.6 = (bf16[1280,256]{1,0:T(8,128)(2,1)S(1)}, bf16[1280,256]{1,0:T(8,128)(2,1)S(1)}, u32[]{:S(2)}, u32[]{:S(2)}) collective-permute-start(bf16[1280,256]{1,0:T(8,128)(2,1)S(1)} %slice.10.refs_4_), channel_id=1, source_target_pairs={{2,6},{3,1},{6,10},{7,3},{10,14},{11,7},{14,12},{15,11},{12,8},{13... | collective-permute-start | bytes 1966088 | tf_op jit(solution)/shard_map/ppermute | solution.py:206
  25.3 12.9 %copy-start.4 = (bf16[1280,256]{1,0:T(8,128)(2,1)}, bf16[1280,256]{1,0:T(8,128)(2,1)S(1)}, u32[]{:S(2)}) copy-start(bf16[1280,256]{1,0:T(8,128)(2,1)S(1)} %pad_maximum_fusion.refs_5_) | copy-start | bytes 1966084
  25.3 11.0 %collective-permute-start.3 = (bf16[1280,256]{1,0:T(8,128)(2,1)S(1)}, bf16[1280,256]{1,0:T(8,128)(2,1)}, u32[]{:S(2)}, u32[]{:S(2)}) collective-permute-start(bf16[1280,256]{1,0:T(8,128)(2,1)S(1)} %pad_maximum_fusion.refs_5_), channel_id=1, source_target_pairs={{2,6},{3,1},{6,10},{7,3},{10,14},{11,7},{14,12},{15,11},{12,8},{13... | collective-permute-start | bytes 1966088 | tf_op jit(solution)/shard_map/ppermute | solution.py:206
  28.8 14.6 %collective-permute-start.7 = (bf16[1280,256]{1,0:T(8,128)(2,1)S(1)}, bf16[1280,256]{1,0:T(8,128)(2,1)}, u32[]{:S(2)}, u32[]{:S(2)}) collective-permute-start(bf16[1280,256]{1,0:T(8,128)(2,1)S(1)} %collective-permute-done.6.refs_4_), channel_id=1, source_target_pairs={{2,6},{3,1},{6,10},{7,3},{10,14},{11,7},{14,12},{15,11},{12,8},{13... | collective-permute-start | bytes 1966088 | tf_op jit(solution)/shard_map/ppermute | solution.py:206
  36.3 14.0 %collective-permute-start.4 = (bf16[1280,256]{1,0:T(8,128)(2,1)}, bf16[1280,256]{1,0:T(8,128)(2,1)}, u32[]{:S(2)}, u32[]{:S(2)}) collective-permute-start(bf16[1280,256]{1,0:T(8,128)(2,1)} %collective-permute-done.3.refs_5_), channel_id=1, source_target_pairs={{2,6},{3,1},{6,10},{7,3},{10,14},{11,7},{14,12},{15,11},{12,8},{13... | collective-permute-start | bytes 1966088 | tf_op jit(solution)/shard_map/ppermute | solution.py:206
  43.4 15.0 %collective-permute-start.8 = (bf16[1280,256]{1,0:T(8,128)(2,1)}, bf16[1280,256]{1,0:T(8,128)(2,1)S(1)}, u32[]{:S(2)}, u32[]{:S(2)}) collective-permute-start(bf16[1280,256]{1,0:T(8,128)(2,1)} %collective-permute-done.7.refs_4_), channel_id=1, source_target_pairs={{2,6},{3,1},{6,10},{7,3},{10,14},{11,7},{14,12},{15,11},{12,8},{13... | collective-permute-start | bytes 1966088 | tf_op jit(solution)/shard_map/ppermute | solution.py:206
  50.4 16.7 %collective-permute-start.5 = (bf16[1280,256]{1,0:T(8,128)(2,1)}, bf16[1280,256]{1,0:T(8,128)(2,1)S(1)}, u32[]{:S(2)}, u32[]{:S(2)}) collective-permute-start(bf16[1280,256]{1,0:T(8,128)(2,1)} %collective-permute-done.4.refs_5_), channel_id=1, source_target_pairs={{2,6},{3,1},{6,10},{7,3},{10,14},{11,7},{14,12},{15,11},{12,8},{13... | collective-permute-start | bytes 1966088 | tf_op jit(solution)/shard_map/ppermute | solution.py:206
  58.4 18.2 %collective-permute-start.13 = (bf16[1280,256]{1,0:T(8,128)(2,1)S(1)}, bf16[1280,256]{1,0:T(8,128)(2,1)S(1)}, u32[]{:S(2)}, u32[]{:S(2)}) collective-permute-start(bf16[1280,256]{1,0:T(8,128)(2,1)S(1)} %collective-permute-done.8.refs_4_), channel_id=1, source_target_pairs={{2,6},{3,1},{6,10},{7,3},{10,14},{11,7},{14,12},{15,11},{12,8},{13... | collective-permute-start | bytes 1966088 | tf_op jit(solution)/shard_map/ppermute | solution.py:206
  60.0 9.2 %collective-permute-start.11 = (bf16[512,256]{1,0:T(8,128)(2,1)S(1)}, bf16[512,256]{1,0:T(8,128)(2,1)S(1)}, u32[]{:S(2)}, u32[]{:S(2)}) collective-permute-start(bf16[512,256]{1,0:T(8,128)(2,1)S(1)} %collective-permute-done.2.refs_4_), channel_id=1, source_target_pairs={{6,2},{1,3},{10,6},{3,7},{14,10},{7,11},{12,14},{11,15},{8,12},{15... | collective-permute-start | bytes 786440 | tf_op jit(solution)/shard_map/ppermute | solution.py:230
  67.1 6.5 %copy-start.6 = (bf16[1280,256]{1,0:T(8,128)(2,1)}, bf16[1280,256]{1,0:T(8,128)(2,1)S(1)}, u32[]{:S(2)}) copy-start(bf16[1280,256]{1,0:T(8,128)(2,1)S(1)} %collective-permute-done.5.refs_5_) | copy-start | bytes 1966084
  69.3 11.9 %collective-permute-start.12 = (bf16[1280,256]{1,0:T(8,128)(2,1)S(1)}, bf16[1280,256]{1,0:T(8,128)(2,1)S(1)}, u32[]{:S(2)}, u32[]{:S(2)}) collective-permute-start(bf16[1280,256]{1,0:T(8,128)(2,1)S(1)} %collective-permute-done.5.refs_5_), channel_id=1, source_target_pairs={{2,6},{3,1},{6,10},{7,3},{10,14},{11,7},{14,12},{15,11},{12,8},{13... | collective-permute-start | bytes 1966088 | tf_op jit(solution)/shard_map/ppermute | solution.py:206
  76.6 12.1 %collective-permute-start.15 = (bf16[1280,256]{1,0:T(8,128)(2,1)S(1)}, bf16[1280,256]{1,0:T(8,128)(2,1)S(1)}, u32[]{:S(2)}, u32[]{:S(2)}) collective-permute-start(bf16[1280,256]{1,0:T(8,128)(2,1)S(1)} %collective-permute-done.13.refs_4_), channel_id=1, source_target_pairs={{2,6},{3,1},{6,10},{7,3},{10,14},{11,7},{14,12},{15,11},{12,8},{13... | collective-permute-start | bytes 1966088 | tf_op jit(solution)/shard_map/ppermute | solution.py:206
  81.2 4.8 %copy-start.5 = (bf16[1280,256]{1,0:T(8,128)(2,1)}, bf16[1280,256]{1,0:T(8,128)(2,1)S(1)}, u32[]{:S(2)}) copy-start(bf16[1280,256]{1,0:T(8,128)(2,1)S(1)} %collective-permute-done.12.refs_5_) | copy-start | bytes 1966084
  81.2 11.2 %collective-permute-start.14 = (bf16[768,256]{1,0:T(8,128)(2,1)S(1)}, bf16[768,256]{1,0:T(8,128)(2,1)S(1)}, u32[]{:S(2)}, u32[]{:S(2)}) collective-permute-start(bf16[768,256]{1,0:T(8,128)(2,1)S(1)} %slice.11), channel_id=1, source_target_pairs={{2,6},{3,1},{6,10},{7,3},{10,14},{11,7},{14,12},{15,11},{12,8},{13... | collective-permute-start | bytes 1179656 | tf_op jit(solution)/shard_map/ppermute | solution.py:206
  88.7 5.6 %copy-start.2 = (s32[2]{0:T(128)S(1)}, s32[2]{0:T(128)}, u32[]{:S(2)}) copy-start(s32[2]{0:T(128)} %refs_7_.1) | copy-start | bytes 28
  88.8 5.6 %copy-start.3 = (s32[2]{0:T(128)S(1)}, s32[2]{0:T(128)}, u32[]{:S(2)}) copy-start(s32[2]{0:T(128)} %refs_8_.1) | copy-start | bytes 28
  88.8 10.7 %collective-permute-start.17 = (bf16[1280,256]{1,0:T(8,128)(2,1)S(1)}, bf16[1280,256]{1,0:T(8,128)(2,1)S(1)}, u32[]{:S(2)}, u32[]{:S(2)}) collective-permute-start(bf16[1280,256]{1,0:T(8,128)(2,1)S(1)} %collective-permute-done.15.refs_2_), channel_id=1, source_target_pairs={{2,6},{3,1},{6,10},{7,3},{10,14},{11,7},{14,12},{15,11},{12,8},{13... | collective-permute-start | bytes 1966088 | tf_op jit(solution)/shard_map/ppermute | solution.py:206
  92.4 11.2 %collective-permute-start.16 = (bf16[768,256]{1,0:T(8,128)(2,1)S(1)}, bf16[768,256]{1,0:T(8,128)(2,1)S(1)}, u32[]{:S(2)}, u32[]{:S(2)}) collective-permute-start(bf16[768,256]{1,0:T(8,128)(2,1)S(1)} %collective-permute-done.14.refs_3_), channel_id=1, source_target_pairs={{2,6},{3,1},{6,10},{7,3},{10,14},{11,7},{14,12},{15,11},{12,8},{13... | collective-permute-start | bytes 1179656 | tf_op jit(solution)/shard_map/ppermute | solution.py:206
  96.4 2.4 %collective-permute-start.18 = (f32[328,256]{1,0:T(8,128)S(1)}, f32[328,256]{1,0:T(8,128)S(1)}, u32[]{:S(2)}, u32[]{:S(2)}) collective-permute-start(f32[328,256]{1,0:T(8,128)S(1)} %turned.1.own_ref), channel_id=1, source_target_pairs={{0,1},{1,0},{2,3},{3,2},{4,5},{5,4},{6,7},{7,6},{8,9},{9,8},{10,11... | collective-permute-start | bytes 1007624 | tf_op jit(solution)/shard_map/ppermute | solution.py:207

commit v23 on v22

--- a/solution.py
+++ b/solution.py
@@ -159,7 +159,8 @@
     query = lax.broadcasted_iota(jnp.int32, (columns, queries), 1)
     fold = (column == query).astype(F32)
     row = lax.broadcasted_iota(jnp.int32, table_ref.shape, 0)
-    owner = table_ref.shape[0] // per_device - 1 - lax.div(row, per_device)
+    count = table_ref.shape[0] // per_device
+    owner = lax.rem(count - lax.div(row, per_device), count)
     row = (owner * per_device + lax.rem(row, per_device)).astype(F32)
     contrib = (total_ref[...] + dot(window_ref[...], block_ref[...])) * inn_ref[:height]
     count = height // LEN
@@ -284,7 +285,7 @@
 
     queries = columns // RANK
     table = score_table([window, early, totals["out"], inn], slots, slots * devices, queries)
-    groups = [list(reversed(range(devices)))]
+    groups = [[0] + list(range(devices - 1, 0, -1))]
     got = lax.all_to_all(
         table.reshape(devices, slots, queries), "dp", 0, 0, axis_index_groups=groups, tiled=True
     )

time: 114 us -> 118 us (1.035)
  blocking collectives: 9.17 us -> 12.6 us
    all_to_all x1, blocking collectives: 9.17 us -> 12.6 us  [shards(): lax.all_to_all(table.reshape(devices, slots, queries), 'dp', 0, 0, axis_i...]
  transfers between devices with their start and end apart: 19 -> 19, of which waited for: 12 -> 12; matrix products, arithmetic and copies ran while one was open for 1% -> 1% of each run, Pallas kernels for 23% -> 22%
where the time goes in v23:
time: 118 us; the launch traced here: 117 us
  waiting for transfers between devices  49.4 us (42%)
  starting transfers between devices  27.4 us (23%)
  Pallas kernels  26.3 us (22%)
  blocking collectives  12.6 us (11%)
    ppermute x14, waiting for transfers between devices, shards(): send = lambda x: lax.ppermute(x, 'dp', pairs)  40.9 us
    pallas_call x11, Pallas kernels, call(): pl.pallas_call(kernel, grid_spec=pltpu.PrefetchScalarGridSpec(num_scalar_...  25.8 us
    ppermute x14, starting transfers between devices, shards(): send = lambda x: lax.ppermute(x, 'dp', pairs)  24.2 us
    all_to_all x1, blocking collectives, shards(): lax.all_to_all(table.reshape(devices, slots, queries), 'dp', 0, 0, axis_i...  12.6 us
    ppermute x1, waiting for transfers between devices, shards(): turned = lax.ppermute(turned, 'dp', [(j, i) for i, j in pairs])  6.32 us
  transfers between devices with their start and end apart: 19, of which 12 were waited for; matrix products, arithmetic and copies ran while one was open for 1% of the time, Pallas kernels for 22%

profile of v23, /device:TPU:0, one launch (start us, length us, event | category | flops | bytes accessed | tf_op | source)
XLA Modules:
  0.0 117.4 jit_solution(17720608141762805169)
XLA Ops:
  0.0 0.0 copy-start
  0.0 0.5 collective-permute-start.10
  0.5 2.6 %collective-permute-start.1 = (bf16[2048,256]{1,0:T(8,128)(2,1)}, bf16[2048,256]{1,0:T(8,128)(2,1)S(1)}, u32[]{:S(2)}, u32[]{:S(2)}) collective-permute-start(bf16[2048,256]{1,0:T(8,128)(2,1)} %refs_4_.1), channel_id=1, source_target_pairs={{2,6},{3,1},{6,10},{7,3},{10,14},{11,7},{14,12},{15,11},{12,8},{13... | collective-permute-start | bytes 3145736 | tf_op jit(solution)/shard_map/ppermute | solution.py:207
  3.0 0.2 collective-permute-start.9
  3.3 1.4 %collective-permute-start = (bf16[512,256]{1,0:T(8,128)(2,1)}, bf16[512,256]{1,0:T(8,128)(2,1)S(1)}, u32[]{:S(2)}, u32[]{:S(2)}) collective-permute-start(bf16[512,256]{1,0:T(8,128)(2,1)} %refs_5_.1), channel_id=1, source_target_pairs={{2,6},{3,1},{6,10},{7,3},{10,14},{11,7},{14,12},{15,11},{12,8},{13... | collective-permute-start | bytes 786440 | tf_op jit(solution)/shard_map/ppermute | solution.py:207
  4.6 11.5 %collective-permute-done.1 = bf16[2048,256]{1,0:T(8,128)(2,1)S(1)} collective-permute-done((bf16[2048,256]{1,0:T(8,128)(2,1)}, bf16[2048,256]{1,0:T(8,128)(2,1)S(1)}, u32[]{:S(2)}, u32[]{:S(2)}) %collective-permute-start.1) | collective-permute-done | bytes 1048608 | tf_op jit(solution)/shard_map/ppermute | solution.py:207
  16.1 2.0 %collective-permute-start.2 = (bf16[512,256]{1,0:T(8,128)(2,1)}, bf16[512,256]{1,0:T(8,128)(2,1)S(1)}, u32[]{:S(2)}, u32[]{:S(2)}) collective-permute-start(bf16[512,256]{1,0:T(8,128)(2,1)} %refs_5_.1), channel_id=1, source_target_pairs={{6,2},{1,3},{10,6},{3,7},{14,10},{7,11},{12,14},{11,15},{8,12},{15... | collective-permute-start | bytes 786440 | tf_op jit(solution)/shard_map/ppermute | solution.py:226
  18.1 0.1 collective-permute-start.6
  18.3 0.7 collective-permute-done
  19.0 6.3 %collective-permute-done.2.refs_4_ = bf16[512,256]{1,0:T(8,128)(2,1)S(1)} collective-permute-done((bf16[512,256]{1,0:T(8,128)(2,1)}, bf16[512,256]{1,0:T(8,128)(2,1)S(1)}, u32[]{:S(2)}, u32[]{:S(2)}) %collective-permute-start.2) | collective-permute-done | bytes 262176 | tf_op jit(solution)/shard_map/ppermute | solution.py:226
  25.3 0.0 copy-start.4
  25.3 2.2 %collective-permute-start.3 = (bf16[1280,256]{1,0:T(8,128)(2,1)S(1)}, bf16[1280,256]{1,0:T(8,128)(2,1)}, u32[]{:S(2)}, u32[]{:S(2)}) collective-permute-start(bf16[1280,256]{1,0:T(8,128)(2,1)S(1)} %pad_maximum_fusion.refs_5_), channel_id=1, source_target_pairs={{2,6},{3,1},{6,10},{7,3},{10,14},{11,7},{14,12},{15,11},{12,8},{13... | collective-permute-start | bytes 1966088 | tf_op jit(solution)/shard_map/ppermute | solution.py:207
  27.5 1.2 %collective-permute-done.6.refs_4_ = bf16[1280,256]{1,0:T(8,128)(2,1)S(1)} collective-permute-done((bf16[1280,256]{1,0:T(8,128)(2,1)S(1)}, bf16[1280,256]{1,0:T(8,128)(2,1)S(1)}, u32[]{:S(2)}, u32[]{:S(2)}) %collective-permute-start.6) | collective-permute-done | bytes 655392 | tf_op jit(solution)/shard_map/ppermute | solution.py:207
  28.8 1.9 %collective-permute-start.7 = (bf16[1280,256]{1,0:T(8,128)(2,1)S(1)}, bf16[1280,256]{1,0:T(8,128)(2,1)}, u32[]{:S(2)}, u32[]{:S(2)}) collective-permute-start(bf16[1280,256]{1,0:T(8,128)(2,1)S(1)} %collective-permute-done.6.refs_4_), channel_id=1, source_target_pairs={{2,6},{3,1},{6,10},{7,3},{10,14},{11,7},{14,12},{15,11},{12,8},{13... | collective-permute-start | bytes 1966088 | tf_op jit(solution)/shard_map/ppermute | solution.py:207
  30.7 5.7 %collective-permute-done.3.refs_5_ = bf16[1280,256]{1,0:T(8,128)(2,1)} collective-permute-done((bf16[1280,256]{1,0:T(8,128)(2,1)S(1)}, bf16[1280,256]{1,0:T(8,128)(2,1)}, u32[]{:S(2)}, u32[]{:S(2)}) %collective-permute-start.3) | collective-permute-done | bytes 655392 | tf_op jit(solution)/shard_map/ppermute | solution.py:207
  36.3 1.9 %collective-permute-start.4 = (bf16[1280,256]{1,0:T(8,128)(2,1)}, bf16[1280,256]{1,0:T(8,128)(2,1)}, u32[]{:S(2)}, u32[]{:S(2)}) collective-permute-start(bf16[1280,256]{1,0:T(8,128)(2,1)} %collective-permute-done.3.refs_5_), channel_id=1, source_target_pairs={{2,6},{3,1},{6,10},{7,3},{10,14},{11,7},{14,12},{15,11},{12,8},{13... | collective-permute-start | bytes 1966088 | tf_op jit(solution)/shard_map/ppermute | solution.py:207
  38.2 0.0 copy-done.4
  38.2 5.1 %collective-permute-done.7.refs_4_ = bf16[1280,256]{1,0:T(8,128)(2,1)} collective-permute-done((bf16[1280,256]{1,0:T(8,128)(2,1)S(1)}, bf16[1280,256]{1,0:T(8,128)(2,1)}, u32[]{:S(2)}, u32[]{:S(2)}) %collective-permute-start.7) | collective-permute-done | bytes 655392 | tf_op jit(solution)/shard_map/ppermute | solution.py:207
  43.4 1.9 %collective-permute-start.8 = (bf16[1280,256]{1,0:T(8,128)(2,1)}, bf16[1280,256]{1,0:T(8,128)(2,1)S(1)}, u32[]{:S(2)}, u32[]{:S(2)}) collective-permute-start(bf16[1280,256]{1,0:T(8,128)(2,1)} %collective-permute-done.7.refs_4_), channel_id=1, source_target_pairs={{2,6},{3,1},{6,10},{7,3},{10,14},{11,7},{14,12},{15,11},{12,8},{13... | collective-permute-start | bytes 1966088 | tf_op jit(solution)/shard_map/ppermute | solution.py:207
  45.3 5.1 %collective-permute-done.4.refs_5_ = bf16[1280,256]{1,0:T(8,128)(2,1)} collective-permute-done((bf16[1280,256]{1,0:T(8,128)(2,1)}, bf16[1280,256]{1,0:T(8,128)(2,1)}, u32[]{:S(2)}, u32[]{:S(2)}) %collective-permute-start.4) | collective-permute-done | bytes 655392 | tf_op jit(solution)/shard_map/ppermute | solution.py:207
  50.4 1.9 %collective-permute-start.5 = (bf16[1280,256]{1,0:T(8,128)(2,1)}, bf16[1280,256]{1,0:T(8,128)(2,1)S(1)}, u32[]{:S(2)}, u32[]{:S(2)}) collective-permute-start(bf16[1280,256]{1,0:T(8,128)(2,1)} %collective-permute-done.4.refs_5_), channel_id=1, source_target_pairs={{2,6},{3,1},{6,10},{7,3},{10,14},{11,7},{14,12},{15,11},{12,8},{13... | collective-permute-start | bytes 1966088 | tf_op jit(solution)/shard_map/ppermute | solution.py:207
  52.3 0.7 dynamic-slice_bitcast_fusion.order_ref
  53.0 0.0 collective-permute-done.9.refs_1_.refs_3_
  53.0 0.0 collective-permute-done.10.refs_3_.sib_ref.refs_1_
  53.0 0.0 copy-done
  53.0 0.0 copy-done.1
  53.0 2.6 %step.8 = (f32[320,256]{1,0:T(8,128)S(1)}, f32[320,256]{1,0:T(8,128)S(1)}) custom-call(s32[8]{0:T(128)S(1)} %dynamic-slice_bitcast_fusion.order_ref, bf16[160,8192]{1,0:T(8,128)(2,1)} %refs_2_.13, bf16[160,8192]{1,0:T(8,128)(2,1)} %collective-permute-done.9.refs_1_.refs_3_, bf16[160,32768]{1,0:T(8,128)(2,1)} %refs_0_.16, ...), custom_call_target="tpu_custom_call" | custom-call | flops 419430400 | bytes 3604480 | tf_op jit(solution)/shard_map/step/pallas_call | solution.py:59
  55.6 2.8 %step.9 = (f32[320,256]{1,0:T(8,128)S(1)}, f32[320,256]{1,0:T(8,128)S(1)}) custom-call(s32[8]{0:T(128)S(1)} %dynamic-slice_bitcast_fusion.order_ref, bf16[160,8192]{1,0:T(8,128)(2,1)} %refs_2_.13, bf16[160,8192]{1,0:T(8,128)(2,1)} %collective-permute-done.9.refs_1_.refs_3_, bf16[160,32768]{1,0:T(8,128)(2,1)} %refs_0_.16, ...), custom_call_target="tpu_custom_call" | custom-call | flops 419430400 | bytes 4259840 | tf_op jit(solution)/shard_map/step/pallas_call | solution.py:59
  58.4 0.0 collective-permute-done.8.refs_4_
  58.4 1.6 %collective-permute-start.13 = (bf16[1280,256]{1,0:T(8,128)(2,1)S(1)}, bf16[1280,256]{1,0:T(8,128)(2,1)S(1)}, u32[]{:S(2)}, u32[]{:S(2)}) collective-permute-start(bf16[1280,256]{1,0:T(8,128)(2,1)S(1)} %collective-permute-done.8.refs_4_), channel_id=1, source_target_pairs={{2,6},{3,1},{6,10},{7,3},{10,14},{11,7},{14,12},{15,11},{12,8},{13... | collective-permute-start | bytes 1966088 | tf_op jit(solution)/shard_map/ppermute | solution.py:207
  60.0 0.4 collective-permute-start.11
  60.5 6.6 %collective-permute-done.5.refs_5_ = bf16[1280,256]{1,0:T(8,128)(2,1)S(1)} collective-permute-done((bf16[1280,256]{1,0:T(8,128)(2,1)}, bf16[1280,256]{1,0:T(8,128)(2,1)S(1)}, u32[]{:S(2)}, u32[]{:S(2)}) %collective-permute-start.5) | collective-permute-done | bytes 655392 | tf_op jit(solution)/shard_map/ppermute | solution.py:207
  67.1 2.2 %collective-permute-done.11.refs_5_ = bf16[512,256]{1,0:T(8,128)(2,1)S(1)} collective-permute-done((bf16[512,256]{1,0:T(8,128)(2,1)S(1)}, bf16[512,256]{1,0:T(8,128)(2,1)S(1)}, u32[]{:S(2)}, u32[]{:S(2)}) %collective-permute-start.11) | collective-permute-done | bytes 262176 | tf_op jit(solution)/shard_map/ppermute | solution.py:231
  69.3 1.6 %collective-permute-start.12 = (bf16[1280,256]{1,0:T(8,128)(2,1)S(1)}, bf16[1280,256]{1,0:T(8,128)(2,1)S(1)}, u32[]{:S(2)}, u32[]{:S(2)}) collective-permute-start(bf16[1280,256]{1,0:T(8,128)(2,1)S(1)} %collective-permute-done.5.refs_5_), channel_id=1, source_target_pairs={{2,6},{3,1},{6,10},{7,3},{10,14},{11,7},{14,12},{15,11},{12,8},{13... | collective-permute-start | bytes 1966088 | tf_op jit(solution)/shard_map/ppermute | solution.py:207
  70.8 2.8 %step.10 = (f32[320,256]{1,0:T(8,128)S(1)}, f32[320,256]{1,0:T(8,128)S(1)}) custom-call(s32[8]{0:T(128)S(1)} %dynamic-slice_bitcast_fusion.order_ref, bf16[160,8192]{1,0:T(8,128)(2,1)} %refs_2_.13, bf16[160,8192]{1,0:T(8,128)(2,1)} %collective-permute-done.9.refs_1_.refs_3_, bf16[160,32768]{1,0:T(8,128)(2,1)} %refs_0_.16, ...), custom_call_target="tpu_custom_call" | custom-call | flops 419430400 | bytes 4259840 | tf_op jit(solution)/shard_map/step/pallas_call | solution.py:59
  73.6 0.0 copy-done.6
  73.6 3.0 %step.11 = (f32[320,256]{1,0:T(8,128)S(1)}, f32[320,256]{1,0:T(8,128)S(1)}) custom-call(s32[8]{0:T(128)S(1)} %dynamic-slice_bitcast_fusion.order_ref, bf16[160,8192]{1,0:T(8,128)(2,1)} %refs_2_.13, bf16[160,8192]{1,0:T(8,128)(2,1)} %collective-permute-done.9.refs_1_.refs_3_, bf16[160,32768]{1,0:T(8,128)(2,1)} %refs_0_.16, ...), custom_call_target="tpu_custom_call" | custom-call | flops 419430400 | bytes 4259840 | tf_op jit(solution)/shard_map/step/pallas_call | solution.py:59
  76.6 0.0 collective-permute-done.13.refs_4_
  76.6 1.7 %collective-permute-start.15 = (bf16[1280,256]{1,0:T(8,128)(2,1)S(1)}, bf16[1280,256]{1,0:T(8,128)(2,1)S(1)}, u32[]{:S(2)}, u32[]{:S(2)}) collective-permute-start(bf16[1280,256]{1,0:T(8,128)(2,1)S(1)} %collective-permute-done.13.refs_4_), channel_id=1, source_target_pairs={{2,6},{3,1},{6,10},{7,3},{10,14},{11,7},{14,12},{15,11},{12,8},{13... | collective-permute-start | bytes 1966088 | tf_op jit(solution)/shard_map/ppermute | solution.py:207
  78.3 2.9 %collective-permute-done.12.refs_5_ = bf16[1280,256]{1,0:T(8,128)(2,1)S(1)} collective-permute-done((bf16[1280,256]{1,0:T(8,128)(2,1)S(1)}, bf16[1280,256]{1,0:T(8,128)(2,1)S(1)}, u32[]{:S(2)}, u32[]{:S(2)}) %collective-permute-start.12) | collective-permute-done | bytes 655392 | tf_op jit(solution)/shard_map/ppermute | solution.py:207
  81.2 2.0 %collective-permute-start.14 = (bf16[768,256]{1,0:T(8,128)(2,1)S(1)}, bf16[768,256]{1,0:T(8,128)(2,1)S(1)}, u32[]{:S(2)}, u32[]{:S(2)}) collective-permute-start(bf16[768,256]{1,0:T(8,128)(2,1)S(1)} %slice.11), channel_id=1, source_target_pairs={{2,6},{3,1},{6,10},{7,3},{10,14},{11,7},{14,12},{15,11},{12,8},{13... | collective-permute-start | bytes 1179656 | tf_op jit(solution)/shard_map/ppermute | solution.py:207
  83.2 2.8 %step.12 = (f32[320,256]{1,0:T(8,128)S(1)}, f32[320,256]{1,0:T(8,128)S(1)}) custom-call(s32[8]{0:T(128)S(1)} %dynamic-slice_bitcast_fusion.order_ref, bf16[160,8192]{1,0:T(8,128)(2,1)} %refs_2_.13, bf16[160,8192]{1,0:T(8,128)(2,1)} %collective-permute-done.9.refs_1_.refs_3_, bf16[160,32768]{1,0:T(8,128)(2,1)} %refs_0_.16, ...), custom_call_target="tpu_custom_call" | custom-call | flops 419430400 | bytes 4259840 | tf_op jit(solution)/shard_map/step/pallas_call | solution.py:59
  85.9 0.0 copy-done.5
  85.9 2.8 %step.13 = (f32[320,256]{1,0:T(8,128)S(1)}, f32[320,256]{1,0:T(8,128)S(1)}) custom-call(s32[8]{0:T(128)S(1)} %dynamic-slice_bitcast_fusion.order_ref, bf16[160,8192]{1,0:T(8,128)(2,1)} %refs_2_.13, bf16[160,8192]{1,0:T(8,128)(2,1)} %collective-permute-done.9.refs_1_.refs_3_, bf16[160,32768]{1,0:T(8,128)(2,1)} %refs_0_.16, ...), custom_call_target="tpu_custom_call" | custom-call | flops 419430400 | bytes 4259840 | tf_op jit(solution)/shard_map/step/pallas_call | solution.py:59
  88.7 0.0 collective-permute-done.15.refs_2_
  88.7 0.0 copy-start.2
  88.8 0.0 copy-start.3
  88.8 1.6 %collective-permute-start.17 = (bf16[1280,256]{1,0:T(8,128)(2,1)S(1)}, bf16[1280,256]{1,0:T(8,128)(2,1)S(1)}, u32[]{:S(2)}, u32[]{:S(2)}) collective-permute-start(bf16[1280,256]{1,0:T(8,128)(2,1)S(1)} %collective-permute-done.15.refs_2_), channel_id=1, source_target_pairs={{2,6},{3,1},{6,10},{7,3},{10,14},{11,7},{14,12},{15,11},{12,8},{13... | collective-permute-start | bytes 1966088 | tf_op jit(solution)/shard_map/ppermute | solution.py:207
  90.4 1.9 %window.1.window_ref = bf16[320,768]{1,0:T(8,128)(2,1)S(1)} custom-call(s32[8]{0:T(128)S(1)} %dynamic-slice_bitcast_fusion.order_ref, bf16[160,32768]{1,0:T(8,128)(2,1)} %refs_0_.16, bf16[160,32768]{1,0:T(8,128)(2,1)} %collective-permute-done.10.refs_3_.sib_ref.refs_1_), custom_call_target="tpu_custom_call" | custom-call | bytes 1802240 | tf_op jit(solution)/shard_map/window/pallas_call | solution.py:59
  92.3 0.1 collective-permute-done.14.refs_3_
  92.4 1.9 %collective-permute-start.16 = (bf16[768,256]{1,0:T(8,128)(2,1)S(1)}, bf16[768,256]{1,0:T(8,128)(2,1)S(1)}, u32[]{:S(2)}, u32[]{:S(2)}) collective-permute-start(bf16[768,256]{1,0:T(8,128)(2,1)S(1)} %collective-permute-done.14.refs_3_), channel_id=1, source_target_pairs={{2,6},{3,1},{6,10},{7,3},{10,14},{11,7},{14,12},{15,11},{12,8},{13... | collective-permute-start | bytes 1179656 | tf_op jit(solution)/shard_map/ppermute | solution.py:207
  94.3 0.0 copy-done.2
  94.3 0.0 copy-done.3
  94.3 2.0 %turned.1.own_ref = f32[328,256]{1,0:T(8,128)S(1)} custom-call(s32[8]{0:T(128)S(1)} %dynamic-slice_bitcast_fusion.order_ref, bf16[160,8192]{1,0:T(8,128)(2,1)} %refs_2_.13, bf16[160,8192]{1,0:T(8,128)(2,1)} %collective-permute-done.9.refs_1_.refs_3_, bf16[160,8192]{1,0:T(8,128)(2,1)} %refs_2_.13, bf16[160,8192]{1,0:T(8,128)(2,1)} %collective-permute-done.9.refs_1_.refs_3_, ...), custom_call_target="tpu_custom_call" | custom-call | flops 167772160 | bytes 1843200 | tf_op jit(solution)/shard_map/turned/pallas_call | solution.py:59
  96.4 0.1 collective-permute-start.18
  96.5 2.4 %step.14.refs_3_ = f32[320,256]{1,0:T(8,128)S(1)} custom-call(s32[8]{0:T(128)S(1)} %dynamic-slice_bitcast_fusion.order_ref, bf16[160,32768]{1,0:T(8,128)(2,1)} %refs_0_.16, bf16[160,32768]{1,0:T(8,128)(2,1)} %collective-permute-done.10.refs_3_.sib_ref.refs_1_, bf16[1280,256]{1,0:T(8,128)(2,1)S(1)} %collective-permute-done.15.refs_2_, ...), custom_call_target="tpu_custom_call" | custom-call | flops 335544320 | bytes 3014656 | tf_op jit(solution)/shard_map/step/pallas_call | solution.py:59
  98.8 0.0 collective-permute-done.18.got_ref
  98.8 0.6 masked.1.inn_ref
  99.5 0.0 collective-permute-done.17.refs_2_
  99.5 2.2 %step.15.total_ref = f32[320,256]{1,0:T(8,128)S(1)} custom-call(s32[8]{0:T(128)S(1)} %dynamic-slice_bitcast_fusion.order_ref, bf16[160,32768]{1,0:T(8,128)(2,1)} %refs_0_.16, bf16[160,32768]{1,0:T(8,128)(2,1)} %collective-permute-done.10.refs_3_.sib_ref.refs_1_, bf16[1280,256]{1,0:T(8,128)(2,1)S(1)} %collective-permute-done.17.refs_2_, ...), custom_call_target="tpu_custom_call" | custom-call | flops 209715200 | bytes 2621440 | tf_op jit(solution)/shard_map/step/pallas_call | solution.py:59
  101.7 1.9 %collective-permute-done.16.block_ref = bf16[768,256]{1,0:T(8,128)(2,1)S(1)} collective-permute-done((bf16[768,256]{1,0:T(8,128)(2,1)S(1)}, bf16[768,256]{1,0:T(8,128)(2,1)S(1)}, u32[]{:S(2)}, u32[]{:S(2)}) %collective-permute-start.16) | collective-permute-done | bytes 393248 | tf_op jit(solution)/shard_map/ppermute | solution.py:207
  103.6 0.6 score.1
  104.2 12.6 %all_to_all.5 = f32[16,2,8]{2,1,0:T(2,128)S(1)} all-to-all(f32[16,2,8]{2,1,0:T(2,128)S(1)} %bitcast.3), channel_id=1, replica_groups={{0,15,14,13,12,11,10,9,8,7,6,5,4,3,2,1},{16,31,30,29,28,27,26,25,24,23,..., dimensions={0} | all-to-all | bytes 2048 | tf_op jit(solution)/shard_map/all_to_all | solution.py:289
  116.8 0.6 reduce_sum.9
  (7 shorter events, 0.1 us)
Async XLA Ops:
  0.0 53.0 %copy-start = (bf16[2048,256]{1,0:T(8,128)(2,1)S(1)}, bf16[2048,256]{1,0:T(8,128)(2,1)}, u32[]{:S(2)}) copy-start(bf16[2048,256]{1,0:T(8,128)(2,1)} %refs_4_.1) | copy-start | bytes 3145732
  0.0 53.0 %copy-start.1 = (bf16[512,256]{1,0:T(8,128)(2,1)S(1)}, bf16[512,256]{1,0:T(8,128)(2,1)}, u32[]{:S(2)}) copy-start(bf16[512,256]{1,0:T(8,128)(2,1)} %refs_5_.1) | copy-start | bytes 786436
  0.0 53.0 %collective-permute-start.10 = (bf16[160,32768]{1,0:T(8,128)(2,1)}, bf16[160,32768]{1,0:T(8,128)(2,1)}, u32[]{:S(2)}, u32[]{:S(2)}) collective-permute-start(bf16[160,32768]{1,0:T(8,128)(2,1)} %refs_0_.16), channel_id=1, source_target_pairs={{0,1},{1,0},{2,3},{3,2},{4,5},{5,4},{6,7},{7,6},{8,9},{9,8},{10,11... | collective-permute-start | bytes 31457288 | tf_op jit(solution)/shard_map/ppermute | solution.py:208
  0.5 15.6 %collective-permute-start.1 = (bf16[2048,256]{1,0:T(8,128)(2,1)}, bf16[2048,256]{1,0:T(8,128)(2,1)S(1)}, u32[]{:S(2)}, u32[]{:S(2)}) collective-permute-start(bf16[2048,256]{1,0:T(8,128)(2,1)} %refs_4_.1), channel_id=1, source_target_pairs={{2,6},{3,1},{6,10},{7,3},{10,14},{11,7},{14,12},{15,11},{12,8},{13... | collective-permute-start | bytes 3145736 | tf_op jit(solution)/shard_map/ppermute | solution.py:207
  3.0 49.9 %collective-permute-start.9 = (bf16[160,8192]{1,0:T(8,128)(2,1)}, bf16[160,8192]{1,0:T(8,128)(2,1)}, u32[]{:S(2)}, u32[]{:S(2)}) collective-permute-start(bf16[160,8192]{1,0:T(8,128)(2,1)} %refs_2_.13), channel_id=1, source_target_pairs={{0,1},{1,0},{2,3},{3,2},{4,5},{5,4},{6,7},{7,6},{8,9},{9,8},{10,11... | collective-permute-start | bytes 7864328 | tf_op jit(solution)/shard_map/ppermute | solution.py:208
  3.3 15.7 %collective-permute-start = (bf16[512,256]{1,0:T(8,128)(2,1)}, bf16[512,256]{1,0:T(8,128)(2,1)S(1)}, u32[]{:S(2)}, u32[]{:S(2)}) collective-permute-start(bf16[512,256]{1,0:T(8,128)(2,1)} %refs_5_.1), channel_id=1, source_target_pairs={{2,6},{3,1},{6,10},{7,3},{10,14},{11,7},{14,12},{15,11},{12,8},{13... | collective-permute-start | bytes 786440 | tf_op jit(solution)/shard_map/ppermute | solution.py:207
  16.1 9.2 %collective-permute-start.2 = (bf16[512,256]{1,0:T(8,128)(2,1)}, bf16[512,256]{1,0:T(8,128)(2,1)S(1)}, u32[]{:S(2)}, u32[]{:S(2)}) collective-permute-start(bf16[512,256]{1,0:T(8,128)(2,1)} %refs_5_.1), channel_id=1, source_target_pairs={{6,2},{1,3},{10,6},{3,7},{14,10},{7,11},{12,14},{11,15},{8,12},{15... | collective-permute-start | bytes 786440 | tf_op jit(solution)/shard_map/ppermute | solution.py:226
  18.1 10.6 %collective-permute-start.6 = (bf16[1280,256]{1,0:T(8,128)(2,1)S(1)}, bf16[1280,256]{1,0:T(8,128)(2,1)S(1)}, u32[]{:S(2)}, u32[]{:S(2)}) collective-permute-start(bf16[1280,256]{1,0:T(8,128)(2,1)S(1)} %slice.10.refs_4_), channel_id=1, source_target_pairs={{2,6},{3,1},{6,10},{7,3},{10,14},{11,7},{14,12},{15,11},{12,8},{13... | collective-permute-start | bytes 1966088 | tf_op jit(solution)/shard_map/ppermute | solution.py:207
  25.3 12.9 %copy-start.4 = (bf16[1280,256]{1,0:T(8,128)(2,1)}, bf16[1280,256]{1,0:T(8,128)(2,1)S(1)}, u32[]{:S(2)}) copy-start(bf16[1280,256]{1,0:T(8,128)(2,1)S(1)} %pad_maximum_fusion.refs_5_) | copy-start | bytes 1966084
  25.3 11.0 %collective-permute-start.3 = (bf16[1280,256]{1,0:T(8,128)(2,1)S(1)}, bf16[1280,256]{1,0:T(8,128)(2,1)}, u32[]{:S(2)}, u32[]{:S(2)}) collective-permute-start(bf16[1280,256]{1,0:T(8,128)(2,1)S(1)} %pad_maximum_fusion.refs_5_), channel_id=1, source_target_pairs={{2,6},{3,1},{6,10},{7,3},{10,14},{11,7},{14,12},{15,11},{12,8},{13... | collective-permute-start | bytes 1966088 | tf_op jit(solution)/shard_map/ppermute | solution.py:207
  28.8 14.6 %collective-permute-start.7 = (bf16[1280,256]{1,0:T(8,128)(2,1)S(1)}, bf16[1280,256]{1,0:T(8,128)(2,1)}, u32[]{:S(2)}, u32[]{:S(2)}) collective-permute-start(bf16[1280,256]{1,0:T(8,128)(2,1)S(1)} %collective-permute-done.6.refs_4_), channel_id=1, source_target_pairs={{2,6},{3,1},{6,10},{7,3},{10,14},{11,7},{14,12},{15,11},{12,8},{13... | collective-permute-start | bytes 1966088 | tf_op jit(solution)/shard_map/ppermute | solution.py:207
  36.3 14.0 %collective-permute-start.4 = (bf16[1280,256]{1,0:T(8,128)(2,1)}, bf16[1280,256]{1,0:T(8,128)(2,1)}, u32[]{:S(2)}, u32[]{:S(2)}) collective-permute-start(bf16[1280,256]{1,0:T(8,128)(2,1)} %collective-permute-done.3.refs_5_), channel_id=1, source_target_pairs={{2,6},{3,1},{6,10},{7,3},{10,14},{11,7},{14,12},{15,11},{12,8},{13... | collective-permute-start | bytes 1966088 | tf_op jit(solution)/shard_map/ppermute | solution.py:207
  43.4 15.0 %collective-permute-start.8 = (bf16[1280,256]{1,0:T(8,128)(2,1)}, bf16[1280,256]{1,0:T(8,128)(2,1)S(1)}, u32[]{:S(2)}, u32[]{:S(2)}) collective-permute-start(bf16[1280,256]{1,0:T(8,128)(2,1)} %collective-permute-done.7.refs_4_), channel_id=1, source_target_pairs={{2,6},{3,1},{6,10},{7,3},{10,14},{11,7},{14,12},{15,11},{12,8},{13... | collective-permute-start | bytes 1966088 | tf_op jit(solution)/shard_map/ppermute | solution.py:207
  50.4 16.7 %collective-permute-start.5 = (bf16[1280,256]{1,0:T(8,128)(2,1)}, bf16[1280,256]{1,0:T(8,128)(2,1)S(1)}, u32[]{:S(2)}, u32[]{:S(2)}) collective-permute-start(bf16[1280,256]{1,0:T(8,128)(2,1)} %collective-permute-done.4.refs_5_), channel_id=1, source_target_pairs={{2,6},{3,1},{6,10},{7,3},{10,14},{11,7},{14,12},{15,11},{12,8},{13... | collective-permute-start | bytes 1966088 | tf_op jit(solution)/shard_map/ppermute | solution.py:207
  58.4 18.2 %collective-permute-start.13 = (bf16[1280,256]{1,0:T(8,128)(2,1)S(1)}, bf16[1280,256]{1,0:T(8,128)(2,1)S(1)}, u32[]{:S(2)}, u32[]{:S(2)}) collective-permute-start(bf16[1280,256]{1,0:T(8,128)(2,1)S(1)} %collective-permute-done.8.refs_4_), channel_id=1, source_target_pairs={{2,6},{3,1},{6,10},{7,3},{10,14},{11,7},{14,12},{15,11},{12,8},{13... | collective-permute-start | bytes 1966088 | tf_op jit(solution)/shard_map/ppermute | solution.py:207
  60.0 9.2 %collective-permute-start.11 = (bf16[512,256]{1,0:T(8,128)(2,1)S(1)}, bf16[512,256]{1,0:T(8,128)(2,1)S(1)}, u32[]{:S(2)}, u32[]{:S(2)}) collective-permute-start(bf16[512,256]{1,0:T(8,128)(2,1)S(1)} %collective-permute-done.2.refs_4_), channel_id=1, source_target_pairs={{6,2},{1,3},{10,6},{3,7},{14,10},{7,11},{12,14},{11,15},{8,12},{15... | collective-permute-start | bytes 786440 | tf_op jit(solution)/shard_map/ppermute | solution.py:231
  67.1 6.5 %copy-start.6 = (bf16[1280,256]{1,0:T(8,128)(2,1)}, bf16[1280,256]{1,0:T(8,128)(2,1)S(1)}, u32[]{:S(2)}) copy-start(bf16[1280,256]{1,0:T(8,128)(2,1)S(1)} %collective-permute-done.5.refs_5_) | copy-start | bytes 1966084
  69.3 11.9 %collective-permute-start.12 = (bf16[1280,256]{1,0:T(8,128)(2,1)S(1)}, bf16[1280,256]{1,0:T(8,128)(2,1)S(1)}, u32[]{:S(2)}, u32[]{:S(2)}) collective-permute-start(bf16[1280,256]{1,0:T(8,128)(2,1)S(1)} %collective-permute-done.5.refs_5_), channel_id=1, source_target_pairs={{2,6},{3,1},{6,10},{7,3},{10,14},{11,7},{14,12},{15,11},{12,8},{13... | collective-permute-start | bytes 1966088 | tf_op jit(solution)/shard_map/ppermute | solution.py:207
  76.6 12.1 %collective-permute-start.15 = (bf16[1280,256]{1,0:T(8,128)(2,1)S(1)}, bf16[1280,256]{1,0:T(8,128)(2,1)S(1)}, u32[]{:S(2)}, u32[]{:S(2)}) collective-permute-start(bf16[1280,256]{1,0:T(8,128)(2,1)S(1)} %collective-permute-done.13.refs_4_), channel_id=1, source_target_pairs={{2,6},{3,1},{6,10},{7,3},{10,14},{11,7},{14,12},{15,11},{12,8},{13... | collective-permute-start | bytes 1966088 | tf_op jit(solution)/shard_map/ppermute | solution.py:207
  81.2 4.8 %copy-start.5 = (bf16[1280,256]{1,0:T(8,128)(2,1)}, bf16[1280,256]{1,0:T(8,128)(2,1)S(1)}, u32[]{:S(2)}) copy-start(bf16[1280,256]{1,0:T(8,128)(2,1)S(1)} %collective-permute-done.12.refs_5_) | copy-start | bytes 1966084
  81.2 11.2 %collective-permute-start.14 = (bf16[768,256]{1,0:T(8,128)(2,1)S(1)}, bf16[768,256]{1,0:T(8,128)(2,1)S(1)}, u32[]{:S(2)}, u32[]{:S(2)}) collective-permute-start(bf16[768,256]{1,0:T(8,128)(2,1)S(1)} %slice.11), channel_id=1, source_target_pairs={{2,6},{3,1},{6,10},{7,3},{10,14},{11,7},{14,12},{15,11},{12,8},{13... | collective-permute-start | bytes 1179656 | tf_op jit(solution)/shard_map/ppermute | solution.py:207
  88.7 5.6 %copy-start.2 = (s32[2]{0:T(128)S(1)}, s32[2]{0:T(128)}, u32[]{:S(2)}) copy-start(s32[2]{0:T(128)} %refs_7_.1) | copy-start | bytes 28
  88.8 5.6 %copy-start.3 = (s32[2]{0:T(128)S(1)}, s32[2]{0:T(128)}, u32[]{:S(2)}) copy-start(s32[2]{0:T(128)} %refs_8_.1) | copy-start | bytes 28
  88.8 10.7 %collective-permute-start.17 = (bf16[1280,256]{1,0:T(8,128)(2,1)S(1)}, bf16[1280,256]{1,0:T(8,128)(2,1)S(1)}, u32[]{:S(2)}, u32[]{:S(2)}) collective-permute-start(bf16[1280,256]{1,0:T(8,128)(2,1)S(1)} %collective-permute-done.15.refs_2_), channel_id=1, source_target_pairs={{2,6},{3,1},{6,10},{7,3},{10,14},{11,7},{14,12},{15,11},{12,8},{13... | collective-permute-start | bytes 1966088 | tf_op jit(solution)/shard_map/ppermute | solution.py:207
  92.4 11.2 %collective-permute-start.16 = (bf16[768,256]{1,0:T(8,128)(2,1)S(1)}, bf16[768,256]{1,0:T(8,128)(2,1)S(1)}, u32[]{:S(2)}, u32[]{:S(2)}) collective-permute-start(bf16[768,256]{1,0:T(8,128)(2,1)S(1)} %collective-permute-done.14.refs_3_), channel_id=1, source_target_pairs={{2,6},{3,1},{6,10},{7,3},{10,14},{11,7},{14,12},{15,11},{12,8},{13... | collective-permute-start | bytes 1179656 | tf_op jit(solution)/shard_map/ppermute | solution.py:207
  96.4 2.4 %collective-permute-start.18 = (f32[328,256]{1,0:T(8,128)S(1)}, f32[328,256]{1,0:T(8,128)S(1)}, u32[]{:S(2)}, u32[]{:S(2)}) collective-permute-start(f32[328,256]{1,0:T(8,128)S(1)} %turned.1.own_ref), channel_id=1, source_target_pairs={{0,1},{1,0},{2,3},{3,2},{4,5},{5,4},{6,7},{7,6},{8,9},{9,8},{10,11... | collective-permute-start | bytes 1007624 | tf_op jit(solution)/shard_map/ppermute | solution.py:208

commit v24 on v23

--- a/solution.py
+++ b/solution.py
@@ -160,7 +160,7 @@
     fold = (column == query).astype(F32)
     row = lax.broadcasted_iota(jnp.int32, table_ref.shape, 0)
     count = table_ref.shape[0] // per_device
-    owner = lax.rem(count - lax.div(row, per_device), count)
+    owner = lax.rem(count + 3 * count // 4 - 1 - lax.div(row, per_device), count)
     row = (owner * per_device + lax.rem(row, per_device)).astype(F32)
     contrib = (total_ref[...] + dot(window_ref[...], block_ref[...])) * inn_ref[:height]
     count = height // LEN
@@ -285,7 +285,7 @@
 
     queries = columns // RANK
     table = score_table([window, early, totals["out"], inn], slots, slots * devices, queries)
-    groups = [[0] + list(range(devices - 1, 0, -1))]
+    groups = [[(3 * devices // 4 - 1 - k) % devices for k in range(devices)]]
     got = lax.all_to_all(
         table.reshape(devices, slots, queries), "dp", 0, 0, axis_index_groups=groups, tiled=True
     )

time: 118 us -> 115 us (0.975)
  blocking collectives: 12.6 us -> 9.64 us
    all_to_all x1, blocking collectives: 12.6 us -> 9.64 us  [shards(): lax.all_to_all(table.reshape(devices, slots, queries), 'dp', 0, 0, axis_i...]
  transfers between devices with their start and end apart: 19 -> 19, of which waited for: 12 -> 12; matrix products, arithmetic and copies ran while one was open for 1% -> 1% of each run, Pallas kernels for 22% -> 23%
where the time goes in v24:
time: 115 us; the launch traced here: 114 us
  waiting for transfers between devices  49.4 us (43%)
  starting transfers between devices  27.4 us (24%)
  Pallas kernels  26.3 us (23%)
  blocking collectives  9.64 us (8%)
    ppermute x14, waiting for transfers between devices, shards(): send = lambda x: lax.ppermute(x, 'dp', pairs)  40.9 us
    pallas_call x11, Pallas kernels, call(): pl.pallas_call(kernel, grid_spec=pltpu.PrefetchScalarGridSpec(num_scalar_...  25.8 us
    ppermute x14, starting transfers between devices, shards(): send = lambda x: lax.ppermute(x, 'dp', pairs)  24.2 us
    all_to_all x1, blocking collectives, shards(): lax.all_to_all(table.reshape(devices, slots, queries), 'dp', 0, 0, axis_i...  9.64 us
    ppermute x1, waiting for transfers between devices, shards(): turned = lax.ppermute(turned, 'dp', [(j, i) for i, j in pairs])  6.32 us
  transfers between devices with their start and end apart: 19, of which 12 were waited for; matrix products, arithmetic and copies ran while one was open for 1% of the time, Pallas kernels for 23%

profile of v24, /device:TPU:0, one launch (start us, length us, event | category | flops | bytes accessed | tf_op | source)
XLA Modules:
  0.0 114.4 jit_solution(6016909566322327732)
XLA Ops:
  0.0 0.0 copy-start
  0.0 0.5 collective-permute-start.10
  0.5 2.6 %collective-permute-start.1 = (bf16[2048,256]{1,0:T(8,128)(2,1)}, bf16[2048,256]{1,0:T(8,128)(2,1)S(1)}, u32[]{:S(2)}, u32[]{:S(2)}) collective-permute-start(bf16[2048,256]{1,0:T(8,128)(2,1)} %refs_4_.1), channel_id=1, source_target_pairs={{2,6},{3,1},{6,10},{7,3},{10,14},{11,7},{14,12},{15,11},{12,8},{13... | collective-permute-start | bytes 3145736 | tf_op jit(solution)/shard_map/ppermute | solution.py:207
  3.0 0.2 collective-permute-start.9
  3.3 1.4 %collective-permute-start = (bf16[512,256]{1,0:T(8,128)(2,1)}, bf16[512,256]{1,0:T(8,128)(2,1)S(1)}, u32[]{:S(2)}, u32[]{:S(2)}) collective-permute-start(bf16[512,256]{1,0:T(8,128)(2,1)} %refs_5_.1), channel_id=1, source_target_pairs={{2,6},{3,1},{6,10},{7,3},{10,14},{11,7},{14,12},{15,11},{12,8},{13... | collective-permute-start | bytes 786440 | tf_op jit(solution)/shard_map/ppermute | solution.py:207
  4.6 11.5 %collective-permute-done.1 = bf16[2048,256]{1,0:T(8,128)(2,1)S(1)} collective-permute-done((bf16[2048,256]{1,0:T(8,128)(2,1)}, bf16[2048,256]{1,0:T(8,128)(2,1)S(1)}, u32[]{:S(2)}, u32[]{:S(2)}) %collective-permute-start.1) | collective-permute-done | bytes 1048608 | tf_op jit(solution)/shard_map/ppermute | solution.py:207
  16.1 2.0 %collective-permute-start.2 = (bf16[512,256]{1,0:T(8,128)(2,1)}, bf16[512,256]{1,0:T(8,128)(2,1)S(1)}, u32[]{:S(2)}, u32[]{:S(2)}) collective-permute-start(bf16[512,256]{1,0:T(8,128)(2,1)} %refs_5_.1), channel_id=1, source_target_pairs={{6,2},{1,3},{10,6},{3,7},{14,10},{7,11},{12,14},{11,15},{8,12},{15... | collective-permute-start | bytes 786440 | tf_op jit(solution)/shard_map/ppermute | solution.py:226
  18.1 0.1 collective-permute-start.6
  18.3 0.7 collective-permute-done
  19.0 6.3 %collective-permute-done.2.refs_4_ = bf16[512,256]{1,0:T(8,128)(2,1)S(1)} collective-permute-done((bf16[512,256]{1,0:T(8,128)(2,1)}, bf16[512,256]{1,0:T(8,128)(2,1)S(1)}, u32[]{:S(2)}, u32[]{:S(2)}) %collective-permute-start.2) | collective-permute-done | bytes 262176 | tf_op jit(solution)/shard_map/ppermute | solution.py:226
  25.3 0.0 copy-start.4
  25.3 2.2 %collective-permute-start.3 = (bf16[1280,256]{1,0:T(8,128)(2,1)S(1)}, bf16[1280,256]{1,0:T(8,128)(2,1)}, u32[]{:S(2)}, u32[]{:S(2)}) collective-permute-start(bf16[1280,256]{1,0:T(8,128)(2,1)S(1)} %pad_maximum_fusion.refs_5_), channel_id=1, source_target_pairs={{2,6},{3,1},{6,10},{7,3},{10,14},{11,7},{14,12},{15,11},{12,8},{13... | collective-permute-start | bytes 1966088 | tf_op jit(solution)/shard_map/ppermute | solution.py:207
  27.5 1.2 %collective-permute-done.6.refs_4_ = bf16[1280,256]{1,0:T(8,128)(2,1)S(1)} collective-permute-done((bf16[1280,256]{1,0:T(8,128)(2,1)S(1)}, bf16[1280,256]{1,0:T(8,128)(2,1)S(1)}, u32[]{:S(2)}, u32[]{:S(2)}) %collective-permute-start.6) | collective-permute-done | bytes 655392 | tf_op jit(solution)/shard_map/ppermute | solution.py:207
  28.8 1.9 %collective-permute-start.7 = (bf16[1280,256]{1,0:T(8,128)(2,1)S(1)}, bf16[1280,256]{1,0:T(8,128)(2,1)}, u32[]{:S(2)}, u32[]{:S(2)}) collective-permute-start(bf16[1280,256]{1,0:T(8,128)(2,1)S(1)} %collective-permute-done.6.refs_4_), channel_id=1, source_target_pairs={{2,6},{3,1},{6,10},{7,3},{10,14},{11,7},{14,12},{15,11},{12,8},{13... | collective-permute-start | bytes 1966088 | tf_op jit(solution)/shard_map/ppermute | solution.py:207
  30.7 5.7 %collective-permute-done.3.refs_5_ = bf16[1280,256]{1,0:T(8,128)(2,1)} collective-permute-done((bf16[1280,256]{1,0:T(8,128)(2,1)S(1)}, bf16[1280,256]{1,0:T(8,128)(2,1)}, u32[]{:S(2)}, u32[]{:S(2)}) %collective-permute-start.3) | collective-permute-done | bytes 655392 | tf_op jit(solution)/shard_map/ppermute | solution.py:207
  36.3 1.9 %collective-permute-start.4 = (bf16[1280,256]{1,0:T(8,128)(2,1)}, bf16[1280,256]{1,0:T(8,128)(2,1)}, u32[]{:S(2)}, u32[]{:S(2)}) collective-permute-start(bf16[1280,256]{1,0:T(8,128)(2,1)} %collective-permute-done.3.refs_5_), channel_id=1, source_target_pairs={{2,6},{3,1},{6,10},{7,3},{10,14},{11,7},{14,12},{15,11},{12,8},{13... | collective-permute-start | bytes 1966088 | tf_op jit(solution)/shard_map/ppermute | solution.py:207
  38.2 0.0 copy-done.4
  38.2 5.1 %collective-permute-done.7.refs_4_ = bf16[1280,256]{1,0:T(8,128)(2,1)} collective-permute-done((bf16[1280,256]{1,0:T(8,128)(2,1)S(1)}, bf16[1280,256]{1,0:T(8,128)(2,1)}, u32[]{:S(2)}, u32[]{:S(2)}) %collective-permute-start.7) | collective-permute-done | bytes 655392 | tf_op jit(solution)/shard_map/ppermute | solution.py:207
  43.4 1.9 %collective-permute-start.8 = (bf16[1280,256]{1,0:T(8,128)(2,1)}, bf16[1280,256]{1,0:T(8,128)(2,1)S(1)}, u32[]{:S(2)}, u32[]{:S(2)}) collective-permute-start(bf16[1280,256]{1,0:T(8,128)(2,1)} %collective-permute-done.7.refs_4_), channel_id=1, source_target_pairs={{2,6},{3,1},{6,10},{7,3},{10,14},{11,7},{14,12},{15,11},{12,8},{13... | collective-permute-start | bytes 1966088 | tf_op jit(solution)/shard_map/ppermute | solution.py:207
  45.3 5.1 %collective-permute-done.4.refs_5_ = bf16[1280,256]{1,0:T(8,128)(2,1)} collective-permute-done((bf16[1280,256]{1,0:T(8,128)(2,1)}, bf16[1280,256]{1,0:T(8,128)(2,1)}, u32[]{:S(2)}, u32[]{:S(2)}) %collective-permute-start.4) | collective-permute-done | bytes 655392 | tf_op jit(solution)/shard_map/ppermute | solution.py:207
  50.4 1.9 %collective-permute-start.5 = (bf16[1280,256]{1,0:T(8,128)(2,1)}, bf16[1280,256]{1,0:T(8,128)(2,1)S(1)}, u32[]{:S(2)}, u32[]{:S(2)}) collective-permute-start(bf16[1280,256]{1,0:T(8,128)(2,1)} %collective-permute-done.4.refs_5_), channel_id=1, source_target_pairs={{2,6},{3,1},{6,10},{7,3},{10,14},{11,7},{14,12},{15,11},{12,8},{13... | collective-permute-start | bytes 1966088 | tf_op jit(solution)/shard_map/ppermute | solution.py:207
  52.3 0.7 dynamic-slice_bitcast_fusion.order_ref
  53.0 0.0 collective-permute-done.9.refs_1_.refs_3_
  53.0 0.0 collective-permute-done.10.refs_3_.sib_ref.refs_1_
  53.0 0.0 copy-done
  53.0 0.0 copy-done.1
  53.0 2.6 %step.8 = (f32[320,256]{1,0:T(8,128)S(1)}, f32[320,256]{1,0:T(8,128)S(1)}) custom-call(s32[8]{0:T(128)S(1)} %dynamic-slice_bitcast_fusion.order_ref, bf16[160,8192]{1,0:T(8,128)(2,1)} %refs_2_.13, bf16[160,8192]{1,0:T(8,128)(2,1)} %collective-permute-done.9.refs_1_.refs_3_, bf16[160,32768]{1,0:T(8,128)(2,1)} %refs_0_.16, ...), custom_call_target="tpu_custom_call" | custom-call | flops 419430400 | bytes 3604480 | tf_op jit(solution)/shard_map/step/pallas_call | solution.py:59
  55.6 2.8 %step.9 = (f32[320,256]{1,0:T(8,128)S(1)}, f32[320,256]{1,0:T(8,128)S(1)}) custom-call(s32[8]{0:T(128)S(1)} %dynamic-slice_bitcast_fusion.order_ref, bf16[160,8192]{1,0:T(8,128)(2,1)} %refs_2_.13, bf16[160,8192]{1,0:T(8,128)(2,1)} %collective-permute-done.9.refs_1_.refs_3_, bf16[160,32768]{1,0:T(8,128)(2,1)} %refs_0_.16, ...), custom_call_target="tpu_custom_call" | custom-call | flops 419430400 | bytes 4259840 | tf_op jit(solution)/shard_map/step/pallas_call | solution.py:59
  58.4 0.0 collective-permute-done.8.refs_4_
  58.4 1.6 %collective-permute-start.13 = (bf16[1280,256]{1,0:T(8,128)(2,1)S(1)}, bf16[1280,256]{1,0:T(8,128)(2,1)S(1)}, u32[]{:S(2)}, u32[]{:S(2)}) collective-permute-start(bf16[1280,256]{1,0:T(8,128)(2,1)S(1)} %collective-permute-done.8.refs_4_), channel_id=1, source_target_pairs={{2,6},{3,1},{6,10},{7,3},{10,14},{11,7},{14,12},{15,11},{12,8},{13... | collective-permute-start | bytes 1966088 | tf_op jit(solution)/shard_map/ppermute | solution.py:207
  60.0 0.4 collective-permute-start.11
  60.5 6.6 %collective-permute-done.5.refs_5_ = bf16[1280,256]{1,0:T(8,128)(2,1)S(1)} collective-permute-done((bf16[1280,256]{1,0:T(8,128)(2,1)}, bf16[1280,256]{1,0:T(8,128)(2,1)S(1)}, u32[]{:S(2)}, u32[]{:S(2)}) %collective-permute-start.5) | collective-permute-done | bytes 655392 | tf_op jit(solution)/shard_map/ppermute | solution.py:207
  67.1 2.2 %collective-permute-done.11.refs_5_ = bf16[512,256]{1,0:T(8,128)(2,1)S(1)} collective-permute-done((bf16[512,256]{1,0:T(8,128)(2,1)S(1)}, bf16[512,256]{1,0:T(8,128)(2,1)S(1)}, u32[]{:S(2)}, u32[]{:S(2)}) %collective-permute-start.11) | collective-permute-done | bytes 262176 | tf_op jit(solution)/shard_map/ppermute | solution.py:231
  69.3 1.6 %collective-permute-start.12 = (bf16[1280,256]{1,0:T(8,128)(2,1)S(1)}, bf16[1280,256]{1,0:T(8,128)(2,1)S(1)}, u32[]{:S(2)}, u32[]{:S(2)}) collective-permute-start(bf16[1280,256]{1,0:T(8,128)(2,1)S(1)} %collective-permute-done.5.refs_5_), channel_id=1, source_target_pairs={{2,6},{3,1},{6,10},{7,3},{10,14},{11,7},{14,12},{15,11},{12,8},{13... | collective-permute-start | bytes 1966088 | tf_op jit(solution)/shard_map/ppermute | solution.py:207
  70.8 2.8 %step.10 = (f32[320,256]{1,0:T(8,128)S(1)}, f32[320,256]{1,0:T(8,128)S(1)}) custom-call(s32[8]{0:T(128)S(1)} %dynamic-slice_bitcast_fusion.order_ref, bf16[160,8192]{1,0:T(8,128)(2,1)} %refs_2_.13, bf16[160,8192]{1,0:T(8,128)(2,1)} %collective-permute-done.9.refs_1_.refs_3_, bf16[160,32768]{1,0:T(8,128)(2,1)} %refs_0_.16, ...), custom_call_target="tpu_custom_call" | custom-call | flops 419430400 | bytes 4259840 | tf_op jit(solution)/shard_map/step/pallas_call | solution.py:59
  73.6 0.0 copy-done.6
  73.6 3.0 %step.11 = (f32[320,256]{1,0:T(8,128)S(1)}, f32[320,256]{1,0:T(8,128)S(1)}) custom-call(s32[8]{0:T(128)S(1)} %dynamic-slice_bitcast_fusion.order_ref, bf16[160,8192]{1,0:T(8,128)(2,1)} %refs_2_.13, bf16[160,8192]{1,0:T(8,128)(2,1)} %collective-permute-done.9.refs_1_.refs_3_, bf16[160,32768]{1,0:T(8,128)(2,1)} %refs_0_.16, ...), custom_call_target="tpu_custom_call" | custom-call | flops 419430400 | bytes 4259840 | tf_op jit(solution)/shard_map/step/pallas_call | solution.py:59
  76.6 0.0 collective-permute-done.13.refs_4_
  76.6 1.7 %collective-permute-start.15 = (bf16[1280,256]{1,0:T(8,128)(2,1)S(1)}, bf16[1280,256]{1,0:T(8,128)(2,1)S(1)}, u32[]{:S(2)}, u32[]{:S(2)}) collective-permute-start(bf16[1280,256]{1,0:T(8,128)(2,1)S(1)} %collective-permute-done.13.refs_4_), channel_id=1, source_target_pairs={{2,6},{3,1},{6,10},{7,3},{10,14},{11,7},{14,12},{15,11},{12,8},{13... | collective-permute-start | bytes 1966088 | tf_op jit(solution)/shard_map/ppermute | solution.py:207
  78.3 2.9 %collective-permute-done.12.refs_5_ = bf16[1280,256]{1,0:T(8,128)(2,1)S(1)} collective-permute-done((bf16[1280,256]{1,0:T(8,128)(2,1)S(1)}, bf16[1280,256]{1,0:T(8,128)(2,1)S(1)}, u32[]{:S(2)}, u32[]{:S(2)}) %collective-permute-start.12) | collective-permute-done | bytes 655392 | tf_op jit(solution)/shard_map/ppermute | solution.py:207
  81.2 2.0 %collective-permute-start.14 = (bf16[768,256]{1,0:T(8,128)(2,1)S(1)}, bf16[768,256]{1,0:T(8,128)(2,1)S(1)}, u32[]{:S(2)}, u32[]{:S(2)}) collective-permute-start(bf16[768,256]{1,0:T(8,128)(2,1)S(1)} %slice.11), channel_id=1, source_target_pairs={{2,6},{3,1},{6,10},{7,3},{10,14},{11,7},{14,12},{15,11},{12,8},{13... | collective-permute-start | bytes 1179656 | tf_op jit(solution)/shard_map/ppermute | solution.py:207
  83.2 2.8 %step.12 = (f32[320,256]{1,0:T(8,128)S(1)}, f32[320,256]{1,0:T(8,128)S(1)}) custom-call(s32[8]{0:T(128)S(1)} %dynamic-slice_bitcast_fusion.order_ref, bf16[160,8192]{1,0:T(8,128)(2,1)} %refs_2_.13, bf16[160,8192]{1,0:T(8,128)(2,1)} %collective-permute-done.9.refs_1_.refs_3_, bf16[160,32768]{1,0:T(8,128)(2,1)} %refs_0_.16, ...), custom_call_target="tpu_custom_call" | custom-call | flops 419430400 | bytes 4259840 | tf_op jit(solution)/shard_map/step/pallas_call | solution.py:59
  85.9 0.0 copy-done.5
  85.9 2.8 %step.13 = (f32[320,256]{1,0:T(8,128)S(1)}, f32[320,256]{1,0:T(8,128)S(1)}) custom-call(s32[8]{0:T(128)S(1)} %dynamic-slice_bitcast_fusion.order_ref, bf16[160,8192]{1,0:T(8,128)(2,1)} %refs_2_.13, bf16[160,8192]{1,0:T(8,128)(2,1)} %collective-permute-done.9.refs_1_.refs_3_, bf16[160,32768]{1,0:T(8,128)(2,1)} %refs_0_.16, ...), custom_call_target="tpu_custom_call" | custom-call | flops 419430400 | bytes 4259840 | tf_op jit(solution)/shard_map/step/pallas_call | solution.py:59
  88.7 0.0 collective-permute-done.15.refs_2_
  88.7 0.0 copy-start.2
  88.8 0.0 copy-start.3
  88.8 1.6 %collective-permute-start.17 = (bf16[1280,256]{1,0:T(8,128)(2,1)S(1)}, bf16[1280,256]{1,0:T(8,128)(2,1)S(1)}, u32[]{:S(2)}, u32[]{:S(2)}) collective-permute-start(bf16[1280,256]{1,0:T(8,128)(2,1)S(1)} %collective-permute-done.15.refs_2_), channel_id=1, source_target_pairs={{2,6},{3,1},{6,10},{7,3},{10,14},{11,7},{14,12},{15,11},{12,8},{13... | collective-permute-start | bytes 1966088 | tf_op jit(solution)/shard_map/ppermute | solution.py:207
  90.4 1.9 %window.1.window_ref = bf16[320,768]{1,0:T(8,128)(2,1)S(1)} custom-call(s32[8]{0:T(128)S(1)} %dynamic-slice_bitcast_fusion.order_ref, bf16[160,32768]{1,0:T(8,128)(2,1)} %refs_0_.16, bf16[160,32768]{1,0:T(8,128)(2,1)} %collective-permute-done.10.refs_3_.sib_ref.refs_1_), custom_call_target="tpu_custom_call" | custom-call | bytes 1802240 | tf_op jit(solution)/shard_map/window/pallas_call | solution.py:59
  92.3 0.1 collective-permute-done.14.refs_3_
  92.4 1.9 %collective-permute-start.16 = (bf16[768,256]{1,0:T(8,128)(2,1)S(1)}, bf16[768,256]{1,0:T(8,128)(2,1)S(1)}, u32[]{:S(2)}, u32[]{:S(2)}) collective-permute-start(bf16[768,256]{1,0:T(8,128)(2,1)S(1)} %collective-permute-done.14.refs_3_), channel_id=1, source_target_pairs={{2,6},{3,1},{6,10},{7,3},{10,14},{11,7},{14,12},{15,11},{12,8},{13... | collective-permute-start | bytes 1179656 | tf_op jit(solution)/shard_map/ppermute | solution.py:207
  94.3 0.0 copy-done.2
  94.3 0.0 copy-done.3
  94.3 2.0 %turned.1.own_ref = f32[328,256]{1,0:T(8,128)S(1)} custom-call(s32[8]{0:T(128)S(1)} %dynamic-slice_bitcast_fusion.order_ref, bf16[160,8192]{1,0:T(8,128)(2,1)} %refs_2_.13, bf16[160,8192]{1,0:T(8,128)(2,1)} %collective-permute-done.9.refs_1_.refs_3_, bf16[160,8192]{1,0:T(8,128)(2,1)} %refs_2_.13, bf16[160,8192]{1,0:T(8,128)(2,1)} %collective-permute-done.9.refs_1_.refs_3_, ...), custom_call_target="tpu_custom_call" | custom-call | flops 167772160 | bytes 1843200 | tf_op jit(solution)/shard_map/turned/pallas_call | solution.py:59
  96.4 0.1 collective-permute-start.18
  96.5 2.4 %step.14.refs_3_ = f32[320,256]{1,0:T(8,128)S(1)} custom-call(s32[8]{0:T(128)S(1)} %dynamic-slice_bitcast_fusion.order_ref, bf16[160,32768]{1,0:T(8,128)(2,1)} %refs_0_.16, bf16[160,32768]{1,0:T(8,128)(2,1)} %collective-permute-done.10.refs_3_.sib_ref.refs_1_, bf16[1280,256]{1,0:T(8,128)(2,1)S(1)} %collective-permute-done.15.refs_2_, ...), custom_call_target="tpu_custom_call" | custom-call | flops 335544320 | bytes 3014656 | tf_op jit(solution)/shard_map/step/pallas_call | solution.py:59
  98.8 0.0 collective-permute-done.18.got_ref
  98.8 0.6 masked.1.inn_ref
  99.5 0.0 collective-permute-done.17.refs_2_
  99.5 2.2 %step.15.total_ref = f32[320,256]{1,0:T(8,128)S(1)} custom-call(s32[8]{0:T(128)S(1)} %dynamic-slice_bitcast_fusion.order_ref, bf16[160,32768]{1,0:T(8,128)(2,1)} %refs_0_.16, bf16[160,32768]{1,0:T(8,128)(2,1)} %collective-permute-done.10.refs_3_.sib_ref.refs_1_, bf16[1280,256]{1,0:T(8,128)(2,1)S(1)} %collective-permute-done.17.refs_2_, ...), custom_call_target="tpu_custom_call" | custom-call | flops 209715200 | bytes 2621440 | tf_op jit(solution)/shard_map/step/pallas_call | solution.py:59
  101.7 1.9 %collective-permute-done.16.block_ref = bf16[768,256]{1,0:T(8,128)(2,1)S(1)} collective-permute-done((bf16[768,256]{1,0:T(8,128)(2,1)S(1)}, bf16[768,256]{1,0:T(8,128)(2,1)S(1)}, u32[]{:S(2)}, u32[]{:S(2)}) %collective-permute-start.16) | collective-permute-done | bytes 393248 | tf_op jit(solution)/shard_map/ppermute | solution.py:207
  103.6 0.6 score.1
  104.2 9.6 %all_to_all.5 = f32[16,2,8]{2,1,0:T(2,128)S(1)} all-to-all(f32[16,2,8]{2,1,0:T(2,128)S(1)} %bitcast.3), channel_id=1, replica_groups={{11,10,9,8,7,6,5,4,3,2,1,0,15,14,13,12},{27,26,25,24,23,22,21,20,19,18,..., dimensions={0} | all-to-all | bytes 2048 | tf_op jit(solution)/shard_map/all_to_all | solution.py:289
  113.8 0.6 reduce_sum.9
  (7 shorter events, 0.1 us)
Async XLA Ops:
  0.0 53.0 %copy-start = (bf16[2048,256]{1,0:T(8,128)(2,1)S(1)}, bf16[2048,256]{1,0:T(8,128)(2,1)}, u32[]{:S(2)}) copy-start(bf16[2048,256]{1,0:T(8,128)(2,1)} %refs_4_.1) | copy-start | bytes 3145732
  0.0 53.0 %copy-start.1 = (bf16[512,256]{1,0:T(8,128)(2,1)S(1)}, bf16[512,256]{1,0:T(8,128)(2,1)}, u32[]{:S(2)}) copy-start(bf16[512,256]{1,0:T(8,128)(2,1)} %refs_5_.1) | copy-start | bytes 786436
  0.0 53.0 %collective-permute-start.10 = (bf16[160,32768]{1,0:T(8,128)(2,1)}, bf16[160,32768]{1,0:T(8,128)(2,1)}, u32[]{:S(2)}, u32[]{:S(2)}) collective-permute-start(bf16[160,32768]{1,0:T(8,128)(2,1)} %refs_0_.16), channel_id=1, source_target_pairs={{0,1},{1,0},{2,3},{3,2},{4,5},{5,4},{6,7},{7,6},{8,9},{9,8},{10,11... | collective-permute-start | bytes 31457288 | tf_op jit(solution)/shard_map/ppermute | solution.py:208
  0.5 15.6 %collective-permute-start.1 = (bf16[2048,256]{1,0:T(8,128)(2,1)}, bf16[2048,256]{1,0:T(8,128)(2,1)S(1)}, u32[]{:S(2)}, u32[]{:S(2)}) collective-permute-start(bf16[2048,256]{1,0:T(8,128)(2,1)} %refs_4_.1), channel_id=1, source_target_pairs={{2,6},{3,1},{6,10},{7,3},{10,14},{11,7},{14,12},{15,11},{12,8},{13... | collective-permute-start | bytes 3145736 | tf_op jit(solution)/shard_map/ppermute | solution.py:207
  3.0 49.9 %collective-permute-start.9 = (bf16[160,8192]{1,0:T(8,128)(2,1)}, bf16[160,8192]{1,0:T(8,128)(2,1)}, u32[]{:S(2)}, u32[]{:S(2)}) collective-permute-start(bf16[160,8192]{1,0:T(8,128)(2,1)} %refs_2_.13), channel_id=1, source_target_pairs={{0,1},{1,0},{2,3},{3,2},{4,5},{5,4},{6,7},{7,6},{8,9},{9,8},{10,11... | collective-permute-start | bytes 7864328 | tf_op jit(solution)/shard_map/ppermute | solution.py:208
  3.3 15.7 %collective-permute-start = (bf16[512,256]{1,0:T(8,128)(2,1)}, bf16[512,256]{1,0:T(8,128)(2,1)S(1)}, u32[]{:S(2)}, u32[]{:S(2)}) collective-permute-start(bf16[512,256]{1,0:T(8,128)(2,1)} %refs_5_.1), channel_id=1, source_target_pairs={{2,6},{3,1},{6,10},{7,3},{10,14},{11,7},{14,12},{15,11},{12,8},{13... | collective-permute-start | bytes 786440 | tf_op jit(solution)/shard_map/ppermute | solution.py:207
  16.1 9.2 %collective-permute-start.2 = (bf16[512,256]{1,0:T(8,128)(2,1)}, bf16[512,256]{1,0:T(8,128)(2,1)S(1)}, u32[]{:S(2)}, u32[]{:S(2)}) collective-permute-start(bf16[512,256]{1,0:T(8,128)(2,1)} %refs_5_.1), channel_id=1, source_target_pairs={{6,2},{1,3},{10,6},{3,7},{14,10},{7,11},{12,14},{11,15},{8,12},{15... | collective-permute-start | bytes 786440 | tf_op jit(solution)/shard_map/ppermute | solution.py:226
  18.1 10.6 %collective-permute-start.6 = (bf16[1280,256]{1,0:T(8,128)(2,1)S(1)}, bf16[1280,256]{1,0:T(8,128)(2,1)S(1)}, u32[]{:S(2)}, u32[]{:S(2)}) collective-permute-start(bf16[1280,256]{1,0:T(8,128)(2,1)S(1)} %slice.10.refs_4_), channel_id=1, source_target_pairs={{2,6},{3,1},{6,10},{7,3},{10,14},{11,7},{14,12},{15,11},{12,8},{13... | collective-permute-start | bytes 1966088 | tf_op jit(solution)/shard_map/ppermute | solution.py:207
  25.3 12.9 %copy-start.4 = (bf16[1280,256]{1,0:T(8,128)(2,1)}, bf16[1280,256]{1,0:T(8,128)(2,1)S(1)}, u32[]{:S(2)}) copy-start(bf16[1280,256]{1,0:T(8,128)(2,1)S(1)} %pad_maximum_fusion.refs_5_) | copy-start | bytes 1966084
  25.3 11.0 %collective-permute-start.3 = (bf16[1280,256]{1,0:T(8,128)(2,1)S(1)}, bf16[1280,256]{1,0:T(8,128)(2,1)}, u32[]{:S(2)}, u32[]{:S(2)}) collective-permute-start(bf16[1280,256]{1,0:T(8,128)(2,1)S(1)} %pad_maximum_fusion.refs_5_), channel_id=1, source_target_pairs={{2,6},{3,1},{6,10},{7,3},{10,14},{11,7},{14,12},{15,11},{12,8},{13... | collective-permute-start | bytes 1966088 | tf_op jit(solution)/shard_map/ppermute | solution.py:207
  28.8 14.6 %collective-permute-start.7 = (bf16[1280,256]{1,0:T(8,128)(2,1)S(1)}, bf16[1280,256]{1,0:T(8,128)(2,1)}, u32[]{:S(2)}, u32[]{:S(2)}) collective-permute-start(bf16[1280,256]{1,0:T(8,128)(2,1)S(1)} %collective-permute-done.6.refs_4_), channel_id=1, source_target_pairs={{2,6},{3,1},{6,10},{7,3},{10,14},{11,7},{14,12},{15,11},{12,8},{13... | collective-permute-start | bytes 1966088 | tf_op jit(solution)/shard_map/ppermute | solution.py:207
  36.3 14.0 %collective-permute-start.4 = (bf16[1280,256]{1,0:T(8,128)(2,1)}, bf16[1280,256]{1,0:T(8,128)(2,1)}, u32[]{:S(2)}, u32[]{:S(2)}) collective-permute-start(bf16[1280,256]{1,0:T(8,128)(2,1)} %collective-permute-done.3.refs_5_), channel_id=1, source_target_pairs={{2,6},{3,1},{6,10},{7,3},{10,14},{11,7},{14,12},{15,11},{12,8},{13... | collective-permute-start | bytes 1966088 | tf_op jit(solution)/shard_map/ppermute | solution.py:207
  43.4 15.0 %collective-permute-start.8 = (bf16[1280,256]{1,0:T(8,128)(2,1)}, bf16[1280,256]{1,0:T(8,128)(2,1)S(1)}, u32[]{:S(2)}, u32[]{:S(2)}) collective-permute-start(bf16[1280,256]{1,0:T(8,128)(2,1)} %collective-permute-done.7.refs_4_), channel_id=1, source_target_pairs={{2,6},{3,1},{6,10},{7,3},{10,14},{11,7},{14,12},{15,11},{12,8},{13... | collective-permute-start | bytes 1966088 | tf_op jit(solution)/shard_map/ppermute | solution.py:207
  50.4 16.7 %collective-permute-start.5 = (bf16[1280,256]{1,0:T(8,128)(2,1)}, bf16[1280,256]{1,0:T(8,128)(2,1)S(1)}, u32[]{:S(2)}, u32[]{:S(2)}) collective-permute-start(bf16[1280,256]{1,0:T(8,128)(2,1)} %collective-permute-done.4.refs_5_), channel_id=1, source_target_pairs={{2,6},{3,1},{6,10},{7,3},{10,14},{11,7},{14,12},{15,11},{12,8},{13... | collective-permute-start | bytes 1966088 | tf_op jit(solution)/shard_map/ppermute | solution.py:207
  58.4 18.2 %collective-permute-start.13 = (bf16[1280,256]{1,0:T(8,128)(2,1)S(1)}, bf16[1280,256]{1,0:T(8,128)(2,1)S(1)}, u32[]{:S(2)}, u32[]{:S(2)}) collective-permute-start(bf16[1280,256]{1,0:T(8,128)(2,1)S(1)} %collective-permute-done.8.refs_4_), channel_id=1, source_target_pairs={{2,6},{3,1},{6,10},{7,3},{10,14},{11,7},{14,12},{15,11},{12,8},{13... | collective-permute-start | bytes 1966088 | tf_op jit(solution)/shard_map/ppermute | solution.py:207
  60.0 9.2 %collective-permute-start.11 = (bf16[512,256]{1,0:T(8,128)(2,1)S(1)}, bf16[512,256]{1,0:T(8,128)(2,1)S(1)}, u32[]{:S(2)}, u32[]{:S(2)}) collective-permute-start(bf16[512,256]{1,0:T(8,128)(2,1)S(1)} %collective-permute-done.2.refs_4_), channel_id=1, source_target_pairs={{6,2},{1,3},{10,6},{3,7},{14,10},{7,11},{12,14},{11,15},{8,12},{15... | collective-permute-start | bytes 786440 | tf_op jit(solution)/shard_map/ppermute | solution.py:231
  67.1 6.5 %copy-start.6 = (bf16[1280,256]{1,0:T(8,128)(2,1)}, bf16[1280,256]{1,0:T(8,128)(2,1)S(1)}, u32[]{:S(2)}) copy-start(bf16[1280,256]{1,0:T(8,128)(2,1)S(1)} %collective-permute-done.5.refs_5_) | copy-start | bytes 1966084
  69.3 11.9 %collective-permute-start.12 = (bf16[1280,256]{1,0:T(8,128)(2,1)S(1)}, bf16[1280,256]{1,0:T(8,128)(2,1)S(1)}, u32[]{:S(2)}, u32[]{:S(2)}) collective-permute-start(bf16[1280,256]{1,0:T(8,128)(2,1)S(1)} %collective-permute-done.5.refs_5_), channel_id=1, source_target_pairs={{2,6},{3,1},{6,10},{7,3},{10,14},{11,7},{14,12},{15,11},{12,8},{13... | collective-permute-start | bytes 1966088 | tf_op jit(solution)/shard_map/ppermute | solution.py:207
  76.6 12.1 %collective-permute-start.15 = (bf16[1280,256]{1,0:T(8,128)(2,1)S(1)}, bf16[1280,256]{1,0:T(8,128)(2,1)S(1)}, u32[]{:S(2)}, u32[]{:S(2)}) collective-permute-start(bf16[1280,256]{1,0:T(8,128)(2,1)S(1)} %collective-permute-done.13.refs_4_), channel_id=1, source_target_pairs={{2,6},{3,1},{6,10},{7,3},{10,14},{11,7},{14,12},{15,11},{12,8},{13... | collective-permute-start | bytes 1966088 | tf_op jit(solution)/shard_map/ppermute | solution.py:207
  81.2 4.8 %copy-start.5 = (bf16[1280,256]{1,0:T(8,128)(2,1)}, bf16[1280,256]{1,0:T(8,128)(2,1)S(1)}, u32[]{:S(2)}) copy-start(bf16[1280,256]{1,0:T(8,128)(2,1)S(1)} %collective-permute-done.12.refs_5_) | copy-start | bytes 1966084
  81.2 11.2 %collective-permute-start.14 = (bf16[768,256]{1,0:T(8,128)(2,1)S(1)}, bf16[768,256]{1,0:T(8,128)(2,1)S(1)}, u32[]{:S(2)}, u32[]{:S(2)}) collective-permute-start(bf16[768,256]{1,0:T(8,128)(2,1)S(1)} %slice.11), channel_id=1, source_target_pairs={{2,6},{3,1},{6,10},{7,3},{10,14},{11,7},{14,12},{15,11},{12,8},{13... | collective-permute-start | bytes 1179656 | tf_op jit(solution)/shard_map/ppermute | solution.py:207
  88.7 5.6 %copy-start.2 = (s32[2]{0:T(128)S(1)}, s32[2]{0:T(128)}, u32[]{:S(2)}) copy-start(s32[2]{0:T(128)} %refs_7_.1) | copy-start | bytes 28
  88.8 5.6 %copy-start.3 = (s32[2]{0:T(128)S(1)}, s32[2]{0:T(128)}, u32[]{:S(2)}) copy-start(s32[2]{0:T(128)} %refs_8_.1) | copy-start | bytes 28
  88.8 10.7 %collective-permute-start.17 = (bf16[1280,256]{1,0:T(8,128)(2,1)S(1)}, bf16[1280,256]{1,0:T(8,128)(2,1)S(1)}, u32[]{:S(2)}, u32[]{:S(2)}) collective-permute-start(bf16[1280,256]{1,0:T(8,128)(2,1)S(1)} %collective-permute-done.15.refs_2_), channel_id=1, source_target_pairs={{2,6},{3,1},{6,10},{7,3},{10,14},{11,7},{14,12},{15,11},{12,8},{13... | collective-permute-start | bytes 1966088 | tf_op jit(solution)/shard_map/ppermute | solution.py:207
  92.4 11.2 %collective-permute-start.16 = (bf16[768,256]{1,0:T(8,128)(2,1)S(1)}, bf16[768,256]{1,0:T(8,128)(2,1)S(1)}, u32[]{:S(2)}, u32[]{:S(2)}) collective-permute-start(bf16[768,256]{1,0:T(8,128)(2,1)S(1)} %collective-permute-done.14.refs_3_), channel_id=1, source_target_pairs={{2,6},{3,1},{6,10},{7,3},{10,14},{11,7},{14,12},{15,11},{12,8},{13... | collective-permute-start | bytes 1179656 | tf_op jit(solution)/shard_map/ppermute | solution.py:207
  96.4 2.4 %collective-permute-start.18 = (f32[328,256]{1,0:T(8,128)S(1)}, f32[328,256]{1,0:T(8,128)S(1)}, u32[]{:S(2)}, u32[]{:S(2)}) collective-permute-start(f32[328,256]{1,0:T(8,128)S(1)} %turned.1.own_ref), channel_id=1, source_target_pairs={{0,1},{1,0},{2,3},{3,2},{4,5},{5,4},{6,7},{7,6},{8,9},{9,8},{10,11... | collective-permute-start | bytes 1007624 | tf_op jit(solution)/shard_map/ppermute | solution.py:208

commit v25 on v24

--- a/solution.py
+++ b/solution.py
@@ -160,7 +160,7 @@
     fold = (column == query).astype(F32)
     row = lax.broadcasted_iota(jnp.int32, table_ref.shape, 0)
     count = table_ref.shape[0] // per_device
-    owner = lax.rem(count + 3 * count // 4 - 1 - lax.div(row, per_device), count)
+    owner = lax.rem(2 * count - 3 - lax.div(row, per_device), count)
     row = (owner * per_device + lax.rem(row, per_device)).astype(F32)
     contrib = (total_ref[...] + dot(window_ref[...], block_ref[...])) * inn_ref[:height]
     count = height // LEN
@@ -285,7 +285,7 @@
 
     queries = columns // RANK
     table = score_table([window, early, totals["out"], inn], slots, slots * devices, queries)
-    groups = [[(3 * devices // 4 - 1 - k) % devices for k in range(devices)]]
+    groups = [[(devices - 3 - k) % devices for k in range(devices)]]
     got = lax.all_to_all(
         table.reshape(devices, slots, queries), "dp", 0, 0, axis_index_groups=groups, tiled=True
     )

time: 115 us -> 115 us (level)
  no operation moved by 1% of the time
where the time goes in v25:
time: 115 us; the launch traced here: 114 us
  waiting for transfers between devices  49.4 us (43%)
  starting transfers between devices  27.4 us (24%)
  Pallas kernels  26.3 us (23%)
  blocking collectives  9.7 us (8%)
    ppermute x14, waiting for transfers between devices, shards(): send = lambda x: lax.ppermute(x, 'dp', pairs)  40.9 us
    pallas_call x11, Pallas kernels, call(): pl.pallas_call(kernel, grid_spec=pltpu.PrefetchScalarGridSpec(num_scalar_...  25.8 us
    ppermute x14, starting transfers between devices, shards(): send = lambda x: lax.ppermute(x, 'dp', pairs)  24.2 us
    all_to_all x1, blocking collectives, shards(): lax.all_to_all(table.reshape(devices, slots, queries), 'dp', 0, 0, axis_i...  9.7 us
    ppermute x1, waiting for transfers between devices, shards(): turned = lax.ppermute(turned, 'dp', [(j, i) for i, j in pairs])  6.32 us
  transfers between devices with their start and end apart: 19, of which 12 were waited for; matrix products, arithmetic and copies ran while one was open for 1% of the time, Pallas kernels for 23%

profile of v25, /device:TPU:0, one launch (start us, length us, event | category | flops | bytes accessed | tf_op | source)
XLA Modules:
  0.0 114.5 jit_solution(3993928455147762255)
XLA Ops:
  0.0 0.0 copy-start
  0.0 0.5 collective-permute-start.10
  0.5 2.6 %collective-permute-start.1 = (bf16[2048,256]{1,0:T(8,128)(2,1)}, bf16[2048,256]{1,0:T(8,128)(2,1)S(1)}, u32[]{:S(2)}, u32[]{:S(2)}) collective-permute-start(bf16[2048,256]{1,0:T(8,128)(2,1)} %refs_4_.1), channel_id=1, source_target_pairs={{2,6},{3,1},{6,10},{7,3},{10,14},{11,7},{14,12},{15,11},{12,8},{13... | collective-permute-start | bytes 3145736 | tf_op jit(solution)/shard_map/ppermute | solution.py:207
  3.0 0.2 collective-permute-start.9
  3.3 1.4 %collective-permute-start = (bf16[512,256]{1,0:T(8,128)(2,1)}, bf16[512,256]{1,0:T(8,128)(2,1)S(1)}, u32[]{:S(2)}, u32[]{:S(2)}) collective-permute-start(bf16[512,256]{1,0:T(8,128)(2,1)} %refs_5_.1), channel_id=1, source_target_pairs={{2,6},{3,1},{6,10},{7,3},{10,14},{11,7},{14,12},{15,11},{12,8},{13... | collective-permute-start | bytes 786440 | tf_op jit(solution)/shard_map/ppermute | solution.py:207
  4.6 11.5 %collective-permute-done.1 = bf16[2048,256]{1,0:T(8,128)(2,1)S(1)} collective-permute-done((bf16[2048,256]{1,0:T(8,128)(2,1)}, bf16[2048,256]{1,0:T(8,128)(2,1)S(1)}, u32[]{:S(2)}, u32[]{:S(2)}) %collective-permute-start.1) | collective-permute-done | bytes 1048608 | tf_op jit(solution)/shard_map/ppermute | solution.py:207
  16.1 2.0 %collective-permute-start.2 = (bf16[512,256]{1,0:T(8,128)(2,1)}, bf16[512,256]{1,0:T(8,128)(2,1)S(1)}, u32[]{:S(2)}, u32[]{:S(2)}) collective-permute-start(bf16[512,256]{1,0:T(8,128)(2,1)} %refs_5_.1), channel_id=1, source_target_pairs={{6,2},{1,3},{10,6},{3,7},{14,10},{7,11},{12,14},{11,15},{8,12},{15... | collective-permute-start | bytes 786440 | tf_op jit(solution)/shard_map/ppermute | solution.py:226
  18.1 0.1 collective-permute-start.6
  18.3 0.7 collective-permute-done
  19.0 6.3 %collective-permute-done.2.refs_4_ = bf16[512,256]{1,0:T(8,128)(2,1)S(1)} collective-permute-done((bf16[512,256]{1,0:T(8,128)(2,1)}, bf16[512,256]{1,0:T(8,128)(2,1)S(1)}, u32[]{:S(2)}, u32[]{:S(2)}) %collective-permute-start.2) | collective-permute-done | bytes 262176 | tf_op jit(solution)/shard_map/ppermute | solution.py:226
  25.3 0.0 copy-start.4
  25.3 2.2 %collective-permute-start.3 = (bf16[1280,256]{1,0:T(8,128)(2,1)S(1)}, bf16[1280,256]{1,0:T(8,128)(2,1)}, u32[]{:S(2)}, u32[]{:S(2)}) collective-permute-start(bf16[1280,256]{1,0:T(8,128)(2,1)S(1)} %pad_maximum_fusion.refs_5_), channel_id=1, source_target_pairs={{2,6},{3,1},{6,10},{7,3},{10,14},{11,7},{14,12},{15,11},{12,8},{13... | collective-permute-start | bytes 1966088 | tf_op jit(solution)/shard_map/ppermute | solution.py:207
  27.5 1.2 %collective-permute-done.6.refs_4_ = bf16[1280,256]{1,0:T(8,128)(2,1)S(1)} collective-permute-done((bf16[1280,256]{1,0:T(8,128)(2,1)S(1)}, bf16[1280,256]{1,0:T(8,128)(2,1)S(1)}, u32[]{:S(2)}, u32[]{:S(2)}) %collective-permute-start.6) | collective-permute-done | bytes 655392 | tf_op jit(solution)/shard_map/ppermute | solution.py:207
  28.8 1.9 %collective-permute-start.7 = (bf16[1280,256]{1,0:T(8,128)(2,1)S(1)}, bf16[1280,256]{1,0:T(8,128)(2,1)}, u32[]{:S(2)}, u32[]{:S(2)}) collective-permute-start(bf16[1280,256]{1,0:T(8,128)(2,1)S(1)} %collective-permute-done.6.refs_4_), channel_id=1, source_target_pairs={{2,6},{3,1},{6,10},{7,3},{10,14},{11,7},{14,12},{15,11},{12,8},{13... | collective-permute-start | bytes 1966088 | tf_op jit(solution)/shard_map/ppermute | solution.py:207
  30.7 5.7 %collective-permute-done.3.refs_5_ = bf16[1280,256]{1,0:T(8,128)(2,1)} collective-permute-done((bf16[1280,256]{1,0:T(8,128)(2,1)S(1)}, bf16[1280,256]{1,0:T(8,128)(2,1)}, u32[]{:S(2)}, u32[]{:S(2)}) %collective-permute-start.3) | collective-permute-done | bytes 655392 | tf_op jit(solution)/shard_map/ppermute | solution.py:207
  36.3 1.9 %collective-permute-start.4 = (bf16[1280,256]{1,0:T(8,128)(2,1)}, bf16[1280,256]{1,0:T(8,128)(2,1)}, u32[]{:S(2)}, u32[]{:S(2)}) collective-permute-start(bf16[1280,256]{1,0:T(8,128)(2,1)} %collective-permute-done.3.refs_5_), channel_id=1, source_target_pairs={{2,6},{3,1},{6,10},{7,3},{10,14},{11,7},{14,12},{15,11},{12,8},{13... | collective-permute-start | bytes 1966088 | tf_op jit(solution)/shard_map/ppermute | solution.py:207
  38.2 0.0 copy-done.4
  38.2 5.1 %collective-permute-done.7.refs_4_ = bf16[1280,256]{1,0:T(8,128)(2,1)} collective-permute-done((bf16[1280,256]{1,0:T(8,128)(2,1)S(1)}, bf16[1280,256]{1,0:T(8,128)(2,1)}, u32[]{:S(2)}, u32[]{:S(2)}) %collective-permute-start.7) | collective-permute-done | bytes 655392 | tf_op jit(solution)/shard_map/ppermute | solution.py:207
  43.4 1.9 %collective-permute-start.8 = (bf16[1280,256]{1,0:T(8,128)(2,1)}, bf16[1280,256]{1,0:T(8,128)(2,1)S(1)}, u32[]{:S(2)}, u32[]{:S(2)}) collective-permute-start(bf16[1280,256]{1,0:T(8,128)(2,1)} %collective-permute-done.7.refs_4_), channel_id=1, source_target_pairs={{2,6},{3,1},{6,10},{7,3},{10,14},{11,7},{14,12},{15,11},{12,8},{13... | collective-permute-start | bytes 1966088 | tf_op jit(solution)/shard_map/ppermute | solution.py:207
  45.3 5.1 %collective-permute-done.4.refs_5_ = bf16[1280,256]{1,0:T(8,128)(2,1)} collective-permute-done((bf16[1280,256]{1,0:T(8,128)(2,1)}, bf16[1280,256]{1,0:T(8,128)(2,1)}, u32[]{:S(2)}, u32[]{:S(2)}) %collective-permute-start.4) | collective-permute-done | bytes 655392 | tf_op jit(solution)/shard_map/ppermute | solution.py:207
  50.4 1.9 %collective-permute-start.5 = (bf16[1280,256]{1,0:T(8,128)(2,1)}, bf16[1280,256]{1,0:T(8,128)(2,1)S(1)}, u32[]{:S(2)}, u32[]{:S(2)}) collective-permute-start(bf16[1280,256]{1,0:T(8,128)(2,1)} %collective-permute-done.4.refs_5_), channel_id=1, source_target_pairs={{2,6},{3,1},{6,10},{7,3},{10,14},{11,7},{14,12},{15,11},{12,8},{13... | collective-permute-start | bytes 1966088 | tf_op jit(solution)/shard_map/ppermute | solution.py:207
  52.3 0.7 dynamic-slice_bitcast_fusion.order_ref
  53.0 0.0 collective-permute-done.9.refs_1_.refs_3_
  53.0 0.0 collective-permute-done.10.refs_3_.sib_ref.refs_1_
  53.0 0.0 copy-done
  53.0 0.0 copy-done.1
  53.0 2.6 %step.8 = (f32[320,256]{1,0:T(8,128)S(1)}, f32[320,256]{1,0:T(8,128)S(1)}) custom-call(s32[8]{0:T(128)S(1)} %dynamic-slice_bitcast_fusion.order_ref, bf16[160,8192]{1,0:T(8,128)(2,1)} %refs_2_.13, bf16[160,8192]{1,0:T(8,128)(2,1)} %collective-permute-done.9.refs_1_.refs_3_, bf16[160,32768]{1,0:T(8,128)(2,1)} %refs_0_.16, ...), custom_call_target="tpu_custom_call" | custom-call | flops 419430400 | bytes 3604480 | tf_op jit(solution)/shard_map/step/pallas_call | solution.py:59
  55.6 2.8 %step.9 = (f32[320,256]{1,0:T(8,128)S(1)}, f32[320,256]{1,0:T(8,128)S(1)}) custom-call(s32[8]{0:T(128)S(1)} %dynamic-slice_bitcast_fusion.order_ref, bf16[160,8192]{1,0:T(8,128)(2,1)} %refs_2_.13, bf16[160,8192]{1,0:T(8,128)(2,1)} %collective-permute-done.9.refs_1_.refs_3_, bf16[160,32768]{1,0:T(8,128)(2,1)} %refs_0_.16, ...), custom_call_target="tpu_custom_call" | custom-call | flops 419430400 | bytes 4259840 | tf_op jit(solution)/shard_map/step/pallas_call | solution.py:59
  58.4 0.0 collective-permute-done.8.refs_4_
  58.4 1.6 %collective-permute-start.13 = (bf16[1280,256]{1,0:T(8,128)(2,1)S(1)}, bf16[1280,256]{1,0:T(8,128)(2,1)S(1)}, u32[]{:S(2)}, u32[]{:S(2)}) collective-permute-start(bf16[1280,256]{1,0:T(8,128)(2,1)S(1)} %collective-permute-done.8.refs_4_), channel_id=1, source_target_pairs={{2,6},{3,1},{6,10},{7,3},{10,14},{11,7},{14,12},{15,11},{12,8},{13... | collective-permute-start | bytes 1966088 | tf_op jit(solution)/shard_map/ppermute | solution.py:207
  60.0 0.4 collective-permute-start.11
  60.5 6.6 %collective-permute-done.5.refs_5_ = bf16[1280,256]{1,0:T(8,128)(2,1)S(1)} collective-permute-done((bf16[1280,256]{1,0:T(8,128)(2,1)}, bf16[1280,256]{1,0:T(8,128)(2,1)S(1)}, u32[]{:S(2)}, u32[]{:S(2)}) %collective-permute-start.5) | collective-permute-done | bytes 655392 | tf_op jit(solution)/shard_map/ppermute | solution.py:207
  67.1 2.2 %collective-permute-done.11.refs_5_ = bf16[512,256]{1,0:T(8,128)(2,1)S(1)} collective-permute-done((bf16[512,256]{1,0:T(8,128)(2,1)S(1)}, bf16[512,256]{1,0:T(8,128)(2,1)S(1)}, u32[]{:S(2)}, u32[]{:S(2)}) %collective-permute-start.11) | collective-permute-done | bytes 262176 | tf_op jit(solution)/shard_map/ppermute | solution.py:231
  69.3 1.6 %collective-permute-start.12 = (bf16[1280,256]{1,0:T(8,128)(2,1)S(1)}, bf16[1280,256]{1,0:T(8,128)(2,1)S(1)}, u32[]{:S(2)}, u32[]{:S(2)}) collective-permute-start(bf16[1280,256]{1,0:T(8,128)(2,1)S(1)} %collective-permute-done.5.refs_5_), channel_id=1, source_target_pairs={{2,6},{3,1},{6,10},{7,3},{10,14},{11,7},{14,12},{15,11},{12,8},{13... | collective-permute-start | bytes 1966088 | tf_op jit(solution)/shard_map/ppermute | solution.py:207
  70.8 2.8 %step.10 = (f32[320,256]{1,0:T(8,128)S(1)}, f32[320,256]{1,0:T(8,128)S(1)}) custom-call(s32[8]{0:T(128)S(1)} %dynamic-slice_bitcast_fusion.order_ref, bf16[160,8192]{1,0:T(8,128)(2,1)} %refs_2_.13, bf16[160,8192]{1,0:T(8,128)(2,1)} %collective-permute-done.9.refs_1_.refs_3_, bf16[160,32768]{1,0:T(8,128)(2,1)} %refs_0_.16, ...), custom_call_target="tpu_custom_call" | custom-call | flops 419430400 | bytes 4259840 | tf_op jit(solution)/shard_map/step/pallas_call | solution.py:59
  73.6 0.0 copy-done.6
  73.6 3.0 %step.11 = (f32[320,256]{1,0:T(8,128)S(1)}, f32[320,256]{1,0:T(8,128)S(1)}) custom-call(s32[8]{0:T(128)S(1)} %dynamic-slice_bitcast_fusion.order_ref, bf16[160,8192]{1,0:T(8,128)(2,1)} %refs_2_.13, bf16[160,8192]{1,0:T(8,128)(2,1)} %collective-permute-done.9.refs_1_.refs_3_, bf16[160,32768]{1,0:T(8,128)(2,1)} %refs_0_.16, ...), custom_call_target="tpu_custom_call" | custom-call | flops 419430400 | bytes 4259840 | tf_op jit(solution)/shard_map/step/pallas_call | solution.py:59
  76.6 0.0 collective-permute-done.13.refs_4_
  76.6 1.7 %collective-permute-start.15 = (bf16[1280,256]{1,0:T(8,128)(2,1)S(1)}, bf16[1280,256]{1,0:T(8,128)(2,1)S(1)}, u32[]{:S(2)}, u32[]{:S(2)}) collective-permute-start(bf16[1280,256]{1,0:T(8,128)(2,1)S(1)} %collective-permute-done.13.refs_4_), channel_id=1, source_target_pairs={{2,6},{3,1},{6,10},{7,3},{10,14},{11,7},{14,12},{15,11},{12,8},{13... | collective-permute-start | bytes 1966088 | tf_op jit(solution)/shard_map/ppermute | solution.py:207
  78.3 2.9 %collective-permute-done.12.refs_5_ = bf16[1280,256]{1,0:T(8,128)(2,1)S(1)} collective-permute-done((bf16[1280,256]{1,0:T(8,128)(2,1)S(1)}, bf16[1280,256]{1,0:T(8,128)(2,1)S(1)}, u32[]{:S(2)}, u32[]{:S(2)}) %collective-permute-start.12) | collective-permute-done | bytes 655392 | tf_op jit(solution)/shard_map/ppermute | solution.py:207
  81.2 2.0 %collective-permute-start.14 = (bf16[768,256]{1,0:T(8,128)(2,1)S(1)}, bf16[768,256]{1,0:T(8,128)(2,1)S(1)}, u32[]{:S(2)}, u32[]{:S(2)}) collective-permute-start(bf16[768,256]{1,0:T(8,128)(2,1)S(1)} %slice.11), channel_id=1, source_target_pairs={{2,6},{3,1},{6,10},{7,3},{10,14},{11,7},{14,12},{15,11},{12,8},{13... | collective-permute-start | bytes 1179656 | tf_op jit(solution)/shard_map/ppermute | solution.py:207
  83.2 2.8 %step.12 = (f32[320,256]{1,0:T(8,128)S(1)}, f32[320,256]{1,0:T(8,128)S(1)}) custom-call(s32[8]{0:T(128)S(1)} %dynamic-slice_bitcast_fusion.order_ref, bf16[160,8192]{1,0:T(8,128)(2,1)} %refs_2_.13, bf16[160,8192]{1,0:T(8,128)(2,1)} %collective-permute-done.9.refs_1_.refs_3_, bf16[160,32768]{1,0:T(8,128)(2,1)} %refs_0_.16, ...), custom_call_target="tpu_custom_call" | custom-call | flops 419430400 | bytes 4259840 | tf_op jit(solution)/shard_map/step/pallas_call | solution.py:59
  85.9 0.0 copy-done.5
  85.9 2.8 %step.13 = (f32[320,256]{1,0:T(8,128)S(1)}, f32[320,256]{1,0:T(8,128)S(1)}) custom-call(s32[8]{0:T(128)S(1)} %dynamic-slice_bitcast_fusion.order_ref, bf16[160,8192]{1,0:T(8,128)(2,1)} %refs_2_.13, bf16[160,8192]{1,0:T(8,128)(2,1)} %collective-permute-done.9.refs_1_.refs_3_, bf16[160,32768]{1,0:T(8,128)(2,1)} %refs_0_.16, ...), custom_call_target="tpu_custom_call" | custom-call | flops 419430400 | bytes 4259840 | tf_op jit(solution)/shard_map/step/pallas_call | solution.py:59
  88.7 0.0 collective-permute-done.15.refs_2_
  88.7 0.0 copy-start.2
  88.8 0.0 copy-start.3
  88.8 1.6 %collective-permute-start.17 = (bf16[1280,256]{1,0:T(8,128)(2,1)S(1)}, bf16[1280,256]{1,0:T(8,128)(2,1)S(1)}, u32[]{:S(2)}, u32[]{:S(2)}) collective-permute-start(bf16[1280,256]{1,0:T(8,128)(2,1)S(1)} %collective-permute-done.15.refs_2_), channel_id=1, source_target_pairs={{2,6},{3,1},{6,10},{7,3},{10,14},{11,7},{14,12},{15,11},{12,8},{13... | collective-permute-start | bytes 1966088 | tf_op jit(solution)/shard_map/ppermute | solution.py:207
  90.4 1.9 %window.1.window_ref = bf16[320,768]{1,0:T(8,128)(2,1)S(1)} custom-call(s32[8]{0:T(128)S(1)} %dynamic-slice_bitcast_fusion.order_ref, bf16[160,32768]{1,0:T(8,128)(2,1)} %refs_0_.16, bf16[160,32768]{1,0:T(8,128)(2,1)} %collective-permute-done.10.refs_3_.sib_ref.refs_1_), custom_call_target="tpu_custom_call" | custom-call | bytes 1802240 | tf_op jit(solution)/shard_map/window/pallas_call | solution.py:59
  92.3 0.1 collective-permute-done.14.refs_3_
  92.4 1.9 %collective-permute-start.16 = (bf16[768,256]{1,0:T(8,128)(2,1)S(1)}, bf16[768,256]{1,0:T(8,128)(2,1)S(1)}, u32[]{:S(2)}, u32[]{:S(2)}) collective-permute-start(bf16[768,256]{1,0:T(8,128)(2,1)S(1)} %collective-permute-done.14.refs_3_), channel_id=1, source_target_pairs={{2,6},{3,1},{6,10},{7,3},{10,14},{11,7},{14,12},{15,11},{12,8},{13... | collective-permute-start | bytes 1179656 | tf_op jit(solution)/shard_map/ppermute | solution.py:207
  94.3 0.0 copy-done.2
  94.3 0.0 copy-done.3
  94.3 2.0 %turned.1.own_ref = f32[328,256]{1,0:T(8,128)S(1)} custom-call(s32[8]{0:T(128)S(1)} %dynamic-slice_bitcast_fusion.order_ref, bf16[160,8192]{1,0:T(8,128)(2,1)} %refs_2_.13, bf16[160,8192]{1,0:T(8,128)(2,1)} %collective-permute-done.9.refs_1_.refs_3_, bf16[160,8192]{1,0:T(8,128)(2,1)} %refs_2_.13, bf16[160,8192]{1,0:T(8,128)(2,1)} %collective-permute-done.9.refs_1_.refs_3_, ...), custom_call_target="tpu_custom_call" | custom-call | flops 167772160 | bytes 1843200 | tf_op jit(solution)/shard_map/turned/pallas_call | solution.py:59
  96.4 0.1 collective-permute-start.18
  96.5 2.4 %step.14.refs_3_ = f32[320,256]{1,0:T(8,128)S(1)} custom-call(s32[8]{0:T(128)S(1)} %dynamic-slice_bitcast_fusion.order_ref, bf16[160,32768]{1,0:T(8,128)(2,1)} %refs_0_.16, bf16[160,32768]{1,0:T(8,128)(2,1)} %collective-permute-done.10.refs_3_.sib_ref.refs_1_, bf16[1280,256]{1,0:T(8,128)(2,1)S(1)} %collective-permute-done.15.refs_2_, ...), custom_call_target="tpu_custom_call" | custom-call | flops 335544320 | bytes 3014656 | tf_op jit(solution)/shard_map/step/pallas_call | solution.py:59
  98.8 0.0 collective-permute-done.18.got_ref
  98.8 0.6 masked.1.inn_ref
  99.5 0.0 collective-permute-done.17.refs_2_
  99.5 2.2 %step.15.total_ref = f32[320,256]{1,0:T(8,128)S(1)} custom-call(s32[8]{0:T(128)S(1)} %dynamic-slice_bitcast_fusion.order_ref, bf16[160,32768]{1,0:T(8,128)(2,1)} %refs_0_.16, bf16[160,32768]{1,0:T(8,128)(2,1)} %collective-permute-done.10.refs_3_.sib_ref.refs_1_, bf16[1280,256]{1,0:T(8,128)(2,1)S(1)} %collective-permute-done.17.refs_2_, ...), custom_call_target="tpu_custom_call" | custom-call | flops 209715200 | bytes 2621440 | tf_op jit(solution)/shard_map/step/pallas_call | solution.py:59
  101.7 1.9 %collective-permute-done.16.block_ref = bf16[768,256]{1,0:T(8,128)(2,1)S(1)} collective-permute-done((bf16[768,256]{1,0:T(8,128)(2,1)S(1)}, bf16[768,256]{1,0:T(8,128)(2,1)S(1)}, u32[]{:S(2)}, u32[]{:S(2)}) %collective-permute-start.16) | collective-permute-done | bytes 393248 | tf_op jit(solution)/shard_map/ppermute | solution.py:207
  103.6 0.6 score.1
  104.2 9.7 %all_to_all.5 = f32[16,2,8]{2,1,0:T(2,128)S(1)} all-to-all(f32[16,2,8]{2,1,0:T(2,128)S(1)} %bitcast.3), channel_id=1, replica_groups={{13,12,11,10,9,8,7,6,5,4,3,2,1,0,15,14},{29,28,27,26,25,24,23,22,21,20,..., dimensions={0} | all-to-all | bytes 2048 | tf_op jit(solution)/shard_map/all_to_all | solution.py:289
  113.9 0.6 reduce_sum.9
  (7 shorter events, 0.1 us)
Async XLA Ops:
  0.0 53.0 %copy-start = (bf16[2048,256]{1,0:T(8,128)(2,1)S(1)}, bf16[2048,256]{1,0:T(8,128)(2,1)}, u32[]{:S(2)}) copy-start(bf16[2048,256]{1,0:T(8,128)(2,1)} %refs_4_.1) | copy-start | bytes 3145732
  0.0 53.0 %copy-start.1 = (bf16[512,256]{1,0:T(8,128)(2,1)S(1)}, bf16[512,256]{1,0:T(8,128)(2,1)}, u32[]{:S(2)}) copy-start(bf16[512,256]{1,0:T(8,128)(2,1)} %refs_5_.1) | copy-start | bytes 786436
  0.0 53.0 %collective-permute-start.10 = (bf16[160,32768]{1,0:T(8,128)(2,1)}, bf16[160,32768]{1,0:T(8,128)(2,1)}, u32[]{:S(2)}, u32[]{:S(2)}) collective-permute-start(bf16[160,32768]{1,0:T(8,128)(2,1)} %refs_0_.16), channel_id=1, source_target_pairs={{0,1},{1,0},{2,3},{3,2},{4,5},{5,4},{6,7},{7,6},{8,9},{9,8},{10,11... | collective-permute-start | bytes 31457288 | tf_op jit(solution)/shard_map/ppermute | solution.py:208
  0.5 15.6 %collective-permute-start.1 = (bf16[2048,256]{1,0:T(8,128)(2,1)}, bf16[2048,256]{1,0:T(8,128)(2,1)S(1)}, u32[]{:S(2)}, u32[]{:S(2)}) collective-permute-start(bf16[2048,256]{1,0:T(8,128)(2,1)} %refs_4_.1), channel_id=1, source_target_pairs={{2,6},{3,1},{6,10},{7,3},{10,14},{11,7},{14,12},{15,11},{12,8},{13... | collective-permute-start | bytes 3145736 | tf_op jit(solution)/shard_map/ppermute | solution.py:207
  3.0 49.9 %collective-permute-start.9 = (bf16[160,8192]{1,0:T(8,128)(2,1)}, bf16[160,8192]{1,0:T(8,128)(2,1)}, u32[]{:S(2)}, u32[]{:S(2)}) collective-permute-start(bf16[160,8192]{1,0:T(8,128)(2,1)} %refs_2_.13), channel_id=1, source_target_pairs={{0,1},{1,0},{2,3},{3,2},{4,5},{5,4},{6,7},{7,6},{8,9},{9,8},{10,11... | collective-permute-start | bytes 7864328 | tf_op jit(solution)/shard_map/ppermute | solution.py:208
  3.3 15.7 %collective-permute-start = (bf16[512,256]{1,0:T(8,128)(2,1)}, bf16[512,256]{1,0:T(8,128)(2,1)S(1)}, u32[]{:S(2)}, u32[]{:S(2)}) collective-permute-start(bf16[512,256]{1,0:T(8,128)(2,1)} %refs_5_.1), channel_id=1, source_target_pairs={{2,6},{3,1},{6,10},{7,3},{10,14},{11,7},{14,12},{15,11},{12,8},{13... | collective-permute-start | bytes 786440 | tf_op jit(solution)/shard_map/ppermute | solution.py:207
  16.1 9.2 %collective-permute-start.2 = (bf16[512,256]{1,0:T(8,128)(2,1)}, bf16[512,256]{1,0:T(8,128)(2,1)S(1)}, u32[]{:S(2)}, u32[]{:S(2)}) collective-permute-start(bf16[512,256]{1,0:T(8,128)(2,1)} %refs_5_.1), channel_id=1, source_target_pairs={{6,2},{1,3},{10,6},{3,7},{14,10},{7,11},{12,14},{11,15},{8,12},{15... | collective-permute-start | bytes 786440 | tf_op jit(solution)/shard_map/ppermute | solution.py:226
  18.1 10.6 %collective-permute-start.6 = (bf16[1280,256]{1,0:T(8,128)(2,1)S(1)}, bf16[1280,256]{1,0:T(8,128)(2,1)S(1)}, u32[]{:S(2)}, u32[]{:S(2)}) collective-permute-start(bf16[1280,256]{1,0:T(8,128)(2,1)S(1)} %slice.10.refs_4_), channel_id=1, source_target_pairs={{2,6},{3,1},{6,10},{7,3},{10,14},{11,7},{14,12},{15,11},{12,8},{13... | collective-permute-start | bytes 1966088 | tf_op jit(solution)/shard_map/ppermute | solution.py:207
  25.3 12.9 %copy-start.4 = (bf16[1280,256]{1,0:T(8,128)(2,1)}, bf16[1280,256]{1,0:T(8,128)(2,1)S(1)}, u32[]{:S(2)}) copy-start(bf16[1280,256]{1,0:T(8,128)(2,1)S(1)} %pad_maximum_fusion.refs_5_) | copy-start | bytes 1966084
  25.3 11.0 %collective-permute-start.3 = (bf16[1280,256]{1,0:T(8,128)(2,1)S(1)}, bf16[1280,256]{1,0:T(8,128)(2,1)}, u32[]{:S(2)}, u32[]{:S(2)}) collective-permute-start(bf16[1280,256]{1,0:T(8,128)(2,1)S(1)} %pad_maximum_fusion.refs_5_), channel_id=1, source_target_pairs={{2,6},{3,1},{6,10},{7,3},{10,14},{11,7},{14,12},{15,11},{12,8},{13... | collective-permute-start | bytes 1966088 | tf_op jit(solution)/shard_map/ppermute | solution.py:207
  28.8 14.6 %collective-permute-start.7 = (bf16[1280,256]{1,0:T(8,128)(2,1)S(1)}, bf16[1280,256]{1,0:T(8,128)(2,1)}, u32[]{:S(2)}, u32[]{:S(2)}) collective-permute-start(bf16[1280,256]{1,0:T(8,128)(2,1)S(1)} %collective-permute-done.6.refs_4_), channel_id=1, source_target_pairs={{2,6},{3,1},{6,10},{7,3},{10,14},{11,7},{14,12},{15,11},{12,8},{13... | collective-permute-start | bytes 1966088 | tf_op jit(solution)/shard_map/ppermute | solution.py:207
  36.3 14.0 %collective-permute-start.4 = (bf16[1280,256]{1,0:T(8,128)(2,1)}, bf16[1280,256]{1,0:T(8,128)(2,1)}, u32[]{:S(2)}, u32[]{:S(2)}) collective-permute-start(bf16[1280,256]{1,0:T(8,128)(2,1)} %collective-permute-done.3.refs_5_), channel_id=1, source_target_pairs={{2,6},{3,1},{6,10},{7,3},{10,14},{11,7},{14,12},{15,11},{12,8},{13... | collective-permute-start | bytes 1966088 | tf_op jit(solution)/shard_map/ppermute | solution.py:207
  43.4 15.0 %collective-permute-start.8 = (bf16[1280,256]{1,0:T(8,128)(2,1)}, bf16[1280,256]{1,0:T(8,128)(2,1)S(1)}, u32[]{:S(2)}, u32[]{:S(2)}) collective-permute-start(bf16[1280,256]{1,0:T(8,128)(2,1)} %collective-permute-done.7.refs_4_), channel_id=1, source_target_pairs={{2,6},{3,1},{6,10},{7,3},{10,14},{11,7},{14,12},{15,11},{12,8},{13... | collective-permute-start | bytes 1966088 | tf_op jit(solution)/shard_map/ppermute | solution.py:207
  50.4 16.7 %collective-permute-start.5 = (bf16[1280,256]{1,0:T(8,128)(2,1)}, bf16[1280,256]{1,0:T(8,128)(2,1)S(1)}, u32[]{:S(2)}, u32[]{:S(2)}) collective-permute-start(bf16[1280,256]{1,0:T(8,128)(2,1)} %collective-permute-done.4.refs_5_), channel_id=1, source_target_pairs={{2,6},{3,1},{6,10},{7,3},{10,14},{11,7},{14,12},{15,11},{12,8},{13... | collective-permute-start | bytes 1966088 | tf_op jit(solution)/shard_map/ppermute | solution.py:207
  58.4 18.2 %collective-permute-start.13 = (bf16[1280,256]{1,0:T(8,128)(2,1)S(1)}, bf16[1280,256]{1,0:T(8,128)(2,1)S(1)}, u32[]{:S(2)}, u32[]{:S(2)}) collective-permute-start(bf16[1280,256]{1,0:T(8,128)(2,1)S(1)} %collective-permute-done.8.refs_4_), channel_id=1, source_target_pairs={{2,6},{3,1},{6,10},{7,3},{10,14},{11,7},{14,12},{15,11},{12,8},{13... | collective-permute-start | bytes 1966088 | tf_op jit(solution)/shard_map/ppermute | solution.py:207
  60.0 9.2 %collective-permute-start.11 = (bf16[512,256]{1,0:T(8,128)(2,1)S(1)}, bf16[512,256]{1,0:T(8,128)(2,1)S(1)}, u32[]{:S(2)}, u32[]{:S(2)}) collective-permute-start(bf16[512,256]{1,0:T(8,128)(2,1)S(1)} %collective-permute-done.2.refs_4_), channel_id=1, source_target_pairs={{6,2},{1,3},{10,6},{3,7},{14,10},{7,11},{12,14},{11,15},{8,12},{15... | collective-permute-start | bytes 786440 | tf_op jit(solution)/shard_map/ppermute | solution.py:231
  67.1 6.5 %copy-start.6 = (bf16[1280,256]{1,0:T(8,128)(2,1)}, bf16[1280,256]{1,0:T(8,128)(2,1)S(1)}, u32[]{:S(2)}) copy-start(bf16[1280,256]{1,0:T(8,128)(2,1)S(1)} %collective-permute-done.5.refs_5_) | copy-start | bytes 1966084
  69.3 11.9 %collective-permute-start.12 = (bf16[1280,256]{1,0:T(8,128)(2,1)S(1)}, bf16[1280,256]{1,0:T(8,128)(2,1)S(1)}, u32[]{:S(2)}, u32[]{:S(2)}) collective-permute-start(bf16[1280,256]{1,0:T(8,128)(2,1)S(1)} %collective-permute-done.5.refs_5_), channel_id=1, source_target_pairs={{2,6},{3,1},{6,10},{7,3},{10,14},{11,7},{14,12},{15,11},{12,8},{13... | collective-permute-start | bytes 1966088 | tf_op jit(solution)/shard_map/ppermute | solution.py:207
  76.6 12.1 %collective-permute-start.15 = (bf16[1280,256]{1,0:T(8,128)(2,1)S(1)}, bf16[1280,256]{1,0:T(8,128)(2,1)S(1)}, u32[]{:S(2)}, u32[]{:S(2)}) collective-permute-start(bf16[1280,256]{1,0:T(8,128)(2,1)S(1)} %collective-permute-done.13.refs_4_), channel_id=1, source_target_pairs={{2,6},{3,1},{6,10},{7,3},{10,14},{11,7},{14,12},{15,11},{12,8},{13... | collective-permute-start | bytes 1966088 | tf_op jit(solution)/shard_map/ppermute | solution.py:207
  81.2 4.8 %copy-start.5 = (bf16[1280,256]{1,0:T(8,128)(2,1)}, bf16[1280,256]{1,0:T(8,128)(2,1)S(1)}, u32[]{:S(2)}) copy-start(bf16[1280,256]{1,0:T(8,128)(2,1)S(1)} %collective-permute-done.12.refs_5_) | copy-start | bytes 1966084
  81.2 11.2 %collective-permute-start.14 = (bf16[768,256]{1,0:T(8,128)(2,1)S(1)}, bf16[768,256]{1,0:T(8,128)(2,1)S(1)}, u32[]{:S(2)}, u32[]{:S(2)}) collective-permute-start(bf16[768,256]{1,0:T(8,128)(2,1)S(1)} %slice.11), channel_id=1, source_target_pairs={{2,6},{3,1},{6,10},{7,3},{10,14},{11,7},{14,12},{15,11},{12,8},{13... | collective-permute-start | bytes 1179656 | tf_op jit(solution)/shard_map/ppermute | solution.py:207
  88.7 5.6 %copy-start.2 = (s32[2]{0:T(128)S(1)}, s32[2]{0:T(128)}, u32[]{:S(2)}) copy-start(s32[2]{0:T(128)} %refs_7_.1) | copy-start | bytes 28
  88.8 5.6 %copy-start.3 = (s32[2]{0:T(128)S(1)}, s32[2]{0:T(128)}, u32[]{:S(2)}) copy-start(s32[2]{0:T(128)} %refs_8_.1) | copy-start | bytes 28
  88.8 10.7 %collective-permute-start.17 = (bf16[1280,256]{1,0:T(8,128)(2,1)S(1)}, bf16[1280,256]{1,0:T(8,128)(2,1)S(1)}, u32[]{:S(2)}, u32[]{:S(2)}) collective-permute-start(bf16[1280,256]{1,0:T(8,128)(2,1)S(1)} %collective-permute-done.15.refs_2_), channel_id=1, source_target_pairs={{2,6},{3,1},{6,10},{7,3},{10,14},{11,7},{14,12},{15,11},{12,8},{13... | collective-permute-start | bytes 1966088 | tf_op jit(solution)/shard_map/ppermute | solution.py:207
  92.4 11.2 %collective-permute-start.16 = (bf16[768,256]{1,0:T(8,128)(2,1)S(1)}, bf16[768,256]{1,0:T(8,128)(2,1)S(1)}, u32[]{:S(2)}, u32[]{:S(2)}) collective-permute-start(bf16[768,256]{1,0:T(8,128)(2,1)S(1)} %collective-permute-done.14.refs_3_), channel_id=1, source_target_pairs={{2,6},{3,1},{6,10},{7,3},{10,14},{11,7},{14,12},{15,11},{12,8},{13... | collective-permute-start | bytes 1179656 | tf_op jit(solution)/shard_map/ppermute | solution.py:207
  96.4 2.4 %collective-permute-start.18 = (f32[328,256]{1,0:T(8,128)S(1)}, f32[328,256]{1,0:T(8,128)S(1)}, u32[]{:S(2)}, u32[]{:S(2)}) collective-permute-start(f32[328,256]{1,0:T(8,128)S(1)} %turned.1.own_ref), channel_id=1, source_target_pairs={{0,1},{1,0},{2,3},{3,2},{4,5},{5,4},{6,7},{7,6},{8,9},{9,8},{10,11... | collective-permute-start | bytes 1007624 | tf_op jit(solution)/shard_map/ppermute | solution.py:208

commit v26 on v25

--- a/solution.py
+++ b/solution.py
@@ -160,7 +160,7 @@
     fold = (column == query).astype(F32)
     row = lax.broadcasted_iota(jnp.int32, table_ref.shape, 0)
     count = table_ref.shape[0] // per_device
-    owner = lax.rem(2 * count - 3 - lax.div(row, per_device), count)
+    owner = lax.rem(2 * count - 2 - lax.div(row, per_device), count)
     row = (owner * per_device + lax.rem(row, per_device)).astype(F32)
     contrib = (total_ref[...] + dot(window_ref[...], block_ref[...])) * inn_ref[:height]
     count = height // LEN
@@ -285,7 +285,7 @@
 
     queries = columns // RANK
     table = score_table([window, early, totals["out"], inn], slots, slots * devices, queries)
-    groups = [[(devices - 3 - k) % devices for k in range(devices)]]
+    groups = [[(devices - 2 - k) % devices for k in range(devices)]]
     got = lax.all_to_all(
         table.reshape(devices, slots, queries), "dp", 0, 0, axis_index_groups=groups, tiled=True
     )

time: 115 us -> 115 us (level)
  transfers between devices with their start and end apart: 19 -> 19, of which waited for: 12 -> 12; matrix products, arithmetic and copies ran while one was open for 1% -> 1% of each run, Pallas kernels for 23% -> 22%
where the time goes in v26:
time: 115 us
  waiting for transfers between devices  49.4 us (43%)
  starting transfers between devices  27.4 us (24%)
  Pallas kernels  26.3 us (23%)
  blocking collectives  9.84 us (9%)
    ppermute x14, waiting for transfers between devices, shards(): send = lambda x: lax.ppermute(x, 'dp', pairs)  40.9 us
    pallas_call x11, Pallas kernels, call(): pl.pallas_call(kernel, grid_spec=pltpu.PrefetchScalarGridSpec(num_scalar_...  25.8 us
    ppermute x14, starting transfers between devices, shards(): send = lambda x: lax.ppermute(x, 'dp', pairs)  24.2 us
    all_to_all x1, blocking collectives, shards(): lax.all_to_all(table.reshape(devices, slots, queries), 'dp', 0, 0, axis_i...  9.84 us
    ppermute x1, waiting for transfers between devices, shards(): turned = lax.ppermute(turned, 'dp', [(j, i) for i, j in pairs])  6.32 us
  transfers between devices with their start and end apart: 19, of which 12 were waited for; matrix products, arithmetic and copies ran while one was open for 1% of the time, Pallas kernels for 22%

profile of v26, /device:TPU:0, one launch (start us, length us, event | category | flops | bytes accessed | tf_op | source)
XLA Modules:
  0.0 114.6 jit_solution(7007837682603152866)
XLA Ops:
  0.0 0.0 copy-start
  0.0 0.5 collective-permute-start.10
  0.5 2.6 %collective-permute-start.1 = (bf16[2048,256]{1,0:T(8,128)(2,1)}, bf16[2048,256]{1,0:T(8,128)(2,1)S(1)}, u32[]{:S(2)}, u32[]{:S(2)}) collective-permute-start(bf16[2048,256]{1,0:T(8,128)(2,1)} %refs_4_.1), channel_id=1, source_target_pairs={{2,6},{3,1},{6,10},{7,3},{10,14},{11,7},{14,12},{15,11},{12,8},{13... | collective-permute-start | bytes 3145736 | tf_op jit(solution)/shard_map/ppermute | solution.py:207
  3.0 0.2 collective-permute-start.9
  3.3 1.4 %collective-permute-start = (bf16[512,256]{1,0:T(8,128)(2,1)}, bf16[512,256]{1,0:T(8,128)(2,1)S(1)}, u32[]{:S(2)}, u32[]{:S(2)}) collective-permute-start(bf16[512,256]{1,0:T(8,128)(2,1)} %refs_5_.1), channel_id=1, source_target_pairs={{2,6},{3,1},{6,10},{7,3},{10,14},{11,7},{14,12},{15,11},{12,8},{13... | collective-permute-start | bytes 786440 | tf_op jit(solution)/shard_map/ppermute | solution.py:207
  4.6 11.5 %collective-permute-done.1 = bf16[2048,256]{1,0:T(8,128)(2,1)S(1)} collective-permute-done((bf16[2048,256]{1,0:T(8,128)(2,1)}, bf16[2048,256]{1,0:T(8,128)(2,1)S(1)}, u32[]{:S(2)}, u32[]{:S(2)}) %collective-permute-start.1) | collective-permute-done | bytes 1048608 | tf_op jit(solution)/shard_map/ppermute | solution.py:207
  16.1 2.0 %collective-permute-start.2 = (bf16[512,256]{1,0:T(8,128)(2,1)}, bf16[512,256]{1,0:T(8,128)(2,1)S(1)}, u32[]{:S(2)}, u32[]{:S(2)}) collective-permute-start(bf16[512,256]{1,0:T(8,128)(2,1)} %refs_5_.1), channel_id=1, source_target_pairs={{6,2},{1,3},{10,6},{3,7},{14,10},{7,11},{12,14},{11,15},{8,12},{15... | collective-permute-start | bytes 786440 | tf_op jit(solution)/shard_map/ppermute | solution.py:226
  18.1 0.1 collective-permute-start.6
  18.3 0.7 collective-permute-done
  19.0 6.3 %collective-permute-done.2.refs_4_ = bf16[512,256]{1,0:T(8,128)(2,1)S(1)} collective-permute-done((bf16[512,256]{1,0:T(8,128)(2,1)}, bf16[512,256]{1,0:T(8,128)(2,1)S(1)}, u32[]{:S(2)}, u32[]{:S(2)}) %collective-permute-start.2) | collective-permute-done | bytes 262176 | tf_op jit(solution)/shard_map/ppermute | solution.py:226
  25.3 0.0 copy-start.4
  25.3 2.2 %collective-permute-start.3 = (bf16[1280,256]{1,0:T(8,128)(2,1)S(1)}, bf16[1280,256]{1,0:T(8,128)(2,1)}, u32[]{:S(2)}, u32[]{:S(2)}) collective-permute-start(bf16[1280,256]{1,0:T(8,128)(2,1)S(1)} %pad_maximum_fusion.refs_5_), channel_id=1, source_target_pairs={{2,6},{3,1},{6,10},{7,3},{10,14},{11,7},{14,12},{15,11},{12,8},{13... | collective-permute-start | bytes 1966088 | tf_op jit(solution)/shard_map/ppermute | solution.py:207
  27.5 1.2 %collective-permute-done.6.refs_4_ = bf16[1280,256]{1,0:T(8,128)(2,1)S(1)} collective-permute-done((bf16[1280,256]{1,0:T(8,128)(2,1)S(1)}, bf16[1280,256]{1,0:T(8,128)(2,1)S(1)}, u32[]{:S(2)}, u32[]{:S(2)}) %collective-permute-start.6) | collective-permute-done | bytes 655392 | tf_op jit(solution)/shard_map/ppermute | solution.py:207
  28.8 1.9 %collective-permute-start.7 = (bf16[1280,256]{1,0:T(8,128)(2,1)S(1)}, bf16[1280,256]{1,0:T(8,128)(2,1)}, u32[]{:S(2)}, u32[]{:S(2)}) collective-permute-start(bf16[1280,256]{1,0:T(8,128)(2,1)S(1)} %collective-permute-done.6.refs_4_), channel_id=1, source_target_pairs={{2,6},{3,1},{6,10},{7,3},{10,14},{11,7},{14,12},{15,11},{12,8},{13... | collective-permute-start | bytes 1966088 | tf_op jit(solution)/shard_map/ppermute | solution.py:207
  30.7 5.7 %collective-permute-done.3.refs_5_ = bf16[1280,256]{1,0:T(8,128)(2,1)} collective-permute-done((bf16[1280,256]{1,0:T(8,128)(2,1)S(1)}, bf16[1280,256]{1,0:T(8,128)(2,1)}, u32[]{:S(2)}, u32[]{:S(2)}) %collective-permute-start.3) | collective-permute-done | bytes 655392 | tf_op jit(solution)/shard_map/ppermute | solution.py:207
  36.3 1.9 %collective-permute-start.4 = (bf16[1280,256]{1,0:T(8,128)(2,1)}, bf16[1280,256]{1,0:T(8,128)(2,1)}, u32[]{:S(2)}, u32[]{:S(2)}) collective-permute-start(bf16[1280,256]{1,0:T(8,128)(2,1)} %collective-permute-done.3.refs_5_), channel_id=1, source_target_pairs={{2,6},{3,1},{6,10},{7,3},{10,14},{11,7},{14,12},{15,11},{12,8},{13... | collective-permute-start | bytes 1966088 | tf_op jit(solution)/shard_map/ppermute | solution.py:207
  38.2 0.0 copy-done.4
  38.2 5.1 %collective-permute-done.7.refs_4_ = bf16[1280,256]{1,0:T(8,128)(2,1)} collective-permute-done((bf16[1280,256]{1,0:T(8,128)(2,1)S(1)}, bf16[1280,256]{1,0:T(8,128)(2,1)}, u32[]{:S(2)}, u32[]{:S(2)}) %collective-permute-start.7) | collective-permute-done | bytes 655392 | tf_op jit(solution)/shard_map/ppermute | solution.py:207
  43.4 1.9 %collective-permute-start.8 = (bf16[1280,256]{1,0:T(8,128)(2,1)}, bf16[1280,256]{1,0:T(8,128)(2,1)S(1)}, u32[]{:S(2)}, u32[]{:S(2)}) collective-permute-start(bf16[1280,256]{1,0:T(8,128)(2,1)} %collective-permute-done.7.refs_4_), channel_id=1, source_target_pairs={{2,6},{3,1},{6,10},{7,3},{10,14},{11,7},{14,12},{15,11},{12,8},{13... | collective-permute-start | bytes 1966088 | tf_op jit(solution)/shard_map/ppermute | solution.py:207
  45.3 5.1 %collective-permute-done.4.refs_5_ = bf16[1280,256]{1,0:T(8,128)(2,1)} collective-permute-done((bf16[1280,256]{1,0:T(8,128)(2,1)}, bf16[1280,256]{1,0:T(8,128)(2,1)}, u32[]{:S(2)}, u32[]{:S(2)}) %collective-permute-start.4) | collective-permute-done | bytes 655392 | tf_op jit(solution)/shard_map/ppermute | solution.py:207
  50.4 1.9 %collective-permute-start.5 = (bf16[1280,256]{1,0:T(8,128)(2,1)}, bf16[1280,256]{1,0:T(8,128)(2,1)S(1)}, u32[]{:S(2)}, u32[]{:S(2)}) collective-permute-start(bf16[1280,256]{1,0:T(8,128)(2,1)} %collective-permute-done.4.refs_5_), channel_id=1, source_target_pairs={{2,6},{3,1},{6,10},{7,3},{10,14},{11,7},{14,12},{15,11},{12,8},{13... | collective-permute-start | bytes 1966088 | tf_op jit(solution)/shard_map/ppermute | solution.py:207
  52.3 0.7 dynamic-slice_bitcast_fusion.order_ref
  53.0 0.0 collective-permute-done.9.refs_1_.refs_3_
  53.0 0.0 collective-permute-done.10.refs_3_.sib_ref.refs_1_
  53.0 0.0 copy-done
  53.0 0.0 copy-done.1
  53.0 2.6 %step.8 = (f32[320,256]{1,0:T(8,128)S(1)}, f32[320,256]{1,0:T(8,128)S(1)}) custom-call(s32[8]{0:T(128)S(1)} %dynamic-slice_bitcast_fusion.order_ref, bf16[160,8192]{1,0:T(8,128)(2,1)} %refs_2_.13, bf16[160,8192]{1,0:T(8,128)(2,1)} %collective-permute-done.9.refs_1_.refs_3_, bf16[160,32768]{1,0:T(8,128)(2,1)} %refs_0_.16, ...), custom_call_target="tpu_custom_call" | custom-call | flops 419430400 | bytes 3604480 | tf_op jit(solution)/shard_map/step/pallas_call | solution.py:59
  55.6 2.8 %step.9 = (f32[320,256]{1,0:T(8,128)S(1)}, f32[320,256]{1,0:T(8,128)S(1)}) custom-call(s32[8]{0:T(128)S(1)} %dynamic-slice_bitcast_fusion.order_ref, bf16[160,8192]{1,0:T(8,128)(2,1)} %refs_2_.13, bf16[160,8192]{1,0:T(8,128)(2,1)} %collective-permute-done.9.refs_1_.refs_3_, bf16[160,32768]{1,0:T(8,128)(2,1)} %refs_0_.16, ...), custom_call_target="tpu_custom_call" | custom-call | flops 419430400 | bytes 4259840 | tf_op jit(solution)/shard_map/step/pallas_call | solution.py:59
  58.4 0.0 collective-permute-done.8.refs_4_
  58.4 1.6 %collective-permute-start.13 = (bf16[1280,256]{1,0:T(8,128)(2,1)S(1)}, bf16[1280,256]{1,0:T(8,128)(2,1)S(1)}, u32[]{:S(2)}, u32[]{:S(2)}) collective-permute-start(bf16[1280,256]{1,0:T(8,128)(2,1)S(1)} %collective-permute-done.8.refs_4_), channel_id=1, source_target_pairs={{2,6},{3,1},{6,10},{7,3},{10,14},{11,7},{14,12},{15,11},{12,8},{13... | collective-permute-start | bytes 1966088 | tf_op jit(solution)/shard_map/ppermute | solution.py:207
  60.0 0.4 collective-permute-start.11
  60.5 6.6 %collective-permute-done.5.refs_5_ = bf16[1280,256]{1,0:T(8,128)(2,1)S(1)} collective-permute-done((bf16[1280,256]{1,0:T(8,128)(2,1)}, bf16[1280,256]{1,0:T(8,128)(2,1)S(1)}, u32[]{:S(2)}, u32[]{:S(2)}) %collective-permute-start.5) | collective-permute-done | bytes 655392 | tf_op jit(solution)/shard_map/ppermute | solution.py:207
  67.1 2.2 %collective-permute-done.11.refs_5_ = bf16[512,256]{1,0:T(8,128)(2,1)S(1)} collective-permute-done((bf16[512,256]{1,0:T(8,128)(2,1)S(1)}, bf16[512,256]{1,0:T(8,128)(2,1)S(1)}, u32[]{:S(2)}, u32[]{:S(2)}) %collective-permute-start.11) | collective-permute-done | bytes 262176 | tf_op jit(solution)/shard_map/ppermute | solution.py:231
  69.3 1.6 %collective-permute-start.12 = (bf16[1280,256]{1,0:T(8,128)(2,1)S(1)}, bf16[1280,256]{1,0:T(8,128)(2,1)S(1)}, u32[]{:S(2)}, u32[]{:S(2)}) collective-permute-start(bf16[1280,256]{1,0:T(8,128)(2,1)S(1)} %collective-permute-done.5.refs_5_), channel_id=1, source_target_pairs={{2,6},{3,1},{6,10},{7,3},{10,14},{11,7},{14,12},{15,11},{12,8},{13... | collective-permute-start | bytes 1966088 | tf_op jit(solution)/shard_map/ppermute | solution.py:207
  70.8 2.8 %step.10 = (f32[320,256]{1,0:T(8,128)S(1)}, f32[320,256]{1,0:T(8,128)S(1)}) custom-call(s32[8]{0:T(128)S(1)} %dynamic-slice_bitcast_fusion.order_ref, bf16[160,8192]{1,0:T(8,128)(2,1)} %refs_2_.13, bf16[160,8192]{1,0:T(8,128)(2,1)} %collective-permute-done.9.refs_1_.refs_3_, bf16[160,32768]{1,0:T(8,128)(2,1)} %refs_0_.16, ...), custom_call_target="tpu_custom_call" | custom-call | flops 419430400 | bytes 4259840 | tf_op jit(solution)/shard_map/step/pallas_call | solution.py:59
  73.6 0.0 copy-done.6
  73.6 3.0 %step.11 = (f32[320,256]{1,0:T(8,128)S(1)}, f32[320,256]{1,0:T(8,128)S(1)}) custom-call(s32[8]{0:T(128)S(1)} %dynamic-slice_bitcast_fusion.order_ref, bf16[160,8192]{1,0:T(8,128)(2,1)} %refs_2_.13, bf16[160,8192]{1,0:T(8,128)(2,1)} %collective-permute-done.9.refs_1_.refs_3_, bf16[160,32768]{1,0:T(8,128)(2,1)} %refs_0_.16, ...), custom_call_target="tpu_custom_call" | custom-call | flops 419430400 | bytes 4259840 | tf_op jit(solution)/shard_map/step/pallas_call | solution.py:59
  76.6 0.0 collective-permute-done.13.refs_4_
  76.6 1.7 %collective-permute-start.15 = (bf16[1280,256]{1,0:T(8,128)(2,1)S(1)}, bf16[1280,256]{1,0:T(8,128)(2,1)S(1)}, u32[]{:S(2)}, u32[]{:S(2)}) collective-permute-start(bf16[1280,256]{1,0:T(8,128)(2,1)S(1)} %collective-permute-done.13.refs_4_), channel_id=1, source_target_pairs={{2,6},{3,1},{6,10},{7,3},{10,14},{11,7},{14,12},{15,11},{12,8},{13... | collective-permute-start | bytes 1966088 | tf_op jit(solution)/shard_map/ppermute | solution.py:207
  78.3 2.9 %collective-permute-done.12.refs_5_ = bf16[1280,256]{1,0:T(8,128)(2,1)S(1)} collective-permute-done((bf16[1280,256]{1,0:T(8,128)(2,1)S(1)}, bf16[1280,256]{1,0:T(8,128)(2,1)S(1)}, u32[]{:S(2)}, u32[]{:S(2)}) %collective-permute-start.12) | collective-permute-done | bytes 655392 | tf_op jit(solution)/shard_map/ppermute | solution.py:207
  81.2 2.0 %collective-permute-start.14 = (bf16[768,256]{1,0:T(8,128)(2,1)S(1)}, bf16[768,256]{1,0:T(8,128)(2,1)S(1)}, u32[]{:S(2)}, u32[]{:S(2)}) collective-permute-start(bf16[768,256]{1,0:T(8,128)(2,1)S(1)} %slice.11), channel_id=1, source_target_pairs={{2,6},{3,1},{6,10},{7,3},{10,14},{11,7},{14,12},{15,11},{12,8},{13... | collective-permute-start | bytes 1179656 | tf_op jit(solution)/shard_map/ppermute | solution.py:207
  83.2 2.8 %step.12 = (f32[320,256]{1,0:T(8,128)S(1)}, f32[320,256]{1,0:T(8,128)S(1)}) custom-call(s32[8]{0:T(128)S(1)} %dynamic-slice_bitcast_fusion.order_ref, bf16[160,8192]{1,0:T(8,128)(2,1)} %refs_2_.13, bf16[160,8192]{1,0:T(8,128)(2,1)} %collective-permute-done.9.refs_1_.refs_3_, bf16[160,32768]{1,0:T(8,128)(2,1)} %refs_0_.16, ...), custom_call_target="tpu_custom_call" | custom-call | flops 419430400 | bytes 4259840 | tf_op jit(solution)/shard_map/step/pallas_call | solution.py:59
  85.9 0.0 copy-done.5
  85.9 2.8 %step.13 = (f32[320,256]{1,0:T(8,128)S(1)}, f32[320,256]{1,0:T(8,128)S(1)}) custom-call(s32[8]{0:T(128)S(1)} %dynamic-slice_bitcast_fusion.order_ref, bf16[160,8192]{1,0:T(8,128)(2,1)} %refs_2_.13, bf16[160,8192]{1,0:T(8,128)(2,1)} %collective-permute-done.9.refs_1_.refs_3_, bf16[160,32768]{1,0:T(8,128)(2,1)} %refs_0_.16, ...), custom_call_target="tpu_custom_call" | custom-call | flops 419430400 | bytes 4259840 | tf_op jit(solution)/shard_map/step/pallas_call | solution.py:59
  88.7 0.0 collective-permute-done.15.refs_2_
  88.7 0.0 copy-start.2
  88.8 0.0 copy-start.3
  88.8 1.6 %collective-permute-start.17 = (bf16[1280,256]{1,0:T(8,128)(2,1)S(1)}, bf16[1280,256]{1,0:T(8,128)(2,1)S(1)}, u32[]{:S(2)}, u32[]{:S(2)}) collective-permute-start(bf16[1280,256]{1,0:T(8,128)(2,1)S(1)} %collective-permute-done.15.refs_2_), channel_id=1, source_target_pairs={{2,6},{3,1},{6,10},{7,3},{10,14},{11,7},{14,12},{15,11},{12,8},{13... | collective-permute-start | bytes 1966088 | tf_op jit(solution)/shard_map/ppermute | solution.py:207
  90.4 1.9 %window.1.window_ref = bf16[320,768]{1,0:T(8,128)(2,1)S(1)} custom-call(s32[8]{0:T(128)S(1)} %dynamic-slice_bitcast_fusion.order_ref, bf16[160,32768]{1,0:T(8,128)(2,1)} %refs_0_.16, bf16[160,32768]{1,0:T(8,128)(2,1)} %collective-permute-done.10.refs_3_.sib_ref.refs_1_), custom_call_target="tpu_custom_call" | custom-call | bytes 1802240 | tf_op jit(solution)/shard_map/window/pallas_call | solution.py:59
  92.3 0.1 collective-permute-done.14.refs_3_
  92.4 1.9 %collective-permute-start.16 = (bf16[768,256]{1,0:T(8,128)(2,1)S(1)}, bf16[768,256]{1,0:T(8,128)(2,1)S(1)}, u32[]{:S(2)}, u32[]{:S(2)}) collective-permute-start(bf16[768,256]{1,0:T(8,128)(2,1)S(1)} %collective-permute-done.14.refs_3_), channel_id=1, source_target_pairs={{2,6},{3,1},{6,10},{7,3},{10,14},{11,7},{14,12},{15,11},{12,8},{13... | collective-permute-start | bytes 1179656 | tf_op jit(solution)/shard_map/ppermute | solution.py:207
  94.3 0.0 copy-done.2
  94.3 0.0 copy-done.3
  94.3 2.0 %turned.1.own_ref = f32[328,256]{1,0:T(8,128)S(1)} custom-call(s32[8]{0:T(128)S(1)} %dynamic-slice_bitcast_fusion.order_ref, bf16[160,8192]{1,0:T(8,128)(2,1)} %refs_2_.13, bf16[160,8192]{1,0:T(8,128)(2,1)} %collective-permute-done.9.refs_1_.refs_3_, bf16[160,8192]{1,0:T(8,128)(2,1)} %refs_2_.13, bf16[160,8192]{1,0:T(8,128)(2,1)} %collective-permute-done.9.refs_1_.refs_3_, ...), custom_call_target="tpu_custom_call" | custom-call | flops 167772160 | bytes 1843200 | tf_op jit(solution)/shard_map/turned/pallas_call | solution.py:59
  96.4 0.1 collective-permute-start.18
  96.5 2.4 %step.14.refs_3_ = f32[320,256]{1,0:T(8,128)S(1)} custom-call(s32[8]{0:T(128)S(1)} %dynamic-slice_bitcast_fusion.order_ref, bf16[160,32768]{1,0:T(8,128)(2,1)} %refs_0_.16, bf16[160,32768]{1,0:T(8,128)(2,1)} %collective-permute-done.10.refs_3_.sib_ref.refs_1_, bf16[1280,256]{1,0:T(8,128)(2,1)S(1)} %collective-permute-done.15.refs_2_, ...), custom_call_target="tpu_custom_call" | custom-call | flops 335544320 | bytes 3014656 | tf_op jit(solution)/shard_map/step/pallas_call | solution.py:59
  98.8 0.0 collective-permute-done.18.got_ref
  98.8 0.6 masked.1.inn_ref
  99.5 0.0 collective-permute-done.17.refs_2_
  99.5 2.2 %step.15.total_ref = f32[320,256]{1,0:T(8,128)S(1)} custom-call(s32[8]{0:T(128)S(1)} %dynamic-slice_bitcast_fusion.order_ref, bf16[160,32768]{1,0:T(8,128)(2,1)} %refs_0_.16, bf16[160,32768]{1,0:T(8,128)(2,1)} %collective-permute-done.10.refs_3_.sib_ref.refs_1_, bf16[1280,256]{1,0:T(8,128)(2,1)S(1)} %collective-permute-done.17.refs_2_, ...), custom_call_target="tpu_custom_call" | custom-call | flops 209715200 | bytes 2621440 | tf_op jit(solution)/shard_map/step/pallas_call | solution.py:59
  101.7 1.9 %collective-permute-done.16.block_ref = bf16[768,256]{1,0:T(8,128)(2,1)S(1)} collective-permute-done((bf16[768,256]{1,0:T(8,128)(2,1)S(1)}, bf16[768,256]{1,0:T(8,128)(2,1)S(1)}, u32[]{:S(2)}, u32[]{:S(2)}) %collective-permute-start.16) | collective-permute-done | bytes 393248 | tf_op jit(solution)/shard_map/ppermute | solution.py:207
  103.6 0.6 score.1
  104.2 9.8 %all_to_all.5 = f32[16,2,8]{2,1,0:T(2,128)S(1)} all-to-all(f32[16,2,8]{2,1,0:T(2,128)S(1)} %bitcast.3), channel_id=1, replica_groups={{14,13,12,11,10,9,8,7,6,5,4,3,2,1,0,15},{30,29,28,27,26,25,24,23,22,21,..., dimensions={0} | all-to-all | bytes 2048 | tf_op jit(solution)/shard_map/all_to_all | solution.py:289
  114.0 0.6 reduce_sum.9
  (7 shorter events, 0.1 us)
Async XLA Ops:
  0.0 53.0 %copy-start = (bf16[2048,256]{1,0:T(8,128)(2,1)S(1)}, bf16[2048,256]{1,0:T(8,128)(2,1)}, u32[]{:S(2)}) copy-start(bf16[2048,256]{1,0:T(8,128)(2,1)} %refs_4_.1) | copy-start | bytes 3145732
  0.0 53.0 %copy-start.1 = (bf16[512,256]{1,0:T(8,128)(2,1)S(1)}, bf16[512,256]{1,0:T(8,128)(2,1)}, u32[]{:S(2)}) copy-start(bf16[512,256]{1,0:T(8,128)(2,1)} %refs_5_.1) | copy-start | bytes 786436
  0.0 53.0 %collective-permute-start.10 = (bf16[160,32768]{1,0:T(8,128)(2,1)}, bf16[160,32768]{1,0:T(8,128)(2,1)}, u32[]{:S(2)}, u32[]{:S(2)}) collective-permute-start(bf16[160,32768]{1,0:T(8,128)(2,1)} %refs_0_.16), channel_id=1, source_target_pairs={{0,1},{1,0},{2,3},{3,2},{4,5},{5,4},{6,7},{7,6},{8,9},{9,8},{10,11... | collective-permute-start | bytes 31457288 | tf_op jit(solution)/shard_map/ppermute | solution.py:208
  0.5 15.6 %collective-permute-start.1 = (bf16[2048,256]{1,0:T(8,128)(2,1)}, bf16[2048,256]{1,0:T(8,128)(2,1)S(1)}, u32[]{:S(2)}, u32[]{:S(2)}) collective-permute-start(bf16[2048,256]{1,0:T(8,128)(2,1)} %refs_4_.1), channel_id=1, source_target_pairs={{2,6},{3,1},{6,10},{7,3},{10,14},{11,7},{14,12},{15,11},{12,8},{13... | collective-permute-start | bytes 3145736 | tf_op jit(solution)/shard_map/ppermute | solution.py:207
  3.0 49.9 %collective-permute-start.9 = (bf16[160,8192]{1,0:T(8,128)(2,1)}, bf16[160,8192]{1,0:T(8,128)(2,1)}, u32[]{:S(2)}, u32[]{:S(2)}) collective-permute-start(bf16[160,8192]{1,0:T(8,128)(2,1)} %refs_2_.13), channel_id=1, source_target_pairs={{0,1},{1,0},{2,3},{3,2},{4,5},{5,4},{6,7},{7,6},{8,9},{9,8},{10,11... | collective-permute-start | bytes 7864328 | tf_op jit(solution)/shard_map/ppermute | solution.py:208
  3.3 15.7 %collective-permute-start = (bf16[512,256]{1,0:T(8,128)(2,1)}, bf16[512,256]{1,0:T(8,128)(2,1)S(1)}, u32[]{:S(2)}, u32[]{:S(2)}) collective-permute-start(bf16[512,256]{1,0:T(8,128)(2,1)} %refs_5_.1), channel_id=1, source_target_pairs={{2,6},{3,1},{6,10},{7,3},{10,14},{11,7},{14,12},{15,11},{12,8},{13... | collective-permute-start | bytes 786440 | tf_op jit(solution)/shard_map/ppermute | solution.py:207
  16.1 9.2 %collective-permute-start.2 = (bf16[512,256]{1,0:T(8,128)(2,1)}, bf16[512,256]{1,0:T(8,128)(2,1)S(1)}, u32[]{:S(2)}, u32[]{:S(2)}) collective-permute-start(bf16[512,256]{1,0:T(8,128)(2,1)} %refs_5_.1), channel_id=1, source_target_pairs={{6,2},{1,3},{10,6},{3,7},{14,10},{7,11},{12,14},{11,15},{8,12},{15... | collective-permute-start | bytes 786440 | tf_op jit(solution)/shard_map/ppermute | solution.py:226
  18.1 10.6 %collective-permute-start.6 = (bf16[1280,256]{1,0:T(8,128)(2,1)S(1)}, bf16[1280,256]{1,0:T(8,128)(2,1)S(1)}, u32[]{:S(2)}, u32[]{:S(2)}) collective-permute-start(bf16[1280,256]{1,0:T(8,128)(2,1)S(1)} %slice.10.refs_4_), channel_id=1, source_target_pairs={{2,6},{3,1},{6,10},{7,3},{10,14},{11,7},{14,12},{15,11},{12,8},{13... | collective-permute-start | bytes 1966088 | tf_op jit(solution)/shard_map/ppermute | solution.py:207
  25.3 12.9 %copy-start.4 = (bf16[1280,256]{1,0:T(8,128)(2,1)}, bf16[1280,256]{1,0:T(8,128)(2,1)S(1)}, u32[]{:S(2)}) copy-start(bf16[1280,256]{1,0:T(8,128)(2,1)S(1)} %pad_maximum_fusion.refs_5_) | copy-start | bytes 1966084
  25.3 11.0 %collective-permute-start.3 = (bf16[1280,256]{1,0:T(8,128)(2,1)S(1)}, bf16[1280,256]{1,0:T(8,128)(2,1)}, u32[]{:S(2)}, u32[]{:S(2)}) collective-permute-start(bf16[1280,256]{1,0:T(8,128)(2,1)S(1)} %pad_maximum_fusion.refs_5_), channel_id=1, source_target_pairs={{2,6},{3,1},{6,10},{7,3},{10,14},{11,7},{14,12},{15,11},{12,8},{13... | collective-permute-start | bytes 1966088 | tf_op jit(solution)/shard_map/ppermute | solution.py:207
  28.8 14.6 %collective-permute-start.7 = (bf16[1280,256]{1,0:T(8,128)(2,1)S(1)}, bf16[1280,256]{1,0:T(8,128)(2,1)}, u32[]{:S(2)}, u32[]{:S(2)}) collective-permute-start(bf16[1280,256]{1,0:T(8,128)(2,1)S(1)} %collective-permute-done.6.refs_4_), channel_id=1, source_target_pairs={{2,6},{3,1},{6,10},{7,3},{10,14},{11,7},{14,12},{15,11},{12,8},{13... | collective-permute-start | bytes 1966088 | tf_op jit(solution)/shard_map/ppermute | solution.py:207
  36.3 14.0 %collective-permute-start.4 = (bf16[1280,256]{1,0:T(8,128)(2,1)}, bf16[1280,256]{1,0:T(8,128)(2,1)}, u32[]{:S(2)}, u32[]{:S(2)}) collective-permute-start(bf16[1280,256]{1,0:T(8,128)(2,1)} %collective-permute-done.3.refs_5_), channel_id=1, source_target_pairs={{2,6},{3,1},{6,10},{7,3},{10,14},{11,7},{14,12},{15,11},{12,8},{13... | collective-permute-start | bytes 1966088 | tf_op jit(solution)/shard_map/ppermute | solution.py:207
  43.4 15.0 %collective-permute-start.8 = (bf16[1280,256]{1,0:T(8,128)(2,1)}, bf16[1280,256]{1,0:T(8,128)(2,1)S(1)}, u32[]{:S(2)}, u32[]{:S(2)}) collective-permute-start(bf16[1280,256]{1,0:T(8,128)(2,1)} %collective-permute-done.7.refs_4_), channel_id=1, source_target_pairs={{2,6},{3,1},{6,10},{7,3},{10,14},{11,7},{14,12},{15,11},{12,8},{13... | collective-permute-start | bytes 1966088 | tf_op jit(solution)/shard_map/ppermute | solution.py:207
  50.4 16.7 %collective-permute-start.5 = (bf16[1280,256]{1,0:T(8,128)(2,1)}, bf16[1280,256]{1,0:T(8,128)(2,1)S(1)}, u32[]{:S(2)}, u32[]{:S(2)}) collective-permute-start(bf16[1280,256]{1,0:T(8,128)(2,1)} %collective-permute-done.4.refs_5_), channel_id=1, source_target_pairs={{2,6},{3,1},{6,10},{7,3},{10,14},{11,7},{14,12},{15,11},{12,8},{13... | collective-permute-start | bytes 1966088 | tf_op jit(solution)/shard_map/ppermute | solution.py:207
  58.4 18.2 %collective-permute-start.13 = (bf16[1280,256]{1,0:T(8,128)(2,1)S(1)}, bf16[1280,256]{1,0:T(8,128)(2,1)S(1)}, u32[]{:S(2)}, u32[]{:S(2)}) collective-permute-start(bf16[1280,256]{1,0:T(8,128)(2,1)S(1)} %collective-permute-done.8.refs_4_), channel_id=1, source_target_pairs={{2,6},{3,1},{6,10},{7,3},{10,14},{11,7},{14,12},{15,11},{12,8},{13... | collective-permute-start | bytes 1966088 | tf_op jit(solution)/shard_map/ppermute | solution.py:207
  60.0 9.2 %collective-permute-start.11 = (bf16[512,256]{1,0:T(8,128)(2,1)S(1)}, bf16[512,256]{1,0:T(8,128)(2,1)S(1)}, u32[]{:S(2)}, u32[]{:S(2)}) collective-permute-start(bf16[512,256]{1,0:T(8,128)(2,1)S(1)} %collective-permute-done.2.refs_4_), channel_id=1, source_target_pairs={{6,2},{1,3},{10,6},{3,7},{14,10},{7,11},{12,14},{11,15},{8,12},{15... | collective-permute-start | bytes 786440 | tf_op jit(solution)/shard_map/ppermute | solution.py:231
  67.1 6.5 %copy-start.6 = (bf16[1280,256]{1,0:T(8,128)(2,1)}, bf16[1280,256]{1,0:T(8,128)(2,1)S(1)}, u32[]{:S(2)}) copy-start(bf16[1280,256]{1,0:T(8,128)(2,1)S(1)} %collective-permute-done.5.refs_5_) | copy-start | bytes 1966084
  69.3 11.9 %collective-permute-start.12 = (bf16[1280,256]{1,0:T(8,128)(2,1)S(1)}, bf16[1280,256]{1,0:T(8,128)(2,1)S(1)}, u32[]{:S(2)}, u32[]{:S(2)}) collective-permute-start(bf16[1280,256]{1,0:T(8,128)(2,1)S(1)} %collective-permute-done.5.refs_5_), channel_id=1, source_target_pairs={{2,6},{3,1},{6,10},{7,3},{10,14},{11,7},{14,12},{15,11},{12,8},{13... | collective-permute-start | bytes 1966088 | tf_op jit(solution)/shard_map/ppermute | solution.py:207
  76.6 12.1 %collective-permute-start.15 = (bf16[1280,256]{1,0:T(8,128)(2,1)S(1)}, bf16[1280,256]{1,0:T(8,128)(2,1)S(1)}, u32[]{:S(2)}, u32[]{:S(2)}) collective-permute-start(bf16[1280,256]{1,0:T(8,128)(2,1)S(1)} %collective-permute-done.13.refs_4_), channel_id=1, source_target_pairs={{2,6},{3,1},{6,10},{7,3},{10,14},{11,7},{14,12},{15,11},{12,8},{13... | collective-permute-start | bytes 1966088 | tf_op jit(solution)/shard_map/ppermute | solution.py:207
  81.2 4.8 %copy-start.5 = (bf16[1280,256]{1,0:T(8,128)(2,1)}, bf16[1280,256]{1,0:T(8,128)(2,1)S(1)}, u32[]{:S(2)}) copy-start(bf16[1280,256]{1,0:T(8,128)(2,1)S(1)} %collective-permute-done.12.refs_5_) | copy-start | bytes 1966084
  81.2 11.2 %collective-permute-start.14 = (bf16[768,256]{1,0:T(8,128)(2,1)S(1)}, bf16[768,256]{1,0:T(8,128)(2,1)S(1)}, u32[]{:S(2)}, u32[]{:S(2)}) collective-permute-start(bf16[768,256]{1,0:T(8,128)(2,1)S(1)} %slice.11), channel_id=1, source_target_pairs={{2,6},{3,1},{6,10},{7,3},{10,14},{11,7},{14,12},{15,11},{12,8},{13... | collective-permute-start | bytes 1179656 | tf_op jit(solution)/shard_map/ppermute | solution.py:207
  88.7 5.6 %copy-start.2 = (s32[2]{0:T(128)S(1)}, s32[2]{0:T(128)}, u32[]{:S(2)}) copy-start(s32[2]{0:T(128)} %refs_7_.1) | copy-start | bytes 28
  88.8 5.6 %copy-start.3 = (s32[2]{0:T(128)S(1)}, s32[2]{0:T(128)}, u32[]{:S(2)}) copy-start(s32[2]{0:T(128)} %refs_8_.1) | copy-start | bytes 28
  88.8 10.7 %collective-permute-start.17 = (bf16[1280,256]{1,0:T(8,128)(2,1)S(1)}, bf16[1280,256]{1,0:T(8,128)(2,1)S(1)}, u32[]{:S(2)}, u32[]{:S(2)}) collective-permute-start(bf16[1280,256]{1,0:T(8,128)(2,1)S(1)} %collective-permute-done.15.refs_2_), channel_id=1, source_target_pairs={{2,6},{3,1},{6,10},{7,3},{10,14},{11,7},{14,12},{15,11},{12,8},{13... | collective-permute-start | bytes 1966088 | tf_op jit(solution)/shard_map/ppermute | solution.py:207
  92.4 11.2 %collective-permute-start.16 = (bf16[768,256]{1,0:T(8,128)(2,1)S(1)}, bf16[768,256]{1,0:T(8,128)(2,1)S(1)}, u32[]{:S(2)}, u32[]{:S(2)}) collective-permute-start(bf16[768,256]{1,0:T(8,128)(2,1)S(1)} %collective-permute-done.14.refs_3_), channel_id=1, source_target_pairs={{2,6},{3,1},{6,10},{7,3},{10,14},{11,7},{14,12},{15,11},{12,8},{13... | collective-permute-start | bytes 1179656 | tf_op jit(solution)/shard_map/ppermute | solution.py:207
  96.4 2.4 %collective-permute-start.18 = (f32[328,256]{1,0:T(8,128)S(1)}, f32[328,256]{1,0:T(8,128)S(1)}, u32[]{:S(2)}, u32[]{:S(2)}) collective-permute-start(f32[328,256]{1,0:T(8,128)S(1)} %turned.1.own_ref), channel_id=1, source_target_pairs={{0,1},{1,0},{2,3},{3,2},{4,5},{5,4},{6,7},{7,6},{8,9},{9,8},{10,11... | collective-permute-start | bytes 1007624 | tf_op jit(solution)/shard_map/ppermute | solution.py:208
